TPU v7x, 32 devices: a whole 2x2x4 slice. The times are simulated.
32 devices in a mesh: parts: 2 (over y), adapter: 4 (over z), tensor: 4 (over x, core).
Axes of the slice: x: 2, y: 2, z: 4, core: 2. Of those that a mesh axis runs over, the one named last changes fastest.
Arguments:
- tokens: bfloat16 [3072, 8192], P(('parts', 'adapter'), 'tensor'), parts along dimension 0, may hold values from -6 to 6
- tenant: int32 [3072, 1], P(('parts', 'adapter')), parts along dimension 0, may hold values from 0 to 3; in each aligned block of 384 rows (0 to 383, 384 to 767, ...) at most 128 rows name the same one
- placement: int32 [4], replicated, may hold values from 0 to 3, each once
- frozen_projection_weight: bfloat16 [8192, 2048], P(None, 'tensor'), may hold values from -0.0625 to 0.0625
- lowrank_down_weight: bfloat16 [4, 8192, 64], P('adapter', None, 'tensor'), may hold values from -0.0625 to 0.0625
- lowrank_up_weight: bfloat16 [4, 64, 2048], P('adapter', None, 'tensor'), may hold values from -0.75 to 0.75
Outputs:
- projected: bfloat16 [3072, 2048], P(('parts', 'adapter'), 'tensor'), parts along dimension 0
There are 2 independent parts, one for each index of `parts`. A program takes and returns all parts, laid end to end along the dimension named above; an argument that names none is the same for every part. Nothing has to cross between parts.
Inputs may be any that keep to these rules, and one draw needn't show every extreme that they name: Within each aligned block of 384 rows (the rows of one device) no tenant is named more than 128 times; in at least one block some tenant is named exactly 128 times; every tenant is named somewhere. `placement`: each storage slot holds exactly one tenant.
All inputs are finite; a program needn't handle non-finite values.
Results may differ from a plain program's by a relative error of at most 0.0054.
Values may be sent and summed in bfloat16 or wider, within the bound.
No kernel may reach another device: no remote copies, remote signals or barrier semaphores. Data moves between devices by JAX's collectives and lax.ppermute only.
A program may use at most 128 MiB of HBM per device.

v0:
```python
import jax
import jax.numpy as jnp
from jax import lax
from jax.sharding import PartitionSpec as P

LOWRANK_SCALE = 2.0


def slot_targets(tenant, placement, group_capacity):
    slot_count = placement.shape[0]
    labels = tenant[:, 0]
    slot_ids = jnp.arange(slot_count, dtype=jnp.int32)
    stored = jnp.sum(jnp.where(labels[:, None] == slot_ids[None, :], placement[None, :], 0), axis=1)
    hot_marks = (stored[:, None] == slot_ids[None, :]).astype(jnp.int32)
    earlier = jnp.cumsum(hot_marks, axis=0) - hot_marks
    position = jnp.sum(earlier * hot_marks, axis=1)
    target = stored * group_capacity + position
    input_rows = (
        jnp.zeros((slot_count * group_capacity,), jnp.int32)
        .at[target]
        .set(jnp.arange(labels.shape[0], dtype=jnp.int32) + 1)
    )
    return (target, input_rows)


def fill_slots(values, input_rows):
    occupied = input_rows > 0
    picked = jnp.take(values, jnp.maximum(input_rows - 1, 0), axis=0)
    return jnp.where(occupied[:, None], picked, jnp.zeros((), values.dtype))


def apply_lowrank(slotted, down_part, up_part):
    shrunk = jnp.einsum(
        "gacd,adr->gacr", slotted, down_part, preferred_element_type=jnp.float32
    ).astype(jnp.bfloat16)
    shrunk = lax.all_gather(shrunk, "tensor", axis=3, tiled=True)
    return jnp.einsum("gacr,arn->gacn", shrunk, up_part, preferred_element_type=jnp.float32).astype(
        jnp.bfloat16
    )


def body(
    tokens, tenant, placement, frozen_projection_weight, lowrank_down_weight, lowrank_up_weight
):
    tok_rows = tokens.shape[0]
    adapters = placement.shape[0]
    group_capacity = 4 * tok_rows // (3 * adapters)
    tenant_groups = lax.axis_size("adapter")
    rows_by_group = lowrank_down_weight.shape[0]
    target, input_rows = slot_targets(tenant, placement, group_capacity)
    gathered = lax.all_gather(tokens, "tensor", axis=1, tiled=True)
    frozen_output = jnp.dot(gathered, frozen_projection_weight, preferred_element_type=jnp.float32)
    slotted = fill_slots(gathered, input_rows).reshape(
        tenant_groups, rows_by_group * group_capacity, -1
    )
    received_rows = lax.all_to_all(slotted, "adapter", split_axis=0, concat_axis=0, tiled=True)
    final_output = apply_lowrank(
        received_rows.reshape(tenant_groups, rows_by_group, group_capacity, -1),
        lowrank_down_weight,
        lowrank_up_weight,
    )
    returned = lax.all_to_all(
        final_output.reshape(tenant_groups, rows_by_group * group_capacity, -1),
        "adapter",
        split_axis=0,
        concat_axis=0,
        tiled=True,
    )
    delta_all = returned.reshape(adapters * group_capacity, -1)
    update_rows = lax.optimization_barrier(jnp.take(delta_all, target, axis=0))
    return (frozen_output + LOWRANK_SCALE * update_rows.astype(jnp.float32)).astype(jnp.bfloat16)


def solution(mesh):
    placed = (
        P(("parts", "adapter"), "tensor"),
        P(("parts", "adapter"), None),
        P(),
        P(None, "tensor"),
        P("adapter", None, "tensor"),
        P("adapter", None, "tensor"),
    )
    return jax.shard_map(
        body,
        mesh=mesh,
        in_specs=placed,
        out_specs=P(("parts", "adapter"), "tensor"),
        check_vma=False,
    )
```

profile of v0, /device:TPU:0, one launch (start us, length us, event | category | flops | bytes accessed | tf_op | source)
XLA Modules:
  0.0 318.5 jit_solution(121392189088975845)
XLA Ops:
  6.5 0.0 copy-start
  6.5 0.0 all-gather.2.cloned.1.call-start
  6.5 0.7 all-gather.2.cloned.1.call-update
  7.3 0.7 reduce
  8.0 0.7 select_reduce_fusion
  8.7 1.2 reduce-window.6
  9.9 0.2 slice_reduce_fusion
  10.1 0.2 reduce-window.9
  10.3 0.1 add_bitcast_fusion
  10.5 2.9 scatter_custom_fusion
  13.4 44.7 %all-gather.2.cloned.1.call-done = bf16[384,8192]{1,0:T(8,128)(2,1)} async-done(((bf16[384,2048]{1,0:T(8,128)(2,1)}), bf16[384,8192]{1,0:T(8,128)(2,1)}) %all-gather.2.cloned.1.call-update) | async-done | bytes 6291472 | tf_op jit(solution)/shard_map/all_gather | solution.py:51
  58.1 19.1 %gather_fusion = bf16[512,8192]{1,0:T(8,128)(2,1)} fusion(bf16[384,8192]{1,0:T(8,128)(2,1)} %all-gather.2.cloned.1.call-done, s32[1024]{0:T(1024)S(1)} %pad_clamp_fusion.1), kind=kCustom, calls=%fused_computation | custom fusion | bytes 16779264 | tf_op jit(solution)/shard_map/jit(_take)/gather | solution.py:28
  77.2 7.6 %select_select_fusion = bf16[4,128,8192]{2,1,0:T(8,128)(2,1)} fusion(bf16[4,128,8192]{2,1,0:T(8,128)(2,1)} %bitcast.46, pred[4,128]{1,0:T(4,128)(4,1)S(1)} %get-tuple-element.8, pred[4,128]{1,0:T(4,128)(4,1)S(1)} %get-tuple-element.7), kind=kLoop, calls=%fused_computation.3 | loop fusion | flops 8388608 | bytes 16778240 | tf_op jit(solution)/shard_map/jit(_where)/select_n | solution.py:29
  84.8 188.0 %all_to_all.10 = bf16[4,128,8192]{2,1,0:T(8,128)(2,1)S(1)} all-to-all(bf16[4,128,8192]{2,1,0:T(8,128)(2,1)} %select_select_fusion), channel_id=1, replica_groups=mesh['parts'=2,'adapter'=4,'tensor'=4] {'adapter'}, dimensions={0} | all-to-all | bytes 16777216 | tf_op jit(solution)/shard_map/all_to_all | solution.py:56
  272.8 0.0 copy-done
  272.8 2.3 fusion.1
  275.1 5.2 %all_gather.7 = bf16[4,1,128,64]{2,3,0,1:T(8,128)(2,1)S(1)} all-gather(bf16[4,1,128,16]{2,3,0,1:T(8,128)(2,1)S(1)} %fusion.1), channel_id=1, replica_groups=mesh['parts'=2,'adapter'=4,'tensor'=4] {'tensor'}, dimensions={3}, use_global_device_ids=true | all-gather | bytes 81920 | tf_op jit(solution)/shard_map/all_gather | solution.py:36
  280.3 0.0 copy-done.1
  280.3 1.1 convolution_convert_fusion
  281.4 3.5 %all-to-all-start.1 = ((bf16[4,128,512]{2,1,0:T(8,128)(2,1)}), bf16[4,128,512]{2,1,0:T(8,128)(2,1)S(1)}, u32[]{:S(2)}, u32[]{:S(2)}) async-start(bf16[4,128,512]{2,1,0:T(8,128)(2,1)} %convolution_convert_fusion), calls=%async_computation.1 | async-start | bytes 1048576 | tf_op jit(solution)/shard_map/all_to_all | solution.py:62
  284.9 15.2 %all-to-all-done.1 = bf16[4,128,512]{2,1,0:T(8,128)(2,1)S(1)} async-done(((bf16[4,128,512]{2,1,0:T(8,128)(2,1)}), bf16[4,128,512]{2,1,0:T(8,128)(2,1)S(1)}, u32[]{:S(2)}, u32[]{:S(2)}) %all-to-all-start.1) | async-done | bytes 524320 | tf_op jit(solution)/shard_map/all_to_all | solution.py:62
  300.2 2.1 gather_fusion.1
  302.2 0.1 broadcast_select_fusion
  302.4 9.4 %fusion = bf16[384,512]{1,0:T(8,128)(2,1)} fusion(bf16[384,8192]{1,0:T(8,128)(2,1)} %all-gather.2.cloned.1.call-done, bf16[8192,512]{1,0:T(8,128)(2,1)} %param.9, bf16[384,512]{1,0:T(8,128)(2,1)S(1)} %broadcast_select_fusion), kind=kOutput, calls=%fused_computation.6 | convolution fusion | flops 3222011904 | bytes 15466496 | tf_op jit(solution)/shard_map/dot_general | solution.py:52
  (10 shorter events, 0.1 us)
Async XLA Ops:
  6.5 266.3 %copy-start = (bf16[1,8192,16]{1,2,0:T(8,128)(2,1)S(1)}, bf16[1,8192,16]{1,2,0:T(8,128)(2,1)}, u32[]{:S(2)}) copy-start(bf16[1,8192,16]{1,2,0:T(8,128)(2,1)} %param.10) | copy-start | bytes 786436
  6.5 51.6 %all-gather.2.cloned.1.call-start = ((), (), s32[]{:S(2)}) async-start(), calls=%async_computation.2 | async-start | bytes 7864320 | tf_op jit(solution)/shard_map/all_gather | solution.py:51
  272.8 7.5 %copy-start.1 = (bf16[1,64,512]{2,1,0:T(8,128)(2,1)S(1)}, bf16[1,64,512]{2,1,0:T(8,128)(2,1)}, u32[]{:S(2)}) copy-start(bf16[1,64,512]{2,1,0:T(8,128)(2,1)} %param.11) | copy-start | bytes 196612
  281.4 18.7 %all-to-all-start.1 = ((bf16[4,128,512]{2,1,0:T(8,128)(2,1)}), bf16[4,128,512]{2,1,0:T(8,128)(2,1)S(1)}, u32[]{:S(2)}, u32[]{:S(2)}) async-start(bf16[4,128,512]{2,1,0:T(8,128)(2,1)} %convolution_convert_fusion), calls=%async_computation.1 | async-start | bytes 1048576 | tf_op jit(solution)/shard_map/all_to_all | solution.py:62
Sparse Core Ops, SparseCore 0:
  8.9 49.1 all-gather.1
where the time goes:
time: 319 us
  blocking collectives  193 us (61%)
  waiting for transfers between devices  60.6 us (19%)
  local copies, waits for them, and re-layouts  24.3 us (8%)
  between operations  13.5 us (4%)
  matrix products  12.7 us (4%)
  other arithmetic  10.7 us (3%)
  starting transfers between devices  3.47 us (1%)
    all_to_all x1, blocking collectives, body(): lax.all_to_all(slotted, 'adapter', split_axis=0, concat_axis=0, tiled=True)  188 us
    all_gather x1, waiting for transfers between devices, body(): gathered = lax.all_gather(tokens, 'tensor', axis=1, tiled=True)  44.7 us
    gather x1, local copies, waits for them, and re-layouts, fill_slots(): picked = jnp.take(values, jnp.maximum(input_rows - 1, 0), axis=0)  19.1 us
    all_to_all x1, waiting for transfers between devices, body(): lax.all_to_all(final_output.reshape(tenant_groups, rows_by_group * group_...  15.2 us
    dot_general x1, matrix products, body(): jnp.dot(gathered, frozen_projection_weight, preferred_element_type=jnp.fl...  9.35 us
    select_n x1, other arithmetic, fill_slots(): return jnp.where(occupied[:, None], picked, jnp.zeros((), values.dtype))  7.61 us
  transfers between devices with their start and end apart: 2, of which 2 were waited for; matrix products, arithmetic and copies ran while one was open for 2% of the time, Pallas kernels for 0%

commit v1 on v0

v1 whole, which is shorter than its diff:
```python
import jax
import jax.numpy as jnp
from jax import lax
from jax.sharding import PartitionSpec as P

LOWRANK_SCALE = 2.0
CORES = 2
CHUNKS = 4


def pair_up(axis_count, flip):
    return [(i, i ^ flip) for i in range(axis_count)]


def in_order(pieces, me):
    bit = 1
    while bit < len(pieces):
        swap = (me & bit) != 0
        pieces = [jnp.where(swap, pieces[j ^ bit], pieces[j]) for j in range(len(pieces))]
        bit *= 2
    return pieces


def sum_over_tensor(value, count):
    flip = 1
    while flip < count:
        value = value + lax.ppermute(value, "tensor", pair_up(count, flip))
        flip *= 2
    return value


def body(
    tokens, tenant, placement, frozen_projection_weight, lowrank_down_weight, lowrank_up_weight
):
    rows, depth = tokens.shape
    slots = placement.shape[0]
    count = lax.axis_size("tensor")
    me = lax.axis_index("tensor")
    rank_part = lowrank_down_weight.shape[2]
    rank = rank_part * count
    step = depth // CHUNKS

    down = lowrank_down_weight[0].T
    pieces = [lax.dynamic_slice_in_dim(down, me * depth, depth, axis=1)]
    for flip in range(1, count):
        piece = lax.dynamic_slice_in_dim(down, (me ^ flip) * depth, depth, axis=1)
        pieces.append(lax.ppermute(piece, "tensor", pair_up(count, flip)))
    down_slice = jnp.concatenate(in_order(pieces, me), axis=0)
    stored_here = jnp.concatenate([down_slice, lowrank_up_weight[0]], axis=1)
    adapters = lax.all_gather(stored_here, "adapter", axis=0, tiled=True)

    local = [(me, 0, tokens), (me ^ 1, 0, lax.ppermute(tokens, "tensor", pair_up(count, 1)))]
    arrived = []
    for m in range(CHUNKS):
        chunk = tokens[:, m * step : (m + 1) * step]
        for flip in range(CORES, count, CORES):
            far = lax.ppermute(chunk, "tensor", pair_up(count, flip))
            arrived.append((me ^ flip, m, far))
            arrived.append((me ^ flip ^ 1, m, lax.ppermute(far, "tensor", pair_up(count, 1))))

    labels = tenant[:, 0]
    slot_ids = jnp.arange(slots, dtype=jnp.int32)
    stored = jnp.sum(jnp.where(labels[:, None] == slot_ids[None, :], placement[None, :], 0), axis=1)
    all_slots = lax.dot_general(
        tokens, adapters[:, :depth], (((1,), (1,)), ((), ())), preferred_element_type=jnp.float32
    )
    partial = jnp.zeros((rows, rank), jnp.float32)
    for s in range(slots):
        partial += jnp.where((stored == s)[:, None], all_slots[:, s * rank : (s + 1) * rank], 0.0)
    shrunk = sum_over_tensor(partial, count).astype(jnp.bfloat16)
    spread = jnp.concatenate(
        [jnp.where((stored == s)[:, None], shrunk, jnp.zeros((), shrunk.dtype)) for s in range(slots)],
        axis=1,
    )
    expanded = jnp.dot(spread, adapters[:, depth:], preferred_element_type=jnp.float32)
    total = LOWRANK_SCALE * expanded.astype(jnp.bfloat16).astype(jnp.float32)

    for owner, m, features in local + arrived:
        part = lax.dynamic_slice_in_dim(
            frozen_projection_weight, owner * depth + m * step, features.shape[1], axis=0
        )
        total += jnp.dot(features, part, preferred_element_type=jnp.float32)
    return total.astype(jnp.bfloat16)


def solution(mesh):
    placed = (
        P(("parts", "adapter"), "tensor"),
        P(("parts", "adapter"), None),
        P(),
        P(None, "tensor"),
        P("adapter", None, "tensor"),
        P("adapter", None, "tensor"),
    )
    return jax.shard_map(
        body,
        mesh=mesh,
        in_specs=placed,
        out_specs=P(("parts", "adapter"), "tensor"),
        check_vma=False,
    )
```

time: 319 us -> 89.1 us (0.28)
  blocking collectives: 193 us -> 0 us
  waiting for transfers between devices: 60.6 us -> 36.4 us
  local copies, waits for them, and re-layouts: 24.3 us -> 2.39 us
  matrix products: 12.7 us -> 22.4 us
  other arithmetic: 10.7 us -> 4.06 us
  starting transfers between devices: 3.47 us -> 9.63 us
    all_to_all x1 -> x0, blocking collectives: 188 us -> none  [body(): lax.all_to_all(slotted, 'adapter', split_axis=0, concat_axis=0, tiled=True)]
    all_gather x1, waiting for transfers between devices: 44.7 us -> 0.02 us  [body(): adapters = lax.all_gather(stored_here, 'adapter', axis=0, tiled=True)]
    ppermute x0 -> x14, waiting for transfers between devices: none -> 36.4 us  [the longest x4 30.9 us: body(): far = lax.ppermute(chunk, 'tensor', pair_up(count, flip))]
    gather x2 -> x0, local copies, waits for them, and re-layouts: 21.1 us -> none  [the longest x1 19.1 us: fill_slots(): picked = jnp.take(values, jnp.maximum(input_rows - 1, 0), axis=0)]
    all_to_all x1 -> x0, waiting for transfers between devices: 15.2 us -> none  [body(): lax.all_to_all(final_output.reshape(tenant_groups, rows_by_group * group_...]
    dot_general x3 -> x12, matrix products: 12.7 us -> 22.4 us  [the longest x10 18.6 us: body(): total += jnp.dot(features, part, preferred_element_type=jnp.float32)]
    ppermute x0 -> x14, starting transfers between devices: none -> 9.63 us  [the longest x4 4.12 us: body(): far = lax.ppermute(chunk, 'tensor', pair_up(count, flip))]
    select_n x3, other arithmetic: 7.75 us -> 0.94 us  [the longest x1 0.9 us: in_order(): jnp.where(swap, pieces[j ^ bit], pieces[j])]
  transfers between devices with their start and end apart: 2 -> 15, of which waited for: 2 -> 7; matrix products, arithmetic and copies ran while one was open for 2% -> 26% of each run, Pallas kernels for 0% -> 0%
where the time goes in v1:
time: 89.1 us; the launch traced here: 88.5 us
  waiting for transfers between devices  36.4 us (41%)
  matrix products  22.4 us (25%)
  between operations  13.6 us (15%)
  starting transfers between devices  9.63 us (11%)
  other arithmetic  4.06 us (5%)
  local copies, waits for them, and re-layouts  2.39 us (3%)
    ppermute x4, waiting for transfers between devices, body(): far = lax.ppermute(chunk, 'tensor', pair_up(count, flip))  30.9 us
    dot_general x10, matrix products, body(): total += jnp.dot(features, part, preferred_element_type=jnp.float32)  18.6 us
    ppermute x4, starting transfers between devices, body(): far = lax.ppermute(chunk, 'tensor', pair_up(count, flip))  4.12 us
    ppermute x3, waiting for transfers between devices, body(): pieces.append(lax.ppermute(piece, 'tensor', pair_up(count, flip)))  4 us
    ppermute x3, starting transfers between devices, body(): pieces.append(lax.ppermute(piece, 'tensor', pair_up(count, flip)))  3.12 us
    dot_general x1, matrix products, body(): lax.dot_general(tokens, adapters[:, :depth], (((1,), (1,)), ((), ())), pr...  2.57 us
    ppermute x2, starting transfers between devices, sum_over_tensor(): value = value + lax.ppermute(value, 'tensor', pair_up(count, flip))  2.37 us
  transfers between devices with their start and end apart: 15, of which 7 were waited for; matrix products, arithmetic and copies ran while one was open for 26% of the time, Pallas kernels for 0%

profile of v1, /device:TPU:0, one launch (start us, length us, event | category | flops | bytes accessed | tf_op | source)
XLA Modules:
  0.0 88.5 jit_solution(18081459449628181359)
XLA Ops:
  7.5 2.4 %collective-permute-start = (bf16[16,2048]{1,0:T(8,128)(2,1)S(1)}, bf16[16,2048]{1,0:T(8,128)(2,1)S(1)}, u32[]{:S(2)}, u32[]{:S(2)}) collective-permute-start(bf16[16,2048]{1,0:T(8,128)(2,1)S(1)} %get-tuple-element.17), channel_id=1, source_target_pairs={{0,3},{1,2},{2,1},{3,0},{4,7},{5,6},{6,5},{7,4},{8,11},{9,10},{10,... | collective-permute-start | bytes 196616 | tf_op jit(solution)/shard_map/ppermute | solution.py:47
  10.6 1.8 %collective-permute-done = bf16[16,2048]{1,0:T(8,128)(2,1)S(1)} collective-permute-done((bf16[16,2048]{1,0:T(8,128)(2,1)S(1)}, bf16[16,2048]{1,0:T(8,128)(2,1)S(1)}, u32[]{:S(2)}, u32[]{:S(2)}) %collective-permute-start) | collective-permute-done | bytes 65568 | tf_op jit(solution)/shard_map/ppermute | solution.py:47
  12.4 2.2 %collective-permute-done.1 = bf16[16,2048]{1,0:T(8,128)(2,1)S(1)} collective-permute-done((bf16[16,2048]{1,0:T(8,128)(2,1)S(1)}, bf16[16,2048]{1,0:T(8,128)(2,1)S(1)}, u32[]{:S(2)}, u32[]{:S(2)}) %collective-permute-start.1) | collective-permute-done | bytes 65568 | tf_op jit(solution)/shard_map/ppermute | solution.py:47
  15.5 1.6 %pad_maximum_fusion = bf16[64,2560]{1,0:T(8,128)(2,1)} fusion(bf16[64,512]{1,0:T(8,128)(2,1)} %bitcast.81, bf16[16,2048]{1,0:T(8,128)(2,1)S(1)} %get-tuple-element.14, bf16[16,2048]{1,0:T(8,128)(2,1)S(1)} %get-tuple-element.13, bf16[16,2048]{1,0:T(8,128)(2,1)S(1)} %get-tuple-element.12, bf16[16,2048]{1,0:T(8,128)(2,1)S(1)} %get-tuple-element.11), kind=kLoop, calls=%fused_computation.38 | loop fusion | flops 1638400 | bytes 655360 | tf_op jit(solution)/shard_map/concatenate | solution.py:49
  17.1 1.5 %fusion.60 = (bf16[384,512]{1,0:T(8,128)(2,1)S(1)}, bf16[384,512]{1,0:T(8,128)(2,1)S(1)}, bf16[384,512]{1,0:T(8,128)(2,1)S(1)}, bf16[384,512]{1,0:T(8,128)(2,1)S(1)}) fusion(bf16[384,2048]{1,0:T(8,128)(2,1)} %param.6), kind=kLoop, calls=%fused_computation.87 | loop fusion | bytes 3145728 | tf_op jit(solution)/shard_map/slice | solution.py:55
  18.6 1.7 %collective-permute-start.8 = (bf16[384,512]{1,0:T(8,128)(2,1)S(1)}, bf16[384,512]{1,0:T(8,128)(2,1)}, u32[]{:S(2)}, u32[]{:S(2)}) collective-permute-start(bf16[384,512]{1,0:T(8,128)(2,1)S(1)} %get-tuple-element.8), channel_id=1, source_target_pairs={{0,2},{1,3},{2,0},{3,1},{4,6},{5,7},{6,4},{7,5},{8,10},{9,11},{10,... | collective-permute-start | bytes 1179656 | tf_op jit(solution)/shard_map/ppermute | solution.py:57
  20.7 1.7 %collective-permute-start.12 = (bf16[384,512]{1,0:T(8,128)(2,1)S(1)}, bf16[384,512]{1,0:T(8,128)(2,1)}, u32[]{:S(2)}, u32[]{:S(2)}) collective-permute-start(bf16[384,512]{1,0:T(8,128)(2,1)S(1)} %get-tuple-element.9), channel_id=1, source_target_pairs={{0,2},{1,3},{2,0},{3,1},{4,6},{5,7},{6,4},{7,5},{8,10},{9,11},{10,... | collective-permute-start | bytes 1179656 | tf_op jit(solution)/shard_map/ppermute | solution.py:57
  24.2 6.5 %collective-permute-done.8 = bf16[384,512]{1,0:T(8,128)(2,1)} collective-permute-done((bf16[384,512]{1,0:T(8,128)(2,1)S(1)}, bf16[384,512]{1,0:T(8,128)(2,1)}, u32[]{:S(2)}, u32[]{:S(2)}) %collective-permute-start.8) | collective-permute-done | bytes 393248 | tf_op jit(solution)/shard_map/ppermute | solution.py:57
  30.7 8.4 %collective-permute-done.6 = bf16[384,512]{1,0:T(8,128)(2,1)} collective-permute-done((bf16[384,512]{1,0:T(8,128)(2,1)S(1)}, bf16[384,512]{1,0:T(8,128)(2,1)}, u32[]{:S(2)}, u32[]{:S(2)}) %collective-permute-start.6) | collective-permute-done | bytes 393248 | tf_op jit(solution)/shard_map/ppermute | solution.py:57
  39.1 8.4 %collective-permute-done.12 = bf16[384,512]{1,0:T(8,128)(2,1)} collective-permute-done((bf16[384,512]{1,0:T(8,128)(2,1)S(1)}, bf16[384,512]{1,0:T(8,128)(2,1)}, u32[]{:S(2)}, u32[]{:S(2)}) %collective-permute-start.12) | collective-permute-done | bytes 393248 | tf_op jit(solution)/shard_map/ppermute | solution.py:57
  47.6 7.5 %collective-permute-done.10 = bf16[384,512]{1,0:T(8,128)(2,1)} collective-permute-done((bf16[384,512]{1,0:T(8,128)(2,1)S(1)}, bf16[384,512]{1,0:T(8,128)(2,1)}, u32[]{:S(2)}, u32[]{:S(2)}) %collective-permute-start.10) | collective-permute-done | bytes 393248 | tf_op jit(solution)/shard_map/ppermute | solution.py:57
  55.1 1.5 %convolution_bitcast_fusion.7 = f32[384,512]{1,0:T(8,128)S(1)} fusion(bf16[384,512]{1,0:T(8,128)(2,1)} %collective-permute-done.6, bf16[8192,512]{1,0:T(8,128)(2,1)} %param.9, s32[]{:T(128)S(6)} %select_n.108), kind=kOutput, calls=%fused_computation.11 | convolution fusion | flops 201326592 | bytes 1703940 | tf_op jit(solution)/shard_map/dot_general | solution.py:82
  56.6 1.5 %convolution_bitcast_fusion.3 = f32[384,512]{1,0:T(8,128)S(1)} fusion(bf16[384,512]{1,0:T(8,128)(2,1)} %collective-permute-done.10, bf16[8192,512]{1,0:T(8,128)(2,1)} %param.9, s32[]{:T(128)S(6)} %select_n.130), kind=kOutput, calls=%fused_computation.7 | convolution fusion | flops 201326592 | bytes 1703940 | tf_op jit(solution)/shard_map/dot_general | solution.py:82
  58.1 1.5 %convolution_bitcast_fusion.5 = f32[384,512]{1,0:T(8,128)S(1)} fusion(bf16[384,512]{1,0:T(8,128)(2,1)} %collective-permute-done.8, bf16[8192,512]{1,0:T(8,128)(2,1)} %param.9, s32[]{:T(128)S(6)} %select_n.128), kind=kOutput, calls=%fused_computation.9 | convolution fusion | flops 201326592 | bytes 1703940 | tf_op jit(solution)/shard_map/dot_general | solution.py:82
  59.7 1.5 %convolution_bitcast_fusion.1 = f32[384,512]{1,0:T(8,128)S(1)} fusion(bf16[384,512]{1,0:T(8,128)(2,1)} %collective-permute-done.12, bf16[8192,512]{1,0:T(8,128)(2,1)} %param.9, s32[]{:T(128)S(6)} %select_n.132), kind=kOutput, calls=%fused_computation.5 | convolution fusion | flops 201326592 | bytes 1703940 | tf_op jit(solution)/shard_map/dot_general | solution.py:82
  61.3 2.6 %convolution_bitcast_fusion.8 = f32[384,256]{0,1:T(8,128)S(1)} fusion(bf16[384,2048]{1,0:T(8,128)(2,1)} %param.6, bf16[256,2560]{1,0:T(8,128)(2,1)} %all-gather.2.cloned.1.call-done), kind=kOutput, calls=%fused_computation.28 | convolution fusion | flops 402653184 | bytes 3014656 | tf_op jit(solution)/shard_map/dot_general | solution.py:64
  64.5 1.5 %convolution_bitcast_fusion.4 = f32[384,512]{1,0:T(8,128)S(1)} fusion(bf16[384,512]{1,0:T(8,128)(2,1)} %collective-permute-done.9, bf16[8192,512]{1,0:T(8,128)(2,1)} %param.9, s32[]{:T(128)S(6)} %select_n.129), kind=kOutput, calls=%fused_computation.8 | convolution fusion | flops 201326592 | bytes 1703940 | tf_op jit(solution)/shard_map/dot_general | solution.py:82
  66.0 1.8 %collective-permute-start.4 = (f32[384,64]{0,1:T(8,128)S(1)}, f32[384,64]{0,1:T(8,128)S(1)}, u32[]{:S(2)}, u32[]{:S(2)}) collective-permute-start(f32[384,64]{0,1:T(8,128)S(1)} %fusion.72), channel_id=1, source_target_pairs={{0,2},{1,3},{2,0},{3,1},{4,6},{5,7},{6,4},{7,5},{8,10},{9,11},{10,... | collective-permute-start | bytes 294920 | tf_op jit(solution)/shard_map/ppermute | solution.py:27
  67.9 1.5 %convolution_bitcast_fusion = f32[384,512]{1,0:T(8,128)S(1)} fusion(bf16[384,512]{1,0:T(8,128)(2,1)} %collective-permute-done.13, bf16[8192,512]{1,0:T(8,128)(2,1)} %param.9, s32[]{:T(128)S(6)} %select_n.133), kind=kOutput, calls=%fused_computation.4 | convolution fusion | flops 201326592 | bytes 1703940 | tf_op jit(solution)/shard_map/dot_general | solution.py:82
  69.4 1.4 %collective-permute-done.4 = f32[384,64]{0,1:T(8,128)S(1)} collective-permute-done((f32[384,64]{0,1:T(8,128)S(1)}, f32[384,64]{0,1:T(8,128)S(1)}, u32[]{:S(2)}, u32[]{:S(2)}) %collective-permute-start.4) | collective-permute-done | bytes 98336 | tf_op jit(solution)/shard_map/ppermute | solution.py:27
  72.1 2.6 %fusion.20 = f32[384,512]{1,0:T(8,128)S(1)} fusion(f32[384,512]{1,0:T(8,128)S(1)} %fusion.28, bf16[384,2048]{1,0:T(8,128)(2,1)S(1)} %copy-done, bf16[8192,512]{1,0:T(8,128)(2,1)} %param.9, s32[]{:T(128)S(6)} %select_n.111), kind=kOutput, calls=%fused_computation.22 | convolution fusion | flops 805502976 | bytes 5242884 | tf_op jit(solution)/shard_map/dot_general | solution.py:82
  74.8 3.1 %fusion.23 = f32[384,512]{1,0:T(8,128)S(1)} fusion(f32[384,512]{1,0:T(8,128)S(1)} %convolution_bitcast_fusion.7, f32[384,512]{1,0:T(8,128)S(1)} %fusion.20, bf16[384,2048]{1,0:T(8,128)(2,1)} %collective-permute-done.5, bf16[8192,512]{1,0:T(8,128)(2,1)} %param.9, s32[]{:T(128)S(6)} %select_n.110), kind=kOutput, calls=%fused_computation.23 | convolution fusion | flops 805699584 | bytes 6029316 | tf_op jit(solution)/shard_map/dot_general | solution.py:82
  77.8 1.5 %fusion.16 = f32[384,512]{1,0:T(8,128)S(1)} fusion(f32[384,512]{1,0:T(8,128)S(1)} %convolution_bitcast_fusion.3, f32[384,512]{1,0:T(8,128)S(1)} %convolution_bitcast_fusion.4, f32[384,512]{1,0:T(8,128)S(1)} %convolution_bitcast_fusion.5, f32[384,512]{1,0:T(8,128)S(1)} %fusion.23, bf16[384,512]{1,0:T(8,128)(2,1)S(1)} %collective-permute-done.7, ...), kind=kOutput, calls=%fused_computation.20 | convolution fusion | flops 202113024 | bytes 4849668 | tf_op jit(solution)/shard_map/dot_general | solution.py:82
  79.3 2.3 %fusion.26 = bf16[384,512]{1,0:T(8,128)(2,1)} fusion(f32[384,512]{1,0:T(8,128)S(1)} %convolution_bitcast_fusion, f32[384,512]{1,0:T(8,128)S(1)} %convolution_bitcast_fusion.1, f32[384,512]{1,0:T(8,128)S(1)} %fusion.16, bf16[384,512]{1,0:T(8,128)(2,1)} %collective-permute-done.11, bf16[8192,512]{1,0:T(8,128)(2,1)} %param.9, s32[]{:T(128)S(6)} %select_n.131), kind=kOutput, calls=%fused_computation.24 | convolution fusion | flops 202113024 | bytes 3670020 | tf_op jit(solution)/shard_map/dot_general | solution.py:82
  (32 shorter events, 6.6 us)
Async XLA Ops:
  6.5 54.7 %all-gather.2.cloned.1.call-start = ((), (), s32[]{:S(2)}) async-start(), calls=%async_computation | async-start | bytes 1638400 | tf_op jit(solution)/shard_map/all_gather | solution.py:50
  7.5 4.9 %collective-permute-start = (bf16[16,2048]{1,0:T(8,128)(2,1)S(1)}, bf16[16,2048]{1,0:T(8,128)(2,1)S(1)}, u32[]{:S(2)}, u32[]{:S(2)}) collective-permute-start(bf16[16,2048]{1,0:T(8,128)(2,1)S(1)} %get-tuple-element.17), channel_id=1, source_target_pairs={{0,3},{1,2},{2,1},{3,0},{4,7},{5,6},{6,5},{7,4},{8,11},{9,10},{10,... | collective-permute-start | bytes 196616 | tf_op jit(solution)/shard_map/ppermute | solution.py:47
  9.9 4.7 %collective-permute-start.1 = (bf16[16,2048]{1,0:T(8,128)(2,1)S(1)}, bf16[16,2048]{1,0:T(8,128)(2,1)S(1)}, u32[]{:S(2)}, u32[]{:S(2)}) collective-permute-start(bf16[16,2048]{1,0:T(8,128)(2,1)S(1)} %get-tuple-element.16), channel_id=1, source_target_pairs={{0,2},{1,3},{2,0},{3,1},{4,6},{5,7},{6,4},{7,5},{8,10},{9,11},{10,... | collective-permute-start | bytes 196616 | tf_op jit(solution)/shard_map/ppermute | solution.py:47
  10.5 4.0 %collective-permute-start.2 = (bf16[16,2048]{1,0:T(8,128)(2,1)S(1)}, bf16[16,2048]{1,0:T(8,128)(2,1)S(1)}, u32[]{:S(2)}, u32[]{:S(2)}) collective-permute-start(bf16[16,2048]{1,0:T(8,128)(2,1)S(1)} %get-tuple-element.15), channel_id=1, source_target_pairs={{0,1},{1,0},{2,3},{3,2},{4,5},{5,4},{6,7},{7,6},{8,9},{9,8},{10,11... | collective-permute-start | bytes 196616 | tf_op jit(solution)/shard_map/ppermute | solution.py:47
  18.6 12.1 %collective-permute-start.8 = (bf16[384,512]{1,0:T(8,128)(2,1)S(1)}, bf16[384,512]{1,0:T(8,128)(2,1)}, u32[]{:S(2)}, u32[]{:S(2)}) collective-permute-start(bf16[384,512]{1,0:T(8,128)(2,1)S(1)} %get-tuple-element.8), channel_id=1, source_target_pairs={{0,2},{1,3},{2,0},{3,1},{4,6},{5,7},{6,4},{7,5},{8,10},{9,11},{10,... | collective-permute-start | bytes 1179656 | tf_op jit(solution)/shard_map/ppermute | solution.py:57
  20.3 18.8 %collective-permute-start.6 = (bf16[384,512]{1,0:T(8,128)(2,1)S(1)}, bf16[384,512]{1,0:T(8,128)(2,1)}, u32[]{:S(2)}, u32[]{:S(2)}) collective-permute-start(bf16[384,512]{1,0:T(8,128)(2,1)S(1)} %get-tuple-element.7), channel_id=1, source_target_pairs={{0,2},{1,3},{2,0},{3,1},{4,6},{5,7},{6,4},{7,5},{8,10},{9,11},{10,... | collective-permute-start | bytes 1179656 | tf_op jit(solution)/shard_map/ppermute | solution.py:57
  20.7 26.9 %collective-permute-start.12 = (bf16[384,512]{1,0:T(8,128)(2,1)S(1)}, bf16[384,512]{1,0:T(8,128)(2,1)}, u32[]{:S(2)}, u32[]{:S(2)}) collective-permute-start(bf16[384,512]{1,0:T(8,128)(2,1)S(1)} %get-tuple-element.9), channel_id=1, source_target_pairs={{0,2},{1,3},{2,0},{3,1},{4,6},{5,7},{6,4},{7,5},{8,10},{9,11},{10,... | collective-permute-start | bytes 1179656 | tf_op jit(solution)/shard_map/ppermute | solution.py:57
  22.3 32.7 %collective-permute-start.10 = (bf16[384,512]{1,0:T(8,128)(2,1)S(1)}, bf16[384,512]{1,0:T(8,128)(2,1)}, u32[]{:S(2)}, u32[]{:S(2)}) collective-permute-start(bf16[384,512]{1,0:T(8,128)(2,1)S(1)} %get-tuple-element.10), channel_id=1, source_target_pairs={{0,2},{1,3},{2,0},{3,1},{4,6},{5,7},{6,4},{7,5},{8,10},{9,11},{10,... | collective-permute-start | bytes 1179656 | tf_op jit(solution)/shard_map/ppermute | solution.py:57
  22.7 52.1 %collective-permute-start.5 = (bf16[384,2048]{1,0:T(8,128)(2,1)}, bf16[384,2048]{1,0:T(8,128)(2,1)}, u32[]{:S(2)}, u32[]{:S(2)}) collective-permute-start(bf16[384,2048]{1,0:T(8,128)(2,1)} %param.6), channel_id=1, source_target_pairs={{0,1},{1,0},{2,3},{3,2},{4,5},{5,4},{6,7},{7,6},{8,9},{9,8},{10,11... | collective-permute-start | bytes 4718600 | tf_op jit(solution)/shard_map/ppermute | solution.py:52
  30.7 33.2 %collective-permute-start.9 = (bf16[384,512]{1,0:T(8,128)(2,1)}, bf16[384,512]{1,0:T(8,128)(2,1)}, u32[]{:S(2)}, u32[]{:S(2)}) collective-permute-start(bf16[384,512]{1,0:T(8,128)(2,1)} %collective-permute-done.8), channel_id=1, source_target_pairs={{0,1},{1,0},{2,3},{3,2},{4,5},{5,4},{6,7},{7,6},{8,9},{9,8},{10,11... | collective-permute-start | bytes 1179656 | tf_op jit(solution)/shard_map/ppermute | solution.py:59
  39.1 38.7 %collective-permute-start.7 = (bf16[384,512]{1,0:T(8,128)(2,1)}, bf16[384,512]{1,0:T(8,128)(2,1)S(1)}, u32[]{:S(2)}, u32[]{:S(2)}) collective-permute-start(bf16[384,512]{1,0:T(8,128)(2,1)} %collective-permute-done.6), channel_id=1, source_target_pairs={{0,1},{1,0},{2,3},{3,2},{4,5},{5,4},{6,7},{7,6},{8,9},{9,8},{10,11... | collective-permute-start | bytes 1179656 | tf_op jit(solution)/shard_map/ppermute | solution.py:59
  47.6 20.3 %collective-permute-start.13 = (bf16[384,512]{1,0:T(8,128)(2,1)}, bf16[384,512]{1,0:T(8,128)(2,1)}, u32[]{:S(2)}, u32[]{:S(2)}) collective-permute-start(bf16[384,512]{1,0:T(8,128)(2,1)} %collective-permute-done.12), channel_id=1, source_target_pairs={{0,1},{1,0},{2,3},{3,2},{4,5},{5,4},{6,7},{7,6},{8,9},{9,8},{10,11... | collective-permute-start | bytes 1179656 | tf_op jit(solution)/shard_map/ppermute | solution.py:59
  55.1 24.2 %collective-permute-start.11 = (bf16[384,512]{1,0:T(8,128)(2,1)}, bf16[384,512]{1,0:T(8,128)(2,1)}, u32[]{:S(2)}, u32[]{:S(2)}) collective-permute-start(bf16[384,512]{1,0:T(8,128)(2,1)} %collective-permute-done.10), channel_id=1, source_target_pairs={{0,1},{1,0},{2,3},{3,2},{4,5},{5,4},{6,7},{7,6},{8,9},{9,8},{10,11... | collective-permute-start | bytes 1179656 | tf_op jit(solution)/shard_map/ppermute | solution.py:59
  61.3 10.9 %copy-start = (bf16[384,2048]{1,0:T(8,128)(2,1)S(1)}, bf16[384,2048]{1,0:T(8,128)(2,1)}, u32[]{:S(2)}) copy-start(bf16[384,2048]{1,0:T(8,128)(2,1)} %param.6) | copy-start | bytes 4718596
  63.9 2.1 %collective-permute-start.3 = (f32[384,64]{0,1:T(8,128)S(1)}, f32[384,64]{0,1:T(8,128)S(1)}, u32[]{:S(2)}, u32[]{:S(2)}) collective-permute-start(f32[384,64]{0,1:T(8,128)S(1)} %fusion.46), channel_id=1, source_target_pairs={{0,1},{1,0},{2,3},{3,2},{4,5},{5,4},{6,7},{7,6},{8,9},{9,8},{10,11... | collective-permute-start | bytes 294920 | tf_op jit(solution)/shard_map/ppermute | solution.py:27
  66.0 4.8 %collective-permute-start.4 = (f32[384,64]{0,1:T(8,128)S(1)}, f32[384,64]{0,1:T(8,128)S(1)}, u32[]{:S(2)}, u32[]{:S(2)}) collective-permute-start(f32[384,64]{0,1:T(8,128)S(1)} %fusion.72), channel_id=1, source_target_pairs={{0,2},{1,3},{2,0},{3,1},{4,6},{5,7},{6,4},{7,5},{8,10},{9,11},{10,... | collective-permute-start | bytes 294920 | tf_op jit(solution)/shard_map/ppermute | solution.py:27
Sparse Core Ops, SparseCore 0:
  17.2 34.1 all-gather.1

commit v2 on v1

--- a/solution.py
+++ b/solution.py
@@ -40,30 +40,56 @@
     rank = rank_part * count
     step = depth // CHUNKS
 
+    parts = lax.axis_size("parts")
+    half = depth // parts
+    mine = lax.axis_index("parts") * half
+
+    chunks = [tokens[:, m * step : (m + 1) * step] for m in range(CHUNKS)]
+
     down = lowrank_down_weight[0].T
-    pieces = [lax.dynamic_slice_in_dim(down, me * depth, depth, axis=1)]
-    for flip in range(1, count):
-        piece = lax.dynamic_slice_in_dim(down, (me ^ flip) * depth, depth, axis=1)
-        pieces.append(lax.ppermute(piece, "tensor", pair_up(count, flip)))
+    pieces = [
+        lax.dynamic_slice_in_dim(down, (me ^ flip) * depth + mine, half, axis=1)
+        for flip in range(count)
+    ]
+    chunks[0], pieces = lax.optimization_barrier((chunks[0], pieces))
+    pieces = [pieces[0]] + [
+        lax.ppermute(pieces[flip], "tensor", pair_up(count, flip)) for flip in range(1, count)
+    ]
     down_slice = jnp.concatenate(in_order(pieces, me), axis=0)
-    stored_here = jnp.concatenate([down_slice, lowrank_up_weight[0]], axis=1)
-    adapters = lax.all_gather(stored_here, "adapter", axis=0, tiled=True)
+    columns = lowrank_up_weight.shape[2]
+    up_share = lax.dynamic_slice_in_dim(
+        lowrank_up_weight[0], lax.axis_index("parts") * (rank // parts), rank // parts, axis=0
+    )
+    up = lax.all_gather(up_share, ("adapter", "parts"), axis=0, tiled=True)
+    down_all = lax.all_gather(down_slice, ("parts", "adapter"), axis=0, tiled=True)
 
-    local = [(me, 0, tokens), (me ^ 1, 0, lax.ppermute(tokens, "tensor", pair_up(count, 1)))]
     arrived = []
+    neighbour = lax.ppermute(tokens, "tensor", pair_up(count, 1))
     for m in range(CHUNKS):
-        chunk = tokens[:, m * step : (m + 1) * step]
         for flip in range(CORES, count, CORES):
-            far = lax.ppermute(chunk, "tensor", pair_up(count, flip))
+            far = lax.ppermute(chunks[m], "tensor", pair_up(count, flip))
             arrived.append((me ^ flip, m, far))
             arrived.append((me ^ flip ^ 1, m, lax.ppermute(far, "tensor", pair_up(count, 1))))
+
+    def weight_rows(owner, m, width):
+        return lax.dynamic_slice_in_dim(
+            frozen_projection_weight, owner * depth + m * step, width, axis=0
+        )
+
+    total = jnp.dot(tokens, weight_rows(me, 0, depth), preferred_element_type=jnp.float32)
+    total += jnp.dot(neighbour, weight_rows(me ^ 1, 0, depth), preferred_element_type=jnp.float32)
 
     labels = tenant[:, 0]
     slot_ids = jnp.arange(slots, dtype=jnp.int32)
     stored = jnp.sum(jnp.where(labels[:, None] == slot_ids[None, :], placement[None, :], 0), axis=1)
-    all_slots = lax.dot_general(
-        tokens, adapters[:, :depth], (((1,), (1,)), ((), ())), preferred_element_type=jnp.float32
-    )
+    all_slots = jnp.zeros((rows, slots * rank), jnp.float32)
+    for p in range(parts):
+        all_slots += lax.dot_general(
+            tokens[:, p * half : (p + 1) * half],
+            down_all[p * slots * rank : (p + 1) * slots * rank],
+            (((1,), (1,)), ((), ())),
+            preferred_element_type=jnp.float32,
+        )
     partial = jnp.zeros((rows, rank), jnp.float32)
     for s in range(slots):
         partial += jnp.where((stored == s)[:, None], all_slots[:, s * rank : (s + 1) * rank], 0.0)
@@ -72,14 +98,10 @@
         [jnp.where((stored == s)[:, None], shrunk, jnp.zeros((), shrunk.dtype)) for s in range(slots)],
         axis=1,
     )
-    expanded = jnp.dot(spread, adapters[:, depth:], preferred_element_type=jnp.float32)
-    total = LOWRANK_SCALE * expanded.astype(jnp.bfloat16).astype(jnp.float32)
-
-    for owner, m, features in local + arrived:
-        part = lax.dynamic_slice_in_dim(
-            frozen_projection_weight, owner * depth + m * step, features.shape[1], axis=0
-        )
-        total += jnp.dot(features, part, preferred_element_type=jnp.float32)
+    expanded = jnp.dot(spread, up, preferred_element_type=jnp.float32)
+    for owner, m, features in arrived:
+        total += jnp.dot(features, weight_rows(owner, m, step), preferred_element_type=jnp.float32)
+    total += LOWRANK_SCALE * expanded.astype(jnp.bfloat16).astype(jnp.float32)
     return total.astype(jnp.bfloat16)
 
 

time: 89.1 us -> 115 us (1.29)
  blocking collectives: 0 us -> 31.1 us
  waiting for transfers between devices: 36.4 us -> 29.2 us
  matrix products: 22.4 us -> 26.7 us
  other arithmetic: 4.06 us -> 0.91 us
    all_gather x0 -> x1, blocking collectives: none -> 31.1 us  [body(): up = lax.all_gather(up_share, ('adapter', 'parts'), axis=0, tiled=True)]
    ppermute x8, waiting for transfers between devices: 34.9 us -> 18.3 us  [the longest x4 18.3 us: body(): far = lax.ppermute(chunks[m], 'tensor', pair_up(count, flip))]
    all_gather x1, waiting for transfers between devices: 0.02 us -> 9.11 us  [body(): lax.all_gather(down_slice, ('parts', 'adapter'), axis=0, tiled=True)]
    dot_general x12 -> x13, matrix products: 22.4 us -> 26.7 us  [the longest x8 14.4 us: body(): jnp.dot(features, weight_rows(owner, m, step), preferred_element_type=jnp...]
  transfers between devices with their start and end apart: 15 -> 15, of which waited for: 7 -> 4; matrix products, arithmetic and copies ran while one was open for 26% -> 25% of each run, Pallas kernels for 0% -> 0%
where the time goes in v2:
time: 115 us
  blocking collectives  31.1 us (27%)
  waiting for transfers between devices  29.2 us (25%)
  matrix products  26.7 us (23%)
  between operations  13.6 us (12%)
  starting transfers between devices  10.1 us (9%)
  local copies, waits for them, and re-layouts  3.25 us (3%)
    all_gather x1, blocking collectives, body(): up = lax.all_gather(up_share, ('adapter', 'parts'), axis=0, tiled=True)  31.1 us
    ppermute x4, waiting for transfers between devices, body(): far = lax.ppermute(chunks[m], 'tensor', pair_up(count, flip))  18.3 us
    dot_general x8, matrix products, body(): jnp.dot(features, weight_rows(owner, m, step), preferred_element_type=jnp...  14.4 us
    all_gather x1, waiting for transfers between devices, body(): lax.all_gather(down_slice, ('parts', 'adapter'), axis=0, tiled=True)  9.11 us
    ppermute x4, starting transfers between devices, body(): far = lax.ppermute(chunks[m], 'tensor', pair_up(count, flip))  5.23 us
    dot_general x1, matrix products, body(): jnp.dot(neighbour, weight_rows(me ^ 1, 0, depth), preferred_element_type=...  4.25 us
    dot_general x1, matrix products, body(): jnp.dot(tokens, weight_rows(me, 0, depth), preferred_element_type=jnp.flo...  4.21 us
    dot_general x2, matrix products, body(): lax.dot_general(tokens[:, p * half:(p + 1) * half], down_all[p * slots *...  3.5 us
  transfers between devices with their start and end apart: 15, of which 4 were waited for; matrix products, arithmetic and copies ran while one was open for 25% of the time, Pallas kernels for 0%

profile of v2, /device:TPU:0, one launch (start us, length us, event | category | flops | bytes accessed | tf_op | source)
XLA Modules:
  0.0 114.8 jit_solution(17794247285427029207)
XLA Ops:
  7.1 1.5 %fusion.56 = (bf16[384,512]{1,0:T(8,128)(2,1)S(1)}, bf16[384,512]{1,0:T(8,128)(2,1)S(1)}, bf16[384,512]{1,0:T(8,128)(2,1)S(1)}, bf16[384,512]{1,0:T(8,128)(2,1)S(1)}) fusion(bf16[384,2048]{1,0:T(8,128)(2,1)} %param.6), kind=kLoop, calls=%fused_computation.91 | loop fusion | bytes 3145728 | tf_op jit(solution)/shard_map/slice | solution.py:47
  8.5 0.8 dynamic-slice_bitcast_fusion
  9.4 2.6 %collective-permute-start.1 = (bf16[384,512]{1,0:T(8,128)(2,1)S(1)}, bf16[384,512]{1,0:T(8,128)(2,1)}, u32[]{:S(2)}, u32[]{:S(2)}) collective-permute-start(bf16[384,512]{1,0:T(8,128)(2,1)S(1)} %get-tuple-element.10), channel_id=1, source_target_pairs={{0,2},{1,3},{2,0},{3,1},{4,6},{5,7},{6,4},{7,5},{8,10},{9,11},{10,... | collective-permute-start | bytes 1179656 | tf_op jit(solution)/shard_map/ppermute | solution.py:70
  12.2 1.9 %collective-permute-start.9 = (bf16[16,1024]{1,0:T(8,128)(2,1)S(1)}, bf16[16,1024]{1,0:T(8,128)(2,1)S(1)}, u32[]{:S(2)}, u32[]{:S(2)}) collective-permute-start(bf16[16,1024]{1,0:T(8,128)(2,1)S(1)} %get-tuple-element.11), channel_id=1, source_target_pairs={{0,3},{1,2},{2,1},{3,0},{4,7},{5,6},{6,5},{7,4},{8,11},{9,10},{10,... | collective-permute-start | bytes 98312 | tf_op jit(solution)/shard_map/ppermute | solution.py:56
  14.1 4.2 %fusion.2 = f32[512,384]{1,0:T(8,128)} fusion(bf16[384,2048]{1,0:T(8,128)(2,1)} %param.6, bf16[8192,512]{1,0:T(8,128)(2,1)} %param.9, s32[]{:T(128)S(6)} %select_n.113), kind=kOutput, calls=%fused_computation.2 | convolution fusion | flops 805306368 | bytes 4456452 | tf_op jit(solution)/shard_map/dot_general | solution.py:79
  18.3 31.1 %all-gather = bf16[1,256,512]{2,1,0:T(8,128)(2,1)S(1)} all-gather(bf16[1,32,512]{2,1,0:T(8,128)(2,1)S(1)} %constant_dynamic-slice_fusion), channel_id=2, replica_groups=mesh['parts'=2,'adapter'=4,'tensor'=4] {'adapter','parts'}, dimensions={1}, use_global_device_ids=true | all-gather | bytes 294912 | tf_op jit(solution)/shard_map/all_gather | solution.py:63
  50.0 1.5 %collective-permute-start.3 = (bf16[384,512]{1,0:T(8,128)(2,1)S(1)}, bf16[384,512]{1,0:T(8,128)(2,1)}, u32[]{:S(2)}, u32[]{:S(2)}) collective-permute-start(bf16[384,512]{1,0:T(8,128)(2,1)S(1)} %get-tuple-element.17), channel_id=1, source_target_pairs={{0,2},{1,3},{2,0},{3,1},{4,6},{5,7},{6,4},{7,5},{8,10},{9,11},{10,... | collective-permute-start | bytes 1179656 | tf_op jit(solution)/shard_map/ppermute | solution.py:70
  53.0 14.1 %collective-permute-done.3 = bf16[384,512]{1,0:T(8,128)(2,1)} collective-permute-done((bf16[384,512]{1,0:T(8,128)(2,1)S(1)}, bf16[384,512]{1,0:T(8,128)(2,1)}, u32[]{:S(2)}, u32[]{:S(2)}) %collective-permute-start.3) | collective-permute-done | bytes 393248 | tf_op jit(solution)/shard_map/ppermute | solution.py:70
  67.1 4.2 %collective-permute-done.7 = bf16[384,512]{1,0:T(8,128)(2,1)} collective-permute-done((bf16[384,512]{1,0:T(8,128)(2,1)S(1)}, bf16[384,512]{1,0:T(8,128)(2,1)}, u32[]{:S(2)}, u32[]{:S(2)}) %collective-permute-start.7) | collective-permute-done | bytes 393248 | tf_op jit(solution)/shard_map/ppermute | solution.py:70
  71.8 1.6 %convolution_bitcast_fusion.3 = f32[384,512]{0,1:T(8,128)S(1)} fusion(bf16[384,512]{1,0:T(8,128)(2,1)} %collective-permute-done.5, bf16[8192,512]{1,0:T(8,128)(2,1)} %param.9, s32[]{:T(128)S(6)} %select_n.123), kind=kOutput, calls=%fused_computation.7 | convolution fusion | flops 201326592 | bytes 1703940 | tf_op jit(solution)/shard_map/dot_general | solution.py:103
  73.5 1.6 %convolution_bitcast_fusion.5 = f32[384,512]{0,1:T(8,128)S(1)} fusion(bf16[384,512]{1,0:T(8,128)(2,1)} %collective-permute-done.3, bf16[8192,512]{1,0:T(8,128)(2,1)} %param.9, s32[]{:T(128)S(6)} %select_n.121), kind=kOutput, calls=%fused_computation.9 | convolution fusion | flops 201326592 | bytes 1703940 | tf_op jit(solution)/shard_map/dot_general | solution.py:103
  75.1 1.6 %convolution_bitcast_fusion.1 = f32[384,512]{0,1:T(8,128)S(1)} fusion(bf16[384,512]{1,0:T(8,128)(2,1)} %collective-permute-done.7, bf16[8192,512]{1,0:T(8,128)(2,1)} %param.9, s32[]{:T(128)S(6)} %select_n.125), kind=kOutput, calls=%fused_computation.5 | convolution fusion | flops 201326592 | bytes 1703940 | tf_op jit(solution)/shard_map/dot_general | solution.py:103
  76.7 2.4 %convolution_bitcast_fusion.4 = f32[384,512]{0,1:T(8,128)} fusion(bf16[384,512]{1,0:T(8,128)(2,1)S(1)} %collective-permute-done.4, bf16[8192,512]{1,0:T(8,128)(2,1)} %param.9, s32[]{:T(128)S(6)} %select_n.122), kind=kOutput, calls=%fused_computation.8 | convolution fusion | flops 201326592 | bytes 1703940 | tf_op jit(solution)/shard_map/dot_general | solution.py:103
  79.2 1.5 %convolution_bitcast_fusion = f32[384,512]{0,1:T(8,128)S(1)} fusion(bf16[384,512]{1,0:T(8,128)(2,1)S(1)} %collective-permute-done.8, bf16[8192,512]{1,0:T(8,128)(2,1)} %param.9, s32[]{:T(128)S(6)} %select_n.126), kind=kOutput, calls=%fused_computation.4 | convolution fusion | flops 201326592 | bytes 1703940 | tf_op jit(solution)/shard_map/dot_general | solution.py:103
  80.7 4.2 %fusion.14 = f32[384,512]{0,1:T(8,128)} fusion(f32[512,384]{1,0:T(8,128)S(1)} %copy-done.3, bf16[384,2048]{1,0:T(8,128)(2,1)} %collective-permute-done, bf16[8192,512]{1,0:T(8,128)(2,1)} %param.9, s32[]{:T(128)S(6)} %select_n.114), kind=kOutput, calls=%fused_computation.20 | convolution fusion | flops 805502976 | bytes 5242884 | tf_op jit(solution)/shard_map/dot_general | solution.py:80
  84.9 9.1 %all-gather.3.cloned.1.call-done = bf16[512,1024]{1,0:T(8,128)(2,1)} async-done(((bf16[64,1024]{1,0:T(8,128)(2,1)}), bf16[512,1024]{1,0:T(8,128)(2,1)}) %all-gather.3.cloned.1.call-update) | async-done | bytes 1048592 | tf_op jit(solution)/shard_map/all_gather | solution.py:64
  94.1 1.7 %fusion.22 = f32[256,384]{1,0:T(8,128)S(1)} fusion(bf16[384,2048]{1,0:T(8,128)(2,1)} %param.6, bf16[512,1024]{1,0:T(8,128)(2,1)} %all-gather.3.cloned.1.call-done), kind=kOutput, calls=%fused_computation.28 | convolution fusion | flops 201326592 | bytes 1703936 | tf_op jit(solution)/shard_map/dot_general | solution.py:87
  95.8 1.8 %fusion.20 = f32[384,256]{0,1:T(8,128)S(1)} fusion(f32[256,384]{1,0:T(8,128)S(1)} %fusion.22, bf16[384,2048]{1,0:T(8,128)(2,1)} %param.6, bf16[512,1024]{1,0:T(8,128)(2,1)} %all-gather.3.cloned.1.call-done), kind=kOutput, calls=%fused_computation.26 | convolution fusion | flops 201424896 | bytes 2097152 | tf_op jit(solution)/shard_map/dot_general | solution.py:87
  97.7 1.9 %convolution_add_fusion.1 = f32[384,512]{0,1:T(8,128)S(1)} fusion(f32[384,512]{0,1:T(8,128)} %fusion.14, bf16[384,512]{1,0:T(8,128)(2,1)} %collective-permute-done.1, bf16[8192,512]{1,0:T(8,128)(2,1)} %param.9, s32[]{:T(128)S(6)} %select_n.119), kind=kOutput, calls=%fused_computation.12 | convolution fusion | flops 201523200 | bytes 2490372 | tf_op jit(solution)/shard_map/dot_general | solution.py:103
  99.7 1.5 %collective-permute-start.13 = (f32[384,64]{0,1:T(8,128)S(1)}, f32[384,64]{0,1:T(8,128)S(1)}, u32[]{:S(2)}, u32[]{:S(2)}) collective-permute-start(f32[384,64]{0,1:T(8,128)S(1)} %fusion.67), channel_id=1, source_target_pairs={{0,2},{1,3},{2,0},{3,1},{4,6},{5,7},{6,4},{7,5},{8,10},{9,11},{10,... | collective-permute-start | bytes 294920 | tf_op jit(solution)/shard_map/ppermute | solution.py:27
  101.2 2.0 %fusion.7 = f32[384,512]{0,1:T(8,128)S(1)} fusion(f32[384,512]{0,1:T(8,128)S(1)} %convolution_bitcast_fusion.3, f32[384,512]{0,1:T(8,128)} %convolution_bitcast_fusion.4, f32[384,512]{0,1:T(8,128)S(1)} %convolution_bitcast_fusion.5, f32[384,512]{0,1:T(8,128)S(1)} %convolution_add_fusion.1, bf16[384,512]{1,0:T(8,128)(2,1)} %collective-permute-done.2, ...), kind=kOutput, calls=%fused_computation.15 | convolution fusion | flops 202113024 | bytes 4849668 | tf_op jit(solution)/shard_map/dot_general | solution.py:103
  103.2 1.7 %collective-permute-done.13 = f32[384,64]{0,1:T(8,128)S(1)} collective-permute-done((f32[384,64]{0,1:T(8,128)S(1)}, f32[384,64]{0,1:T(8,128)S(1)}, u32[]{:S(2)}, u32[]{:S(2)}) %collective-permute-start.13) | collective-permute-done | bytes 98336 | tf_op jit(solution)/shard_map/ppermute | solution.py:27
  105.3 1.7 %fusion.17 = bf16[384,512]{0,1:T(8,128)(2,1)S(1)} fusion(f32[384,512]{0,1:T(8,128)S(1)} %fusion.19, f32[384,512]{0,1:T(8,128)S(1)} %convolution_bitcast_fusion, f32[384,512]{0,1:T(8,128)S(1)} %convolution_bitcast_fusion.1, f32[384,512]{0,1:T(8,128)S(1)} %fusion.7, bf16[384,512]{1,0:T(8,128)(2,1)} %collective-permute-done.6, bf16[8192,512]{1,0:T(8,128)(2,1)} %param.9, ...), kind=kOutput, calls=%fused_computation.21 | convolution fusion | flops 202309632 | bytes 4456452 | tf_op jit(solution)/shard_map/dot_general | solution.py:103
  107.0 0.9 copy.14
  (42 shorter events, 3.9 us)
Async XLA Ops:
  6.5 11.8 %copy-start = (bf16[1,64,512]{2,1,0:T(8,128)(2,1)S(1)}, bf16[1,64,512]{2,1,0:T(8,128)(2,1)}, u32[]{:S(2)}) copy-start(bf16[1,64,512]{2,1,0:T(8,128)(2,1)} %param.11) | copy-start | bytes 196612
  6.5 42.9 %copy-start.1 = (s32[384,1]{0,1:T(1,128)S(1)}, s32[384,1]{0,1:T(1,128)}, u32[]{:S(2)}) copy-start(s32[384,1]{0,1:T(1,128)} %param.7) | copy-start | bytes 4612
  6.5 46.2 %copy-start.2 = (s32[4]{0:T(128)S(1)}, s32[4]{0:T(128)}, u32[]{:S(2)}) copy-start(s32[4]{0:T(128)} %param.8) | copy-start | bytes 52
  6.5 87.5 %all-gather.3.cloned.1.call-start = ((), (), s32[]{:S(2)}) async-start(), calls=%async_computation | async-start | bytes 1179648 | tf_op jit(solution)/shard_map/all_gather | solution.py:64
  6.5 74.1 %collective-permute-start = (bf16[384,2048]{1,0:T(8,128)(2,1)}, bf16[384,2048]{1,0:T(8,128)(2,1)}, u32[]{:S(2)}, u32[]{:S(2)}) collective-permute-start(bf16[384,2048]{1,0:T(8,128)(2,1)} %param.6), channel_id=1, source_target_pairs={{0,1},{1,0},{2,3},{3,2},{4,5},{5,4},{6,7},{7,6},{8,9},{9,8},{10,11... | collective-permute-start | bytes 4718600 | tf_op jit(solution)/shard_map/ppermute | solution.py:67
  9.4 43.5 %collective-permute-start.1 = (bf16[384,512]{1,0:T(8,128)(2,1)S(1)}, bf16[384,512]{1,0:T(8,128)(2,1)}, u32[]{:S(2)}, u32[]{:S(2)}) collective-permute-start(bf16[384,512]{1,0:T(8,128)(2,1)S(1)} %get-tuple-element.10), channel_id=1, source_target_pairs={{0,2},{1,3},{2,0},{3,1},{4,6},{5,7},{6,4},{7,5},{8,10},{9,11},{10,... | collective-permute-start | bytes 1179656 | tf_op jit(solution)/shard_map/ppermute | solution.py:70
  12.0 37.5 %collective-permute-start.10 = (bf16[16,1024]{1,0:T(8,128)(2,1)S(1)}, bf16[16,1024]{1,0:T(8,128)(2,1)S(1)}, u32[]{:S(2)}, u32[]{:S(2)}) collective-permute-start(bf16[16,1024]{1,0:T(8,128)(2,1)S(1)} %get-tuple-element.12), channel_id=1, source_target_pairs={{0,2},{1,3},{2,0},{3,1},{4,6},{5,7},{6,4},{7,5},{8,10},{9,11},{10,... | collective-permute-start | bytes 98312 | tf_op jit(solution)/shard_map/ppermute | solution.py:56
  12.1 38.0 %collective-permute-start.11 = (bf16[16,1024]{1,0:T(8,128)(2,1)S(1)}, bf16[16,1024]{1,0:T(8,128)(2,1)S(1)}, u32[]{:S(2)}, u32[]{:S(2)}) collective-permute-start(bf16[16,1024]{1,0:T(8,128)(2,1)S(1)} %get-tuple-element.13), channel_id=1, source_target_pairs={{0,1},{1,0},{2,3},{3,2},{4,5},{5,4},{6,7},{7,6},{8,9},{9,8},{10,11... | collective-permute-start | bytes 98312 | tf_op jit(solution)/shard_map/ppermute | solution.py:56
  12.2 39.3 %collective-permute-start.9 = (bf16[16,1024]{1,0:T(8,128)(2,1)S(1)}, bf16[16,1024]{1,0:T(8,128)(2,1)S(1)}, u32[]{:S(2)}, u32[]{:S(2)}) collective-permute-start(bf16[16,1024]{1,0:T(8,128)(2,1)S(1)} %get-tuple-element.11), channel_id=1, source_target_pairs={{0,3},{1,2},{2,1},{3,0},{4,7},{5,6},{6,5},{7,4},{8,11},{9,10},{10,... | collective-permute-start | bytes 98312 | tf_op jit(solution)/shard_map/ppermute | solution.py:56
  49.4 21.9 %collective-permute-start.5 = (bf16[384,512]{1,0:T(8,128)(2,1)S(1)}, bf16[384,512]{1,0:T(8,128)(2,1)}, u32[]{:S(2)}, u32[]{:S(2)}) collective-permute-start(bf16[384,512]{1,0:T(8,128)(2,1)S(1)} %get-tuple-element.19), channel_id=1, source_target_pairs={{0,2},{1,3},{2,0},{3,1},{4,6},{5,7},{6,4},{7,5},{8,10},{9,11},{10,... | collective-permute-start | bytes 1179656 | tf_op jit(solution)/shard_map/ppermute | solution.py:70
  50.0 17.1 %collective-permute-start.3 = (bf16[384,512]{1,0:T(8,128)(2,1)S(1)}, bf16[384,512]{1,0:T(8,128)(2,1)}, u32[]{:S(2)}, u32[]{:S(2)}) collective-permute-start(bf16[384,512]{1,0:T(8,128)(2,1)S(1)} %get-tuple-element.17), channel_id=1, source_target_pairs={{0,2},{1,3},{2,0},{3,1},{4,6},{5,7},{6,4},{7,5},{8,10},{9,11},{10,... | collective-permute-start | bytes 1179656 | tf_op jit(solution)/shard_map/ppermute | solution.py:70
  51.5 19.8 %collective-permute-start.7 = (bf16[384,512]{1,0:T(8,128)(2,1)S(1)}, bf16[384,512]{1,0:T(8,128)(2,1)}, u32[]{:S(2)}, u32[]{:S(2)}) collective-permute-start(bf16[384,512]{1,0:T(8,128)(2,1)S(1)} %get-tuple-element.18), channel_id=1, source_target_pairs={{0,2},{1,3},{2,0},{3,1},{4,6},{5,7},{6,4},{7,5},{8,10},{9,11},{10,... | collective-permute-start | bytes 1179656 | tf_op jit(solution)/shard_map/ppermute | solution.py:70
  52.9 27.8 %copy-start.3 = (f32[512,384]{1,0:T(8,128)S(1)}, f32[512,384]{1,0:T(8,128)}, u32[]{:S(2)}) copy-start(f32[512,384]{1,0:T(8,128)} %fusion.2) | copy-start | bytes 2359300
  52.9 48.3 %collective-permute-start.2 = (bf16[384,512]{1,0:T(8,128)(2,1)}, bf16[384,512]{1,0:T(8,128)(2,1)}, u32[]{:S(2)}, u32[]{:S(2)}) collective-permute-start(bf16[384,512]{1,0:T(8,128)(2,1)} %collective-permute-done.1), channel_id=1, source_target_pairs={{0,1},{1,0},{2,3},{3,2},{4,5},{5,4},{6,7},{7,6},{8,9},{9,8},{10,11... | collective-permute-start | bytes 1179656 | tf_op jit(solution)/shard_map/ppermute | solution.py:72
  67.1 9.6 %collective-permute-start.4 = (bf16[384,512]{1,0:T(8,128)(2,1)}, bf16[384,512]{1,0:T(8,128)(2,1)S(1)}, u32[]{:S(2)}, u32[]{:S(2)}) collective-permute-start(bf16[384,512]{1,0:T(8,128)(2,1)} %collective-permute-done.3), channel_id=1, source_target_pairs={{0,1},{1,0},{2,3},{3,2},{4,5},{5,4},{6,7},{7,6},{8,9},{9,8},{10,11... | collective-permute-start | bytes 1179656 | tf_op jit(solution)/shard_map/ppermute | solution.py:72
  71.3 7.9 %collective-permute-start.8 = (bf16[384,512]{1,0:T(8,128)(2,1)}, bf16[384,512]{1,0:T(8,128)(2,1)S(1)}, u32[]{:S(2)}, u32[]{:S(2)}) collective-permute-start(bf16[384,512]{1,0:T(8,128)(2,1)} %collective-permute-done.7), channel_id=1, source_target_pairs={{0,1},{1,0},{2,3},{3,2},{4,5},{5,4},{6,7},{7,6},{8,9},{9,8},{10,11... | collective-permute-start | bytes 1179656 | tf_op jit(solution)/shard_map/ppermute | solution.py:72
  71.3 34.0 %collective-permute-start.6 = (bf16[384,512]{1,0:T(8,128)(2,1)}, bf16[384,512]{1,0:T(8,128)(2,1)}, u32[]{:S(2)}, u32[]{:S(2)}) collective-permute-start(bf16[384,512]{1,0:T(8,128)(2,1)} %collective-permute-done.5), channel_id=1, source_target_pairs={{0,1},{1,0},{2,3},{3,2},{4,5},{5,4},{6,7},{7,6},{8,9},{9,8},{10,11... | collective-permute-start | bytes 1179656 | tf_op jit(solution)/shard_map/ppermute | solution.py:72
  97.6 2.0 %collective-permute-start.12 = (f32[384,64]{0,1:T(8,128)S(1)}, f32[384,64]{0,1:T(8,128)S(1)}, u32[]{:S(2)}, u32[]{:S(2)}) collective-permute-start(f32[384,64]{0,1:T(8,128)S(1)} %fusion.42), channel_id=1, source_target_pairs={{0,1},{1,0},{2,3},{3,2},{4,5},{5,4},{6,7},{7,6},{8,9},{9,8},{10,11... | collective-permute-start | bytes 294920 | tf_op jit(solution)/shard_map/ppermute | solution.py:27
  99.7 5.3 %collective-permute-start.13 = (f32[384,64]{0,1:T(8,128)S(1)}, f32[384,64]{0,1:T(8,128)S(1)}, u32[]{:S(2)}, u32[]{:S(2)}) collective-permute-start(f32[384,64]{0,1:T(8,128)S(1)} %fusion.67), channel_id=1, source_target_pairs={{0,2},{1,3},{2,0},{3,1},{4,6},{5,7},{6,4},{7,5},{8,10},{9,11},{10,... | collective-permute-start | bytes 294920 | tf_op jit(solution)/shard_map/ppermute | solution.py:27
Sparse Core Ops, SparseCore 0:
  52.9 41.1 all-gather.2

commit v3 on v1

v3 whole, which is shorter than its diff:
```python
import jax
import jax.numpy as jnp
from jax import lax
from jax.sharding import PartitionSpec as P

LOWRANK_SCALE = 2.0
CORES = 2
SHARES = (2, 6, 5, 3)


def flipped(value, axis, flip):
    count = lax.axis_size(axis)
    return lax.ppermute(value, axis, [(i, i ^ flip) for i in range(count)])


def by_device(pieces, me):
    bit = 1
    while bit < len(pieces):
        swap = (me & bit) != 0
        pieces = [jnp.where(swap, pieces[j ^ bit], pieces[j]) for j in range(len(pieces))]
        bit *= 2
    return pieces


def chained(*values):
    return lax.optimization_barrier(values)


def body(
    tokens, tenant, placement, frozen_projection_weight, lowrank_down_weight, lowrank_up_weight
):
    rows, depth = tokens.shape
    slots = placement.shape[0]
    tensors = lax.axis_size("tensor")
    groups = lax.axis_size("adapter")
    parts = lax.axis_size("parts")
    me = lax.axis_index("tensor")
    group = lax.axis_index("adapter")
    part = lax.axis_index("parts")
    rank = lowrank_up_weight.shape[1]
    share = depth // parts
    unit = depth // sum(SHARES)
    edges = [unit * sum(SHARES[:m]) for m in range(len(SHARES) + 1)]
    columns = lowrank_up_weight.shape[2]

    down = lowrank_down_weight[0].T
    pieces = [
        lax.dynamic_slice_in_dim(down, (me ^ flip) * depth + part * share, share, axis=1)
        for flip in range(tensors)
    ]
    chunks = [tokens[:, edges[m] : edges[m + 1]] for m in range(len(SHARES))]
    pieces = [pieces[0]] + [flipped(pieces[f], "tensor", f) for f in range(1, tensors)]
    hops = range(CORES, tensors, CORES)
    far = [[flipped(chunk, "tensor", hop) for hop in hops] for chunk in chunks]
    ups = [lowrank_up_weight[0]] + [
        flipped(lowrank_up_weight[0], "adapter", f) for f in range(1, groups)
    ]
    neighbour = flipped(tokens, "tensor", 1)

    def weight_rows(owner, start, width):
        return lax.dynamic_slice_in_dim(
            frozen_projection_weight, owner * depth + start, width, axis=0
        )

    def times_weight(features, owner, start):
        return jnp.dot(
            features,
            weight_rows(owner, start, features.shape[1]),
            preferred_element_type=jnp.float32,
        )

    pieces, far[0] = chained(pieces, far[0])
    own = jnp.concatenate(by_device(pieces, me), axis=0)
    downs = [own] + [flipped(own, "adapter", f) for f in range(1, groups)]
    shares = [[piece] + [flipped(piece, "parts", f) for f in range(1, parts)] for piece in downs]

    total = times_weight(tokens, me, 0)
    total, neighbour = chained(total, neighbour)
    total += times_weight(neighbour, me ^ 1, 0)
    for m in range(len(SHARES) - 1):
        total, far[m] = chained(total, far[m])
        for hop, value in zip(hops, far[m]):
            near = flipped(value, "tensor", 1)
            total += times_weight(value, me ^ hop, edges[m])
            total, near = chained(total, near)
            total += times_weight(near, me ^ hop ^ 1, edges[m])

    labels = tenant[:, 0]
    slot_ids = jnp.arange(slots, dtype=jnp.int32)
    stored = jnp.sum(jnp.where(labels[:, None] == slot_ids[None, :], placement[None, :], 0), axis=1)
    masks = [(stored == (group ^ f))[:, None] for f in range(groups)]
    partial = jnp.zeros((rows, rank), jnp.float32)
    for f in range(groups):
        for p in range(parts):
            mine = lax.dynamic_slice_in_dim(tokens, (part ^ p) * share, share, axis=1)
            partial += jnp.where(
                masks[f],
                lax.dot_general(
                    mine,
                    shares[f][p],
                    (((1,), (1,)), ((), ())),
                    preferred_element_type=jnp.float32,
                ),
                0.0,
            )
    flip = 1
    while flip < tensors:
        partial += flipped(partial, "tensor", flip)
        flip *= 2
    shrunk = partial.astype(jnp.bfloat16)
    spread = jnp.concatenate(
        [jnp.where(mask, shrunk, jnp.zeros((), shrunk.dtype)) for mask in masks], axis=1
    )
    expanded = jnp.dot(
        spread, jnp.concatenate(ups, axis=0), preferred_element_type=jnp.float32
    ).astype(jnp.bfloat16)
    total += LOWRANK_SCALE * expanded.astype(jnp.float32)

    for hop, value in zip(hops, far[-1]):
        near = flipped(value, "tensor", 1)
        total += times_weight(value, me ^ hop, edges[-2])
        total, near = chained(total, near)
        total += times_weight(near, me ^ hop ^ 1, edges[-2])
    return total.astype(jnp.bfloat16)


def solution(mesh):
    placed = (
        P(("parts", "adapter"), "tensor"),
        P(("parts", "adapter"), None),
        P(),
        P(None, "tensor"),
        P("adapter", None, "tensor"),
        P("adapter", None, "tensor"),
    )
    return jax.shard_map(
        body,
        mesh=mesh,
        in_specs=placed,
        out_specs=P(("parts", "adapter"), "tensor"),
        check_vma=False,
    )
```

time: 89.1 us -> 86.4 us (0.970)
  starting transfers between devices: 9.63 us -> 25.8 us
  between operations: 13.6 us -> 0.4 us
  waiting for transfers between devices: 36.4 us -> 26.5 us
  local copies, waits for them, and re-layouts: 2.39 us -> 5.63 us
  matrix products: 22.4 us -> 23.6 us
    ppermute x14 -> x24, starting transfers between devices: 9.63 us -> 25.8 us  [flipped(): return lax.ppermute(value, axis, [(i, i ^ flip) for i in range(count)])]
    ppermute x14 -> x24, waiting for transfers between devices: 36.4 us -> 26.5 us  [flipped(): return lax.ppermute(value, axis, [(i, i ^ flip) for i in range(count)])]
    slice x1 -> x4, local copies, waits for them, and re-layouts: 1.47 us -> 3.24 us  [body(): chunks = [tokens[:, edges[m]:edges[m + 1]] for m in range(len(SHARES))]]
    concatenate x1, other arithmetic: 1.59 us -> 0.01 us  [body(): own = jnp.concatenate(by_device(pieces, me), axis=0)]
    dot_general x12 -> x19, matrix products: 22.4 us -> 23.6 us  [the longest x10 19.5 us: times_weight(): jnp.dot(features, weight_rows(owner, start, features.shape[1]), preferred...]
    add x2 -> x6, other arithmetic: 0.08 us -> 1.08 us  [the longest x1 0.65 us: body(): partial += flipped(partial, 'tensor', flip)]
    convert_element_type x0 -> x1, local copies, waits for them, and re-layouts: none -> 0.94 us  [body(): return total.astype(jnp.bfloat16)]
  transfers between devices with their start and end apart: 15 -> 24, of which waited for: 7 -> 7; matrix products, arithmetic and copies ran while one was open for 26% -> 34% of each run, Pallas kernels for 0% -> 0%
where the time goes in v3:
time: 86.4 us; the launch traced here: 85.7 us
  waiting for transfers between devices  26.5 us (31%)
  starting transfers between devices  25.8 us (30%)
  matrix products  23.6 us (27%)
  local copies, waits for them, and re-layouts  5.63 us (7%)
  other arithmetic  3.77 us (4%)
    ppermute x24, waiting for transfers between devices, flipped(): return lax.ppermute(value, axis, [(i, i ^ flip) for i in range(count)])  26.5 us
    ppermute x24, starting transfers between devices, flipped(): return lax.ppermute(value, axis, [(i, i ^ flip) for i in range(count)])  25.8 us
    dot_general x10, matrix products, times_weight(): jnp.dot(features, weight_rows(owner, start, features.shape[1]), preferred...  19.5 us
    slice x4, local copies, waits for them, and re-layouts, body(): chunks = [tokens[:, edges[m]:edges[m + 1]] for m in range(len(SHARES))]  3.24 us
    dot_general x8, matrix products, body(): lax.dot_general(mine, shares[f][p], (((1,), (1,)), ((), ())), preferred_e...  2.92 us
  transfers between devices with their start and end apart: 24, of which 7 were waited for; matrix products, arithmetic and copies ran while one was open for 34% of the time, Pallas kernels for 0%

profile of v3, /device:TPU:0, one launch (start us, length us, event | category | flops | bytes accessed | tf_op | source)
XLA Modules:
  0.0 85.7 jit_solution(15308902471227100180)
XLA Ops:
  1.9 2.5 %collective-permute-start.2 = (bf16[16,1024]{1,0:T(8,128)(2,1)}, bf16[16,1024]{1,0:T(8,128)(2,1)}, u32[]{:S(2)}, u32[]{:S(2)}) collective-permute-start(bf16[16,1024]{1,0:T(8,128)(2,1)} %get-tuple-element.52), channel_id=1, source_target_pairs={{0,2},{1,3},{2,0},{3,1},{4,6},{5,7},{6,4},{7,5},{8,10},{9,11},{10,... | collective-permute-start | bytes 98312 | tf_op jit(solution)/shard_map/ppermute | solution.py:13
  4.6 1.6 %slice.12 = bf16[384,256]{1,0:T(8,128)(2,1)} slice(bf16[384,2048]{1,0:T(8,128)(2,1)} %param.6), slice={[0:384], [0:256]} | slice | bytes 393216 | tf_op jit(solution)/shard_map/slice | solution.py:51
  6.2 1.9 %collective-permute-start.4 = (bf16[384,256]{1,0:T(8,128)(2,1)}, bf16[384,256]{1,0:T(8,128)(2,1)}, u32[]{:S(2)}, u32[]{:S(2)}) collective-permute-start(bf16[384,256]{1,0:T(8,128)(2,1)} %slice.12), channel_id=1, source_target_pairs={{0,2},{1,3},{2,0},{3,1},{4,6},{5,7},{6,4},{7,5},{8,10},{9,11},{10,... | collective-permute-start | bytes 589832 | tf_op jit(solution)/shard_map/ppermute | solution.py:13
  8.9 3.5 %fusion.4 = f32[384,512]{0,1:T(8,128)S(1)} fusion(bf16[384,2048]{1,0:T(8,128)(2,1)} %param.6, bf16[8192,512]{1,0:T(8,128)(2,1)} %param.9, s32[]{:T(128)S(6)} %select_n.134), kind=kOutput, calls=%fused_computation.4 | convolution fusion | flops 805306368 | bytes 4456452 | tf_op jit(solution)/shard_map/dot_general | solution.py:66
  14.6 1.8 %collective-permute-start.10 = (bf16[64,1024]{1,0:T(8,128)(2,1)S(1)}, bf16[64,1024]{1,0:T(8,128)(2,1)S(1)}, u32[]{:S(2)}, u32[]{:S(2)}) collective-permute-start(bf16[64,1024]{1,0:T(8,128)(2,1)S(1)} %pad_maximum_fusion), channel_id=1, source_target_pairs={{0,16},{16,0},{1,17},{17,1},{2,18},{18,2},{3,19},{19,3},{4,20},{20... | collective-permute-start | bytes 393224 | tf_op jit(solution)/shard_map/ppermute | solution.py:13
  16.4 1.6 %collective-permute-start.11 = (bf16[64,1024]{1,0:T(8,128)(2,1)S(1)}, bf16[64,1024]{1,0:T(8,128)(2,1)S(1)}, u32[]{:S(2)}, u32[]{:S(2)}) collective-permute-start(bf16[64,1024]{1,0:T(8,128)(2,1)S(1)} %pad_maximum_fusion), channel_id=1, source_target_pairs={{0,4},{4,0},{8,12},{12,8},{1,5},{5,1},{9,13},{13,9},{2,6},{6,2},{1... | collective-permute-start | bytes 393224 | tf_op jit(solution)/shard_map/ppermute | solution.py:13
  18.0 2.6 %collective-permute-start.13 = (bf16[64,1024]{1,0:T(8,128)(2,1)S(1)}, bf16[64,1024]{1,0:T(8,128)(2,1)S(1)}, u32[]{:S(2)}, u32[]{:S(2)}) collective-permute-start(bf16[64,1024]{1,0:T(8,128)(2,1)S(1)} %pad_maximum_fusion), channel_id=1, source_target_pairs={{0,8},{4,12},{8,0},{12,4},{1,9},{5,13},{9,1},{13,5},{2,10},{6,14},... | collective-permute-start | bytes 393224 | tf_op jit(solution)/shard_map/ppermute | solution.py:13
  21.0 5.0 %collective-permute-done.13 = bf16[64,1024]{1,0:T(8,128)(2,1)S(1)} collective-permute-done((bf16[64,1024]{1,0:T(8,128)(2,1)S(1)}, bf16[64,1024]{1,0:T(8,128)(2,1)S(1)}, u32[]{:S(2)}, u32[]{:S(2)}) %collective-permute-start.13) | collective-permute-done | bytes 131104 | tf_op jit(solution)/shard_map/ppermute | solution.py:13
  26.0 2.6 %collective-permute-start.15 = (bf16[64,1024]{1,0:T(8,128)(2,1)S(1)}, bf16[64,1024]{1,0:T(8,128)(2,1)S(1)}, u32[]{:S(2)}, u32[]{:S(2)}) collective-permute-start(bf16[64,1024]{1,0:T(8,128)(2,1)S(1)} %pad_maximum_fusion), channel_id=1, source_target_pairs={{0,12},{4,8},{8,4},{12,0},{1,13},{5,9},{9,5},{13,1},{2,14},{6,10},... | collective-permute-start | bytes 393224 | tf_op jit(solution)/shard_map/ppermute | solution.py:13
  29.5 1.5 %collective-permute-start.12 = (bf16[64,1024]{1,0:T(8,128)(2,1)S(1)}, bf16[64,1024]{1,0:T(8,128)(2,1)S(1)}, u32[]{:S(2)}, u32[]{:S(2)}) collective-permute-start(bf16[64,1024]{1,0:T(8,128)(2,1)S(1)} %collective-permute-done.11), channel_id=1, source_target_pairs={{0,16},{16,0},{1,17},{17,1},{2,18},{18,2},{3,19},{19,3},{4,20},{20... | collective-permute-start | bytes 393224 | tf_op jit(solution)/shard_map/ppermute | solution.py:13
  31.0 1.7 %collective-permute-done.15 = bf16[64,1024]{1,0:T(8,128)(2,1)S(1)} collective-permute-done((bf16[64,1024]{1,0:T(8,128)(2,1)S(1)}, bf16[64,1024]{1,0:T(8,128)(2,1)S(1)}, u32[]{:S(2)}, u32[]{:S(2)}) %collective-permute-start.15) | collective-permute-done | bytes 131104 | tf_op jit(solution)/shard_map/ppermute | solution.py:13
  36.1 1.6 %collective-permute-done.16 = bf16[64,1024]{1,0:T(8,128)(2,1)S(1)} collective-permute-done((bf16[64,1024]{1,0:T(8,128)(2,1)S(1)}, bf16[64,1024]{1,0:T(8,128)(2,1)S(1)}, u32[]{:S(2)}, u32[]{:S(2)}) %collective-permute-start.16) | collective-permute-done | bytes 131104 | tf_op jit(solution)/shard_map/ppermute | solution.py:13
  38.2 3.4 %fusion = f32[384,512]{0,1:T(8,128)S(1)} fusion(bf16[384,2048]{1,0:T(8,128)(2,1)} %collective-permute-done, bf16[8192,512]{1,0:T(8,128)(2,1)} %param.9, s32[]{:T(128)S(6)} %select_n.135), kind=kOutput, calls=%fused_computation | convolution fusion | flops 805306368 | bytes 4456452 | tf_op jit(solution)/shard_map/dot_general | solution.py:66
  46.0 1.5 %collective-permute-start.18 = (f32[384,64]{0,1:T(8,128)}, f32[384,64]{0,1:T(8,128)}, u32[]{:S(2)}, u32[]{:S(2)}) collective-permute-start(f32[384,64]{0,1:T(8,128)} %add.189), channel_id=1, source_target_pairs={{0,2},{1,3},{2,0},{3,1},{4,6},{5,7},{6,4},{7,5},{8,10},{9,11},{10,... | collective-permute-start | bytes 294920 | tf_op jit(solution)/shard_map/ppermute | solution.py:13
  47.5 3.1 %collective-permute-start.20 = (bf16[64,512]{1,0:T(8,128)(2,1)}, bf16[64,512]{1,0:T(8,128)(2,1)}, u32[]{:S(2)}, u32[]{:S(2)}) collective-permute-start(bf16[64,512]{1,0:T(8,128)(2,1)} %bitcast.9), channel_id=1, source_target_pairs={{0,8},{4,12},{8,0},{12,4},{1,9},{5,13},{9,1},{13,5},{2,10},{6,14},... | collective-permute-start | bytes 196616 | tf_op jit(solution)/shard_map/ppermute | solution.py:13
  52.7 1.5 %collective-permute-start.22 = (bf16[384,384]{1,0:T(8,128)(2,1)}, bf16[384,384]{1,0:T(8,128)(2,1)S(1)}, u32[]{:S(2)}, u32[]{:S(2)}) collective-permute-start(bf16[384,384]{1,0:T(8,128)(2,1)} %slice.15), channel_id=1, source_target_pairs={{0,2},{1,3},{2,0},{3,1},{4,6},{5,7},{6,4},{7,5},{8,10},{9,11},{10,... | collective-permute-start | bytes 884744 | tf_op jit(solution)/shard_map/ppermute | solution.py:13
  55.2 1.8 %fusion.18 = f32[384,512]{0,1:T(8,128)S(1)} fusion(bf16[384,768]{1,0:T(8,128)(2,1)S(1)} %collective-permute-done.6, bf16[8192,512]{1,0:T(8,128)(2,1)} %param.9, s32[]{:T(128)S(6)} %select_n.142), kind=kOutput, calls=%fused_computation.29 | convolution fusion | flops 301989888 | bytes 2162692 | tf_op jit(solution)/shard_map/dot_general | solution.py:66
  57.0 13.5 %collective-permute-done.22 = bf16[384,384]{1,0:T(8,128)(2,1)S(1)} collective-permute-done((bf16[384,384]{1,0:T(8,128)(2,1)}, bf16[384,384]{1,0:T(8,128)(2,1)S(1)}, u32[]{:S(2)}, u32[]{:S(2)}) %collective-permute-start.22) | collective-permute-done | bytes 294944 | tf_op jit(solution)/shard_map/ppermute | solution.py:13
  71.8 1.7 %fusion.16 = f32[384,512]{0,1:T(8,128)S(1)} fusion(bf16[384,768]{1,0:T(8,128)(2,1)S(1)} %collective-permute-done.7, bf16[8192,512]{1,0:T(8,128)(2,1)} %param.9, s32[]{:T(128)S(6)} %select_n.143), kind=kOutput, calls=%fused_computation.27 | convolution fusion | flops 301989888 | bytes 2162692 | tf_op jit(solution)/shard_map/dot_general | solution.py:66
  74.3 2.5 %collective-permute-done.21 = bf16[64,512]{1,0:T(8,128)(2,1)S(1)} collective-permute-done((bf16[64,512]{1,0:T(8,128)(2,1)}, bf16[64,512]{1,0:T(8,128)(2,1)S(1)}, u32[]{:S(2)}, u32[]{:S(2)}) %collective-permute-start.21) | collective-permute-done | bytes 65568 | tf_op jit(solution)/shard_map/ppermute | solution.py:13
  78.1 1.8 %fusion.22 = f32[384,512]{0,1:T(8,128)S(1)} fusion(bf16[384,640]{1,0:T(8,128)(2,1)} %collective-permute-done.8, bf16[8192,512]{1,0:T(8,128)(2,1)} %param.9, s32[]{:T(128)S(6)} %select_n.144), kind=kOutput, calls=%fused_computation.33 | convolution fusion | flops 251658240 | bytes 1933316 | tf_op jit(solution)/shard_map/dot_general | solution.py:66
  80.0 1.7 %fusion.20 = f32[384,512]{0,1:T(8,128)S(1)} fusion(bf16[384,640]{1,0:T(8,128)(2,1)S(1)} %collective-permute-done.9, bf16[8192,512]{1,0:T(8,128)(2,1)} %param.9, s32[]{:T(128)S(6)} %select_n.145), kind=kOutput, calls=%fused_computation.31 | convolution fusion | flops 251658240 | bytes 1933316 | tf_op jit(solution)/shard_map/dot_general | solution.py:66
  81.7 1.5 %add_add_fusion = f32[384,512]{0,1:T(8,128)S(1)} fusion(f32[384,512]{0,1:T(8,128)S(1)} %fusion.8, f32[384,512]{0,1:T(8,128)S(1)} %add.176, f32[384,512]{0,1:T(8,128)S(1)} %fusion.20, bf16[384,384]{1,0:T(8,128)(2,1)S(1)} %collective-permute-done.22, bf16[8192,512]{1,0:T(8,128)(2,1)} %param.9, s32[]{:T(128)S(6)} %select_n.171), kind=kOutput, calls=%fused_computation.26 | convolution fusion | flops 151584768 | bytes 3833860 | tf_op jit(solution)/shard_map/dot_general | solution.py:66
  83.2 1.5 %fusion.32 = f32[384,512]{0,1:T(8,128)S(1)} fusion(bf16[384,384]{1,0:T(8,128)(2,1)S(1)} %collective-permute-done.23, bf16[8192,512]{1,0:T(8,128)(2,1)} %param.9, s32[]{:T(128)S(6)} %select_n.172), kind=kOutput, calls=%fused_computation.43 | convolution fusion | flops 150994944 | bytes 1474564 | tf_op jit(solution)/shard_map/dot_general | solution.py:66
  (67 shorter events, 22.0 us)
Async XLA Ops:
  1.4 11.1 %collective-permute-start.1 = (bf16[16,1024]{1,0:T(8,128)(2,1)S(1)}, bf16[16,1024]{1,0:T(8,128)(2,1)}, u32[]{:S(2)}, u32[]{:S(2)}) collective-permute-start(bf16[16,1024]{1,0:T(8,128)(2,1)S(1)} %get-tuple-element.50), channel_id=1, source_target_pairs={{0,1},{1,0},{2,3},{3,2},{4,5},{5,4},{6,7},{7,6},{8,9},{9,8},{10,11... | collective-permute-start | bytes 98312 | tf_op jit(solution)/shard_map/ppermute | solution.py:13
  1.9 10.8 %collective-permute-start.2 = (bf16[16,1024]{1,0:T(8,128)(2,1)}, bf16[16,1024]{1,0:T(8,128)(2,1)}, u32[]{:S(2)}, u32[]{:S(2)}) collective-permute-start(bf16[16,1024]{1,0:T(8,128)(2,1)} %get-tuple-element.52), channel_id=1, source_target_pairs={{0,2},{1,3},{2,0},{3,1},{4,6},{5,7},{6,4},{7,5},{8,10},{9,11},{10,... | collective-permute-start | bytes 98312 | tf_op jit(solution)/shard_map/ppermute | solution.py:13
  4.4 8.3 %collective-permute-start.3 = (bf16[16,1024]{1,0:T(8,128)(2,1)}, bf16[16,1024]{1,0:T(8,128)(2,1)}, u32[]{:S(2)}, u32[]{:S(2)}) collective-permute-start(bf16[16,1024]{1,0:T(8,128)(2,1)} %get-tuple-element.49), channel_id=1, source_target_pairs={{0,3},{1,2},{2,1},{3,0},{4,7},{5,6},{6,5},{7,4},{8,11},{9,10},{10,... | collective-permute-start | bytes 98312 | tf_op jit(solution)/shard_map/ppermute | solution.py:13
  4.5 33.7 %collective-permute-start = (bf16[384,2048]{1,0:T(8,128)(2,1)}, bf16[384,2048]{1,0:T(8,128)(2,1)}, u32[]{:S(2)}, u32[]{:S(2)}) collective-permute-start(bf16[384,2048]{1,0:T(8,128)(2,1)} %param.6), channel_id=1, source_target_pairs={{0,1},{1,0},{2,3},{3,2},{4,5},{5,4},{6,7},{7,6},{8,9},{9,8},{10,11... | collective-permute-start | bytes 4718600 | tf_op jit(solution)/shard_map/ppermute | solution.py:13
  6.2 7.6 %collective-permute-start.4 = (bf16[384,256]{1,0:T(8,128)(2,1)}, bf16[384,256]{1,0:T(8,128)(2,1)}, u32[]{:S(2)}, u32[]{:S(2)}) collective-permute-start(bf16[384,256]{1,0:T(8,128)(2,1)} %slice.12), channel_id=1, source_target_pairs={{0,2},{1,3},{2,0},{3,1},{4,6},{5,7},{6,4},{7,5},{8,10},{9,11},{10,... | collective-permute-start | bytes 589832 | tf_op jit(solution)/shard_map/ppermute | solution.py:13
  12.5 32.5 %collective-permute-start.6 = (bf16[384,768]{1,0:T(8,128)(2,1)S(1)}, bf16[384,768]{1,0:T(8,128)(2,1)S(1)}, u32[]{:S(2)}, u32[]{:S(2)}) collective-permute-start(bf16[384,768]{1,0:T(8,128)(2,1)S(1)} %slice.13), channel_id=1, source_target_pairs={{0,2},{1,3},{2,0},{3,1},{4,6},{5,7},{6,4},{7,5},{8,10},{9,11},{10,... | collective-permute-start | bytes 1769480 | tf_op jit(solution)/shard_map/ppermute | solution.py:13
  14.6 14.3 %collective-permute-start.10 = (bf16[64,1024]{1,0:T(8,128)(2,1)S(1)}, bf16[64,1024]{1,0:T(8,128)(2,1)S(1)}, u32[]{:S(2)}, u32[]{:S(2)}) collective-permute-start(bf16[64,1024]{1,0:T(8,128)(2,1)S(1)} %pad_maximum_fusion), channel_id=1, source_target_pairs={{0,16},{16,0},{1,17},{17,1},{2,18},{18,2},{3,19},{19,3},{4,20},{20... | collective-permute-start | bytes 393224 | tf_op jit(solution)/shard_map/ppermute | solution.py:13
  16.4 13.1 %collective-permute-start.11 = (bf16[64,1024]{1,0:T(8,128)(2,1)S(1)}, bf16[64,1024]{1,0:T(8,128)(2,1)S(1)}, u32[]{:S(2)}, u32[]{:S(2)}) collective-permute-start(bf16[64,1024]{1,0:T(8,128)(2,1)S(1)} %pad_maximum_fusion), channel_id=1, source_target_pairs={{0,4},{4,0},{8,12},{12,8},{1,5},{5,1},{9,13},{13,9},{2,6},{6,2},{1... | collective-permute-start | bytes 393224 | tf_op jit(solution)/shard_map/ppermute | solution.py:13
  18.0 8.0 %collective-permute-start.13 = (bf16[64,1024]{1,0:T(8,128)(2,1)S(1)}, bf16[64,1024]{1,0:T(8,128)(2,1)S(1)}, u32[]{:S(2)}, u32[]{:S(2)}) collective-permute-start(bf16[64,1024]{1,0:T(8,128)(2,1)S(1)} %pad_maximum_fusion), channel_id=1, source_target_pairs={{0,8},{4,12},{8,0},{12,4},{1,9},{5,13},{9,1},{13,5},{2,10},{6,14},... | collective-permute-start | bytes 393224 | tf_op jit(solution)/shard_map/ppermute | solution.py:13
  26.0 6.8 %collective-permute-start.15 = (bf16[64,1024]{1,0:T(8,128)(2,1)S(1)}, bf16[64,1024]{1,0:T(8,128)(2,1)S(1)}, u32[]{:S(2)}, u32[]{:S(2)}) collective-permute-start(bf16[64,1024]{1,0:T(8,128)(2,1)S(1)} %pad_maximum_fusion), channel_id=1, source_target_pairs={{0,12},{4,8},{8,4},{12,0},{1,13},{5,9},{9,5},{13,1},{2,14},{6,10},... | collective-permute-start | bytes 393224 | tf_op jit(solution)/shard_map/ppermute | solution.py:13
  28.9 6.8 %collective-permute-start.14 = (bf16[64,1024]{1,0:T(8,128)(2,1)S(1)}, bf16[64,1024]{1,0:T(8,128)(2,1)S(1)}, u32[]{:S(2)}, u32[]{:S(2)}) collective-permute-start(bf16[64,1024]{1,0:T(8,128)(2,1)S(1)} %collective-permute-done.13), channel_id=1, source_target_pairs={{0,16},{16,0},{1,17},{17,1},{2,18},{18,2},{3,19},{19,3},{4,20},{20... | collective-permute-start | bytes 393224 | tf_op jit(solution)/shard_map/ppermute | solution.py:13
  29.5 5.9 %collective-permute-start.12 = (bf16[64,1024]{1,0:T(8,128)(2,1)S(1)}, bf16[64,1024]{1,0:T(8,128)(2,1)S(1)}, u32[]{:S(2)}, u32[]{:S(2)}) collective-permute-start(bf16[64,1024]{1,0:T(8,128)(2,1)S(1)} %collective-permute-done.11), channel_id=1, source_target_pairs={{0,16},{16,0},{1,17},{17,1},{2,18},{18,2},{3,19},{19,3},{4,20},{20... | collective-permute-start | bytes 393224 | tf_op jit(solution)/shard_map/ppermute | solution.py:13
  32.8 5.0 %collective-permute-start.16 = (bf16[64,1024]{1,0:T(8,128)(2,1)S(1)}, bf16[64,1024]{1,0:T(8,128)(2,1)S(1)}, u32[]{:S(2)}, u32[]{:S(2)}) collective-permute-start(bf16[64,1024]{1,0:T(8,128)(2,1)S(1)} %collective-permute-done.15), channel_id=1, source_target_pairs={{0,16},{16,0},{1,17},{17,1},{2,18},{18,2},{3,19},{19,3},{4,20},{20... | collective-permute-start | bytes 393224 | tf_op jit(solution)/shard_map/ppermute | solution.py:13
  38.1 7.2 %collective-permute-start.17 = (f32[384,64]{0,1:T(8,128)S(1)}, f32[384,64]{0,1:T(8,128)S(1)}, u32[]{:S(2)}, u32[]{:S(2)}) collective-permute-start(f32[384,64]{0,1:T(8,128)S(1)} %fusion.9), channel_id=1, source_target_pairs={{0,1},{1,0},{2,3},{3,2},{4,5},{5,4},{6,7},{7,6},{8,9},{9,8},{10,11... | collective-permute-start | bytes 294920 | tf_op jit(solution)/shard_map/ppermute | solution.py:13
  41.7 1.9 %collective-permute-start.5 = (bf16[384,256]{1,0:T(8,128)(2,1)}, bf16[384,256]{1,0:T(8,128)(2,1)S(1)}, u32[]{:S(2)}, u32[]{:S(2)}) collective-permute-start(bf16[384,256]{1,0:T(8,128)(2,1)} %collective-permute-done.4), channel_id=1, source_target_pairs={{0,1},{1,0},{2,3},{3,2},{4,5},{5,4},{6,7},{7,6},{8,9},{9,8},{10,11... | collective-permute-start | bytes 589832 | tf_op jit(solution)/shard_map/ppermute | solution.py:13
  45.0 26.8 %collective-permute-start.7 = (bf16[384,768]{1,0:T(8,128)(2,1)S(1)}, bf16[384,768]{1,0:T(8,128)(2,1)S(1)}, u32[]{:S(2)}, u32[]{:S(2)}) collective-permute-start(bf16[384,768]{1,0:T(8,128)(2,1)S(1)} %collective-permute-done.6), channel_id=1, source_target_pairs={{0,1},{1,0},{2,3},{3,2},{4,5},{5,4},{6,7},{7,6},{8,9},{9,8},{10,11... | collective-permute-start | bytes 1769480 | tf_op jit(solution)/shard_map/ppermute | solution.py:13
  46.0 6.7 %collective-permute-start.18 = (f32[384,64]{0,1:T(8,128)}, f32[384,64]{0,1:T(8,128)}, u32[]{:S(2)}, u32[]{:S(2)}) collective-permute-start(f32[384,64]{0,1:T(8,128)} %add.189), channel_id=1, source_target_pairs={{0,2},{1,3},{2,0},{3,1},{4,6},{5,7},{6,4},{7,5},{8,10},{9,11},{10,... | collective-permute-start | bytes 294920 | tf_op jit(solution)/shard_map/ppermute | solution.py:13
  47.5 26.8 %collective-permute-start.19 = (bf16[64,512]{1,0:T(8,128)(2,1)}, bf16[64,512]{1,0:T(8,128)(2,1)}, u32[]{:S(2)}, u32[]{:S(2)}) collective-permute-start(bf16[64,512]{1,0:T(8,128)(2,1)} %bitcast.9), channel_id=1, source_target_pairs={{0,4},{4,0},{8,12},{12,8},{1,5},{5,1},{9,13},{13,9},{2,6},{6,2},{1... | collective-permute-start | bytes 196616 | tf_op jit(solution)/shard_map/ppermute | solution.py:13
  47.5 26.8 %collective-permute-start.20 = (bf16[64,512]{1,0:T(8,128)(2,1)}, bf16[64,512]{1,0:T(8,128)(2,1)}, u32[]{:S(2)}, u32[]{:S(2)}) collective-permute-start(bf16[64,512]{1,0:T(8,128)(2,1)} %bitcast.9), channel_id=1, source_target_pairs={{0,8},{4,12},{8,0},{12,4},{1,9},{5,13},{9,1},{13,5},{2,10},{6,14},... | collective-permute-start | bytes 196616 | tf_op jit(solution)/shard_map/ppermute | solution.py:13
  51.4 22.2 %collective-permute-start.8 = (bf16[384,640]{1,0:T(8,128)(2,1)}, bf16[384,640]{1,0:T(8,128)(2,1)}, u32[]{:S(2)}, u32[]{:S(2)}) collective-permute-start(bf16[384,640]{1,0:T(8,128)(2,1)} %slice.14), channel_id=1, source_target_pairs={{0,2},{1,3},{2,0},{3,1},{4,6},{5,7},{6,4},{7,5},{8,10},{9,11},{10,... | collective-permute-start | bytes 1474568 | tf_op jit(solution)/shard_map/ppermute | solution.py:13
  52.7 17.8 %collective-permute-start.22 = (bf16[384,384]{1,0:T(8,128)(2,1)}, bf16[384,384]{1,0:T(8,128)(2,1)S(1)}, u32[]{:S(2)}, u32[]{:S(2)}) collective-permute-start(bf16[384,384]{1,0:T(8,128)(2,1)} %slice.15), channel_id=1, source_target_pairs={{0,2},{1,3},{2,0},{3,1},{4,6},{5,7},{6,4},{7,5},{8,10},{9,11},{10,... | collective-permute-start | bytes 884744 | tf_op jit(solution)/shard_map/ppermute | solution.py:13
  70.5 6.3 %collective-permute-start.21 = (bf16[64,512]{1,0:T(8,128)(2,1)}, bf16[64,512]{1,0:T(8,128)(2,1)S(1)}, u32[]{:S(2)}, u32[]{:S(2)}) collective-permute-start(bf16[64,512]{1,0:T(8,128)(2,1)} %bitcast.9), channel_id=1, source_target_pairs={{0,12},{4,8},{8,4},{12,0},{1,13},{5,9},{9,5},{13,1},{2,14},{6,10},... | collective-permute-start | bytes 196616 | tf_op jit(solution)/shard_map/ppermute | solution.py:13
  71.8 11.4 %collective-permute-start.23 = (bf16[384,384]{1,0:T(8,128)(2,1)S(1)}, bf16[384,384]{1,0:T(8,128)(2,1)S(1)}, u32[]{:S(2)}, u32[]{:S(2)}) collective-permute-start(bf16[384,384]{1,0:T(8,128)(2,1)S(1)} %collective-permute-done.22), channel_id=1, source_target_pairs={{0,1},{1,0},{2,3},{3,2},{4,5},{5,4},{6,7},{7,6},{8,9},{9,8},{10,11... | collective-permute-start | bytes 884744 | tf_op jit(solution)/shard_map/ppermute | solution.py:13
  73.7 6.3 %collective-permute-start.9 = (bf16[384,640]{1,0:T(8,128)(2,1)}, bf16[384,640]{1,0:T(8,128)(2,1)S(1)}, u32[]{:S(2)}, u32[]{:S(2)}) collective-permute-start(bf16[384,640]{1,0:T(8,128)(2,1)} %collective-permute-done.8), channel_id=1, source_target_pairs={{0,1},{1,0},{2,3},{3,2},{4,5},{5,4},{6,7},{7,6},{8,9},{9,8},{10,11... | collective-permute-start | bytes 1474568 | tf_op jit(solution)/shard_map/ppermute | solution.py:13
  (2 other events, 7.1 us)

commit v4 on v1

v4 whole, which is shorter than its diff:
```python
import functools

import jax
import jax.numpy as jnp
from jax import lax
from jax.experimental import pallas as pl
from jax.experimental.pallas import tpu as pltpu
from jax.sharding import PartitionSpec as P

LOWRANK_SCALE = 2.0
CORES = 2
LANES = 128
CUTS = (0.1875, 0.75)
VMEM_BYTES = 24 * 1024 * 1024
FREE = pl.CostEstimate(flops=0, bytes_accessed=0, transcendentals=0)
LONG = pl.CostEstimate(flops=10**10, bytes_accessed=0, transcendentals=0)
ANYWHERE = pl.BlockSpec(memory_space=pl.ANY)
IN_HBM = pl.BlockSpec(memory_space=pltpu.HBM)
VECTOR = pl.BlockSpec(memory_space=pltpu.VMEM)
SCALAR = pl.BlockSpec(memory_space=pltpu.SMEM)


def flipped(value, axis, flip):
    count = lax.axis_size(axis)
    return lax.ppermute(value, axis, [(i, i ^ flip) for i in range(count)])


def chained(*values):
    return lax.optimization_barrier(values)


def tile_of(width):
    return max(t for t in range(1, width + 1) if width % t == 0 and (t == width or t % LANES == 0) and t <= 768)


def call(kernel, out_shape, in_specs, scratch, out_specs=VECTOR, cost=FREE):
    return pl.pallas_call(
        kernel,
        out_shape=out_shape,
        in_specs=in_specs,
        out_specs=out_specs,
        scratch_shapes=scratch,
        cost_estimate=cost,
        compiler_params=pltpu.CompilerParams(vmem_limit_bytes=VMEM_BYTES),
    )


def row_masks(tenant, placement_ref, slots, wanted):
    stored = jnp.zeros(tenant.shape, jnp.int32)
    for slot in range(slots):
        stored = jnp.where(tenant == slot, placement_ref[slot], stored)
    return [stored == slot for slot in wanted]


def add_products(starts_ref, features, weight_ref, held_ref, sems, total_ref, begun=False):
    copies, base = [], 0
    for i, part in enumerate(features):
        width = part.shape[1]
        start = pl.multiple_of(starts_ref[i], LANES)
        copies.append(
            pltpu.make_async_copy(
                weight_ref.at[pl.ds(start, width)], held_ref.at[pl.ds(base, width)], sems.at[i]
            )
        )
        copies[-1].start()
        base += width

    def finish():
        base = 0
        for i, part in enumerate(features):
            width = part.shape[1]
            tile = tile_of(width)
            copies[i].wait()
            for k in range(0, width, tile):
                total_ref[...] += jnp.dot(
                    part[:, k : k + tile],
                    held_ref[base + k : base + k + tile],
                    preferred_element_type=jnp.float32,
                )
            base += width

    return finish


def products_kernel(count, has_total, starts_ref, weight_ref, *refs):
    features = refs[:count]
    given = refs[count] if has_total else None
    out_ref, held_ref, sems = refs[count + has_total :]
    finish = add_products(starts_ref, features, weight_ref, held_ref, sems, out_ref)
    out_ref[...] = given[...] if has_total else jnp.zeros_like(out_ref)
    finish()


def products(starts, features, weight, total=None, cost=FREE):
    rows, columns = features[0].shape[0], weight.shape[1]
    count = len(features)
    given = [] if total is None else [total]
    return call(
        functools.partial(products_kernel, count, len(given)),
        jax.ShapeDtypeStruct((rows, columns), jnp.float32),
        [SCALAR, IN_HBM] + [VECTOR] * (count + len(given)),
        [
            pltpu.VMEM((sum(f.shape[1] for f in features), columns), weight.dtype),
            pltpu.SemaphoreType.DMA((count,)),
        ],
        cost=cost,
    )(jnp.stack(starts), weight, *features, *given)


def last_kernel(count, offsets, slots, starts_ref, ids_ref, placement_ref, weight_ref, *refs):
    features = refs[:count]
    given, tenant_ref, sum_ref, more_ref, ups_ref = refs[count : count + 5]
    out_ref, held_ref, total_ref, sems = refs[count + 5 :]
    finish = add_products(starts_ref, features, weight_ref, held_ref, sems, total_ref)
    shrunk = (sum_ref[...] + more_ref[...]).astype(jnp.bfloat16)
    masks = row_masks(
        tenant_ref[...], placement_ref, slots, [ids_ref[0] ^ offset for offset in offsets]
    )
    spread = jnp.concatenate(
        [jnp.where(mask, shrunk, jnp.zeros((), shrunk.dtype)) for mask in masks], axis=1
    )
    expanded = jnp.dot(spread, ups_ref[...], preferred_element_type=jnp.float32)
    expanded = expanded.astype(jnp.bfloat16).astype(jnp.float32)
    total_ref[...] = given[...] + LOWRANK_SCALE * expanded
    finish()
    out_ref[...] = total_ref[...].astype(out_ref.dtype)


def shrink_kernel(offsets, slots, rank, shares, ids_ref, placement_ref, tokens_ref, tenant_ref, *refs):
    downs, out_ref = refs[:-1], refs[-1]
    share = downs[0].shape[1]
    masks = row_masks(
        tenant_ref[...], placement_ref, slots, [ids_ref[0] ^ offset for offset in offsets]
    )
    total = jnp.zeros(out_ref.shape, jnp.float32)
    per_share = len(downs) // shares
    for p in range(shares):
        start = pl.multiple_of((ids_ref[1] ^ p) * share, LANES)
        own = tokens_ref[:, pl.ds(start, share)]
        slot = 0
        for down in downs[p * per_share : (p + 1) * per_share]:
            sums = lax.dot_general(
                own, down[...], (((1,), (1,)), ((), ())), preferred_element_type=jnp.float32
            )
            for b in range(down.shape[0] // rank):
                total += jnp.where(masks[slot], sums[:, b * rank : (b + 1) * rank], 0.0)
                slot += 1
    out_ref[...] = total


def order_kernel(rank_part, ids_ref, *refs):
    pieces, out_ref, sems = refs[:-2], refs[-2], refs[-1]
    copies = [
        pltpu.make_async_copy(
            piece,
            out_ref.at[pl.ds(pl.multiple_of((ids_ref[2] ^ flip) * rank_part, rank_part), rank_part)],
            sems.at[flip],
        )
        for flip, piece in enumerate(pieces)
    ]
    for copy in copies:
        copy.start()
    for copy in copies:
        copy.wait()


def body(
    tokens, tenant, placement, frozen_projection_weight, lowrank_down_weight, lowrank_up_weight
):
    rows, depth = tokens.shape
    slots = placement.shape[0]
    tensors = lax.axis_size("tensor")
    groups = lax.axis_size("adapter")
    parts = lax.axis_size("parts")
    me = lax.axis_index("tensor")
    part = lax.axis_index("parts")
    ids = jnp.stack([lax.axis_index("adapter"), part, me])
    rank, columns = lowrank_up_weight.shape[1:]
    share = depth // parts
    edges = [0] + [int(depth * cut) // LANES * LANES for cut in CUTS] + [depth]

    down = lowrank_down_weight[0].T
    pieces = [
        lax.dynamic_slice_in_dim(down, (me ^ flip) * depth + part * share, share, axis=1)
        for flip in range(tensors)
    ]
    chunks = [tokens[:, a:b] for a, b in zip(edges, edges[1:])]
    pieces = [pieces[0]] + [flipped(pieces[f], "tensor", f) for f in range(1, tensors)]
    hops = range(CORES, tensors, CORES)
    neighbour = flipped(tokens, "tensor", 1)
    if lowrank_down_weight.shape[2] % 16 == 0:
        own = call(
            functools.partial(order_kernel, lowrank_down_weight.shape[2]),
            jax.ShapeDtypeStruct((rank, share), down.dtype),
            [SCALAR] + [ANYWHERE] * tensors,
            [pltpu.SemaphoreType.DMA((tensors,))],
            ANYWHERE,
        )(ids, *pieces)
    else:
        own = jnp.concatenate(
            [
                sum(jnp.where((me ^ f) == j, pieces[f], jnp.zeros((), down.dtype)) for f in range(tensors))
                for j in range(tensors)
            ],
            axis=0,
        )

    def send(m):
        return [flipped(chunks[m], "tensor", hop) for hop in hops]

    def spread_out(m, far):
        starts, features = [], []
        for hop, value in zip(hops, far):
            features += [value, flipped(value, "tensor", 1)]
            starts += [(me ^ hop) * depth + edges[m], (me ^ hop ^ 1) * depth + edges[m]]
        return starts, features

    first = send(0)
    own, chunks[1], chunks[2] = chained(own, chunks[1], chunks[2])
    second, third = send(1), send(2)
    total = products([me * depth, (me ^ 1) * depth], [tokens, neighbour], frozen_projection_weight)
    first, total = chained(first, total)

    offsets, held = [0], own
    mask = groups - 1
    while mask:
        arriving = flipped(held, "adapter", mask)
        if mask == groups - 1:
            arriving, total, up = chained(arriving, total, lowrank_up_weight[0])
        offsets = offsets + [offset ^ mask for offset in offsets]
        mask //= 2
        if mask:
            held = jnp.concatenate([held, arriving], axis=0)
    starts, features = spread_out(0, first)
    downs = [held, arriving]
    downs = downs + [flipped(value, "parts", p) for p in range(1, parts) for value in downs]
    ups = [up] + [flipped(up, "adapter", offset) for offset in offsets[1:]]
    ups, downs = chained(ups, downs)
    ups = jnp.concatenate(ups, axis=0)

    partial = call(
        functools.partial(shrink_kernel, offsets, slots, rank, parts),
        jax.ShapeDtypeStruct((rows, rank), jnp.float32),
        [SCALAR, SCALAR] + [VECTOR] * (2 + len(downs)),
        [],
    )(ids, placement, tokens, tenant, *downs)
    second, partial = chained(second, partial)
    more_starts, more_features = spread_out(1, second)
    flip = 1
    while flip < tensors // 2:
        partial += flipped(partial, "tensor", flip)
        flip *= 2
    more_features, partial = chained(more_features, partial)
    more = flipped(partial, "tensor", flip)
    total = products(
        starts + more_starts, features + more_features, frozen_projection_weight, total, LONG
    )
    third, total = chained(third, total)
    starts, features = spread_out(2, third)

    return call(
        functools.partial(last_kernel, len(features), offsets, slots),
        jax.ShapeDtypeStruct((rows, columns), jnp.bfloat16),
        [SCALAR, SCALAR, SCALAR, IN_HBM] + [VECTOR] * (len(features) + 5),
        [
            pltpu.VMEM((sum(f.shape[1] for f in features), columns), jnp.bfloat16),
            pltpu.VMEM((rows, columns), jnp.float32),
            pltpu.SemaphoreType.DMA((len(features),)),
        ],
    )(
        jnp.stack(starts), ids, placement, frozen_projection_weight, *features, total, tenant,
        partial, more, ups,
    )


def solution(mesh):
    placed = (
        P(("parts", "adapter"), "tensor"),
        P(("parts", "adapter"), None),
        P(),
        P(None, "tensor"),
        P("adapter", None, "tensor"),
        P("adapter", None, "tensor"),
    )
    return jax.shard_map(
        body,
        mesh=mesh,
        in_specs=placed,
        out_specs=P(("parts", "adapter"), "tensor"),
        check_vma=False,
    )
```

time: 89.1 us -> 72.2 us (0.81)
  matrix products: 22.4 us -> 0 us
  local copies, waits for them, and re-layouts: 2.39 us -> 16.7 us
  between operations: 13.6 us -> 0.18 us
  Pallas kernels: 0 us -> 12.6 us
  waiting for transfers between devices: 36.4 us -> 25.8 us
  starting transfers between devices: 9.63 us -> 16.2 us
  other arithmetic: 4.06 us -> 0.34 us
    dot_general x12 -> x0, matrix products: 22.4 us -> none  [the longest x10 18.6 us: body(): total += jnp.dot(features, part, preferred_element_type=jnp.float32)]
    pallas_call x0 -> x5, Pallas kernels: none -> 12.6 us  [the longest x2 7.18 us: products(): call(functools.partial(products_kernel, count, len(given)), jax.ShapeDtyp...]
    unnamed x2 -> x28, local copies, waits for them, and re-layouts: 0.01 us -> 11.2 us
    ppermute x14 -> x19, waiting for transfers between devices: 36.4 us -> 25.8 us  [flipped(): return lax.ppermute(value, axis, [(i, i ^ flip) for i in range(count)])]
    ppermute x14 -> x19, starting transfers between devices: 9.63 us -> 16.2 us  [flipped(): return lax.ppermute(value, axis, [(i, i ^ flip) for i in range(count)])]
    slice x1 -> x3, local copies, waits for them, and re-layouts: 1.47 us -> 4.63 us  [body(): chunks = [tokens[:, a:b] for a, b in zip(edges, edges[1:])]]
    concatenate x1, other arithmetic: 1.59 us -> 0.02 us  [body(): ups = jnp.concatenate(ups, axis=0)]
    select_n x3 -> x0, other arithmetic: 0.94 us -> none  [the longest x1 0.9 us: in_order(): jnp.where(swap, pieces[j ^ bit], pieces[j])]
  transfers between devices with their start and end apart: 15 -> 19, of which waited for: 7 -> 7; matrix products, arithmetic and copies ran while one was open for 26% -> 8% of each run, Pallas kernels for 0% -> 14%
where the time goes in v4:
time: 72.2 us; the launch traced here: 71.8 us
  waiting for transfers between devices  25.8 us (36%)
  local copies, waits for them, and re-layouts  16.7 us (23%)
  starting transfers between devices  16.2 us (22%)
  Pallas kernels  12.6 us (17%)
    ppermute x19, waiting for transfers between devices, flipped(): return lax.ppermute(value, axis, [(i, i ^ flip) for i in range(count)])  25.8 us
    ppermute x19, starting transfers between devices, flipped(): return lax.ppermute(value, axis, [(i, i ^ flip) for i in range(count)])  16.2 us
    unnamed x28, local copies, waits for them, and re-layouts  11.2 us
    pallas_call x2, Pallas kernels, products(): call(functools.partial(products_kernel, count, len(given)), jax.ShapeDtyp...  7.18 us
    slice x3, local copies, waits for them, and re-layouts, body(): chunks = [tokens[:, a:b] for a, b in zip(edges, edges[1:])]  4.63 us
    pallas_call x1, Pallas kernels, body(): call(functools.partial(last_kernel, len(features), offsets, slots), jax.S...  2.58 us
    pallas_call x1, Pallas kernels, body(): call(functools.partial(shrink_kernel, offsets, slots, rank, parts), jax.S...  2.11 us
  transfers between devices with their start and end apart: 19, of which 7 were waited for; matrix products, arithmetic and copies ran while one was open for 8% of the time, Pallas kernels for 14%

profile of v4, /device:TPU:0, one launch (start us, length us, event | category | flops | bytes accessed | tf_op | source)
XLA Modules:
  0.0 71.8 jit_solution(8080173086216296272)
XLA Ops:
  0.5 0.8 %dynamic-slice_bitcast_fusion = (bf16[16,1024]{1,0:T(8,128)(2,1)S(1)}, bf16[16,1024]{1,0:T(8,128)(2,1)S(1)}, bf16[16,1024]{1,0:T(8,128)(2,1)S(1)}, bf16[16,1024]{1,0:T(8,128)(2,1)S(1)}) fusion(bf16[1,8192,16]{1,2,0:T(8,128)(2,1)} %param.10, s32[]{:T(128)S(6)} %select_n.15, s32[]{:T(128)S(6)} %select_n.13, s32[]{:T(128)S(6)} %select_n.12, s32[]{:T(128)S(6)} %select_n.14), kind=kLoop, calls=%fused_computation.1 | loop fusion | bytes 262160 | tf_op jit(solution)/shard_map/dynamic_slice | solution.py:184
  1.5 2.8 %collective-permute-start.1 = (bf16[16,1024]{1,0:T(8,128)(2,1)S(1)}, bf16[16,1024]{1,0:T(8,128)(2,1)S(1)}, u32[]{:S(2)}, u32[]{:S(2)}) collective-permute-start(bf16[16,1024]{1,0:T(8,128)(2,1)S(1)} %get-tuple-element.54), channel_id=1, source_target_pairs={{0,2},{1,3},{2,0},{3,1},{4,6},{5,7},{6,4},{7,5},{8,10},{9,11},{10,... | collective-permute-start | bytes 98312 | tf_op jit(solution)/shard_map/ppermute | solution.py:25
  4.3 1.7 %slice.11 = bf16[384,384]{1,0:T(8,128)(2,1)} slice(bf16[384,2048]{1,0:T(8,128)(2,1)} %tokens_ref.1), slice={[0:384], [0:384]} | slice | bytes 589824 | tf_op jit(solution)/shard_map/slice | solution.py:187
  6.0 1.5 %collective-permute-start.4 = (bf16[384,384]{1,0:T(8,128)(2,1)}, bf16[384,384]{1,0:T(8,128)(2,1)}, u32[]{:S(2)}, u32[]{:S(2)}) collective-permute-start(bf16[384,384]{1,0:T(8,128)(2,1)} %slice.11), channel_id=1, source_target_pairs={{0,2},{1,3},{2,0},{3,1},{4,6},{5,7},{6,4},{7,5},{8,10},{9,11},{10,... | collective-permute-start | bytes 884744 | tf_op jit(solution)/shard_map/ppermute | solution.py:25
  7.6 2.2 %slice.9 = bf16[384,1152]{1,0:T(8,128)(2,1)} slice(bf16[384,2048]{1,0:T(8,128)(2,1)} %tokens_ref.1), slice={[0:384], [384:1536]} | slice | bytes 1769472 | tf_op jit(solution)/shard_map/slice | solution.py:187
  11.9 3.6 %collective-permute-start.8 = (bf16[64,1024]{1,0:T(8,128)(2,1)S(1)}, bf16[64,1024]{1,0:T(8,128)(2,1)S(1)}, u32[]{:S(2)}, u32[]{:S(2)}) collective-permute-start(bf16[64,1024]{1,0:T(8,128)(2,1)S(1)} %shard_map.64), channel_id=1, source_target_pairs={{0,12},{4,8},{8,4},{12,0},{1,13},{5,9},{9,5},{13,1},{2,14},{6,10},... | collective-permute-start | bytes 393224 | tf_op jit(solution)/shard_map/ppermute | solution.py:25
  15.7 3.4 %copy-done = bf16[8192,512]{1,0:T(8,128)(2,1)S(1)} copy-done((bf16[8192,512]{1,0:T(8,128)(2,1)S(1)}, bf16[8192,512]{1,0:T(8,128)(2,1)}, u32[]{:S(2)}) %copy-start) | copy-done | bytes 8388632
  19.0 2.8 %shard_map.65.refs_4_ = f32[384,512]{1,0:T(8,128)S(1)} custom-call(s32[2]{0:T(128)S(1)} %pad_add_fusion.3.starts_ref, bf16[8192,512]{1,0:T(8,128)(2,1)S(1)} %copy-done, bf16[384,2048]{1,0:T(8,128)(2,1)S(1)} %copy-done.3, bf16[384,2048]{1,0:T(8,128)(2,1)S(1)} %collective-permute-done.5.refs_1_), custom_call_target="tpu_custom_call" | custom-call | tf_op jit(solution)/shard_map/pallas_call | solution.py:98
  21.8 0.9 %copy-done.4 = f32[384,512]{1,0:T(8,128)} copy-done((f32[384,512]{1,0:T(8,128)}, f32[384,512]{1,0:T(8,128)S(1)}, u32[]{:S(2)}) %copy-start.4) | copy-done | bytes 786456
  22.8 1.6 %collective-permute-start.13 = (bf16[128,1024]{1,0:T(8,128)(2,1)S(1)}, bf16[128,1024]{1,0:T(8,128)(2,1)}, u32[]{:S(2)}, u32[]{:S(2)}) collective-permute-start(bf16[128,1024]{1,0:T(8,128)(2,1)S(1)} %constant_dynamic-update-slice_fusion.refs_0_), channel_id=1, source_target_pairs={{0,16},{16,0},{1,17},{17,1},{2,18},{18,2},{3,19},{19,3},{4,20},{20... | collective-permute-start | bytes 786440 | tf_op jit(solution)/shard_map/ppermute | solution.py:25
  24.4 6.4 %collective-permute-done.12.refs_1_ = bf16[128,1024]{1,0:T(8,128)(2,1)S(1)} collective-permute-done((bf16[128,1024]{1,0:T(8,128)(2,1)S(1)}, bf16[128,1024]{1,0:T(8,128)(2,1)S(1)}, u32[]{:S(2)}, u32[]{:S(2)}) %collective-permute-start.12) | collective-permute-done | bytes 262176 | tf_op jit(solution)/shard_map/ppermute | solution.py:25
  30.8 1.5 %collective-permute-start.14 = (bf16[128,1024]{1,0:T(8,128)(2,1)S(1)}, bf16[128,1024]{1,0:T(8,128)(2,1)}, u32[]{:S(2)}, u32[]{:S(2)}) collective-permute-start(bf16[128,1024]{1,0:T(8,128)(2,1)S(1)} %collective-permute-done.12.refs_1_), channel_id=1, source_target_pairs={{0,16},{16,0},{1,17},{17,1},{2,18},{18,2},{3,19},{19,3},{4,20},{20... | collective-permute-start | bytes 786440 | tf_op jit(solution)/shard_map/ppermute | solution.py:25
  32.6 6.1 %collective-permute-done.9 = bf16[64,512]{1,0:T(8,128)(2,1)S(1)} collective-permute-done((bf16[64,512]{1,0:T(8,128)(2,1)S(1)}, bf16[64,512]{1,0:T(8,128)(2,1)S(1)}, u32[]{:S(2)}, u32[]{:S(2)}) %collective-permute-start.9) | collective-permute-done | bytes 65568 | tf_op jit(solution)/shard_map/ppermute | solution.py:25
  38.9 5.0 %collective-permute-done.11 = bf16[64,512]{1,0:T(8,128)(2,1)S(1)} collective-permute-done((bf16[64,512]{1,0:T(8,128)(2,1)S(1)}, bf16[64,512]{1,0:T(8,128)(2,1)S(1)}, u32[]{:S(2)}, u32[]{:S(2)}) %collective-permute-start.11) | collective-permute-done | bytes 65568 | tf_op jit(solution)/shard_map/ppermute | solution.py:25
  43.9 2.1 %shard_map.66 = f32[384,64]{1,0:T(8,128)S(1)} custom-call(s32[3]{0:T(128)S(1)} %pad_add_fusion.1.ids_ref, s32[4]{0:T(128)S(1)} %copy-done.6, bf16[384,2048]{1,0:T(8,128)(2,1)S(1)} %copy-done.3, s32[384,1]{1,0:T(8,128)S(1)} %copy.7.tenant_ref.refs_3_, bf16[128,1024]{1,0:T(8,128)(2,1)S(1)} %constant_dynamic-update-slice_fusion.refs_0_, ...), custom_call_target="tpu_custom_call" | custom-call | tf_op jit(solution)/shard_map/pallas_call | solution.py:241
  46.8 1.4 %collective-permute-start.3 = (bf16[384,512]{1,0:T(8,128)(2,1)}, bf16[384,512]{1,0:T(8,128)(2,1)S(1)}, u32[]{:S(2)}, u32[]{:S(2)}) collective-permute-start(bf16[384,512]{1,0:T(8,128)(2,1)} %slice.10), channel_id=1, source_target_pairs={{0,2},{1,3},{2,0},{3,1},{4,6},{5,7},{6,4},{7,5},{8,10},{9,11},{10,... | collective-permute-start | bytes 1179656 | tf_op jit(solution)/shard_map/ppermute | solution.py:25
  48.2 1.0 %collective-permute-done.16 = f32[384,64]{1,0:T(8,128)S(1)} collective-permute-done((f32[384,64]{1,0:T(8,128)S(1)}, f32[384,64]{1,0:T(8,128)S(1)}, u32[]{:S(2)}, u32[]{:S(2)}) %collective-permute-start.16) | collective-permute-done | bytes 98336 | tf_op jit(solution)/shard_map/ppermute | solution.py:25
  49.3 3.4 %copy-done.1 = bf16[8192,512]{1,0:T(8,128)(2,1)S(1)} copy-done((bf16[8192,512]{1,0:T(8,128)(2,1)S(1)}, bf16[8192,512]{1,0:T(8,128)(2,1)}, u32[]{:S(2)}) %copy-start.1) | copy-done | bytes 8388632
  52.7 4.4 %shard_map.67.refs_2_ = f32[384,512]{1,0:T(8,128)S(1)} custom-call(s32[4]{0:T(128)S(1)} %pad_add_fusion.2.starts_ref, bf16[8192,512]{1,0:T(8,128)(2,1)S(1)} %copy-done.1, bf16[384,384]{1,0:T(8,128)(2,1)} %collective-permute-done.4.refs_0_, bf16[384,384]{1,0:T(8,128)(2,1)S(1)} %collective-permute-done.6.refs_1_, ...), custom_call_target="tpu_custom_call" | custom-call | flops 10000000000 | tf_op jit(solution)/shard_map/pallas_call | solution.py:98
  57.2 1.3 %collective-permute-done.3.refs_0_ = bf16[384,512]{1,0:T(8,128)(2,1)S(1)} collective-permute-done((bf16[384,512]{1,0:T(8,128)(2,1)}, bf16[384,512]{1,0:T(8,128)(2,1)S(1)}, u32[]{:S(2)}, u32[]{:S(2)}) %collective-permute-start.3) | collective-permute-done | bytes 393248 | tf_op jit(solution)/shard_map/ppermute | solution.py:25
  58.5 1.4 %collective-permute-start.18 = (f32[384,64]{1,0:T(8,128)S(1)}, f32[384,64]{1,0:T(8,128)S(1)}, u32[]{:S(2)}, u32[]{:S(2)}) collective-permute-start(f32[384,64]{1,0:T(8,128)S(1)} %add.51.refs_4_), channel_id=1, source_target_pairs={{0,2},{1,3},{2,0},{3,1},{4,6},{5,7},{6,4},{7,5},{8,10},{9,11},{10,... | collective-permute-start | bytes 294920 | tf_op jit(solution)/shard_map/ppermute | solution.py:25
  60.0 5.9 %collective-permute-done.18.refs_5_ = f32[384,64]{1,0:T(8,128)S(1)} collective-permute-done((f32[384,64]{1,0:T(8,128)S(1)}, f32[384,64]{1,0:T(8,128)S(1)}, u32[]{:S(2)}, u32[]{:S(2)}) %collective-permute-start.18) | collective-permute-done | bytes 98336 | tf_op jit(solution)/shard_map/ppermute | solution.py:25
  65.9 3.4 %copy-done.2 = bf16[8192,512]{1,0:T(8,128)(2,1)S(1)} copy-done((bf16[8192,512]{1,0:T(8,128)(2,1)S(1)}, bf16[8192,512]{1,0:T(8,128)(2,1)}, u32[]{:S(2)}) %copy-start.2) | copy-done | bytes 8388632
  69.2 2.6 %shard_map.68 = bf16[384,512]{1,0:T(8,128)(2,1)} custom-call(s32[2]{0:T(128)S(1)} %pad_add_fusion.starts_ref, s32[3]{0:T(128)S(1)} %pad_add_fusion.1.ids_ref, s32[4]{0:T(128)S(1)} %copy-done.6, bf16[8192,512]{1,0:T(8,128)(2,1)S(1)} %copy-done.2, bf16[384,512]{1,0:T(8,128)(2,1)S(1)} %collective-permute-done.3.refs_0_, ...), custom_call_target="tpu_custom_call" | custom-call | tf_op jit(solution)/shard_map/pallas_call | solution.py:261
  (58 shorter events, 4.5 us)
Async XLA Ops:
  0.0 15.6 %collective-permute-start.5 = (bf16[384,2048]{1,0:T(8,128)(2,1)}, bf16[384,2048]{1,0:T(8,128)(2,1)S(1)}, u32[]{:S(2)}, u32[]{:S(2)}) collective-permute-start(bf16[384,2048]{1,0:T(8,128)(2,1)} %tokens_ref.1), channel_id=1, source_target_pairs={{0,1},{1,0},{2,3},{3,2},{4,5},{5,4},{6,7},{7,6},{8,9},{9,8},{10,11... | collective-permute-start | bytes 4718600 | tf_op jit(solution)/shard_map/ppermute | solution.py:25
  1.3 9.2 %collective-permute-start = (bf16[16,1024]{1,0:T(8,128)(2,1)S(1)}, bf16[16,1024]{1,0:T(8,128)(2,1)S(1)}, u32[]{:S(2)}, u32[]{:S(2)}) collective-permute-start(bf16[16,1024]{1,0:T(8,128)(2,1)S(1)} %get-tuple-element.52), channel_id=1, source_target_pairs={{0,1},{1,0},{2,3},{3,2},{4,5},{5,4},{6,7},{7,6},{8,9},{9,8},{10,11... | collective-permute-start | bytes 98312 | tf_op jit(solution)/shard_map/ppermute | solution.py:25
  1.5 9.0 %collective-permute-start.1 = (bf16[16,1024]{1,0:T(8,128)(2,1)S(1)}, bf16[16,1024]{1,0:T(8,128)(2,1)S(1)}, u32[]{:S(2)}, u32[]{:S(2)}) collective-permute-start(bf16[16,1024]{1,0:T(8,128)(2,1)S(1)} %get-tuple-element.54), channel_id=1, source_target_pairs={{0,2},{1,3},{2,0},{3,1},{4,6},{5,7},{6,4},{7,5},{8,10},{9,11},{10,... | collective-permute-start | bytes 98312 | tf_op jit(solution)/shard_map/ppermute | solution.py:25
  4.3 6.2 %collective-permute-start.2 = (bf16[16,1024]{1,0:T(8,128)(2,1)S(1)}, bf16[16,1024]{1,0:T(8,128)(2,1)S(1)}, u32[]{:S(2)}, u32[]{:S(2)}) collective-permute-start(bf16[16,1024]{1,0:T(8,128)(2,1)S(1)} %get-tuple-element.51), channel_id=1, source_target_pairs={{0,3},{1,2},{2,1},{3,0},{4,7},{5,6},{6,5},{7,4},{8,11},{9,10},{10,... | collective-permute-start | bytes 98312 | tf_op jit(solution)/shard_map/ppermute | solution.py:25
  6.0 16.7 %collective-permute-start.4 = (bf16[384,384]{1,0:T(8,128)(2,1)}, bf16[384,384]{1,0:T(8,128)(2,1)}, u32[]{:S(2)}, u32[]{:S(2)}) collective-permute-start(bf16[384,384]{1,0:T(8,128)(2,1)} %slice.11), channel_id=1, source_target_pairs={{0,2},{1,3},{2,0},{3,1},{4,6},{5,7},{6,4},{7,5},{8,10},{9,11},{10,... | collective-permute-start | bytes 884744 | tf_op jit(solution)/shard_map/ppermute | solution.py:25
  11.3 34.7 %collective-permute-start.7 = (bf16[384,1152]{1,0:T(8,128)(2,1)}, bf16[384,1152]{1,0:T(8,128)(2,1)}, u32[]{:S(2)}, u32[]{:S(2)}) collective-permute-start(bf16[384,1152]{1,0:T(8,128)(2,1)} %slice.9), channel_id=1, source_target_pairs={{0,2},{1,3},{2,0},{3,1},{4,6},{5,7},{6,4},{7,5},{8,10},{9,11},{10,... | collective-permute-start | bytes 2654216 | tf_op jit(solution)/shard_map/ppermute | solution.py:25
  11.9 10.8 %collective-permute-start.8 = (bf16[64,1024]{1,0:T(8,128)(2,1)S(1)}, bf16[64,1024]{1,0:T(8,128)(2,1)S(1)}, u32[]{:S(2)}, u32[]{:S(2)}) collective-permute-start(bf16[64,1024]{1,0:T(8,128)(2,1)S(1)} %shard_map.64), channel_id=1, source_target_pairs={{0,12},{4,8},{8,4},{12,0},{1,13},{5,9},{9,5},{13,1},{2,14},{6,10},... | collective-permute-start | bytes 393224 | tf_op jit(solution)/shard_map/ppermute | solution.py:25
  19.0 13.3 %copy-start.7 = (bf16[1,64,512]{2,1,0:T(8,128)(2,1)S(1)}, bf16[1,64,512]{2,1,0:T(8,128)(2,1)}, u32[]{:S(2)}) copy-start(bf16[1,64,512]{2,1,0:T(8,128)(2,1)} %param.11) | copy-start | bytes 196612
  19.0 19.7 %copy-start.12 = (s32[384,1]{0,1:T(1,128)S(1)}, s32[384,1]{0,1:T(1,128)}, u32[]{:S(2)}) copy-start(s32[384,1]{0,1:T(1,128)} %param.7) | copy-start | bytes 4612
  19.0 24.9 %copy-start.6 = (s32[4]{0:T(128)S(1)}, s32[4]{0:T(128)}, u32[]{:S(2)}) copy-start(s32[4]{0:T(128)} %placement_ref.3) | copy-start | bytes 52
  22.7 8.1 %collective-permute-start.12 = (bf16[128,1024]{1,0:T(8,128)(2,1)S(1)}, bf16[128,1024]{1,0:T(8,128)(2,1)S(1)}, u32[]{:S(2)}, u32[]{:S(2)}) collective-permute-start(bf16[128,1024]{1,0:T(8,128)(2,1)S(1)} %constant_dynamic-update-slice_fusion.refs_0_), channel_id=1, source_target_pairs={{0,4},{4,0},{8,12},{12,8},{1,5},{5,1},{9,13},{13,9},{2,6},{6,2},{1... | collective-permute-start | bytes 786440 | tf_op jit(solution)/shard_map/ppermute | solution.py:25
  22.8 21.1 %collective-permute-start.13 = (bf16[128,1024]{1,0:T(8,128)(2,1)S(1)}, bf16[128,1024]{1,0:T(8,128)(2,1)}, u32[]{:S(2)}, u32[]{:S(2)}) collective-permute-start(bf16[128,1024]{1,0:T(8,128)(2,1)S(1)} %constant_dynamic-update-slice_fusion.refs_0_), channel_id=1, source_target_pairs={{0,16},{16,0},{1,17},{17,1},{2,18},{18,2},{3,19},{19,3},{4,20},{20... | collective-permute-start | bytes 786440 | tf_op jit(solution)/shard_map/ppermute | solution.py:25
  30.8 13.1 %collective-permute-start.14 = (bf16[128,1024]{1,0:T(8,128)(2,1)S(1)}, bf16[128,1024]{1,0:T(8,128)(2,1)}, u32[]{:S(2)}, u32[]{:S(2)}) collective-permute-start(bf16[128,1024]{1,0:T(8,128)(2,1)S(1)} %collective-permute-done.12.refs_1_), channel_id=1, source_target_pairs={{0,16},{16,0},{1,17},{17,1},{2,18},{18,2},{3,19},{19,3},{4,20},{20... | collective-permute-start | bytes 786440 | tf_op jit(solution)/shard_map/ppermute | solution.py:25
  32.3 6.4 %collective-permute-start.9 = (bf16[64,512]{1,0:T(8,128)(2,1)S(1)}, bf16[64,512]{1,0:T(8,128)(2,1)S(1)}, u32[]{:S(2)}, u32[]{:S(2)}) collective-permute-start(bf16[64,512]{1,0:T(8,128)(2,1)S(1)} %bitcast.28), channel_id=1, source_target_pairs={{0,12},{4,8},{8,4},{12,0},{1,13},{5,9},{9,5},{13,1},{2,14},{6,10},... | collective-permute-start | bytes 196616 | tf_op jit(solution)/shard_map/ppermute | solution.py:25
  32.6 6.3 %collective-permute-start.10 = (bf16[64,512]{1,0:T(8,128)(2,1)S(1)}, bf16[64,512]{1,0:T(8,128)(2,1)S(1)}, u32[]{:S(2)}, u32[]{:S(2)}) collective-permute-start(bf16[64,512]{1,0:T(8,128)(2,1)S(1)} %bitcast.29), channel_id=1, source_target_pairs={{0,4},{4,0},{8,12},{12,8},{1,5},{5,1},{9,13},{13,9},{2,6},{6,2},{1... | collective-permute-start | bytes 196616 | tf_op jit(solution)/shard_map/ppermute | solution.py:25
  38.7 5.2 %collective-permute-start.11 = (bf16[64,512]{1,0:T(8,128)(2,1)S(1)}, bf16[64,512]{1,0:T(8,128)(2,1)S(1)}, u32[]{:S(2)}, u32[]{:S(2)}) collective-permute-start(bf16[64,512]{1,0:T(8,128)(2,1)S(1)} %bitcast.30), channel_id=1, source_target_pairs={{0,8},{4,12},{8,0},{12,4},{1,9},{5,13},{9,1},{13,5},{2,10},{6,14},... | collective-permute-start | bytes 196616 | tf_op jit(solution)/shard_map/ppermute | solution.py:25
  46.0 3.3 %collective-permute-start.15 = (bf16[384,1152]{1,0:T(8,128)(2,1)}, bf16[384,1152]{1,0:T(8,128)(2,1)}, u32[]{:S(2)}, u32[]{:S(2)}) collective-permute-start(bf16[384,1152]{1,0:T(8,128)(2,1)} %collective-permute-done.7.refs_2_), channel_id=1, source_target_pairs={{0,1},{1,0},{2,3},{3,2},{4,5},{5,4},{6,7},{7,6},{8,9},{9,8},{10,11... | collective-permute-start | bytes 2654216 | tf_op jit(solution)/shard_map/ppermute | solution.py:25
  46.1 3.2 %collective-permute-start.6 = (bf16[384,384]{1,0:T(8,128)(2,1)}, bf16[384,384]{1,0:T(8,128)(2,1)S(1)}, u32[]{:S(2)}, u32[]{:S(2)}) collective-permute-start(bf16[384,384]{1,0:T(8,128)(2,1)} %collective-permute-done.4.refs_0_), channel_id=1, source_target_pairs={{0,1},{1,0},{2,3},{3,2},{4,5},{5,4},{6,7},{7,6},{8,9},{9,8},{10,11... | collective-permute-start | bytes 884744 | tf_op jit(solution)/shard_map/ppermute | solution.py:25
  46.6 2.6 %collective-permute-start.16 = (f32[384,64]{1,0:T(8,128)S(1)}, f32[384,64]{1,0:T(8,128)S(1)}, u32[]{:S(2)}, u32[]{:S(2)}) collective-permute-start(f32[384,64]{1,0:T(8,128)S(1)} %shard_map.66), channel_id=1, source_target_pairs={{0,1},{1,0},{2,3},{3,2},{4,5},{5,4},{6,7},{7,6},{8,9},{9,8},{10,11... | collective-permute-start | bytes 294920 | tf_op jit(solution)/shard_map/ppermute | solution.py:25
  46.8 11.7 %collective-permute-start.3 = (bf16[384,512]{1,0:T(8,128)(2,1)}, bf16[384,512]{1,0:T(8,128)(2,1)S(1)}, u32[]{:S(2)}, u32[]{:S(2)}) collective-permute-start(bf16[384,512]{1,0:T(8,128)(2,1)} %slice.10), channel_id=1, source_target_pairs={{0,2},{1,3},{2,0},{3,1},{4,6},{5,7},{6,4},{7,5},{8,10},{9,11},{10,... | collective-permute-start | bytes 1179656 | tf_op jit(solution)/shard_map/ppermute | solution.py:25
  49.2 10.7 %copy-start.9 = (bf16[64,512]{1,0:T(8,128)(2,1)S(1)}, bf16[64,512]{1,0:T(8,128)(2,1)}, u32[]{:S(2)}) copy-start(bf16[64,512]{1,0:T(8,128)(2,1)} %copy-done.8) | copy-start | bytes 196612
  49.2 10.7 %copy-start.11 = (bf16[64,512]{1,0:T(8,128)(2,1)S(1)}, bf16[64,512]{1,0:T(8,128)(2,1)}, u32[]{:S(2)}) copy-start(bf16[64,512]{1,0:T(8,128)(2,1)} %copy-done.10) | copy-start | bytes 196612
  58.5 7.4 %collective-permute-start.17 = (bf16[384,512]{1,0:T(8,128)(2,1)S(1)}, bf16[384,512]{1,0:T(8,128)(2,1)S(1)}, u32[]{:S(2)}, u32[]{:S(2)}) collective-permute-start(bf16[384,512]{1,0:T(8,128)(2,1)S(1)} %collective-permute-done.3.refs_0_), channel_id=1, source_target_pairs={{0,1},{1,0},{2,3},{3,2},{4,5},{5,4},{6,7},{7,6},{8,9},{9,8},{10,11... | collective-permute-start | bytes 1179656 | tf_op jit(solution)/shard_map/ppermute | solution.py:25
  58.5 7.3 %collective-permute-start.18 = (f32[384,64]{1,0:T(8,128)S(1)}, f32[384,64]{1,0:T(8,128)S(1)}, u32[]{:S(2)}, u32[]{:S(2)}) collective-permute-start(f32[384,64]{1,0:T(8,128)S(1)} %add.51.refs_4_), channel_id=1, source_target_pairs={{0,2},{1,3},{2,0},{3,1},{4,6},{5,7},{6,4},{7,5},{8,10},{9,11},{10,... | collective-permute-start | bytes 294920 | tf_op jit(solution)/shard_map/ppermute | solution.py:25
  (8 other events, 41.9 us)

commit v5 on v4

--- a/solution.py
+++ b/solution.py
@@ -11,7 +11,7 @@
 CORES = 2
 LANES = 128
 CUTS = (0.1875, 0.75)
-VMEM_BYTES = 24 * 1024 * 1024
+VMEM_BYTES = 48 * 1024 * 1024
 FREE = pl.CostEstimate(flops=0, bytes_accessed=0, transcendentals=0)
 LONG = pl.CostEstimate(flops=10**10, bytes_accessed=0, transcendentals=0)
 ANYWHERE = pl.BlockSpec(memory_space=pl.ANY)
@@ -45,7 +45,7 @@
     )
 
 
-def row_masks(tenant, placement_ref, slots, wanted):
+def slot_masks(tenant, placement_ref, slots, wanted):
     stored = jnp.zeros(tenant.shape, jnp.int32)
     for slot in range(slots):
         stored = jnp.where(tenant == slot, placement_ref[slot], stored)
@@ -109,17 +109,18 @@
 
 def last_kernel(count, offsets, slots, starts_ref, ids_ref, placement_ref, weight_ref, *refs):
     features = refs[:count]
-    given, tenant_ref, sum_ref, more_ref, ups_ref = refs[count : count + 5]
-    out_ref, held_ref, total_ref, sems = refs[count + 5 :]
+    given, tenant_ref, sum_ref, more_ref = refs[count : count + 4]
+    ups = refs[count + 4 : count + 4 + len(offsets)]
+    out_ref, held_ref, total_ref, sems = refs[count + 4 + len(offsets) :]
     finish = add_products(starts_ref, features, weight_ref, held_ref, sems, total_ref)
-    shrunk = (sum_ref[...] + more_ref[...]).astype(jnp.bfloat16)
-    masks = row_masks(
+    shrunk = (sum_ref[...] + more_ref[...]).astype(jnp.bfloat16).astype(jnp.float32)
+    masks = slot_masks(
         tenant_ref[...], placement_ref, slots, [ids_ref[0] ^ offset for offset in offsets]
     )
-    spread = jnp.concatenate(
-        [jnp.where(mask, shrunk, jnp.zeros((), shrunk.dtype)) for mask in masks], axis=1
-    )
-    expanded = jnp.dot(spread, ups_ref[...], preferred_element_type=jnp.float32)
+    spread = jnp.concatenate([jnp.where(mask, shrunk, 0.0) for mask in masks], axis=0)
+    spread = spread.T.astype(jnp.bfloat16)
+    stacked = jnp.concatenate([up[...] for up in ups], axis=0)
+    expanded = jnp.dot(spread, stacked, preferred_element_type=jnp.float32)
     expanded = expanded.astype(jnp.bfloat16).astype(jnp.float32)
     total_ref[...] = given[...] + LOWRANK_SCALE * expanded
     finish()
@@ -129,7 +130,7 @@
 def shrink_kernel(offsets, slots, rank, shares, ids_ref, placement_ref, tokens_ref, tenant_ref, *refs):
     downs, out_ref = refs[:-1], refs[-1]
     share = downs[0].shape[1]
-    masks = row_masks(
+    masks = slot_masks(
         tenant_ref[...], placement_ref, slots, [ids_ref[0] ^ offset for offset in offsets]
     )
     total = jnp.zeros(out_ref.shape, jnp.float32)
@@ -140,12 +141,32 @@
         slot = 0
         for down in downs[p * per_share : (p + 1) * per_share]:
             sums = lax.dot_general(
-                own, down[...], (((1,), (1,)), ((), ())), preferred_element_type=jnp.float32
+                down[...], own, (((1,), (1,)), ((), ())), preferred_element_type=jnp.float32
             )
             for b in range(down.shape[0] // rank):
-                total += jnp.where(masks[slot], sums[:, b * rank : (b + 1) * rank], 0.0)
+                total += jnp.where(masks[slot], sums[b * rank : (b + 1) * rank], 0.0)
                 slot += 1
     out_ref[...] = total
+
+
+def cut_kernel(edges, share, ids_ref, tokens_ref, down_ref, *refs):
+    outs, sems = refs[:-1], refs[-1]
+    depth = tokens_ref.shape[1]
+    chunks, pieces = outs[: len(edges) - 1], outs[len(edges) - 1 :]
+    copies = []
+    for flip, piece in enumerate(pieces):
+        start = pl.multiple_of((ids_ref[2] ^ flip) * depth + ids_ref[1] * share, LANES)
+        copies.append((down_ref.at[:, pl.ds(start, share)], piece))
+    for a, b, chunk in zip(edges, edges[1:], chunks):
+        copies.append((tokens_ref.at[:, a:b], chunk))
+    copies = [
+        pltpu.make_async_copy(source, target, sems.at[i])
+        for i, (source, target) in enumerate(copies)
+    ]
+    for copy in copies:
+        copy.start()
+    for copy in copies:
+        copy.wait()
 
 
 def order_kernel(rank_part, ids_ref, *refs):
@@ -177,18 +198,31 @@
     ids = jnp.stack([lax.axis_index("adapter"), part, me])
     rank, columns = lowrank_up_weight.shape[1:]
     share = depth // parts
+    tenant_row = tenant.reshape(1, rows)
     edges = [0] + [int(depth * cut) // LANES * LANES for cut in CUTS] + [depth]
 
     down = lowrank_down_weight[0].T
-    pieces = [
-        lax.dynamic_slice_in_dim(down, (me ^ flip) * depth + part * share, share, axis=1)
-        for flip in range(tensors)
-    ]
-    chunks = [tokens[:, a:b] for a, b in zip(edges, edges[1:])]
+    whole_tiles = down.shape[0] % 16 == 0
+    if whole_tiles:
+        cut = call(
+            functools.partial(cut_kernel, edges, share),
+            [jax.ShapeDtypeStruct((rows, b - a), tokens.dtype) for a, b in zip(edges, edges[1:])]
+            + [jax.ShapeDtypeStruct((down.shape[0], share), down.dtype)] * tensors,
+            [SCALAR, ANYWHERE, ANYWHERE],
+            [pltpu.SemaphoreType.DMA((len(edges) - 1 + tensors,))],
+            [ANYWHERE] * (len(edges) - 1 + tensors),
+        )(ids, tokens, down)
+        chunks, pieces = list(cut[: len(edges) - 1]), list(cut[len(edges) - 1 :])
+    else:
+        chunks = [tokens[:, a:b] for a, b in zip(edges, edges[1:])]
+        pieces = [
+            lax.dynamic_slice_in_dim(down, (me ^ flip) * depth + part * share, share, axis=1)
+            for flip in range(tensors)
+        ]
     pieces = [pieces[0]] + [flipped(pieces[f], "tensor", f) for f in range(1, tensors)]
     hops = range(CORES, tensors, CORES)
     neighbour = flipped(tokens, "tensor", 1)
-    if lowrank_down_weight.shape[2] % 16 == 0:
+    if whole_tiles:
         own = call(
             functools.partial(order_kernel, lowrank_down_weight.shape[2]),
             jax.ShapeDtypeStruct((rank, share), down.dtype),
@@ -215,61 +249,59 @@
             starts += [(me ^ hop) * depth + edges[m], (me ^ hop ^ 1) * depth + edges[m]]
         return starts, features
 
-    first = send(0)
-    own, chunks[1], chunks[2] = chained(own, chunks[1], chunks[2])
-    second, third = send(1), send(2)
-    total = products([me * depth, (me ^ 1) * depth], [tokens, neighbour], frozen_projection_weight)
-    first, total = chained(first, total)
-
-    offsets, held = [0], own
-    mask = groups - 1
-    while mask:
-        arriving = flipped(held, "adapter", mask)
-        if mask == groups - 1:
-            arriving, total, up = chained(arriving, total, lowrank_up_weight[0])
-        offsets = offsets + [offset ^ mask for offset in offsets]
-        mask //= 2
-        if mask:
-            held = jnp.concatenate([held, arriving], axis=0)
-    starts, features = spread_out(0, first)
-    downs = [held, arriving]
-    downs = downs + [flipped(value, "parts", p) for p in range(1, parts) for value in downs]
+    far = [send(m) for m in range(len(chunks))]
+
+    offsets = list(range(groups))
+    up = lowrank_up_weight[0]
     ups = [up] + [flipped(up, "adapter", offset) for offset in offsets[1:]]
-    ups, downs = chained(ups, downs)
-    ups = jnp.concatenate(ups, axis=0)
+    arriving = [own] + [flipped(own, "adapter", offset) for offset in offsets[1:]]
+    own, neighbour, ups = chained(own, neighbour, ups)
+    total = products(
+        [me * depth, (me ^ 1) * depth], [tokens, neighbour], frozen_projection_weight, cost=LONG
+    )
+    for offset in offsets[1:]:
+        arriving[offset], total = chained(arriving[offset], total)
+    exchanged = [
+        [flipped(value, "parts", p) for value in arriving] for p in range(1, parts)
+    ]
+    starts, features = spread_out(0, far[0])
+    total = products(starts, features, frozen_projection_weight, total, LONG)
+    exchanged, total = chained(exchanged, total)
+    downs = arriving + [value for values in exchanged for value in values]
+    far[1], downs = chained(far[1], downs)
 
     partial = call(
         functools.partial(shrink_kernel, offsets, slots, rank, parts),
-        jax.ShapeDtypeStruct((rows, rank), jnp.float32),
+        jax.ShapeDtypeStruct((rank, rows), jnp.float32),
         [SCALAR, SCALAR] + [VECTOR] * (2 + len(downs)),
         [],
-    )(ids, placement, tokens, tenant, *downs)
-    second, partial = chained(second, partial)
-    more_starts, more_features = spread_out(1, second)
+        cost=LONG,
+    )(ids, placement, tokens, tenant_row, *downs)
+    starts, features = spread_out(1, far[1])
+    total = products(starts, features, frozen_projection_weight, total, LONG)
     flip = 1
     while flip < tensors // 2:
-        partial += flipped(partial, "tensor", flip)
+        received = flipped(partial, "tensor", flip)
+        if flip == 1:
+            received, total = chained(received, total)
+        partial += received
         flip *= 2
-    more_features, partial = chained(more_features, partial)
     more = flipped(partial, "tensor", flip)
-    total = products(
-        starts + more_starts, features + more_features, frozen_projection_weight, total, LONG
-    )
-    third, total = chained(third, total)
-    starts, features = spread_out(2, third)
+    far[2], total, partial = chained(far[2], total, partial)
+    starts, features = spread_out(2, far[2])
 
     return call(
         functools.partial(last_kernel, len(features), offsets, slots),
         jax.ShapeDtypeStruct((rows, columns), jnp.bfloat16),
-        [SCALAR, SCALAR, SCALAR, IN_HBM] + [VECTOR] * (len(features) + 5),
+        [SCALAR, SCALAR, SCALAR, IN_HBM] + [VECTOR] * (len(features) + 4 + groups),
         [
             pltpu.VMEM((sum(f.shape[1] for f in features), columns), jnp.bfloat16),
             pltpu.VMEM((rows, columns), jnp.float32),
             pltpu.SemaphoreType.DMA((len(features),)),
         ],
     )(
-        jnp.stack(starts), ids, placement, frozen_projection_weight, *features, total, tenant,
-        partial, more, ups,
+        jnp.stack(starts), ids, placement, frozen_projection_weight, *features, total, tenant_row,
+        partial, more, *ups,
     )
 
 

time: 72.2 us -> 57.9 us (0.80)
  local copies, waits for them, and re-layouts: 16.7 us -> 2.38 us
  waiting for transfers between devices: 25.8 us -> 12.6 us
  starting transfers between devices: 16.2 us -> 23.6 us
  Pallas kernels: 12.6 us -> 18.5 us
    ppermute x19 -> x22, waiting for transfers between devices: 25.8 us -> 12.6 us  [flipped(): return lax.ppermute(value, axis, [(i, i ^ flip) for i in range(count)])]
    unnamed x28 -> x12, local copies, waits for them, and re-layouts: 11.2 us -> 2.38 us
    ppermute x19 -> x22, starting transfers between devices: 16.2 us -> 23.6 us  [flipped(): return lax.ppermute(value, axis, [(i, i ^ flip) for i in range(count)])]
    slice x3 -> x0, local copies, waits for them, and re-layouts: 4.63 us -> none  [body(): chunks = [tokens[:, a:b] for a, b in zip(edges, edges[1:])]]
    pallas_call x2 -> x3, Pallas kernels: 7.18 us -> 10.7 us  [products(): call(functools.partial(products_kernel, count, len(given)), jax.ShapeDtyp...]
    pallas_call x0 -> x1, Pallas kernels: none -> 1.41 us  [body(): call(functools.partial(cut_kernel, edges, share), [jax.ShapeDtypeStruct((...]
    dynamic_slice x1 -> x0, local copies, waits for them, and re-layouts: 0.85 us -> none  [body(): lax.dynamic_slice_in_dim(down, (me ^ flip) * depth + part * share, share,...]
  transfers between devices with their start and end apart: 19 -> 22, of which waited for: 7 -> 7; matrix products, arithmetic and copies ran while one was open for 8% -> 1% of each run, Pallas kernels for 14% -> 27%
where the time goes in v5:
time: 57.9 us; the launch traced here: 57.6 us
  starting transfers between devices  23.6 us (41%)
  Pallas kernels  18.5 us (32%)
  waiting for transfers between devices  12.6 us (22%)
  local copies, waits for them, and re-layouts  2.38 us (4%)
    ppermute x22, starting transfers between devices, flipped(): return lax.ppermute(value, axis, [(i, i ^ flip) for i in range(count)])  23.6 us
    ppermute x22, waiting for transfers between devices, flipped(): return lax.ppermute(value, axis, [(i, i ^ flip) for i in range(count)])  12.6 us
    pallas_call x3, Pallas kernels, products(): call(functools.partial(products_kernel, count, len(given)), jax.ShapeDtyp...  10.7 us
    pallas_call x1, Pallas kernels, body(): call(functools.partial(last_kernel, len(features), offsets, slots), jax.S...  3.01 us
    pallas_call x1, Pallas kernels, body(): call(functools.partial(shrink_kernel, offsets, slots, rank, parts), jax.S...  2.6 us
    unnamed x12, local copies, waits for them, and re-layouts  2.38 us
    pallas_call x1, Pallas kernels, body(): call(functools.partial(cut_kernel, edges, share), [jax.ShapeDtypeStruct((...  1.41 us
  transfers between devices with their start and end apart: 22, of which 7 were waited for; matrix products, arithmetic and copies ran while one was open for 1% of the time, Pallas kernels for 27%

profile of v5, /device:TPU:0, one launch (start us, length us, event | category | flops | bytes accessed | tf_op | source)
XLA Modules:
  0.0 57.6 jit_solution(11949320631381411897)
XLA Ops:
  0.5 1.4 %copy-done = bf16[384,2048]{1,0:T(8,128)(2,1)S(1)} copy-done((bf16[384,2048]{1,0:T(8,128)(2,1)S(1)}, bf16[384,2048]{1,0:T(8,128)(2,1)}, u32[]{:S(2)}) %copy-start) | copy-done | bytes 1572888
  1.9 0.9 %copy-done.2 = bf16[1,8192,16]{1,2,0:T(8,128)(2,1)S(1)} copy-done((bf16[1,8192,16]{1,2,0:T(8,128)(2,1)S(1)}, bf16[1,8192,16]{1,2,0:T(8,128)(2,1)}, u32[]{:S(2)}) %copy-start.2) | copy-done | bytes 262168
  2.9 1.4 %shard_map.64 = (bf16[384,384]{1,0:T(8,128)(2,1)}, bf16[384,1152]{1,0:T(8,128)(2,1)S(1)}, bf16[384,512]{1,0:T(8,128)(2,1)S(1)}, bf16[16,1024]{1,0:T(8,128)(2,1)S...) custom-call(s32[3]{0:T(128)S(1)} %pad_add_fusion.1.ids_ref, ...), custom_call_target="tpu_custom_call" | custom-call | tf_op jit(solution)/shard_map/pallas_call | solution.py:207
  4.4 2.9 %collective-permute-start.3 = (bf16[16,1024]{1,0:T(8,128)(2,1)S(1)}, bf16[16,1024]{1,0:T(8,128)(2,1)S(1)}, u32[]{:S(2)}, u32[]{:S(2)}) collective-permute-start(bf16[16,1024]{1,0:T(8,128)(2,1)S(1)} %get-tuple-element.46), channel_id=1, source_target_pairs={{0,2},{1,3},{2,0},{3,1},{4,6},{5,7},{6,4},{7,5},{8,10},{9,11},{10,... | collective-permute-start | bytes 98312 | tf_op jit(solution)/shard_map/ppermute | solution.py:25
  7.4 1.4 %collective-permute-start.16 = (bf16[384,384]{1,0:T(8,128)(2,1)}, bf16[384,384]{1,0:T(8,128)(2,1)}, u32[]{:S(2)}, u32[]{:S(2)}) collective-permute-start(bf16[384,384]{1,0:T(8,128)(2,1)} %get-tuple-element.54), channel_id=1, source_target_pairs={{0,2},{1,3},{2,0},{3,1},{4,6},{5,7},{6,4},{7,5},{8,10},{9,11},{10,... | collective-permute-start | bytes 884744 | tf_op jit(solution)/shard_map/ppermute | solution.py:25
  9.0 3.6 %collective-permute-start.9 = (bf16[64,512]{1,0:T(8,128)(2,1)S(1)}, bf16[64,512]{1,0:T(8,128)(2,1)S(1)}, u32[]{:S(2)}, u32[]{:S(2)}) collective-permute-start(bf16[64,512]{1,0:T(8,128)(2,1)S(1)} %bitcast.17), channel_id=1, source_target_pairs={{0,12},{4,8},{8,4},{12,0},{1,13},{5,9},{9,5},{13,1},{2,14},{6,10},... | collective-permute-start | bytes 196616 | tf_op jit(solution)/shard_map/ppermute | solution.py:25
  12.6 1.4 %collective-permute-start.7 = (bf16[64,512]{1,0:T(8,128)(2,1)S(1)}, bf16[64,512]{1,0:T(8,128)(2,1)S(1)}, u32[]{:S(2)}, u32[]{:S(2)}) collective-permute-start(bf16[64,512]{1,0:T(8,128)(2,1)S(1)} %bitcast.19), channel_id=1, source_target_pairs={{0,4},{4,0},{8,12},{12,8},{1,5},{5,1},{9,13},{13,9},{2,6},{6,2},{1... | collective-permute-start | bytes 196616 | tf_op jit(solution)/shard_map/ppermute | solution.py:25
  15.5 1.2 %collective-permute-start.1 = (bf16[384,1152]{1,0:T(8,128)(2,1)S(1)}, bf16[384,1152]{1,0:T(8,128)(2,1)S(1)}, u32[]{:S(2)}, u32[]{:S(2)}) collective-permute-start(bf16[384,1152]{1,0:T(8,128)(2,1)S(1)} %get-tuple-element.43), channel_id=1, source_target_pairs={{0,2},{1,3},{2,0},{3,1},{4,6},{5,7},{6,4},{7,5},{8,10},{9,11},{10,... | collective-permute-start | bytes 2654216 | tf_op jit(solution)/shard_map/ppermute | solution.py:25
  16.7 2.0 %collective-permute-done.8.refs_8_ = bf16[64,512]{1,0:T(8,128)(2,1)S(1)} collective-permute-done((bf16[64,512]{1,0:T(8,128)(2,1)S(1)}, bf16[64,512]{1,0:T(8,128)(2,1)S(1)}, u32[]{:S(2)}, u32[]{:S(2)}) %collective-permute-start.8) | collective-permute-done | bytes 65568 | tf_op jit(solution)/shard_map/ppermute | solution.py:25
  18.6 2.5 %collective-permute-start.11 = (bf16[64,1024]{1,0:T(8,128)(2,1)S(1)}, bf16[64,1024]{1,0:T(8,128)(2,1)S(1)}, u32[]{:S(2)}, u32[]{:S(2)}) collective-permute-start(bf16[64,1024]{1,0:T(8,128)(2,1)S(1)} %shard_map.65.refs_0_), channel_id=1, source_target_pairs={{0,12},{4,8},{8,4},{12,0},{1,13},{5,9},{9,5},{13,1},{2,14},{6,10},... | collective-permute-start | bytes 393224 | tf_op jit(solution)/shard_map/ppermute | solution.py:25
  21.1 1.9 %collective-permute-start.5 = (bf16[64,1024]{1,0:T(8,128)(2,1)S(1)}, bf16[64,1024]{1,0:T(8,128)(2,1)S(1)}, u32[]{:S(2)}, u32[]{:S(2)}) collective-permute-start(bf16[64,1024]{1,0:T(8,128)(2,1)S(1)} %shard_map.65.refs_0_), channel_id=1, source_target_pairs={{0,4},{4,0},{8,12},{12,8},{1,5},{5,1},{9,13},{13,9},{2,6},{6,2},{1... | collective-permute-start | bytes 393224 | tf_op jit(solution)/shard_map/ppermute | solution.py:25
  23.0 4.9 %shard_map.66.refs_2_ = f32[384,512]{1,0:T(8,128)S(1)} custom-call(s32[2]{0:T(128)S(1)} %pad_add_fusion.2.starts_ref, bf16[8192,512]{1,0:T(8,128)(2,1)} %weight_ref.7, bf16[384,2048]{1,0:T(8,128)(2,1)S(1)} %copy-done.1, bf16[384,2048]{1,0:T(8,128)(2,1)} %collective-permute-done.6.refs_1_), custom_call_target="tpu_custom_call" | custom-call | flops 10000000000 | tf_op jit(solution)/shard_map/pallas_call | solution.py:98
  27.9 1.4 %collective-permute-done.5.refs_1_ = bf16[64,1024]{1,0:T(8,128)(2,1)S(1)} collective-permute-done((bf16[64,1024]{1,0:T(8,128)(2,1)S(1)}, bf16[64,1024]{1,0:T(8,128)(2,1)S(1)}, u32[]{:S(2)}, u32[]{:S(2)}) %collective-permute-start.5) | collective-permute-done | bytes 131104 | tf_op jit(solution)/shard_map/ppermute | solution.py:25
  29.3 1.5 %collective-permute-start.12 = (bf16[64,1024]{1,0:T(8,128)(2,1)S(1)}, bf16[64,1024]{1,0:T(8,128)(2,1)S(1)}, u32[]{:S(2)}, u32[]{:S(2)}) collective-permute-start(bf16[64,1024]{1,0:T(8,128)(2,1)S(1)} %shard_map.65.refs_0_), channel_id=1, source_target_pairs={{0,16},{16,0},{1,17},{17,1},{2,18},{18,2},{3,19},{19,3},{4,20},{20... | collective-permute-start | bytes 393224 | tf_op jit(solution)/shard_map/ppermute | solution.py:25
  31.4 1.5 %collective-permute-start.15 = (bf16[64,1024]{1,0:T(8,128)(2,1)S(1)}, bf16[64,1024]{1,0:T(8,128)(2,1)S(1)}, u32[]{:S(2)}, u32[]{:S(2)}) collective-permute-start(bf16[64,1024]{1,0:T(8,128)(2,1)S(1)} %collective-permute-done.11.refs_3_), channel_id=1, source_target_pairs={{0,16},{16,0},{1,17},{17,1},{2,18},{18,2},{3,19},{19,3},{4,20},{20... | collective-permute-start | bytes 393224 | tf_op jit(solution)/shard_map/ppermute | solution.py:25
  33.4 1.5 %collective-permute-start.13 = (bf16[64,1024]{1,0:T(8,128)(2,1)S(1)}, bf16[64,1024]{1,0:T(8,128)(2,1)S(1)}, u32[]{:S(2)}, u32[]{:S(2)}) collective-permute-start(bf16[64,1024]{1,0:T(8,128)(2,1)S(1)} %collective-permute-done.5.refs_1_), channel_id=1, source_target_pairs={{0,16},{16,0},{1,17},{17,1},{2,18},{18,2},{3,19},{19,3},{4,20},{20... | collective-permute-start | bytes 393224 | tf_op jit(solution)/shard_map/ppermute | solution.py:25
  34.9 2.6 %shard_map.67.refs_2_ = f32[384,512]{1,0:T(8,128)S(1)} custom-call(s32[2]{0:T(128)S(1)} %pad_add_fusion.3.starts_ref, bf16[8192,512]{1,0:T(8,128)(2,1)} %weight_ref.7, bf16[384,384]{1,0:T(8,128)(2,1)} %collective-permute-done.16.refs_0_, bf16[384,384]{1,0:T(8,128)(2,1)S(1)} %collective-permute-done.17.refs_1_, f32[384,512]{1,0:T(8,128)S(1)} %shard_map.66.refs_2_), custom_call_target="tpu_custom_call" | custom-call | flops 10000000000 | tf_op jit(solution)/shard_map/pallas_call | solution.py:98
  37.6 1.8 %collective-permute-start = (bf16[384,512]{1,0:T(8,128)(2,1)S(1)}, bf16[384,512]{1,0:T(8,128)(2,1)S(1)}, u32[]{:S(2)}, u32[]{:S(2)}) collective-permute-start(bf16[384,512]{1,0:T(8,128)(2,1)S(1)} %get-tuple-element.42), channel_id=1, source_target_pairs={{0,2},{1,3},{2,0},{3,1},{4,6},{5,7},{6,4},{7,5},{8,10},{9,11},{10,... | collective-permute-start | bytes 1179656 | tf_op jit(solution)/shard_map/ppermute | solution.py:25
  39.4 1.2 %collective-permute-done.14.refs_6_ = bf16[64,1024]{1,0:T(8,128)(2,1)S(1)} collective-permute-done((bf16[64,1024]{1,0:T(8,128)(2,1)S(1)}, bf16[64,1024]{1,0:T(8,128)(2,1)S(1)}, u32[]{:S(2)}, u32[]{:S(2)}) %collective-permute-start.14) | collective-permute-done | bytes 131104 | tf_op jit(solution)/shard_map/ppermute | solution.py:25
  40.6 2.2 %collective-permute-done.13.refs_5_ = bf16[64,1024]{1,0:T(8,128)(2,1)S(1)} collective-permute-done((bf16[64,1024]{1,0:T(8,128)(2,1)S(1)}, bf16[64,1024]{1,0:T(8,128)(2,1)S(1)}, u32[]{:S(2)}, u32[]{:S(2)}) %collective-permute-start.13) | collective-permute-done | bytes 131104 | tf_op jit(solution)/shard_map/ppermute | solution.py:25
  42.8 2.6 %shard_map.68 = f32[64,384]{1,0:T(8,128)S(1)} custom-call(s32[3]{0:T(128)S(1)} %pad_add_fusion.1.ids_ref, s32[4]{0:T(128)S(1)} %copy-done.5, bf16[384,2048]{1,0:T(8,128)(2,1)S(1)} %copy-done.1, s32[1,384]{1,0:T(1,128)S(1)} %bitcast.21, bf16[64,1024]{1,0:T(8,128)(2,1)S(1)} %shard_map.65.refs_0_, bf16[64,1024]{1,0:T(8,128)(2,1)S(1)} %collective-permute-done.5.refs_1_, ...), custom_call_target="tpu_custom_call" | custom-call | flops 10000000000 | tf_op jit(solution)/shard_map/pallas_call | solution.py:273
  46.0 3.3 %shard_map.69.refs_2_ = f32[384,512]{1,0:T(8,128)S(1)} custom-call(s32[2]{0:T(128)S(1)} %pad_add_fusion.4.starts_ref, bf16[8192,512]{1,0:T(8,128)(2,1)} %weight_ref.7, bf16[384,1152]{1,0:T(8,128)(2,1)S(1)} %collective-permute-done.1.refs_0_, bf16[384,1152]{1,0:T(8,128)(2,1)S(1)} %collective-permute-done.19.refs_1_, f32[384,512]{1,0:T(8,128)S(1)} %shard_map.67.refs_2_), custom_call_target="tpu_custom_call" | custom-call | flops 10000000000 | tf_op jit(solution)/shard_map/pallas_call | solution.py:98
  50.1 4.6 %collective-permute-done.21.refs_5_ = f32[64,384]{1,0:T(8,128)S(1)} collective-permute-done((f32[64,384]{1,0:T(8,128)S(1)}, f32[64,384]{1,0:T(8,128)S(1)}, u32[]{:S(2)}, u32[]{:S(2)}) %collective-permute-start.21) | collective-permute-done | bytes 98336 | tf_op jit(solution)/shard_map/ppermute | solution.py:25
  54.6 3.0 %shard_map.70 = bf16[384,512]{1,0:T(8,128)(2,1)} custom-call(s32[2]{0:T(128)S(1)} %pad_add_fusion.starts_ref, s32[3]{0:T(128)S(1)} %pad_add_fusion.1.ids_ref, s32[4]{0:T(128)S(1)} %copy-done.5, bf16[8192,512]{1,0:T(8,128)(2,1)} %weight_ref.7, bf16[384,512]{1,0:T(8,128)(2,1)S(1)} %collective-permute-done.refs_0_, ...), custom_call_target="tpu_custom_call" | custom-call | tf_op jit(solution)/shard_map/pallas_call | solution.py:293
  (45 shorter events, 4.7 us)
Async XLA Ops:
  0.0 23.0 %collective-permute-start.6 = (bf16[384,2048]{1,0:T(8,128)(2,1)}, bf16[384,2048]{1,0:T(8,128)(2,1)}, u32[]{:S(2)}, u32[]{:S(2)}) collective-permute-start(bf16[384,2048]{1,0:T(8,128)(2,1)} %tokens_ref.3), channel_id=1, source_target_pairs={{0,1},{1,0},{2,3},{3,2},{4,5},{5,4},{6,7},{7,6},{8,9},{9,8},{10,11... | collective-permute-start | bytes 4718600 | tf_op jit(solution)/shard_map/ppermute | solution.py:25
  2.9 20.2 %copy-start.1 = (bf16[384,2048]{1,0:T(8,128)(2,1)S(1)}, bf16[384,2048]{1,0:T(8,128)(2,1)}, u32[]{:S(2)}) copy-start(bf16[384,2048]{1,0:T(8,128)(2,1)} %tokens_ref.3) | copy-start | bytes 4718596
  4.3 4.6 %collective-permute-start.2 = (bf16[16,1024]{1,0:T(8,128)(2,1)S(1)}, bf16[16,1024]{1,0:T(8,128)(2,1)S(1)}, u32[]{:S(2)}, u32[]{:S(2)}) collective-permute-start(bf16[16,1024]{1,0:T(8,128)(2,1)S(1)} %get-tuple-element.45), channel_id=1, source_target_pairs={{0,1},{1,0},{2,3},{3,2},{4,5},{5,4},{6,7},{7,6},{8,9},{9,8},{10,11... | collective-permute-start | bytes 98312 | tf_op jit(solution)/shard_map/ppermute | solution.py:25
  4.4 8.1 %collective-permute-start.3 = (bf16[16,1024]{1,0:T(8,128)(2,1)S(1)}, bf16[16,1024]{1,0:T(8,128)(2,1)S(1)}, u32[]{:S(2)}, u32[]{:S(2)}) collective-permute-start(bf16[16,1024]{1,0:T(8,128)(2,1)S(1)} %get-tuple-element.46), channel_id=1, source_target_pairs={{0,2},{1,3},{2,0},{3,1},{4,6},{5,7},{6,4},{7,5},{8,10},{9,11},{10,... | collective-permute-start | bytes 98312 | tf_op jit(solution)/shard_map/ppermute | solution.py:25
  7.4 5.2 %collective-permute-start.4 = (bf16[16,1024]{1,0:T(8,128)(2,1)S(1)}, bf16[16,1024]{1,0:T(8,128)(2,1)S(1)}, u32[]{:S(2)}, u32[]{:S(2)}) collective-permute-start(bf16[16,1024]{1,0:T(8,128)(2,1)S(1)} %get-tuple-element.47), channel_id=1, source_target_pairs={{0,3},{1,2},{2,1},{3,0},{4,7},{5,6},{6,5},{7,4},{8,11},{9,10},{10,... | collective-permute-start | bytes 98312 | tf_op jit(solution)/shard_map/ppermute | solution.py:25
  7.4 13.7 %collective-permute-start.16 = (bf16[384,384]{1,0:T(8,128)(2,1)}, bf16[384,384]{1,0:T(8,128)(2,1)}, u32[]{:S(2)}, u32[]{:S(2)}) collective-permute-start(bf16[384,384]{1,0:T(8,128)(2,1)} %get-tuple-element.54), channel_id=1, source_target_pairs={{0,2},{1,3},{2,0},{3,1},{4,6},{5,7},{6,4},{7,5},{8,10},{9,11},{10,... | collective-permute-start | bytes 884744 | tf_op jit(solution)/shard_map/ppermute | solution.py:25
  9.0 6.5 %collective-permute-start.9 = (bf16[64,512]{1,0:T(8,128)(2,1)S(1)}, bf16[64,512]{1,0:T(8,128)(2,1)S(1)}, u32[]{:S(2)}, u32[]{:S(2)}) collective-permute-start(bf16[64,512]{1,0:T(8,128)(2,1)S(1)} %bitcast.17), channel_id=1, source_target_pairs={{0,12},{4,8},{8,4},{12,0},{1,13},{5,9},{9,5},{13,1},{2,14},{6,10},... | collective-permute-start | bytes 196616 | tf_op jit(solution)/shard_map/ppermute | solution.py:25
  12.6 6.1 %collective-permute-start.8 = (bf16[64,512]{1,0:T(8,128)(2,1)S(1)}, bf16[64,512]{1,0:T(8,128)(2,1)S(1)}, u32[]{:S(2)}, u32[]{:S(2)}) collective-permute-start(bf16[64,512]{1,0:T(8,128)(2,1)S(1)} %bitcast.18), channel_id=1, source_target_pairs={{0,8},{4,12},{8,0},{12,4},{1,9},{5,13},{9,1},{13,5},{2,10},{6,14},... | collective-permute-start | bytes 196616 | tf_op jit(solution)/shard_map/ppermute | solution.py:25
  12.6 8.5 %collective-permute-start.7 = (bf16[64,512]{1,0:T(8,128)(2,1)S(1)}, bf16[64,512]{1,0:T(8,128)(2,1)S(1)}, u32[]{:S(2)}, u32[]{:S(2)}) collective-permute-start(bf16[64,512]{1,0:T(8,128)(2,1)S(1)} %bitcast.19), channel_id=1, source_target_pairs={{0,4},{4,0},{8,12},{12,8},{1,5},{5,1},{9,13},{13,9},{2,6},{6,2},{1... | collective-permute-start | bytes 196616 | tf_op jit(solution)/shard_map/ppermute | solution.py:25
  15.5 27.4 %collective-permute-start.1 = (bf16[384,1152]{1,0:T(8,128)(2,1)S(1)}, bf16[384,1152]{1,0:T(8,128)(2,1)S(1)}, u32[]{:S(2)}, u32[]{:S(2)}) collective-permute-start(bf16[384,1152]{1,0:T(8,128)(2,1)S(1)} %get-tuple-element.43), channel_id=1, source_target_pairs={{0,2},{1,3},{2,0},{3,1},{4,6},{5,7},{6,4},{7,5},{8,10},{9,11},{10,... | collective-permute-start | bytes 2654216 | tf_op jit(solution)/shard_map/ppermute | solution.py:25
  18.6 12.7 %collective-permute-start.11 = (bf16[64,1024]{1,0:T(8,128)(2,1)S(1)}, bf16[64,1024]{1,0:T(8,128)(2,1)S(1)}, u32[]{:S(2)}, u32[]{:S(2)}) collective-permute-start(bf16[64,1024]{1,0:T(8,128)(2,1)S(1)} %shard_map.65.refs_0_), channel_id=1, source_target_pairs={{0,12},{4,8},{8,4},{12,0},{1,13},{5,9},{9,5},{13,1},{2,14},{6,10},... | collective-permute-start | bytes 393224 | tf_op jit(solution)/shard_map/ppermute | solution.py:25
  21.1 10.3 %collective-permute-start.10 = (bf16[64,1024]{1,0:T(8,128)(2,1)S(1)}, bf16[64,1024]{1,0:T(8,128)(2,1)S(1)}, u32[]{:S(2)}, u32[]{:S(2)}) collective-permute-start(bf16[64,1024]{1,0:T(8,128)(2,1)S(1)} %shard_map.65.refs_0_), channel_id=1, source_target_pairs={{0,8},{4,12},{8,0},{12,4},{1,9},{5,13},{9,1},{13,5},{2,10},{6,14},... | collective-permute-start | bytes 393224 | tf_op jit(solution)/shard_map/ppermute | solution.py:25
  21.1 8.2 %collective-permute-start.5 = (bf16[64,1024]{1,0:T(8,128)(2,1)S(1)}, bf16[64,1024]{1,0:T(8,128)(2,1)S(1)}, u32[]{:S(2)}, u32[]{:S(2)}) collective-permute-start(bf16[64,1024]{1,0:T(8,128)(2,1)S(1)} %shard_map.65.refs_0_), channel_id=1, source_target_pairs={{0,4},{4,0},{8,12},{12,8},{1,5},{5,1},{9,13},{13,9},{2,6},{6,2},{1... | collective-permute-start | bytes 393224 | tf_op jit(solution)/shard_map/ppermute | solution.py:25
  23.0 10.4 %collective-permute-start.17 = (bf16[384,384]{1,0:T(8,128)(2,1)}, bf16[384,384]{1,0:T(8,128)(2,1)S(1)}, u32[]{:S(2)}, u32[]{:S(2)}) collective-permute-start(bf16[384,384]{1,0:T(8,128)(2,1)} %collective-permute-done.16.refs_0_), channel_id=1, source_target_pairs={{0,1},{1,0},{2,3},{3,2},{4,5},{5,4},{6,7},{7,6},{8,9},{9,8},{10,11... | collective-permute-start | bytes 884744 | tf_op jit(solution)/shard_map/ppermute | solution.py:25
  27.9 14.9 %copy-start.4 = (s32[384,1]{0,1:T(1,128)S(1)}, s32[384,1]{0,1:T(1,128)}, u32[]{:S(2)}) copy-start(s32[384,1]{0,1:T(1,128)} %param.7) | copy-start | bytes 4612
  29.3 8.2 %collective-permute-start.12 = (bf16[64,1024]{1,0:T(8,128)(2,1)S(1)}, bf16[64,1024]{1,0:T(8,128)(2,1)S(1)}, u32[]{:S(2)}, u32[]{:S(2)}) collective-permute-start(bf16[64,1024]{1,0:T(8,128)(2,1)S(1)} %shard_map.65.refs_0_), channel_id=1, source_target_pairs={{0,16},{16,0},{1,17},{17,1},{2,18},{18,2},{3,19},{19,3},{4,20},{20... | collective-permute-start | bytes 393224 | tf_op jit(solution)/shard_map/ppermute | solution.py:25
  31.4 8.0 %collective-permute-start.15 = (bf16[64,1024]{1,0:T(8,128)(2,1)S(1)}, bf16[64,1024]{1,0:T(8,128)(2,1)S(1)}, u32[]{:S(2)}, u32[]{:S(2)}) collective-permute-start(bf16[64,1024]{1,0:T(8,128)(2,1)S(1)} %collective-permute-done.11.refs_3_), channel_id=1, source_target_pairs={{0,16},{16,0},{1,17},{17,1},{2,18},{18,2},{3,19},{19,3},{4,20},{20... | collective-permute-start | bytes 393224 | tf_op jit(solution)/shard_map/ppermute | solution.py:25
  32.9 7.7 %collective-permute-start.14 = (bf16[64,1024]{1,0:T(8,128)(2,1)S(1)}, bf16[64,1024]{1,0:T(8,128)(2,1)S(1)}, u32[]{:S(2)}, u32[]{:S(2)}) collective-permute-start(bf16[64,1024]{1,0:T(8,128)(2,1)S(1)} %collective-permute-done.10.refs_2_), channel_id=1, source_target_pairs={{0,16},{16,0},{1,17},{17,1},{2,18},{18,2},{3,19},{19,3},{4,20},{20... | collective-permute-start | bytes 393224 | tf_op jit(solution)/shard_map/ppermute | solution.py:25
  33.4 9.4 %collective-permute-start.13 = (bf16[64,1024]{1,0:T(8,128)(2,1)S(1)}, bf16[64,1024]{1,0:T(8,128)(2,1)S(1)}, u32[]{:S(2)}, u32[]{:S(2)}) collective-permute-start(bf16[64,1024]{1,0:T(8,128)(2,1)S(1)} %collective-permute-done.5.refs_1_), channel_id=1, source_target_pairs={{0,16},{16,0},{1,17},{17,1},{2,18},{18,2},{3,19},{19,3},{4,20},{20... | collective-permute-start | bytes 393224 | tf_op jit(solution)/shard_map/ppermute | solution.py:25
  37.6 11.8 %collective-permute-start = (bf16[384,512]{1,0:T(8,128)(2,1)S(1)}, bf16[384,512]{1,0:T(8,128)(2,1)S(1)}, u32[]{:S(2)}, u32[]{:S(2)}) collective-permute-start(bf16[384,512]{1,0:T(8,128)(2,1)S(1)} %get-tuple-element.42), channel_id=1, source_target_pairs={{0,2},{1,3},{2,0},{3,1},{4,6},{5,7},{6,4},{7,5},{8,10},{9,11},{10,... | collective-permute-start | bytes 1179656 | tf_op jit(solution)/shard_map/ppermute | solution.py:25
  42.8 3.2 %collective-permute-start.19 = (bf16[384,1152]{1,0:T(8,128)(2,1)S(1)}, bf16[384,1152]{1,0:T(8,128)(2,1)S(1)}, u32[]{:S(2)}, u32[]{:S(2)}) collective-permute-start(bf16[384,1152]{1,0:T(8,128)(2,1)S(1)} %collective-permute-done.1.refs_0_), channel_id=1, source_target_pairs={{0,1},{1,0},{2,3},{3,2},{4,5},{5,4},{6,7},{7,6},{8,9},{9,8},{10,11... | collective-permute-start | bytes 2654216 | tf_op jit(solution)/shard_map/ppermute | solution.py:25
  45.4 3.8 %collective-permute-start.18 = (f32[64,384]{1,0:T(8,128)S(1)}, f32[64,384]{1,0:T(8,128)S(1)}, u32[]{:S(2)}, u32[]{:S(2)}) collective-permute-start(f32[64,384]{1,0:T(8,128)S(1)} %shard_map.68), channel_id=1, source_target_pairs={{0,1},{1,0},{2,3},{3,2},{4,5},{5,4},{6,7},{7,6},{8,9},{9,8},{10,11... | collective-permute-start | bytes 294920 | tf_op jit(solution)/shard_map/ppermute | solution.py:25
  49.3 5.3 %collective-permute-start.20 = (bf16[384,512]{1,0:T(8,128)(2,1)S(1)}, bf16[384,512]{1,0:T(8,128)(2,1)S(1)}, u32[]{:S(2)}, u32[]{:S(2)}) collective-permute-start(bf16[384,512]{1,0:T(8,128)(2,1)S(1)} %collective-permute-done.refs_0_), channel_id=1, source_target_pairs={{0,1},{1,0},{2,3},{3,2},{4,5},{5,4},{6,7},{7,6},{8,9},{9,8},{10,11... | collective-permute-start | bytes 1179656 | tf_op jit(solution)/shard_map/ppermute | solution.py:25
  49.4 5.2 %collective-permute-start.21 = (f32[64,384]{1,0:T(8,128)S(1)}, f32[64,384]{1,0:T(8,128)S(1)}, u32[]{:S(2)}, u32[]{:S(2)}) collective-permute-start(f32[64,384]{1,0:T(8,128)S(1)} %add.19.refs_4_), channel_id=1, source_target_pairs={{0,2},{1,3},{2,0},{3,1},{4,6},{5,7},{6,4},{7,5},{8,10},{9,11},{10,... | collective-permute-start | bytes 294920 | tf_op jit(solution)/shard_map/ppermute | solution.py:25
  (4 other events, 23.3 us)

commit v6 on v1

v6 whole, which is shorter than its diff:
```python
import functools
import math

import jax
import jax.numpy as jnp
from jax import lax
from jax.experimental import pallas as pl
from jax.experimental.pallas import tpu as pltpu
from jax.sharding import PartitionSpec as P

LOWRANK_SCALE = 2.0
CORES = 2
LANES = 128
CUTS = (0.75,)
MIB = 1024 * 1024
FREE = pl.CostEstimate(flops=0, bytes_accessed=0, transcendentals=0)
LONG = pl.CostEstimate(flops=10**11, bytes_accessed=0, transcendentals=0)
ANYWHERE = pl.BlockSpec(memory_space=pl.ANY)
VECTOR = pl.BlockSpec(memory_space=pltpu.VMEM)
SCALAR = pl.BlockSpec(memory_space=pltpu.SMEM)


def flipped(value, axis, flip):
    count = lax.axis_size(axis)
    return lax.ppermute(value, axis, [(i, i ^ flip) for i in range(count)])


def chained(*values):
    return lax.optimization_barrier(values)


def call(kernel, out_shape, in_specs, scratch, out_specs=VECTOR, cost=LONG, mib=48):
    return pl.pallas_call(
        kernel,
        out_shape=out_shape,
        in_specs=in_specs,
        out_specs=out_specs,
        scratch_shapes=scratch,
        cost_estimate=cost,
        compiler_params=pltpu.CompilerParams(vmem_limit_bytes=mib * MIB),
    )


def run_copies(pairs, sems):
    copies = [
        pltpu.make_async_copy(source, target, sems.at[i]) for i, (source, target) in enumerate(pairs)
    ]
    for copy in copies:
        copy.start()
    for copy in copies:
        copy.wait()


def cut_kernel(edges, source_ref, *refs):
    run_copies(
        [(source_ref.at[:, a:b], out) for a, b, out in zip(edges, edges[1:], refs[:-1])], refs[-1]
    )


def slice_kernel(ids_ref, down_ref, *refs):
    outs, sems = refs[:-1], refs[-1]
    depth = outs[0].shape[1]
    run_copies(
        [
            (down_ref.at[:, pl.ds(pl.multiple_of((ids_ref[0] ^ flip) * depth, LANES), depth)], out)
            for flip, out in enumerate(outs)
        ],
        sems,
    )


def order_kernel(rank_part, ids_ref, *refs):
    pieces, out_ref, sems = refs[:-2], refs[-2], refs[-1]
    run_copies(
        [
            (piece, out_ref.at[pl.ds(pl.multiple_of((ids_ref[0] ^ f) * rank_part, rank_part), rank_part)])
            for f, piece in enumerate(pieces)
        ],
        sems,
    )


def slot_of_row(tenant, placement_ref, slots):
    stored = jnp.zeros(tenant.shape, jnp.int32)
    for slot in range(slots):
        stored = jnp.where(tenant == slot, placement_ref[slot], stored)
    return stored


def start_tiles(tile, starts_ref, features, weight_ref, held_ref, rows_ref, sems):
    t = 0
    for i, part in enumerate(features):
        for k in range(0, part.shape[1], tile):
            start = pl.multiple_of(starts_ref[i] + k, LANES)
            pltpu.make_async_copy(part.at[:, pl.ds(k, tile)], held_ref.at[t], sems.at[0, t]).start()
            pltpu.make_async_copy(
                weight_ref.at[pl.ds(start, tile)], rows_ref.at[t], sems.at[1, t]
            ).start()
            t += 1


def add_tiles(held_ref, rows_ref, sems, total_ref):
    @pl.loop(0, held_ref.shape[0])
    def _(t):
        pltpu.make_async_copy(held_ref.at[t], held_ref.at[t], sems.at[0, t]).wait()
        pltpu.make_async_copy(rows_ref.at[t], rows_ref.at[t], sems.at[1, t]).wait()
        total_ref[...] += jnp.dot(held_ref[t], rows_ref[t], preferred_element_type=jnp.float32)


def tile_scratch(tile, features, columns):
    tiles = sum(f.shape[1] for f in features) // tile
    rows = features[0].shape[0]
    return [
        pltpu.VMEM((tiles, rows, tile), jnp.bfloat16),
        pltpu.VMEM((tiles, tile, columns), jnp.bfloat16),
        pltpu.SemaphoreType.DMA((2, tiles)),
    ]


def products_kernel(tile, count, has_total, starts_ref, weight_ref, *refs):
    features = refs[:count]
    given = refs[count] if has_total else None
    out_ref, held_ref, rows_ref, sems = refs[count + has_total :]
    start_tiles(tile, starts_ref, features, weight_ref, held_ref, rows_ref, sems)
    out_ref[...] = given[...] if has_total else jnp.zeros_like(out_ref)
    add_tiles(held_ref, rows_ref, sems, out_ref)


def products(tile, starts, features, weight, total=None):
    given = [] if total is None else [total]
    return call(
        functools.partial(products_kernel, tile, len(features), len(given)),
        jax.ShapeDtypeStruct((features[0].shape[0], weight.shape[1]), jnp.float32),
        [SCALAR, ANYWHERE] + [ANYWHERE] * len(features) + [VECTOR] * len(given),
        tile_scratch(tile, features, weight.shape[1]),
    )(jnp.stack(starts), weight, *features, *given)


def last_kernel(tile, count, slots, starts_ref, ids_ref, placement_ref, weight_ref, *refs):
    features = refs[:count]
    given, tenant_ref, sum_ref, more_ref = refs[count : count + 4]
    ups = refs[count + 4 : count + 4 + slots]
    out_ref, total_ref, held_ref, rows_ref, sems = refs[count + 4 + slots :]
    start_tiles(tile, starts_ref, features, weight_ref, held_ref, rows_ref, sems)
    shrunk = (sum_ref[...] + more_ref[...]).astype(jnp.bfloat16).astype(jnp.float32)
    stored = slot_of_row(tenant_ref[...], placement_ref, slots)
    spread = jnp.concatenate(
        [jnp.where(stored == (ids_ref[1] ^ offset), shrunk, 0.0) for offset in range(slots)], axis=0
    )
    stacked = jnp.concatenate([up[...] for up in ups], axis=0)
    expanded = jnp.dot(
        spread.T.astype(jnp.bfloat16), stacked, preferred_element_type=jnp.float32
    )
    expanded = expanded.astype(jnp.bfloat16).astype(jnp.float32)
    total_ref[...] = given[...] + LOWRANK_SCALE * expanded
    add_tiles(held_ref, rows_ref, sems, total_ref)
    out_ref[...] = total_ref[...].astype(out_ref.dtype)


def shrink_kernel(tile, slots, owners_ref, placement_ref, tokens_ref, tenant_ref, *refs):
    downs, out_ref, held_ref, down_ref, sums_ref, sems = (
        refs[:slots], refs[slots], *refs[slots + 1 :]
    )
    rank = downs[0].shape[0]
    tiles = tokens_ref.shape[1] // tile
    for k in range(tiles):
        here = pl.ds(k * tile, tile)
        pltpu.make_async_copy(tokens_ref.at[:, here], held_ref.at[k], sems.at[0, k]).start()
        for b, down in enumerate(downs):
            pltpu.make_async_copy(
                down.at[:, here], down_ref.at[k, pl.ds(b * rank, rank)], sems.at[1 + b, k]
            ).start()
    stored = slot_of_row(tenant_ref[...], placement_ref, slots)
    sums_ref[...] = jnp.zeros_like(sums_ref)

    @pl.loop(0, tiles)
    def _(k):
        pltpu.make_async_copy(held_ref.at[k], held_ref.at[k], sems.at[0, k]).wait()
        for b in range(slots):
            block = down_ref.at[k, pl.ds(b * rank, rank)]
            pltpu.make_async_copy(block, block, sems.at[1 + b, k]).wait()
        sums_ref[...] += lax.dot_general(
            held_ref[k], down_ref[k], (((1,), (1,)), ((), ())), preferred_element_type=jnp.float32
        )

    sums = sums_ref[...].T
    total = jnp.zeros(out_ref.shape, jnp.float32)
    for b in range(slots):
        total += jnp.where(stored == owners_ref[b], sums[b * rank : (b + 1) * rank], 0.0)
    out_ref[...] = total


def body(
    tokens, tenant, placement, frozen_projection_weight, lowrank_down_weight, lowrank_up_weight
):
    rows, depth = tokens.shape
    slots = placement.shape[0]
    tensors = lax.axis_size("tensor")
    groups = lax.axis_size("adapter")
    parts = lax.axis_size("parts")
    me = lax.axis_index("tensor")
    group = lax.axis_index("adapter")
    part = lax.axis_index("parts")
    ids = jnp.stack([me, group])
    rank, columns = lowrank_up_weight.shape[1:]
    tenant_row = tenant.reshape(1, rows)
    edges = [0] + [int(depth * cut) // LANES * LANES for cut in CUTS] + [depth]
    tile = math.gcd(*edges)

    down = lowrank_down_weight[0].T
    whole_tiles = down.shape[0] % 16 == 0
    if whole_tiles:
        pieces = call(
            slice_kernel,
            [jax.ShapeDtypeStruct((down.shape[0], depth), down.dtype)] * tensors,
            [SCALAR, ANYWHERE],
            [pltpu.SemaphoreType.DMA((tensors,))],
            [ANYWHERE] * tensors,
            cost=FREE,
            mib=60,
        )(ids, down)
    else:
        pieces = [
            lax.dynamic_slice_in_dim(down, (me ^ flip) * depth, depth, axis=1)
            for flip in range(tensors)
        ]
    neighbour = flipped(tokens, "tensor", 1)
    uncut, pieces = chained(tokens, pieces)
    chunks = call(
        functools.partial(cut_kernel, edges),
        [jax.ShapeDtypeStruct((rows, b - a), tokens.dtype) for a, b in zip(edges, edges[1:])],
        [ANYWHERE],
        [pltpu.SemaphoreType.DMA((len(edges) - 1,))],
        [ANYWHERE] * (len(edges) - 1),
        mib=60,
    )(uncut)
    pieces = [pieces[0]] + [flipped(pieces[f], "tensor", f) for f in range(1, tensors)]
    pieces, chunks = chained(pieces, chunks)
    if whole_tiles:
        own = call(
            functools.partial(order_kernel, down.shape[0]),
            jax.ShapeDtypeStruct((rank, depth), down.dtype),
            [SCALAR] + [ANYWHERE] * tensors,
            [pltpu.SemaphoreType.DMA((tensors,))],
            ANYWHERE,
            cost=FREE,
        )(ids, *pieces)
    else:
        none = jnp.zeros((), down.dtype)
        own = jnp.concatenate(
            [sum(jnp.where((me ^ f) == j, pieces[f], none) for f in range(tensors)) for j in range(tensors)],
            axis=0,
        )

    hops = range(CORES, tensors, CORES)
    far = [[flipped(chunks[0], "tensor", hop) for hop in hops]]

    def spread_out(m):
        starts, features = [], []
        for hop, value in zip(hops, far[m]):
            features += [value, flipped(value, "tensor", 1)]
            starts += [(me ^ hop) * depth + edges[m], (me ^ hop ^ 1) * depth + edges[m]]
        return starts, features

    downs, owners, fetched = [own], [group], []
    flips = list(range(1, groups))
    if parts == 2:
        while len(flips) > 1:
            pair = (flips.pop(-2), flips.pop(-1))
            route = [
                (p * groups + z, p * groups + (z ^ pair[p])) for p in range(parts) for z in range(groups)
            ]
            fetched.append((pair, lax.ppermute(own, ("parts", "adapter"), route)))
    singles = [(flip, flipped(own, "adapter", flip)) for flip in flips]

    own, here = chained(own, tokens)
    total = products(tile, [me * depth], [here], frozen_projection_weight)
    total, last = chained(total, chunks[1])
    far.append([flipped(last, "tensor", hop) for hop in hops])
    for flip, value in singles:
        value, total = chained(value, total)
        downs.append(value)
        owners.append(group ^ flip)
    up = lowrank_up_weight[0]
    for pair, value in fetched:
        value, total = chained(value, total)
        swapped = flipped(value, "parts", 1)
        if pair == fetched[0][0]:
            total, neighbour = chained(total, neighbour)
            total = products(
                tile, [(me ^ 1) * depth], [neighbour], frozen_projection_weight, total
            )
            total, up = chained(total, up)
        swapped, total = chained(swapped, total)
        downs += [value, swapped]
        mine, other = (jnp.where(part == 0, *order) for order in (pair, pair[::-1]))
        owners += [group ^ mine, group ^ other]
    ups = [up] + [flipped(up, "adapter", flip) for flip in range(1, groups)]
    downs, ups = chained(downs, ups)

    tiles = depth // tile
    partial = call(
        functools.partial(shrink_kernel, tile, slots),
        jax.ShapeDtypeStruct((rank, rows), jnp.float32),
        [SCALAR, SCALAR, ANYWHERE, VECTOR] + [ANYWHERE] * slots,
        [
            pltpu.VMEM((tiles, rows, tile), jnp.bfloat16),
            pltpu.VMEM((tiles, slots * rank, tile), jnp.bfloat16),
            pltpu.VMEM((rows, slots * rank), jnp.float32),
            pltpu.SemaphoreType.DMA((1 + slots, tiles)),
        ],
    )(jnp.stack(owners), placement, tokens, tenant_row, *downs)
    far[0], partial = chained(far[0], partial)
    starts, features = spread_out(0)
    total = products(tile, starts[::2], features[::2], frozen_projection_weight, total)
    near, total = chained(features[1::2], total)
    total = products(tile, starts[1::2], near, frozen_projection_weight, total)
    flip = 1
    while flip < tensors // 2:
        received = flipped(partial, "tensor", flip)
        if flip == 1:
            received, total = chained(received, total)
        partial += received
        flip *= 2
    more = flipped(partial, "tensor", flip)
    far[1], total, partial = chained(far[1], total, partial)
    starts, features = spread_out(1)

    return call(
        functools.partial(last_kernel, tile, len(features), slots),
        jax.ShapeDtypeStruct((rows, columns), jnp.bfloat16),
        [SCALAR, SCALAR, SCALAR, ANYWHERE]
        + [ANYWHERE] * len(features)
        + [VECTOR] * (4 + slots),
        [pltpu.VMEM((rows, columns), jnp.float32)] + tile_scratch(tile, features, columns),
    )(
        jnp.stack(starts), ids, placement, frozen_projection_weight, *features, total, tenant_row,
        partial, more, *ups,
    )


def solution(mesh):
    placed = (
        P(("parts", "adapter"), "tensor"),
        P(("parts", "adapter"), None),
        P(),
        P(None, "tensor"),
        P("adapter", None, "tensor"),
        P("adapter", None, "tensor"),
    )
    return jax.shard_map(
        body,
        mesh=mesh,
        in_specs=placed,
        out_specs=P(("parts", "adapter"), "tensor"),
        check_vma=False,
    )
```

time: 89.1 us -> 133 us (1.49)
  Pallas kernels: 0 us -> 75.8 us
  matrix products: 22.4 us -> 0 us
  between operations: 13.6 us -> 0.3 us
  starting transfers between devices: 9.63 us -> 17 us
  local copies, waits for them, and re-layouts: 2.39 us -> 0.07 us
  other arithmetic: 4.06 us -> 1.75 us
    pallas_call x0 -> x9, Pallas kernels: none -> 75.8 us  [the longest x1 48.8 us: body(): call(functools.partial(cut_kernel, edges), [jax.ShapeDtypeStruct((rows, b...]
    dot_general x12 -> x0, matrix products: 22.4 us -> none  [the longest x10 18.6 us: body(): total += jnp.dot(features, part, preferred_element_type=jnp.float32)]
    ppermute x14 -> x16, starting transfers between devices: 9.63 us -> 17 us  [the longest x15 14.4 us: flipped(): return lax.ppermute(value, axis, [(i, i ^ flip) for i in range(count)])]
    concatenate x1 -> x0, other arithmetic: 1.59 us -> none  [body(): stored_here = jnp.concatenate([down_slice, lowrank_up_weight[0]], axis=1)]
    slice x1 -> x0, local copies, waits for them, and re-layouts: 1.47 us -> none  [body(): chunk = tokens[:, m * step:(m + 1) * step]]
    ppermute x14 -> x16, waiting for transfers between devices: 36.4 us -> 37.4 us  [the longest x15 34.9 us: flipped(): return lax.ppermute(value, axis, [(i, i ^ flip) for i in range(count)])]
  transfers between devices with their start and end apart: 15 -> 16, of which waited for: 7 -> 7; matrix products, arithmetic and copies ran while one was open for 26% -> 1% of each run, Pallas kernels for 0% -> 55%
where the time goes in v6:
time: 133 us; the launch traced here: 132 us
  Pallas kernels  75.8 us (57%)
  waiting for transfers between devices  37.4 us (28%)
  starting transfers between devices  17 us (13%)
  other arithmetic  1.75 us (1%)
    pallas_call x1, Pallas kernels, body(): call(functools.partial(cut_kernel, edges), [jax.ShapeDtypeStruct((rows, b...  48.8 us
    ppermute x15, waiting for transfers between devices, flipped(): return lax.ppermute(value, axis, [(i, i ^ flip) for i in range(count)])  34.9 us
    ppermute x15, starting transfers between devices, flipped(): return lax.ppermute(value, axis, [(i, i ^ flip) for i in range(count)])  14.4 us
    pallas_call x4, Pallas kernels, products(): call(functools.partial(products_kernel, tile, len(features), len(given)),...  10 us
    pallas_call x1, Pallas kernels, body(): call(slice_kernel, [jax.ShapeDtypeStruct((down.shape[0], depth), down.dty...  9.74 us
    pallas_call x1, Pallas kernels, body(): call(functools.partial(last_kernel, tile, len(features), slots), jax.Shap...  3.27 us
    pallas_call x1, Pallas kernels, body(): call(functools.partial(shrink_kernel, tile, slots), jax.ShapeDtypeStruct(...  3.08 us
  transfers between devices with their start and end apart: 16, of which 7 were waited for; matrix products, arithmetic and copies ran while one was open for 1% of the time, Pallas kernels for 55%

profile of v6, /device:TPU:0, one launch (start us, length us, event | category | flops | bytes accessed | tf_op | source)
XLA Modules:
  0.0 132.3 jit_solution(1804758569610650781)
XLA Ops:
  1.1 9.7 %shard_map.64 = (bf16[16,2048]{1,0:T(8,128)(2,1)}, bf16[16,2048]{1,0:T(8,128)(2,1)}, bf16[16,2048]{1,0:T(8,128)(2,1)}, bf16[16,2048]{1,0:T(8,128)(2,1)}) custom-call(s32[2]{0:T(128)} %pad_add_fusion.1.ids_ref, bf16[16,8192]{1,0:T(8,128)(2,1)} %bitcast.22), custom_call_target="tpu_custom_call" | custom-call | tf_op jit(solution)/shard_map/pallas_call | solution.py:213
  11.0 2.9 %collective-permute-start.1 = (bf16[16,2048]{1,0:T(8,128)(2,1)}, bf16[16,2048]{1,0:T(8,128)(2,1)S(1)}, u32[]{:S(2)}, u32[]{:S(2)}) collective-permute-start(bf16[16,2048]{1,0:T(8,128)(2,1)} %get-tuple-element.58), channel_id=1, source_target_pairs={{0,2},{1,3},{2,0},{3,1},{4,6},{5,7},{6,4},{7,5},{8,10},{9,11},{10,... | collective-permute-start | bytes 196616 | tf_op jit(solution)/shard_map/ppermute | solution.py:25
  13.9 48.8 %shard_map.65 = (bf16[384,1536]{1,0:T(8,128)(2,1)}, bf16[384,512]{1,0:T(8,128)(2,1)}) custom-call(bf16[384,2048]{1,0:T(8,128)(2,1)} %tokens_ref.1), custom_call_target="tpu_custom_call" | custom-call | flops 99999997952 | tf_op jit(solution)/shard_map/pallas_call | solution.py:229
  62.8 0.9 shard_map.66.refs_0_
  63.7 1.6 %collective-permute-start.5 = (bf16[64,2048]{1,0:T(8,128)(2,1)S(1)}, bf16[64,2048]{1,0:T(8,128)(2,1)S(1)}, u32[]{:S(2)}, u32[]{:S(2)}) collective-permute-start(bf16[64,2048]{1,0:T(8,128)(2,1)S(1)} %shard_map.66.refs_0_), channel_id=1, source_target_pairs={{0,4},{4,0},{8,12},{12,8},{1,5},{5,1},{9,13},{13,9},{2,6},{6,2},{1... | collective-permute-start | bytes 786440 | tf_op jit(solution)/shard_map/ppermute | solution.py:25
  65.4 2.6 %collective-permute-start.6 = (bf16[64,2048]{1,0:T(8,128)(2,1)S(1)}, bf16[64,2048]{1,0:T(8,128)(2,1)S(1)}, u32[]{:S(2)}, u32[]{:S(2)}) collective-permute-start(bf16[64,2048]{1,0:T(8,128)(2,1)S(1)} %shard_map.66.refs_0_), channel_id=1, source_target_pairs={{0,8},{4,12},{8,0},{12,4},{16,28},{20,24},{24,20},{28,16},{1,9},{5... | collective-permute-start | bytes 786440 | tf_op jit(solution)/shard_map/ppermute | solution.py:273
  68.0 2.6 %shard_map.67.refs_1_ = f32[384,512]{1,0:T(8,128)S(1)} custom-call(s32[1]{0:T(128)} %bitcast.4.starts_ref, bf16[8192,512]{1,0:T(8,128)(2,1)} %weight_ref.9, bf16[384,2048]{1,0:T(8,128)(2,1)S(1)} %copy-done.2), custom_call_target="tpu_custom_call" | custom-call | flops 99999997952 | tf_op jit(solution)/shard_map/pallas_call | solution.py:131
  70.6 7.4 %collective-permute-done.5.refs_1_ = bf16[64,2048]{1,0:T(8,128)(2,1)S(1)} collective-permute-done((bf16[64,2048]{1,0:T(8,128)(2,1)S(1)}, bf16[64,2048]{1,0:T(8,128)(2,1)S(1)}, u32[]{:S(2)}, u32[]{:S(2)}) %collective-permute-start.5) | collective-permute-done | bytes 262176 | tf_op jit(solution)/shard_map/ppermute | solution.py:25
  78.0 2.5 %collective-permute-done.6.refs_2_ = bf16[64,2048]{1,0:T(8,128)(2,1)S(1)} collective-permute-done((bf16[64,2048]{1,0:T(8,128)(2,1)S(1)}, bf16[64,2048]{1,0:T(8,128)(2,1)S(1)}, u32[]{:S(2)}, u32[]{:S(2)}) %collective-permute-start.6) | collective-permute-done | bytes 262176 | tf_op jit(solution)/shard_map/ppermute | solution.py:273
  80.5 1.4 %collective-permute-start.7 = (bf16[64,2048]{1,0:T(8,128)(2,1)S(1)}, bf16[64,2048]{1,0:T(8,128)(2,1)S(1)}, u32[]{:S(2)}, u32[]{:S(2)}) collective-permute-start(bf16[64,2048]{1,0:T(8,128)(2,1)S(1)} %collective-permute-done.6.refs_2_), channel_id=1, source_target_pairs={{0,16},{16,0},{1,17},{17,1},{2,18},{18,2},{3,19},{19,3},{4,20},{20... | collective-permute-start | bytes 786440 | tf_op jit(solution)/shard_map/ppermute | solution.py:25
  81.9 2.8 %shard_map.68.refs_1_ = f32[384,512]{1,0:T(8,128)S(1)} custom-call(s32[1]{0:T(128)} %bitcast.11.starts_ref, bf16[8192,512]{1,0:T(8,128)(2,1)} %weight_ref.9, bf16[384,2048]{1,0:T(8,128)(2,1)} %collective-permute-done.8.refs_0_, f32[384,512]{1,0:T(8,128)S(1)} %shard_map.67.refs_1_), custom_call_target="tpu_custom_call" | custom-call | flops 99999997952 | tf_op jit(solution)/shard_map/pallas_call | solution.py:131
  84.8 1.8 %collective-permute-start.10 = (bf16[64,512]{1,0:T(8,128)(2,1)S(1)}, bf16[64,512]{1,0:T(8,128)(2,1)S(1)}, u32[]{:S(2)}, u32[]{:S(2)}) collective-permute-start(bf16[64,512]{1,0:T(8,128)(2,1)S(1)} %bitcast.16), channel_id=1, source_target_pairs={{0,8},{4,12},{8,0},{12,4},{1,9},{5,13},{9,1},{13,5},{2,10},{6,14},... | collective-permute-start | bytes 196616 | tf_op jit(solution)/shard_map/ppermute | solution.py:25
  86.6 1.2 collective-permute-start.11
  88.4 1.5 %collective-permute-start.4 = (bf16[384,1536]{1,0:T(8,128)(2,1)S(1)}, bf16[384,1536]{1,0:T(8,128)(2,1)S(1)}, u32[]{:S(2)}, u32[]{:S(2)}) collective-permute-start(bf16[384,1536]{1,0:T(8,128)(2,1)S(1)} %copy-done.15), channel_id=1, source_target_pairs={{0,2},{1,3},{2,0},{3,1},{4,6},{5,7},{6,4},{7,5},{8,10},{9,11},{10,... | collective-permute-start | bytes 3538952 | tf_op jit(solution)/shard_map/ppermute | solution.py:25
  90.5 1.0 collective-permute-done.10.refs_8_
  91.4 1.4 %collective-permute-done.11.refs_9_ = bf16[64,512]{1,0:T(8,128)(2,1)S(1)} collective-permute-done((bf16[64,512]{1,0:T(8,128)(2,1)S(1)}, bf16[64,512]{1,0:T(8,128)(2,1)S(1)}, u32[]{:S(2)}, u32[]{:S(2)}) %collective-permute-start.11) | collective-permute-done | bytes 65568 | tf_op jit(solution)/shard_map/ppermute | solution.py:25
  92.8 3.1 %shard_map.69 = f32[64,384]{1,0:T(8,128)} custom-call(s32[4]{0:T(128)S(1)} %pad_add_fusion.2.owners_ref, s32[4]{0:T(128)S(1)} %copy-done.13, bf16[384,2048]{1,0:T(8,128)(2,1)S(1)} %copy-done.2, s32[1,384]{1,0:T(1,128)S(1)} %bitcast.20, bf16[64,2048]{1,0:T(8,128)(2,1)S(1)} %shard_map.66.refs_0_, bf16[64,2048]{1,0:T(8,128)(2,1)S(1)} %collective-permute-done.5.refs_1_, ...), custom_call_target="tpu_custom_call" | custom-call | flops 99999997952 | tf_op jit(solution)/shard_map/pallas_call | solution.py:302
  96.0 21.4 %collective-permute-done.4.refs_0_ = bf16[384,1536]{1,0:T(8,128)(2,1)S(1)} collective-permute-done((bf16[384,1536]{1,0:T(8,128)(2,1)S(1)}, bf16[384,1536]{1,0:T(8,128)(2,1)S(1)}, u32[]{:S(2)}, u32[]{:S(2)}) %collective-permute-start.4) | collective-permute-done | bytes 1179680 | tf_op jit(solution)/shard_map/ppermute | solution.py:25
  117.8 2.2 %shard_map.70.refs_1_ = f32[384,512]{1,0:T(8,128)S(1)} custom-call(s32[1]{0:T(128)} %bitcast.14.starts_ref, bf16[8192,512]{1,0:T(8,128)(2,1)} %weight_ref.9, bf16[384,1536]{1,0:T(8,128)(2,1)S(1)} %collective-permute-done.4.refs_0_, f32[384,512]{1,0:T(8,128)S(1)} %shard_map.68.refs_1_), custom_call_target="tpu_custom_call" | custom-call | flops 99999997952 | tf_op jit(solution)/shard_map/pallas_call | solution.py:131
  120.4 2.3 %shard_map.71.refs_2_ = f32[384,512]{1,0:T(8,128)S(1)} custom-call(s32[1]{0:T(128)} %bitcast.13.starts_ref, bf16[8192,512]{1,0:T(8,128)(2,1)} %weight_ref.9, bf16[384,1536]{1,0:T(8,128)(2,1)S(1)} %collective-permute-done.13.refs_0_, f32[384,512]{1,0:T(8,128)S(1)} %shard_map.70.refs_1_), custom_call_target="tpu_custom_call" | custom-call | flops 99999997952 | tf_op jit(solution)/shard_map/pallas_call | solution.py:131
  122.7 1.0 add.11.refs_4_
  123.9 1.5 %collective-permute-start.15 = (f32[64,384]{1,0:T(8,128)S(1)}, f32[64,384]{1,0:T(8,128)S(1)}, u32[]{:S(2)}, u32[]{:S(2)}) collective-permute-start(f32[64,384]{1,0:T(8,128)S(1)} %add.11.refs_4_), channel_id=1, source_target_pairs={{0,2},{1,3},{2,0},{3,1},{4,6},{5,7},{6,4},{7,5},{8,10},{9,11},{10,... | collective-permute-start | bytes 294920 | tf_op jit(solution)/shard_map/ppermute | solution.py:25
  125.5 3.5 %collective-permute-done.15.refs_5_ = f32[64,384]{1,0:T(8,128)S(1)} collective-permute-done((f32[64,384]{1,0:T(8,128)S(1)}, f32[64,384]{1,0:T(8,128)S(1)}, u32[]{:S(2)}, u32[]{:S(2)}) %collective-permute-start.15) | collective-permute-done | bytes 98336 | tf_op jit(solution)/shard_map/ppermute | solution.py:25
  129.0 3.3 %shard_map.72 = bf16[384,512]{1,0:T(8,128)(2,1)} custom-call(s32[2]{0:T(128)S(1)} %pad_add_fusion.starts_ref, s32[2]{0:T(128)S(1)} %copy-done.1, s32[4]{0:T(128)S(1)} %copy-done.14, bf16[8192,512]{1,0:T(8,128)(2,1)} %weight_ref.9, bf16[384,512]{1,0:T(8,128)(2,1)} %collective-permute-done.3.refs_0_, bf16[384,512]{1,0:T(8,128)(2,1)S(1)} %collective-permute-done.14.refs_1_, ...), custom_call_target="tpu_custom_call" | custom-call | flops 99999997952 | tf_op jit(solution)/shard_map/pallas_call | solution.py:329
  (53 shorter events, 3.5 us)
Async XLA Ops:
  0.0 81.9 %collective-permute-start.8 = (bf16[384,2048]{1,0:T(8,128)(2,1)}, bf16[384,2048]{1,0:T(8,128)(2,1)}, u32[]{:S(2)}, u32[]{:S(2)}) collective-permute-start(bf16[384,2048]{1,0:T(8,128)(2,1)} %tokens_ref.1), channel_id=1, source_target_pairs={{0,1},{1,0},{2,3},{3,2},{4,5},{5,4},{6,7},{7,6},{8,9},{9,8},{10,11... | collective-permute-start | bytes 4718600 | tf_op jit(solution)/shard_map/ppermute | solution.py:25
  10.8 51.9 %copy-start = (bf16[16,2048]{1,0:T(8,128)(2,1)S(1)}, bf16[16,2048]{1,0:T(8,128)(2,1)}, u32[]{:S(2)}) copy-start(bf16[16,2048]{1,0:T(8,128)(2,1)} %get-tuple-element.63.refs_0_) | copy-start | bytes 196612
  10.9 51.9 %copy-start.1 = (s32[2]{0:T(128)S(1)}, s32[2]{0:T(128)}, u32[]{:S(2)}) copy-start(s32[2]{0:T(128)} %pad_add_fusion.1.ids_ref) | copy-start | bytes 28
  10.9 57.1 %copy-start.2 = (bf16[384,2048]{1,0:T(8,128)(2,1)S(1)}, bf16[384,2048]{1,0:T(8,128)(2,1)}, u32[]{:S(2)}) copy-start(bf16[384,2048]{1,0:T(8,128)(2,1)} %tokens_ref.1) | copy-start | bytes 4718596
  10.9 51.9 %collective-permute-start = (bf16[16,2048]{1,0:T(8,128)(2,1)}, bf16[16,2048]{1,0:T(8,128)(2,1)S(1)}, u32[]{:S(2)}, u32[]{:S(2)}) collective-permute-start(bf16[16,2048]{1,0:T(8,128)(2,1)} %get-tuple-element.57), channel_id=1, source_target_pairs={{0,1},{1,0},{2,3},{3,2},{4,5},{5,4},{6,7},{7,6},{8,9},{9,8},{10,11... | collective-permute-start | bytes 196616 | tf_op jit(solution)/shard_map/ppermute | solution.py:25
  11.0 51.7 %collective-permute-start.1 = (bf16[16,2048]{1,0:T(8,128)(2,1)}, bf16[16,2048]{1,0:T(8,128)(2,1)S(1)}, u32[]{:S(2)}, u32[]{:S(2)}) collective-permute-start(bf16[16,2048]{1,0:T(8,128)(2,1)} %get-tuple-element.58), channel_id=1, source_target_pairs={{0,2},{1,3},{2,0},{3,1},{4,6},{5,7},{6,4},{7,5},{8,10},{9,11},{10,... | collective-permute-start | bytes 196616 | tf_op jit(solution)/shard_map/ppermute | solution.py:25
  13.9 48.8 %collective-permute-start.2 = (bf16[16,2048]{1,0:T(8,128)(2,1)}, bf16[16,2048]{1,0:T(8,128)(2,1)S(1)}, u32[]{:S(2)}, u32[]{:S(2)}) collective-permute-start(bf16[16,2048]{1,0:T(8,128)(2,1)} %get-tuple-element.59), channel_id=1, source_target_pairs={{0,3},{1,2},{2,1},{3,0},{4,7},{5,6},{6,5},{7,4},{8,11},{9,10},{10,... | collective-permute-start | bytes 196616 | tf_op jit(solution)/shard_map/ppermute | solution.py:25
  63.7 14.3 %collective-permute-start.5 = (bf16[64,2048]{1,0:T(8,128)(2,1)S(1)}, bf16[64,2048]{1,0:T(8,128)(2,1)S(1)}, u32[]{:S(2)}, u32[]{:S(2)}) collective-permute-start(bf16[64,2048]{1,0:T(8,128)(2,1)S(1)} %shard_map.66.refs_0_), channel_id=1, source_target_pairs={{0,4},{4,0},{8,12},{12,8},{1,5},{5,1},{9,13},{13,9},{2,6},{6,2},{1... | collective-permute-start | bytes 786440 | tf_op jit(solution)/shard_map/ppermute | solution.py:25
  65.4 15.1 %collective-permute-start.6 = (bf16[64,2048]{1,0:T(8,128)(2,1)S(1)}, bf16[64,2048]{1,0:T(8,128)(2,1)S(1)}, u32[]{:S(2)}, u32[]{:S(2)}) collective-permute-start(bf16[64,2048]{1,0:T(8,128)(2,1)S(1)} %shard_map.66.refs_0_), channel_id=1, source_target_pairs={{0,8},{4,12},{8,0},{12,4},{16,28},{20,24},{24,20},{28,16},{1,9},{5... | collective-permute-start | bytes 786440 | tf_op jit(solution)/shard_map/ppermute | solution.py:273
  80.5 9.4 %collective-permute-start.7 = (bf16[64,2048]{1,0:T(8,128)(2,1)S(1)}, bf16[64,2048]{1,0:T(8,128)(2,1)S(1)}, u32[]{:S(2)}, u32[]{:S(2)}) collective-permute-start(bf16[64,2048]{1,0:T(8,128)(2,1)S(1)} %collective-permute-done.6.refs_2_), channel_id=1, source_target_pairs={{0,16},{16,0},{1,17},{17,1},{2,18},{18,2},{3,19},{19,3},{4,20},{20... | collective-permute-start | bytes 786440 | tf_op jit(solution)/shard_map/ppermute | solution.py:25
  81.9 10.9 %copy-start.11 = (s32[384,1]{0,1:T(1,128)S(1)}, s32[384,1]{0,1:T(1,128)}, u32[]{:S(2)}) copy-start(s32[384,1]{0,1:T(1,128)} %param.7) | copy-start | bytes 4612
  81.9 10.9 %copy-start.13 = (s32[4]{0:T(128)S(1)}, s32[4]{0:T(128)}, u32[]{:S(2)}) copy-start(s32[4]{0:T(128)} %placement_ref.3) | copy-start | bytes 52
  84.8 6.6 %collective-permute-start.10 = (bf16[64,512]{1,0:T(8,128)(2,1)S(1)}, bf16[64,512]{1,0:T(8,128)(2,1)S(1)}, u32[]{:S(2)}, u32[]{:S(2)}) collective-permute-start(bf16[64,512]{1,0:T(8,128)(2,1)S(1)} %bitcast.16), channel_id=1, source_target_pairs={{0,8},{4,12},{8,0},{12,4},{1,9},{5,13},{9,1},{13,5},{2,10},{6,14},... | collective-permute-start | bytes 196616 | tf_op jit(solution)/shard_map/ppermute | solution.py:25
  86.6 6.2 %collective-permute-start.11 = (bf16[64,512]{1,0:T(8,128)(2,1)S(1)}, bf16[64,512]{1,0:T(8,128)(2,1)S(1)}, u32[]{:S(2)}, u32[]{:S(2)}) collective-permute-start(bf16[64,512]{1,0:T(8,128)(2,1)S(1)} %bitcast.17), channel_id=1, source_target_pairs={{0,12},{4,8},{8,4},{12,0},{1,13},{5,9},{9,5},{13,1},{2,14},{6,10},... | collective-permute-start | bytes 196616 | tf_op jit(solution)/shard_map/ppermute | solution.py:25
  87.8 5.0 %collective-permute-start.9 = (bf16[64,512]{1,0:T(8,128)(2,1)S(1)}, bf16[64,512]{1,0:T(8,128)(2,1)S(1)}, u32[]{:S(2)}, u32[]{:S(2)}) collective-permute-start(bf16[64,512]{1,0:T(8,128)(2,1)S(1)} %bitcast.18), channel_id=1, source_target_pairs={{0,4},{4,0},{8,12},{12,8},{1,5},{5,1},{9,13},{13,9},{2,6},{6,2},{1... | collective-permute-start | bytes 196616 | tf_op jit(solution)/shard_map/ppermute | solution.py:25
  88.4 28.9 %collective-permute-start.4 = (bf16[384,1536]{1,0:T(8,128)(2,1)S(1)}, bf16[384,1536]{1,0:T(8,128)(2,1)S(1)}, u32[]{:S(2)}, u32[]{:S(2)}) collective-permute-start(bf16[384,1536]{1,0:T(8,128)(2,1)S(1)} %copy-done.15), channel_id=1, source_target_pairs={{0,2},{1,3},{2,0},{3,1},{4,6},{5,7},{6,4},{7,5},{8,10},{9,11},{10,... | collective-permute-start | bytes 3538952 | tf_op jit(solution)/shard_map/ppermute | solution.py:25
  89.9 33.7 %collective-permute-start.3 = (bf16[384,512]{1,0:T(8,128)(2,1)}, bf16[384,512]{1,0:T(8,128)(2,1)}, u32[]{:S(2)}, u32[]{:S(2)}) collective-permute-start(bf16[384,512]{1,0:T(8,128)(2,1)} %get-tuple-element.69), channel_id=1, source_target_pairs={{0,2},{1,3},{2,0},{3,1},{4,6},{5,7},{6,4},{7,5},{8,10},{9,11},{10,... | collective-permute-start | bytes 1179656 | tf_op jit(solution)/shard_map/ppermute | solution.py:25
  117.3 3.0 %collective-permute-start.13 = (bf16[384,1536]{1,0:T(8,128)(2,1)S(1)}, bf16[384,1536]{1,0:T(8,128)(2,1)S(1)}, u32[]{:S(2)}, u32[]{:S(2)}) collective-permute-start(bf16[384,1536]{1,0:T(8,128)(2,1)S(1)} %collective-permute-done.4.refs_0_), channel_id=1, source_target_pairs={{0,1},{1,0},{2,3},{3,2},{4,5},{5,4},{6,7},{7,6},{8,9},{9,8},{10,11... | collective-permute-start | bytes 3538952 | tf_op jit(solution)/shard_map/ppermute | solution.py:25
  117.3 5.4 %collective-permute-start.12 = (f32[64,384]{1,0:T(8,128)}, f32[64,384]{1,0:T(8,128)}, u32[]{:S(2)}, u32[]{:S(2)}) collective-permute-start(f32[64,384]{1,0:T(8,128)} %shard_map.69), channel_id=1, source_target_pairs={{0,1},{1,0},{2,3},{3,2},{4,5},{5,4},{6,7},{7,6},{8,9},{9,8},{10,11... | collective-permute-start | bytes 294920 | tf_op jit(solution)/shard_map/ppermute | solution.py:25
  120.3 8.6 %copy-start.10 = (bf16[64,512]{1,0:T(8,128)(2,1)S(1)}, bf16[64,512]{1,0:T(8,128)(2,1)}, u32[]{:S(2)}) copy-start(bf16[64,512]{1,0:T(8,128)(2,1)} %copy-done.9) | copy-start | bytes 196612
  120.3 8.6 %copy-start.12 = (s32[384,1]{0,1:T(1,128)S(1)}, s32[384,1]{0,1:T(1,128)}, u32[]{:S(2)}) copy-start(s32[384,1]{0,1:T(1,128)} %param.7) | copy-start | bytes 4612
  120.3 8.6 %copy-start.14 = (s32[4]{0:T(128)S(1)}, s32[4]{0:T(128)}, u32[]{:S(2)}) copy-start(s32[4]{0:T(128)} %placement_ref.3) | copy-start | bytes 52
  123.7 5.3 %collective-permute-start.14 = (bf16[384,512]{1,0:T(8,128)(2,1)}, bf16[384,512]{1,0:T(8,128)(2,1)S(1)}, u32[]{:S(2)}, u32[]{:S(2)}) collective-permute-start(bf16[384,512]{1,0:T(8,128)(2,1)} %collective-permute-done.3.refs_0_), channel_id=1, source_target_pairs={{0,1},{1,0},{2,3},{3,2},{4,5},{5,4},{6,7},{7,6},{8,9},{9,8},{10,11... | collective-permute-start | bytes 1179656 | tf_op jit(solution)/shard_map/ppermute | solution.py:25
  123.9 5.1 %collective-permute-start.15 = (f32[64,384]{1,0:T(8,128)S(1)}, f32[64,384]{1,0:T(8,128)S(1)}, u32[]{:S(2)}, u32[]{:S(2)}) collective-permute-start(f32[64,384]{1,0:T(8,128)S(1)} %add.11.refs_4_), channel_id=1, source_target_pairs={{0,2},{1,3},{2,0},{3,1},{4,6},{5,7},{6,4},{7,5},{8,10},{9,11},{10,... | collective-permute-start | bytes 294920 | tf_op jit(solution)/shard_map/ppermute | solution.py:25
  (8 other events, 46.0 us)

commit v7 on v6

--- a/solution.py
+++ b/solution.py
@@ -11,7 +11,7 @@
 LOWRANK_SCALE = 2.0
 CORES = 2
 LANES = 128
-CUTS = (0.75,)
+CUTS = (0.25, 0.75)
 MIB = 1024 * 1024
 FREE = pl.CostEstimate(flops=0, bytes_accessed=0, transcendentals=0)
 LONG = pl.CostEstimate(flops=10**11, bytes_accessed=0, transcendentals=0)
@@ -57,23 +57,24 @@
     )
 
 
-def slice_kernel(ids_ref, down_ref, *refs):
+def slice_kernel(down_ref, *refs):
     outs, sems = refs[:-1], refs[-1]
-    depth = outs[0].shape[1]
+    me, depth = lax.axis_index("tensor"), outs[0].shape[1]
     run_copies(
         [
-            (down_ref.at[:, pl.ds(pl.multiple_of((ids_ref[0] ^ flip) * depth, LANES), depth)], out)
+            (down_ref.at[:, pl.ds(pl.multiple_of((me ^ flip) * depth, LANES), depth)], out)
             for flip, out in enumerate(outs)
         ],
         sems,
     )
 
 
-def order_kernel(rank_part, ids_ref, *refs):
+def order_kernel(rank_part, *refs):
     pieces, out_ref, sems = refs[:-2], refs[-2], refs[-1]
+    me = lax.axis_index("tensor")
     run_copies(
         [
-            (piece, out_ref.at[pl.ds(pl.multiple_of((ids_ref[0] ^ f) * rank_part, rank_part), rank_part)])
+            (piece, out_ref.at[pl.ds(pl.multiple_of((me ^ f) * rank_part, rank_part), rank_part)])
             for f, piece in enumerate(pieces)
         ],
         sems,
@@ -136,16 +137,17 @@
     )(jnp.stack(starts), weight, *features, *given)
 
 
-def last_kernel(tile, count, slots, starts_ref, ids_ref, placement_ref, weight_ref, *refs):
+def last_kernel(tile, count, slots, starts_ref, placement_ref, weight_ref, *refs):
     features = refs[:count]
     given, tenant_ref, sum_ref, more_ref = refs[count : count + 4]
     ups = refs[count + 4 : count + 4 + slots]
     out_ref, total_ref, held_ref, rows_ref, sems = refs[count + 4 + slots :]
     start_tiles(tile, starts_ref, features, weight_ref, held_ref, rows_ref, sems)
     shrunk = (sum_ref[...] + more_ref[...]).astype(jnp.bfloat16).astype(jnp.float32)
+    group = lax.axis_index("adapter")
     stored = slot_of_row(tenant_ref[...], placement_ref, slots)
     spread = jnp.concatenate(
-        [jnp.where(stored == (ids_ref[1] ^ offset), shrunk, 0.0) for offset in range(slots)], axis=0
+        [jnp.where(stored == (group ^ offset), shrunk, 0.0) for offset in range(slots)], axis=0
     )
     stacked = jnp.concatenate([up[...] for up in ups], axis=0)
     expanded = jnp.dot(
@@ -201,7 +203,6 @@
     me = lax.axis_index("tensor")
     group = lax.axis_index("adapter")
     part = lax.axis_index("parts")
-    ids = jnp.stack([me, group])
     rank, columns = lowrank_up_weight.shape[1:]
     tenant_row = tenant.reshape(1, rows)
     edges = [0] + [int(depth * cut) // LANES * LANES for cut in CUTS] + [depth]
@@ -213,12 +214,12 @@
         pieces = call(
             slice_kernel,
             [jax.ShapeDtypeStruct((down.shape[0], depth), down.dtype)] * tensors,
-            [SCALAR, ANYWHERE],
+            [ANYWHERE],
             [pltpu.SemaphoreType.DMA((tensors,))],
-            [ANYWHERE] * tensors,
+            [VECTOR] * tensors,
             cost=FREE,
             mib=60,
-        )(ids, down)
+        )(down)
     else:
         pieces = [
             lax.dynamic_slice_in_dim(down, (me ^ flip) * depth, depth, axis=1)
@@ -231,20 +232,20 @@
         [jax.ShapeDtypeStruct((rows, b - a), tokens.dtype) for a, b in zip(edges, edges[1:])],
         [ANYWHERE],
         [pltpu.SemaphoreType.DMA((len(edges) - 1,))],
-        [ANYWHERE] * (len(edges) - 1),
+        [VECTOR] * (len(edges) - 1),
+        cost=FREE,
         mib=60,
     )(uncut)
     pieces = [pieces[0]] + [flipped(pieces[f], "tensor", f) for f in range(1, tensors)]
-    pieces, chunks = chained(pieces, chunks)
     if whole_tiles:
         own = call(
             functools.partial(order_kernel, down.shape[0]),
             jax.ShapeDtypeStruct((rank, depth), down.dtype),
-            [SCALAR] + [ANYWHERE] * tensors,
+            [ANYWHERE] * tensors,
             [pltpu.SemaphoreType.DMA((tensors,))],
             ANYWHERE,
             cost=FREE,
-        )(ids, *pieces)
+        )(*pieces)
     else:
         none = jnp.zeros((), down.dtype)
         own = jnp.concatenate(
@@ -253,7 +254,7 @@
         )
 
     hops = range(CORES, tensors, CORES)
-    far = [[flipped(chunks[0], "tensor", hop) for hop in hops]]
+    far = [[flipped(chunk, "tensor", hop) for hop in hops] for chunk in chunks[:2]]
 
     def spread_out(m):
         starts, features = [], []
@@ -275,28 +276,29 @@
 
     own, here = chained(own, tokens)
     total = products(tile, [me * depth], [here], frozen_projection_weight)
-    total, last = chained(total, chunks[1])
+    total, last, up = chained(total, chunks[2], lowrank_up_weight[0])
     far.append([flipped(last, "tensor", hop) for hop in hops])
     for flip, value in singles:
         value, total = chained(value, total)
         downs.append(value)
         owners.append(group ^ flip)
-    up = lowrank_up_weight[0]
+    swaps = []
     for pair, value in fetched:
         value, total = chained(value, total)
-        swapped = flipped(value, "parts", 1)
-        if pair == fetched[0][0]:
-            total, neighbour = chained(total, neighbour)
-            total = products(
-                tile, [(me ^ 1) * depth], [neighbour], frozen_projection_weight, total
-            )
-            total, up = chained(total, up)
+        swaps.append((value, flipped(value, "parts", 1)))
+        mine, other = (jnp.where(part == 0, *order) for order in (pair, pair[::-1]))
+        owners += [group ^ mine, group ^ other]
+    ups = [flipped(up, "adapter", flip) for flip in range(1, groups)]
+    total = products(tile, [(me ^ 1) * depth], [neighbour], frozen_projection_weight, total)
+    starts, features = spread_out(0)
+    features, total = chained(features, total)
+    total = products(tile, starts, features, frozen_projection_weight, total)
+    for value, swapped in swaps:
         swapped, total = chained(swapped, total)
         downs += [value, swapped]
-        mine, other = (jnp.where(part == 0, *order) for order in (pair, pair[::-1]))
-        owners += [group ^ mine, group ^ other]
-    ups = [up] + [flipped(up, "adapter", flip) for flip in range(1, groups)]
-    downs, ups = chained(downs, ups)
+    ups, total = chained(ups, total)
+    ups = [up] + ups
+    far[1], downs, ups = chained(far[1], downs, ups)
 
     tiles = depth // tile
     partial = call(
@@ -310,11 +312,9 @@
             pltpu.SemaphoreType.DMA((1 + slots, tiles)),
         ],
     )(jnp.stack(owners), placement, tokens, tenant_row, *downs)
-    far[0], partial = chained(far[0], partial)
-    starts, features = spread_out(0)
-    total = products(tile, starts[::2], features[::2], frozen_projection_weight, total)
-    near, total = chained(features[1::2], total)
-    total = products(tile, starts[1::2], near, frozen_projection_weight, total)
+    starts, features = spread_out(1)
+    features, partial = chained(features, partial)
+    total = products(tile, starts, features, frozen_projection_weight, total)
     flip = 1
     while flip < tensors // 2:
         received = flipped(partial, "tensor", flip)
@@ -323,18 +323,18 @@
         partial += received
         flip *= 2
     more = flipped(partial, "tensor", flip)
-    far[1], total, partial = chained(far[1], total, partial)
-    starts, features = spread_out(1)
+    far[2], total, partial = chained(far[2], total, partial)
+    starts, features = spread_out(2)
 
     return call(
         functools.partial(last_kernel, tile, len(features), slots),
         jax.ShapeDtypeStruct((rows, columns), jnp.bfloat16),
-        [SCALAR, SCALAR, SCALAR, ANYWHERE]
+        [SCALAR, SCALAR, ANYWHERE]
         + [ANYWHERE] * len(features)
         + [VECTOR] * (4 + slots),
         [pltpu.VMEM((rows, columns), jnp.float32)] + tile_scratch(tile, features, columns),
     )(
-        jnp.stack(starts), ids, placement, frozen_projection_weight, *features, total, tenant_row,
+        jnp.stack(starts), placement, frozen_projection_weight, *features, total, tenant_row,
         partial, more, *ups,
     )
 

time: 133 us -> 61.3 us (0.46)
  Pallas kernels: 75.8 us -> 21.7 us
  waiting for transfers between devices: 37.4 us -> 20.8 us
  other arithmetic: 1.75 us -> 0.32 us
    pallas_call x1, Pallas kernels: 48.8 us -> 2.56 us  [body(): call(functools.partial(cut_kernel, edges), [jax.ShapeDtypeStruct((rows, b...]
    ppermute x15 -> x17, waiting for transfers between devices: 34.9 us -> 19 us  [flipped(): return lax.ppermute(value, axis, [(i, i ^ flip) for i in range(count)])]
    pallas_call x1, Pallas kernels: 9.74 us -> 1.71 us  [body(): call(slice_kernel, [jax.ShapeDtypeStruct((down.shape[0], depth), down.dty...]
    ppermute x15 -> x17, starting transfers between devices: 14.4 us -> 14.6 us  [flipped(): return lax.ppermute(value, axis, [(i, i ^ flip) for i in range(count)])]
  transfers between devices with their start and end apart: 16 -> 18, of which waited for: 7 -> 5; matrix products, arithmetic and copies ran while one was open for 1% -> 1% of each run, Pallas kernels for 55% -> 30%
where the time goes in v7:
time: 61.3 us; the launch traced here: 61 us
  Pallas kernels  21.7 us (35%)
  waiting for transfers between devices  20.8 us (34%)
  starting transfers between devices  17.2 us (28%)
  local copies, waits for them, and re-layouts  0.75 us (1%)
    ppermute x17, waiting for transfers between devices, flipped(): return lax.ppermute(value, axis, [(i, i ^ flip) for i in range(count)])  19 us
    ppermute x17, starting transfers between devices, flipped(): return lax.ppermute(value, axis, [(i, i ^ flip) for i in range(count)])  14.6 us
    pallas_call x4, Pallas kernels, products(): call(functools.partial(products_kernel, tile, len(features), len(given)),...  11 us
    pallas_call x1, Pallas kernels, body(): call(functools.partial(last_kernel, tile, len(features), slots), jax.Shap...  3.66 us
    ppermute x1, starting transfers between devices, body(): fetched.append((pair, lax.ppermute(own, ('parts', 'adapter'), route)))  2.59 us
    pallas_call x1, Pallas kernels, body(): call(functools.partial(cut_kernel, edges), [jax.ShapeDtypeStruct((rows, b...  2.56 us
    pallas_call x1, Pallas kernels, body(): call(functools.partial(shrink_kernel, tile, slots), jax.ShapeDtypeStruct(...  2.44 us
    ppermute x1, waiting for transfers between devices, body(): fetched.append((pair, lax.ppermute(own, ('parts', 'adapter'), route)))  1.8 us
  transfers between devices with their start and end apart: 18, of which 5 were waited for; matrix products, arithmetic and copies ran while one was open for 1% of the time, Pallas kernels for 30%

profile of v7, /device:TPU:0, one launch (start us, length us, event | category | flops | bytes accessed | tf_op | source)
XLA Modules:
  0.0 61.0 jit_solution(3560801294762420421)
XLA Ops:
  0.5 1.7 %shard_map.64 = (bf16[16,2048]{1,0:T(8,128)(2,1)}, bf16[16,2048]{1,0:T(8,128)(2,1)}, bf16[16,2048]{1,0:T(8,128)(2,1)}, bf16[16,2048]{1,0:T(8,128)(2,1)}) custom-call(bf16[16,8192]{1,0:T(8,128)(2,1)} %bitcast.19), custom_call_target="tpu_custom_call" | custom-call | tf_op jit(solution)/shard_map/pallas_call | solution.py:214
  2.4 2.8 %collective-permute-start.1 = (bf16[16,2048]{1,0:T(8,128)(2,1)}, bf16[16,2048]{1,0:T(8,128)(2,1)S(1)}, u32[]{:S(2)}, u32[]{:S(2)}) collective-permute-start(bf16[16,2048]{1,0:T(8,128)(2,1)} %get-tuple-element.57), channel_id=1, source_target_pairs={{0,2},{1,3},{2,0},{3,1},{4,6},{5,7},{6,4},{7,5},{8,10},{9,11},{10,... | collective-permute-start | bytes 196616 | tf_op jit(solution)/shard_map/ppermute | solution.py:25
  5.2 2.6 %shard_map.67 = (bf16[384,512]{1,0:T(8,128)(2,1)}, bf16[384,1024]{1,0:T(8,128)(2,1)}, bf16[384,512]{1,0:T(8,128)(2,1)}) custom-call(bf16[384,2048]{1,0:T(8,128)(2,1)} %tokens_ref.1), custom_call_target="tpu_custom_call" | custom-call | tf_op jit(solution)/shard_map/pallas_call | solution.py:230
  7.8 1.5 %collective-permute-start.8 = (bf16[384,512]{1,0:T(8,128)(2,1)}, bf16[384,512]{1,0:T(8,128)(2,1)}, u32[]{:S(2)}, u32[]{:S(2)}) collective-permute-start(bf16[384,512]{1,0:T(8,128)(2,1)} %get-tuple-element.68), channel_id=1, source_target_pairs={{0,2},{1,3},{2,0},{3,1},{4,6},{5,7},{6,4},{7,5},{8,10},{9,11},{10,... | collective-permute-start | bytes 1179656 | tf_op jit(solution)/shard_map/ppermute | solution.py:25
  9.5 0.6 collective-permute-start.4
  10.5 1.7 %collective-permute-start.5 = (bf16[64,2048]{1,0:T(8,128)(2,1)S(1)}, bf16[64,2048]{1,0:T(8,128)(2,1)S(1)}, u32[]{:S(2)}, u32[]{:S(2)}) collective-permute-start(bf16[64,2048]{1,0:T(8,128)(2,1)S(1)} %shard_map.65.refs_0_), channel_id=1, source_target_pairs={{0,4},{4,0},{8,12},{12,8},{1,5},{5,1},{9,13},{13,9},{2,6},{6,2},{1... | collective-permute-start | bytes 786440 | tf_op jit(solution)/shard_map/ppermute | solution.py:25
  12.2 2.6 %collective-permute-start.6 = (bf16[64,2048]{1,0:T(8,128)(2,1)S(1)}, bf16[64,2048]{1,0:T(8,128)(2,1)S(1)}, u32[]{:S(2)}, u32[]{:S(2)}) collective-permute-start(bf16[64,2048]{1,0:T(8,128)(2,1)S(1)} %shard_map.65.refs_0_), channel_id=1, source_target_pairs={{0,8},{4,12},{8,0},{12,4},{16,28},{20,24},{24,20},{28,16},{1,9},{5... | collective-permute-start | bytes 786440 | tf_op jit(solution)/shard_map/ppermute | solution.py:274
  14.8 2.6 %shard_map.66.refs_1_ = f32[384,512]{1,0:T(8,128)S(1)} custom-call(s32[1]{0:T(128)} %bitcast.2.starts_ref, bf16[8192,512]{1,0:T(8,128)(2,1)} %weight_ref.9, bf16[384,2048]{1,0:T(8,128)(2,1)S(1)} %copy-done), custom_call_target="tpu_custom_call" | custom-call | flops 99999997952 | tf_op jit(solution)/shard_map/pallas_call | solution.py:132
  17.4 6.8 %collective-permute-done.5.refs_1_ = bf16[64,2048]{1,0:T(8,128)(2,1)S(1)} collective-permute-done((bf16[64,2048]{1,0:T(8,128)(2,1)S(1)}, bf16[64,2048]{1,0:T(8,128)(2,1)S(1)}, u32[]{:S(2)}, u32[]{:S(2)}) %collective-permute-start.5) | collective-permute-done | bytes 262176 | tf_op jit(solution)/shard_map/ppermute | solution.py:25
  24.2 0.7 %copy-done.4 = bf16[64,2048]{1,0:T(8,128)(2,1)} copy-done((bf16[64,2048]{1,0:T(8,128)(2,1)}, bf16[64,2048]{1,0:T(8,128)(2,1)S(1)}, u32[]{:S(2)}) %copy-start.4) | copy-done | bytes 262168
  25.0 1.8 %collective-permute-done.6.refs_2_ = bf16[64,2048]{1,0:T(8,128)(2,1)S(1)} collective-permute-done((bf16[64,2048]{1,0:T(8,128)(2,1)S(1)}, bf16[64,2048]{1,0:T(8,128)(2,1)S(1)}, u32[]{:S(2)}, u32[]{:S(2)}) %collective-permute-start.6) | collective-permute-done | bytes 262176 | tf_op jit(solution)/shard_map/ppermute | solution.py:274
  26.8 1.4 %collective-permute-start.12 = (bf16[64,512]{1,0:T(8,128)(2,1)}, bf16[64,512]{1,0:T(8,128)(2,1)}, u32[]{:S(2)}, u32[]{:S(2)}) collective-permute-start(bf16[64,512]{1,0:T(8,128)(2,1)} %bitcast.5.refs_6_), channel_id=1, source_target_pairs={{0,8},{4,12},{8,0},{12,4},{1,9},{5,13},{9,1},{13,5},{2,10},{6,14},... | collective-permute-start | bytes 196616 | tf_op jit(solution)/shard_map/ppermute | solution.py:25
  28.2 1.4 %collective-permute-start.13 = (bf16[64,512]{1,0:T(8,128)(2,1)}, bf16[64,512]{1,0:T(8,128)(2,1)}, u32[]{:S(2)}, u32[]{:S(2)}) collective-permute-start(bf16[64,512]{1,0:T(8,128)(2,1)} %bitcast.5.refs_6_), channel_id=1, source_target_pairs={{0,12},{4,8},{8,4},{12,0},{1,13},{5,9},{9,5},{13,1},{2,14},{6,10},... | collective-permute-start | bytes 196616 | tf_op jit(solution)/shard_map/ppermute | solution.py:25
  29.6 2.6 %shard_map.68.refs_2_ = f32[384,512]{1,0:T(8,128)S(1)} custom-call(s32[1]{0:T(128)} %bitcast.8.starts_ref, bf16[8192,512]{1,0:T(8,128)(2,1)} %weight_ref.9, bf16[384,2048]{1,0:T(8,128)(2,1)S(1)} %collective-permute-done.10.refs_0_, f32[384,512]{1,0:T(8,128)S(1)} %shard_map.66.refs_1_), custom_call_target="tpu_custom_call" | custom-call | flops 99999997952 | tf_op jit(solution)/shard_map/pallas_call | solution.py:132
  32.3 0.9 %collective-permute-start.7 = (bf16[64,2048]{1,0:T(8,128)(2,1)S(1)}, bf16[64,2048]{1,0:T(8,128)(2,1)S(1)}, u32[]{:S(2)}, u32[]{:S(2)}) collective-permute-start(bf16[64,2048]{1,0:T(8,128)(2,1)S(1)} %collective-permute-done.6.refs_2_), channel_id=1, source_target_pairs={{0,16},{16,0},{1,17},{17,1},{2,18},{18,2},{3,19},{19,3},{4,20},{20... | collective-permute-start | bytes 786440 | tf_op jit(solution)/shard_map/ppermute | solution.py:25
  33.1 2.5 %shard_map.69.refs_2_ = f32[384,512]{1,0:T(8,128)S(1)} custom-call(s32[2]{0:T(128)S(1)} %pad_add_fusion.1.starts_ref, bf16[8192,512]{1,0:T(8,128)(2,1)} %weight_ref.9, bf16[384,512]{1,0:T(8,128)(2,1)} %collective-permute-done.8.refs_0_, bf16[384,512]{1,0:T(8,128)(2,1)S(1)} %collective-permute-done.9.refs_1_, f32[384,512]{1,0:T(8,128)S(1)} %shard_map.68.refs_2_), custom_call_target="tpu_custom_call" | custom-call | flops 99999997952 | tf_op jit(solution)/shard_map/pallas_call | solution.py:132
  35.6 5.4 %collective-permute-done.7.refs_3_ = bf16[64,2048]{1,0:T(8,128)(2,1)S(1)} collective-permute-done((bf16[64,2048]{1,0:T(8,128)(2,1)S(1)}, bf16[64,2048]{1,0:T(8,128)(2,1)S(1)}, u32[]{:S(2)}, u32[]{:S(2)}) %collective-permute-start.7) | collective-permute-done | bytes 262176 | tf_op jit(solution)/shard_map/ppermute | solution.py:25
  41.0 1.5 %collective-permute-start.3 = (bf16[384,512]{1,0:T(8,128)(2,1)}, bf16[384,512]{1,0:T(8,128)(2,1)}, u32[]{:S(2)}, u32[]{:S(2)}) collective-permute-start(bf16[384,512]{1,0:T(8,128)(2,1)} %get-tuple-element.62), channel_id=1, source_target_pairs={{0,2},{1,3},{2,0},{3,1},{4,6},{5,7},{6,4},{7,5},{8,10},{9,11},{10,... | collective-permute-start | bytes 1179656 | tf_op jit(solution)/shard_map/ppermute | solution.py:25
  42.7 2.4 %shard_map.70 = f32[64,384]{1,0:T(8,128)S(1)} custom-call(s32[4]{0:T(128)S(1)} %pad_add_fusion.2.owners_ref, s32[4]{0:T(128)S(1)} %copy-done.7, bf16[384,2048]{1,0:T(8,128)(2,1)S(1)} %copy-done, s32[1,384]{1,0:T(1,128)S(1)} %bitcast.17, bf16[64,2048]{1,0:T(8,128)(2,1)S(1)} %copy-done.2, bf16[64,2048]{1,0:T(8,128)(2,1)S(1)} %copy-done.5, ...), custom_call_target="tpu_custom_call" | custom-call | flops 99999997952 | tf_op jit(solution)/shard_map/pallas_call | solution.py:304
  45.7 3.3 %shard_map.71.refs_2_ = f32[384,512]{1,0:T(8,128)S(1)} custom-call(s32[2]{0:T(128)S(1)} %pad_add_fusion.3.starts_ref, bf16[8192,512]{1,0:T(8,128)(2,1)} %weight_ref.9, bf16[384,1024]{1,0:T(8,128)(2,1)} %collective-permute-done.4.refs_0_, bf16[384,1024]{1,0:T(8,128)(2,1)S(1)} %collective-permute-done.14.refs_1_, f32[384,512]{1,0:T(8,128)S(1)} %shard_map.69.refs_2_), custom_call_target="tpu_custom_call" | custom-call | flops 99999997952 | tf_op jit(solution)/shard_map/pallas_call | solution.py:132
  49.0 3.1 %collective-permute-done.3.refs_0_ = bf16[384,512]{1,0:T(8,128)(2,1)} collective-permute-done((bf16[384,512]{1,0:T(8,128)(2,1)}, bf16[384,512]{1,0:T(8,128)(2,1)}, u32[]{:S(2)}, u32[]{:S(2)}) %collective-permute-start.3) | collective-permute-done | bytes 393248 | tf_op jit(solution)/shard_map/ppermute | solution.py:25
  52.1 1.5 %collective-permute-start.17 = (f32[64,384]{1,0:T(8,128)S(1)}, f32[64,384]{1,0:T(8,128)S(1)}, u32[]{:S(2)}, u32[]{:S(2)}) collective-permute-start(f32[64,384]{1,0:T(8,128)S(1)} %add.19.refs_4_), channel_id=1, source_target_pairs={{0,2},{1,3},{2,0},{3,1},{4,6},{5,7},{6,4},{7,5},{8,10},{9,11},{10,... | collective-permute-start | bytes 294920 | tf_op jit(solution)/shard_map/ppermute | solution.py:25
  53.7 3.6 %collective-permute-done.17.refs_5_ = f32[64,384]{1,0:T(8,128)S(1)} collective-permute-done((f32[64,384]{1,0:T(8,128)S(1)}, f32[64,384]{1,0:T(8,128)S(1)}, u32[]{:S(2)}, u32[]{:S(2)}) %collective-permute-start.17) | collective-permute-done | bytes 98336 | tf_op jit(solution)/shard_map/ppermute | solution.py:25
  57.3 3.7 %shard_map.72 = bf16[384,512]{1,0:T(8,128)(2,1)} custom-call(s32[2]{0:T(128)S(1)} %pad_add_fusion.starts_ref, s32[4]{0:T(128)S(1)} %copy-done.7, bf16[8192,512]{1,0:T(8,128)(2,1)} %weight_ref.9, bf16[384,512]{1,0:T(8,128)(2,1)} %collective-permute-done.3.refs_0_, bf16[384,512]{1,0:T(8,128)(2,1)S(1)} %collective-permute-done.16.refs_1_, ...), custom_call_target="tpu_custom_call" | custom-call | flops 99999997952 | tf_op jit(solution)/shard_map/pallas_call | solution.py:329
  (42 shorter events, 2.1 us)
Async XLA Ops:
  0.0 14.8 %copy-start = (bf16[384,2048]{1,0:T(8,128)(2,1)S(1)}, bf16[384,2048]{1,0:T(8,128)(2,1)}, u32[]{:S(2)}) copy-start(bf16[384,2048]{1,0:T(8,128)(2,1)} %tokens_ref.1) | copy-start | bytes 4718596
  0.0 29.6 %collective-permute-start.10 = (bf16[384,2048]{1,0:T(8,128)(2,1)}, bf16[384,2048]{1,0:T(8,128)(2,1)S(1)}, u32[]{:S(2)}, u32[]{:S(2)}) collective-permute-start(bf16[384,2048]{1,0:T(8,128)(2,1)} %tokens_ref.1), channel_id=1, source_target_pairs={{0,1},{1,0},{2,3},{3,2},{4,5},{5,4},{6,7},{7,6},{8,9},{9,8},{10,11... | collective-permute-start | bytes 4718600 | tf_op jit(solution)/shard_map/ppermute | solution.py:25
  2.2 7.9 %copy-start.3 = (bf16[16,2048]{1,0:T(8,128)(2,1)S(1)}, bf16[16,2048]{1,0:T(8,128)(2,1)}, u32[]{:S(2)}) copy-start(bf16[16,2048]{1,0:T(8,128)(2,1)} %get-tuple-element.55.refs_0_) | copy-start | bytes 196612
  2.2 7.4 %collective-permute-start = (bf16[16,2048]{1,0:T(8,128)(2,1)}, bf16[16,2048]{1,0:T(8,128)(2,1)S(1)}, u32[]{:S(2)}, u32[]{:S(2)}) collective-permute-start(bf16[16,2048]{1,0:T(8,128)(2,1)} %get-tuple-element.56), channel_id=1, source_target_pairs={{0,1},{1,0},{2,3},{3,2},{4,5},{5,4},{6,7},{7,6},{8,9},{9,8},{10,11... | collective-permute-start | bytes 196616 | tf_op jit(solution)/shard_map/ppermute | solution.py:25
  2.4 7.7 %collective-permute-start.1 = (bf16[16,2048]{1,0:T(8,128)(2,1)}, bf16[16,2048]{1,0:T(8,128)(2,1)S(1)}, u32[]{:S(2)}, u32[]{:S(2)}) collective-permute-start(bf16[16,2048]{1,0:T(8,128)(2,1)} %get-tuple-element.57), channel_id=1, source_target_pairs={{0,2},{1,3},{2,0},{3,1},{4,6},{5,7},{6,4},{7,5},{8,10},{9,11},{10,... | collective-permute-start | bytes 196616 | tf_op jit(solution)/shard_map/ppermute | solution.py:25
  5.2 4.9 %collective-permute-start.2 = (bf16[16,2048]{1,0:T(8,128)(2,1)}, bf16[16,2048]{1,0:T(8,128)(2,1)S(1)}, u32[]{:S(2)}, u32[]{:S(2)}) collective-permute-start(bf16[16,2048]{1,0:T(8,128)(2,1)} %get-tuple-element.58), channel_id=1, source_target_pairs={{0,3},{1,2},{2,1},{3,0},{4,7},{5,6},{6,5},{7,4},{8,11},{9,10},{10,... | collective-permute-start | bytes 196616 | tf_op jit(solution)/shard_map/ppermute | solution.py:25
  7.8 20.4 %collective-permute-start.8 = (bf16[384,512]{1,0:T(8,128)(2,1)}, bf16[384,512]{1,0:T(8,128)(2,1)}, u32[]{:S(2)}, u32[]{:S(2)}) collective-permute-start(bf16[384,512]{1,0:T(8,128)(2,1)} %get-tuple-element.68), channel_id=1, source_target_pairs={{0,2},{1,3},{2,0},{3,1},{4,6},{5,7},{6,4},{7,5},{8,10},{9,11},{10,... | collective-permute-start | bytes 1179656 | tf_op jit(solution)/shard_map/ppermute | solution.py:25
  9.5 33.1 %collective-permute-start.4 = (bf16[384,1024]{1,0:T(8,128)(2,1)}, bf16[384,1024]{1,0:T(8,128)(2,1)}, u32[]{:S(2)}, u32[]{:S(2)}) collective-permute-start(bf16[384,1024]{1,0:T(8,128)(2,1)} %get-tuple-element.63), channel_id=1, source_target_pairs={{0,2},{1,3},{2,0},{3,1},{4,6},{5,7},{6,4},{7,5},{8,10},{9,11},{10,... | collective-permute-start | bytes 2359304 | tf_op jit(solution)/shard_map/ppermute | solution.py:25
  10.5 13.7 %collective-permute-start.5 = (bf16[64,2048]{1,0:T(8,128)(2,1)S(1)}, bf16[64,2048]{1,0:T(8,128)(2,1)S(1)}, u32[]{:S(2)}, u32[]{:S(2)}) collective-permute-start(bf16[64,2048]{1,0:T(8,128)(2,1)S(1)} %shard_map.65.refs_0_), channel_id=1, source_target_pairs={{0,4},{4,0},{8,12},{12,8},{1,5},{5,1},{9,13},{13,9},{2,6},{6,2},{1... | collective-permute-start | bytes 786440 | tf_op jit(solution)/shard_map/ppermute | solution.py:25
  12.2 14.6 %collective-permute-start.6 = (bf16[64,2048]{1,0:T(8,128)(2,1)S(1)}, bf16[64,2048]{1,0:T(8,128)(2,1)S(1)}, u32[]{:S(2)}, u32[]{:S(2)}) collective-permute-start(bf16[64,2048]{1,0:T(8,128)(2,1)S(1)} %shard_map.65.refs_0_), channel_id=1, source_target_pairs={{0,8},{4,12},{8,0},{12,4},{16,28},{20,24},{24,20},{28,16},{1,9},{5... | collective-permute-start | bytes 786440 | tf_op jit(solution)/shard_map/ppermute | solution.py:274
  25.0 17.6 %collective-permute-start.11 = (bf16[64,512]{1,0:T(8,128)(2,1)}, bf16[64,512]{1,0:T(8,128)(2,1)}, u32[]{:S(2)}, u32[]{:S(2)}) collective-permute-start(bf16[64,512]{1,0:T(8,128)(2,1)} %bitcast.5.refs_6_), channel_id=1, source_target_pairs={{0,4},{4,0},{8,12},{12,8},{1,5},{5,1},{9,13},{13,9},{2,6},{6,2},{1... | collective-permute-start | bytes 196616 | tf_op jit(solution)/shard_map/ppermute | solution.py:25
  26.8 15.8 %collective-permute-start.12 = (bf16[64,512]{1,0:T(8,128)(2,1)}, bf16[64,512]{1,0:T(8,128)(2,1)}, u32[]{:S(2)}, u32[]{:S(2)}) collective-permute-start(bf16[64,512]{1,0:T(8,128)(2,1)} %bitcast.5.refs_6_), channel_id=1, source_target_pairs={{0,8},{4,12},{8,0},{12,4},{1,9},{5,13},{9,1},{13,5},{2,10},{6,14},... | collective-permute-start | bytes 196616 | tf_op jit(solution)/shard_map/ppermute | solution.py:25
  28.2 14.4 %collective-permute-start.13 = (bf16[64,512]{1,0:T(8,128)(2,1)}, bf16[64,512]{1,0:T(8,128)(2,1)}, u32[]{:S(2)}, u32[]{:S(2)}) collective-permute-start(bf16[64,512]{1,0:T(8,128)(2,1)} %bitcast.5.refs_6_), channel_id=1, source_target_pairs={{0,12},{4,8},{8,4},{12,0},{1,13},{5,9},{9,5},{13,1},{2,14},{6,10},... | collective-permute-start | bytes 196616 | tf_op jit(solution)/shard_map/ppermute | solution.py:25
  29.6 2.7 %collective-permute-start.9 = (bf16[384,512]{1,0:T(8,128)(2,1)}, bf16[384,512]{1,0:T(8,128)(2,1)S(1)}, u32[]{:S(2)}, u32[]{:S(2)}) collective-permute-start(bf16[384,512]{1,0:T(8,128)(2,1)} %collective-permute-done.8.refs_0_), channel_id=1, source_target_pairs={{0,1},{1,0},{2,3},{3,2},{4,5},{5,4},{6,7},{7,6},{8,9},{9,8},{10,11... | collective-permute-start | bytes 1179656 | tf_op jit(solution)/shard_map/ppermute | solution.py:25
  32.2 10.5 %copy-start.2 = (bf16[64,2048]{1,0:T(8,128)(2,1)S(1)}, bf16[64,2048]{1,0:T(8,128)(2,1)}, u32[]{:S(2)}) copy-start(bf16[64,2048]{1,0:T(8,128)(2,1)} %copy-done.1) | copy-start | bytes 786436
  32.2 10.5 %copy-start.5 = (bf16[64,2048]{1,0:T(8,128)(2,1)S(1)}, bf16[64,2048]{1,0:T(8,128)(2,1)}, u32[]{:S(2)}) copy-start(bf16[64,2048]{1,0:T(8,128)(2,1)} %copy-done.4) | copy-start | bytes 786436
  32.2 10.5 %copy-start.6 = (s32[384,1]{0,1:T(1,128)S(1)}, s32[384,1]{0,1:T(1,128)}, u32[]{:S(2)}) copy-start(s32[384,1]{0,1:T(1,128)} %param.7) | copy-start | bytes 4612
  32.2 10.5 %copy-start.7 = (s32[4]{0:T(128)S(1)}, s32[4]{0:T(128)}, u32[]{:S(2)}) copy-start(s32[4]{0:T(128)} %placement_ref.3) | copy-start | bytes 52
  32.3 8.8 %collective-permute-start.7 = (bf16[64,2048]{1,0:T(8,128)(2,1)S(1)}, bf16[64,2048]{1,0:T(8,128)(2,1)S(1)}, u32[]{:S(2)}, u32[]{:S(2)}) collective-permute-start(bf16[64,2048]{1,0:T(8,128)(2,1)S(1)} %collective-permute-done.6.refs_2_), channel_id=1, source_target_pairs={{0,16},{16,0},{1,17},{17,1},{2,18},{18,2},{3,19},{19,3},{4,20},{20... | collective-permute-start | bytes 786440 | tf_op jit(solution)/shard_map/ppermute | solution.py:25
  41.0 11.1 %collective-permute-start.3 = (bf16[384,512]{1,0:T(8,128)(2,1)}, bf16[384,512]{1,0:T(8,128)(2,1)}, u32[]{:S(2)}, u32[]{:S(2)}) collective-permute-start(bf16[384,512]{1,0:T(8,128)(2,1)} %get-tuple-element.62), channel_id=1, source_target_pairs={{0,2},{1,3},{2,0},{3,1},{4,6},{5,7},{6,4},{7,5},{8,10},{9,11},{10,... | collective-permute-start | bytes 1179656 | tf_op jit(solution)/shard_map/ppermute | solution.py:25
  42.6 2.6 %collective-permute-start.14 = (bf16[384,1024]{1,0:T(8,128)(2,1)}, bf16[384,1024]{1,0:T(8,128)(2,1)S(1)}, u32[]{:S(2)}, u32[]{:S(2)}) collective-permute-start(bf16[384,1024]{1,0:T(8,128)(2,1)} %collective-permute-done.4.refs_0_), channel_id=1, source_target_pairs={{0,1},{1,0},{2,3},{3,2},{4,5},{5,4},{6,7},{7,6},{8,9},{9,8},{10,11... | collective-permute-start | bytes 2359304 | tf_op jit(solution)/shard_map/ppermute | solution.py:25
  45.2 3.8 %collective-permute-start.15 = (f32[64,384]{1,0:T(8,128)S(1)}, f32[64,384]{1,0:T(8,128)S(1)}, u32[]{:S(2)}, u32[]{:S(2)}) collective-permute-start(f32[64,384]{1,0:T(8,128)S(1)} %shard_map.70), channel_id=1, source_target_pairs={{0,1},{1,0},{2,3},{3,2},{4,5},{5,4},{6,7},{7,6},{8,9},{9,8},{10,11... | collective-permute-start | bytes 294920 | tf_op jit(solution)/shard_map/ppermute | solution.py:25
  52.1 5.2 %collective-permute-start.16 = (bf16[384,512]{1,0:T(8,128)(2,1)}, bf16[384,512]{1,0:T(8,128)(2,1)S(1)}, u32[]{:S(2)}, u32[]{:S(2)}) collective-permute-start(bf16[384,512]{1,0:T(8,128)(2,1)} %collective-permute-done.3.refs_0_), channel_id=1, source_target_pairs={{0,1},{1,0},{2,3},{3,2},{4,5},{5,4},{6,7},{7,6},{8,9},{9,8},{10,11... | collective-permute-start | bytes 1179656 | tf_op jit(solution)/shard_map/ppermute | solution.py:25
  52.1 5.2 %collective-permute-start.17 = (f32[64,384]{1,0:T(8,128)S(1)}, f32[64,384]{1,0:T(8,128)S(1)}, u32[]{:S(2)}, u32[]{:S(2)}) collective-permute-start(f32[64,384]{1,0:T(8,128)S(1)} %add.19.refs_4_), channel_id=1, source_target_pairs={{0,2},{1,3},{2,0},{3,1},{4,6},{5,7},{6,4},{7,5},{8,10},{9,11},{10,... | collective-permute-start | bytes 294920 | tf_op jit(solution)/shard_map/ppermute | solution.py:25
  (2 other events, 7.6 us)

commit v8 on v7

--- a/solution.py
+++ b/solution.py
@@ -11,7 +11,7 @@
 LOWRANK_SCALE = 2.0
 CORES = 2
 LANES = 128
-CUTS = (0.25, 0.75)
+CUTS = (0.75,)
 MIB = 1024 * 1024
 FREE = pl.CostEstimate(flops=0, bytes_accessed=0, transcendentals=0)
 LONG = pl.CostEstimate(flops=10**11, bytes_accessed=0, transcendentals=0)
@@ -137,17 +137,16 @@
     )(jnp.stack(starts), weight, *features, *given)
 
 
-def last_kernel(tile, count, slots, starts_ref, placement_ref, weight_ref, *refs):
+def last_kernel(tile, count, slots, starts_ref, owners_ref, placement_ref, weight_ref, *refs):
     features = refs[:count]
     given, tenant_ref, sum_ref, more_ref = refs[count : count + 4]
     ups = refs[count + 4 : count + 4 + slots]
     out_ref, total_ref, held_ref, rows_ref, sems = refs[count + 4 + slots :]
     start_tiles(tile, starts_ref, features, weight_ref, held_ref, rows_ref, sems)
     shrunk = (sum_ref[...] + more_ref[...]).astype(jnp.bfloat16).astype(jnp.float32)
-    group = lax.axis_index("adapter")
     stored = slot_of_row(tenant_ref[...], placement_ref, slots)
     spread = jnp.concatenate(
-        [jnp.where(stored == (group ^ offset), shrunk, 0.0) for offset in range(slots)], axis=0
+        [jnp.where(stored == owners_ref[b], shrunk, 0.0) for b in range(slots)], axis=0
     )
     stacked = jnp.concatenate([up[...] for up in ups], axis=0)
     expanded = jnp.dot(
@@ -254,7 +253,7 @@
         )
 
     hops = range(CORES, tensors, CORES)
-    far = [[flipped(chunk, "tensor", hop) for hop in hops] for chunk in chunks[:2]]
+    far = [[flipped(chunk, "tensor", hop) for hop in hops] for chunk in chunks]
 
     def spread_out(m):
         starts, features = [], []
@@ -263,42 +262,43 @@
             starts += [(me ^ hop) * depth + edges[m], (me ^ hop ^ 1) * depth + edges[m]]
         return starts, features
 
-    downs, owners, fetched = [own], [group], []
     flips = list(range(1, groups))
+    pairs = []
     if parts == 2:
         while len(flips) > 1:
-            pair = (flips.pop(-2), flips.pop(-1))
-            route = [
-                (p * groups + z, p * groups + (z ^ pair[p])) for p in range(parts) for z in range(groups)
-            ]
-            fetched.append((pair, lax.ppermute(own, ("parts", "adapter"), route)))
-    singles = [(flip, flipped(own, "adapter", flip)) for flip in flips]
-
-    own, here = chained(own, tokens)
+            pairs.append((flips.pop(-2), flips.pop(-1)))
+    routes = [
+        [(p * groups + z, p * groups + (z ^ pair[p])) for p in range(parts) for z in range(groups)]
+        for pair in pairs
+    ]
+
+    def fetch(value):
+        single = [flipped(value, "adapter", flip) for flip in flips]
+        return single, [lax.ppermute(value, ("parts", "adapter"), route) for route in routes]
+
+    owners = [group] + [group ^ flip for flip in flips]
+    for pair in pairs:
+        owners += [
+            group ^ jnp.where(part == 0, *pair), group ^ jnp.where(part == 0, pair[1], pair[0])
+        ]
+    own, neighbour, here = chained(own, neighbour, tokens)
+    single, fetched = fetch(own)
     total = products(tile, [me * depth], [here], frozen_projection_weight)
-    total, last, up = chained(total, chunks[2], lowrank_up_weight[0])
-    far.append([flipped(last, "tensor", hop) for hop in hops])
-    for flip, value in singles:
-        value, total = chained(value, total)
-        downs.append(value)
-        owners.append(group ^ flip)
-    swaps = []
-    for pair, value in fetched:
-        value, total = chained(value, total)
-        swaps.append((value, flipped(value, "parts", 1)))
-        mine, other = (jnp.where(part == 0, *order) for order in (pair, pair[::-1]))
-        owners += [group ^ mine, group ^ other]
-    ups = [flipped(up, "adapter", flip) for flip in range(1, groups)]
+    total, up = chained(total, lowrank_up_weight[0])
+    single_up, fetched_up = fetch(up)
+    single, fetched, total = chained(single, fetched, total)
+    swapped = [flipped(value, "parts", 1) for value in fetched]
+    total, neighbour = chained(total, neighbour)
     total = products(tile, [(me ^ 1) * depth], [neighbour], frozen_projection_weight, total)
-    starts, features = spread_out(0)
-    features, total = chained(features, total)
-    total = products(tile, starts, features, frozen_projection_weight, total)
-    for value, swapped in swaps:
-        swapped, total = chained(swapped, total)
-        downs += [value, swapped]
-    ups, total = chained(ups, total)
-    ups = [up] + ups
-    far[1], downs, ups = chained(far[1], downs, ups)
+    single_up, fetched_up, total = chained(single_up, fetched_up, total)
+    swapped_up = [flipped(value, "parts", 1) for value in fetched_up]
+    downs, ups = [own] + single, [up] + single_up
+    for i in range(len(pairs)):
+        downs += [fetched[i], swapped[i]]
+        ups += [fetched_up[i], swapped_up[i]]
+    far[0], downs, ups = chained(far[0], downs, ups)
+
+    owners = jnp.stack(owners)
 
     tiles = depth // tile
     partial = call(
@@ -311,10 +311,10 @@
             pltpu.VMEM((rows, slots * rank), jnp.float32),
             pltpu.SemaphoreType.DMA((1 + slots, tiles)),
         ],
-    )(jnp.stack(owners), placement, tokens, tenant_row, *downs)
-    starts, features = spread_out(1)
-    features, partial = chained(features, partial)
-    total = products(tile, starts, features, frozen_projection_weight, total)
+    )(owners, placement, tokens, tenant_row, *downs)
+    starts, features = spread_out(0)
+    partial, total = chained(partial, total)
+    total = products(tile, starts[::2], features[::2], frozen_projection_weight, total)
     flip = 1
     while flip < tensors // 2:
         received = flipped(partial, "tensor", flip)
@@ -323,18 +323,27 @@
         partial += received
         flip *= 2
     more = flipped(partial, "tensor", flip)
-    far[2], total, partial = chained(far[2], total, partial)
-    starts, features = spread_out(2)
+    far[1], partial = chained(far[1], partial)
+    last_starts, last = spread_out(1)
+    total = products(
+        tile,
+        starts[1::2] + last_starts[::2],
+        features[1::2] + last[::2],
+        frozen_projection_weight,
+        total,
+    )
+    starts = last_starts[1::2]
+    features, more, total = chained(last[1::2], more, total)
 
     return call(
         functools.partial(last_kernel, tile, len(features), slots),
         jax.ShapeDtypeStruct((rows, columns), jnp.bfloat16),
-        [SCALAR, SCALAR, ANYWHERE]
+        [SCALAR, SCALAR, SCALAR, ANYWHERE]
         + [ANYWHERE] * len(features)
         + [VECTOR] * (4 + slots),
         [pltpu.VMEM((rows, columns), jnp.float32)] + tile_scratch(tile, features, columns),
     )(
-        jnp.stack(starts), placement, frozen_projection_weight, *features, total, tenant_row,
+        jnp.stack(starts), owners, placement, frozen_projection_weight, *features, total, tenant_row,
         partial, more, *ups,
     )
 

time: 61.3 us -> 51.5 us (0.84)
  waiting for transfers between devices: 20.8 us -> 15.2 us
  starting transfers between devices: 17.2 us -> 14.5 us
  Pallas kernels: 21.7 us -> 20.8 us
  local copies, waits for them, and re-layouts: 0.75 us -> 0.07 us
    ppermute x17 -> x14, waiting for transfers between devices: 19 us -> 10.5 us  [flipped(): return lax.ppermute(value, axis, [(i, i ^ flip) for i in range(count)])]
    ppermute x17 -> x14, starting transfers between devices: 14.6 us -> 11.6 us  [flipped(): return lax.ppermute(value, axis, [(i, i ^ flip) for i in range(count)])]
    ppermute x1 -> x2, waiting for transfers between devices: 1.8 us -> 4.69 us  [fetch(): lax.ppermute(value, ('parts', 'adapter'), route)]
    pallas_call x1, Pallas kernels: 3.66 us -> 2.96 us  [body(): call(functools.partial(last_kernel, tile, len(features), slots), jax.Shap...]
    unnamed x16 -> x32, local copies, waits for them, and re-layouts: 0.75 us -> 0.07 us
    ppermute x1 -> x2, starting transfers between devices: 2.59 us -> 2.99 us  [fetch(): lax.ppermute(value, ('parts', 'adapter'), route)]
  transfers between devices with their start and end apart: 18 -> 16, of which waited for: 5 -> 4; matrix products, arithmetic and copies ran while one was open for 1% -> 0% of each run, Pallas kernels for 30% -> 35%
where the time goes in v8:
time: 51.5 us; the launch traced here: 51.1 us
  Pallas kernels  20.8 us (40%)
  waiting for transfers between devices  15.2 us (30%)
  starting transfers between devices  14.5 us (28%)
    ppermute x14, starting transfers between devices, flipped(): return lax.ppermute(value, axis, [(i, i ^ flip) for i in range(count)])  11.6 us
    pallas_call x4, Pallas kernels, products(): call(functools.partial(products_kernel, tile, len(features), len(given)),...  10.8 us
    ppermute x14, waiting for transfers between devices, flipped(): return lax.ppermute(value, axis, [(i, i ^ flip) for i in range(count)])  10.5 us
    ppermute x2, waiting for transfers between devices, fetch(): lax.ppermute(value, ('parts', 'adapter'), route)  4.69 us
    ppermute x2, starting transfers between devices, fetch(): lax.ppermute(value, ('parts', 'adapter'), route)  2.99 us
    pallas_call x1, Pallas kernels, body(): call(functools.partial(last_kernel, tile, len(features), slots), jax.Shap...  2.96 us
    pallas_call x1, Pallas kernels, body(): call(functools.partial(cut_kernel, edges), [jax.ShapeDtypeStruct((rows, b...  2.5 us
    pallas_call x1, Pallas kernels, body(): call(functools.partial(shrink_kernel, tile, slots), jax.ShapeDtypeStruct(...  2.43 us
  transfers between devices with their start and end apart: 16, of which 4 were waited for; matrix products, arithmetic and copies ran while one was open for 0% of the time, Pallas kernels for 35%

profile of v8, /device:TPU:0, one launch (start us, length us, event | category | flops | bytes accessed | tf_op | source)
XLA Modules:
  0.0 51.1 jit_solution(3388115901025333037)
XLA Ops:
  0.0 0.5 collective-permute-start.5
  0.5 1.7 %shard_map.64 = (bf16[16,2048]{1,0:T(8,128)(2,1)}, bf16[16,2048]{1,0:T(8,128)(2,1)}, bf16[16,2048]{1,0:T(8,128)(2,1)}, bf16[16,2048]{1,0:T(8,128)(2,1)}) custom-call(bf16[16,8192]{1,0:T(8,128)(2,1)} %bitcast.20), custom_call_target="tpu_custom_call" | custom-call | tf_op jit(solution)/shard_map/pallas_call | solution.py:213
  2.2 0.2 collective-permute-start.2
  2.4 2.8 %collective-permute-start.3 = (bf16[16,2048]{1,0:T(8,128)(2,1)}, bf16[16,2048]{1,0:T(8,128)(2,1)S(1)}, u32[]{:S(2)}, u32[]{:S(2)}) collective-permute-start(bf16[16,2048]{1,0:T(8,128)(2,1)} %get-tuple-element.56), channel_id=1, source_target_pairs={{0,2},{1,3},{2,0},{3,1},{4,6},{5,7},{6,4},{7,5},{8,10},{9,11},{10,... | collective-permute-start | bytes 196616 | tf_op jit(solution)/shard_map/ppermute | solution.py:25
  5.2 2.5 %shard_map.65 = (bf16[384,1536]{1,0:T(8,128)(2,1)}, bf16[384,512]{1,0:T(8,128)(2,1)}) custom-call(bf16[384,2048]{1,0:T(8,128)(2,1)} %tokens_ref.1), custom_call_target="tpu_custom_call" | custom-call | tf_op jit(solution)/shard_map/pallas_call | solution.py:229
  7.7 1.5 %collective-permute-start.1 = (bf16[384,1536]{1,0:T(8,128)(2,1)}, bf16[384,1536]{1,0:T(8,128)(2,1)}, u32[]{:S(2)}, u32[]{:S(2)}) collective-permute-start(bf16[384,1536]{1,0:T(8,128)(2,1)} %get-tuple-element.53), channel_id=1, source_target_pairs={{0,2},{1,3},{2,0},{3,1},{4,6},{5,7},{6,4},{7,5},{8,10},{9,11},{10,... | collective-permute-start | bytes 3538952 | tf_op jit(solution)/shard_map/ppermute | solution.py:25
  9.3 0.6 %collective-permute-start = (bf16[384,512]{1,0:T(8,128)(2,1)}, bf16[384,512]{1,0:T(8,128)(2,1)}, u32[]{:S(2)}, u32[]{:S(2)}) collective-permute-start(bf16[384,512]{1,0:T(8,128)(2,1)} %get-tuple-element.52), channel_id=1, source_target_pairs={{0,2},{1,3},{2,0},{3,1},{4,6},{5,7},{6,4},{7,5},{8,10},{9,11},{10,... | collective-permute-start | bytes 1179656 | tf_op jit(solution)/shard_map/ppermute | solution.py:25
  9.9 0.4 shard_map.66.refs_0_
  10.3 1.7 %collective-permute-start.6 = (bf16[64,2048]{1,0:T(8,128)(2,1)S(1)}, bf16[64,2048]{1,0:T(8,128)(2,1)S(1)}, u32[]{:S(2)}, u32[]{:S(2)}) collective-permute-start(bf16[64,2048]{1,0:T(8,128)(2,1)S(1)} %shard_map.66.refs_0_), channel_id=1, source_target_pairs={{0,4},{4,0},{8,12},{12,8},{1,5},{5,1},{9,13},{13,9},{2,6},{6,2},{1... | collective-permute-start | bytes 786440 | tf_op jit(solution)/shard_map/ppermute | solution.py:25
  12.0 2.6 %collective-permute-start.7 = (bf16[64,2048]{1,0:T(8,128)(2,1)S(1)}, bf16[64,2048]{1,0:T(8,128)(2,1)S(1)}, u32[]{:S(2)}, u32[]{:S(2)}) collective-permute-start(bf16[64,2048]{1,0:T(8,128)(2,1)S(1)} %shard_map.66.refs_0_), channel_id=1, source_target_pairs={{0,8},{4,12},{8,0},{12,4},{16,28},{20,24},{24,20},{28,16},{1,9},{5... | collective-permute-start | bytes 786440 | tf_op jit(solution)/shard_map/ppermute | solution.py:277
  14.6 2.6 %shard_map.67.refs_1_ = f32[384,512]{1,0:T(8,128)S(1)} custom-call(s32[1]{0:T(128)} %bitcast.8.starts_ref, bf16[8192,512]{1,0:T(8,128)(2,1)} %weight_ref.9, bf16[384,2048]{1,0:T(8,128)(2,1)S(1)} %copy-done), custom_call_target="tpu_custom_call" | custom-call | flops 99999997952 | tf_op jit(solution)/shard_map/pallas_call | solution.py:132
  17.2 0.4 collective-permute-start.10
  17.6 6.4 %collective-permute-done.6.refs_1_ = bf16[64,2048]{1,0:T(8,128)(2,1)S(1)} collective-permute-done((bf16[64,2048]{1,0:T(8,128)(2,1)S(1)}, bf16[64,2048]{1,0:T(8,128)(2,1)S(1)}, u32[]{:S(2)}, u32[]{:S(2)}) %collective-permute-start.6) | collective-permute-done | bytes 262176 | tf_op jit(solution)/shard_map/ppermute | solution.py:25
  24.1 4.7 %collective-permute-done.7.refs_2_ = bf16[64,2048]{1,0:T(8,128)(2,1)S(1)} collective-permute-done((bf16[64,2048]{1,0:T(8,128)(2,1)S(1)}, bf16[64,2048]{1,0:T(8,128)(2,1)S(1)}, u32[]{:S(2)}, u32[]{:S(2)}) %collective-permute-start.7) | collective-permute-done | bytes 262176 | tf_op jit(solution)/shard_map/ppermute | solution.py:277
  28.8 2.6 %shard_map.68.refs_1_ = f32[384,512]{1,0:T(8,128)S(1)} custom-call(s32[1]{0:T(128)} %bitcast.10.starts_ref, bf16[8192,512]{1,0:T(8,128)(2,1)} %weight_ref.9, bf16[384,2048]{1,0:T(8,128)(2,1)S(1)} %collective-permute-done.5.refs_0_, f32[384,512]{1,0:T(8,128)S(1)} %shard_map.67.refs_1_), custom_call_target="tpu_custom_call" | custom-call | flops 99999997952 | tf_op jit(solution)/shard_map/pallas_call | solution.py:132
  31.5 2.1 %collective-permute-start.11 = (bf16[64,512]{1,0:T(8,128)(2,1)S(1)}, bf16[64,512]{1,0:T(8,128)(2,1)S(1)}, u32[]{:S(2)}, u32[]{:S(2)}) collective-permute-start(bf16[64,512]{1,0:T(8,128)(2,1)S(1)} %collective-permute-done.10.refs_7_), channel_id=1, source_target_pairs={{0,16},{16,0},{1,17},{17,1},{2,18},{18,2},{3,19},{19,3},{4,20},{20... | collective-permute-start | bytes 196616 | tf_op jit(solution)/shard_map/ppermute | solution.py:25
  33.6 3.3 %collective-permute-done.1.refs_0_ = bf16[384,1536]{1,0:T(8,128)(2,1)} collective-permute-done((bf16[384,1536]{1,0:T(8,128)(2,1)}, bf16[384,1536]{1,0:T(8,128)(2,1)}, u32[]{:S(2)}, u32[]{:S(2)}) %collective-permute-start.1) | collective-permute-done | bytes 1179680 | tf_op jit(solution)/shard_map/ppermute | solution.py:25
  37.0 2.4 %shard_map.69 = f32[64,384]{1,0:T(8,128)S(1)} custom-call(s32[4]{0:T(128)S(1)} %pad_add_fusion.owners_ref, s32[4]{0:T(128)S(1)} %copy-done.14, bf16[384,2048]{1,0:T(8,128)(2,1)S(1)} %copy-done, s32[1,384]{1,0:T(1,128)S(1)} %bitcast.18, bf16[64,2048]{1,0:T(8,128)(2,1)S(1)} %shard_map.66.refs_0_, bf16[64,2048]{1,0:T(8,128)(2,1)S(1)} %collective-permute-done.6.refs_1_, ...), custom_call_target="tpu_custom_call" | custom-call | flops 99999997952 | tf_op jit(solution)/shard_map/pallas_call | solution.py:304
  39.5 0.6 %collective-permute-start.12 = (f32[64,384]{1,0:T(8,128)S(1)}, f32[64,384]{1,0:T(8,128)S(1)}, u32[]{:S(2)}, u32[]{:S(2)}) collective-permute-start(f32[64,384]{1,0:T(8,128)S(1)} %shard_map.69), channel_id=1, source_target_pairs={{0,1},{1,0},{2,3},{3,2},{4,5},{5,4},{6,7},{7,6},{8,9},{9,8},{10,11... | collective-permute-start | bytes 294920 | tf_op jit(solution)/shard_map/ppermute | solution.py:25
  40.0 2.3 %shard_map.70.refs_2_ = f32[384,512]{1,0:T(8,128)S(1)} custom-call(s32[1]{0:T(128)} %bitcast.11.starts_ref, bf16[8192,512]{1,0:T(8,128)(2,1)} %weight_ref.9, bf16[384,1536]{1,0:T(8,128)(2,1)} %collective-permute-done.1.refs_0_, f32[384,512]{1,0:T(8,128)S(1)} %shard_map.68.refs_1_), custom_call_target="tpu_custom_call" | custom-call | flops 99999997952 | tf_op jit(solution)/shard_map/pallas_call | solution.py:132
  42.5 1.6 %collective-permute-start.14 = (f32[64,384]{1,0:T(8,128)S(1)}, f32[64,384]{1,0:T(8,128)S(1)}, u32[]{:S(2)}, u32[]{:S(2)}) collective-permute-start(f32[64,384]{1,0:T(8,128)S(1)} %add.10.refs_3_), channel_id=1, source_target_pairs={{0,2},{1,3},{2,0},{3,1},{4,6},{5,7},{6,4},{7,5},{8,10},{9,11},{10,... | collective-permute-start | bytes 294920 | tf_op jit(solution)/shard_map/ppermute | solution.py:25
  44.1 0.7 %collective-permute-done.refs_1_ = bf16[384,512]{1,0:T(8,128)(2,1)} collective-permute-done((bf16[384,512]{1,0:T(8,128)(2,1)}, bf16[384,512]{1,0:T(8,128)(2,1)}, u32[]{:S(2)}, u32[]{:S(2)}) %collective-permute-start) | collective-permute-done | bytes 393248 | tf_op jit(solution)/shard_map/ppermute | solution.py:25
  44.8 3.3 %shard_map.71.refs_1_ = f32[384,512]{1,0:T(8,128)S(1)} custom-call(s32[2]{0:T(128)S(1)} %pad_add_fusion.1.starts_ref, bf16[8192,512]{1,0:T(8,128)(2,1)} %weight_ref.9, bf16[384,1536]{1,0:T(8,128)(2,1)} %collective-permute-done.15.refs_0_, bf16[384,512]{1,0:T(8,128)(2,1)} %collective-permute-done.refs_1_, f32[384,512]{1,0:T(8,128)S(1)} %shard_map.70.refs_2_), custom_call_target="tpu_custom_call" | custom-call | flops 99999997952 | tf_op jit(solution)/shard_map/pallas_call | solution.py:132
  48.2 3.0 %shard_map.72 = bf16[384,512]{1,0:T(8,128)(2,1)} custom-call(s32[1]{0:T(128)} %bitcast.starts_ref, s32[4]{0:T(128)S(1)} %copy-done.3, s32[4]{0:T(128)S(1)} %copy-done.15, bf16[8192,512]{1,0:T(8,128)(2,1)} %weight_ref.9, bf16[384,512]{1,0:T(8,128)(2,1)S(1)} %collective-permute-done.13.refs_0_, f32[384,512]{1,0:T(8,128)S(1)} %shard_map.71.refs_1_, ...), custom_call_target="tpu_custom_call" | custom-call | flops 99999997952 | tf_op jit(solution)/shard_map/pallas_call | solution.py:338
  (52 shorter events, 0.4 us)
Async XLA Ops:
  0.0 14.6 %copy-start = (bf16[384,2048]{1,0:T(8,128)(2,1)S(1)}, bf16[384,2048]{1,0:T(8,128)(2,1)}, u32[]{:S(2)}) copy-start(bf16[384,2048]{1,0:T(8,128)(2,1)} %tokens_ref.1) | copy-start | bytes 4718596
  0.0 10.3 %collective-permute-start.5 = (bf16[384,2048]{1,0:T(8,128)(2,1)}, bf16[384,2048]{1,0:T(8,128)(2,1)S(1)}, u32[]{:S(2)}, u32[]{:S(2)}) collective-permute-start(bf16[384,2048]{1,0:T(8,128)(2,1)} %tokens_ref.1), channel_id=1, source_target_pairs={{0,1},{1,0},{2,3},{3,2},{4,5},{5,4},{6,7},{7,6},{8,9},{9,8},{10,11... | collective-permute-start | bytes 4718600 | tf_op jit(solution)/shard_map/ppermute | solution.py:25
  2.2 7.7 %copy-start.1 = (bf16[16,2048]{1,0:T(8,128)(2,1)S(1)}, bf16[16,2048]{1,0:T(8,128)(2,1)}, u32[]{:S(2)}) copy-start(bf16[16,2048]{1,0:T(8,128)(2,1)} %get-tuple-element.54.refs_0_) | copy-start | bytes 196612
  2.2 7.2 %collective-permute-start.2 = (bf16[16,2048]{1,0:T(8,128)(2,1)}, bf16[16,2048]{1,0:T(8,128)(2,1)S(1)}, u32[]{:S(2)}, u32[]{:S(2)}) collective-permute-start(bf16[16,2048]{1,0:T(8,128)(2,1)} %get-tuple-element.55), channel_id=1, source_target_pairs={{0,1},{1,0},{2,3},{3,2},{4,5},{5,4},{6,7},{7,6},{8,9},{9,8},{10,11... | collective-permute-start | bytes 196616 | tf_op jit(solution)/shard_map/ppermute | solution.py:25
  2.4 7.5 %collective-permute-start.3 = (bf16[16,2048]{1,0:T(8,128)(2,1)}, bf16[16,2048]{1,0:T(8,128)(2,1)S(1)}, u32[]{:S(2)}, u32[]{:S(2)}) collective-permute-start(bf16[16,2048]{1,0:T(8,128)(2,1)} %get-tuple-element.56), channel_id=1, source_target_pairs={{0,2},{1,3},{2,0},{3,1},{4,6},{5,7},{6,4},{7,5},{8,10},{9,11},{10,... | collective-permute-start | bytes 196616 | tf_op jit(solution)/shard_map/ppermute | solution.py:25
  5.2 4.7 %collective-permute-start.4 = (bf16[16,2048]{1,0:T(8,128)(2,1)}, bf16[16,2048]{1,0:T(8,128)(2,1)S(1)}, u32[]{:S(2)}, u32[]{:S(2)}) collective-permute-start(bf16[16,2048]{1,0:T(8,128)(2,1)} %get-tuple-element.57), channel_id=1, source_target_pairs={{0,3},{1,2},{2,1},{3,0},{4,7},{5,6},{6,5},{7,4},{8,11},{9,10},{10,... | collective-permute-start | bytes 196616 | tf_op jit(solution)/shard_map/ppermute | solution.py:25
  7.7 29.2 %collective-permute-start.1 = (bf16[384,1536]{1,0:T(8,128)(2,1)}, bf16[384,1536]{1,0:T(8,128)(2,1)}, u32[]{:S(2)}, u32[]{:S(2)}) collective-permute-start(bf16[384,1536]{1,0:T(8,128)(2,1)} %get-tuple-element.53), channel_id=1, source_target_pairs={{0,2},{1,3},{2,0},{3,1},{4,6},{5,7},{6,4},{7,5},{8,10},{9,11},{10,... | collective-permute-start | bytes 3538952 | tf_op jit(solution)/shard_map/ppermute | solution.py:25
  9.3 35.5 %collective-permute-start = (bf16[384,512]{1,0:T(8,128)(2,1)}, bf16[384,512]{1,0:T(8,128)(2,1)}, u32[]{:S(2)}, u32[]{:S(2)}) collective-permute-start(bf16[384,512]{1,0:T(8,128)(2,1)} %get-tuple-element.52), channel_id=1, source_target_pairs={{0,2},{1,3},{2,0},{3,1},{4,6},{5,7},{6,4},{7,5},{8,10},{9,11},{10,... | collective-permute-start | bytes 1179656 | tf_op jit(solution)/shard_map/ppermute | solution.py:25
  10.3 13.7 %collective-permute-start.6 = (bf16[64,2048]{1,0:T(8,128)(2,1)S(1)}, bf16[64,2048]{1,0:T(8,128)(2,1)S(1)}, u32[]{:S(2)}, u32[]{:S(2)}) collective-permute-start(bf16[64,2048]{1,0:T(8,128)(2,1)S(1)} %shard_map.66.refs_0_), channel_id=1, source_target_pairs={{0,4},{4,0},{8,12},{12,8},{1,5},{5,1},{9,13},{13,9},{2,6},{6,2},{1... | collective-permute-start | bytes 786440 | tf_op jit(solution)/shard_map/ppermute | solution.py:25
  12.0 16.8 %collective-permute-start.7 = (bf16[64,2048]{1,0:T(8,128)(2,1)S(1)}, bf16[64,2048]{1,0:T(8,128)(2,1)S(1)}, u32[]{:S(2)}, u32[]{:S(2)}) collective-permute-start(bf16[64,2048]{1,0:T(8,128)(2,1)S(1)} %shard_map.66.refs_0_), channel_id=1, source_target_pairs={{0,8},{4,12},{8,0},{12,4},{16,28},{20,24},{24,20},{28,16},{1,9},{5... | collective-permute-start | bytes 786440 | tf_op jit(solution)/shard_map/ppermute | solution.py:277
  17.2 14.2 %collective-permute-start.10 = (bf16[64,512]{1,0:T(8,128)(2,1)S(1)}, bf16[64,512]{1,0:T(8,128)(2,1)S(1)}, u32[]{:S(2)}, u32[]{:S(2)}) collective-permute-start(bf16[64,512]{1,0:T(8,128)(2,1)S(1)} %bitcast.15), channel_id=1, source_target_pairs={{0,8},{4,12},{8,0},{12,4},{16,28},{20,24},{24,20},{28,16},{1,9},{5... | collective-permute-start | bytes 196616 | tf_op jit(solution)/shard_map/ppermute | solution.py:277
  24.1 7.4 %collective-permute-start.9 = (bf16[64,512]{1,0:T(8,128)(2,1)S(1)}, bf16[64,512]{1,0:T(8,128)(2,1)S(1)}, u32[]{:S(2)}, u32[]{:S(2)}) collective-permute-start(bf16[64,512]{1,0:T(8,128)(2,1)S(1)} %bitcast.16), channel_id=1, source_target_pairs={{0,4},{4,0},{8,12},{12,8},{1,5},{5,1},{9,13},{13,9},{2,6},{6,2},{1... | collective-permute-start | bytes 196616 | tf_op jit(solution)/shard_map/ppermute | solution.py:25
  28.8 8.1 %collective-permute-start.8 = (bf16[64,2048]{1,0:T(8,128)(2,1)S(1)}, bf16[64,2048]{1,0:T(8,128)(2,1)S(1)}, u32[]{:S(2)}, u32[]{:S(2)}) collective-permute-start(bf16[64,2048]{1,0:T(8,128)(2,1)S(1)} %collective-permute-done.7.refs_2_), channel_id=1, source_target_pairs={{0,16},{16,0},{1,17},{17,1},{2,18},{18,2},{3,19},{19,3},{4,20},{20... | collective-permute-start | bytes 786440 | tf_op jit(solution)/shard_map/ppermute | solution.py:25
  28.8 8.2 %copy-start.12 = (s32[384,1]{0,1:T(1,128)S(1)}, s32[384,1]{0,1:T(1,128)}, u32[]{:S(2)}) copy-start(s32[384,1]{0,1:T(1,128)} %param.7) | copy-start | bytes 4612
  28.8 8.2 %copy-start.14 = (s32[4]{0:T(128)S(1)}, s32[4]{0:T(128)}, u32[]{:S(2)}) copy-start(s32[4]{0:T(128)} %placement_ref.3) | copy-start | bytes 52
  31.4 8.0 %copy-start.6 = (bf16[64,512]{1,0:T(8,128)(2,1)}, bf16[64,512]{1,0:T(8,128)(2,1)S(1)}, u32[]{:S(2)}) copy-start(bf16[64,512]{1,0:T(8,128)(2,1)S(1)} %collective-permute-done.10.refs_7_) | copy-start | bytes 196612
  31.4 8.0 %copy-start.8 = (bf16[64,512]{1,0:T(8,128)(2,1)}, bf16[64,512]{1,0:T(8,128)(2,1)S(1)}, u32[]{:S(2)}) copy-start(bf16[64,512]{1,0:T(8,128)(2,1)S(1)} %collective-permute-done.9.refs_6_) | copy-start | bytes 196612
  31.5 5.4 %collective-permute-start.11 = (bf16[64,512]{1,0:T(8,128)(2,1)S(1)}, bf16[64,512]{1,0:T(8,128)(2,1)S(1)}, u32[]{:S(2)}, u32[]{:S(2)}) collective-permute-start(bf16[64,512]{1,0:T(8,128)(2,1)S(1)} %collective-permute-done.10.refs_7_), channel_id=1, source_target_pairs={{0,16},{16,0},{1,17},{17,1},{2,18},{18,2},{3,19},{19,3},{4,20},{20... | collective-permute-start | bytes 196616 | tf_op jit(solution)/shard_map/ppermute | solution.py:25
  33.6 5.9 %copy-start.2 = (s32[4]{0:T(128)}, s32[4]{0:T(128)S(1)}, u32[]{:S(2)}) copy-start(s32[4]{0:T(128)S(1)} %pad_add_fusion.owners_ref) | copy-start | bytes 52
  36.9 7.9 %collective-permute-start.15 = (bf16[384,1536]{1,0:T(8,128)(2,1)}, bf16[384,1536]{1,0:T(8,128)(2,1)}, u32[]{:S(2)}, u32[]{:S(2)}) collective-permute-start(bf16[384,1536]{1,0:T(8,128)(2,1)} %collective-permute-done.1.refs_0_), channel_id=1, source_target_pairs={{0,1},{1,0},{2,3},{3,2},{4,5},{5,4},{6,7},{7,6},{8,9},{9,8},{10,11... | collective-permute-start | bytes 3538952 | tf_op jit(solution)/shard_map/ppermute | solution.py:25
  39.5 2.9 %collective-permute-start.12 = (f32[64,384]{1,0:T(8,128)S(1)}, f32[64,384]{1,0:T(8,128)S(1)}, u32[]{:S(2)}, u32[]{:S(2)}) collective-permute-start(f32[64,384]{1,0:T(8,128)S(1)} %shard_map.69), channel_id=1, source_target_pairs={{0,1},{1,0},{2,3},{3,2},{4,5},{5,4},{6,7},{7,6},{8,9},{9,8},{10,11... | collective-permute-start | bytes 294920 | tf_op jit(solution)/shard_map/ppermute | solution.py:25
  42.4 5.7 %copy-start.3 = (s32[4]{0:T(128)S(1)}, s32[4]{0:T(128)}, u32[]{:S(2)}) copy-start(s32[4]{0:T(128)} %copy-done.2) | copy-start | bytes 52
  42.5 5.6 %collective-permute-start.14 = (f32[64,384]{1,0:T(8,128)S(1)}, f32[64,384]{1,0:T(8,128)S(1)}, u32[]{:S(2)}, u32[]{:S(2)}) collective-permute-start(f32[64,384]{1,0:T(8,128)S(1)} %add.10.refs_3_), channel_id=1, source_target_pairs={{0,2},{1,3},{2,0},{3,1},{4,6},{5,7},{6,4},{7,5},{8,10},{9,11},{10,... | collective-permute-start | bytes 294920 | tf_op jit(solution)/shard_map/ppermute | solution.py:25
  44.8 3.3 %collective-permute-start.13 = (bf16[384,512]{1,0:T(8,128)(2,1)}, bf16[384,512]{1,0:T(8,128)(2,1)S(1)}, u32[]{:S(2)}, u32[]{:S(2)}) collective-permute-start(bf16[384,512]{1,0:T(8,128)(2,1)} %collective-permute-done.refs_1_), channel_id=1, source_target_pairs={{0,1},{1,0},{2,3},{3,2},{4,5},{5,4},{6,7},{7,6},{8,9},{9,8},{10,11... | collective-permute-start | bytes 1179656 | tf_op jit(solution)/shard_map/ppermute | solution.py:25
  (8 other events, 39.4 us)

commit v9 on v8

--- a/solution.py
+++ b/solution.py
@@ -51,22 +51,17 @@
         copy.wait()
 
 
-def cut_kernel(edges, source_ref, *refs):
-    run_copies(
-        [(source_ref.at[:, a:b], out) for a, b, out in zip(edges, edges[1:], refs[:-1])], refs[-1]
-    )
-
-
-def slice_kernel(down_ref, *refs):
+def cut_kernel(edges, tokens_ref, down_ref, *refs):
     outs, sems = refs[:-1], refs[-1]
-    me, depth = lax.axis_index("tensor"), outs[0].shape[1]
-    run_copies(
-        [
-            (down_ref.at[:, pl.ds(pl.multiple_of((me ^ flip) * depth, LANES), depth)], out)
-            for flip, out in enumerate(outs)
-        ],
-        sems,
-    )
+    me, depth = lax.axis_index("tensor"), tokens_ref.shape[1]
+    cuts = len(edges) - 1
+    pairs = []
+    for flip, piece in enumerate(outs[cuts:]):
+        start = pl.multiple_of((me ^ flip) * depth, LANES)
+        pairs.append((down_ref.at[:, pl.ds(start, depth)], piece))
+    for a, b, chunk in zip(edges, edges[1:], outs):
+        pairs.append((tokens_ref.at[:, a:b], chunk))
+    run_copies(pairs, sems)
 
 
 def order_kernel(rank_part, *refs):
@@ -209,32 +204,26 @@
 
     down = lowrank_down_weight[0].T
     whole_tiles = down.shape[0] % 16 == 0
+    cuts = len(edges) - 1
     if whole_tiles:
-        pieces = call(
-            slice_kernel,
-            [jax.ShapeDtypeStruct((down.shape[0], depth), down.dtype)] * tensors,
-            [ANYWHERE],
-            [pltpu.SemaphoreType.DMA((tensors,))],
-            [VECTOR] * tensors,
+        cut = call(
+            functools.partial(cut_kernel, edges),
+            [jax.ShapeDtypeStruct((rows, b - a), tokens.dtype) for a, b in zip(edges, edges[1:])]
+            + [jax.ShapeDtypeStruct((down.shape[0], depth), down.dtype)] * tensors,
+            [ANYWHERE, ANYWHERE],
+            [pltpu.SemaphoreType.DMA((cuts + tensors,))],
+            [VECTOR] * (cuts + tensors),
             cost=FREE,
             mib=60,
-        )(down)
+        )(tokens, down)
+        chunks, pieces = list(cut[:cuts]), list(cut[cuts:])
     else:
+        chunks = [tokens[:, a:b] for a, b in zip(edges, edges[1:])]
         pieces = [
             lax.dynamic_slice_in_dim(down, (me ^ flip) * depth, depth, axis=1)
             for flip in range(tensors)
         ]
     neighbour = flipped(tokens, "tensor", 1)
-    uncut, pieces = chained(tokens, pieces)
-    chunks = call(
-        functools.partial(cut_kernel, edges),
-        [jax.ShapeDtypeStruct((rows, b - a), tokens.dtype) for a, b in zip(edges, edges[1:])],
-        [ANYWHERE],
-        [pltpu.SemaphoreType.DMA((len(edges) - 1,))],
-        [VECTOR] * (len(edges) - 1),
-        cost=FREE,
-        mib=60,
-    )(uncut)
     pieces = [pieces[0]] + [flipped(pieces[f], "tensor", f) for f in range(1, tensors)]
     if whole_tiles:
         own = call(
@@ -284,20 +273,16 @@
     own, neighbour, here = chained(own, neighbour, tokens)
     single, fetched = fetch(own)
     total = products(tile, [me * depth], [here], frozen_projection_weight)
-    total, up = chained(total, lowrank_up_weight[0])
-    single_up, fetched_up = fetch(up)
     single, fetched, total = chained(single, fetched, total)
     swapped = [flipped(value, "parts", 1) for value in fetched]
     total, neighbour = chained(total, neighbour)
     total = products(tile, [(me ^ 1) * depth], [neighbour], frozen_projection_weight, total)
-    single_up, fetched_up, total = chained(single_up, fetched_up, total)
-    swapped_up = [flipped(value, "parts", 1) for value in fetched_up]
-    downs, ups = [own] + single, [up] + single_up
+    total, up = chained(total, lowrank_up_weight[0])
+    single_up, fetched_up = fetch(up)
+    swapped, total = chained(swapped, total)
+    downs = [own] + single
     for i in range(len(pairs)):
         downs += [fetched[i], swapped[i]]
-        ups += [fetched_up[i], swapped_up[i]]
-    far[0], downs, ups = chained(far[0], downs, ups)
-
     owners = jnp.stack(owners)
 
     tiles = depth // tile
@@ -312,8 +297,12 @@
             pltpu.SemaphoreType.DMA((1 + slots, tiles)),
         ],
     )(owners, placement, tokens, tenant_row, *downs)
+    far[0], fetched_up, partial = chained(far[0], fetched_up, partial)
+    swapped_up = [flipped(value, "parts", 1) for value in fetched_up]
+    ups = [up] + single_up
+    for i in range(len(pairs)):
+        ups += [fetched_up[i], swapped_up[i]]
     starts, features = spread_out(0)
-    partial, total = chained(partial, total)
     total = products(tile, starts[::2], features[::2], frozen_projection_weight, total)
     flip = 1
     while flip < tensors // 2:
@@ -323,17 +312,13 @@
         partial += received
         flip *= 2
     more = flipped(partial, "tensor", flip)
-    far[1], partial = chained(far[1], partial)
-    last_starts, last = spread_out(1)
-    total = products(
-        tile,
-        starts[1::2] + last_starts[::2],
-        features[1::2] + last[::2],
-        frozen_projection_weight,
-        total,
-    )
-    starts = last_starts[1::2]
-    features, more, total = chained(last[1::2], more, total)
+    total, partial = chained(total, partial)
+    total = products(tile, starts[1::2], features[1::2], frozen_projection_weight, total)
+    far[1], ups, total = chained(far[1], ups, total)
+    starts, features = spread_out(1)
+    total = products(tile, starts[::2], features[::2], frozen_projection_weight, total)
+    starts = starts[1::2]
+    features, more, total = chained(features[1::2], more, total)
 
     return call(
         functools.partial(last_kernel, tile, len(features), slots),

time: 51.5 us -> 53.3 us (1.035)
  starting transfers between devices: 14.5 us -> 17 us
  waiting for transfers between devices: 15.2 us -> 13.9 us
  local copies, waits for them, and re-layouts: 0.07 us -> 0.86 us
  other arithmetic: 0.16 us -> 0.73 us
    pallas_call x1 -> x0, Pallas kernels: 1.71 us -> none  [body(): call(slice_kernel, [jax.ShapeDtypeStruct((down.shape[0], depth), down.dty...]
    ppermute x2, waiting for transfers between devices: 4.69 us -> 3.17 us  [fetch(): lax.ppermute(value, ('parts', 'adapter'), route)]
    ppermute x2, starting transfers between devices: 2.99 us -> 4.41 us  [fetch(): lax.ppermute(value, ('parts', 'adapter'), route)]
    ppermute x14, starting transfers between devices: 11.6 us -> 12.6 us  [flipped(): return lax.ppermute(value, axis, [(i, i ^ flip) for i in range(count)])]
    unnamed x32 -> x10, local copies, waits for them, and re-layouts: 0.07 us -> 0.86 us
    add x1, other arithmetic: 0.01 us -> 0.65 us  [body(): partial += received]
    pallas_call x4 -> x5, Pallas kernels: 10.8 us -> 11.4 us  [products(): call(functools.partial(products_kernel, tile, len(features), len(given)),...]
  transfers between devices with their start and end apart: 16 -> 16, of which waited for: 4 -> 7; matrix products, arithmetic and copies ran while one was open for 0% -> 1% of each run, Pallas kernels for 35% -> 32%
where the time goes in v9:
time: 53.3 us; the launch traced here: 53 us
  Pallas kernels  20.4 us (38%)
  starting transfers between devices  17 us (32%)
  waiting for transfers between devices  13.9 us (26%)
  local copies, waits for them, and re-layouts  0.86 us (2%)
  other arithmetic  0.73 us (1%)
    ppermute x14, starting transfers between devices, flipped(): return lax.ppermute(value, axis, [(i, i ^ flip) for i in range(count)])  12.6 us
    pallas_call x5, Pallas kernels, products(): call(functools.partial(products_kernel, tile, len(features), len(given)),...  11.4 us
    ppermute x14, waiting for transfers between devices, flipped(): return lax.ppermute(value, axis, [(i, i ^ flip) for i in range(count)])  10.7 us
    ppermute x2, starting transfers between devices, fetch(): lax.ppermute(value, ('parts', 'adapter'), route)  4.41 us
    pallas_call x1, Pallas kernels, body(): call(functools.partial(last_kernel, tile, len(features), slots), jax.Shap...  3.45 us
    ppermute x2, waiting for transfers between devices, fetch(): lax.ppermute(value, ('parts', 'adapter'), route)  3.17 us
    pallas_call x1, Pallas kernels, body(): call(functools.partial(cut_kernel, edges), [jax.ShapeDtypeStruct((rows, b...  2.77 us
    pallas_call x1, Pallas kernels, body(): call(functools.partial(shrink_kernel, tile, slots), jax.ShapeDtypeStruct(...  2.43 us
  transfers between devices with their start and end apart: 16, of which 7 were waited for; matrix products, arithmetic and copies ran while one was open for 1% of the time, Pallas kernels for 32%

profile of v9, /device:TPU:0, one launch (start us, length us, event | category | flops | bytes accessed | tf_op | source)
XLA Modules:
  0.0 53.0 jit_solution(12264499661374065889)
XLA Ops:
  0.5 2.8 %shard_map.64 = (bf16[384,1536]{1,0:T(8,128)(2,1)}, bf16[384,512]{1,0:T(8,128)(2,1)}, bf16[16,2048]{1,0:T(8,128)(2,1)}, bf16[16,2048]{1,0:T(8,128)(2,1)}, bf16[1...) custom-call(bf16[384,2048]{1,0:T(8,128)(2,1)} %tokens_ref.3, bf16[16,8192]{1,0:T(8,128)(2,1)} %bitcast.17), custom_call_target="tpu_custom_call" | custom-call | tf_op jit(solution)/shard_map/pallas_call | solution.py:209
  3.4 2.8 %collective-permute-start.2 = (bf16[16,2048]{1,0:T(8,128)(2,1)}, bf16[16,2048]{1,0:T(8,128)(2,1)S(1)}, u32[]{:S(2)}, u32[]{:S(2)}) collective-permute-start(bf16[16,2048]{1,0:T(8,128)(2,1)} %get-tuple-element.42), channel_id=1, source_target_pairs={{0,2},{1,3},{2,0},{3,1},{4,6},{5,7},{6,4},{7,5},{8,10},{9,11},{10,... | collective-permute-start | bytes 196616 | tf_op jit(solution)/shard_map/ppermute | solution.py:25
  6.3 1.5 %collective-permute-start.8 = (bf16[384,1536]{1,0:T(8,128)(2,1)}, bf16[384,1536]{1,0:T(8,128)(2,1)}, u32[]{:S(2)}, u32[]{:S(2)}) collective-permute-start(bf16[384,1536]{1,0:T(8,128)(2,1)} %get-tuple-element.51), channel_id=1, source_target_pairs={{0,2},{1,3},{2,0},{3,1},{4,6},{5,7},{6,4},{7,5},{8,10},{9,11},{10,... | collective-permute-start | bytes 3538952 | tf_op jit(solution)/shard_map/ppermute | solution.py:25
  7.8 0.6 %collective-permute-start = (bf16[384,512]{1,0:T(8,128)(2,1)}, bf16[384,512]{1,0:T(8,128)(2,1)}, u32[]{:S(2)}, u32[]{:S(2)}) collective-permute-start(bf16[384,512]{1,0:T(8,128)(2,1)} %get-tuple-element.39), channel_id=1, source_target_pairs={{0,2},{1,3},{2,0},{3,1},{4,6},{5,7},{6,4},{7,5},{8,10},{9,11},{10,... | collective-permute-start | bytes 1179656 | tf_op jit(solution)/shard_map/ppermute | solution.py:25
  9.0 1.9 %collective-permute-done.3.refs_3_ = bf16[16,2048]{1,0:T(8,128)(2,1)S(1)} collective-permute-done((bf16[16,2048]{1,0:T(8,128)(2,1)}, bf16[16,2048]{1,0:T(8,128)(2,1)S(1)}, u32[]{:S(2)}, u32[]{:S(2)}) %collective-permute-start.3) | collective-permute-done | bytes 65568 | tf_op jit(solution)/shard_map/ppermute | solution.py:25
  10.9 0.8 %copy-done.1 = bf16[16,2048]{1,0:T(8,128)(2,1)S(1)} copy-done((bf16[16,2048]{1,0:T(8,128)(2,1)S(1)}, bf16[16,2048]{1,0:T(8,128)(2,1)}, u32[]{:S(2)}) %copy-start.1) | copy-done | bytes 65560
  12.1 1.7 %collective-permute-start.5 = (bf16[64,2048]{1,0:T(8,128)(2,1)S(1)}, bf16[64,2048]{1,0:T(8,128)(2,1)S(1)}, u32[]{:S(2)}, u32[]{:S(2)}) collective-permute-start(bf16[64,2048]{1,0:T(8,128)(2,1)S(1)} %shard_map.65.refs_0_), channel_id=1, source_target_pairs={{0,4},{4,0},{8,12},{12,8},{1,5},{5,1},{9,13},{13,9},{2,6},{6,2},{1... | collective-permute-start | bytes 786440 | tf_op jit(solution)/shard_map/ppermute | solution.py:25
  13.7 2.6 %collective-permute-start.6 = (bf16[64,2048]{1,0:T(8,128)(2,1)S(1)}, bf16[64,2048]{1,0:T(8,128)(2,1)S(1)}, u32[]{:S(2)}, u32[]{:S(2)}) collective-permute-start(bf16[64,2048]{1,0:T(8,128)(2,1)S(1)} %shard_map.65.refs_0_), channel_id=1, source_target_pairs={{0,8},{4,12},{8,0},{12,4},{16,28},{20,24},{24,20},{28,16},{1,9},{5... | collective-permute-start | bytes 786440 | tf_op jit(solution)/shard_map/ppermute | solution.py:266
  16.3 2.6 %shard_map.66.refs_1_ = f32[384,512]{1,0:T(8,128)S(1)} custom-call(s32[1]{0:T(128)} %bitcast.8.starts_ref, bf16[8192,512]{1,0:T(8,128)(2,1)} %weight_ref.11, bf16[384,2048]{1,0:T(8,128)(2,1)S(1)} %copy-done), custom_call_target="tpu_custom_call" | custom-call | flops 99999997952 | tf_op jit(solution)/shard_map/pallas_call | solution.py:127
  19.0 7.0 %collective-permute-done.5.refs_1_ = bf16[64,2048]{1,0:T(8,128)(2,1)S(1)} collective-permute-done((bf16[64,2048]{1,0:T(8,128)(2,1)S(1)}, bf16[64,2048]{1,0:T(8,128)(2,1)S(1)}, u32[]{:S(2)}, u32[]{:S(2)}) %collective-permute-start.5) | collective-permute-done | bytes 262176 | tf_op jit(solution)/shard_map/ppermute | solution.py:25
  26.0 2.4 %collective-permute-done.6.refs_2_ = bf16[64,2048]{1,0:T(8,128)(2,1)S(1)} collective-permute-done((bf16[64,2048]{1,0:T(8,128)(2,1)S(1)}, bf16[64,2048]{1,0:T(8,128)(2,1)S(1)}, u32[]{:S(2)}, u32[]{:S(2)}) %collective-permute-start.6) | collective-permute-done | bytes 262176 | tf_op jit(solution)/shard_map/ppermute | solution.py:266
  28.3 1.4 %collective-permute-start.10 = (bf16[64,2048]{1,0:T(8,128)(2,1)S(1)}, bf16[64,2048]{1,0:T(8,128)(2,1)S(1)}, u32[]{:S(2)}, u32[]{:S(2)}) collective-permute-start(bf16[64,2048]{1,0:T(8,128)(2,1)S(1)} %collective-permute-done.6.refs_2_), channel_id=1, source_target_pairs={{0,16},{16,0},{1,17},{17,1},{2,18},{18,2},{3,19},{19,3},{4,20},{20... | collective-permute-start | bytes 786440 | tf_op jit(solution)/shard_map/ppermute | solution.py:25
  29.7 2.6 %shard_map.67.refs_1_ = f32[384,512]{1,0:T(8,128)S(1)} custom-call(s32[1]{0:T(128)} %bitcast.7.starts_ref, bf16[8192,512]{1,0:T(8,128)(2,1)} %weight_ref.11, bf16[384,2048]{1,0:T(8,128)(2,1)S(1)} %collective-permute-done.4.refs_0_, f32[384,512]{1,0:T(8,128)S(1)} %shard_map.66.refs_1_), custom_call_target="tpu_custom_call" | custom-call | flops 99999997952 | tf_op jit(solution)/shard_map/pallas_call | solution.py:127
  32.4 1.8 %collective-permute-start.9 = (bf16[64,512]{1,0:T(8,128)(2,1)}, bf16[64,512]{1,0:T(8,128)(2,1)}, u32[]{:S(2)}, u32[]{:S(2)}) collective-permute-start(bf16[64,512]{1,0:T(8,128)(2,1)} %bitcast.9.refs_5_), channel_id=1, source_target_pairs={{0,8},{4,12},{8,0},{12,4},{16,28},{20,24},{24,20},{28,16},{1,9},{5... | collective-permute-start | bytes 196616 | tf_op jit(solution)/shard_map/ppermute | solution.py:266
  34.5 0.9 %collective-permute-done.10.refs_3_ = bf16[64,2048]{1,0:T(8,128)(2,1)S(1)} collective-permute-done((bf16[64,2048]{1,0:T(8,128)(2,1)S(1)}, bf16[64,2048]{1,0:T(8,128)(2,1)S(1)}, u32[]{:S(2)}, u32[]{:S(2)}) %collective-permute-start.10) | collective-permute-done | bytes 262176 | tf_op jit(solution)/shard_map/ppermute | solution.py:25
  35.4 2.4 %shard_map.68 = f32[64,384]{1,0:T(8,128)S(1)} custom-call(s32[4]{0:T(128)S(1)} %pad_add_fusion.owners_ref, s32[4]{0:T(128)S(1)} %copy-done.4, bf16[384,2048]{1,0:T(8,128)(2,1)S(1)} %copy-done, s32[1,384]{1,0:T(1,128)S(1)} %bitcast.15, bf16[64,2048]{1,0:T(8,128)(2,1)S(1)} %shard_map.65.refs_0_, bf16[64,2048]{1,0:T(8,128)(2,1)S(1)} %collective-permute-done.5.refs_1_, ...), custom_call_target="tpu_custom_call" | custom-call | flops 99999997952 | tf_op jit(solution)/shard_map/pallas_call | solution.py:289
  37.9 0.8 %collective-permute-done.9.refs_7_ = bf16[64,512]{1,0:T(8,128)(2,1)} collective-permute-done((bf16[64,512]{1,0:T(8,128)(2,1)}, bf16[64,512]{1,0:T(8,128)(2,1)}, u32[]{:S(2)}, u32[]{:S(2)}) %collective-permute-start.9) | collective-permute-done | bytes 65568 | tf_op jit(solution)/shard_map/ppermute | solution.py:266
  39.2 1.0 %collective-permute-start.11 = (bf16[64,512]{1,0:T(8,128)(2,1)}, bf16[64,512]{1,0:T(8,128)(2,1)}, u32[]{:S(2)}, u32[]{:S(2)}) collective-permute-start(bf16[64,512]{1,0:T(8,128)(2,1)} %collective-permute-done.9.refs_7_), channel_id=1, source_target_pairs={{0,16},{16,0},{1,17},{17,1},{2,18},{18,2},{3,19},{19,3},{4,20},{20... | collective-permute-start | bytes 196616 | tf_op jit(solution)/shard_map/ppermute | solution.py:25
  40.2 2.3 %shard_map.69.refs_1_ = f32[384,512]{1,0:T(8,128)S(1)} custom-call(s32[1]{0:T(128)} %bitcast.12.starts_ref, bf16[8192,512]{1,0:T(8,128)(2,1)} %weight_ref.11, bf16[384,1536]{1,0:T(8,128)(2,1)} %collective-permute-done.8.refs_0_, f32[384,512]{1,0:T(8,128)S(1)} %shard_map.67.refs_1_), custom_call_target="tpu_custom_call" | custom-call | flops 99999997952 | tf_op jit(solution)/shard_map/pallas_call | solution.py:127
  42.6 0.7 %add.10.refs_3_ = f32[64,384]{1,0:T(8,128)} add(f32[64,384]{1,0:T(8,128)S(1)} %shard_map.68, f32[64,384]{1,0:T(8,128)S(1)} %collective-permute-done.13) | non-fusion elementwise | flops 24576 | bytes 294912 | tf_op jit(solution)/shard_map/add | solution.py:312
  43.2 2.1 %collective-permute-start.15 = (f32[64,384]{1,0:T(8,128)}, f32[64,384]{1,0:T(8,128)}, u32[]{:S(2)}, u32[]{:S(2)}) collective-permute-start(f32[64,384]{1,0:T(8,128)} %add.10.refs_3_), channel_id=1, source_target_pairs={{0,2},{1,3},{2,0},{3,1},{4,6},{5,7},{6,4},{7,5},{8,10},{9,11},{10,... | collective-permute-start | bytes 294920 | tf_op jit(solution)/shard_map/ppermute | solution.py:25
  45.3 2.2 %shard_map.70.refs_1_ = f32[384,512]{1,0:T(8,128)S(1)} custom-call(s32[1]{0:T(128)} %bitcast.11.starts_ref, bf16[8192,512]{1,0:T(8,128)(2,1)} %weight_ref.11, bf16[384,1536]{1,0:T(8,128)(2,1)S(1)} %collective-permute-done.12.refs_0_, f32[384,512]{1,0:T(8,128)S(1)} %shard_map.69.refs_1_), custom_call_target="tpu_custom_call" | custom-call | flops 99999997952 | tf_op jit(solution)/shard_map/pallas_call | solution.py:127
  47.6 1.6 %shard_map.71.refs_1_ = f32[384,512]{1,0:T(8,128)S(1)} custom-call(s32[1]{0:T(128)} %bitcast.13.starts_ref, bf16[8192,512]{1,0:T(8,128)(2,1)} %weight_ref.11, bf16[384,512]{1,0:T(8,128)(2,1)} %collective-permute-done.refs_0_, f32[384,512]{1,0:T(8,128)S(1)} %shard_map.70.refs_1_), custom_call_target="tpu_custom_call" | custom-call | flops 99999997952 | tf_op jit(solution)/shard_map/pallas_call | solution.py:127
  49.5 3.5 %shard_map.72 = bf16[384,512]{1,0:T(8,128)(2,1)} custom-call(s32[1]{0:T(128)} %bitcast.starts_ref, s32[4]{0:T(128)S(1)} %pad_add_fusion.owners_ref, s32[4]{0:T(128)S(1)} %copy-done.4, bf16[8192,512]{1,0:T(8,128)(2,1)} %weight_ref.11, bf16[384,512]{1,0:T(8,128)(2,1)S(1)} %collective-permute-done.14.refs_0_, f32[384,512]{1,0:T(8,128)S(1)} %shard_map.71.refs_1_, ...), custom_call_target="tpu_custom_call" | custom-call | flops 99999997952 | tf_op jit(solution)/shard_map/pallas_call | solution.py:323
  (29 shorter events, 2.9 us)
Async XLA Ops:
  0.0 16.3 %copy-start = (bf16[384,2048]{1,0:T(8,128)(2,1)S(1)}, bf16[384,2048]{1,0:T(8,128)(2,1)}, u32[]{:S(2)}) copy-start(bf16[384,2048]{1,0:T(8,128)(2,1)} %tokens_ref.3) | copy-start | bytes 4718596
  0.0 12.1 %collective-permute-start.4 = (bf16[384,2048]{1,0:T(8,128)(2,1)}, bf16[384,2048]{1,0:T(8,128)(2,1)S(1)}, u32[]{:S(2)}, u32[]{:S(2)}) collective-permute-start(bf16[384,2048]{1,0:T(8,128)(2,1)} %tokens_ref.3), channel_id=1, source_target_pairs={{0,1},{1,0},{2,3},{3,2},{4,5},{5,4},{6,7},{7,6},{8,9},{9,8},{10,11... | collective-permute-start | bytes 4718600 | tf_op jit(solution)/shard_map/ppermute | solution.py:25
  3.2 4.6 %collective-permute-start.1 = (bf16[16,2048]{1,0:T(8,128)(2,1)}, bf16[16,2048]{1,0:T(8,128)(2,1)S(1)}, u32[]{:S(2)}, u32[]{:S(2)}) collective-permute-start(bf16[16,2048]{1,0:T(8,128)(2,1)} %get-tuple-element.41), channel_id=1, source_target_pairs={{0,1},{1,0},{2,3},{3,2},{4,5},{5,4},{6,7},{7,6},{8,9},{9,8},{10,11... | collective-permute-start | bytes 196616 | tf_op jit(solution)/shard_map/ppermute | solution.py:25
  3.4 5.5 %collective-permute-start.2 = (bf16[16,2048]{1,0:T(8,128)(2,1)}, bf16[16,2048]{1,0:T(8,128)(2,1)S(1)}, u32[]{:S(2)}, u32[]{:S(2)}) collective-permute-start(bf16[16,2048]{1,0:T(8,128)(2,1)} %get-tuple-element.42), channel_id=1, source_target_pairs={{0,2},{1,3},{2,0},{3,1},{4,6},{5,7},{6,4},{7,5},{8,10},{9,11},{10,... | collective-permute-start | bytes 196616 | tf_op jit(solution)/shard_map/ppermute | solution.py:25
  6.3 4.6 %collective-permute-start.3 = (bf16[16,2048]{1,0:T(8,128)(2,1)}, bf16[16,2048]{1,0:T(8,128)(2,1)S(1)}, u32[]{:S(2)}, u32[]{:S(2)}) collective-permute-start(bf16[16,2048]{1,0:T(8,128)(2,1)} %get-tuple-element.43), channel_id=1, source_target_pairs={{0,3},{1,2},{2,1},{3,0},{4,7},{5,6},{6,5},{7,4},{8,11},{9,10},{10,... | collective-permute-start | bytes 196616 | tf_op jit(solution)/shard_map/ppermute | solution.py:25
  6.3 31.6 %collective-permute-start.8 = (bf16[384,1536]{1,0:T(8,128)(2,1)}, bf16[384,1536]{1,0:T(8,128)(2,1)}, u32[]{:S(2)}, u32[]{:S(2)}) collective-permute-start(bf16[384,1536]{1,0:T(8,128)(2,1)} %get-tuple-element.51), channel_id=1, source_target_pairs={{0,2},{1,3},{2,0},{3,1},{4,6},{5,7},{6,4},{7,5},{8,10},{9,11},{10,... | collective-permute-start | bytes 3538952 | tf_op jit(solution)/shard_map/ppermute | solution.py:25
  7.8 39.7 %collective-permute-start = (bf16[384,512]{1,0:T(8,128)(2,1)}, bf16[384,512]{1,0:T(8,128)(2,1)}, u32[]{:S(2)}, u32[]{:S(2)}) collective-permute-start(bf16[384,512]{1,0:T(8,128)(2,1)} %get-tuple-element.39), channel_id=1, source_target_pairs={{0,2},{1,3},{2,0},{3,1},{4,6},{5,7},{6,4},{7,5},{8,10},{9,11},{10,... | collective-permute-start | bytes 1179656 | tf_op jit(solution)/shard_map/ppermute | solution.py:25
  10.9 0.8 %copy-start.1 = (bf16[16,2048]{1,0:T(8,128)(2,1)S(1)}, bf16[16,2048]{1,0:T(8,128)(2,1)}, u32[]{:S(2)}) copy-start(bf16[16,2048]{1,0:T(8,128)(2,1)} %get-tuple-element.40.refs_0_) | copy-start | bytes 196612
  12.1 13.9 %collective-permute-start.5 = (bf16[64,2048]{1,0:T(8,128)(2,1)S(1)}, bf16[64,2048]{1,0:T(8,128)(2,1)S(1)}, u32[]{:S(2)}, u32[]{:S(2)}) collective-permute-start(bf16[64,2048]{1,0:T(8,128)(2,1)S(1)} %shard_map.65.refs_0_), channel_id=1, source_target_pairs={{0,4},{4,0},{8,12},{12,8},{1,5},{5,1},{9,13},{13,9},{2,6},{6,2},{1... | collective-permute-start | bytes 786440 | tf_op jit(solution)/shard_map/ppermute | solution.py:25
  13.7 14.6 %collective-permute-start.6 = (bf16[64,2048]{1,0:T(8,128)(2,1)S(1)}, bf16[64,2048]{1,0:T(8,128)(2,1)S(1)}, u32[]{:S(2)}, u32[]{:S(2)}) collective-permute-start(bf16[64,2048]{1,0:T(8,128)(2,1)S(1)} %shard_map.65.refs_0_), channel_id=1, source_target_pairs={{0,8},{4,12},{8,0},{12,4},{16,28},{20,24},{24,20},{28,16},{1,9},{5... | collective-permute-start | bytes 786440 | tf_op jit(solution)/shard_map/ppermute | solution.py:266
  28.3 7.1 %collective-permute-start.10 = (bf16[64,2048]{1,0:T(8,128)(2,1)S(1)}, bf16[64,2048]{1,0:T(8,128)(2,1)S(1)}, u32[]{:S(2)}, u32[]{:S(2)}) collective-permute-start(bf16[64,2048]{1,0:T(8,128)(2,1)S(1)} %collective-permute-done.6.refs_2_), channel_id=1, source_target_pairs={{0,16},{16,0},{1,17},{17,1},{2,18},{18,2},{3,19},{19,3},{4,20},{20... | collective-permute-start | bytes 786440 | tf_op jit(solution)/shard_map/ppermute | solution.py:25
  29.7 5.7 %copy-start.2 = (s32[384,1]{0,1:T(1,128)S(1)}, s32[384,1]{0,1:T(1,128)}, u32[]{:S(2)}) copy-start(s32[384,1]{0,1:T(1,128)} %param.7) | copy-start | bytes 4612
  29.7 5.7 %copy-start.4 = (s32[4]{0:T(128)S(1)}, s32[4]{0:T(128)}, u32[]{:S(2)}) copy-start(s32[4]{0:T(128)} %placement_ref.3) | copy-start | bytes 52
  32.4 6.3 %collective-permute-start.9 = (bf16[64,512]{1,0:T(8,128)(2,1)}, bf16[64,512]{1,0:T(8,128)(2,1)}, u32[]{:S(2)}, u32[]{:S(2)}) collective-permute-start(bf16[64,512]{1,0:T(8,128)(2,1)} %bitcast.9.refs_5_), channel_id=1, source_target_pairs={{0,8},{4,12},{8,0},{12,4},{16,28},{20,24},{24,20},{28,16},{1,9},{5... | collective-permute-start | bytes 196616 | tf_op jit(solution)/shard_map/ppermute | solution.py:266
  34.2 13.3 %collective-permute-start.7 = (bf16[64,512]{1,0:T(8,128)(2,1)}, bf16[64,512]{1,0:T(8,128)(2,1)}, u32[]{:S(2)}, u32[]{:S(2)}) collective-permute-start(bf16[64,512]{1,0:T(8,128)(2,1)} %bitcast.9.refs_5_), channel_id=1, source_target_pairs={{0,4},{4,0},{8,12},{12,8},{1,5},{5,1},{9,13},{13,9},{2,6},{6,2},{1... | collective-permute-start | bytes 196616 | tf_op jit(solution)/shard_map/ppermute | solution.py:25
  38.7 3.9 %collective-permute-start.13 = (f32[64,384]{1,0:T(8,128)S(1)}, f32[64,384]{1,0:T(8,128)S(1)}, u32[]{:S(2)}, u32[]{:S(2)}) collective-permute-start(f32[64,384]{1,0:T(8,128)S(1)} %shard_map.68), channel_id=1, source_target_pairs={{0,1},{1,0},{2,3},{3,2},{4,5},{5,4},{6,7},{7,6},{8,9},{9,8},{10,11... | collective-permute-start | bytes 294920 | tf_op jit(solution)/shard_map/ppermute | solution.py:25
  38.7 6.6 %collective-permute-start.12 = (bf16[384,1536]{1,0:T(8,128)(2,1)}, bf16[384,1536]{1,0:T(8,128)(2,1)S(1)}, u32[]{:S(2)}, u32[]{:S(2)}) collective-permute-start(bf16[384,1536]{1,0:T(8,128)(2,1)} %collective-permute-done.8.refs_0_), channel_id=1, source_target_pairs={{0,1},{1,0},{2,3},{3,2},{4,5},{5,4},{6,7},{7,6},{8,9},{9,8},{10,11... | collective-permute-start | bytes 3538952 | tf_op jit(solution)/shard_map/ppermute | solution.py:25
  39.2 8.3 %collective-permute-start.11 = (bf16[64,512]{1,0:T(8,128)(2,1)}, bf16[64,512]{1,0:T(8,128)(2,1)}, u32[]{:S(2)}, u32[]{:S(2)}) collective-permute-start(bf16[64,512]{1,0:T(8,128)(2,1)} %collective-permute-done.9.refs_7_), channel_id=1, source_target_pairs={{0,16},{16,0},{1,17},{17,1},{2,18},{18,2},{3,19},{19,3},{4,20},{20... | collective-permute-start | bytes 196616 | tf_op jit(solution)/shard_map/ppermute | solution.py:25
  43.2 6.0 %collective-permute-start.15 = (f32[64,384]{1,0:T(8,128)}, f32[64,384]{1,0:T(8,128)}, u32[]{:S(2)}, u32[]{:S(2)}) collective-permute-start(f32[64,384]{1,0:T(8,128)} %add.10.refs_3_), channel_id=1, source_target_pairs={{0,2},{1,3},{2,0},{3,1},{4,6},{5,7},{6,4},{7,5},{8,10},{9,11},{10,... | collective-permute-start | bytes 294920 | tf_op jit(solution)/shard_map/ppermute | solution.py:25
  47.5 2.0 %collective-permute-start.14 = (bf16[384,512]{1,0:T(8,128)(2,1)}, bf16[384,512]{1,0:T(8,128)(2,1)S(1)}, u32[]{:S(2)}, u32[]{:S(2)}) collective-permute-start(bf16[384,512]{1,0:T(8,128)(2,1)} %collective-permute-done.refs_0_), channel_id=1, source_target_pairs={{0,1},{1,0},{2,3},{3,2},{4,5},{5,4},{6,7},{7,6},{8,9},{9,8},{10,11... | collective-permute-start | bytes 1179656 | tf_op jit(solution)/shard_map/ppermute | solution.py:25
  47.6 1.9 %copy-start.3 = (s32[384,1]{0,1:T(1,128)S(1)}, s32[384,1]{0,1:T(1,128)}, u32[]{:S(2)}) copy-start(s32[384,1]{0,1:T(1,128)} %param.7) | copy-start | bytes 4612

commit v10 on v9

--- a/solution.py
+++ b/solution.py
@@ -11,7 +11,7 @@
 LOWRANK_SCALE = 2.0
 CORES = 2
 LANES = 128
-CUTS = (0.75,)
+CUTS = (0.5, 0.75)
 MIB = 1024 * 1024
 FREE = pl.CostEstimate(flops=0, bytes_accessed=0, transcendentals=0)
 LONG = pl.CostEstimate(flops=10**11, bytes_accessed=0, transcendentals=0)
@@ -76,22 +76,15 @@
     )
 
 
-def slot_of_row(tenant, placement_ref, slots):
-    stored = jnp.zeros(tenant.shape, jnp.int32)
-    for slot in range(slots):
-        stored = jnp.where(tenant == slot, placement_ref[slot], stored)
-    return stored
-
-
-def start_tiles(tile, starts_ref, features, weight_ref, held_ref, rows_ref, sems):
-    t = 0
-    for i, part in enumerate(features):
+def start_tiles(tile, depth, places, features, weight_ref, held_ref, rows_ref, sems):
+    me, t = lax.axis_index("tensor"), 0
+    for (flip, first), part in zip(places, features):
         for k in range(0, part.shape[1], tile):
-            start = pl.multiple_of(starts_ref[i] + k, LANES)
-            pltpu.make_async_copy(part.at[:, pl.ds(k, tile)], held_ref.at[t], sems.at[0, t]).start()
+            start = pl.multiple_of((me ^ flip) * depth + first + k, LANES)
             pltpu.make_async_copy(
                 weight_ref.at[pl.ds(start, tile)], rows_ref.at[t], sems.at[1, t]
             ).start()
+            pltpu.make_async_copy(part.at[:, pl.ds(k, tile)], held_ref.at[t], sems.at[0, t]).start()
             t += 1
 
 
@@ -113,39 +106,62 @@
     ]
 
 
-def products_kernel(tile, count, has_total, starts_ref, weight_ref, *refs):
+def first_kernel(tile, depth, places, slots, placement_ref, tenant_ref, weight_ref, *refs):
+    count = len(places)
     features = refs[:count]
-    given = refs[count] if has_total else None
-    out_ref, held_ref, rows_ref, sems = refs[count + has_total :]
-    start_tiles(tile, starts_ref, features, weight_ref, held_ref, rows_ref, sems)
-    out_ref[...] = given[...] if has_total else jnp.zeros_like(out_ref)
+    out_ref, stored_ref, held_ref, rows_ref, sems = refs[count:]
+    start_tiles(tile, depth, places, features, weight_ref, held_ref, rows_ref, sems)
+    out_ref[...] = jnp.zeros_like(out_ref)
+    stored = jnp.zeros(stored_ref.shape, jnp.int32)
+    for slot in range(slots):
+        stored = jnp.where(tenant_ref[...] == slot, placement_ref[slot], stored)
+    stored_ref[...] = stored
     add_tiles(held_ref, rows_ref, sems, out_ref)
 
 
-def products(tile, starts, features, weight, total=None):
-    given = [] if total is None else [total]
-    return call(
-        functools.partial(products_kernel, tile, len(features), len(given)),
-        jax.ShapeDtypeStruct((features[0].shape[0], weight.shape[1]), jnp.float32),
-        [SCALAR, ANYWHERE] + [ANYWHERE] * len(features) + [VECTOR] * len(given),
-        tile_scratch(tile, features, weight.shape[1]),
-    )(jnp.stack(starts), weight, *features, *given)
-
-
-def last_kernel(tile, count, slots, starts_ref, owners_ref, placement_ref, weight_ref, *refs):
+def products_kernel(tile, depth, places, weight_ref, *refs):
+    count = len(places)
+    features, given = refs[:count], refs[count]
+    out_ref, held_ref, rows_ref, sems = refs[count + 1 :]
+    start_tiles(tile, depth, places, features, weight_ref, held_ref, rows_ref, sems)
+    out_ref[...] = given[...]
+    add_tiles(held_ref, rows_ref, sems, out_ref)
+
+
+def owners_of(flips, pairs):
+    group, part = lax.axis_index("adapter"), lax.axis_index("parts")
+    owners = [group] + [group ^ flip for flip in flips]
+    for near, far in pairs:
+        owners += [group ^ (near + part * (far - near)), group ^ (far + part * (near - far))]
+    return owners
+
+
+def last_kernel(tile, depth, places, flips, pairs, slots, weight_ref, *refs):
+    count = len(places)
     features = refs[:count]
-    given, tenant_ref, sum_ref, more_ref = refs[count : count + 4]
+    given, stored_ref, sum_ref, more_ref = refs[count : count + 4]
     ups = refs[count + 4 : count + 4 + slots]
-    out_ref, total_ref, held_ref, rows_ref, sems = refs[count + 4 + slots :]
-    start_tiles(tile, starts_ref, features, weight_ref, held_ref, rows_ref, sems)
-    shrunk = (sum_ref[...] + more_ref[...]).astype(jnp.bfloat16).astype(jnp.float32)
-    stored = slot_of_row(tenant_ref[...], placement_ref, slots)
+    (
+        out_ref, total_ref, sums_ref, stacked_ref, held_ref, rows_ref, sems, small_sems,
+    ) = refs[count + 4 + slots :]
+    rank = ups[0].shape[0]
+    copies = [(sum_ref, sums_ref.at[0]), (more_ref, sums_ref.at[1])]
+    copies += [(up, stacked_ref.at[pl.ds(b * rank, rank)]) for b, up in enumerate(ups)]
+    copies = [
+        pltpu.make_async_copy(source, target, small_sems.at[i])
+        for i, (source, target) in enumerate(copies)
+    ]
+    for copy in copies:
+        copy.start()
+    start_tiles(tile, depth, places, features, weight_ref, held_ref, rows_ref, sems)
+    for copy in copies:
+        copy.wait()
+    shrunk = (sums_ref[0] + sums_ref[1]).astype(jnp.bfloat16).astype(jnp.float32)
     spread = jnp.concatenate(
-        [jnp.where(stored == owners_ref[b], shrunk, 0.0) for b in range(slots)], axis=0
-    )
-    stacked = jnp.concatenate([up[...] for up in ups], axis=0)
+        [jnp.where(stored_ref[...] == owner, shrunk, 0.0) for owner in owners_of(flips, pairs)], axis=0
+    )
     expanded = jnp.dot(
-        spread.T.astype(jnp.bfloat16), stacked, preferred_element_type=jnp.float32
+        spread.T.astype(jnp.bfloat16), stacked_ref[...], preferred_element_type=jnp.float32
     )
     expanded = expanded.astype(jnp.bfloat16).astype(jnp.float32)
     total_ref[...] = given[...] + LOWRANK_SCALE * expanded
@@ -153,7 +169,7 @@
     out_ref[...] = total_ref[...].astype(out_ref.dtype)
 
 
-def shrink_kernel(tile, slots, owners_ref, placement_ref, tokens_ref, tenant_ref, *refs):
+def shrink_kernel(tile, flips, pairs, slots, tokens_ref, stored_ref, *refs):
     downs, out_ref, held_ref, down_ref, sums_ref, sems = (
         refs[:slots], refs[slots], *refs[slots + 1 :]
     )
@@ -166,7 +182,6 @@
             pltpu.make_async_copy(
                 down.at[:, here], down_ref.at[k, pl.ds(b * rank, rank)], sems.at[1 + b, k]
             ).start()
-    stored = slot_of_row(tenant_ref[...], placement_ref, slots)
     sums_ref[...] = jnp.zeros_like(sums_ref)
 
     @pl.loop(0, tiles)
@@ -181,8 +196,8 @@
 
     sums = sums_ref[...].T
     total = jnp.zeros(out_ref.shape, jnp.float32)
-    for b in range(slots):
-        total += jnp.where(stored == owners_ref[b], sums[b * rank : (b + 1) * rank], 0.0)
+    for b, owner in enumerate(owners_of(flips, pairs)):
+        total += jnp.where(stored_ref[...] == owner, sums[b * rank : (b + 1) * rank], 0.0)
     out_ref[...] = total
 
 
@@ -195,10 +210,7 @@
     groups = lax.axis_size("adapter")
     parts = lax.axis_size("parts")
     me = lax.axis_index("tensor")
-    group = lax.axis_index("adapter")
-    part = lax.axis_index("parts")
     rank, columns = lowrank_up_weight.shape[1:]
-    tenant_row = tenant.reshape(1, rows)
     edges = [0] + [int(depth * cut) // LANES * LANES for cut in CUTS] + [depth]
     tile = math.gcd(*edges)
 
@@ -244,12 +256,22 @@
     hops = range(CORES, tensors, CORES)
     far = [[flipped(chunk, "tensor", hop) for hop in hops] for chunk in chunks]
 
-    def spread_out(m):
-        starts, features = [], []
-        for hop, value in zip(hops, far[m]):
-            features += [value, flipped(value, "tensor", 1)]
-            starts += [(me ^ hop) * depth + edges[m], (me ^ hop ^ 1) * depth + edges[m]]
-        return starts, features
+    def across(m):
+        return [flipped(value, "tensor", 1) for value in far[m]]
+
+    def far_places(m):
+        return [(hop, edges[m]) for hop in hops]
+
+    def near_places(m):
+        return [(hop ^ 1, edges[m]) for hop in hops]
+
+    def products(places, features, total):
+        return call(
+            functools.partial(products_kernel, tile, depth, places),
+            jax.ShapeDtypeStruct((rows, columns), jnp.float32),
+            [ANYWHERE] + [ANYWHERE] * len(features) + [VECTOR],
+            tile_scratch(tile, features, columns),
+        )(frozen_projection_weight, *features, total)
 
     flips = list(range(1, groups))
     pairs = []
@@ -261,49 +283,60 @@
         for pair in pairs
     ]
 
-    def fetch(value):
-        single = [flipped(value, "adapter", flip) for flip in flips]
-        return single, [lax.ppermute(value, ("parts", "adapter"), route) for route in routes]
-
-    owners = [group] + [group ^ flip for flip in flips]
-    for pair in pairs:
-        owners += [
-            group ^ jnp.where(part == 0, *pair), group ^ jnp.where(part == 0, pair[1], pair[0])
-        ]
+    def fetch_far(value):
+        return [lax.ppermute(value, ("parts", "adapter"), route) for route in routes]
+
+    def fetch_near(value):
+        return [flipped(value, "adapter", flip) for flip in flips]
+
+    def swap(values):
+        return [flipped(value, "parts", 1) for value in values]
+
     own, neighbour, here = chained(own, neighbour, tokens)
-    single, fetched = fetch(own)
-    total = products(tile, [me * depth], [here], frozen_projection_weight)
-    single, fetched, total = chained(single, fetched, total)
-    swapped = [flipped(value, "parts", 1) for value in fetched]
+    fetched = fetch_far(own)
+    total, stored = call(
+        functools.partial(first_kernel, tile, depth, [(0, 0)], slots),
+        [
+            jax.ShapeDtypeStruct((rows, columns), jnp.float32),
+            jax.ShapeDtypeStruct((1, rows), jnp.int32),
+        ],
+        [SCALAR, VECTOR, ANYWHERE, ANYWHERE],
+        tile_scratch(tile, [tokens], columns),
+        [VECTOR, VECTOR],
+    )(placement, tenant.reshape(1, rows), frozen_projection_weight, here)
+    total, own, far[0] = chained(total, own, far[0])
+    single = fetch_near(own)
+    fetched, total = chained(fetched, total)
+    swapped = swap(fetched)
     total, neighbour = chained(total, neighbour)
-    total = products(tile, [(me ^ 1) * depth], [neighbour], frozen_projection_weight, total)
+    total = products([(1, 0)], [neighbour], total)
+    near = across(0)
+    total = products(far_places(0) + near_places(0), far[0] + near, total)
     total, up = chained(total, lowrank_up_weight[0])
-    single_up, fetched_up = fetch(up)
-    swapped, total = chained(swapped, total)
+    single_up, fetched_up = fetch_near(up), fetch_far(up)
+    single, swapped, total = chained(single, swapped, total)
     downs = [own] + single
-    for i in range(len(pairs)):
-        downs += [fetched[i], swapped[i]]
-    owners = jnp.stack(owners)
+    for pair in zip(fetched, swapped):
+        downs += pair
 
     tiles = depth // tile
     partial = call(
-        functools.partial(shrink_kernel, tile, slots),
+        functools.partial(shrink_kernel, tile, flips, pairs, slots),
         jax.ShapeDtypeStruct((rank, rows), jnp.float32),
-        [SCALAR, SCALAR, ANYWHERE, VECTOR] + [ANYWHERE] * slots,
+        [ANYWHERE, VECTOR] + [ANYWHERE] * slots,
         [
             pltpu.VMEM((tiles, rows, tile), jnp.bfloat16),
             pltpu.VMEM((tiles, slots * rank, tile), jnp.bfloat16),
             pltpu.VMEM((rows, slots * rank), jnp.float32),
             pltpu.SemaphoreType.DMA((1 + slots, tiles)),
         ],
-    )(owners, placement, tokens, tenant_row, *downs)
-    far[0], fetched_up, partial = chained(far[0], fetched_up, partial)
-    swapped_up = [flipped(value, "parts", 1) for value in fetched_up]
+    )(tokens, stored, *downs)
+    far[1], fetched_up, partial = chained(far[1], fetched_up, partial)
     ups = [up] + single_up
-    for i in range(len(pairs)):
-        ups += [fetched_up[i], swapped_up[i]]
-    starts, features = spread_out(0)
-    total = products(tile, starts[::2], features[::2], frozen_projection_weight, total)
+    for pair in zip(fetched_up, swap(fetched_up)):
+        ups += pair
+    middle = across(1)
+    total = products(far_places(1), far[1], total)
     flip = 1
     while flip < tensors // 2:
         received = flipped(partial, "tensor", flip)
@@ -312,25 +345,23 @@
         partial += received
         flip *= 2
     more = flipped(partial, "tensor", flip)
-    total, partial = chained(total, partial)
-    total = products(tile, starts[1::2], features[1::2], frozen_projection_weight, total)
-    far[1], ups, total = chained(far[1], ups, total)
-    starts, features = spread_out(1)
-    total = products(tile, starts[::2], features[::2], frozen_projection_weight, total)
-    starts = starts[1::2]
-    features, more, total = chained(features[1::2], more, total)
+    far[2], ups, total, partial = chained(far[2], ups, total, partial)
+    near = across(2)
+    total = products(near_places(1) + far_places(2), middle + far[2], total)
+    near, more, total = chained(near, more, total)
 
     return call(
-        functools.partial(last_kernel, tile, len(features), slots),
+        functools.partial(last_kernel, tile, depth, near_places(2), flips, pairs, slots),
         jax.ShapeDtypeStruct((rows, columns), jnp.bfloat16),
-        [SCALAR, SCALAR, SCALAR, ANYWHERE]
-        + [ANYWHERE] * len(features)
-        + [VECTOR] * (4 + slots),
-        [pltpu.VMEM((rows, columns), jnp.float32)] + tile_scratch(tile, features, columns),
-    )(
-        jnp.stack(starts), owners, placement, frozen_projection_weight, *features, total, tenant_row,
-        partial, more, *ups,
-    )
+        [ANYWHERE] + [ANYWHERE] * len(near) + [VECTOR] * 2 + [ANYWHERE] * (2 + slots),
+        [
+            pltpu.VMEM((rows, columns), jnp.float32),
+            pltpu.VMEM((2, rank, rows), jnp.float32),
+            pltpu.VMEM((slots * rank, columns), jnp.bfloat16),
+        ]
+        + tile_scratch(tile, near, columns)
+        + [pltpu.SemaphoreType.DMA((2 + slots,))],
+    )(frozen_projection_weight, *near, total, stored, partial, more, *ups)
 
 
 def solution(mesh):

time: 53.3 us -> 53.7 us (level)
  starting transfers between devices: 17 us -> 20 us
  waiting for transfers between devices: 13.9 us -> 12 us
  other arithmetic: 0.73 us -> 0.02 us
    ppermute x2, waiting for transfers between devices: 3.17 us -> 0.64 us  [fetch_far(): lax.ppermute(value, ('parts', 'adapter'), route)]
    ppermute x14 -> x16, starting transfers between devices: 12.6 us -> 14.5 us  [flipped(): return lax.ppermute(value, axis, [(i, i ^ flip) for i in range(count)])]
    ppermute x2, starting transfers between devices: 4.41 us -> 5.43 us  [fetch_far(): lax.ppermute(value, ('parts', 'adapter'), route)]
    add x1, other arithmetic: 0.65 us -> 0.02 us  [body(): partial += received]
    ppermute x14 -> x16, waiting for transfers between devices: 10.7 us -> 11.3 us  [flipped(): return lax.ppermute(value, axis, [(i, i ^ flip) for i in range(count)])]
  transfers between devices with their start and end apart: 16 -> 18, of which waited for: 7 -> 5; matrix products, arithmetic and copies ran while one was open for 1% -> 0% of each run, Pallas kernels for 32% -> 33%
where the time goes in v10:
time: 53.7 us; the launch traced here: 53.3 us
  Pallas kernels  20.4 us (38%)
  starting transfers between devices  20 us (37%)
  waiting for transfers between devices  12 us (22%)
  local copies, waits for them, and re-layouts  0.86 us (2%)
    ppermute x16, starting transfers between devices, flipped(): return lax.ppermute(value, axis, [(i, i ^ flip) for i in range(count)])  14.5 us
    ppermute x16, waiting for transfers between devices, flipped(): return lax.ppermute(value, axis, [(i, i ^ flip) for i in range(count)])  11.3 us
    pallas_call x4, Pallas kernels, products(): call(functools.partial(products_kernel, tile, depth, places), jax.ShapeDt...  8.57 us
    ppermute x2, starting transfers between devices, fetch_far(): lax.ppermute(value, ('parts', 'adapter'), route)  5.43 us
    pallas_call x1, Pallas kernels, body(): call(functools.partial(first_kernel, tile, depth, [(0, 0)], slots), [jax....  3.14 us
    pallas_call x1, Pallas kernels, body(): call(functools.partial(cut_kernel, edges), [jax.ShapeDtypeStruct((rows, b...  2.76 us
    pallas_call x1, Pallas kernels, body(): call(functools.partial(last_kernel, tile, depth, near_places(2), flips, p...  2.67 us
    pallas_call x1, Pallas kernels, body(): call(functools.partial(shrink_kernel, tile, flips, pairs, slots), jax.Sha...  2.52 us
  transfers between devices with their start and end apart: 18, of which 5 were waited for; matrix products, arithmetic and copies ran while one was open for 0% of the time, Pallas kernels for 33%

profile of v10, /device:TPU:0, one launch (start us, length us, event | category | flops | bytes accessed | tf_op | source)
XLA Modules:
  0.0 53.3 jit_solution(7131800059786272709)
XLA Ops:
  0.5 2.8 %shard_map.64 = (bf16[384,1024]{1,0:T(8,128)(2,1)}, bf16[384,512]{1,0:T(8,128)(2,1)}, bf16[384,512]{1,0:T(8,128)(2,1)}, bf16[16,2048]{1,0:T(8,128)(2,1)}, bf16[1...) custom-call(bf16[384,2048]{1,0:T(8,128)(2,1)} %tokens_ref.3, bf16[16,8192]{1,0:T(8,128)(2,1)} %bitcast.6), custom_call_target="tpu_custom_call" | custom-call | tf_op jit(solution)/shard_map/pallas_call | solution.py:221
  3.5 2.9 %collective-permute-start.2 = (bf16[16,2048]{1,0:T(8,128)(2,1)}, bf16[16,2048]{1,0:T(8,128)(2,1)S(1)}, u32[]{:S(2)}, u32[]{:S(2)}) collective-permute-start(bf16[16,2048]{1,0:T(8,128)(2,1)} %get-tuple-element.47), channel_id=1, source_target_pairs={{0,2},{1,3},{2,0},{3,1},{4,6},{5,7},{6,4},{7,5},{8,10},{9,11},{10,... | collective-permute-start | bytes 196616 | tf_op jit(solution)/shard_map/ppermute | solution.py:25
  6.4 1.5 %collective-permute-start.5 = (bf16[384,1024]{1,0:T(8,128)(2,1)}, bf16[384,1024]{1,0:T(8,128)(2,1)S(1)}, u32[]{:S(2)}, u32[]{:S(2)}) collective-permute-start(bf16[384,1024]{1,0:T(8,128)(2,1)} %get-tuple-element.52), channel_id=1, source_target_pairs={{0,2},{1,3},{2,0},{3,1},{4,6},{5,7},{6,4},{7,5},{8,10},{9,11},{10,... | collective-permute-start | bytes 2359304 | tf_op jit(solution)/shard_map/ppermute | solution.py:25
  7.8 0.6 %collective-permute-start.9 = (bf16[384,512]{1,0:T(8,128)(2,1)}, bf16[384,512]{1,0:T(8,128)(2,1)}, u32[]{:S(2)}, u32[]{:S(2)}) collective-permute-start(bf16[384,512]{1,0:T(8,128)(2,1)} %get-tuple-element.60), channel_id=1, source_target_pairs={{0,2},{1,3},{2,0},{3,1},{4,6},{5,7},{6,4},{7,5},{8,10},{9,11},{10,... | collective-permute-start | bytes 1179656 | tf_op jit(solution)/shard_map/ppermute | solution.py:25
  8.4 0.6 %collective-permute-done.2.refs_2_ = bf16[16,2048]{1,0:T(8,128)(2,1)S(1)} collective-permute-done((bf16[16,2048]{1,0:T(8,128)(2,1)}, bf16[16,2048]{1,0:T(8,128)(2,1)S(1)}, u32[]{:S(2)}, u32[]{:S(2)}) %collective-permute-start.2) | collective-permute-done | bytes 65568 | tf_op jit(solution)/shard_map/ppermute | solution.py:25
  9.0 2.4 %collective-permute-start = (bf16[384,512]{1,0:T(8,128)(2,1)}, bf16[384,512]{1,0:T(8,128)(2,1)}, u32[]{:S(2)}, u32[]{:S(2)}) collective-permute-start(bf16[384,512]{1,0:T(8,128)(2,1)} %get-tuple-element.44), channel_id=1, source_target_pairs={{0,2},{1,3},{2,0},{3,1},{4,6},{5,7},{6,4},{7,5},{8,10},{9,11},{10,... | collective-permute-start | bytes 1179656 | tf_op jit(solution)/shard_map/ppermute | solution.py:25
  11.4 0.8 %copy-done.1 = bf16[16,2048]{1,0:T(8,128)(2,1)S(1)} copy-done((bf16[16,2048]{1,0:T(8,128)(2,1)S(1)}, bf16[16,2048]{1,0:T(8,128)(2,1)}, u32[]{:S(2)}) %copy-start.1) | copy-done | bytes 65560
  12.3 0.7 %shard_map.65.refs_0_ = bf16[64,2048]{1,0:T(8,128)(2,1)} custom-call(bf16[16,2048]{1,0:T(8,128)(2,1)S(1)} %copy-done.1, bf16[16,2048]{1,0:T(8,128)(2,1)S(1)} %collective-permute-done.1.refs_1_, bf16[16,2048]{1,0:T(8,128)(2,1)S(1)} %collective-permute-done.2.refs_2_, bf16[16,2048]{1,0:T(8,128)(2,1)S(1)} %collective-permute-done.3.refs_3_), custom_call_target="tpu_custom_call" | custom-call | tf_op jit(solution)/shard_map/pallas_call | solution.py:241
  13.0 2.8 %collective-permute-start.7 = (bf16[64,2048]{1,0:T(8,128)(2,1)}, bf16[64,2048]{1,0:T(8,128)(2,1)}, u32[]{:S(2)}, u32[]{:S(2)}) collective-permute-start(bf16[64,2048]{1,0:T(8,128)(2,1)} %shard_map.65.refs_0_), channel_id=1, source_target_pairs={{0,8},{4,12},{8,0},{12,4},{16,28},{20,24},{24,20},{28,16},{1,9},{5... | collective-permute-start | bytes 786440 | tf_op jit(solution)/shard_map/ppermute | solution.py:287
  15.8 3.1 %shard_map.66 = (f32[384,512]{1,0:T(8,128)S(1)}, s32[1,384]{1,0:T(1,128)S(1)}) custom-call(s32[4]{0:T(128)S(1)} %copy-done.3, s32[1,384]{1,0:T(1,128)S(1)} %bitcast.5, bf16[8192,512]{1,0:T(8,128)(2,1)} %weight_ref.11, bf16[384,2048]{1,0:T(8,128)(2,1)S(1)} %copy-done), custom_call_target="tpu_custom_call" | custom-call | flops 99999997952 | tf_op jit(solution)/shard_map/pallas_call | solution.py:297
  19.0 8.8 %collective-permute-done.5.refs_0_ = bf16[384,1024]{1,0:T(8,128)(2,1)S(1)} collective-permute-done((bf16[384,1024]{1,0:T(8,128)(2,1)}, bf16[384,1024]{1,0:T(8,128)(2,1)S(1)}, u32[]{:S(2)}, u32[]{:S(2)}) %collective-permute-start.5) | collective-permute-done | bytes 786464 | tf_op jit(solution)/shard_map/ppermute | solution.py:25
  27.9 1.7 %collective-permute-start.11 = (bf16[64,2048]{1,0:T(8,128)(2,1)}, bf16[64,2048]{1,0:T(8,128)(2,1)}, u32[]{:S(2)}, u32[]{:S(2)}) collective-permute-start(bf16[64,2048]{1,0:T(8,128)(2,1)} %shard_map.65.refs_0_), channel_id=1, source_target_pairs={{0,4},{4,0},{8,12},{12,8},{1,5},{5,1},{9,13},{13,9},{2,6},{6,2},{1... | collective-permute-start | bytes 786440 | tf_op jit(solution)/shard_map/ppermute | solution.py:25
  29.6 1.5 %collective-permute-start.12 = (bf16[64,2048]{1,0:T(8,128)(2,1)}, bf16[64,2048]{1,0:T(8,128)(2,1)}, u32[]{:S(2)}, u32[]{:S(2)}) collective-permute-start(bf16[64,2048]{1,0:T(8,128)(2,1)} %collective-permute-done.7.refs_2_), channel_id=1, source_target_pairs={{0,16},{16,0},{1,17},{17,1},{2,18},{18,2},{3,19},{19,3},{4,20},{20... | collective-permute-start | bytes 786440 | tf_op jit(solution)/shard_map/ppermute | solution.py:25
  31.1 2.6 %shard_map.67.refs_2_ = f32[384,512]{1,0:T(8,128)S(1)} custom-call(bf16[8192,512]{1,0:T(8,128)(2,1)} %weight_ref.11, bf16[384,2048]{1,0:T(8,128)(2,1)S(1)} %collective-permute-done.4.refs_0_, f32[384,512]{1,0:T(8,128)S(1)} %get-tuple-element.58.refs_1_), custom_call_target="tpu_custom_call" | custom-call | flops 99999997952 | tf_op jit(solution)/shard_map/pallas_call | solution.py:269
  33.8 2.6 %shard_map.68.refs_1_ = f32[384,512]{1,0:T(8,128)S(1)} custom-call(bf16[8192,512]{1,0:T(8,128)(2,1)} %weight_ref.11, bf16[384,1024]{1,0:T(8,128)(2,1)S(1)} %collective-permute-done.5.refs_0_, bf16[384,1024]{1,0:T(8,128)(2,1)S(1)} %collective-permute-done.6.refs_1_, f32[384,512]{1,0:T(8,128)S(1)} %shard_map.67.refs_2_), custom_call_target="tpu_custom_call" | custom-call | flops 99999997952 | tf_op jit(solution)/shard_map/pallas_call | solution.py:269
  36.4 2.7 %collective-permute-start.10 = (bf16[64,512]{1,0:T(8,128)(2,1)}, bf16[64,512]{1,0:T(8,128)(2,1)S(1)}, u32[]{:S(2)}, u32[]{:S(2)}) collective-permute-start(bf16[64,512]{1,0:T(8,128)(2,1)} %bitcast.3.refs_5_), channel_id=1, source_target_pairs={{0,8},{4,12},{8,0},{12,4},{16,28},{20,24},{24,20},{28,16},{1,9},{5... | collective-permute-start | bytes 196616 | tf_op jit(solution)/shard_map/ppermute | solution.py:287
  39.5 2.5 %shard_map.69 = f32[64,384]{1,0:T(8,128)S(1)} custom-call(bf16[384,2048]{1,0:T(8,128)(2,1)S(1)} %copy-done, s32[1,384]{1,0:T(1,128)S(1)} %get-tuple-element.61.stored_ref.refs_2_, bf16[64,2048]{1,0:T(8,128)(2,1)} %shard_map.65.refs_0_, bf16[64,2048]{1,0:T(8,128)(2,1)} %collective-permute-done.11.refs_1_, bf16[64,2048]{1,0:T(8,128)(2,1)} %collective-permute-done.7.refs_2_, ...), custom_call_target="tpu_custom_call" | custom-call | flops 99999997952 | tf_op jit(solution)/shard_map/pallas_call | solution.py:323
  42.0 0.6 %collective-permute-done.10.refs_7_ = bf16[64,512]{1,0:T(8,128)(2,1)S(1)} collective-permute-done((bf16[64,512]{1,0:T(8,128)(2,1)}, bf16[64,512]{1,0:T(8,128)(2,1)S(1)}, u32[]{:S(2)}, u32[]{:S(2)}) %collective-permute-start.10) | collective-permute-done | bytes 65568 | tf_op jit(solution)/shard_map/ppermute | solution.py:287
  42.7 1.1 %collective-permute-start.13 = (bf16[64,512]{1,0:T(8,128)(2,1)S(1)}, bf16[64,512]{1,0:T(8,128)(2,1)S(1)}, u32[]{:S(2)}, u32[]{:S(2)}) collective-permute-start(bf16[64,512]{1,0:T(8,128)(2,1)S(1)} %collective-permute-done.10.refs_7_), channel_id=1, source_target_pairs={{0,16},{16,0},{1,17},{17,1},{2,18},{18,2},{3,19},{19,3},{4,20},{20... | collective-permute-start | bytes 196616 | tf_op jit(solution)/shard_map/ppermute | solution.py:25
  44.0 1.5 %shard_map.70.refs_2_ = f32[384,512]{1,0:T(8,128)S(1)} custom-call(bf16[8192,512]{1,0:T(8,128)(2,1)} %weight_ref.11, bf16[384,512]{1,0:T(8,128)(2,1)} %collective-permute-done.9.refs_0_, f32[384,512]{1,0:T(8,128)S(1)} %shard_map.68.refs_1_), custom_call_target="tpu_custom_call" | custom-call | flops 99999997952 | tf_op jit(solution)/shard_map/pallas_call | solution.py:269
  45.6 1.4 %collective-permute-start.16 = (f32[64,384]{1,0:T(8,128)S(1)}, f32[64,384]{1,0:T(8,128)S(1)}, u32[]{:S(2)}, u32[]{:S(2)}) collective-permute-start(f32[64,384]{1,0:T(8,128)S(1)} %add.3.refs_3_), channel_id=1, source_target_pairs={{0,2},{1,3},{2,0},{3,1},{4,6},{5,7},{6,4},{7,5},{8,10},{9,11},{10,... | collective-permute-start | bytes 294920 | tf_op jit(solution)/shard_map/ppermute | solution.py:25
  47.2 1.8 %shard_map.71.refs_1_ = f32[384,512]{1,0:T(8,128)S(1)} custom-call(bf16[8192,512]{1,0:T(8,128)(2,1)} %weight_ref.11, bf16[384,512]{1,0:T(8,128)(2,1)S(1)} %collective-permute-done.17.refs_0_, bf16[384,512]{1,0:T(8,128)(2,1)} %collective-permute-done.refs_1_, f32[384,512]{1,0:T(8,128)S(1)} %shard_map.70.refs_2_), custom_call_target="tpu_custom_call" | custom-call | flops 99999997952 | tf_op jit(solution)/shard_map/pallas_call | solution.py:269
  49.0 1.7 %collective-permute-done.16.refs_4_ = f32[64,384]{1,0:T(8,128)S(1)} collective-permute-done((f32[64,384]{1,0:T(8,128)S(1)}, f32[64,384]{1,0:T(8,128)S(1)}, u32[]{:S(2)}, u32[]{:S(2)}) %collective-permute-start.16) | collective-permute-done | bytes 98336 | tf_op jit(solution)/shard_map/ppermute | solution.py:25
  50.7 2.7 %shard_map.72 = bf16[384,512]{1,0:T(8,128)(2,1)} custom-call(bf16[8192,512]{1,0:T(8,128)(2,1)} %weight_ref.11, bf16[384,512]{1,0:T(8,128)(2,1)S(1)} %collective-permute-done.15.refs_0_, f32[384,512]{1,0:T(8,128)S(1)} %shard_map.71.refs_1_, s32[1,384]{1,0:T(1,128)S(1)} %copy-done.5, f32[64,384]{1,0:T(8,128)S(1)} %add.3.refs_3_, ...), custom_call_target="tpu_custom_call" | custom-call | flops 99999997952 | tf_op jit(solution)/shard_map/pallas_call | solution.py:353
  (34 shorter events, 1.7 us)
Async XLA Ops:
  0.0 15.8 %copy-start = (bf16[384,2048]{1,0:T(8,128)(2,1)S(1)}, bf16[384,2048]{1,0:T(8,128)(2,1)}, u32[]{:S(2)}) copy-start(bf16[384,2048]{1,0:T(8,128)(2,1)} %tokens_ref.3) | copy-start | bytes 4718596
  0.0 15.8 %copy-start.2 = (s32[384,1]{0,1:T(1,128)S(1)}, s32[384,1]{0,1:T(1,128)}, u32[]{:S(2)}) copy-start(s32[384,1]{0,1:T(1,128)} %param.7) | copy-start | bytes 4612
  0.0 15.8 %copy-start.3 = (s32[4]{0:T(128)S(1)}, s32[4]{0:T(128)}, u32[]{:S(2)}) copy-start(s32[4]{0:T(128)} %placement_ref.1) | copy-start | bytes 52
  0.0 13.0 %collective-permute-start.4 = (bf16[384,2048]{1,0:T(8,128)(2,1)}, bf16[384,2048]{1,0:T(8,128)(2,1)S(1)}, u32[]{:S(2)}, u32[]{:S(2)}) collective-permute-start(bf16[384,2048]{1,0:T(8,128)(2,1)} %tokens_ref.3), channel_id=1, source_target_pairs={{0,1},{1,0},{2,3},{3,2},{4,5},{5,4},{6,7},{7,6},{8,9},{9,8},{10,11... | collective-permute-start | bytes 4718600 | tf_op jit(solution)/shard_map/ppermute | solution.py:25
  3.3 4.5 %collective-permute-start.1 = (bf16[16,2048]{1,0:T(8,128)(2,1)}, bf16[16,2048]{1,0:T(8,128)(2,1)S(1)}, u32[]{:S(2)}, u32[]{:S(2)}) collective-permute-start(bf16[16,2048]{1,0:T(8,128)(2,1)} %get-tuple-element.46), channel_id=1, source_target_pairs={{0,1},{1,0},{2,3},{3,2},{4,5},{5,4},{6,7},{7,6},{8,9},{9,8},{10,11... | collective-permute-start | bytes 196616 | tf_op jit(solution)/shard_map/ppermute | solution.py:25
  3.5 5.6 %collective-permute-start.2 = (bf16[16,2048]{1,0:T(8,128)(2,1)}, bf16[16,2048]{1,0:T(8,128)(2,1)S(1)}, u32[]{:S(2)}, u32[]{:S(2)}) collective-permute-start(bf16[16,2048]{1,0:T(8,128)(2,1)} %get-tuple-element.47), channel_id=1, source_target_pairs={{0,2},{1,3},{2,0},{3,1},{4,6},{5,7},{6,4},{7,5},{8,10},{9,11},{10,... | collective-permute-start | bytes 196616 | tf_op jit(solution)/shard_map/ppermute | solution.py:25
  6.4 5.1 %collective-permute-start.3 = (bf16[16,2048]{1,0:T(8,128)(2,1)}, bf16[16,2048]{1,0:T(8,128)(2,1)S(1)}, u32[]{:S(2)}, u32[]{:S(2)}) collective-permute-start(bf16[16,2048]{1,0:T(8,128)(2,1)} %get-tuple-element.48), channel_id=1, source_target_pairs={{0,3},{1,2},{2,1},{3,0},{4,7},{5,6},{6,5},{7,4},{8,11},{9,10},{10,... | collective-permute-start | bytes 196616 | tf_op jit(solution)/shard_map/ppermute | solution.py:25
  6.4 21.5 %collective-permute-start.5 = (bf16[384,1024]{1,0:T(8,128)(2,1)}, bf16[384,1024]{1,0:T(8,128)(2,1)S(1)}, u32[]{:S(2)}, u32[]{:S(2)}) collective-permute-start(bf16[384,1024]{1,0:T(8,128)(2,1)} %get-tuple-element.52), channel_id=1, source_target_pairs={{0,2},{1,3},{2,0},{3,1},{4,6},{5,7},{6,4},{7,5},{8,10},{9,11},{10,... | collective-permute-start | bytes 2359304 | tf_op jit(solution)/shard_map/ppermute | solution.py:25
  7.8 34.2 %collective-permute-start.9 = (bf16[384,512]{1,0:T(8,128)(2,1)}, bf16[384,512]{1,0:T(8,128)(2,1)}, u32[]{:S(2)}, u32[]{:S(2)}) collective-permute-start(bf16[384,512]{1,0:T(8,128)(2,1)} %get-tuple-element.60), channel_id=1, source_target_pairs={{0,2},{1,3},{2,0},{3,1},{4,6},{5,7},{6,4},{7,5},{8,10},{9,11},{10,... | collective-permute-start | bytes 1179656 | tf_op jit(solution)/shard_map/ppermute | solution.py:25
  9.0 38.0 %collective-permute-start = (bf16[384,512]{1,0:T(8,128)(2,1)}, bf16[384,512]{1,0:T(8,128)(2,1)}, u32[]{:S(2)}, u32[]{:S(2)}) collective-permute-start(bf16[384,512]{1,0:T(8,128)(2,1)} %get-tuple-element.44), channel_id=1, source_target_pairs={{0,2},{1,3},{2,0},{3,1},{4,6},{5,7},{6,4},{7,5},{8,10},{9,11},{10,... | collective-permute-start | bytes 1179656 | tf_op jit(solution)/shard_map/ppermute | solution.py:25
  11.4 0.8 %copy-start.1 = (bf16[16,2048]{1,0:T(8,128)(2,1)S(1)}, bf16[16,2048]{1,0:T(8,128)(2,1)}, u32[]{:S(2)}) copy-start(bf16[16,2048]{1,0:T(8,128)(2,1)} %get-tuple-element.45.refs_0_) | copy-start | bytes 196612
  13.0 16.6 %collective-permute-start.7 = (bf16[64,2048]{1,0:T(8,128)(2,1)}, bf16[64,2048]{1,0:T(8,128)(2,1)}, u32[]{:S(2)}, u32[]{:S(2)}) collective-permute-start(bf16[64,2048]{1,0:T(8,128)(2,1)} %shard_map.65.refs_0_), channel_id=1, source_target_pairs={{0,8},{4,12},{8,0},{12,4},{16,28},{20,24},{24,20},{28,16},{1,9},{5... | collective-permute-start | bytes 786440 | tf_op jit(solution)/shard_map/ppermute | solution.py:287
  19.0 20.5 %copy-start.4 = (s32[1,384]{1,0:T(1,128)}, s32[1,384]{1,0:T(1,128)S(1)}, u32[]{:S(2)}) copy-start(s32[1,384]{1,0:T(1,128)S(1)} %get-tuple-element.61.stored_ref.refs_2_) | copy-start | bytes 4612
  27.8 5.9 %collective-permute-start.6 = (bf16[384,1024]{1,0:T(8,128)(2,1)S(1)}, bf16[384,1024]{1,0:T(8,128)(2,1)S(1)}, u32[]{:S(2)}, u32[]{:S(2)}) collective-permute-start(bf16[384,1024]{1,0:T(8,128)(2,1)S(1)} %collective-permute-done.5.refs_0_), channel_id=1, source_target_pairs={{0,1},{1,0},{2,3},{3,2},{4,5},{5,4},{6,7},{7,6},{8,9},{9,8},{10,11... | collective-permute-start | bytes 2359304 | tf_op jit(solution)/shard_map/ppermute | solution.py:25
  27.9 11.1 %collective-permute-start.11 = (bf16[64,2048]{1,0:T(8,128)(2,1)}, bf16[64,2048]{1,0:T(8,128)(2,1)}, u32[]{:S(2)}, u32[]{:S(2)}) collective-permute-start(bf16[64,2048]{1,0:T(8,128)(2,1)} %shard_map.65.refs_0_), channel_id=1, source_target_pairs={{0,4},{4,0},{8,12},{12,8},{1,5},{5,1},{9,13},{13,9},{2,6},{6,2},{1... | collective-permute-start | bytes 786440 | tf_op jit(solution)/shard_map/ppermute | solution.py:25
  29.6 9.9 %collective-permute-start.12 = (bf16[64,2048]{1,0:T(8,128)(2,1)}, bf16[64,2048]{1,0:T(8,128)(2,1)}, u32[]{:S(2)}, u32[]{:S(2)}) collective-permute-start(bf16[64,2048]{1,0:T(8,128)(2,1)} %collective-permute-done.7.refs_2_), channel_id=1, source_target_pairs={{0,16},{16,0},{1,17},{17,1},{2,18},{18,2},{3,19},{19,3},{4,20},{20... | collective-permute-start | bytes 786440 | tf_op jit(solution)/shard_map/ppermute | solution.py:25
  36.4 6.3 %collective-permute-start.10 = (bf16[64,512]{1,0:T(8,128)(2,1)}, bf16[64,512]{1,0:T(8,128)(2,1)S(1)}, u32[]{:S(2)}, u32[]{:S(2)}) collective-permute-start(bf16[64,512]{1,0:T(8,128)(2,1)} %bitcast.3.refs_5_), channel_id=1, source_target_pairs={{0,8},{4,12},{8,0},{12,4},{16,28},{20,24},{24,20},{28,16},{1,9},{5... | collective-permute-start | bytes 196616 | tf_op jit(solution)/shard_map/ppermute | solution.py:287
  39.0 8.0 %collective-permute-start.8 = (bf16[64,512]{1,0:T(8,128)(2,1)}, bf16[64,512]{1,0:T(8,128)(2,1)}, u32[]{:S(2)}, u32[]{:S(2)}) collective-permute-start(bf16[64,512]{1,0:T(8,128)(2,1)} %bitcast.3.refs_5_), channel_id=1, source_target_pairs={{0,4},{4,0},{8,12},{12,8},{1,5},{5,1},{9,13},{13,9},{2,6},{6,2},{1... | collective-permute-start | bytes 196616 | tf_op jit(solution)/shard_map/ppermute | solution.py:25
  42.7 2.9 %collective-permute-start.14 = (f32[64,384]{1,0:T(8,128)S(1)}, f32[64,384]{1,0:T(8,128)S(1)}, u32[]{:S(2)}, u32[]{:S(2)}) collective-permute-start(f32[64,384]{1,0:T(8,128)S(1)} %shard_map.69), channel_id=1, source_target_pairs={{0,1},{1,0},{2,3},{3,2},{4,5},{5,4},{6,7},{7,6},{8,9},{9,8},{10,11... | collective-permute-start | bytes 294920 | tf_op jit(solution)/shard_map/ppermute | solution.py:25
  42.7 4.5 %collective-permute-start.13 = (bf16[64,512]{1,0:T(8,128)(2,1)S(1)}, bf16[64,512]{1,0:T(8,128)(2,1)S(1)}, u32[]{:S(2)}, u32[]{:S(2)}) collective-permute-start(bf16[64,512]{1,0:T(8,128)(2,1)S(1)} %collective-permute-done.10.refs_7_), channel_id=1, source_target_pairs={{0,16},{16,0},{1,17},{17,1},{2,18},{18,2},{3,19},{19,3},{4,20},{20... | collective-permute-start | bytes 196616 | tf_op jit(solution)/shard_map/ppermute | solution.py:25
  43.8 3.4 %collective-permute-start.17 = (bf16[384,512]{1,0:T(8,128)(2,1)}, bf16[384,512]{1,0:T(8,128)(2,1)S(1)}, u32[]{:S(2)}, u32[]{:S(2)}) collective-permute-start(bf16[384,512]{1,0:T(8,128)(2,1)} %collective-permute-done.9.refs_0_), channel_id=1, source_target_pairs={{0,1},{1,0},{2,3},{3,2},{4,5},{5,4},{6,7},{7,6},{8,9},{9,8},{10,11... | collective-permute-start | bytes 1179656 | tf_op jit(solution)/shard_map/ppermute | solution.py:25
  45.6 5.1 %copy-start.5 = (s32[1,384]{1,0:T(1,128)S(1)}, s32[1,384]{1,0:T(1,128)}, u32[]{:S(2)}) copy-start(s32[1,384]{1,0:T(1,128)} %copy-done.4) | copy-start | bytes 4612
  45.6 5.0 %collective-permute-start.16 = (f32[64,384]{1,0:T(8,128)S(1)}, f32[64,384]{1,0:T(8,128)S(1)}, u32[]{:S(2)}, u32[]{:S(2)}) collective-permute-start(f32[64,384]{1,0:T(8,128)S(1)} %add.3.refs_3_), channel_id=1, source_target_pairs={{0,2},{1,3},{2,0},{3,1},{4,6},{5,7},{6,4},{7,5},{8,10},{9,11},{10,... | collective-permute-start | bytes 294920 | tf_op jit(solution)/shard_map/ppermute | solution.py:25
  47.2 3.5 %collective-permute-start.15 = (bf16[384,512]{1,0:T(8,128)(2,1)}, bf16[384,512]{1,0:T(8,128)(2,1)S(1)}, u32[]{:S(2)}, u32[]{:S(2)}) collective-permute-start(bf16[384,512]{1,0:T(8,128)(2,1)} %collective-permute-done.refs_1_), channel_id=1, source_target_pairs={{0,1},{1,0},{2,3},{3,2},{4,5},{5,4},{6,7},{7,6},{8,9},{9,8},{10,11... | collective-permute-start | bytes 1179656 | tf_op jit(solution)/shard_map/ppermute | solution.py:25

commit v11 on v10

--- a/solution.py
+++ b/solution.py
@@ -51,17 +51,10 @@
         copy.wait()
 
 
-def cut_kernel(edges, tokens_ref, down_ref, *refs):
-    outs, sems = refs[:-1], refs[-1]
-    me, depth = lax.axis_index("tensor"), tokens_ref.shape[1]
-    cuts = len(edges) - 1
-    pairs = []
-    for flip, piece in enumerate(outs[cuts:]):
-        start = pl.multiple_of((me ^ flip) * depth, LANES)
-        pairs.append((down_ref.at[:, pl.ds(start, depth)], piece))
-    for a, b, chunk in zip(edges, edges[1:], outs):
-        pairs.append((tokens_ref.at[:, a:b], chunk))
-    run_copies(pairs, sems)
+def cut_kernel(edges, source_ref, *refs):
+    run_copies(
+        [(source_ref.at[:, a:b], out) for a, b, out in zip(edges, edges[1:], refs[:-1])], refs[-1]
+    )
 
 
 def order_kernel(rank_part, *refs):
@@ -142,10 +135,10 @@
     given, stored_ref, sum_ref, more_ref = refs[count : count + 4]
     ups = refs[count + 4 : count + 4 + slots]
     (
-        out_ref, total_ref, sums_ref, stacked_ref, held_ref, rows_ref, sems, small_sems,
+        out_ref, total_ref, sums_ref, received_ref, stacked_ref, held_ref, rows_ref, sems, small_sems,
     ) = refs[count + 4 + slots :]
     rank = ups[0].shape[0]
-    copies = [(sum_ref, sums_ref.at[0]), (more_ref, sums_ref.at[1])]
+    copies = [(sum_ref, sums_ref), (more_ref, received_ref)]
     copies += [(up, stacked_ref.at[pl.ds(b * rank, rank)]) for b, up in enumerate(ups)]
     copies = [
         pltpu.make_async_copy(source, target, small_sems.at[i])
@@ -156,7 +149,7 @@
     start_tiles(tile, depth, places, features, weight_ref, held_ref, rows_ref, sems)
     for copy in copies:
         copy.wait()
-    shrunk = (sums_ref[0] + sums_ref[1]).astype(jnp.bfloat16).astype(jnp.float32)
+    shrunk = (sums_ref[...] + received_ref[...].astype(jnp.float32)).astype(jnp.bfloat16).astype(jnp.float32)
     spread = jnp.concatenate(
         [jnp.where(stored_ref[...] == owner, shrunk, 0.0) for owner in owners_of(flips, pairs)], axis=0
     )
@@ -215,29 +208,23 @@
     tile = math.gcd(*edges)
 
     down = lowrank_down_weight[0].T
-    whole_tiles = down.shape[0] % 16 == 0
-    cuts = len(edges) - 1
-    if whole_tiles:
-        cut = call(
-            functools.partial(cut_kernel, edges),
-            [jax.ShapeDtypeStruct((rows, b - a), tokens.dtype) for a, b in zip(edges, edges[1:])]
-            + [jax.ShapeDtypeStruct((down.shape[0], depth), down.dtype)] * tensors,
-            [ANYWHERE, ANYWHERE],
-            [pltpu.SemaphoreType.DMA((cuts + tensors,))],
-            [VECTOR] * (cuts + tensors),
-            cost=FREE,
-            mib=60,
-        )(tokens, down)
-        chunks, pieces = list(cut[:cuts]), list(cut[cuts:])
-    else:
-        chunks = [tokens[:, a:b] for a, b in zip(edges, edges[1:])]
-        pieces = [
-            lax.dynamic_slice_in_dim(down, (me ^ flip) * depth, depth, axis=1)
-            for flip in range(tensors)
-        ]
-    neighbour = flipped(tokens, "tensor", 1)
+    pieces = [
+        lax.dynamic_slice_in_dim(down, (me ^ flip) * depth, depth, axis=1)
+        for flip in range(tensors)
+    ]
+    uncut, pieces = chained(tokens, pieces)
+    chunks = list(call(
+        functools.partial(cut_kernel, edges),
+        [jax.ShapeDtypeStruct((rows, b - a), tokens.dtype) for a, b in zip(edges, edges[1:])],
+        [ANYWHERE],
+        [pltpu.SemaphoreType.DMA((len(edges) - 1,))],
+        [VECTOR] * (len(edges) - 1),
+        mib=40,
+    )(uncut))
+    neighbour = flipped(uncut, "tensor", 1)
     pieces = [pieces[0]] + [flipped(pieces[f], "tensor", f) for f in range(1, tensors)]
-    if whole_tiles:
+    pieces, chunks[1] = chained(pieces, chunks[1])
+    if down.shape[0] % 16 == 0:
         own = call(
             functools.partial(order_kernel, down.shape[0]),
             jax.ShapeDtypeStruct((rank, depth), down.dtype),
@@ -254,7 +241,11 @@
         )
 
     hops = range(CORES, tensors, CORES)
-    far = [[flipped(chunk, "tensor", hop) for hop in hops] for chunk in chunks]
+
+    def send(m):
+        return [flipped(chunks[m], "tensor", hop) for hop in hops]
+
+    far = [send(0), send(1)]
 
     def across(m):
         return [flipped(value, "tensor", 1) for value in far[m]]
@@ -304,10 +295,12 @@
         tile_scratch(tile, [tokens], columns),
         [VECTOR, VECTOR],
     )(placement, tenant.reshape(1, rows), frozen_projection_weight, here)
-    total, own, far[0] = chained(total, own, far[0])
+    total, own, chunks[2] = chained(total, own, chunks[2])
+    far.append(send(2))
     single = fetch_near(own)
     fetched, total = chained(fetched, total)
     swapped = swap(fetched)
+    far[0], total = chained(far[0], total)
     total, neighbour = chained(total, neighbour)
     total = products([(1, 0)], [neighbour], total)
     near = across(0)
@@ -344,7 +337,7 @@
             received, total = chained(received, total)
         partial += received
         flip *= 2
-    more = flipped(partial, "tensor", flip)
+    more = flipped(partial.astype(jnp.bfloat16), "tensor", flip)
     far[2], ups, total, partial = chained(far[2], ups, total, partial)
     near = across(2)
     total = products(near_places(1) + far_places(2), middle + far[2], total)
@@ -356,7 +349,8 @@
         [ANYWHERE] + [ANYWHERE] * len(near) + [VECTOR] * 2 + [ANYWHERE] * (2 + slots),
         [
             pltpu.VMEM((rows, columns), jnp.float32),
-            pltpu.VMEM((2, rank, rows), jnp.float32),
+            pltpu.VMEM((rank, rows), jnp.float32),
+            pltpu.VMEM((rank, rows), jnp.bfloat16),
             pltpu.VMEM((slots * rank, columns), jnp.bfloat16),
         ]
         + tile_scratch(tile, near, columns)

time: 53.7 us -> 55 us (1.024)
  Pallas kernels: 20.4 us -> 18.8 us
  local copies, waits for them, and re-layouts: 0.86 us -> 2.39 us
  waiting for transfers between devices: 12 us -> 13 us
    ppermute x2, waiting for transfers between devices: 0.64 us -> 6.59 us  [fetch_far(): lax.ppermute(value, ('parts', 'adapter'), route)]
    ppermute x16, waiting for transfers between devices: 11.3 us -> 6.45 us  [flipped(): return lax.ppermute(value, axis, [(i, i ^ flip) for i in range(count)])]
    pallas_call x1, Pallas kernels: 2.76 us -> 1.05 us  [body(): call(functools.partial(cut_kernel, edges), [jax.ShapeDtypeStruct((rows, b...]
    dynamic_slice x0 -> x1, local copies, waits for them, and re-layouts: none -> 0.95 us  [body(): lax.dynamic_slice_in_dim(down, (me ^ flip) * depth, depth, axis=1)]
    unnamed x12 -> x14, local copies, waits for them, and re-layouts: 0.86 us -> 1.44 us
  transfers between devices with their start and end apart: 18 -> 18, of which waited for: 5 -> 5; matrix products, arithmetic and copies ran while one was open for 0% -> 0% of each run, Pallas kernels for 33% -> 30%
where the time goes in v11:
time: 55 us; the launch traced here: 54.7 us
  starting transfers between devices  20.3 us (37%)
  Pallas kernels  18.8 us (34%)
  waiting for transfers between devices  13 us (24%)
  local copies, waits for them, and re-layouts  2.39 us (4%)
    ppermute x16, starting transfers between devices, flipped(): return lax.ppermute(value, axis, [(i, i ^ flip) for i in range(count)])  15 us
    pallas_call x4, Pallas kernels, products(): call(functools.partial(products_kernel, tile, depth, places), jax.ShapeDt...  8.68 us
    ppermute x2, waiting for transfers between devices, fetch_far(): lax.ppermute(value, ('parts', 'adapter'), route)  6.59 us
    ppermute x16, waiting for transfers between devices, flipped(): return lax.ppermute(value, axis, [(i, i ^ flip) for i in range(count)])  6.45 us
    ppermute x2, starting transfers between devices, fetch_far(): lax.ppermute(value, ('parts', 'adapter'), route)  5.31 us
    pallas_call x1, Pallas kernels, body(): call(functools.partial(first_kernel, tile, depth, [(0, 0)], slots), [jax....  3.14 us
    pallas_call x1, Pallas kernels, body(): call(functools.partial(last_kernel, tile, depth, near_places(2), flips, p...  2.61 us
    pallas_call x1, Pallas kernels, body(): call(functools.partial(shrink_kernel, tile, flips, pairs, slots), jax.Sha...  2.53 us
  transfers between devices with their start and end apart: 18, of which 5 were waited for; matrix products, arithmetic and copies ran while one was open for 0% of the time, Pallas kernels for 30%

profile of v11, /device:TPU:0, one launch (start us, length us, event | category | flops | bytes accessed | tf_op | source)
XLA Modules:
  0.0 54.7 jit_solution(1293428530488122020)
XLA Ops:
  0.0 1.0 %dynamic-slice_bitcast_fusion = (bf16[16,2048]{1,0:T(8,128)(2,1)S(1)}, bf16[16,2048]{1,0:T(8,128)(2,1)S(1)}, bf16[16,2048]{1,0:T(8,128)(2,1)S(1)}, bf16[16,2048]{1,0:T(8,128)(2,1)S(1)}) fusion(bf16[1,8192,16]{1,2,0:T(8,128)(2,1)} %param.10, s32[]{:T(128)S(6)} %select_n.15, s32[]{:T(128)S(6)} %select_n.13, s32[]{:T(128)S(6)} %select_n.12, s32[]{:T(128)S(6)} %select_n.14), kind=kLoop, calls=%fused_computation | loop fusion | bytes 524304 | tf_op jit(solution)/shard_map/dynamic_slice | solution.py:212
  1.5 2.6 %collective-permute-start.1 = (bf16[16,2048]{1,0:T(8,128)(2,1)S(1)}, bf16[16,2048]{1,0:T(8,128)(2,1)S(1)}, u32[]{:S(2)}, u32[]{:S(2)}) collective-permute-start(bf16[16,2048]{1,0:T(8,128)(2,1)S(1)} %get-tuple-element.54), channel_id=1, source_target_pairs={{0,2},{1,3},{2,0},{3,1},{4,6},{5,7},{6,4},{7,5},{8,10},{9,11},{10,... | collective-permute-start | bytes 196616 | tf_op jit(solution)/shard_map/ppermute | solution.py:25
  4.3 1.4 %copy-done = bf16[384,2048]{1,0:T(8,128)(2,1)S(1)} copy-done((bf16[384,2048]{1,0:T(8,128)(2,1)S(1)}, bf16[384,2048]{1,0:T(8,128)(2,1)}, u32[]{:S(2)}) %copy-start) | copy-done | bytes 1572888
  5.7 1.1 %shard_map.64 = (bf16[384,1024]{1,0:T(8,128)(2,1)S(1)}, bf16[384,512]{1,0:T(8,128)(2,1)}, bf16[384,512]{1,0:T(8,128)(2,1)}) custom-call(bf16[384,2048]{1,0:T(8,128)(2,1)S(1)} %copy-done), custom_call_target="tpu_custom_call" | custom-call | flops 99999997952 | tf_op jit(solution)/shard_map/pallas_call | solution.py:216
  6.7 2.0 %collective-permute-start.5 = (bf16[384,1024]{1,0:T(8,128)(2,1)S(1)}, bf16[384,1024]{1,0:T(8,128)(2,1)S(1)}, u32[]{:S(2)}, u32[]{:S(2)}) collective-permute-start(bf16[384,1024]{1,0:T(8,128)(2,1)S(1)} %get-tuple-element.67), channel_id=1, source_target_pairs={{0,2},{1,3},{2,0},{3,1},{4,6},{5,7},{6,4},{7,5},{8,10},{9,11},{10,... | collective-permute-start | bytes 2359304 | tf_op jit(solution)/shard_map/ppermute | solution.py:25
  9.5 0.7 %shard_map.65.refs_0_ = bf16[64,2048]{1,0:T(8,128)(2,1)} custom-call(bf16[16,2048]{1,0:T(8,128)(2,1)S(1)} %get-tuple-element.58.refs_0_, bf16[16,2048]{1,0:T(8,128)(2,1)S(1)} %collective-permute-done.refs_1_, bf16[16,2048]{1,0:T(8,128)(2,1)S(1)} %collective-permute-done.1.refs_2_, bf16[16,2048]{1,0:T(8,128)(2,1)S(1)} %collective-permute-done.2.refs_3_), custom_call_target="tpu_custom_call" | custom-call | tf_op jit(solution)/shard_map/pallas_call | solution.py:228
  10.2 2.7 %collective-permute-start.6 = (bf16[64,2048]{1,0:T(8,128)(2,1)}, bf16[64,2048]{1,0:T(8,128)(2,1)}, u32[]{:S(2)}, u32[]{:S(2)}) collective-permute-start(bf16[64,2048]{1,0:T(8,128)(2,1)} %shard_map.65.refs_0_), channel_id=1, source_target_pairs={{0,8},{4,12},{8,0},{12,4},{16,28},{20,24},{24,20},{28,16},{1,9},{5... | collective-permute-start | bytes 786440 | tf_op jit(solution)/shard_map/ppermute | solution.py:278
  12.9 3.1 %shard_map.66 = (f32[384,512]{1,0:T(8,128)S(1)}, s32[1,384]{1,0:T(1,128)S(1)}) custom-call(s32[4]{0:T(128)S(1)} %copy-done.4, s32[1,384]{1,0:T(1,128)S(1)} %bitcast.18, bf16[8192,512]{1,0:T(8,128)(2,1)} %weight_ref.11, bf16[384,2048]{1,0:T(8,128)(2,1)S(1)} %copy-done.1), custom_call_target="tpu_custom_call" | custom-call | flops 99999997952 | tf_op jit(solution)/shard_map/pallas_call | solution.py:288
  16.0 1.6 %collective-permute-start.11 = (bf16[64,2048]{1,0:T(8,128)(2,1)}, bf16[64,2048]{1,0:T(8,128)(2,1)}, u32[]{:S(2)}, u32[]{:S(2)}) collective-permute-start(bf16[64,2048]{1,0:T(8,128)(2,1)} %shard_map.65.refs_0_), channel_id=1, source_target_pairs={{0,4},{4,0},{8,12},{12,8},{1,5},{5,1},{9,13},{13,9},{2,6},{6,2},{1... | collective-permute-start | bytes 786440 | tf_op jit(solution)/shard_map/ppermute | solution.py:25
  17.7 1.4 %collective-permute-start.4 = (bf16[384,512]{1,0:T(8,128)(2,1)}, bf16[384,512]{1,0:T(8,128)(2,1)}, u32[]{:S(2)}, u32[]{:S(2)}) collective-permute-start(bf16[384,512]{1,0:T(8,128)(2,1)} %get-tuple-element.66), channel_id=1, source_target_pairs={{0,2},{1,3},{2,0},{3,1},{4,6},{5,7},{6,4},{7,5},{8,10},{9,11},{10,... | collective-permute-start | bytes 1179656 | tf_op jit(solution)/shard_map/ppermute | solution.py:25
  19.1 6.3 %collective-permute-done.6.refs_2_ = bf16[64,2048]{1,0:T(8,128)(2,1)} collective-permute-done((bf16[64,2048]{1,0:T(8,128)(2,1)}, bf16[64,2048]{1,0:T(8,128)(2,1)}, u32[]{:S(2)}, u32[]{:S(2)}) %collective-permute-start.6) | collective-permute-done | bytes 262176 | tf_op jit(solution)/shard_map/ppermute | solution.py:278
  25.4 1.8 %collective-permute-done.5.refs_0_ = bf16[384,1024]{1,0:T(8,128)(2,1)S(1)} collective-permute-done((bf16[384,1024]{1,0:T(8,128)(2,1)S(1)}, bf16[384,1024]{1,0:T(8,128)(2,1)S(1)}, u32[]{:S(2)}, u32[]{:S(2)}) %collective-permute-start.5) | collective-permute-done | bytes 786464 | tf_op jit(solution)/shard_map/ppermute | solution.py:25
  27.2 2.0 %collective-permute-start.12 = (bf16[64,2048]{1,0:T(8,128)(2,1)}, bf16[64,2048]{1,0:T(8,128)(2,1)}, u32[]{:S(2)}, u32[]{:S(2)}) collective-permute-start(bf16[64,2048]{1,0:T(8,128)(2,1)} %collective-permute-done.6.refs_2_), channel_id=1, source_target_pairs={{0,16},{16,0},{1,17},{17,1},{2,18},{18,2},{3,19},{19,3},{4,20},{20... | collective-permute-start | bytes 786440 | tf_op jit(solution)/shard_map/ppermute | solution.py:25
  29.2 2.6 %shard_map.67.refs_2_ = f32[384,512]{1,0:T(8,128)S(1)} custom-call(bf16[8192,512]{1,0:T(8,128)(2,1)} %weight_ref.11, bf16[384,2048]{1,0:T(8,128)(2,1)S(1)} %collective-permute-done.3.refs_0_, f32[384,512]{1,0:T(8,128)S(1)} %get-tuple-element.74.refs_1_), custom_call_target="tpu_custom_call" | custom-call | flops 99999997952 | tf_op jit(solution)/shard_map/pallas_call | solution.py:260
  31.8 2.7 %shard_map.68.refs_1_ = f32[384,512]{1,0:T(8,128)S(1)} custom-call(bf16[8192,512]{1,0:T(8,128)(2,1)} %weight_ref.11, bf16[384,1024]{1,0:T(8,128)(2,1)S(1)} %collective-permute-done.5.refs_0_, bf16[384,1024]{1,0:T(8,128)(2,1)S(1)} %collective-permute-done.7.refs_1_, f32[384,512]{1,0:T(8,128)S(1)} %shard_map.67.refs_2_), custom_call_target="tpu_custom_call" | custom-call | flops 99999997952 | tf_op jit(solution)/shard_map/pallas_call | solution.py:260
  34.5 2.7 %collective-permute-start.10 = (bf16[64,512]{1,0:T(8,128)(2,1)}, bf16[64,512]{1,0:T(8,128)(2,1)S(1)}, u32[]{:S(2)}, u32[]{:S(2)}) collective-permute-start(bf16[64,512]{1,0:T(8,128)(2,1)} %bitcast.9.refs_5_), channel_id=1, source_target_pairs={{0,8},{4,12},{8,0},{12,4},{16,28},{20,24},{24,20},{28,16},{1,9},{5... | collective-permute-start | bytes 196616 | tf_op jit(solution)/shard_map/ppermute | solution.py:278
  37.2 1.6 %collective-permute-start.8 = (bf16[64,512]{1,0:T(8,128)(2,1)}, bf16[64,512]{1,0:T(8,128)(2,1)}, u32[]{:S(2)}, u32[]{:S(2)}) collective-permute-start(bf16[64,512]{1,0:T(8,128)(2,1)} %bitcast.9.refs_5_), channel_id=1, source_target_pairs={{0,4},{4,0},{8,12},{12,8},{1,5},{5,1},{9,13},{13,9},{2,6},{6,2},{1... | collective-permute-start | bytes 196616 | tf_op jit(solution)/shard_map/ppermute | solution.py:25
  38.8 2.5 %shard_map.69 = f32[64,384]{1,0:T(8,128)S(1)} custom-call(bf16[384,2048]{1,0:T(8,128)(2,1)S(1)} %copy-done.2, s32[1,384]{1,0:T(1,128)S(1)} %get-tuple-element.77.stored_ref.refs_2_, bf16[64,2048]{1,0:T(8,128)(2,1)} %shard_map.65.refs_0_, bf16[64,2048]{1,0:T(8,128)(2,1)} %collective-permute-done.11.refs_1_, bf16[64,2048]{1,0:T(8,128)(2,1)} %collective-permute-done.6.refs_2_, ...), custom_call_target="tpu_custom_call" | custom-call | flops 99999997952 | tf_op jit(solution)/shard_map/pallas_call | solution.py:316
  42.1 1.5 %shard_map.70.refs_2_ = f32[384,512]{1,0:T(8,128)S(1)} custom-call(bf16[8192,512]{1,0:T(8,128)(2,1)} %weight_ref.11, bf16[384,512]{1,0:T(8,128)(2,1)} %collective-permute-done.9.refs_0_, f32[384,512]{1,0:T(8,128)S(1)} %shard_map.68.refs_1_), custom_call_target="tpu_custom_call" | custom-call | flops 99999997952 | tf_op jit(solution)/shard_map/pallas_call | solution.py:260
  44.1 3.9 %collective-permute-done.13.refs_8_ = bf16[64,512]{1,0:T(8,128)(2,1)S(1)} collective-permute-done((bf16[64,512]{1,0:T(8,128)(2,1)S(1)}, bf16[64,512]{1,0:T(8,128)(2,1)S(1)}, u32[]{:S(2)}, u32[]{:S(2)}) %collective-permute-start.13) | collective-permute-done | bytes 65568 | tf_op jit(solution)/shard_map/ppermute | solution.py:25
  48.0 1.5 %collective-permute-start.16 = (bf16[64,384]{1,0:T(8,128)(2,1)S(1)}, bf16[64,384]{1,0:T(8,128)(2,1)S(1)}, u32[]{:S(2)}, u32[]{:S(2)}) collective-permute-start(bf16[64,384]{1,0:T(8,128)(2,1)S(1)} %get-tuple-element.99), channel_id=1, source_target_pairs={{0,2},{1,3},{2,0},{3,1},{4,6},{5,7},{6,4},{7,5},{8,10},{9,11},{10,... | collective-permute-start | bytes 147464 | tf_op jit(solution)/shard_map/ppermute | solution.py:25
  49.5 1.8 %shard_map.71.refs_1_ = f32[384,512]{1,0:T(8,128)S(1)} custom-call(bf16[8192,512]{1,0:T(8,128)(2,1)} %weight_ref.11, bf16[384,512]{1,0:T(8,128)(2,1)S(1)} %collective-permute-done.17.refs_0_, bf16[384,512]{1,0:T(8,128)(2,1)} %collective-permute-done.4.refs_1_, f32[384,512]{1,0:T(8,128)S(1)} %shard_map.70.refs_2_), custom_call_target="tpu_custom_call" | custom-call | flops 99999997952 | tf_op jit(solution)/shard_map/pallas_call | solution.py:260
  51.3 0.8 %collective-permute-done.16.refs_4_ = bf16[64,384]{1,0:T(8,128)(2,1)S(1)} collective-permute-done((bf16[64,384]{1,0:T(8,128)(2,1)S(1)}, bf16[64,384]{1,0:T(8,128)(2,1)S(1)}, u32[]{:S(2)}, u32[]{:S(2)}) %collective-permute-start.16) | collective-permute-done | bytes 49184 | tf_op jit(solution)/shard_map/ppermute | solution.py:25
  52.1 2.6 %shard_map.72 = bf16[384,512]{1,0:T(8,128)(2,1)} custom-call(bf16[8192,512]{1,0:T(8,128)(2,1)} %weight_ref.11, bf16[384,512]{1,0:T(8,128)(2,1)S(1)} %collective-permute-done.15.refs_0_, f32[384,512]{1,0:T(8,128)S(1)} %shard_map.71.refs_1_, s32[1,384]{1,0:T(1,128)S(1)} %copy-done.6, f32[64,384]{1,0:T(8,128)S(1)} %get-tuple-element.93.refs_3_, ...), custom_call_target="tpu_custom_call" | custom-call | flops 99999997952 | tf_op jit(solution)/shard_map/pallas_call | solution.py:346
  (37 shorter events, 2.7 us)
Async XLA Ops:
  1.0 11.9 %copy-start.4 = (s32[4]{0:T(128)S(1)}, s32[4]{0:T(128)}, u32[]{:S(2)}) copy-start(s32[4]{0:T(128)} %placement_ref.1) | copy-start | bytes 52
  1.0 11.9 %copy-start.3 = (s32[384,1]{0,1:T(1,128)S(1)}, s32[384,1]{0,1:T(1,128)}, u32[]{:S(2)}) copy-start(s32[384,1]{0,1:T(1,128)} %param.7) | copy-start | bytes 4612
  1.0 7.8 %collective-permute-start = (bf16[16,2048]{1,0:T(8,128)(2,1)S(1)}, bf16[16,2048]{1,0:T(8,128)(2,1)S(1)}, u32[]{:S(2)}, u32[]{:S(2)}) collective-permute-start(bf16[16,2048]{1,0:T(8,128)(2,1)S(1)} %get-tuple-element.53), channel_id=1, source_target_pairs={{0,1},{1,0},{2,3},{3,2},{4,5},{5,4},{6,7},{7,6},{8,9},{9,8},{10,11... | collective-permute-start | bytes 196616 | tf_op jit(solution)/shard_map/ppermute | solution.py:25
  1.5 7.2 %collective-permute-start.1 = (bf16[16,2048]{1,0:T(8,128)(2,1)S(1)}, bf16[16,2048]{1,0:T(8,128)(2,1)S(1)}, u32[]{:S(2)}, u32[]{:S(2)}) collective-permute-start(bf16[16,2048]{1,0:T(8,128)(2,1)S(1)} %get-tuple-element.54), channel_id=1, source_target_pairs={{0,2},{1,3},{2,0},{3,1},{4,6},{5,7},{6,4},{7,5},{8,10},{9,11},{10,... | collective-permute-start | bytes 196616 | tf_op jit(solution)/shard_map/ppermute | solution.py:25
  4.1 4.7 %collective-permute-start.2 = (bf16[16,2048]{1,0:T(8,128)(2,1)S(1)}, bf16[16,2048]{1,0:T(8,128)(2,1)S(1)}, u32[]{:S(2)}, u32[]{:S(2)}) collective-permute-start(bf16[16,2048]{1,0:T(8,128)(2,1)S(1)} %get-tuple-element.55), channel_id=1, source_target_pairs={{0,3},{1,2},{2,1},{3,0},{4,7},{5,6},{6,5},{7,4},{8,11},{9,10},{10,... | collective-permute-start | bytes 196616 | tf_op jit(solution)/shard_map/ppermute | solution.py:25
  4.1 6.1 %collective-permute-start.3 = (bf16[384,2048]{1,0:T(8,128)(2,1)}, bf16[384,2048]{1,0:T(8,128)(2,1)S(1)}, u32[]{:S(2)}, u32[]{:S(2)}) collective-permute-start(bf16[384,2048]{1,0:T(8,128)(2,1)} %tokens_ref.1), channel_id=1, source_target_pairs={{0,1},{1,0},{2,3},{3,2},{4,5},{5,4},{6,7},{7,6},{8,9},{9,8},{10,11... | collective-permute-start | bytes 4718600 | tf_op jit(solution)/shard_map/ppermute | solution.py:25
  5.7 7.2 %copy-start.1 = (bf16[384,2048]{1,0:T(8,128)(2,1)S(1)}, bf16[384,2048]{1,0:T(8,128)(2,1)}, u32[]{:S(2)}) copy-start(bf16[384,2048]{1,0:T(8,128)(2,1)} %tokens_ref.1) | copy-start | bytes 4718596
  6.7 20.4 %collective-permute-start.5 = (bf16[384,1024]{1,0:T(8,128)(2,1)S(1)}, bf16[384,1024]{1,0:T(8,128)(2,1)S(1)}, u32[]{:S(2)}, u32[]{:S(2)}) collective-permute-start(bf16[384,1024]{1,0:T(8,128)(2,1)S(1)} %get-tuple-element.67), channel_id=1, source_target_pairs={{0,2},{1,3},{2,0},{3,1},{4,6},{5,7},{6,4},{7,5},{8,10},{9,11},{10,... | collective-permute-start | bytes 2359304 | tf_op jit(solution)/shard_map/ppermute | solution.py:25
  8.8 32.6 %collective-permute-start.9 = (bf16[384,512]{1,0:T(8,128)(2,1)}, bf16[384,512]{1,0:T(8,128)(2,1)}, u32[]{:S(2)}, u32[]{:S(2)}) collective-permute-start(bf16[384,512]{1,0:T(8,128)(2,1)} %get-tuple-element.76), channel_id=1, source_target_pairs={{0,2},{1,3},{2,0},{3,1},{4,6},{5,7},{6,4},{7,5},{8,10},{9,11},{10,... | collective-permute-start | bytes 1179656 | tf_op jit(solution)/shard_map/ppermute | solution.py:25
  10.2 15.2 %collective-permute-start.6 = (bf16[64,2048]{1,0:T(8,128)(2,1)}, bf16[64,2048]{1,0:T(8,128)(2,1)}, u32[]{:S(2)}, u32[]{:S(2)}) collective-permute-start(bf16[64,2048]{1,0:T(8,128)(2,1)} %shard_map.65.refs_0_), channel_id=1, source_target_pairs={{0,8},{4,12},{8,0},{12,4},{16,28},{20,24},{24,20},{28,16},{1,9},{5... | collective-permute-start | bytes 786440 | tf_op jit(solution)/shard_map/ppermute | solution.py:278
  16.0 22.7 %copy-start.5 = (s32[1,384]{1,0:T(1,128)}, s32[1,384]{1,0:T(1,128)S(1)}, u32[]{:S(2)}) copy-start(s32[1,384]{1,0:T(1,128)S(1)} %get-tuple-element.77.stored_ref.refs_2_) | copy-start | bytes 4612
  16.0 21.1 %collective-permute-start.11 = (bf16[64,2048]{1,0:T(8,128)(2,1)}, bf16[64,2048]{1,0:T(8,128)(2,1)}, u32[]{:S(2)}, u32[]{:S(2)}) collective-permute-start(bf16[64,2048]{1,0:T(8,128)(2,1)} %shard_map.65.refs_0_), channel_id=1, source_target_pairs={{0,4},{4,0},{8,12},{12,8},{1,5},{5,1},{9,13},{13,9},{2,6},{6,2},{1... | collective-permute-start | bytes 786440 | tf_op jit(solution)/shard_map/ppermute | solution.py:25
  17.7 26.4 %collective-permute-start.4 = (bf16[384,512]{1,0:T(8,128)(2,1)}, bf16[384,512]{1,0:T(8,128)(2,1)}, u32[]{:S(2)}, u32[]{:S(2)}) collective-permute-start(bf16[384,512]{1,0:T(8,128)(2,1)} %get-tuple-element.66), channel_id=1, source_target_pairs={{0,2},{1,3},{2,0},{3,1},{4,6},{5,7},{6,4},{7,5},{8,10},{9,11},{10,... | collective-permute-start | bytes 1179656 | tf_op jit(solution)/shard_map/ppermute | solution.py:25
  27.2 11.6 %collective-permute-start.12 = (bf16[64,2048]{1,0:T(8,128)(2,1)}, bf16[64,2048]{1,0:T(8,128)(2,1)}, u32[]{:S(2)}, u32[]{:S(2)}) collective-permute-start(bf16[64,2048]{1,0:T(8,128)(2,1)} %collective-permute-done.6.refs_2_), channel_id=1, source_target_pairs={{0,16},{16,0},{1,17},{17,1},{2,18},{18,2},{3,19},{19,3},{4,20},{20... | collective-permute-start | bytes 786440 | tf_op jit(solution)/shard_map/ppermute | solution.py:25
  29.2 2.6 %collective-permute-start.7 = (bf16[384,1024]{1,0:T(8,128)(2,1)S(1)}, bf16[384,1024]{1,0:T(8,128)(2,1)S(1)}, u32[]{:S(2)}, u32[]{:S(2)}) collective-permute-start(bf16[384,1024]{1,0:T(8,128)(2,1)S(1)} %collective-permute-done.5.refs_0_), channel_id=1, source_target_pairs={{0,1},{1,0},{2,3},{3,2},{4,5},{5,4},{6,7},{7,6},{8,9},{9,8},{10,11... | collective-permute-start | bytes 2359304 | tf_op jit(solution)/shard_map/ppermute | solution.py:25
  31.8 7.0 %copy-start.2 = (bf16[384,2048]{1,0:T(8,128)(2,1)S(1)}, bf16[384,2048]{1,0:T(8,128)(2,1)}, u32[]{:S(2)}) copy-start(bf16[384,2048]{1,0:T(8,128)(2,1)} %tokens_ref.1) | copy-start | bytes 4718596
  34.5 7.0 %collective-permute-start.10 = (bf16[64,512]{1,0:T(8,128)(2,1)}, bf16[64,512]{1,0:T(8,128)(2,1)S(1)}, u32[]{:S(2)}, u32[]{:S(2)}) collective-permute-start(bf16[64,512]{1,0:T(8,128)(2,1)} %bitcast.9.refs_5_), channel_id=1, source_target_pairs={{0,8},{4,12},{8,0},{12,4},{16,28},{20,24},{24,20},{28,16},{1,9},{5... | collective-permute-start | bytes 196616 | tf_op jit(solution)/shard_map/ppermute | solution.py:278
  37.2 6.9 %collective-permute-start.8 = (bf16[64,512]{1,0:T(8,128)(2,1)}, bf16[64,512]{1,0:T(8,128)(2,1)}, u32[]{:S(2)}, u32[]{:S(2)}) collective-permute-start(bf16[64,512]{1,0:T(8,128)(2,1)} %bitcast.9.refs_5_), channel_id=1, source_target_pairs={{0,4},{4,0},{8,12},{12,8},{1,5},{5,1},{9,13},{13,9},{2,6},{6,2},{1... | collective-permute-start | bytes 196616 | tf_op jit(solution)/shard_map/ppermute | solution.py:25
  41.6 2.5 %collective-permute-start.14 = (f32[64,384]{1,0:T(8,128)S(1)}, f32[64,384]{1,0:T(8,128)S(1)}, u32[]{:S(2)}, u32[]{:S(2)}) collective-permute-start(f32[64,384]{1,0:T(8,128)S(1)} %shard_map.69), channel_id=1, source_target_pairs={{0,1},{1,0},{2,3},{3,2},{4,5},{5,4},{6,7},{7,6},{8,9},{9,8},{10,11... | collective-permute-start | bytes 294920 | tf_op jit(solution)/shard_map/ppermute | solution.py:25
  41.6 7.9 %collective-permute-start.17 = (bf16[384,512]{1,0:T(8,128)(2,1)}, bf16[384,512]{1,0:T(8,128)(2,1)S(1)}, u32[]{:S(2)}, u32[]{:S(2)}) collective-permute-start(bf16[384,512]{1,0:T(8,128)(2,1)} %collective-permute-done.9.refs_0_), channel_id=1, source_target_pairs={{0,1},{1,0},{2,3},{3,2},{4,5},{5,4},{6,7},{7,6},{8,9},{9,8},{10,11... | collective-permute-start | bytes 1179656 | tf_op jit(solution)/shard_map/ppermute | solution.py:25
  43.6 4.3 %collective-permute-start.13 = (bf16[64,512]{1,0:T(8,128)(2,1)S(1)}, bf16[64,512]{1,0:T(8,128)(2,1)S(1)}, u32[]{:S(2)}, u32[]{:S(2)}) collective-permute-start(bf16[64,512]{1,0:T(8,128)(2,1)S(1)} %collective-permute-done.10.refs_7_), channel_id=1, source_target_pairs={{0,16},{16,0},{1,17},{17,1},{2,18},{18,2},{3,19},{19,3},{4,20},{20... | collective-permute-start | bytes 196616 | tf_op jit(solution)/shard_map/ppermute | solution.py:25
  48.0 4.1 %copy-start.6 = (s32[1,384]{1,0:T(1,128)S(1)}, s32[1,384]{1,0:T(1,128)}, u32[]{:S(2)}) copy-start(s32[1,384]{1,0:T(1,128)} %copy-done.5) | copy-start | bytes 4612
  48.0 4.1 %collective-permute-start.16 = (bf16[64,384]{1,0:T(8,128)(2,1)S(1)}, bf16[64,384]{1,0:T(8,128)(2,1)S(1)}, u32[]{:S(2)}, u32[]{:S(2)}) collective-permute-start(bf16[64,384]{1,0:T(8,128)(2,1)S(1)} %get-tuple-element.99), channel_id=1, source_target_pairs={{0,2},{1,3},{2,0},{3,1},{4,6},{5,7},{6,4},{7,5},{8,10},{9,11},{10,... | collective-permute-start | bytes 147464 | tf_op jit(solution)/shard_map/ppermute | solution.py:25
  49.5 2.6 %collective-permute-start.15 = (bf16[384,512]{1,0:T(8,128)(2,1)}, bf16[384,512]{1,0:T(8,128)(2,1)S(1)}, u32[]{:S(2)}, u32[]{:S(2)}) collective-permute-start(bf16[384,512]{1,0:T(8,128)(2,1)} %collective-permute-done.4.refs_1_), channel_id=1, source_target_pairs={{0,1},{1,0},{2,3},{3,2},{4,5},{5,4},{6,7},{7,6},{8,9},{9,8},{10,11... | collective-permute-start | bytes 1179656 | tf_op jit(solution)/shard_map/ppermute | solution.py:25
  (1 other events, 1.4 us)

commit v12 on v11

--- a/solution.py
+++ b/solution.py
@@ -11,7 +11,7 @@
 LOWRANK_SCALE = 2.0
 CORES = 2
 LANES = 128
-CUTS = (0.5, 0.75)
+CUTS = (0.75,)
 MIB = 1024 * 1024
 FREE = pl.CostEstimate(flops=0, bytes_accessed=0, transcendentals=0)
 LONG = pl.CostEstimate(flops=10**11, bytes_accessed=0, transcendentals=0)
@@ -223,7 +223,6 @@
     )(uncut))
     neighbour = flipped(uncut, "tensor", 1)
     pieces = [pieces[0]] + [flipped(pieces[f], "tensor", f) for f in range(1, tensors)]
-    pieces, chunks[1] = chained(pieces, chunks[1])
     if down.shape[0] % 16 == 0:
         own = call(
             functools.partial(order_kernel, down.shape[0]),
@@ -242,10 +241,7 @@
 
     hops = range(CORES, tensors, CORES)
 
-    def send(m):
-        return [flipped(chunks[m], "tensor", hop) for hop in hops]
-
-    far = [send(0), send(1)]
+    far = [[flipped(chunk, "tensor", hop) for hop in hops] for chunk in chunks]
 
     def across(m):
         return [flipped(value, "tensor", 1) for value in far[m]]
@@ -295,18 +291,13 @@
         tile_scratch(tile, [tokens], columns),
         [VECTOR, VECTOR],
     )(placement, tenant.reshape(1, rows), frozen_projection_weight, here)
-    total, own, chunks[2] = chained(total, own, chunks[2])
-    far.append(send(2))
-    single = fetch_near(own)
+    total, own, up = chained(total, own, lowrank_up_weight[0])
+    single, single_up = fetch_near(own), fetch_near(up)
     fetched, total = chained(fetched, total)
     swapped = swap(fetched)
-    far[0], total = chained(far[0], total)
+    fetched_up = fetch_far(up)
     total, neighbour = chained(total, neighbour)
     total = products([(1, 0)], [neighbour], total)
-    near = across(0)
-    total = products(far_places(0) + near_places(0), far[0] + near, total)
-    total, up = chained(total, lowrank_up_weight[0])
-    single_up, fetched_up = fetch_near(up), fetch_far(up)
     single, swapped, total = chained(single, swapped, total)
     downs = [own] + single
     for pair in zip(fetched, swapped):
@@ -324,12 +315,12 @@
             pltpu.SemaphoreType.DMA((1 + slots, tiles)),
         ],
     )(tokens, stored, *downs)
-    far[1], fetched_up, partial = chained(far[1], fetched_up, partial)
+    far[0], fetched_up, partial = chained(far[0], fetched_up, partial)
     ups = [up] + single_up
     for pair in zip(fetched_up, swap(fetched_up)):
         ups += pair
-    middle = across(1)
-    total = products(far_places(1), far[1], total)
+    near = across(0)
+    total = products(far_places(0), far[0], total)
     flip = 1
     while flip < tensors // 2:
         received = flipped(partial, "tensor", flip)
@@ -338,13 +329,15 @@
         partial += received
         flip *= 2
     more = flipped(partial.astype(jnp.bfloat16), "tensor", flip)
-    far[2], ups, total, partial = chained(far[2], ups, total, partial)
-    near = across(2)
-    total = products(near_places(1) + far_places(2), middle + far[2], total)
+    total, partial = chained(total, partial)
+    total = products(near_places(0), near, total)
+    far[1], ups, total = chained(far[1], ups, total)
+    near = across(1)
+    total = products(far_places(1), far[1], total)
     near, more, total = chained(near, more, total)
 
     return call(
-        functools.partial(last_kernel, tile, depth, near_places(2), flips, pairs, slots),
+        functools.partial(last_kernel, tile, depth, near_places(1), flips, pairs, slots),
         jax.ShapeDtypeStruct((rows, columns), jnp.bfloat16),
         [ANYWHERE] + [ANYWHERE] * len(near) + [VECTOR] * 2 + [ANYWHERE] * (2 + slots),
         [

time: 55 us -> 50.1 us (0.911)
  starting transfers between devices: 20.3 us -> 15.2 us
  Pallas kernels: 18.8 us -> 17.9 us
  other arithmetic: 0.01 us -> 0.63 us
    ppermute x16 -> x14, starting transfers between devices: 15 us -> 12.2 us  [flipped(): return lax.ppermute(value, axis, [(i, i ^ flip) for i in range(count)])]
    ppermute x2, starting transfers between devices: 5.31 us -> 3 us  [fetch_far(): lax.ppermute(value, ('parts', 'adapter'), route)]
    ppermute x2, waiting for transfers between devices: 6.59 us -> 8.28 us  [fetch_far(): lax.ppermute(value, ('parts', 'adapter'), route)]
    ppermute x16 -> x14, waiting for transfers between devices: 6.45 us -> 5.15 us  [flipped(): return lax.ppermute(value, axis, [(i, i ^ flip) for i in range(count)])]
    pallas_call x1, Pallas kernels: 2.53 us -> 1.88 us  [body(): call(functools.partial(shrink_kernel, tile, flips, pairs, slots), jax.Sha...]
    convert_element_type x1, other arithmetic: 0.01 us -> 0.63 us  [body(): more = flipped(partial.astype(jnp.bfloat16), 'tensor', flip)]
    unnamed x14 -> x12, local copies, waits for them, and re-layouts: 1.44 us -> 1.43 us
  transfers between devices with their start and end apart: 18 -> 16, of which waited for: 5 -> 5; matrix products, arithmetic and copies ran while one was open for 0% -> 1% of each run, Pallas kernels for 30% -> 31%
where the time goes in v12:
time: 50.1 us; the launch traced here: 49.7 us
  Pallas kernels  17.9 us (36%)
  starting transfers between devices  15.2 us (30%)
  waiting for transfers between devices  13.4 us (27%)
  local copies, waits for them, and re-layouts  2.39 us (5%)
  other arithmetic  0.63 us (1%)
    ppermute x14, starting transfers between devices, flipped(): return lax.ppermute(value, axis, [(i, i ^ flip) for i in range(count)])  12.2 us
    pallas_call x4, Pallas kernels, products(): call(functools.partial(products_kernel, tile, depth, places), jax.ShapeDt...  8.68 us
    ppermute x2, waiting for transfers between devices, fetch_far(): lax.ppermute(value, ('parts', 'adapter'), route)  8.28 us
    ppermute x14, waiting for transfers between devices, flipped(): return lax.ppermute(value, axis, [(i, i ^ flip) for i in range(count)])  5.15 us
    pallas_call x1, Pallas kernels, body(): call(functools.partial(first_kernel, tile, depth, [(0, 0)], slots), [jax....  3.15 us
    ppermute x2, starting transfers between devices, fetch_far(): lax.ppermute(value, ('parts', 'adapter'), route)  3 us
    pallas_call x1, Pallas kernels, body(): call(functools.partial(last_kernel, tile, depth, near_places(1), flips, p...  2.56 us
    pallas_call x1, Pallas kernels, body(): call(functools.partial(shrink_kernel, tile, flips, pairs, slots), jax.Sha...  1.88 us
  transfers between devices with their start and end apart: 16, of which 5 were waited for; matrix products, arithmetic and copies ran while one was open for 1% of the time, Pallas kernels for 31%

profile of v12, /device:TPU:0, one launch (start us, length us, event | category | flops | bytes accessed | tf_op | source)
XLA Modules:
  0.0 49.7 jit_solution(12580832838084796771)
XLA Ops:
  0.0 1.0 %dynamic-slice_bitcast_fusion = (bf16[16,2048]{1,0:T(8,128)(2,1)S(1)}, bf16[16,2048]{1,0:T(8,128)(2,1)S(1)}, bf16[16,2048]{1,0:T(8,128)(2,1)S(1)}, bf16[16,2048]{1,0:T(8,128)(2,1)S(1)}) fusion(bf16[1,8192,16]{1,2,0:T(8,128)(2,1)} %param.10, s32[]{:T(128)S(6)} %select_n.15, s32[]{:T(128)S(6)} %select_n.13, s32[]{:T(128)S(6)} %select_n.12, s32[]{:T(128)S(6)} %select_n.14), kind=kLoop, calls=%fused_computation | loop fusion | bytes 524304 | tf_op jit(solution)/shard_map/dynamic_slice | solution.py:212
  1.0 0.5 %collective-permute-start.4 = (bf16[384,2048]{1,0:T(8,128)(2,1)}, bf16[384,2048]{1,0:T(8,128)(2,1)S(1)}, u32[]{:S(2)}, u32[]{:S(2)}) collective-permute-start(bf16[384,2048]{1,0:T(8,128)(2,1)} %tokens_ref.1), channel_id=1, source_target_pairs={{0,1},{1,0},{2,3},{3,2},{4,5},{5,4},{6,7},{7,6},{8,9},{9,8},{10,11... | collective-permute-start | bytes 4718600 | tf_op jit(solution)/shard_map/ppermute | solution.py:25
  1.6 2.9 %collective-permute-start.2 = (bf16[16,2048]{1,0:T(8,128)(2,1)S(1)}, bf16[16,2048]{1,0:T(8,128)(2,1)S(1)}, u32[]{:S(2)}, u32[]{:S(2)}) collective-permute-start(bf16[16,2048]{1,0:T(8,128)(2,1)S(1)} %get-tuple-element.47), channel_id=1, source_target_pairs={{0,2},{1,3},{2,0},{3,1},{4,6},{5,7},{6,4},{7,5},{8,10},{9,11},{10,... | collective-permute-start | bytes 196616 | tf_op jit(solution)/shard_map/ppermute | solution.py:25
  4.5 1.4 %copy-done = bf16[384,2048]{1,0:T(8,128)(2,1)S(1)} copy-done((bf16[384,2048]{1,0:T(8,128)(2,1)S(1)}, bf16[384,2048]{1,0:T(8,128)(2,1)}, u32[]{:S(2)}) %copy-start) | copy-done | bytes 1572888
  5.9 1.3 %shard_map.64 = (bf16[384,1536]{1,0:T(8,128)(2,1)}, bf16[384,512]{1,0:T(8,128)(2,1)}) custom-call(bf16[384,2048]{1,0:T(8,128)(2,1)S(1)} %copy-done), custom_call_target="tpu_custom_call" | custom-call | flops 99999997952 | tf_op jit(solution)/shard_map/pallas_call | solution.py:216
  7.2 1.5 %collective-permute-start.6 = (bf16[384,1536]{1,0:T(8,128)(2,1)}, bf16[384,1536]{1,0:T(8,128)(2,1)}, u32[]{:S(2)}, u32[]{:S(2)}) collective-permute-start(bf16[384,1536]{1,0:T(8,128)(2,1)} %get-tuple-element.53), channel_id=1, source_target_pairs={{0,2},{1,3},{2,0},{3,1},{4,6},{5,7},{6,4},{7,5},{8,10},{9,11},{10,... | collective-permute-start | bytes 3538952 | tf_op jit(solution)/shard_map/ppermute | solution.py:25
  8.7 0.6 %collective-permute-start = (bf16[384,512]{1,0:T(8,128)(2,1)}, bf16[384,512]{1,0:T(8,128)(2,1)}, u32[]{:S(2)}, u32[]{:S(2)}) collective-permute-start(bf16[384,512]{1,0:T(8,128)(2,1)} %get-tuple-element.44), channel_id=1, source_target_pairs={{0,2},{1,3},{2,0},{3,1},{4,6},{5,7},{6,4},{7,5},{8,10},{9,11},{10,... | collective-permute-start | bytes 1179656 | tf_op jit(solution)/shard_map/ppermute | solution.py:25
  9.7 2.7 %collective-permute-start.9 = (bf16[64,2048]{1,0:T(8,128)(2,1)S(1)}, bf16[64,2048]{1,0:T(8,128)(2,1)S(1)}, u32[]{:S(2)}, u32[]{:S(2)}) collective-permute-start(bf16[64,2048]{1,0:T(8,128)(2,1)S(1)} %shard_map.65.refs_0_), channel_id=1, source_target_pairs={{0,8},{4,12},{8,0},{12,4},{16,28},{20,24},{24,20},{28,16},{1,9},{5... | collective-permute-start | bytes 786440 | tf_op jit(solution)/shard_map/ppermute | solution.py:274
  12.4 3.1 %shard_map.66 = (f32[384,512]{1,0:T(8,128)S(1)}, s32[1,384]{1,0:T(1,128)S(1)}) custom-call(s32[4]{0:T(128)S(1)} %copy-done.3, s32[1,384]{1,0:T(1,128)S(1)} %bitcast.18, bf16[8192,512]{1,0:T(8,128)(2,1)} %weight_ref.11, bf16[384,2048]{1,0:T(8,128)(2,1)S(1)} %copy-done.1), custom_call_target="tpu_custom_call" | custom-call | flops 99999997952 | tf_op jit(solution)/shard_map/pallas_call | solution.py:284
  15.5 1.6 %collective-permute-start.8 = (bf16[64,2048]{1,0:T(8,128)(2,1)S(1)}, bf16[64,2048]{1,0:T(8,128)(2,1)S(1)}, u32[]{:S(2)}, u32[]{:S(2)}) collective-permute-start(bf16[64,2048]{1,0:T(8,128)(2,1)S(1)} %shard_map.65.refs_0_), channel_id=1, source_target_pairs={{0,4},{4,0},{8,12},{12,8},{1,5},{5,1},{9,13},{13,9},{2,6},{6,2},{1... | collective-permute-start | bytes 786440 | tf_op jit(solution)/shard_map/ppermute | solution.py:25
  17.5 8.3 %collective-permute-done.9.refs_2_ = bf16[64,2048]{1,0:T(8,128)(2,1)S(1)} collective-permute-done((bf16[64,2048]{1,0:T(8,128)(2,1)S(1)}, bf16[64,2048]{1,0:T(8,128)(2,1)S(1)}, u32[]{:S(2)}, u32[]{:S(2)}) %collective-permute-start.9) | collective-permute-done | bytes 262176 | tf_op jit(solution)/shard_map/ppermute | solution.py:274
  25.8 2.6 %shard_map.67.refs_1_ = f32[384,512]{1,0:T(8,128)S(1)} custom-call(bf16[8192,512]{1,0:T(8,128)(2,1)} %weight_ref.11, bf16[384,2048]{1,0:T(8,128)(2,1)S(1)} %collective-permute-done.4.refs_0_, f32[384,512]{1,0:T(8,128)S(1)} %get-tuple-element.61.refs_1_), custom_call_target="tpu_custom_call" | custom-call | flops 99999997952 | tf_op jit(solution)/shard_map/pallas_call | solution.py:256
  28.4 1.1 %collective-permute-done.8.refs_1_ = bf16[64,2048]{1,0:T(8,128)(2,1)S(1)} collective-permute-done((bf16[64,2048]{1,0:T(8,128)(2,1)S(1)}, bf16[64,2048]{1,0:T(8,128)(2,1)S(1)}, u32[]{:S(2)}, u32[]{:S(2)}) %collective-permute-start.8) | collective-permute-done | bytes 262176 | tf_op jit(solution)/shard_map/ppermute | solution.py:25
  29.5 1.3 %collective-permute-start.5 = (bf16[64,512]{1,0:T(8,128)(2,1)}, bf16[64,512]{1,0:T(8,128)(2,1)}, u32[]{:S(2)}, u32[]{:S(2)}) collective-permute-start(bf16[64,512]{1,0:T(8,128)(2,1)} %bitcast.9.refs_5_), channel_id=1, source_target_pairs={{0,4},{4,0},{8,12},{12,8},{1,5},{5,1},{9,13},{13,9},{2,6},{6,2},{1... | collective-permute-start | bytes 196616 | tf_op jit(solution)/shard_map/ppermute | solution.py:25
  30.8 1.4 %collective-permute-done.10.refs_3_ = bf16[64,2048]{1,0:T(8,128)(2,1)S(1)} collective-permute-done((bf16[64,2048]{1,0:T(8,128)(2,1)S(1)}, bf16[64,2048]{1,0:T(8,128)(2,1)S(1)}, u32[]{:S(2)}, u32[]{:S(2)}) %collective-permute-start.10) | collective-permute-done | bytes 262176 | tf_op jit(solution)/shard_map/ppermute | solution.py:25
  32.2 1.9 %shard_map.68 = f32[64,384]{1,0:T(8,128)S(1)} custom-call(bf16[384,2048]{1,0:T(8,128)(2,1)S(1)} %copy-done.1, s32[1,384]{1,0:T(1,128)S(1)} %get-tuple-element.54.stored_ref.refs_2_, bf16[64,2048]{1,0:T(8,128)(2,1)S(1)} %shard_map.65.refs_0_, bf16[64,2048]{1,0:T(8,128)(2,1)S(1)} %collective-permute-done.8.refs_1_, ...), custom_call_target="tpu_custom_call" | custom-call | flops 99999997952 | tf_op jit(solution)/shard_map/pallas_call | solution.py:307
  34.0 2.3 %collective-permute-done.6.refs_0_ = bf16[384,1536]{1,0:T(8,128)(2,1)} collective-permute-done((bf16[384,1536]{1,0:T(8,128)(2,1)}, bf16[384,1536]{1,0:T(8,128)(2,1)}, u32[]{:S(2)}, u32[]{:S(2)}) %collective-permute-start.6) | collective-permute-done | bytes 1179680 | tf_op jit(solution)/shard_map/ppermute | solution.py:25
  36.9 2.3 %shard_map.69.refs_1_ = f32[384,512]{1,0:T(8,128)S(1)} custom-call(bf16[8192,512]{1,0:T(8,128)(2,1)} %weight_ref.11, bf16[384,1536]{1,0:T(8,128)(2,1)} %collective-permute-done.6.refs_0_, f32[384,512]{1,0:T(8,128)S(1)} %shard_map.67.refs_1_), custom_call_target="tpu_custom_call" | custom-call | flops 99999997952 | tf_op jit(solution)/shard_map/pallas_call | solution.py:256
  39.2 1.6 %collective-permute-start.11 = (bf16[64,512]{1,0:T(8,128)(2,1)}, bf16[64,512]{1,0:T(8,128)(2,1)S(1)}, u32[]{:S(2)}, u32[]{:S(2)}) collective-permute-start(bf16[64,512]{1,0:T(8,128)(2,1)} %collective-permute-done.7.refs_7_), channel_id=1, source_target_pairs={{0,16},{16,0},{1,17},{17,1},{2,18},{18,2},{3,19},{19,3},{4,20},{20... | collective-permute-start | bytes 196616 | tf_op jit(solution)/shard_map/ppermute | solution.py:25
  40.9 0.6 %fusion = (bf16[64,384]{1,0:T(8,128)(2,1)}, f32[64,384]{1,0:T(8,128)S(1)}) fusion(f32[64,384]{1,0:T(8,128)S(1)} %shard_map.68, f32[64,384]{1,0:T(8,128)S(1)} %collective-permute-done.13), kind=kLoop, calls=%fused_computation.4 | loop fusion | flops 49152 | bytes 344064 | tf_op jit(solution)/shard_map/convert_element_type | solution.py:331
  41.5 1.4 %collective-permute-start.15 = (bf16[64,384]{1,0:T(8,128)(2,1)}, bf16[64,384]{1,0:T(8,128)(2,1)}, u32[]{:S(2)}, u32[]{:S(2)}) collective-permute-start(bf16[64,384]{1,0:T(8,128)(2,1)} %get-tuple-element.81), channel_id=1, source_target_pairs={{0,2},{1,3},{2,0},{3,1},{4,6},{5,7},{6,4},{7,5},{8,10},{9,11},{10,... | collective-permute-start | bytes 147464 | tf_op jit(solution)/shard_map/ppermute | solution.py:25
  42.9 2.2 %shard_map.70.refs_1_ = f32[384,512]{1,0:T(8,128)S(1)} custom-call(bf16[8192,512]{1,0:T(8,128)(2,1)} %weight_ref.11, bf16[384,1536]{1,0:T(8,128)(2,1)S(1)} %collective-permute-done.12.refs_0_, f32[384,512]{1,0:T(8,128)S(1)} %shard_map.69.refs_1_), custom_call_target="tpu_custom_call" | custom-call | flops 99999997952 | tf_op jit(solution)/shard_map/pallas_call | solution.py:256
  45.3 1.6 %shard_map.71.refs_1_ = f32[384,512]{1,0:T(8,128)S(1)} custom-call(bf16[8192,512]{1,0:T(8,128)(2,1)} %weight_ref.11, bf16[384,512]{1,0:T(8,128)(2,1)} %collective-permute-done.refs_0_, f32[384,512]{1,0:T(8,128)S(1)} %shard_map.70.refs_1_), custom_call_target="tpu_custom_call" | custom-call | flops 99999997952 | tf_op jit(solution)/shard_map/pallas_call | solution.py:256
  47.2 2.6 %shard_map.72 = bf16[384,512]{1,0:T(8,128)(2,1)} custom-call(bf16[8192,512]{1,0:T(8,128)(2,1)} %weight_ref.11, bf16[384,512]{1,0:T(8,128)(2,1)S(1)} %collective-permute-done.14.refs_0_, f32[384,512]{1,0:T(8,128)S(1)} %shard_map.71.refs_1_, s32[1,384]{1,0:T(1,128)S(1)} %copy-done.5, f32[64,384]{1,0:T(8,128)S(1)} %get-tuple-element.75.refs_3_, ...), custom_call_target="tpu_custom_call" | custom-call | flops 99999997952 | tf_op jit(solution)/shard_map/pallas_call | solution.py:339
  (31 shorter events, 1.8 us)
Async XLA Ops:
  1.0 11.4 %copy-start.3 = (s32[4]{0:T(128)S(1)}, s32[4]{0:T(128)}, u32[]{:S(2)}) copy-start(s32[4]{0:T(128)} %placement_ref.1) | copy-start | bytes 52
  1.0 11.4 %copy-start.2 = (s32[384,1]{0,1:T(1,128)S(1)}, s32[384,1]{0,1:T(1,128)}, u32[]{:S(2)}) copy-start(s32[384,1]{0,1:T(1,128)} %param.7) | copy-start | bytes 4612
  1.0 8.7 %collective-permute-start.4 = (bf16[384,2048]{1,0:T(8,128)(2,1)}, bf16[384,2048]{1,0:T(8,128)(2,1)S(1)}, u32[]{:S(2)}, u32[]{:S(2)}) collective-permute-start(bf16[384,2048]{1,0:T(8,128)(2,1)} %tokens_ref.1), channel_id=1, source_target_pairs={{0,1},{1,0},{2,3},{3,2},{4,5},{5,4},{6,7},{7,6},{8,9},{9,8},{10,11... | collective-permute-start | bytes 4718600 | tf_op jit(solution)/shard_map/ppermute | solution.py:25
  1.5 7.2 %collective-permute-start.1 = (bf16[16,2048]{1,0:T(8,128)(2,1)S(1)}, bf16[16,2048]{1,0:T(8,128)(2,1)S(1)}, u32[]{:S(2)}, u32[]{:S(2)}) collective-permute-start(bf16[16,2048]{1,0:T(8,128)(2,1)S(1)} %get-tuple-element.46), channel_id=1, source_target_pairs={{0,1},{1,0},{2,3},{3,2},{4,5},{5,4},{6,7},{7,6},{8,9},{9,8},{10,11... | collective-permute-start | bytes 196616 | tf_op jit(solution)/shard_map/ppermute | solution.py:25
  1.6 7.7 %collective-permute-start.2 = (bf16[16,2048]{1,0:T(8,128)(2,1)S(1)}, bf16[16,2048]{1,0:T(8,128)(2,1)S(1)}, u32[]{:S(2)}, u32[]{:S(2)}) collective-permute-start(bf16[16,2048]{1,0:T(8,128)(2,1)S(1)} %get-tuple-element.47), channel_id=1, source_target_pairs={{0,2},{1,3},{2,0},{3,1},{4,6},{5,7},{6,4},{7,5},{8,10},{9,11},{10,... | collective-permute-start | bytes 196616 | tf_op jit(solution)/shard_map/ppermute | solution.py:25
  4.5 4.8 %collective-permute-start.3 = (bf16[16,2048]{1,0:T(8,128)(2,1)S(1)}, bf16[16,2048]{1,0:T(8,128)(2,1)S(1)}, u32[]{:S(2)}, u32[]{:S(2)}) collective-permute-start(bf16[16,2048]{1,0:T(8,128)(2,1)S(1)} %get-tuple-element.48), channel_id=1, source_target_pairs={{0,3},{1,2},{2,1},{3,0},{4,7},{5,6},{6,5},{7,4},{8,11},{9,10},{10,... | collective-permute-start | bytes 196616 | tf_op jit(solution)/shard_map/ppermute | solution.py:25
  4.5 1.4 %copy-start = (bf16[384,2048]{1,0:T(8,128)(2,1)S(1)}, bf16[384,2048]{1,0:T(8,128)(2,1)}, u32[]{:S(2)}) copy-start(bf16[384,2048]{1,0:T(8,128)(2,1)} %tokens_ref.1) | copy-start | bytes 4718596
  5.9 6.5 %copy-start.1 = (bf16[384,2048]{1,0:T(8,128)(2,1)S(1)}, bf16[384,2048]{1,0:T(8,128)(2,1)}, u32[]{:S(2)}) copy-start(bf16[384,2048]{1,0:T(8,128)(2,1)} %tokens_ref.1) | copy-start | bytes 4718596
  7.2 29.2 %collective-permute-start.6 = (bf16[384,1536]{1,0:T(8,128)(2,1)}, bf16[384,1536]{1,0:T(8,128)(2,1)}, u32[]{:S(2)}, u32[]{:S(2)}) collective-permute-start(bf16[384,1536]{1,0:T(8,128)(2,1)} %get-tuple-element.53), channel_id=1, source_target_pairs={{0,2},{1,3},{2,0},{3,1},{4,6},{5,7},{6,4},{7,5},{8,10},{9,11},{10,... | collective-permute-start | bytes 3538952 | tf_op jit(solution)/shard_map/ppermute | solution.py:25
  8.7 36.5 %collective-permute-start = (bf16[384,512]{1,0:T(8,128)(2,1)}, bf16[384,512]{1,0:T(8,128)(2,1)}, u32[]{:S(2)}, u32[]{:S(2)}) collective-permute-start(bf16[384,512]{1,0:T(8,128)(2,1)} %get-tuple-element.44), channel_id=1, source_target_pairs={{0,2},{1,3},{2,0},{3,1},{4,6},{5,7},{6,4},{7,5},{8,10},{9,11},{10,... | collective-permute-start | bytes 1179656 | tf_op jit(solution)/shard_map/ppermute | solution.py:25
  9.7 16.1 %collective-permute-start.9 = (bf16[64,2048]{1,0:T(8,128)(2,1)S(1)}, bf16[64,2048]{1,0:T(8,128)(2,1)S(1)}, u32[]{:S(2)}, u32[]{:S(2)}) collective-permute-start(bf16[64,2048]{1,0:T(8,128)(2,1)S(1)} %shard_map.65.refs_0_), channel_id=1, source_target_pairs={{0,8},{4,12},{8,0},{12,4},{16,28},{20,24},{24,20},{28,16},{1,9},{5... | collective-permute-start | bytes 786440 | tf_op jit(solution)/shard_map/ppermute | solution.py:274
  15.5 16.6 %copy-start.4 = (s32[1,384]{1,0:T(1,128)}, s32[1,384]{1,0:T(1,128)S(1)}, u32[]{:S(2)}) copy-start(s32[1,384]{1,0:T(1,128)S(1)} %get-tuple-element.54.stored_ref.refs_2_) | copy-start | bytes 4612
  15.5 13.9 %collective-permute-start.8 = (bf16[64,2048]{1,0:T(8,128)(2,1)S(1)}, bf16[64,2048]{1,0:T(8,128)(2,1)S(1)}, u32[]{:S(2)}, u32[]{:S(2)}) collective-permute-start(bf16[64,2048]{1,0:T(8,128)(2,1)S(1)} %shard_map.65.refs_0_), channel_id=1, source_target_pairs={{0,4},{4,0},{8,12},{12,8},{1,5},{5,1},{9,13},{13,9},{2,6},{6,2},{1... | collective-permute-start | bytes 786440 | tf_op jit(solution)/shard_map/ppermute | solution.py:25
  17.2 19.2 %collective-permute-start.7 = (bf16[64,512]{1,0:T(8,128)(2,1)}, bf16[64,512]{1,0:T(8,128)(2,1)}, u32[]{:S(2)}, u32[]{:S(2)}) collective-permute-start(bf16[64,512]{1,0:T(8,128)(2,1)} %bitcast.9.refs_5_), channel_id=1, source_target_pairs={{0,8},{4,12},{8,0},{12,4},{16,28},{20,24},{24,20},{28,16},{1,9},{5... | collective-permute-start | bytes 196616 | tf_op jit(solution)/shard_map/ppermute | solution.py:274
  25.8 6.4 %collective-permute-start.10 = (bf16[64,2048]{1,0:T(8,128)(2,1)S(1)}, bf16[64,2048]{1,0:T(8,128)(2,1)S(1)}, u32[]{:S(2)}, u32[]{:S(2)}) collective-permute-start(bf16[64,2048]{1,0:T(8,128)(2,1)S(1)} %collective-permute-done.9.refs_2_), channel_id=1, source_target_pairs={{0,16},{16,0},{1,17},{17,1},{2,18},{18,2},{3,19},{19,3},{4,20},{20... | collective-permute-start | bytes 786440 | tf_op jit(solution)/shard_map/ppermute | solution.py:25
  29.5 15.7 %collective-permute-start.5 = (bf16[64,512]{1,0:T(8,128)(2,1)}, bf16[64,512]{1,0:T(8,128)(2,1)}, u32[]{:S(2)}, u32[]{:S(2)}) collective-permute-start(bf16[64,512]{1,0:T(8,128)(2,1)} %bitcast.9.refs_5_), channel_id=1, source_target_pairs={{0,4},{4,0},{8,12},{12,8},{1,5},{5,1},{9,13},{13,9},{2,6},{6,2},{1... | collective-permute-start | bytes 196616 | tf_op jit(solution)/shard_map/ppermute | solution.py:25
  36.4 4.5 %collective-permute-start.13 = (f32[64,384]{1,0:T(8,128)S(1)}, f32[64,384]{1,0:T(8,128)S(1)}, u32[]{:S(2)}, u32[]{:S(2)}) collective-permute-start(f32[64,384]{1,0:T(8,128)S(1)} %shard_map.68), channel_id=1, source_target_pairs={{0,1},{1,0},{2,3},{3,2},{4,5},{5,4},{6,7},{7,6},{8,9},{9,8},{10,11... | collective-permute-start | bytes 294920 | tf_op jit(solution)/shard_map/ppermute | solution.py:25
  36.4 6.6 %collective-permute-start.12 = (bf16[384,1536]{1,0:T(8,128)(2,1)}, bf16[384,1536]{1,0:T(8,128)(2,1)S(1)}, u32[]{:S(2)}, u32[]{:S(2)}) collective-permute-start(bf16[384,1536]{1,0:T(8,128)(2,1)} %collective-permute-done.6.refs_0_), channel_id=1, source_target_pairs={{0,1},{1,0},{2,3},{3,2},{4,5},{5,4},{6,7},{7,6},{8,9},{9,8},{10,11... | collective-permute-start | bytes 3538952 | tf_op jit(solution)/shard_map/ppermute | solution.py:25
  39.2 6.0 %collective-permute-start.11 = (bf16[64,512]{1,0:T(8,128)(2,1)}, bf16[64,512]{1,0:T(8,128)(2,1)S(1)}, u32[]{:S(2)}, u32[]{:S(2)}) collective-permute-start(bf16[64,512]{1,0:T(8,128)(2,1)} %collective-permute-done.7.refs_7_), channel_id=1, source_target_pairs={{0,16},{16,0},{1,17},{17,1},{2,18},{18,2},{3,19},{19,3},{4,20},{20... | collective-permute-start | bytes 196616 | tf_op jit(solution)/shard_map/ppermute | solution.py:25
  41.5 5.3 %collective-permute-start.15 = (bf16[64,384]{1,0:T(8,128)(2,1)}, bf16[64,384]{1,0:T(8,128)(2,1)}, u32[]{:S(2)}, u32[]{:S(2)}) collective-permute-start(bf16[64,384]{1,0:T(8,128)(2,1)} %get-tuple-element.81), channel_id=1, source_target_pairs={{0,2},{1,3},{2,0},{3,1},{4,6},{5,7},{6,4},{7,5},{8,10},{9,11},{10,... | collective-permute-start | bytes 147464 | tf_op jit(solution)/shard_map/ppermute | solution.py:25
  45.1 2.0 %copy-start.5 = (s32[1,384]{1,0:T(1,128)S(1)}, s32[1,384]{1,0:T(1,128)}, u32[]{:S(2)}) copy-start(s32[1,384]{1,0:T(1,128)} %copy-done.4) | copy-start | bytes 4612
  45.2 2.0 %collective-permute-start.14 = (bf16[384,512]{1,0:T(8,128)(2,1)}, bf16[384,512]{1,0:T(8,128)(2,1)S(1)}, u32[]{:S(2)}, u32[]{:S(2)}) collective-permute-start(bf16[384,512]{1,0:T(8,128)(2,1)} %collective-permute-done.refs_0_), channel_id=1, source_target_pairs={{0,1},{1,0},{2,3},{3,2},{4,5},{5,4},{6,7},{7,6},{8,9},{9,8},{10,11... | collective-permute-start | bytes 1179656 | tf_op jit(solution)/shard_map/ppermute | solution.py:25

commit v13 on v12

--- a/solution.py
+++ b/solution.py
@@ -52,9 +52,28 @@
 
 
 def cut_kernel(edges, source_ref, *refs):
-    run_copies(
-        [(source_ref.at[:, a:b], out) for a, b, out in zip(edges, edges[1:], refs[:-1])], refs[-1]
-    )
+    outs, (held_ref, sems) = refs[:-2], refs[-2:]
+    steps, rows = held_ref.shape[:2]
+    copies = [
+        pltpu.make_async_copy(source_ref.at[pl.ds(i * rows, rows)], held_ref.at[i], sems.at[0, i])
+        for i in range(steps)
+    ]
+    for copy in copies:
+        copy.start()
+    leaving = []
+    for i in range(steps):
+        copies[i].wait()
+        for m, (a, b, out) in enumerate(zip(edges, edges[1:], outs)):
+            leaving.append(
+                pltpu.make_async_copy(
+                    held_ref.at[i, :, pl.ds(a, b - a)],
+                    out.at[pl.ds(i * rows, rows)],
+                    sems.at[1 + m, i],
+                )
+            )
+            leaving[-1].start()
+    for copy in leaving:
+        copy.wait()
 
 
 def order_kernel(rank_part, *refs):
@@ -213,16 +232,23 @@
         for flip in range(tensors)
     ]
     uncut, pieces = chained(tokens, pieces)
-    chunks = list(call(
-        functools.partial(cut_kernel, edges),
-        [jax.ShapeDtypeStruct((rows, b - a), tokens.dtype) for a, b in zip(edges, edges[1:])],
-        [ANYWHERE],
-        [pltpu.SemaphoreType.DMA((len(edges) - 1,))],
-        [VECTOR] * (len(edges) - 1),
-        mib=40,
-    )(uncut))
-    neighbour = flipped(uncut, "tensor", 1)
+    steps = 6
+    chunks = list(
+        call(
+            functools.partial(cut_kernel, edges),
+            [jax.ShapeDtypeStruct((rows, b - a), tokens.dtype) for a, b in zip(edges, edges[1:])],
+            [ANYWHERE],
+            [
+                pltpu.VMEM((steps, rows // steps, depth), tokens.dtype),
+                pltpu.SemaphoreType.DMA((len(edges), steps)),
+            ],
+            [ANYWHERE] * (len(edges) - 1),
+            mib=56,
+        )(uncut)
+    )
     pieces = [pieces[0]] + [flipped(pieces[f], "tensor", f) for f in range(1, tensors)]
+    pieces[1], here = chained(pieces[1], tokens)
+    neighbour = flipped(here, "tensor", 1)
     if down.shape[0] % 16 == 0:
         own = call(
             functools.partial(order_kernel, down.shape[0]),
@@ -241,7 +267,10 @@
 
     hops = range(CORES, tensors, CORES)
 
-    far = [[flipped(chunk, "tensor", hop) for hop in hops] for chunk in chunks]
+    def send(m):
+        return [flipped(chunks[m], "tensor", hop) for hop in hops]
+
+    far = [send(0)]
 
     def across(m):
         return [flipped(value, "tensor", 1) for value in far[m]]
@@ -279,7 +308,7 @@
     def swap(values):
         return [flipped(value, "parts", 1) for value in values]
 
-    own, neighbour, here = chained(own, neighbour, tokens)
+    own, here = chained(own, tokens)
     fetched = fetch_far(own)
     total, stored = call(
         functools.partial(first_kernel, tile, depth, [(0, 0)], slots),
@@ -291,7 +320,10 @@
         tile_scratch(tile, [tokens], columns),
         [VECTOR, VECTOR],
     )(placement, tenant.reshape(1, rows), frozen_projection_weight, here)
-    total, own, up = chained(total, own, lowrank_up_weight[0])
+    total, own, up, neighbour, chunks[1] = chained(
+        total, own, lowrank_up_weight[0], neighbour, chunks[1]
+    )
+    far.append(send(1))
     single, single_up = fetch_near(own), fetch_near(up)
     fetched, total = chained(fetched, total)
     swapped = swap(fetched)

time: 50.1 us -> 49.5 us (0.988)
  waiting for transfers between devices: 13.4 us -> 11.5 us
  starting transfers between devices: 15.2 us -> 16.9 us
  local copies, waits for them, and re-layouts: 2.39 us -> 0.98 us
  Pallas kernels: 17.9 us -> 18.9 us
    ppermute x14, waiting for transfers between devices: 5.15 us -> 2.54 us  [flipped(): return lax.ppermute(value, axis, [(i, i ^ flip) for i in range(count)])]
    ppermute x14, starting transfers between devices: 12.2 us -> 13.9 us  [flipped(): return lax.ppermute(value, axis, [(i, i ^ flip) for i in range(count)])]
    unnamed x12 -> x10, local copies, waits for them, and re-layouts: 1.43 us -> 0.03 us
    pallas_call x1, Pallas kernels: 1.28 us -> 2.23 us  [body(): call(functools.partial(cut_kernel, edges), [jax.ShapeDtypeStruct((rows, b...]
    ppermute x2, waiting for transfers between devices: 8.28 us -> 8.99 us  [fetch_far(): lax.ppermute(value, ('parts', 'adapter'), route)]
  transfers between devices with their start and end apart: 16 -> 16, of which waited for: 5 -> 4; matrix products, arithmetic and copies ran while one was open for 1% -> 1% of each run, Pallas kernels for 31% -> 33%
where the time goes in v13:
time: 49.5 us; the launch traced here: 49.2 us
  Pallas kernels  18.9 us (38%)
  starting transfers between devices  16.9 us (34%)
  waiting for transfers between devices  11.5 us (23%)
  local copies, waits for them, and re-layouts  0.98 us (2%)
  other arithmetic  0.63 us (1%)
    ppermute x14, starting transfers between devices, flipped(): return lax.ppermute(value, axis, [(i, i ^ flip) for i in range(count)])  13.9 us
    ppermute x2, waiting for transfers between devices, fetch_far(): lax.ppermute(value, ('parts', 'adapter'), route)  8.99 us
    pallas_call x4, Pallas kernels, products(): call(functools.partial(products_kernel, tile, depth, places), jax.ShapeDt...  8.68 us
    pallas_call x1, Pallas kernels, body(): call(functools.partial(first_kernel, tile, depth, [(0, 0)], slots), [jax....  3.15 us
    ppermute x2, starting transfers between devices, fetch_far(): lax.ppermute(value, ('parts', 'adapter'), route)  2.99 us
    pallas_call x1, Pallas kernels, body(): call(functools.partial(last_kernel, tile, depth, near_places(1), flips, p...  2.56 us
    ppermute x14, waiting for transfers between devices, flipped(): return lax.ppermute(value, axis, [(i, i ^ flip) for i in range(count)])  2.54 us
    pallas_call x1, Pallas kernels, body(): call(functools.partial(cut_kernel, edges), [jax.ShapeDtypeStruct((rows, b...  2.23 us
  transfers between devices with their start and end apart: 16, of which 4 were waited for; matrix products, arithmetic and copies ran while one was open for 1% of the time, Pallas kernels for 33%

profile of v13, /device:TPU:0, one launch (start us, length us, event | category | flops | bytes accessed | tf_op | source)
XLA Modules:
  0.0 49.2 jit_solution(1734898129878787292)
XLA Ops:
  0.0 1.0 %dynamic-slice_bitcast_fusion = (bf16[16,2048]{1,0:T(8,128)(2,1)S(1)}, bf16[16,2048]{1,0:T(8,128)(2,1)S(1)}, bf16[16,2048]{1,0:T(8,128)(2,1)S(1)}, bf16[16,2048]{1,0:T(8,128)(2,1)S(1)}) fusion(bf16[1,8192,16]{1,2,0:T(8,128)(2,1)} %param.10, s32[]{:T(128)S(6)} %select_n.15, s32[]{:T(128)S(6)} %select_n.13, s32[]{:T(128)S(6)} %select_n.12, s32[]{:T(128)S(6)} %select_n.14), kind=kLoop, calls=%fused_computation | loop fusion | bytes 524304 | tf_op jit(solution)/shard_map/dynamic_slice | solution.py:231
  1.0 0.5 %collective-permute-start = (bf16[16,2048]{1,0:T(8,128)(2,1)S(1)}, bf16[16,2048]{1,0:T(8,128)(2,1)S(1)}, u32[]{:S(2)}, u32[]{:S(2)}) collective-permute-start(bf16[16,2048]{1,0:T(8,128)(2,1)S(1)} %get-tuple-element.47), channel_id=1, source_target_pairs={{0,1},{1,0},{2,3},{3,2},{4,5},{5,4},{6,7},{7,6},{8,9},{9,8},{10,11... | collective-permute-start | bytes 196616 | tf_op jit(solution)/shard_map/ppermute | solution.py:25
  1.5 2.6 %collective-permute-start.1 = (bf16[16,2048]{1,0:T(8,128)(2,1)S(1)}, bf16[16,2048]{1,0:T(8,128)(2,1)S(1)}, u32[]{:S(2)}, u32[]{:S(2)}) collective-permute-start(bf16[16,2048]{1,0:T(8,128)(2,1)S(1)} %get-tuple-element.49), channel_id=1, source_target_pairs={{0,2},{1,3},{2,0},{3,1},{4,6},{5,7},{6,4},{7,5},{8,10},{9,11},{10,... | collective-permute-start | bytes 196616 | tf_op jit(solution)/shard_map/ppermute | solution.py:25
  4.1 2.2 %shard_map.66 = (bf16[384,1536]{1,0:T(8,128)(2,1)}, bf16[384,512]{1,0:T(8,128)(2,1)}) custom-call(bf16[384,2048]{1,0:T(8,128)(2,1)} %tokens_ref.1), custom_call_target="tpu_custom_call" | custom-call | flops 99999997952 | tf_op jit(solution)/shard_map/pallas_call | solution.py:237
  6.4 1.8 %collective-permute-start.6 = (bf16[384,1536]{1,0:T(8,128)(2,1)}, bf16[384,1536]{1,0:T(8,128)(2,1)}, u32[]{:S(2)}, u32[]{:S(2)}) collective-permute-start(bf16[384,1536]{1,0:T(8,128)(2,1)} %get-tuple-element.59), channel_id=1, source_target_pairs={{0,2},{1,3},{2,0},{3,1},{4,6},{5,7},{6,4},{7,5},{8,10},{9,11},{10,... | collective-permute-start | bytes 3538952 | tf_op jit(solution)/shard_map/ppermute | solution.py:25
  8.2 0.4 shard_map.64.refs_0_
  8.6 2.7 %collective-permute-start.9 = (bf16[64,2048]{1,0:T(8,128)(2,1)S(1)}, bf16[64,2048]{1,0:T(8,128)(2,1)S(1)}, u32[]{:S(2)}, u32[]{:S(2)}) collective-permute-start(bf16[64,2048]{1,0:T(8,128)(2,1)S(1)} %shard_map.64.refs_0_), channel_id=1, source_target_pairs={{0,8},{4,12},{8,0},{12,4},{16,28},{20,24},{24,20},{28,16},{1,9},{5... | collective-permute-start | bytes 786440 | tf_op jit(solution)/shard_map/ppermute | solution.py:303
  11.3 3.1 %shard_map.65 = (f32[384,512]{1,0:T(8,128)S(1)}, s32[1,384]{1,0:T(1,128)S(1)}) custom-call(s32[4]{0:T(128)S(1)} %copy-done.2, s32[1,384]{1,0:T(1,128)S(1)} %bitcast.18, bf16[8192,512]{1,0:T(8,128)(2,1)} %weight_ref.11, bf16[384,2048]{1,0:T(8,128)(2,1)S(1)} %copy-done), custom_call_target="tpu_custom_call" | custom-call | flops 99999997952 | tf_op jit(solution)/shard_map/pallas_call | solution.py:313
  15.0 1.6 %collective-permute-start.5 = (bf16[64,512]{1,0:T(8,128)(2,1)}, bf16[64,512]{1,0:T(8,128)(2,1)}, u32[]{:S(2)}, u32[]{:S(2)}) collective-permute-start(bf16[64,512]{1,0:T(8,128)(2,1)} %bitcast.9.refs_5_), channel_id=1, source_target_pairs={{0,4},{4,0},{8,12},{12,8},{1,5},{5,1},{9,13},{13,9},{2,6},{6,2},{1... | collective-permute-start | bytes 196616 | tf_op jit(solution)/shard_map/ppermute | solution.py:25
  16.6 9.0 %collective-permute-done.9.refs_2_ = bf16[64,2048]{1,0:T(8,128)(2,1)S(1)} collective-permute-done((bf16[64,2048]{1,0:T(8,128)(2,1)S(1)}, bf16[64,2048]{1,0:T(8,128)(2,1)S(1)}, u32[]{:S(2)}, u32[]{:S(2)}) %collective-permute-start.9) | collective-permute-done | bytes 262176 | tf_op jit(solution)/shard_map/ppermute | solution.py:303
  25.6 2.2 %collective-permute-start.8 = (bf16[64,2048]{1,0:T(8,128)(2,1)S(1)}, bf16[64,2048]{1,0:T(8,128)(2,1)S(1)}, u32[]{:S(2)}, u32[]{:S(2)}) collective-permute-start(bf16[64,2048]{1,0:T(8,128)(2,1)S(1)} %shard_map.64.refs_0_), channel_id=1, source_target_pairs={{0,4},{4,0},{8,12},{12,8},{1,5},{5,1},{9,13},{13,9},{2,6},{6,2},{1... | collective-permute-start | bytes 786440 | tf_op jit(solution)/shard_map/ppermute | solution.py:25
  27.8 2.6 %shard_map.67.refs_1_ = f32[384,512]{1,0:T(8,128)S(1)} custom-call(bf16[8192,512]{1,0:T(8,128)(2,1)} %weight_ref.11, bf16[384,2048]{1,0:T(8,128)(2,1)S(1)} %collective-permute-done.3.refs_0_, f32[384,512]{1,0:T(8,128)S(1)} %get-tuple-element.67.refs_1_), custom_call_target="tpu_custom_call" | custom-call | flops 99999997952 | tf_op jit(solution)/shard_map/pallas_call | solution.py:285
  30.4 1.9 %collective-permute-done.10.refs_3_ = bf16[64,2048]{1,0:T(8,128)(2,1)S(1)} collective-permute-done((bf16[64,2048]{1,0:T(8,128)(2,1)S(1)}, bf16[64,2048]{1,0:T(8,128)(2,1)S(1)}, u32[]{:S(2)}, u32[]{:S(2)}) %collective-permute-start.10) | collective-permute-done | bytes 262176 | tf_op jit(solution)/shard_map/ppermute | solution.py:25
  32.3 1.7 %collective-permute-start.4 = (bf16[384,512]{1,0:T(8,128)(2,1)}, bf16[384,512]{1,0:T(8,128)(2,1)}, u32[]{:S(2)}, u32[]{:S(2)}) collective-permute-start(bf16[384,512]{1,0:T(8,128)(2,1)} %get-tuple-element.57), channel_id=1, source_target_pairs={{0,2},{1,3},{2,0},{3,1},{4,6},{5,7},{6,4},{7,5},{8,10},{9,11},{10,... | collective-permute-start | bytes 1179656 | tf_op jit(solution)/shard_map/ppermute | solution.py:25
  34.0 1.9 %shard_map.68 = f32[64,384]{1,0:T(8,128)S(1)} custom-call(bf16[384,2048]{1,0:T(8,128)(2,1)S(1)} %copy-done, s32[1,384]{1,0:T(1,128)S(1)} %get-tuple-element.60.stored_ref.refs_2_, bf16[64,2048]{1,0:T(8,128)(2,1)S(1)} %shard_map.64.refs_0_, bf16[64,2048]{1,0:T(8,128)(2,1)S(1)} %collective-permute-done.8.refs_1_, ...), custom_call_target="tpu_custom_call" | custom-call | flops 99999997952 | tf_op jit(solution)/shard_map/pallas_call | solution.py:339
  36.0 0.5 %collective-permute-start.12 = (bf16[384,1536]{1,0:T(8,128)(2,1)}, bf16[384,1536]{1,0:T(8,128)(2,1)S(1)}, u32[]{:S(2)}, u32[]{:S(2)}) collective-permute-start(bf16[384,1536]{1,0:T(8,128)(2,1)} %collective-permute-done.6.refs_0_), channel_id=1, source_target_pairs={{0,1},{1,0},{2,3},{3,2},{4,5},{5,4},{6,7},{7,6},{8,9},{9,8},{10,11... | collective-permute-start | bytes 3538952 | tf_op jit(solution)/shard_map/ppermute | solution.py:25
  36.5 2.3 %shard_map.69.refs_1_ = f32[384,512]{1,0:T(8,128)S(1)} custom-call(bf16[8192,512]{1,0:T(8,128)(2,1)} %weight_ref.11, bf16[384,1536]{1,0:T(8,128)(2,1)} %collective-permute-done.6.refs_0_, f32[384,512]{1,0:T(8,128)S(1)} %shard_map.67.refs_1_), custom_call_target="tpu_custom_call" | custom-call | flops 99999997952 | tf_op jit(solution)/shard_map/pallas_call | solution.py:285
  38.8 1.4 %collective-permute-start.11 = (bf16[64,512]{1,0:T(8,128)(2,1)}, bf16[64,512]{1,0:T(8,128)(2,1)S(1)}, u32[]{:S(2)}, u32[]{:S(2)}) collective-permute-start(bf16[64,512]{1,0:T(8,128)(2,1)} %collective-permute-done.7.refs_7_), channel_id=1, source_target_pairs={{0,16},{16,0},{1,17},{17,1},{2,18},{18,2},{3,19},{19,3},{4,20},{20... | collective-permute-start | bytes 196616 | tf_op jit(solution)/shard_map/ppermute | solution.py:25
  40.2 0.6 %fusion = (bf16[64,384]{1,0:T(8,128)(2,1)}, f32[64,384]{1,0:T(8,128)S(1)}) fusion(f32[64,384]{1,0:T(8,128)S(1)} %shard_map.68, f32[64,384]{1,0:T(8,128)S(1)} %collective-permute-done.13), kind=kLoop, calls=%fused_computation.4 | loop fusion | flops 49152 | bytes 344064 | tf_op jit(solution)/shard_map/convert_element_type | solution.py:363
  40.9 1.5 %collective-permute-start.15 = (bf16[64,384]{1,0:T(8,128)(2,1)}, bf16[64,384]{1,0:T(8,128)(2,1)}, u32[]{:S(2)}, u32[]{:S(2)}) collective-permute-start(bf16[64,384]{1,0:T(8,128)(2,1)} %get-tuple-element.87), channel_id=1, source_target_pairs={{0,2},{1,3},{2,0},{3,1},{4,6},{5,7},{6,4},{7,5},{8,10},{9,11},{10,... | collective-permute-start | bytes 147464 | tf_op jit(solution)/shard_map/ppermute | solution.py:25
  42.3 2.2 %shard_map.70.refs_1_ = f32[384,512]{1,0:T(8,128)S(1)} custom-call(bf16[8192,512]{1,0:T(8,128)(2,1)} %weight_ref.11, bf16[384,1536]{1,0:T(8,128)(2,1)S(1)} %collective-permute-done.12.refs_0_, f32[384,512]{1,0:T(8,128)S(1)} %shard_map.69.refs_1_), custom_call_target="tpu_custom_call" | custom-call | flops 99999997952 | tf_op jit(solution)/shard_map/pallas_call | solution.py:285
  44.7 1.6 %shard_map.71.refs_1_ = f32[384,512]{1,0:T(8,128)S(1)} custom-call(bf16[8192,512]{1,0:T(8,128)(2,1)} %weight_ref.11, bf16[384,512]{1,0:T(8,128)(2,1)} %collective-permute-done.4.refs_0_, f32[384,512]{1,0:T(8,128)S(1)} %shard_map.70.refs_1_), custom_call_target="tpu_custom_call" | custom-call | flops 99999997952 | tf_op jit(solution)/shard_map/pallas_call | solution.py:285
  46.3 0.4 collective-permute-done.14.refs_0_
  46.6 2.6 %shard_map.72 = bf16[384,512]{1,0:T(8,128)(2,1)} custom-call(bf16[8192,512]{1,0:T(8,128)(2,1)} %weight_ref.11, bf16[384,512]{1,0:T(8,128)(2,1)S(1)} %collective-permute-done.14.refs_0_, f32[384,512]{1,0:T(8,128)S(1)} %shard_map.71.refs_1_, s32[1,384]{1,0:T(1,128)S(1)} %copy-done.4, f32[64,384]{1,0:T(8,128)S(1)} %get-tuple-element.81.refs_3_, ...), custom_call_target="tpu_custom_call" | custom-call | flops 99999997952 | tf_op jit(solution)/shard_map/pallas_call | solution.py:371
  (29 shorter events, 0.8 us)
Async XLA Ops:
  1.0 10.3 %copy-start = (bf16[384,2048]{1,0:T(8,128)(2,1)S(1)}, bf16[384,2048]{1,0:T(8,128)(2,1)}, u32[]{:S(2)}) copy-start(bf16[384,2048]{1,0:T(8,128)(2,1)} %tokens_ref.1) | copy-start | bytes 4718596
  1.0 10.3 %copy-start.1 = (s32[384,1]{0,1:T(1,128)S(1)}, s32[384,1]{0,1:T(1,128)}, u32[]{:S(2)}) copy-start(s32[384,1]{0,1:T(1,128)} %param.7) | copy-start | bytes 4612
  1.0 10.3 %copy-start.2 = (s32[4]{0:T(128)S(1)}, s32[4]{0:T(128)}, u32[]{:S(2)}) copy-start(s32[4]{0:T(128)} %placement_ref.1) | copy-start | bytes 52
  1.0 7.2 %collective-permute-start = (bf16[16,2048]{1,0:T(8,128)(2,1)S(1)}, bf16[16,2048]{1,0:T(8,128)(2,1)S(1)}, u32[]{:S(2)}, u32[]{:S(2)}) collective-permute-start(bf16[16,2048]{1,0:T(8,128)(2,1)S(1)} %get-tuple-element.47), channel_id=1, source_target_pairs={{0,1},{1,0},{2,3},{3,2},{4,5},{5,4},{6,7},{7,6},{8,9},{9,8},{10,11... | collective-permute-start | bytes 196616 | tf_op jit(solution)/shard_map/ppermute | solution.py:25
  1.5 6.7 %collective-permute-start.1 = (bf16[16,2048]{1,0:T(8,128)(2,1)S(1)}, bf16[16,2048]{1,0:T(8,128)(2,1)S(1)}, u32[]{:S(2)}, u32[]{:S(2)}) collective-permute-start(bf16[16,2048]{1,0:T(8,128)(2,1)S(1)} %get-tuple-element.49), channel_id=1, source_target_pairs={{0,2},{1,3},{2,0},{3,1},{4,6},{5,7},{6,4},{7,5},{8,10},{9,11},{10,... | collective-permute-start | bytes 196616 | tf_op jit(solution)/shard_map/ppermute | solution.py:25
  4.1 4.1 %collective-permute-start.2 = (bf16[16,2048]{1,0:T(8,128)(2,1)S(1)}, bf16[16,2048]{1,0:T(8,128)(2,1)S(1)}, u32[]{:S(2)}, u32[]{:S(2)}) collective-permute-start(bf16[16,2048]{1,0:T(8,128)(2,1)S(1)} %get-tuple-element.50), channel_id=1, source_target_pairs={{0,3},{1,2},{2,1},{3,0},{4,7},{5,6},{6,5},{7,4},{8,11},{9,10},{10,... | collective-permute-start | bytes 196616 | tf_op jit(solution)/shard_map/ppermute | solution.py:25
  6.4 29.5 %collective-permute-start.6 = (bf16[384,1536]{1,0:T(8,128)(2,1)}, bf16[384,1536]{1,0:T(8,128)(2,1)}, u32[]{:S(2)}, u32[]{:S(2)}) collective-permute-start(bf16[384,1536]{1,0:T(8,128)(2,1)} %get-tuple-element.59), channel_id=1, source_target_pairs={{0,2},{1,3},{2,0},{3,1},{4,6},{5,7},{6,4},{7,5},{8,10},{9,11},{10,... | collective-permute-start | bytes 3538952 | tf_op jit(solution)/shard_map/ppermute | solution.py:25
  8.6 17.0 %collective-permute-start.9 = (bf16[64,2048]{1,0:T(8,128)(2,1)S(1)}, bf16[64,2048]{1,0:T(8,128)(2,1)S(1)}, u32[]{:S(2)}, u32[]{:S(2)}) collective-permute-start(bf16[64,2048]{1,0:T(8,128)(2,1)S(1)} %shard_map.64.refs_0_), channel_id=1, source_target_pairs={{0,8},{4,12},{8,0},{12,4},{16,28},{20,24},{24,20},{28,16},{1,9},{5... | collective-permute-start | bytes 786440 | tf_op jit(solution)/shard_map/ppermute | solution.py:303
  11.2 3.4 %collective-permute-start.3 = (bf16[384,2048]{1,0:T(8,128)(2,1)S(1)}, bf16[384,2048]{1,0:T(8,128)(2,1)S(1)}, u32[]{:S(2)}, u32[]{:S(2)}) collective-permute-start(bf16[384,2048]{1,0:T(8,128)(2,1)S(1)} %copy-done), channel_id=1, source_target_pairs={{0,1},{1,0},{2,3},{3,2},{4,5},{5,4},{6,7},{7,6},{8,9},{9,8},{10,11... | collective-permute-start | bytes 4718600 | tf_op jit(solution)/shard_map/ppermute | solution.py:25
  14.4 19.6 %copy-start.3 = (s32[1,384]{1,0:T(1,128)}, s32[1,384]{1,0:T(1,128)S(1)}, u32[]{:S(2)}) copy-start(s32[1,384]{1,0:T(1,128)S(1)} %get-tuple-element.60.stored_ref.refs_2_) | copy-start | bytes 4612
  14.7 21.2 %collective-permute-start.7 = (bf16[64,512]{1,0:T(8,128)(2,1)}, bf16[64,512]{1,0:T(8,128)(2,1)}, u32[]{:S(2)}, u32[]{:S(2)}) collective-permute-start(bf16[64,512]{1,0:T(8,128)(2,1)} %bitcast.9.refs_5_), channel_id=1, source_target_pairs={{0,8},{4,12},{8,0},{12,4},{16,28},{20,24},{24,20},{28,16},{1,9},{5... | collective-permute-start | bytes 196616 | tf_op jit(solution)/shard_map/ppermute | solution.py:303
  15.0 29.6 %collective-permute-start.5 = (bf16[64,512]{1,0:T(8,128)(2,1)}, bf16[64,512]{1,0:T(8,128)(2,1)}, u32[]{:S(2)}, u32[]{:S(2)}) collective-permute-start(bf16[64,512]{1,0:T(8,128)(2,1)} %bitcast.9.refs_5_), channel_id=1, source_target_pairs={{0,4},{4,0},{8,12},{12,8},{1,5},{5,1},{9,13},{13,9},{2,6},{6,2},{1... | collective-permute-start | bytes 196616 | tf_op jit(solution)/shard_map/ppermute | solution.py:25
  25.6 6.7 %collective-permute-start.10 = (bf16[64,2048]{1,0:T(8,128)(2,1)S(1)}, bf16[64,2048]{1,0:T(8,128)(2,1)S(1)}, u32[]{:S(2)}, u32[]{:S(2)}) collective-permute-start(bf16[64,2048]{1,0:T(8,128)(2,1)S(1)} %collective-permute-done.9.refs_2_), channel_id=1, source_target_pairs={{0,16},{16,0},{1,17},{17,1},{2,18},{18,2},{3,19},{19,3},{4,20},{20... | collective-permute-start | bytes 786440 | tf_op jit(solution)/shard_map/ppermute | solution.py:25
  25.6 8.4 %collective-permute-start.8 = (bf16[64,2048]{1,0:T(8,128)(2,1)S(1)}, bf16[64,2048]{1,0:T(8,128)(2,1)S(1)}, u32[]{:S(2)}, u32[]{:S(2)}) collective-permute-start(bf16[64,2048]{1,0:T(8,128)(2,1)S(1)} %shard_map.64.refs_0_), channel_id=1, source_target_pairs={{0,4},{4,0},{8,12},{12,8},{1,5},{5,1},{9,13},{13,9},{2,6},{6,2},{1... | collective-permute-start | bytes 786440 | tf_op jit(solution)/shard_map/ppermute | solution.py:25
  32.3 12.3 %collective-permute-start.4 = (bf16[384,512]{1,0:T(8,128)(2,1)}, bf16[384,512]{1,0:T(8,128)(2,1)}, u32[]{:S(2)}, u32[]{:S(2)}) collective-permute-start(bf16[384,512]{1,0:T(8,128)(2,1)} %get-tuple-element.57), channel_id=1, source_target_pairs={{0,2},{1,3},{2,0},{3,1},{4,6},{5,7},{6,4},{7,5},{8,10},{9,11},{10,... | collective-permute-start | bytes 1179656 | tf_op jit(solution)/shard_map/ppermute | solution.py:25
  35.9 4.3 %collective-permute-start.13 = (f32[64,384]{1,0:T(8,128)S(1)}, f32[64,384]{1,0:T(8,128)S(1)}, u32[]{:S(2)}, u32[]{:S(2)}) collective-permute-start(f32[64,384]{1,0:T(8,128)S(1)} %shard_map.68), channel_id=1, source_target_pairs={{0,1},{1,0},{2,3},{3,2},{4,5},{5,4},{6,7},{7,6},{8,9},{9,8},{10,11... | collective-permute-start | bytes 294920 | tf_op jit(solution)/shard_map/ppermute | solution.py:25
  36.0 6.4 %collective-permute-start.12 = (bf16[384,1536]{1,0:T(8,128)(2,1)}, bf16[384,1536]{1,0:T(8,128)(2,1)S(1)}, u32[]{:S(2)}, u32[]{:S(2)}) collective-permute-start(bf16[384,1536]{1,0:T(8,128)(2,1)} %collective-permute-done.6.refs_0_), channel_id=1, source_target_pairs={{0,1},{1,0},{2,3},{3,2},{4,5},{5,4},{6,7},{7,6},{8,9},{9,8},{10,11... | collective-permute-start | bytes 3538952 | tf_op jit(solution)/shard_map/ppermute | solution.py:25
  38.8 5.8 %collective-permute-start.11 = (bf16[64,512]{1,0:T(8,128)(2,1)}, bf16[64,512]{1,0:T(8,128)(2,1)S(1)}, u32[]{:S(2)}, u32[]{:S(2)}) collective-permute-start(bf16[64,512]{1,0:T(8,128)(2,1)} %collective-permute-done.7.refs_7_), channel_id=1, source_target_pairs={{0,16},{16,0},{1,17},{17,1},{2,18},{18,2},{3,19},{19,3},{4,20},{20... | collective-permute-start | bytes 196616 | tf_op jit(solution)/shard_map/ppermute | solution.py:25
  40.9 5.4 %collective-permute-start.15 = (bf16[64,384]{1,0:T(8,128)(2,1)}, bf16[64,384]{1,0:T(8,128)(2,1)}, u32[]{:S(2)}, u32[]{:S(2)}) collective-permute-start(bf16[64,384]{1,0:T(8,128)(2,1)} %get-tuple-element.87), channel_id=1, source_target_pairs={{0,2},{1,3},{2,0},{3,1},{4,6},{5,7},{6,4},{7,5},{8,10},{9,11},{10,... | collective-permute-start | bytes 147464 | tf_op jit(solution)/shard_map/ppermute | solution.py:25
  44.6 2.0 %copy-start.4 = (s32[1,384]{1,0:T(1,128)S(1)}, s32[1,384]{1,0:T(1,128)}, u32[]{:S(2)}) copy-start(s32[1,384]{1,0:T(1,128)} %copy-done.3) | copy-start | bytes 4612
  44.6 2.0 %collective-permute-start.14 = (bf16[384,512]{1,0:T(8,128)(2,1)}, bf16[384,512]{1,0:T(8,128)(2,1)S(1)}, u32[]{:S(2)}, u32[]{:S(2)}) collective-permute-start(bf16[384,512]{1,0:T(8,128)(2,1)} %collective-permute-done.4.refs_0_), channel_id=1, source_target_pairs={{0,1},{1,0},{2,3},{3,2},{4,5},{5,4},{6,7},{7,6},{8,9},{9,8},{10,11... | collective-permute-start | bytes 1179656 | tf_op jit(solution)/shard_map/ppermute | solution.py:25

commit v14 on v13

--- a/solution.py
+++ b/solution.py
@@ -39,6 +39,11 @@
         cost_estimate=cost,
         compiler_params=pltpu.CompilerParams(vmem_limit_bytes=mib * MIB),
     )
+
+
+def tile_of(*widths):
+    whole = math.gcd(*widths)
+    return max(t for t in range(1, whole + 1) if whole % t == 0 and (t == whole or t % LANES == 0) and t <= 768)
 
 
 def run_copies(pairs, sems):
@@ -282,6 +287,7 @@
         return [(hop ^ 1, edges[m]) for hop in hops]
 
     def products(places, features, total):
+        tile = tile_of(*[f.shape[1] for f in features])
         return call(
             functools.partial(products_kernel, tile, depth, places),
             jax.ShapeDtypeStruct((rows, columns), jnp.float32),
@@ -330,7 +336,9 @@
     fetched_up = fetch_far(up)
     total, neighbour = chained(total, neighbour)
     total = products([(1, 0)], [neighbour], total)
-    single, swapped, total = chained(single, swapped, total)
+    single, swapped, single_up, fetched_up, total = chained(
+        single, swapped, single_up, fetched_up, total
+    )
     downs = [own] + single
     for pair in zip(fetched, swapped):
         downs += pair
@@ -347,9 +355,10 @@
             pltpu.SemaphoreType.DMA((1 + slots, tiles)),
         ],
     )(tokens, stored, *downs)
-    far[0], fetched_up, partial = chained(far[0], fetched_up, partial)
+    swapped_up = swap(fetched_up)
+    far[0], swapped_up, partial = chained(far[0], swapped_up, partial)
     ups = [up] + single_up
-    for pair in zip(fetched_up, swap(fetched_up)):
+    for pair in zip(fetched_up, swapped_up):
         ups += pair
     near = across(0)
     total = products(far_places(0), far[0], total)

time: 49.5 us -> 49.9 us (level)
  local copies, waits for them, and re-layouts: 0.98 us -> 1.64 us
    unnamed x10 -> x26, local copies, waits for them, and re-layouts: 0.03 us -> 0.68 us
  transfers between devices with their start and end apart: 16 -> 16, of which waited for: 4 -> 6; matrix products, arithmetic and copies ran while one was open for 1% -> 1% of each run, Pallas kernels for 33% -> 33%
where the time goes in v14:
time: 49.9 us; the launch traced here: 49.5 us
  Pallas kernels  18.9 us (38%)
  starting transfers between devices  16.9 us (34%)
  waiting for transfers between devices  11.2 us (22%)
  local copies, waits for them, and re-layouts  1.64 us (3%)
  other arithmetic  0.63 us (1%)
    ppermute x14, starting transfers between devices, flipped(): return lax.ppermute(value, axis, [(i, i ^ flip) for i in range(count)])  13.9 us
    ppermute x2, waiting for transfers between devices, fetch_far(): lax.ppermute(value, ('parts', 'adapter'), route)  8.98 us
    pallas_call x4, Pallas kernels, products(): call(functools.partial(products_kernel, tile, depth, places), jax.ShapeDt...  8.55 us
    pallas_call x1, Pallas kernels, body(): call(functools.partial(first_kernel, tile, depth, [(0, 0)], slots), [jax....  3.15 us
    ppermute x2, starting transfers between devices, fetch_far(): lax.ppermute(value, ('parts', 'adapter'), route)  2.99 us
    pallas_call x1, Pallas kernels, body(): call(functools.partial(last_kernel, tile, depth, near_places(1), flips, p...  2.71 us
    pallas_call x1, Pallas kernels, body(): call(functools.partial(cut_kernel, edges), [jax.ShapeDtypeStruct((rows, b...  2.23 us
    ppermute x14, waiting for transfers between devices, flipped(): return lax.ppermute(value, axis, [(i, i ^ flip) for i in range(count)])  2.21 us
  transfers between devices with their start and end apart: 16, of which 6 were waited for; matrix products, arithmetic and copies ran while one was open for 1% of the time, Pallas kernels for 33%

profile of v14, /device:TPU:0, one launch (start us, length us, event | category | flops | bytes accessed | tf_op | source)
XLA Modules:
  0.0 49.5 jit_solution(17510008265612471143)
XLA Ops:
  0.0 1.0 %dynamic-slice_bitcast_fusion = (bf16[16,2048]{1,0:T(8,128)(2,1)S(1)}, bf16[16,2048]{1,0:T(8,128)(2,1)S(1)}, bf16[16,2048]{1,0:T(8,128)(2,1)S(1)}, bf16[16,2048]{1,0:T(8,128)(2,1)S(1)}) fusion(bf16[1,8192,16]{1,2,0:T(8,128)(2,1)} %param.10, s32[]{:T(128)S(6)} %select_n.15, s32[]{:T(128)S(6)} %select_n.13, s32[]{:T(128)S(6)} %select_n.12, s32[]{:T(128)S(6)} %select_n.14), kind=kLoop, calls=%fused_computation | loop fusion | bytes 524304 | tf_op jit(solution)/shard_map/dynamic_slice | solution.py:236
  1.0 0.5 %collective-permute-start = (bf16[16,2048]{1,0:T(8,128)(2,1)S(1)}, bf16[16,2048]{1,0:T(8,128)(2,1)S(1)}, u32[]{:S(2)}, u32[]{:S(2)}) collective-permute-start(bf16[16,2048]{1,0:T(8,128)(2,1)S(1)} %get-tuple-element.49), channel_id=1, source_target_pairs={{0,1},{1,0},{2,3},{3,2},{4,5},{5,4},{6,7},{7,6},{8,9},{9,8},{10,11... | collective-permute-start | bytes 196616 | tf_op jit(solution)/shard_map/ppermute | solution.py:25
  1.5 2.6 %collective-permute-start.1 = (bf16[16,2048]{1,0:T(8,128)(2,1)S(1)}, bf16[16,2048]{1,0:T(8,128)(2,1)S(1)}, u32[]{:S(2)}, u32[]{:S(2)}) collective-permute-start(bf16[16,2048]{1,0:T(8,128)(2,1)S(1)} %get-tuple-element.51), channel_id=1, source_target_pairs={{0,2},{1,3},{2,0},{3,1},{4,6},{5,7},{6,4},{7,5},{8,10},{9,11},{10,... | collective-permute-start | bytes 196616 | tf_op jit(solution)/shard_map/ppermute | solution.py:25
  4.1 2.2 %shard_map.66 = (bf16[384,1536]{1,0:T(8,128)(2,1)}, bf16[384,512]{1,0:T(8,128)(2,1)}) custom-call(bf16[384,2048]{1,0:T(8,128)(2,1)} %tokens_ref.1), custom_call_target="tpu_custom_call" | custom-call | flops 99999997952 | tf_op jit(solution)/shard_map/pallas_call | solution.py:242
  6.4 1.8 %collective-permute-start.10 = (bf16[384,1536]{1,0:T(8,128)(2,1)}, bf16[384,1536]{1,0:T(8,128)(2,1)}, u32[]{:S(2)}, u32[]{:S(2)}) collective-permute-start(bf16[384,1536]{1,0:T(8,128)(2,1)} %get-tuple-element.70), channel_id=1, source_target_pairs={{0,2},{1,3},{2,0},{3,1},{4,6},{5,7},{6,4},{7,5},{8,10},{9,11},{10,... | collective-permute-start | bytes 3538952 | tf_op jit(solution)/shard_map/ppermute | solution.py:25
  8.6 2.7 %collective-permute-start.6 = (bf16[64,2048]{1,0:T(8,128)(2,1)S(1)}, bf16[64,2048]{1,0:T(8,128)(2,1)S(1)}, u32[]{:S(2)}, u32[]{:S(2)}) collective-permute-start(bf16[64,2048]{1,0:T(8,128)(2,1)S(1)} %shard_map.64.refs_0_), channel_id=1, source_target_pairs={{0,8},{4,12},{8,0},{12,4},{16,28},{20,24},{24,20},{28,16},{1,9},{5... | collective-permute-start | bytes 786440 | tf_op jit(solution)/shard_map/ppermute | solution.py:309
  11.3 3.1 %shard_map.65 = (f32[384,512]{1,0:T(8,128)S(1)}, s32[1,384]{1,0:T(1,128)S(1)}) custom-call(s32[4]{0:T(128)S(1)} %copy-done.10, s32[1,384]{1,0:T(1,128)S(1)} %bitcast.21, bf16[8192,512]{1,0:T(8,128)(2,1)} %weight_ref.11, bf16[384,2048]{1,0:T(8,128)(2,1)S(1)} %copy-done), custom_call_target="tpu_custom_call" | custom-call | flops 99999997952 | tf_op jit(solution)/shard_map/pallas_call | solution.py:319
  15.0 1.6 %collective-permute-start.8 = (bf16[64,512]{1,0:T(8,128)(2,1)S(1)}, bf16[64,512]{1,0:T(8,128)(2,1)S(1)}, u32[]{:S(2)}, u32[]{:S(2)}) collective-permute-start(bf16[64,512]{1,0:T(8,128)(2,1)S(1)} %bitcast.19), channel_id=1, source_target_pairs={{0,4},{4,0},{8,12},{12,8},{1,5},{5,1},{9,13},{13,9},{2,6},{6,2},{1... | collective-permute-start | bytes 196616 | tf_op jit(solution)/shard_map/ppermute | solution.py:25
  16.6 9.0 %collective-permute-done.6.refs_2_ = bf16[64,2048]{1,0:T(8,128)(2,1)S(1)} collective-permute-done((bf16[64,2048]{1,0:T(8,128)(2,1)S(1)}, bf16[64,2048]{1,0:T(8,128)(2,1)S(1)}, u32[]{:S(2)}, u32[]{:S(2)}) %collective-permute-start.6) | collective-permute-done | bytes 262176 | tf_op jit(solution)/shard_map/ppermute | solution.py:309
  25.6 2.2 %collective-permute-start.5 = (bf16[64,2048]{1,0:T(8,128)(2,1)S(1)}, bf16[64,2048]{1,0:T(8,128)(2,1)S(1)}, u32[]{:S(2)}, u32[]{:S(2)}) collective-permute-start(bf16[64,2048]{1,0:T(8,128)(2,1)S(1)} %shard_map.64.refs_0_), channel_id=1, source_target_pairs={{0,4},{4,0},{8,12},{12,8},{1,5},{5,1},{9,13},{13,9},{2,6},{6,2},{1... | collective-permute-start | bytes 786440 | tf_op jit(solution)/shard_map/ppermute | solution.py:25
  27.8 2.6 %shard_map.67.refs_1_ = f32[384,512]{1,0:T(8,128)S(1)} custom-call(bf16[8192,512]{1,0:T(8,128)(2,1)} %weight_ref.11, bf16[384,2048]{1,0:T(8,128)(2,1)S(1)} %collective-permute-done.3.refs_0_, f32[384,512]{1,0:T(8,128)S(1)} %get-tuple-element.67.refs_1_), custom_call_target="tpu_custom_call" | custom-call | flops 99999997952 | tf_op jit(solution)/shard_map/pallas_call | solution.py:291
  30.4 1.5 %collective-permute-start.4 = (bf16[384,512]{1,0:T(8,128)(2,1)}, bf16[384,512]{1,0:T(8,128)(2,1)}, u32[]{:S(2)}, u32[]{:S(2)}) collective-permute-start(bf16[384,512]{1,0:T(8,128)(2,1)} %get-tuple-element.59), channel_id=1, source_target_pairs={{0,2},{1,3},{2,0},{3,1},{4,6},{5,7},{6,4},{7,5},{8,10},{9,11},{10,... | collective-permute-start | bytes 1179656 | tf_op jit(solution)/shard_map/ppermute | solution.py:25
  31.8 0.4 collective-permute-done.7.refs_3_
  32.6 1.5 %collective-permute-start.11 = (bf16[64,512]{1,0:T(8,128)(2,1)S(1)}, bf16[64,512]{1,0:T(8,128)(2,1)S(1)}, u32[]{:S(2)}, u32[]{:S(2)}) collective-permute-start(bf16[64,512]{1,0:T(8,128)(2,1)S(1)} %collective-permute-done.9.refs_7_), channel_id=1, source_target_pairs={{0,16},{16,0},{1,17},{17,1},{2,18},{18,2},{3,19},{19,3},{4,20},{20... | collective-permute-start | bytes 196616 | tf_op jit(solution)/shard_map/ppermute | solution.py:25
  34.0 1.9 %shard_map.68 = f32[64,384]{1,0:T(8,128)S(1)} custom-call(bf16[384,2048]{1,0:T(8,128)(2,1)S(1)} %copy-done, s32[1,384]{1,0:T(1,128)S(1)} %get-tuple-element.71.stored_ref.refs_2_, bf16[64,2048]{1,0:T(8,128)(2,1)S(1)} %shard_map.64.refs_0_, bf16[64,2048]{1,0:T(8,128)(2,1)S(1)} %collective-permute-done.5.refs_1_, ...), custom_call_target="tpu_custom_call" | custom-call | flops 99999997952 | tf_op jit(solution)/shard_map/pallas_call | solution.py:347
  36.0 0.9 %collective-permute-done.11.refs_8_ = bf16[64,512]{1,0:T(8,128)(2,1)S(1)} collective-permute-done((bf16[64,512]{1,0:T(8,128)(2,1)S(1)}, bf16[64,512]{1,0:T(8,128)(2,1)S(1)}, u32[]{:S(2)}, u32[]{:S(2)}) %collective-permute-start.11) | collective-permute-done | bytes 65568 | tf_op jit(solution)/shard_map/ppermute | solution.py:25
  36.8 0.6 %copy-done.7 = bf16[64,512]{1,0:T(8,128)(2,1)} copy-done((bf16[64,512]{1,0:T(8,128)(2,1)}, bf16[64,512]{1,0:T(8,128)(2,1)S(1)}, u32[]{:S(2)}) %copy-start.7) | copy-done | bytes 65560
  37.5 0.5 %collective-permute-start.12 = (bf16[384,1536]{1,0:T(8,128)(2,1)}, bf16[384,1536]{1,0:T(8,128)(2,1)S(1)}, u32[]{:S(2)}, u32[]{:S(2)}) collective-permute-start(bf16[384,1536]{1,0:T(8,128)(2,1)} %collective-permute-done.10.refs_0_), channel_id=1, source_target_pairs={{0,1},{1,0},{2,3},{3,2},{4,5},{5,4},{6,7},{7,6},{8,9},{9,8},{10,11... | collective-permute-start | bytes 3538952 | tf_op jit(solution)/shard_map/ppermute | solution.py:25
  38.0 2.3 %shard_map.69.refs_1_ = f32[384,512]{1,0:T(8,128)S(1)} custom-call(bf16[8192,512]{1,0:T(8,128)(2,1)} %weight_ref.11, bf16[384,1536]{1,0:T(8,128)(2,1)} %collective-permute-done.10.refs_0_, f32[384,512]{1,0:T(8,128)S(1)} %shard_map.67.refs_1_), custom_call_target="tpu_custom_call" | custom-call | flops 99999997952 | tf_op jit(solution)/shard_map/pallas_call | solution.py:291
  40.3 0.6 %fusion = (bf16[64,384]{1,0:T(8,128)(2,1)}, f32[64,384]{1,0:T(8,128)S(1)}) fusion(f32[64,384]{1,0:T(8,128)S(1)} %shard_map.68, f32[64,384]{1,0:T(8,128)S(1)} %collective-permute-done.13), kind=kLoop, calls=%fused_computation.4 | loop fusion | flops 49152 | bytes 344064 | tf_op jit(solution)/shard_map/convert_element_type | solution.py:372
  40.9 1.7 %collective-permute-start.15 = (bf16[64,384]{1,0:T(8,128)(2,1)}, bf16[64,384]{1,0:T(8,128)(2,1)}, u32[]{:S(2)}, u32[]{:S(2)}) collective-permute-start(bf16[64,384]{1,0:T(8,128)(2,1)} %get-tuple-element.91), channel_id=1, source_target_pairs={{0,2},{1,3},{2,0},{3,1},{4,6},{5,7},{6,4},{7,5},{8,10},{9,11},{10,... | collective-permute-start | bytes 147464 | tf_op jit(solution)/shard_map/ppermute | solution.py:25
  42.6 2.1 %shard_map.70.refs_1_ = f32[384,512]{1,0:T(8,128)S(1)} custom-call(bf16[8192,512]{1,0:T(8,128)(2,1)} %weight_ref.11, bf16[384,1536]{1,0:T(8,128)(2,1)S(1)} %collective-permute-done.12.refs_0_, f32[384,512]{1,0:T(8,128)S(1)} %shard_map.69.refs_1_), custom_call_target="tpu_custom_call" | custom-call | flops 99999997952 | tf_op jit(solution)/shard_map/pallas_call | solution.py:291
  44.9 1.6 %shard_map.71.refs_1_ = f32[384,512]{1,0:T(8,128)S(1)} custom-call(bf16[8192,512]{1,0:T(8,128)(2,1)} %weight_ref.11, bf16[384,512]{1,0:T(8,128)(2,1)} %collective-permute-done.4.refs_0_, f32[384,512]{1,0:T(8,128)S(1)} %shard_map.70.refs_1_), custom_call_target="tpu_custom_call" | custom-call | flops 99999997952 | tf_op jit(solution)/shard_map/pallas_call | solution.py:291
  46.8 2.7 %shard_map.72 = bf16[384,512]{1,0:T(8,128)(2,1)} custom-call(bf16[8192,512]{1,0:T(8,128)(2,1)} %weight_ref.11, bf16[384,512]{1,0:T(8,128)(2,1)S(1)} %collective-permute-done.14.refs_0_, f32[384,512]{1,0:T(8,128)S(1)} %shard_map.71.refs_1_, s32[1,384]{1,0:T(1,128)S(1)} %copy-done.12, f32[64,384]{1,0:T(8,128)S(1)} %get-tuple-element.85.refs_3_, ...), custom_call_target="tpu_custom_call" | custom-call | flops 99999997952 | tf_op jit(solution)/shard_map/pallas_call | solution.py:380
  (45 shorter events, 1.8 us)
Async XLA Ops:
  1.0 10.3 %copy-start = (bf16[384,2048]{1,0:T(8,128)(2,1)S(1)}, bf16[384,2048]{1,0:T(8,128)(2,1)}, u32[]{:S(2)}) copy-start(bf16[384,2048]{1,0:T(8,128)(2,1)} %tokens_ref.1) | copy-start | bytes 4718596
  1.0 10.3 %copy-start.9 = (s32[384,1]{0,1:T(1,128)S(1)}, s32[384,1]{0,1:T(1,128)}, u32[]{:S(2)}) copy-start(s32[384,1]{0,1:T(1,128)} %param.7) | copy-start | bytes 4612
  1.0 10.3 %copy-start.10 = (s32[4]{0:T(128)S(1)}, s32[4]{0:T(128)}, u32[]{:S(2)}) copy-start(s32[4]{0:T(128)} %placement_ref.1) | copy-start | bytes 52
  1.0 7.2 %collective-permute-start = (bf16[16,2048]{1,0:T(8,128)(2,1)S(1)}, bf16[16,2048]{1,0:T(8,128)(2,1)S(1)}, u32[]{:S(2)}, u32[]{:S(2)}) collective-permute-start(bf16[16,2048]{1,0:T(8,128)(2,1)S(1)} %get-tuple-element.49), channel_id=1, source_target_pairs={{0,1},{1,0},{2,3},{3,2},{4,5},{5,4},{6,7},{7,6},{8,9},{9,8},{10,11... | collective-permute-start | bytes 196616 | tf_op jit(solution)/shard_map/ppermute | solution.py:25
  1.5 6.7 %collective-permute-start.1 = (bf16[16,2048]{1,0:T(8,128)(2,1)S(1)}, bf16[16,2048]{1,0:T(8,128)(2,1)S(1)}, u32[]{:S(2)}, u32[]{:S(2)}) collective-permute-start(bf16[16,2048]{1,0:T(8,128)(2,1)S(1)} %get-tuple-element.51), channel_id=1, source_target_pairs={{0,2},{1,3},{2,0},{3,1},{4,6},{5,7},{6,4},{7,5},{8,10},{9,11},{10,... | collective-permute-start | bytes 196616 | tf_op jit(solution)/shard_map/ppermute | solution.py:25
  4.1 4.1 %collective-permute-start.2 = (bf16[16,2048]{1,0:T(8,128)(2,1)S(1)}, bf16[16,2048]{1,0:T(8,128)(2,1)S(1)}, u32[]{:S(2)}, u32[]{:S(2)}) collective-permute-start(bf16[16,2048]{1,0:T(8,128)(2,1)S(1)} %get-tuple-element.52), channel_id=1, source_target_pairs={{0,3},{1,2},{2,1},{3,0},{4,7},{5,6},{6,5},{7,4},{8,11},{9,10},{10,... | collective-permute-start | bytes 196616 | tf_op jit(solution)/shard_map/ppermute | solution.py:25
  6.4 29.6 %collective-permute-start.10 = (bf16[384,1536]{1,0:T(8,128)(2,1)}, bf16[384,1536]{1,0:T(8,128)(2,1)}, u32[]{:S(2)}, u32[]{:S(2)}) collective-permute-start(bf16[384,1536]{1,0:T(8,128)(2,1)} %get-tuple-element.70), channel_id=1, source_target_pairs={{0,2},{1,3},{2,0},{3,1},{4,6},{5,7},{6,4},{7,5},{8,10},{9,11},{10,... | collective-permute-start | bytes 3538952 | tf_op jit(solution)/shard_map/ppermute | solution.py:25
  8.6 17.0 %collective-permute-start.6 = (bf16[64,2048]{1,0:T(8,128)(2,1)S(1)}, bf16[64,2048]{1,0:T(8,128)(2,1)S(1)}, u32[]{:S(2)}, u32[]{:S(2)}) collective-permute-start(bf16[64,2048]{1,0:T(8,128)(2,1)S(1)} %shard_map.64.refs_0_), channel_id=1, source_target_pairs={{0,8},{4,12},{8,0},{12,4},{16,28},{20,24},{24,20},{28,16},{1,9},{5... | collective-permute-start | bytes 786440 | tf_op jit(solution)/shard_map/ppermute | solution.py:309
  11.2 3.4 %collective-permute-start.3 = (bf16[384,2048]{1,0:T(8,128)(2,1)S(1)}, bf16[384,2048]{1,0:T(8,128)(2,1)S(1)}, u32[]{:S(2)}, u32[]{:S(2)}) collective-permute-start(bf16[384,2048]{1,0:T(8,128)(2,1)S(1)} %copy-done), channel_id=1, source_target_pairs={{0,1},{1,0},{2,3},{3,2},{4,5},{5,4},{6,7},{7,6},{8,9},{9,8},{10,11... | collective-permute-start | bytes 4718600 | tf_op jit(solution)/shard_map/ppermute | solution.py:25
  11.3 3.4 %copy-start.1 = (bf16[1,64,512]{2,1,0:T(8,128)(2,1)S(1)}, bf16[1,64,512]{2,1,0:T(8,128)(2,1)}, u32[]{:S(2)}) copy-start(bf16[1,64,512]{2,1,0:T(8,128)(2,1)} %param.11) | copy-start | bytes 196612
  14.4 19.6 %copy-start.11 = (s32[1,384]{1,0:T(1,128)}, s32[1,384]{1,0:T(1,128)S(1)}, u32[]{:S(2)}) copy-start(s32[1,384]{1,0:T(1,128)S(1)} %get-tuple-element.71.stored_ref.refs_2_) | copy-start | bytes 4612
  14.7 15.7 %collective-permute-start.9 = (bf16[64,512]{1,0:T(8,128)(2,1)S(1)}, bf16[64,512]{1,0:T(8,128)(2,1)S(1)}, u32[]{:S(2)}, u32[]{:S(2)}) collective-permute-start(bf16[64,512]{1,0:T(8,128)(2,1)S(1)} %bitcast.18), channel_id=1, source_target_pairs={{0,8},{4,12},{8,0},{12,4},{16,28},{20,24},{24,20},{28,16},{1,9},{5... | collective-permute-start | bytes 196616 | tf_op jit(solution)/shard_map/ppermute | solution.py:309
  15.0 16.8 %collective-permute-start.8 = (bf16[64,512]{1,0:T(8,128)(2,1)S(1)}, bf16[64,512]{1,0:T(8,128)(2,1)S(1)}, u32[]{:S(2)}, u32[]{:S(2)}) collective-permute-start(bf16[64,512]{1,0:T(8,128)(2,1)S(1)} %bitcast.19), channel_id=1, source_target_pairs={{0,4},{4,0},{8,12},{12,8},{1,5},{5,1},{9,13},{13,9},{2,6},{6,2},{1... | collective-permute-start | bytes 196616 | tf_op jit(solution)/shard_map/ppermute | solution.py:25
  25.6 6.7 %collective-permute-start.7 = (bf16[64,2048]{1,0:T(8,128)(2,1)S(1)}, bf16[64,2048]{1,0:T(8,128)(2,1)S(1)}, u32[]{:S(2)}, u32[]{:S(2)}) collective-permute-start(bf16[64,2048]{1,0:T(8,128)(2,1)S(1)} %collective-permute-done.6.refs_2_), channel_id=1, source_target_pairs={{0,16},{16,0},{1,17},{17,1},{2,18},{18,2},{3,19},{19,3},{4,20},{20... | collective-permute-start | bytes 786440 | tf_op jit(solution)/shard_map/ppermute | solution.py:25
  25.6 7.0 %collective-permute-start.5 = (bf16[64,2048]{1,0:T(8,128)(2,1)S(1)}, bf16[64,2048]{1,0:T(8,128)(2,1)S(1)}, u32[]{:S(2)}, u32[]{:S(2)}) collective-permute-start(bf16[64,2048]{1,0:T(8,128)(2,1)S(1)} %shard_map.64.refs_0_), channel_id=1, source_target_pairs={{0,4},{4,0},{8,12},{12,8},{1,5},{5,1},{9,13},{13,9},{2,6},{6,2},{1... | collective-permute-start | bytes 786440 | tf_op jit(solution)/shard_map/ppermute | solution.py:25
  30.4 5.6 %copy-start.3 = (bf16[64,512]{1,0:T(8,128)(2,1)}, bf16[64,512]{1,0:T(8,128)(2,1)S(1)}, u32[]{:S(2)}) copy-start(bf16[64,512]{1,0:T(8,128)(2,1)S(1)} %collective-permute-done.9.refs_7_) | copy-start | bytes 196612
  30.4 14.4 %collective-permute-start.4 = (bf16[384,512]{1,0:T(8,128)(2,1)}, bf16[384,512]{1,0:T(8,128)(2,1)}, u32[]{:S(2)}, u32[]{:S(2)}) collective-permute-start(bf16[384,512]{1,0:T(8,128)(2,1)} %get-tuple-element.59), channel_id=1, source_target_pairs={{0,2},{1,3},{2,0},{3,1},{4,6},{5,7},{6,4},{7,5},{8,10},{9,11},{10,... | collective-permute-start | bytes 1179656 | tf_op jit(solution)/shard_map/ppermute | solution.py:25
  31.8 4.1 %copy-start.5 = (bf16[64,512]{1,0:T(8,128)(2,1)}, bf16[64,512]{1,0:T(8,128)(2,1)S(1)}, u32[]{:S(2)}) copy-start(bf16[64,512]{1,0:T(8,128)(2,1)S(1)} %collective-permute-done.8.refs_6_) | copy-start | bytes 196612
  32.6 4.3 %collective-permute-start.11 = (bf16[64,512]{1,0:T(8,128)(2,1)S(1)}, bf16[64,512]{1,0:T(8,128)(2,1)S(1)}, u32[]{:S(2)}, u32[]{:S(2)}) collective-permute-start(bf16[64,512]{1,0:T(8,128)(2,1)S(1)} %collective-permute-done.9.refs_7_), channel_id=1, source_target_pairs={{0,16},{16,0},{1,17},{17,1},{2,18},{18,2},{3,19},{19,3},{4,20},{20... | collective-permute-start | bytes 196616 | tf_op jit(solution)/shard_map/ppermute | solution.py:25
  37.5 2.8 %collective-permute-start.13 = (f32[64,384]{1,0:T(8,128)S(1)}, f32[64,384]{1,0:T(8,128)S(1)}, u32[]{:S(2)}, u32[]{:S(2)}) collective-permute-start(f32[64,384]{1,0:T(8,128)S(1)} %shard_map.68), channel_id=1, source_target_pairs={{0,1},{1,0},{2,3},{3,2},{4,5},{5,4},{6,7},{7,6},{8,9},{9,8},{10,11... | collective-permute-start | bytes 294920 | tf_op jit(solution)/shard_map/ppermute | solution.py:25
  37.5 5.1 %collective-permute-start.12 = (bf16[384,1536]{1,0:T(8,128)(2,1)}, bf16[384,1536]{1,0:T(8,128)(2,1)S(1)}, u32[]{:S(2)}, u32[]{:S(2)}) collective-permute-start(bf16[384,1536]{1,0:T(8,128)(2,1)} %collective-permute-done.10.refs_0_), channel_id=1, source_target_pairs={{0,1},{1,0},{2,3},{3,2},{4,5},{5,4},{6,7},{7,6},{8,9},{9,8},{10,11... | collective-permute-start | bytes 3538952 | tf_op jit(solution)/shard_map/ppermute | solution.py:25
  40.9 5.5 %collective-permute-start.15 = (bf16[64,384]{1,0:T(8,128)(2,1)}, bf16[64,384]{1,0:T(8,128)(2,1)}, u32[]{:S(2)}, u32[]{:S(2)}) collective-permute-start(bf16[64,384]{1,0:T(8,128)(2,1)} %get-tuple-element.91), channel_id=1, source_target_pairs={{0,2},{1,3},{2,0},{3,1},{4,6},{5,7},{6,4},{7,5},{8,10},{9,11},{10,... | collective-permute-start | bytes 147464 | tf_op jit(solution)/shard_map/ppermute | solution.py:25
  44.7 2.1 %copy-start.2 = (bf16[1,64,512]{2,1,0:T(8,128)(2,1)S(1)}, bf16[1,64,512]{2,1,0:T(8,128)(2,1)}, u32[]{:S(2)}) copy-start(bf16[1,64,512]{2,1,0:T(8,128)(2,1)} %param.11) | copy-start | bytes 196612
  44.8 2.0 %collective-permute-start.14 = (bf16[384,512]{1,0:T(8,128)(2,1)}, bf16[384,512]{1,0:T(8,128)(2,1)S(1)}, u32[]{:S(2)}, u32[]{:S(2)}) collective-permute-start(bf16[384,512]{1,0:T(8,128)(2,1)} %collective-permute-done.4.refs_0_), channel_id=1, source_target_pairs={{0,1},{1,0},{2,3},{3,2},{4,5},{5,4},{6,7},{7,6},{8,9},{9,8},{10,11... | collective-permute-start | bytes 1179656 | tf_op jit(solution)/shard_map/ppermute | solution.py:25
  (5 other events, 8.8 us)

commit v15 on v13

--- a/solution.py
+++ b/solution.py
@@ -90,13 +90,13 @@
 
 def start_tiles(tile, depth, places, features, weight_ref, held_ref, rows_ref, sems):
     me, t = lax.axis_index("tensor"), 0
-    for (flip, first), part in zip(places, features):
-        for k in range(0, part.shape[1], tile):
+    for (flip, first, skip, width), part in zip(places, features):
+        for k in range(0, width, tile):
             start = pl.multiple_of((me ^ flip) * depth + first + k, LANES)
             pltpu.make_async_copy(
                 weight_ref.at[pl.ds(start, tile)], rows_ref.at[t], sems.at[1, t]
             ).start()
-            pltpu.make_async_copy(part.at[:, pl.ds(k, tile)], held_ref.at[t], sems.at[0, t]).start()
+            pltpu.make_async_copy(part.at[:, pl.ds(skip + k, tile)], held_ref.at[t], sems.at[0, t]).start()
             t += 1
 
 
@@ -108,9 +108,8 @@
         total_ref[...] += jnp.dot(held_ref[t], rows_ref[t], preferred_element_type=jnp.float32)
 
 
-def tile_scratch(tile, features, columns):
-    tiles = sum(f.shape[1] for f in features) // tile
-    rows = features[0].shape[0]
+def tile_scratch(tile, rows, places, columns):
+    tiles = sum(place[3] for place in places) // tile
     return [
         pltpu.VMEM((tiles, rows, tile), jnp.bfloat16),
         pltpu.VMEM((tiles, tile, columns), jnp.bfloat16),
@@ -243,6 +242,7 @@
                 pltpu.SemaphoreType.DMA((len(edges), steps)),
             ],
             [ANYWHERE] * (len(edges) - 1),
+            cost=FREE,
             mib=56,
         )(uncut)
     )
@@ -276,17 +276,17 @@
         return [flipped(value, "tensor", 1) for value in far[m]]
 
     def far_places(m):
-        return [(hop, edges[m]) for hop in hops]
+        return [(hop, edges[m], 0, edges[m + 1] - edges[m]) for hop in hops]
 
     def near_places(m):
-        return [(hop ^ 1, edges[m]) for hop in hops]
+        return [(hop ^ 1, edges[m], 0, edges[m + 1] - edges[m]) for hop in hops]
 
     def products(places, features, total):
         return call(
             functools.partial(products_kernel, tile, depth, places),
             jax.ShapeDtypeStruct((rows, columns), jnp.float32),
             [ANYWHERE] + [ANYWHERE] * len(features) + [VECTOR],
-            tile_scratch(tile, features, columns),
+            tile_scratch(tile, rows, places, columns),
         )(frozen_projection_weight, *features, total)
 
     flips = list(range(1, groups))
@@ -310,14 +310,15 @@
 
     own, here = chained(own, tokens)
     fetched = fetch_far(own)
+    places = [(0, 0, 0, depth // 2)]
     total, stored = call(
-        functools.partial(first_kernel, tile, depth, [(0, 0)], slots),
+        functools.partial(first_kernel, tile, depth, places, slots),
         [
             jax.ShapeDtypeStruct((rows, columns), jnp.float32),
             jax.ShapeDtypeStruct((1, rows), jnp.int32),
         ],
         [SCALAR, VECTOR, ANYWHERE, ANYWHERE],
-        tile_scratch(tile, [tokens], columns),
+        tile_scratch(tile, rows, places, columns),
         [VECTOR, VECTOR],
     )(placement, tenant.reshape(1, rows), frozen_projection_weight, here)
     total, own, up, neighbour, chunks[1] = chained(
@@ -325,11 +326,14 @@
     )
     far.append(send(1))
     single, single_up = fetch_near(own), fetch_near(up)
-    fetched, total = chained(fetched, total)
+    total = products([(0, depth // 2, depth // 2, depth // 2)], [here], total)
+    fetched, single_up, total, up = chained(fetched, single_up, total, up)
     swapped = swap(fetched)
     fetched_up = fetch_far(up)
     total, neighbour = chained(total, neighbour)
-    total = products([(1, 0)], [neighbour], total)
+    total = products([(1, 0, 0, depth)], [neighbour], total)
+    fetched_up, total = chained(fetched_up, total)
+    swapped_up = swap(fetched_up)
     single, swapped, total = chained(single, swapped, total)
     downs = [own] + single
     for pair in zip(fetched, swapped):
@@ -347,9 +351,9 @@
             pltpu.SemaphoreType.DMA((1 + slots, tiles)),
         ],
     )(tokens, stored, *downs)
-    far[0], fetched_up, partial = chained(far[0], fetched_up, partial)
+    far[0], partial = chained(far[0], partial)
     ups = [up] + single_up
-    for pair in zip(fetched_up, swap(fetched_up)):
+    for pair in zip(fetched_up, swapped_up):
         ups += pair
     near = across(0)
     total = products(far_places(0), far[0], total)
@@ -368,8 +372,9 @@
     total = products(far_places(1), far[1], total)
     near, more, total = chained(near, more, total)
 
+    places = near_places(1)
     return call(
-        functools.partial(last_kernel, tile, depth, near_places(1), flips, pairs, slots),
+        functools.partial(last_kernel, tile, depth, places, flips, pairs, slots),
         jax.ShapeDtypeStruct((rows, columns), jnp.bfloat16),
         [ANYWHERE] + [ANYWHERE] * len(near) + [VECTOR] * 2 + [ANYWHERE] * (2 + slots),
         [
@@ -378,7 +383,7 @@
             pltpu.VMEM((rank, rows), jnp.bfloat16),
             pltpu.VMEM((slots * rank, columns), jnp.bfloat16),
         ]
-        + tile_scratch(tile, near, columns)
+        + tile_scratch(tile, rows, places, columns)
         + [pltpu.SemaphoreType.DMA((2 + slots,))],
     )(frozen_projection_weight, *near, total, stored, partial, more, *ups)
 

time: 49.5 us -> 49.4 us (level)
  starting transfers between devices: 16.9 us -> 14.5 us
  Pallas kernels: 18.9 us -> 21 us
    ppermute x14, starting transfers between devices: 13.9 us -> 11.8 us  [flipped(): return lax.ppermute(value, axis, [(i, i ^ flip) for i in range(count)])]
    pallas_call x4 -> x5, Pallas kernels: 8.68 us -> 10.5 us  [products(): call(functools.partial(products_kernel, tile, depth, places), jax.ShapeDt...]
    ppermute x2, waiting for transfers between devices: 8.99 us -> 7.69 us  [fetch_far(): lax.ppermute(value, ('parts', 'adapter'), route)]
    ppermute x14, waiting for transfers between devices: 2.54 us -> 3.57 us  [flipped(): return lax.ppermute(value, axis, [(i, i ^ flip) for i in range(count)])]
    pallas_call x2, Pallas kernels: 5.7 us -> 5.06 us  [the longest x1 2.69 us: body(): call(functools.partial(last_kernel, tile, depth, places, flips, pairs, sl...]
    pallas_call x1, Pallas kernels: 1.88 us -> 2.46 us  [body(): call(functools.partial(shrink_kernel, tile, flips, pairs, slots), jax.Sha...]
  transfers between devices with their start and end apart: 16 -> 16, of which waited for: 4 -> 6; matrix products, arithmetic and copies ran while one was open for 1% -> 1% of each run, Pallas kernels for 33% -> 38%
where the time goes in v15:
time: 49.4 us; the launch traced here: 48.7 us
  Pallas kernels  21 us (43%)
  starting transfers between devices  14.5 us (29%)
  waiting for transfers between devices  11.3 us (23%)
  local copies, waits for them, and re-layouts  1.11 us (2%)
  other arithmetic  0.63 us (1%)
    ppermute x14, starting transfers between devices, flipped(): return lax.ppermute(value, axis, [(i, i ^ flip) for i in range(count)])  11.8 us
    pallas_call x5, Pallas kernels, products(): call(functools.partial(products_kernel, tile, depth, places), jax.ShapeDt...  10.5 us
    ppermute x2, waiting for transfers between devices, fetch_far(): lax.ppermute(value, ('parts', 'adapter'), route)  7.69 us
    ppermute x14, waiting for transfers between devices, flipped(): return lax.ppermute(value, axis, [(i, i ^ flip) for i in range(count)])  3.57 us
    pallas_call x1, Pallas kernels, body(): call(functools.partial(last_kernel, tile, depth, places, flips, pairs, sl...  2.69 us
    ppermute x2, starting transfers between devices, fetch_far(): lax.ppermute(value, ('parts', 'adapter'), route)  2.66 us
    pallas_call x1, Pallas kernels, body(): call(functools.partial(shrink_kernel, tile, flips, pairs, slots), jax.Sha...  2.46 us
    pallas_call x1, Pallas kernels, body(): call(functools.partial(first_kernel, tile, depth, places, slots), [jax.Sh...  2.37 us
  transfers between devices with their start and end apart: 16, of which 6 were waited for; matrix products, arithmetic and copies ran while one was open for 1% of the time, Pallas kernels for 38%

profile of v15, /device:TPU:0, one launch (start us, length us, event | category | flops | bytes accessed | tf_op | source)
XLA Modules:
  0.0 48.7 jit_solution(449662984997208369)
XLA Ops:
  0.0 1.1 %dynamic-slice_bitcast_fusion = (bf16[16,2048]{1,0:T(8,128)(2,1)S(1)}, bf16[16,2048]{1,0:T(8,128)(2,1)S(1)}, bf16[16,2048]{1,0:T(8,128)(2,1)S(1)}, bf16[16,2048]{1,0:T(8,128)(2,1)S(1)}) fusion(bf16[1,8192,16]{1,2,0:T(8,128)(2,1)} %param.10, s32[]{:T(128)S(6)} %select_n.15, s32[]{:T(128)S(6)} %select_n.13, s32[]{:T(128)S(6)} %select_n.12, s32[]{:T(128)S(6)} %select_n.14), kind=kLoop, calls=%fused_computation | loop fusion | bytes 524304 | tf_op jit(solution)/shard_map/dynamic_slice | solution.py:230
  1.1 0.5 %collective-permute-start = (bf16[16,2048]{1,0:T(8,128)(2,1)S(1)}, bf16[16,2048]{1,0:T(8,128)(2,1)S(1)}, u32[]{:S(2)}, u32[]{:S(2)}) collective-permute-start(bf16[16,2048]{1,0:T(8,128)(2,1)S(1)} %get-tuple-element.50), channel_id=1, source_target_pairs={{0,1},{1,0},{2,3},{3,2},{4,5},{5,4},{6,7},{7,6},{8,9},{9,8},{10,11... | collective-permute-start | bytes 196616 | tf_op jit(solution)/shard_map/ppermute | solution.py:25
  1.6 2.6 %collective-permute-start.1 = (bf16[16,2048]{1,0:T(8,128)(2,1)S(1)}, bf16[16,2048]{1,0:T(8,128)(2,1)S(1)}, u32[]{:S(2)}, u32[]{:S(2)}) collective-permute-start(bf16[16,2048]{1,0:T(8,128)(2,1)S(1)} %get-tuple-element.52), channel_id=1, source_target_pairs={{0,2},{1,3},{2,0},{3,1},{4,6},{5,7},{6,4},{7,5},{8,10},{9,11},{10,... | collective-permute-start | bytes 196616 | tf_op jit(solution)/shard_map/ppermute | solution.py:25
  4.3 2.2 %shard_map.66 = (bf16[384,1536]{1,0:T(8,128)(2,1)}, bf16[384,512]{1,0:T(8,128)(2,1)}) custom-call(bf16[384,2048]{1,0:T(8,128)(2,1)} %tokens_ref.1), custom_call_target="tpu_custom_call" | custom-call | tf_op jit(solution)/shard_map/pallas_call | solution.py:236
  6.5 1.8 %collective-permute-start.9 = (bf16[384,1536]{1,0:T(8,128)(2,1)}, bf16[384,1536]{1,0:T(8,128)(2,1)}, u32[]{:S(2)}, u32[]{:S(2)}) collective-permute-start(bf16[384,1536]{1,0:T(8,128)(2,1)} %get-tuple-element.70), channel_id=1, source_target_pairs={{0,2},{1,3},{2,0},{3,1},{4,6},{5,7},{6,4},{7,5},{8,10},{9,11},{10,... | collective-permute-start | bytes 3538952 | tf_op jit(solution)/shard_map/ppermute | solution.py:25
  8.4 0.7 %shard_map.64.refs_0_ = bf16[64,2048]{1,0:T(8,128)(2,1)} custom-call(bf16[16,2048]{1,0:T(8,128)(2,1)S(1)} %get-tuple-element.49.refs_0_, bf16[16,2048]{1,0:T(8,128)(2,1)S(1)} %collective-permute-done.refs_1_, bf16[16,2048]{1,0:T(8,128)(2,1)S(1)} %collective-permute-done.1.refs_2_, bf16[16,2048]{1,0:T(8,128)(2,1)S(1)} %collective-permute-done.2.refs_3_), custom_call_target="tpu_custom_call" | custom-call | tf_op jit(solution)/shard_map/pallas_call | solution.py:253
  9.1 2.7 %collective-permute-start.5 = (bf16[64,2048]{1,0:T(8,128)(2,1)}, bf16[64,2048]{1,0:T(8,128)(2,1)}, u32[]{:S(2)}, u32[]{:S(2)}) collective-permute-start(bf16[64,2048]{1,0:T(8,128)(2,1)} %shard_map.64.refs_0_), channel_id=1, source_target_pairs={{0,8},{4,12},{8,0},{12,4},{16,28},{20,24},{24,20},{28,16},{1,9},{5... | collective-permute-start | bytes 786440 | tf_op jit(solution)/shard_map/ppermute | solution.py:303
  11.8 2.4 %shard_map.65 = (f32[384,512]{1,0:T(8,128)S(1)}, s32[1,384]{1,0:T(1,128)S(1)}) custom-call(s32[4]{0:T(128)S(1)} %copy-done.6, s32[1,384]{1,0:T(1,128)S(1)} %bitcast.21, bf16[8192,512]{1,0:T(8,128)(2,1)} %weight_ref.13, bf16[384,2048]{1,0:T(8,128)(2,1)S(1)} %copy-done), custom_call_target="tpu_custom_call" | custom-call | flops 99999997952 | tf_op jit(solution)/shard_map/pallas_call | solution.py:314
  14.2 1.6 %collective-permute-start.6 = (bf16[64,512]{1,0:T(8,128)(2,1)S(1)}, bf16[64,512]{1,0:T(8,128)(2,1)S(1)}, u32[]{:S(2)}, u32[]{:S(2)}) collective-permute-start(bf16[64,512]{1,0:T(8,128)(2,1)S(1)} %bitcast.18), channel_id=1, source_target_pairs={{0,4},{4,0},{8,12},{12,8},{1,5},{5,1},{9,13},{13,9},{2,6},{6,2},{1... | collective-permute-start | bytes 196616 | tf_op jit(solution)/shard_map/ppermute | solution.py:25
  15.8 1.8 %shard_map.67.refs_1_ = f32[384,512]{1,0:T(8,128)S(1)} custom-call(bf16[8192,512]{1,0:T(8,128)(2,1)} %weight_ref.13, bf16[384,2048]{1,0:T(8,128)(2,1)S(1)} %copy-done, f32[384,512]{1,0:T(8,128)S(1)} %get-tuple-element.62.refs_1_), custom_call_target="tpu_custom_call" | custom-call | flops 99999997952 | tf_op jit(solution)/shard_map/pallas_call | solution.py:285
  18.2 1.2 %collective-permute-start.4 = (bf16[384,512]{1,0:T(8,128)(2,1)}, bf16[384,512]{1,0:T(8,128)(2,1)}, u32[]{:S(2)}, u32[]{:S(2)}) collective-permute-start(bf16[384,512]{1,0:T(8,128)(2,1)} %get-tuple-element.60), channel_id=1, source_target_pairs={{0,2},{1,3},{2,0},{3,1},{4,6},{5,7},{6,4},{7,5},{8,10},{9,11},{10,... | collective-permute-start | bytes 1179656 | tf_op jit(solution)/shard_map/ppermute | solution.py:25
  19.4 5.4 %collective-permute-done.5.refs_2_ = bf16[64,2048]{1,0:T(8,128)(2,1)} collective-permute-done((bf16[64,2048]{1,0:T(8,128)(2,1)}, bf16[64,2048]{1,0:T(8,128)(2,1)}, u32[]{:S(2)}, u32[]{:S(2)}) %collective-permute-start.5) | collective-permute-done | bytes 262176 | tf_op jit(solution)/shard_map/ppermute | solution.py:303
  24.8 1.8 %collective-permute-start.11 = (bf16[64,2048]{1,0:T(8,128)(2,1)}, bf16[64,2048]{1,0:T(8,128)(2,1)S(1)}, u32[]{:S(2)}, u32[]{:S(2)}) collective-permute-start(bf16[64,2048]{1,0:T(8,128)(2,1)} %collective-permute-done.5.refs_2_), channel_id=1, source_target_pairs={{0,16},{16,0},{1,17},{17,1},{2,18},{18,2},{3,19},{19,3},{4,20},{20... | collective-permute-start | bytes 786440 | tf_op jit(solution)/shard_map/ppermute | solution.py:25
  26.5 2.6 %shard_map.68.refs_1_ = f32[384,512]{1,0:T(8,128)S(1)} custom-call(bf16[8192,512]{1,0:T(8,128)(2,1)} %weight_ref.13, bf16[384,2048]{1,0:T(8,128)(2,1)S(1)} %collective-permute-done.3.refs_0_, f32[384,512]{1,0:T(8,128)S(1)} %shard_map.67.refs_1_), custom_call_target="tpu_custom_call" | custom-call | flops 99999997952 | tf_op jit(solution)/shard_map/pallas_call | solution.py:285
  29.1 2.3 %collective-permute-done.7.refs_7_ = bf16[64,512]{1,0:T(8,128)(2,1)} collective-permute-done((bf16[64,512]{1,0:T(8,128)(2,1)S(1)}, bf16[64,512]{1,0:T(8,128)(2,1)}, u32[]{:S(2)}, u32[]{:S(2)}) %collective-permute-start.7) | collective-permute-done | bytes 65568 | tf_op jit(solution)/shard_map/ppermute | solution.py:303
  31.6 2.2 %collective-permute-done.11.refs_3_ = bf16[64,2048]{1,0:T(8,128)(2,1)S(1)} collective-permute-done((bf16[64,2048]{1,0:T(8,128)(2,1)}, bf16[64,2048]{1,0:T(8,128)(2,1)S(1)}, u32[]{:S(2)}, u32[]{:S(2)}) %collective-permute-start.11) | collective-permute-done | bytes 262176 | tf_op jit(solution)/shard_map/ppermute | solution.py:25
  33.7 2.5 %shard_map.69 = f32[64,384]{1,0:T(8,128)S(1)} custom-call(bf16[384,2048]{1,0:T(8,128)(2,1)S(1)} %copy-done, s32[1,384]{1,0:T(1,128)S(1)} %get-tuple-element.71.stored_ref.refs_2_, bf16[64,2048]{1,0:T(8,128)(2,1)} %shard_map.64.refs_0_, bf16[64,2048]{1,0:T(8,128)(2,1)S(1)} %collective-permute-done.10.refs_1_, ...), custom_call_target="tpu_custom_call" | custom-call | flops 99999997952 | tf_op jit(solution)/shard_map/pallas_call | solution.py:343
  36.8 2.3 %shard_map.70.refs_1_ = f32[384,512]{1,0:T(8,128)S(1)} custom-call(bf16[8192,512]{1,0:T(8,128)(2,1)} %weight_ref.13, bf16[384,1536]{1,0:T(8,128)(2,1)} %collective-permute-done.9.refs_0_, f32[384,512]{1,0:T(8,128)S(1)} %shard_map.68.refs_1_), custom_call_target="tpu_custom_call" | custom-call | flops 99999997952 | tf_op jit(solution)/shard_map/pallas_call | solution.py:285
  39.1 0.6 %fusion = (bf16[64,384]{1,0:T(8,128)(2,1)}, f32[64,384]{1,0:T(8,128)S(1)}) fusion(f32[64,384]{1,0:T(8,128)S(1)} %shard_map.69, f32[64,384]{1,0:T(8,128)S(1)} %collective-permute-done.13), kind=kLoop, calls=%fused_computation.4 | loop fusion | flops 49152 | bytes 344064 | tf_op jit(solution)/shard_map/convert_element_type | solution.py:367
  39.8 1.1 %collective-permute-start.15 = (bf16[64,384]{1,0:T(8,128)(2,1)}, bf16[64,384]{1,0:T(8,128)(2,1)}, u32[]{:S(2)}, u32[]{:S(2)}) collective-permute-start(bf16[64,384]{1,0:T(8,128)(2,1)} %get-tuple-element.93), channel_id=1, source_target_pairs={{0,2},{1,3},{2,0},{3,1},{4,6},{5,7},{6,4},{7,5},{8,10},{9,11},{10,... | collective-permute-start | bytes 147464 | tf_op jit(solution)/shard_map/ppermute | solution.py:25
  40.9 2.2 %shard_map.71.refs_1_ = f32[384,512]{1,0:T(8,128)S(1)} custom-call(bf16[8192,512]{1,0:T(8,128)(2,1)} %weight_ref.13, bf16[384,1536]{1,0:T(8,128)(2,1)S(1)} %collective-permute-done.12.refs_0_, f32[384,512]{1,0:T(8,128)S(1)} %shard_map.70.refs_1_), custom_call_target="tpu_custom_call" | custom-call | flops 99999997952 | tf_op jit(solution)/shard_map/pallas_call | solution.py:285
  43.1 0.9 %collective-permute-done.4.refs_0_ = bf16[384,512]{1,0:T(8,128)(2,1)} collective-permute-done((bf16[384,512]{1,0:T(8,128)(2,1)}, bf16[384,512]{1,0:T(8,128)(2,1)}, u32[]{:S(2)}, u32[]{:S(2)}) %collective-permute-start.4) | collective-permute-done | bytes 393248 | tf_op jit(solution)/shard_map/ppermute | solution.py:25
  44.0 1.6 %shard_map.72.refs_1_ = f32[384,512]{1,0:T(8,128)S(1)} custom-call(bf16[8192,512]{1,0:T(8,128)(2,1)} %weight_ref.13, bf16[384,512]{1,0:T(8,128)(2,1)} %collective-permute-done.4.refs_0_, f32[384,512]{1,0:T(8,128)S(1)} %shard_map.71.refs_1_), custom_call_target="tpu_custom_call" | custom-call | flops 99999997952 | tf_op jit(solution)/shard_map/pallas_call | solution.py:285
  46.0 2.7 %shard_map.73 = bf16[384,512]{1,0:T(8,128)(2,1)} custom-call(bf16[8192,512]{1,0:T(8,128)(2,1)} %weight_ref.13, bf16[384,512]{1,0:T(8,128)(2,1)S(1)} %collective-permute-done.14.refs_0_, f32[384,512]{1,0:T(8,128)S(1)} %shard_map.72.refs_1_, s32[1,384]{1,0:T(1,128)S(1)} %copy-done.8, f32[64,384]{1,0:T(8,128)S(1)} %get-tuple-element.87.refs_3_, ...), custom_call_target="tpu_custom_call" | custom-call | flops 99999997952 | tf_op jit(solution)/shard_map/pallas_call | solution.py:376
  (38 shorter events, 1.8 us)
Async XLA Ops:
  0.0 8.3 %copy-start = (bf16[384,2048]{1,0:T(8,128)(2,1)S(1)}, bf16[384,2048]{1,0:T(8,128)(2,1)}, u32[]{:S(2)}) copy-start(bf16[384,2048]{1,0:T(8,128)(2,1)} %tokens_ref.1) | copy-start | bytes 4718596
  0.0 11.8 %copy-start.5 = (s32[384,1]{0,1:T(1,128)S(1)}, s32[384,1]{0,1:T(1,128)}, u32[]{:S(2)}) copy-start(s32[384,1]{0,1:T(1,128)} %param.7) | copy-start | bytes 4612
  0.0 11.8 %copy-start.6 = (s32[4]{0:T(128)S(1)}, s32[4]{0:T(128)}, u32[]{:S(2)}) copy-start(s32[4]{0:T(128)} %placement_ref.1) | copy-start | bytes 52
  1.1 7.2 %collective-permute-start = (bf16[16,2048]{1,0:T(8,128)(2,1)S(1)}, bf16[16,2048]{1,0:T(8,128)(2,1)S(1)}, u32[]{:S(2)}, u32[]{:S(2)}) collective-permute-start(bf16[16,2048]{1,0:T(8,128)(2,1)S(1)} %get-tuple-element.50), channel_id=1, source_target_pairs={{0,1},{1,0},{2,3},{3,2},{4,5},{5,4},{6,7},{7,6},{8,9},{9,8},{10,11... | collective-permute-start | bytes 196616 | tf_op jit(solution)/shard_map/ppermute | solution.py:25
  1.6 6.7 %collective-permute-start.1 = (bf16[16,2048]{1,0:T(8,128)(2,1)S(1)}, bf16[16,2048]{1,0:T(8,128)(2,1)S(1)}, u32[]{:S(2)}, u32[]{:S(2)}) collective-permute-start(bf16[16,2048]{1,0:T(8,128)(2,1)S(1)} %get-tuple-element.52), channel_id=1, source_target_pairs={{0,2},{1,3},{2,0},{3,1},{4,6},{5,7},{6,4},{7,5},{8,10},{9,11},{10,... | collective-permute-start | bytes 196616 | tf_op jit(solution)/shard_map/ppermute | solution.py:25
  4.2 4.2 %collective-permute-start.2 = (bf16[16,2048]{1,0:T(8,128)(2,1)S(1)}, bf16[16,2048]{1,0:T(8,128)(2,1)S(1)}, u32[]{:S(2)}, u32[]{:S(2)}) collective-permute-start(bf16[16,2048]{1,0:T(8,128)(2,1)S(1)} %get-tuple-element.53), channel_id=1, source_target_pairs={{0,3},{1,2},{2,1},{3,0},{4,7},{5,6},{6,5},{7,4},{8,11},{9,10},{10,... | collective-permute-start | bytes 196616 | tf_op jit(solution)/shard_map/ppermute | solution.py:25
  6.5 29.7 %collective-permute-start.9 = (bf16[384,1536]{1,0:T(8,128)(2,1)}, bf16[384,1536]{1,0:T(8,128)(2,1)}, u32[]{:S(2)}, u32[]{:S(2)}) collective-permute-start(bf16[384,1536]{1,0:T(8,128)(2,1)} %get-tuple-element.70), channel_id=1, source_target_pairs={{0,2},{1,3},{2,0},{3,1},{4,6},{5,7},{6,4},{7,5},{8,10},{9,11},{10,... | collective-permute-start | bytes 3538952 | tf_op jit(solution)/shard_map/ppermute | solution.py:25
  8.3 5.9 %collective-permute-start.3 = (bf16[384,2048]{1,0:T(8,128)(2,1)S(1)}, bf16[384,2048]{1,0:T(8,128)(2,1)S(1)}, u32[]{:S(2)}, u32[]{:S(2)}) collective-permute-start(bf16[384,2048]{1,0:T(8,128)(2,1)S(1)} %copy-done), channel_id=1, source_target_pairs={{0,1},{1,0},{2,3},{3,2},{4,5},{5,4},{6,7},{7,6},{8,9},{9,8},{10,11... | collective-permute-start | bytes 4718600 | tf_op jit(solution)/shard_map/ppermute | solution.py:25
  9.1 15.7 %collective-permute-start.5 = (bf16[64,2048]{1,0:T(8,128)(2,1)}, bf16[64,2048]{1,0:T(8,128)(2,1)}, u32[]{:S(2)}, u32[]{:S(2)}) collective-permute-start(bf16[64,2048]{1,0:T(8,128)(2,1)} %shard_map.64.refs_0_), channel_id=1, source_target_pairs={{0,8},{4,12},{8,0},{12,4},{16,28},{20,24},{24,20},{28,16},{1,9},{5... | collective-permute-start | bytes 786440 | tf_op jit(solution)/shard_map/ppermute | solution.py:303
  14.2 19.6 %copy-start.7 = (s32[1,384]{1,0:T(1,128)}, s32[1,384]{1,0:T(1,128)S(1)}, u32[]{:S(2)}) copy-start(s32[1,384]{1,0:T(1,128)S(1)} %get-tuple-element.71.stored_ref.refs_2_) | copy-start | bytes 4612
  14.2 10.6 %collective-permute-start.6 = (bf16[64,512]{1,0:T(8,128)(2,1)S(1)}, bf16[64,512]{1,0:T(8,128)(2,1)S(1)}, u32[]{:S(2)}, u32[]{:S(2)}) collective-permute-start(bf16[64,512]{1,0:T(8,128)(2,1)S(1)} %bitcast.18), channel_id=1, source_target_pairs={{0,4},{4,0},{8,12},{12,8},{1,5},{5,1},{9,13},{13,9},{2,6},{6,2},{1... | collective-permute-start | bytes 196616 | tf_op jit(solution)/shard_map/ppermute | solution.py:25
  17.6 13.9 %collective-permute-start.10 = (bf16[64,2048]{1,0:T(8,128)(2,1)}, bf16[64,2048]{1,0:T(8,128)(2,1)S(1)}, u32[]{:S(2)}, u32[]{:S(2)}) collective-permute-start(bf16[64,2048]{1,0:T(8,128)(2,1)} %shard_map.64.refs_0_), channel_id=1, source_target_pairs={{0,4},{4,0},{8,12},{12,8},{1,5},{5,1},{9,13},{13,9},{2,6},{6,2},{1... | collective-permute-start | bytes 786440 | tf_op jit(solution)/shard_map/ppermute | solution.py:25
  18.2 25.9 %collective-permute-start.4 = (bf16[384,512]{1,0:T(8,128)(2,1)}, bf16[384,512]{1,0:T(8,128)(2,1)}, u32[]{:S(2)}, u32[]{:S(2)}) collective-permute-start(bf16[384,512]{1,0:T(8,128)(2,1)} %get-tuple-element.60), channel_id=1, source_target_pairs={{0,2},{1,3},{2,0},{3,1},{4,6},{5,7},{6,4},{7,5},{8,10},{9,11},{10,... | collective-permute-start | bytes 1179656 | tf_op jit(solution)/shard_map/ppermute | solution.py:25
  24.8 4.4 %copy-start.3 = (bf16[64,512]{1,0:T(8,128)(2,1)}, bf16[64,512]{1,0:T(8,128)(2,1)S(1)}, u32[]{:S(2)}) copy-start(bf16[64,512]{1,0:T(8,128)(2,1)S(1)} %collective-permute-done.6.refs_6_) | copy-start | bytes 196612
  24.8 6.7 %collective-permute-start.7 = (bf16[64,512]{1,0:T(8,128)(2,1)S(1)}, bf16[64,512]{1,0:T(8,128)(2,1)}, u32[]{:S(2)}, u32[]{:S(2)}) collective-permute-start(bf16[64,512]{1,0:T(8,128)(2,1)S(1)} %bitcast.19), channel_id=1, source_target_pairs={{0,8},{4,12},{8,0},{12,4},{16,28},{20,24},{24,20},{28,16},{1,9},{5... | collective-permute-start | bytes 196616 | tf_op jit(solution)/shard_map/ppermute | solution.py:303
  24.8 8.9 %collective-permute-start.11 = (bf16[64,2048]{1,0:T(8,128)(2,1)}, bf16[64,2048]{1,0:T(8,128)(2,1)S(1)}, u32[]{:S(2)}, u32[]{:S(2)}) collective-permute-start(bf16[64,2048]{1,0:T(8,128)(2,1)} %collective-permute-done.5.refs_2_), channel_id=1, source_target_pairs={{0,16},{16,0},{1,17},{17,1},{2,18},{18,2},{3,19},{19,3},{4,20},{20... | collective-permute-start | bytes 786440 | tf_op jit(solution)/shard_map/ppermute | solution.py:25
  31.4 11.7 %collective-permute-start.8 = (bf16[64,512]{1,0:T(8,128)(2,1)}, bf16[64,512]{1,0:T(8,128)(2,1)}, u32[]{:S(2)}, u32[]{:S(2)}) collective-permute-start(bf16[64,512]{1,0:T(8,128)(2,1)} %collective-permute-done.7.refs_7_), channel_id=1, source_target_pairs={{0,16},{16,0},{1,17},{17,1},{2,18},{18,2},{3,19},{19,3},{4,20},{20... | collective-permute-start | bytes 196616 | tf_op jit(solution)/shard_map/ppermute | solution.py:25
  36.2 2.9 %collective-permute-start.13 = (f32[64,384]{1,0:T(8,128)S(1)}, f32[64,384]{1,0:T(8,128)S(1)}, u32[]{:S(2)}, u32[]{:S(2)}) collective-permute-start(f32[64,384]{1,0:T(8,128)S(1)} %shard_map.69), channel_id=1, source_target_pairs={{0,1},{1,0},{2,3},{3,2},{4,5},{5,4},{6,7},{7,6},{8,9},{9,8},{10,11... | collective-permute-start | bytes 294920 | tf_op jit(solution)/shard_map/ppermute | solution.py:25
  36.3 4.6 %collective-permute-start.12 = (bf16[384,1536]{1,0:T(8,128)(2,1)}, bf16[384,1536]{1,0:T(8,128)(2,1)S(1)}, u32[]{:S(2)}, u32[]{:S(2)}) collective-permute-start(bf16[384,1536]{1,0:T(8,128)(2,1)} %collective-permute-done.9.refs_0_), channel_id=1, source_target_pairs={{0,1},{1,0},{2,3},{3,2},{4,5},{5,4},{6,7},{7,6},{8,9},{9,8},{10,11... | collective-permute-start | bytes 3538952 | tf_op jit(solution)/shard_map/ppermute | solution.py:25
  39.8 5.8 %collective-permute-start.15 = (bf16[64,384]{1,0:T(8,128)(2,1)}, bf16[64,384]{1,0:T(8,128)(2,1)}, u32[]{:S(2)}, u32[]{:S(2)}) collective-permute-start(bf16[64,384]{1,0:T(8,128)(2,1)} %get-tuple-element.93), channel_id=1, source_target_pairs={{0,2},{1,3},{2,0},{3,1},{4,6},{5,7},{6,4},{7,5},{8,10},{9,11},{10,... | collective-permute-start | bytes 147464 | tf_op jit(solution)/shard_map/ppermute | solution.py:25
  43.1 2.9 %copy-start.2 = (bf16[1,64,512]{2,1,0:T(8,128)(2,1)S(1)}, bf16[1,64,512]{2,1,0:T(8,128)(2,1)}, u32[]{:S(2)}) copy-start(bf16[1,64,512]{2,1,0:T(8,128)(2,1)} %param.11) | copy-start | bytes 196612
  43.1 2.9 %copy-start.4 = (bf16[64,512]{1,0:T(8,128)(2,1)S(1)}, bf16[64,512]{1,0:T(8,128)(2,1)}, u32[]{:S(2)}) copy-start(bf16[64,512]{1,0:T(8,128)(2,1)} %copy-done.3) | copy-start | bytes 196612
  43.1 2.9 %copy-start.8 = (s32[1,384]{1,0:T(1,128)S(1)}, s32[1,384]{1,0:T(1,128)}, u32[]{:S(2)}) copy-start(s32[1,384]{1,0:T(1,128)} %copy-done.7) | copy-start | bytes 4612
  44.0 1.9 %collective-permute-start.14 = (bf16[384,512]{1,0:T(8,128)(2,1)}, bf16[384,512]{1,0:T(8,128)(2,1)S(1)}, u32[]{:S(2)}, u32[]{:S(2)}) collective-permute-start(bf16[384,512]{1,0:T(8,128)(2,1)} %collective-permute-done.4.refs_0_), channel_id=1, source_target_pairs={{0,1},{1,0},{2,3},{3,2},{4,5},{5,4},{6,7},{7,6},{8,9},{9,8},{10,11... | collective-permute-start | bytes 1179656 | tf_op jit(solution)/shard_map/ppermute | solution.py:25
  (1 other events, 2.4 us)

commit v16 on v15

--- a/solution.py
+++ b/solution.py
@@ -29,7 +29,7 @@
     return lax.optimization_barrier(values)
 
 
-def call(kernel, out_shape, in_specs, scratch, out_specs=VECTOR, cost=LONG, mib=48):
+def call(kernel, out_shape, in_specs, scratch, out_specs=VECTOR, cost=LONG, mib=24):
     return pl.pallas_call(
         kernel,
         out_shape=out_shape,
@@ -165,6 +165,8 @@
     for copy in copies:
         copy.start()
     start_tiles(tile, depth, places, features, weight_ref, held_ref, rows_ref, sems)
+    total_ref[...] = given[...]
+    add_tiles(held_ref, rows_ref, sems, total_ref)
     for copy in copies:
         copy.wait()
     shrunk = (sums_ref[...] + received_ref[...].astype(jnp.float32)).astype(jnp.bfloat16).astype(jnp.float32)
@@ -175,9 +177,7 @@
         spread.T.astype(jnp.bfloat16), stacked_ref[...], preferred_element_type=jnp.float32
     )
     expanded = expanded.astype(jnp.bfloat16).astype(jnp.float32)
-    total_ref[...] = given[...] + LOWRANK_SCALE * expanded
-    add_tiles(held_ref, rows_ref, sems, total_ref)
-    out_ref[...] = total_ref[...].astype(out_ref.dtype)
+    out_ref[...] = (total_ref[...] + LOWRANK_SCALE * expanded).astype(out_ref.dtype)
 
 
 def shrink_kernel(tile, flips, pairs, slots, tokens_ref, stored_ref, *refs):

time: 49.4 us -> 48.7 us (0.986)
  Pallas kernels: 21 us -> 17.1 us
  local copies, waits for them, and re-layouts: 1.11 us -> 4.71 us
    unnamed x18, local copies, waits for them, and re-layouts: 0.04 us -> 3.64 us
    pallas_call x5, Pallas kernels: 10.5 us -> 7.86 us  [products(): call(functools.partial(products_kernel, tile, depth, places), jax.ShapeDt...]
    ppermute x2, waiting for transfers between devices: 7.69 us -> 5.69 us  [fetch_far(): lax.ppermute(value, ('parts', 'adapter'), route)]
    ppermute x14, waiting for transfers between devices: 3.57 us -> 5.37 us  [flipped(): return lax.ppermute(value, axis, [(i, i ^ flip) for i in range(count)])]
    pallas_call x1, Pallas kernels: 2.37 us -> 1.51 us  [body(): call(functools.partial(first_kernel, tile, depth, places, slots), [jax.Sh...]
  transfers between devices with their start and end apart: 16 -> 16, of which waited for: 6 -> 7; matrix products, arithmetic and copies ran while one was open for 1% -> 1% of each run, Pallas kernels for 38% -> 31%
where the time goes in v16:
time: 48.7 us; the launch traced here: 48.3 us
  Pallas kernels  17.1 us (35%)
  starting transfers between devices  14.6 us (30%)
  waiting for transfers between devices  11.1 us (23%)
  local copies, waits for them, and re-layouts  4.71 us (10%)
  other arithmetic  0.63 us (1%)
    ppermute x14, starting transfers between devices, flipped(): return lax.ppermute(value, axis, [(i, i ^ flip) for i in range(count)])  11.9 us
    pallas_call x5, Pallas kernels, products(): call(functools.partial(products_kernel, tile, depth, places), jax.ShapeDt...  7.86 us
    ppermute x2, waiting for transfers between devices, fetch_far(): lax.ppermute(value, ('parts', 'adapter'), route)  5.69 us
    ppermute x14, waiting for transfers between devices, flipped(): return lax.ppermute(value, axis, [(i, i ^ flip) for i in range(count)])  5.37 us
    unnamed x18, local copies, waits for them, and re-layouts  3.64 us
    ppermute x2, starting transfers between devices, fetch_far(): lax.ppermute(value, ('parts', 'adapter'), route)  2.66 us
    pallas_call x1, Pallas kernels, body(): call(functools.partial(shrink_kernel, tile, flips, pairs, slots), jax.Sha...  2.46 us
    pallas_call x1, Pallas kernels, body(): call(functools.partial(last_kernel, tile, depth, places, flips, pairs, sl...  2.31 us
  transfers between devices with their start and end apart: 16, of which 7 were waited for; matrix products, arithmetic and copies ran while one was open for 1% of the time, Pallas kernels for 31%

profile of v16, /device:TPU:0, one launch (start us, length us, event | category | flops | bytes accessed | tf_op | source)
XLA Modules:
  0.0 48.3 jit_solution(17662724768510556079)
XLA Ops:
  0.0 1.1 %dynamic-slice_bitcast_fusion = (bf16[16,2048]{1,0:T(8,128)(2,1)S(1)}, bf16[16,2048]{1,0:T(8,128)(2,1)S(1)}, bf16[16,2048]{1,0:T(8,128)(2,1)S(1)}, bf16[16,2048]{1,0:T(8,128)(2,1)S(1)}) fusion(bf16[1,8192,16]{1,2,0:T(8,128)(2,1)} %param.10, s32[]{:T(128)S(6)} %select_n.15, s32[]{:T(128)S(6)} %select_n.13, s32[]{:T(128)S(6)} %select_n.12, s32[]{:T(128)S(6)} %select_n.14), kind=kLoop, calls=%fused_computation | loop fusion | bytes 524304 | tf_op jit(solution)/shard_map/dynamic_slice | solution.py:230
  1.6 2.6 %collective-permute-start.1 = (bf16[16,2048]{1,0:T(8,128)(2,1)S(1)}, bf16[16,2048]{1,0:T(8,128)(2,1)S(1)}, u32[]{:S(2)}, u32[]{:S(2)}) collective-permute-start(bf16[16,2048]{1,0:T(8,128)(2,1)S(1)} %get-tuple-element.52), channel_id=1, source_target_pairs={{0,2},{1,3},{2,0},{3,1},{4,6},{5,7},{6,4},{7,5},{8,10},{9,11},{10,... | collective-permute-start | bytes 196616 | tf_op jit(solution)/shard_map/ppermute | solution.py:25
  4.3 2.2 %shard_map.66 = (bf16[384,1536]{1,0:T(8,128)(2,1)}, bf16[384,512]{1,0:T(8,128)(2,1)}) custom-call(bf16[384,2048]{1,0:T(8,128)(2,1)} %tokens_ref.1), custom_call_target="tpu_custom_call" | custom-call | tf_op jit(solution)/shard_map/pallas_call | solution.py:236
  6.5 1.8 %collective-permute-start.9 = (bf16[384,1536]{1,0:T(8,128)(2,1)}, bf16[384,1536]{1,0:T(8,128)(2,1)}, u32[]{:S(2)}, u32[]{:S(2)}) collective-permute-start(bf16[384,1536]{1,0:T(8,128)(2,1)} %get-tuple-element.70), channel_id=1, source_target_pairs={{0,2},{1,3},{2,0},{3,1},{4,6},{5,7},{6,4},{7,5},{8,10},{9,11},{10,... | collective-permute-start | bytes 3538952 | tf_op jit(solution)/shard_map/ppermute | solution.py:25
  8.4 0.7 %shard_map.64.refs_0_ = bf16[64,2048]{1,0:T(8,128)(2,1)} custom-call(bf16[16,2048]{1,0:T(8,128)(2,1)S(1)} %get-tuple-element.49.refs_0_, bf16[16,2048]{1,0:T(8,128)(2,1)S(1)} %collective-permute-done.refs_1_, bf16[16,2048]{1,0:T(8,128)(2,1)S(1)} %collective-permute-done.1.refs_2_, bf16[16,2048]{1,0:T(8,128)(2,1)S(1)} %collective-permute-done.2.refs_3_), custom_call_target="tpu_custom_call" | custom-call | tf_op jit(solution)/shard_map/pallas_call | solution.py:253
  9.1 2.7 %collective-permute-start.5 = (bf16[64,2048]{1,0:T(8,128)(2,1)}, bf16[64,2048]{1,0:T(8,128)(2,1)}, u32[]{:S(2)}, u32[]{:S(2)}) collective-permute-start(bf16[64,2048]{1,0:T(8,128)(2,1)} %shard_map.64.refs_0_), channel_id=1, source_target_pairs={{0,8},{4,12},{8,0},{12,4},{16,28},{20,24},{24,20},{28,16},{1,9},{5... | collective-permute-start | bytes 786440 | tf_op jit(solution)/shard_map/ppermute | solution.py:303
  11.8 3.4 %copy-done.1 = bf16[8192,512]{1,0:T(8,128)(2,1)S(1)} copy-done((bf16[8192,512]{1,0:T(8,128)(2,1)S(1)}, bf16[8192,512]{1,0:T(8,128)(2,1)}, u32[]{:S(2)}) %copy-start.1) | copy-done | bytes 8388632
  15.2 1.5 %shard_map.65 = (f32[384,512]{1,0:T(8,128)S(1)}, s32[1,384]{1,0:T(1,128)S(1)}) custom-call(s32[4]{0:T(128)S(1)} %copy-done.6, s32[1,384]{1,0:T(1,128)S(1)} %bitcast.21, bf16[8192,512]{1,0:T(8,128)(2,1)S(1)} %copy-done.1, bf16[384,2048]{1,0:T(8,128)(2,1)S(1)} %copy-done), custom_call_target="tpu_custom_call" | custom-call | flops 99999997952 | tf_op jit(solution)/shard_map/pallas_call | solution.py:314
  16.7 1.6 %collective-permute-start.6 = (bf16[64,512]{1,0:T(8,128)(2,1)S(1)}, bf16[64,512]{1,0:T(8,128)(2,1)S(1)}, u32[]{:S(2)}, u32[]{:S(2)}) collective-permute-start(bf16[64,512]{1,0:T(8,128)(2,1)S(1)} %bitcast.18), channel_id=1, source_target_pairs={{0,4},{4,0},{8,12},{12,8},{1,5},{5,1},{9,13},{13,9},{2,6},{6,2},{1... | collective-permute-start | bytes 196616 | tf_op jit(solution)/shard_map/ppermute | solution.py:25
  18.6 1.0 %shard_map.67.refs_1_ = f32[384,512]{1,0:T(8,128)S(1)} custom-call(bf16[8192,512]{1,0:T(8,128)(2,1)S(1)} %copy-done.2, bf16[384,2048]{1,0:T(8,128)(2,1)S(1)} %copy-done, f32[384,512]{1,0:T(8,128)S(1)} %get-tuple-element.62.refs_1_), custom_call_target="tpu_custom_call" | custom-call | flops 99999997952 | tf_op jit(solution)/shard_map/pallas_call | solution.py:285
  19.6 1.6 %collective-permute-start.10 = (bf16[64,2048]{1,0:T(8,128)(2,1)}, bf16[64,2048]{1,0:T(8,128)(2,1)S(1)}, u32[]{:S(2)}, u32[]{:S(2)}) collective-permute-start(bf16[64,2048]{1,0:T(8,128)(2,1)} %shard_map.64.refs_0_), channel_id=1, source_target_pairs={{0,4},{4,0},{8,12},{12,8},{1,5},{5,1},{9,13},{13,9},{2,6},{6,2},{1... | collective-permute-start | bytes 786440 | tf_op jit(solution)/shard_map/ppermute | solution.py:25
  21.2 1.2 %collective-permute-start.4 = (bf16[384,512]{1,0:T(8,128)(2,1)}, bf16[384,512]{1,0:T(8,128)(2,1)}, u32[]{:S(2)}, u32[]{:S(2)}) collective-permute-start(bf16[384,512]{1,0:T(8,128)(2,1)} %get-tuple-element.60), channel_id=1, source_target_pairs={{0,2},{1,3},{2,0},{3,1},{4,6},{5,7},{6,4},{7,5},{8,10},{9,11},{10,... | collective-permute-start | bytes 1179656 | tf_op jit(solution)/shard_map/ppermute | solution.py:25
  22.4 2.4 %collective-permute-done.5.refs_2_ = bf16[64,2048]{1,0:T(8,128)(2,1)} collective-permute-done((bf16[64,2048]{1,0:T(8,128)(2,1)}, bf16[64,2048]{1,0:T(8,128)(2,1)}, u32[]{:S(2)}, u32[]{:S(2)}) %collective-permute-start.5) | collective-permute-done | bytes 262176 | tf_op jit(solution)/shard_map/ppermute | solution.py:303
  24.8 1.1 %collective-permute-done.6.refs_6_ = bf16[64,512]{1,0:T(8,128)(2,1)S(1)} collective-permute-done((bf16[64,512]{1,0:T(8,128)(2,1)S(1)}, bf16[64,512]{1,0:T(8,128)(2,1)S(1)}, u32[]{:S(2)}, u32[]{:S(2)}) %collective-permute-start.6) | collective-permute-done | bytes 65568 | tf_op jit(solution)/shard_map/ppermute | solution.py:25
  26.5 1.9 %shard_map.68.refs_1_ = f32[384,512]{1,0:T(8,128)S(1)} custom-call(bf16[8192,512]{1,0:T(8,128)(2,1)S(1)} %copy-done.2, bf16[384,2048]{1,0:T(8,128)(2,1)S(1)} %collective-permute-done.3.refs_0_, f32[384,512]{1,0:T(8,128)S(1)} %shard_map.67.refs_1_), custom_call_target="tpu_custom_call" | custom-call | flops 99999997952 | tf_op jit(solution)/shard_map/pallas_call | solution.py:285
  28.4 3.3 %collective-permute-done.7.refs_7_ = bf16[64,512]{1,0:T(8,128)(2,1)} collective-permute-done((bf16[64,512]{1,0:T(8,128)(2,1)S(1)}, bf16[64,512]{1,0:T(8,128)(2,1)}, u32[]{:S(2)}, u32[]{:S(2)}) %collective-permute-start.7) | collective-permute-done | bytes 65568 | tf_op jit(solution)/shard_map/ppermute | solution.py:303
  32.5 1.2 %collective-permute-done.11.refs_3_ = bf16[64,2048]{1,0:T(8,128)(2,1)S(1)} collective-permute-done((bf16[64,2048]{1,0:T(8,128)(2,1)}, bf16[64,2048]{1,0:T(8,128)(2,1)S(1)}, u32[]{:S(2)}, u32[]{:S(2)}) %collective-permute-start.11) | collective-permute-done | bytes 262176 | tf_op jit(solution)/shard_map/ppermute | solution.py:25
  33.6 2.5 %shard_map.69 = f32[64,384]{1,0:T(8,128)S(1)} custom-call(bf16[384,2048]{1,0:T(8,128)(2,1)S(1)} %copy-done, s32[1,384]{1,0:T(1,128)S(1)} %get-tuple-element.71.stored_ref.refs_2_, bf16[64,2048]{1,0:T(8,128)(2,1)} %shard_map.64.refs_0_, bf16[64,2048]{1,0:T(8,128)(2,1)S(1)} %collective-permute-done.10.refs_1_, ...), custom_call_target="tpu_custom_call" | custom-call | flops 99999997952 | tf_op jit(solution)/shard_map/pallas_call | solution.py:343
  36.7 2.2 %shard_map.70.refs_1_ = f32[384,512]{1,0:T(8,128)S(1)} custom-call(bf16[8192,512]{1,0:T(8,128)(2,1)S(1)} %copy-done.2, bf16[384,1536]{1,0:T(8,128)(2,1)} %collective-permute-done.9.refs_0_, f32[384,512]{1,0:T(8,128)S(1)} %shard_map.68.refs_1_), custom_call_target="tpu_custom_call" | custom-call | flops 99999997952 | tf_op jit(solution)/shard_map/pallas_call | solution.py:285
  39.6 1.2 %collective-permute-start.15 = (bf16[64,384]{1,0:T(8,128)(2,1)}, bf16[64,384]{1,0:T(8,128)(2,1)}, u32[]{:S(2)}, u32[]{:S(2)}) collective-permute-start(bf16[64,384]{1,0:T(8,128)(2,1)} %get-tuple-element.93), channel_id=1, source_target_pairs={{0,2},{1,3},{2,0},{3,1},{4,6},{5,7},{6,4},{7,5},{8,10},{9,11},{10,... | collective-permute-start | bytes 147464 | tf_op jit(solution)/shard_map/ppermute | solution.py:25
  40.8 1.4 %shard_map.71.refs_1_ = f32[384,512]{1,0:T(8,128)S(1)} custom-call(bf16[8192,512]{1,0:T(8,128)(2,1)S(1)} %copy-done.2, bf16[384,1536]{1,0:T(8,128)(2,1)S(1)} %collective-permute-done.12.refs_0_, f32[384,512]{1,0:T(8,128)S(1)} %shard_map.70.refs_1_), custom_call_target="tpu_custom_call" | custom-call | flops 99999997952 | tf_op jit(solution)/shard_map/pallas_call | solution.py:285
  42.2 1.8 %collective-permute-done.4.refs_0_ = bf16[384,512]{1,0:T(8,128)(2,1)} collective-permute-done((bf16[384,512]{1,0:T(8,128)(2,1)}, bf16[384,512]{1,0:T(8,128)(2,1)}, u32[]{:S(2)}, u32[]{:S(2)}) %collective-permute-start.4) | collective-permute-done | bytes 393248 | tf_op jit(solution)/shard_map/ppermute | solution.py:25
  44.0 1.4 %shard_map.72.refs_1_ = f32[384,512]{1,0:T(8,128)S(1)} custom-call(bf16[8192,512]{1,0:T(8,128)(2,1)S(1)} %copy-done.2, bf16[384,512]{1,0:T(8,128)(2,1)} %collective-permute-done.4.refs_0_, f32[384,512]{1,0:T(8,128)S(1)} %shard_map.71.refs_1_), custom_call_target="tpu_custom_call" | custom-call | flops 99999997952 | tf_op jit(solution)/shard_map/pallas_call | solution.py:285
  46.0 2.3 %shard_map.73 = bf16[384,512]{1,0:T(8,128)(2,1)} custom-call(bf16[8192,512]{1,0:T(8,128)(2,1)S(1)} %copy-done.2, bf16[384,512]{1,0:T(8,128)(2,1)S(1)} %collective-permute-done.14.refs_0_, f32[384,512]{1,0:T(8,128)S(1)} %shard_map.72.refs_1_, s32[1,384]{1,0:T(1,128)S(1)} %copy-done.8, f32[64,384]{1,0:T(8,128)S(1)} %get-tuple-element.87.refs_3_, ...), custom_call_target="tpu_custom_call" | custom-call | flops 99999997952 | tf_op jit(solution)/shard_map/pallas_call | solution.py:376
  (38 shorter events, 4.0 us)
Async XLA Ops:
  0.0 8.3 %copy-start = (bf16[384,2048]{1,0:T(8,128)(2,1)S(1)}, bf16[384,2048]{1,0:T(8,128)(2,1)}, u32[]{:S(2)}) copy-start(bf16[384,2048]{1,0:T(8,128)(2,1)} %tokens_ref.1) | copy-start | bytes 4718596
  0.0 11.8 %copy-start.5 = (s32[384,1]{0,1:T(1,128)S(1)}, s32[384,1]{0,1:T(1,128)}, u32[]{:S(2)}) copy-start(s32[384,1]{0,1:T(1,128)} %param.7) | copy-start | bytes 4612
  0.0 11.8 %copy-start.6 = (s32[4]{0:T(128)S(1)}, s32[4]{0:T(128)}, u32[]{:S(2)}) copy-start(s32[4]{0:T(128)} %placement_ref.1) | copy-start | bytes 52
  1.1 7.2 %collective-permute-start = (bf16[16,2048]{1,0:T(8,128)(2,1)S(1)}, bf16[16,2048]{1,0:T(8,128)(2,1)S(1)}, u32[]{:S(2)}, u32[]{:S(2)}) collective-permute-start(bf16[16,2048]{1,0:T(8,128)(2,1)S(1)} %get-tuple-element.50), channel_id=1, source_target_pairs={{0,1},{1,0},{2,3},{3,2},{4,5},{5,4},{6,7},{7,6},{8,9},{9,8},{10,11... | collective-permute-start | bytes 196616 | tf_op jit(solution)/shard_map/ppermute | solution.py:25
  1.6 6.7 %collective-permute-start.1 = (bf16[16,2048]{1,0:T(8,128)(2,1)S(1)}, bf16[16,2048]{1,0:T(8,128)(2,1)S(1)}, u32[]{:S(2)}, u32[]{:S(2)}) collective-permute-start(bf16[16,2048]{1,0:T(8,128)(2,1)S(1)} %get-tuple-element.52), channel_id=1, source_target_pairs={{0,2},{1,3},{2,0},{3,1},{4,6},{5,7},{6,4},{7,5},{8,10},{9,11},{10,... | collective-permute-start | bytes 196616 | tf_op jit(solution)/shard_map/ppermute | solution.py:25
  4.2 4.2 %collective-permute-start.2 = (bf16[16,2048]{1,0:T(8,128)(2,1)S(1)}, bf16[16,2048]{1,0:T(8,128)(2,1)S(1)}, u32[]{:S(2)}, u32[]{:S(2)}) collective-permute-start(bf16[16,2048]{1,0:T(8,128)(2,1)S(1)} %get-tuple-element.53), channel_id=1, source_target_pairs={{0,3},{1,2},{2,1},{3,0},{4,7},{5,6},{6,5},{7,4},{8,11},{9,10},{10,... | collective-permute-start | bytes 196616 | tf_op jit(solution)/shard_map/ppermute | solution.py:25
  6.5 29.6 %collective-permute-start.9 = (bf16[384,1536]{1,0:T(8,128)(2,1)}, bf16[384,1536]{1,0:T(8,128)(2,1)}, u32[]{:S(2)}, u32[]{:S(2)}) collective-permute-start(bf16[384,1536]{1,0:T(8,128)(2,1)} %get-tuple-element.70), channel_id=1, source_target_pairs={{0,2},{1,3},{2,0},{3,1},{4,6},{5,7},{6,4},{7,5},{8,10},{9,11},{10,... | collective-permute-start | bytes 3538952 | tf_op jit(solution)/shard_map/ppermute | solution.py:25
  8.3 8.4 %collective-permute-start.3 = (bf16[384,2048]{1,0:T(8,128)(2,1)S(1)}, bf16[384,2048]{1,0:T(8,128)(2,1)S(1)}, u32[]{:S(2)}, u32[]{:S(2)}) collective-permute-start(bf16[384,2048]{1,0:T(8,128)(2,1)S(1)} %copy-done), channel_id=1, source_target_pairs={{0,1},{1,0},{2,3},{3,2},{4,5},{5,4},{6,7},{7,6},{8,9},{9,8},{10,11... | collective-permute-start | bytes 4718600 | tf_op jit(solution)/shard_map/ppermute | solution.py:25
  9.1 15.7 %collective-permute-start.5 = (bf16[64,2048]{1,0:T(8,128)(2,1)}, bf16[64,2048]{1,0:T(8,128)(2,1)}, u32[]{:S(2)}, u32[]{:S(2)}) collective-permute-start(bf16[64,2048]{1,0:T(8,128)(2,1)} %shard_map.64.refs_0_), channel_id=1, source_target_pairs={{0,8},{4,12},{8,0},{12,4},{16,28},{20,24},{24,20},{28,16},{1,9},{5... | collective-permute-start | bytes 786440 | tf_op jit(solution)/shard_map/ppermute | solution.py:303
  11.8 3.4 %copy-start.1 = (bf16[8192,512]{1,0:T(8,128)(2,1)S(1)}, bf16[8192,512]{1,0:T(8,128)(2,1)}, u32[]{:S(2)}) copy-start(bf16[8192,512]{1,0:T(8,128)(2,1)} %weight_ref.13) | copy-start | bytes 25165828
  15.2 3.4 %copy-start.2 = (bf16[8192,512]{1,0:T(8,128)(2,1)S(1)}, bf16[8192,512]{1,0:T(8,128)(2,1)}, u32[]{:S(2)}) copy-start(bf16[8192,512]{1,0:T(8,128)(2,1)} %weight_ref.13) | copy-start | bytes 25165828
  16.7 17.0 %copy-start.7 = (s32[1,384]{1,0:T(1,128)}, s32[1,384]{1,0:T(1,128)S(1)}, u32[]{:S(2)}) copy-start(s32[1,384]{1,0:T(1,128)S(1)} %get-tuple-element.71.stored_ref.refs_2_) | copy-start | bytes 4612
  16.7 9.2 %collective-permute-start.6 = (bf16[64,512]{1,0:T(8,128)(2,1)S(1)}, bf16[64,512]{1,0:T(8,128)(2,1)S(1)}, u32[]{:S(2)}, u32[]{:S(2)}) collective-permute-start(bf16[64,512]{1,0:T(8,128)(2,1)S(1)} %bitcast.18), channel_id=1, source_target_pairs={{0,4},{4,0},{8,12},{12,8},{1,5},{5,1},{9,13},{13,9},{2,6},{6,2},{1... | collective-permute-start | bytes 196616 | tf_op jit(solution)/shard_map/ppermute | solution.py:25
  19.6 12.9 %collective-permute-start.10 = (bf16[64,2048]{1,0:T(8,128)(2,1)}, bf16[64,2048]{1,0:T(8,128)(2,1)S(1)}, u32[]{:S(2)}, u32[]{:S(2)}) collective-permute-start(bf16[64,2048]{1,0:T(8,128)(2,1)} %shard_map.64.refs_0_), channel_id=1, source_target_pairs={{0,4},{4,0},{8,12},{12,8},{1,5},{5,1},{9,13},{13,9},{2,6},{6,2},{1... | collective-permute-start | bytes 786440 | tf_op jit(solution)/shard_map/ppermute | solution.py:25
  21.2 22.8 %collective-permute-start.4 = (bf16[384,512]{1,0:T(8,128)(2,1)}, bf16[384,512]{1,0:T(8,128)(2,1)}, u32[]{:S(2)}, u32[]{:S(2)}) collective-permute-start(bf16[384,512]{1,0:T(8,128)(2,1)} %get-tuple-element.60), channel_id=1, source_target_pairs={{0,2},{1,3},{2,0},{3,1},{4,6},{5,7},{6,4},{7,5},{8,10},{9,11},{10,... | collective-permute-start | bytes 1179656 | tf_op jit(solution)/shard_map/ppermute | solution.py:25
  25.9 5.8 %collective-permute-start.7 = (bf16[64,512]{1,0:T(8,128)(2,1)S(1)}, bf16[64,512]{1,0:T(8,128)(2,1)}, u32[]{:S(2)}, u32[]{:S(2)}) collective-permute-start(bf16[64,512]{1,0:T(8,128)(2,1)S(1)} %bitcast.19), channel_id=1, source_target_pairs={{0,8},{4,12},{8,0},{12,4},{16,28},{20,24},{24,20},{28,16},{1,9},{5... | collective-permute-start | bytes 196616 | tf_op jit(solution)/shard_map/ppermute | solution.py:303
  25.9 7.8 %collective-permute-start.11 = (bf16[64,2048]{1,0:T(8,128)(2,1)}, bf16[64,2048]{1,0:T(8,128)(2,1)S(1)}, u32[]{:S(2)}, u32[]{:S(2)}) collective-permute-start(bf16[64,2048]{1,0:T(8,128)(2,1)} %collective-permute-done.5.refs_2_), channel_id=1, source_target_pairs={{0,16},{16,0},{1,17},{17,1},{2,18},{18,2},{3,19},{19,3},{4,20},{20... | collective-permute-start | bytes 786440 | tf_op jit(solution)/shard_map/ppermute | solution.py:25
  31.7 10.5 %collective-permute-start.8 = (bf16[64,512]{1,0:T(8,128)(2,1)}, bf16[64,512]{1,0:T(8,128)(2,1)}, u32[]{:S(2)}, u32[]{:S(2)}) collective-permute-start(bf16[64,512]{1,0:T(8,128)(2,1)} %collective-permute-done.7.refs_7_), channel_id=1, source_target_pairs={{0,16},{16,0},{1,17},{17,1},{2,18},{18,2},{3,19},{19,3},{4,20},{20... | collective-permute-start | bytes 196616 | tf_op jit(solution)/shard_map/ppermute | solution.py:25
  36.1 2.8 %collective-permute-start.13 = (f32[64,384]{1,0:T(8,128)S(1)}, f32[64,384]{1,0:T(8,128)S(1)}, u32[]{:S(2)}, u32[]{:S(2)}) collective-permute-start(f32[64,384]{1,0:T(8,128)S(1)} %shard_map.69), channel_id=1, source_target_pairs={{0,1},{1,0},{2,3},{3,2},{4,5},{5,4},{6,7},{7,6},{8,9},{9,8},{10,11... | collective-permute-start | bytes 294920 | tf_op jit(solution)/shard_map/ppermute | solution.py:25
  36.2 4.5 %collective-permute-start.12 = (bf16[384,1536]{1,0:T(8,128)(2,1)}, bf16[384,1536]{1,0:T(8,128)(2,1)S(1)}, u32[]{:S(2)}, u32[]{:S(2)}) collective-permute-start(bf16[384,1536]{1,0:T(8,128)(2,1)} %collective-permute-done.9.refs_0_), channel_id=1, source_target_pairs={{0,1},{1,0},{2,3},{3,2},{4,5},{5,4},{6,7},{7,6},{8,9},{9,8},{10,11... | collective-permute-start | bytes 3538952 | tf_op jit(solution)/shard_map/ppermute | solution.py:25
  39.6 5.9 %collective-permute-start.15 = (bf16[64,384]{1,0:T(8,128)(2,1)}, bf16[64,384]{1,0:T(8,128)(2,1)}, u32[]{:S(2)}, u32[]{:S(2)}) collective-permute-start(bf16[64,384]{1,0:T(8,128)(2,1)} %get-tuple-element.93), channel_id=1, source_target_pairs={{0,2},{1,3},{2,0},{3,1},{4,6},{5,7},{6,4},{7,5},{8,10},{9,11},{10,... | collective-permute-start | bytes 147464 | tf_op jit(solution)/shard_map/ppermute | solution.py:25
  42.2 3.8 %copy-start.4 = (bf16[1,64,512]{2,1,0:T(8,128)(2,1)S(1)}, bf16[1,64,512]{2,1,0:T(8,128)(2,1)}, u32[]{:S(2)}) copy-start(bf16[1,64,512]{2,1,0:T(8,128)(2,1)} %param.11) | copy-start | bytes 196612
  42.2 3.8 %copy-start.8 = (s32[1,384]{1,0:T(1,128)S(1)}, s32[1,384]{1,0:T(1,128)}, u32[]{:S(2)}) copy-start(s32[1,384]{1,0:T(1,128)} %copy-done.7) | copy-start | bytes 4612
  44.0 1.9 %collective-permute-start.14 = (bf16[384,512]{1,0:T(8,128)(2,1)}, bf16[384,512]{1,0:T(8,128)(2,1)S(1)}, u32[]{:S(2)}, u32[]{:S(2)}) collective-permute-start(bf16[384,512]{1,0:T(8,128)(2,1)} %collective-permute-done.4.refs_0_), channel_id=1, source_target_pairs={{0,1},{1,0},{2,3},{3,2},{4,5},{5,4},{6,7},{7,6},{8,9},{9,8},{10,11... | collective-permute-start | bytes 1179656 | tf_op jit(solution)/shard_map/ppermute | solution.py:25
  (1 other events, 1.5 us)

commit v17 on v16

--- a/solution.py
+++ b/solution.py
@@ -51,16 +51,31 @@
         copy.wait()
 
 
-def cut_kernel(edges, source_ref, *refs):
-    outs, (held_ref, sems) = refs[:-2], refs[-2:]
+def cut_kernel(edges, tokens_ref, down_ref, *refs):
+    cuts = len(edges) - 1
+    outs, pieces = refs[:cuts], refs[cuts:-4]
+    held_ref, slices_ref, sems, slice_sems = refs[-4:]
+    me, depth = lax.axis_index("tensor"), tokens_ref.shape[1]
     steps, rows = held_ref.shape[:2]
+    arriving = []
+    for i in range(len(pieces)):
+        start = pl.multiple_of((me ^ (i + 1)) * depth, LANES)
+        arriving.append(
+            pltpu.make_async_copy(
+                down_ref.at[:, pl.ds(start, depth)], slices_ref.at[i], slice_sems.at[0, i]
+            )
+        )
     copies = [
-        pltpu.make_async_copy(source_ref.at[pl.ds(i * rows, rows)], held_ref.at[i], sems.at[0, i])
+        pltpu.make_async_copy(tokens_ref.at[pl.ds(i * rows, rows)], held_ref.at[i], sems.at[0, i])
         for i in range(steps)
     ]
-    for copy in copies:
+    for copy in arriving + copies:
         copy.start()
     leaving = []
+    for i, piece in enumerate(pieces):
+        arriving[i].wait()
+        leaving.append(pltpu.make_async_copy(slices_ref.at[i], piece, slice_sems.at[1, i]))
+        leaving[-1].start()
     for i in range(steps):
         copies[i].wait()
         for m, (a, b, out) in enumerate(zip(edges, edges[1:], outs)):
@@ -76,13 +91,15 @@
         copy.wait()
 
 
-def order_kernel(rank_part, *refs):
+def order_kernel(down_ref, *refs):
     pieces, out_ref, sems = refs[:-2], refs[-2], refs[-1]
     me = lax.axis_index("tensor")
+    part, depth = pieces[0].shape
+    mine = down_ref.at[:, pl.ds(pl.multiple_of(me * depth, LANES), depth)]
     run_copies(
         [
-            (piece, out_ref.at[pl.ds(pl.multiple_of((me ^ f) * rank_part, rank_part), rank_part)])
-            for f, piece in enumerate(pieces)
+            (piece, out_ref.at[pl.ds(pl.multiple_of((me ^ f) * part, part), part)])
+            for f, piece in enumerate((mine, *pieces))
         ],
         sems,
     )
@@ -226,39 +243,45 @@
     tile = math.gcd(*edges)
 
     down = lowrank_down_weight[0].T
-    pieces = [
-        lax.dynamic_slice_in_dim(down, (me ^ flip) * depth, depth, axis=1)
-        for flip in range(tensors)
-    ]
-    uncut, pieces = chained(tokens, pieces)
-    steps = 6
-    chunks = list(
-        call(
+    by_copies = down.shape[0] % 16 == 0
+    cuts, steps = len(edges) - 1, 6
+    if by_copies:
+        made = call(
             functools.partial(cut_kernel, edges),
-            [jax.ShapeDtypeStruct((rows, b - a), tokens.dtype) for a, b in zip(edges, edges[1:])],
-            [ANYWHERE],
+            [jax.ShapeDtypeStruct((rows, b - a), tokens.dtype) for a, b in zip(edges, edges[1:])]
+            + [jax.ShapeDtypeStruct((down.shape[0], depth), down.dtype)] * (tensors - 1),
+            [ANYWHERE] * 2,
             [
                 pltpu.VMEM((steps, rows // steps, depth), tokens.dtype),
-                pltpu.SemaphoreType.DMA((len(edges), steps)),
+                pltpu.VMEM((tensors - 1, down.shape[0], depth), down.dtype),
+                pltpu.SemaphoreType.DMA((1 + cuts, steps)),
+                pltpu.SemaphoreType.DMA((2, tensors - 1)),
             ],
-            [ANYWHERE] * (len(edges) - 1),
+            [ANYWHERE] * (cuts + tensors - 1),
             cost=FREE,
             mib=56,
-        )(uncut)
-    )
-    pieces = [pieces[0]] + [flipped(pieces[f], "tensor", f) for f in range(1, tensors)]
-    pieces[1], here = chained(pieces[1], tokens)
+        )(tokens, down)
+        chunks, pieces = list(made[:cuts]), list(made[cuts:])
+    else:
+        chunks = [tokens[:, a:b] for a, b in zip(edges, edges[1:])]
+        pieces = [
+            lax.dynamic_slice_in_dim(down, (me ^ flip) * depth, depth, axis=1)
+            for flip in range(1, tensors)
+        ]
+    pieces = [flipped(piece, "tensor", i + 1) for i, piece in enumerate(pieces)]
+    pieces[0], here = chained(pieces[0], tokens)
     neighbour = flipped(here, "tensor", 1)
-    if down.shape[0] % 16 == 0:
+    if by_copies:
         own = call(
-            functools.partial(order_kernel, down.shape[0]),
+            order_kernel,
             jax.ShapeDtypeStruct((rank, depth), down.dtype),
             [ANYWHERE] * tensors,
             [pltpu.SemaphoreType.DMA((tensors,))],
-            ANYWHERE,
+            VECTOR,
             cost=FREE,
-        )(*pieces)
+        )(down, *pieces)
     else:
+        pieces = [lax.dynamic_slice_in_dim(down, me * depth, depth, axis=1)] + pieces
         none = jnp.zeros((), down.dtype)
         own = jnp.concatenate(
             [sum(jnp.where((me ^ f) == j, pieces[f], none) for f in range(tensors)) for j in range(tensors)],
@@ -327,13 +350,12 @@
     far.append(send(1))
     single, single_up = fetch_near(own), fetch_near(up)
     total = products([(0, depth // 2, depth // 2, depth // 2)], [here], total)
-    fetched, single_up, total, up = chained(fetched, single_up, total, up)
+    fetched, single_up, total = chained(fetched, single_up, total)
     swapped = swap(fetched)
-    fetched_up = fetch_far(up)
     total, neighbour = chained(total, neighbour)
     total = products([(1, 0, 0, depth)], [neighbour], total)
-    fetched_up, total = chained(fetched_up, total)
-    swapped_up = swap(fetched_up)
+    total, up = chained(total, up)
+    fetched_up = fetch_far(up)
     single, swapped, total = chained(single, swapped, total)
     downs = [own] + single
     for pair in zip(fetched, swapped):
@@ -351,7 +373,8 @@
             pltpu.SemaphoreType.DMA((1 + slots, tiles)),
         ],
     )(tokens, stored, *downs)
-    far[0], partial = chained(far[0], partial)
+    far[0], fetched_up, partial = chained(far[0], fetched_up, partial)
+    swapped_up = swap(fetched_up)
     ups = [up] + single_up
     for pair in zip(fetched_up, swapped_up):
         ups += pair

time: 48.7 us -> 49.8 us (1.023)
  starting transfers between devices: 14.6 us -> 17.2 us
  waiting for transfers between devices: 11.1 us -> 10 us
  local copies, waits for them, and re-layouts: 4.71 us -> 3.66 us
  Pallas kernels: 17.1 us -> 17.9 us
    ppermute x2, waiting for transfers between devices: 5.69 us -> 1.65 us  [fetch_far(): lax.ppermute(value, ('parts', 'adapter'), route)]
    ppermute x14, waiting for transfers between devices: 5.37 us -> 8.35 us  [flipped(): return lax.ppermute(value, axis, [(i, i ^ flip) for i in range(count)])]
    ppermute x2, starting transfers between devices: 2.66 us -> 4.58 us  [fetch_far(): lax.ppermute(value, ('parts', 'adapter'), route)]
    dynamic_slice x1 -> x0, local copies, waits for them, and re-layouts: 1.07 us -> none  [body(): lax.dynamic_slice_in_dim(down, (me ^ flip) * depth, depth, axis=1)]
    ppermute x14, starting transfers between devices: 11.9 us -> 12.6 us  [flipped(): return lax.ppermute(value, axis, [(i, i ^ flip) for i in range(count)])]
    pallas_call x1, Pallas kernels: 2.23 us -> 2.76 us  [body(): call(functools.partial(cut_kernel, edges), [jax.ShapeDtypeStruct((rows, b...]
    unnamed x18 -> x26, local copies, waits for them, and re-layouts: 3.64 us -> 3.66 us
  transfers between devices with their start and end apart: 16 -> 16, of which waited for: 7 -> 8; matrix products, arithmetic and copies ran while one was open for 1% -> 1% of each run, Pallas kernels for 31% -> 26%
where the time goes in v17:
time: 49.8 us; the launch traced here: 49.6 us
  Pallas kernels  17.9 us (36%)
  starting transfers between devices  17.2 us (35%)
  waiting for transfers between devices  10 us (20%)
  local copies, waits for them, and re-layouts  3.66 us (7%)
  other arithmetic  0.63 us (1%)
    ppermute x14, starting transfers between devices, flipped(): return lax.ppermute(value, axis, [(i, i ^ flip) for i in range(count)])  12.6 us
    ppermute x14, waiting for transfers between devices, flipped(): return lax.ppermute(value, axis, [(i, i ^ flip) for i in range(count)])  8.35 us
    pallas_call x5, Pallas kernels, products(): call(functools.partial(products_kernel, tile, depth, places), jax.ShapeDt...  7.86 us
    ppermute x2, starting transfers between devices, fetch_far(): lax.ppermute(value, ('parts', 'adapter'), route)  4.58 us
    unnamed x26, local copies, waits for them, and re-layouts  3.66 us
    pallas_call x1, Pallas kernels, body(): call(functools.partial(cut_kernel, edges), [jax.ShapeDtypeStruct((rows, b...  2.76 us
    pallas_call x1, Pallas kernels, body(): call(functools.partial(shrink_kernel, tile, flips, pairs, slots), jax.Sha...  2.46 us
    pallas_call x1, Pallas kernels, body(): call(functools.partial(last_kernel, tile, depth, places, flips, pairs, sl...  2.27 us
  transfers between devices with their start and end apart: 16, of which 8 were waited for; matrix products, arithmetic and copies ran while one was open for 1% of the time, Pallas kernels for 26%

profile of v17, /device:TPU:0, one launch (start us, length us, event | category | flops | bytes accessed | tf_op | source)
XLA Modules:
  0.0 49.6 jit_solution(14913902173448232880)
XLA Ops:
  0.0 2.8 %shard_map.64 = (bf16[384,1536]{1,0:T(8,128)(2,1)}, bf16[384,512]{1,0:T(8,128)(2,1)}, bf16[16,2048]{1,0:T(8,128)(2,1)}, bf16[16,2048]{1,0:T(8,128)(2,1)}, bf16[16,2048]{1,0:T(8,128)(2,1)}) custom-call(bf16[384,2048]{1,0:T(8,128)(2,1)} %tokens_ref.3, bf16[16,8192]{1,0:T(8,128)(2,1)} %bitcast.5), custom_call_target="tpu_custom_call" | custom-call | tf_op jit(solution)/shard_map/pallas_call | solution.py:249
  3.3 2.6 %collective-permute-start.1 = (bf16[16,2048]{1,0:T(8,128)(2,1)}, bf16[16,2048]{1,0:T(8,128)(2,1)S(1)}, u32[]{:S(2)}, u32[]{:S(2)}) collective-permute-start(bf16[16,2048]{1,0:T(8,128)(2,1)} %get-tuple-element.49), channel_id=1, source_target_pairs={{0,2},{1,3},{2,0},{3,1},{4,6},{5,7},{6,4},{7,5},{8,10},{9,11},{10,... | collective-permute-start | bytes 196616 | tf_op jit(solution)/shard_map/ppermute | solution.py:25
  5.9 1.7 %collective-permute-start.7 = (bf16[384,1536]{1,0:T(8,128)(2,1)}, bf16[384,1536]{1,0:T(8,128)(2,1)}, u32[]{:S(2)}, u32[]{:S(2)}) collective-permute-start(bf16[384,1536]{1,0:T(8,128)(2,1)} %get-tuple-element.65), channel_id=1, source_target_pairs={{0,2},{1,3},{2,0},{3,1},{4,6},{5,7},{6,4},{7,5},{8,10},{9,11},{10,... | collective-permute-start | bytes 3538952 | tf_op jit(solution)/shard_map/ppermute | solution.py:25
  7.7 1.1 %collective-permute-done.1.refs_1_ = bf16[16,2048]{1,0:T(8,128)(2,1)S(1)} collective-permute-done((bf16[16,2048]{1,0:T(8,128)(2,1)}, bf16[16,2048]{1,0:T(8,128)(2,1)S(1)}, u32[]{:S(2)}, u32[]{:S(2)}) %collective-permute-start.1) | collective-permute-done | bytes 65568 | tf_op jit(solution)/shard_map/ppermute | solution.py:25
  8.8 1.4 %collective-permute-done.2.refs_2_ = bf16[16,2048]{1,0:T(8,128)(2,1)S(1)} collective-permute-done((bf16[16,2048]{1,0:T(8,128)(2,1)}, bf16[16,2048]{1,0:T(8,128)(2,1)S(1)}, u32[]{:S(2)}, u32[]{:S(2)}) %collective-permute-start.2) | collective-permute-done | bytes 65568 | tf_op jit(solution)/shard_map/ppermute | solution.py:25
  10.2 1.0 %shard_map.65.refs_0_ = bf16[64,2048]{1,0:T(8,128)(2,1)} custom-call(bf16[16,8192]{1,0:T(8,128)(2,1)S(1)} %bitcast.6, bf16[16,2048]{1,0:T(8,128)(2,1)S(1)} %collective-permute-done.refs_0_, bf16[16,2048]{1,0:T(8,128)(2,1)S(1)} %collective-permute-done.1.refs_1_, bf16[16,2048]{1,0:T(8,128)(2,1)S(1)} %collective-permute-done.2.refs_2_), custom_call_target="tpu_custom_call" | custom-call | tf_op jit(solution)/shard_map/pallas_call | solution.py:275
  11.7 2.6 %collective-permute-start.5 = (bf16[64,2048]{1,0:T(8,128)(2,1)}, bf16[64,2048]{1,0:T(8,128)(2,1)}, u32[]{:S(2)}, u32[]{:S(2)}) collective-permute-start(bf16[64,2048]{1,0:T(8,128)(2,1)} %shard_map.65.refs_0_), channel_id=1, source_target_pairs={{0,8},{4,12},{8,0},{12,4},{16,28},{20,24},{24,20},{28,16},{1,9},{5... | collective-permute-start | bytes 786440 | tf_op jit(solution)/shard_map/ppermute | solution.py:326
  14.3 3.4 %copy-done.2 = bf16[8192,512]{1,0:T(8,128)(2,1)S(1)} copy-done((bf16[8192,512]{1,0:T(8,128)(2,1)S(1)}, bf16[8192,512]{1,0:T(8,128)(2,1)}, u32[]{:S(2)}) %copy-start.2) | copy-done | bytes 8388632
  17.6 1.5 %shard_map.66 = (f32[384,512]{1,0:T(8,128)S(1)}, s32[1,384]{1,0:T(1,128)S(1)}) custom-call(s32[4]{0:T(128)S(1)} %copy-done.10, s32[1,384]{1,0:T(1,128)S(1)} %bitcast.10, bf16[8192,512]{1,0:T(8,128)(2,1)S(1)} %copy-done.2, bf16[384,2048]{1,0:T(8,128)(2,1)S(1)} %copy-done), custom_call_target="tpu_custom_call" | custom-call | flops 99999997952 | tf_op jit(solution)/shard_map/pallas_call | solution.py:337
  19.2 1.6 %collective-permute-start.6 = (bf16[64,512]{1,0:T(8,128)(2,1)S(1)}, bf16[64,512]{1,0:T(8,128)(2,1)S(1)}, u32[]{:S(2)}, u32[]{:S(2)}) collective-permute-start(bf16[64,512]{1,0:T(8,128)(2,1)S(1)} %bitcast.7), channel_id=1, source_target_pairs={{0,4},{4,0},{8,12},{12,8},{1,5},{5,1},{9,13},{13,9},{2,6},{6,2},{1... | collective-permute-start | bytes 196616 | tf_op jit(solution)/shard_map/ppermute | solution.py:25
  22.0 1.6 %collective-permute-start.9 = (bf16[64,2048]{1,0:T(8,128)(2,1)}, bf16[64,2048]{1,0:T(8,128)(2,1)S(1)}, u32[]{:S(2)}, u32[]{:S(2)}) collective-permute-start(bf16[64,2048]{1,0:T(8,128)(2,1)} %shard_map.65.refs_0_), channel_id=1, source_target_pairs={{0,4},{4,0},{8,12},{12,8},{1,5},{5,1},{9,13},{13,9},{2,6},{6,2},{1... | collective-permute-start | bytes 786440 | tf_op jit(solution)/shard_map/ppermute | solution.py:25
  23.7 1.7 %collective-permute-start.4 = (bf16[384,512]{1,0:T(8,128)(2,1)}, bf16[384,512]{1,0:T(8,128)(2,1)}, u32[]{:S(2)}, u32[]{:S(2)}) collective-permute-start(bf16[384,512]{1,0:T(8,128)(2,1)} %get-tuple-element.56), channel_id=1, source_target_pairs={{0,2},{1,3},{2,0},{3,1},{4,6},{5,7},{6,4},{7,5},{8,10},{9,11},{10,... | collective-permute-start | bytes 1179656 | tf_op jit(solution)/shard_map/ppermute | solution.py:25
  25.3 1.6 %collective-permute-done.5.refs_2_ = bf16[64,2048]{1,0:T(8,128)(2,1)} collective-permute-done((bf16[64,2048]{1,0:T(8,128)(2,1)}, bf16[64,2048]{1,0:T(8,128)(2,1)}, u32[]{:S(2)}, u32[]{:S(2)}) %collective-permute-start.5) | collective-permute-done | bytes 262176 | tf_op jit(solution)/shard_map/ppermute | solution.py:326
  27.0 1.2 %collective-permute-done.6.refs_6_ = bf16[64,512]{1,0:T(8,128)(2,1)S(1)} collective-permute-done((bf16[64,512]{1,0:T(8,128)(2,1)S(1)}, bf16[64,512]{1,0:T(8,128)(2,1)S(1)}, u32[]{:S(2)}, u32[]{:S(2)}) %collective-permute-start.6) | collective-permute-done | bytes 65568 | tf_op jit(solution)/shard_map/ppermute | solution.py:25
  28.2 1.9 %shard_map.68.refs_1_ = f32[384,512]{1,0:T(8,128)S(1)} custom-call(bf16[8192,512]{1,0:T(8,128)(2,1)S(1)} %copy-done.3, bf16[384,2048]{1,0:T(8,128)(2,1)S(1)} %collective-permute-done.3.refs_0_, f32[384,512]{1,0:T(8,128)S(1)} %shard_map.67.refs_1_), custom_call_target="tpu_custom_call" | custom-call | flops 99999997952 | tf_op jit(solution)/shard_map/pallas_call | solution.py:308
  30.1 2.0 %collective-permute-start.8 = (bf16[64,512]{1,0:T(8,128)(2,1)S(1)}, bf16[64,512]{1,0:T(8,128)(2,1)S(1)}, u32[]{:S(2)}, u32[]{:S(2)}) collective-permute-start(bf16[64,512]{1,0:T(8,128)(2,1)S(1)} %bitcast.8), channel_id=1, source_target_pairs={{0,8},{4,12},{8,0},{12,4},{16,28},{20,24},{24,20},{28,16},{1,9},{5... | collective-permute-start | bytes 196616 | tf_op jit(solution)/shard_map/ppermute | solution.py:326
  32.1 1.8 %collective-permute-done.9.refs_1_ = bf16[64,2048]{1,0:T(8,128)(2,1)S(1)} collective-permute-done((bf16[64,2048]{1,0:T(8,128)(2,1)}, bf16[64,2048]{1,0:T(8,128)(2,1)S(1)}, u32[]{:S(2)}, u32[]{:S(2)}) %collective-permute-start.9) | collective-permute-done | bytes 262176 | tf_op jit(solution)/shard_map/ppermute | solution.py:25
  33.9 1.9 %collective-permute-done.10.refs_3_ = bf16[64,2048]{1,0:T(8,128)(2,1)S(1)} collective-permute-done((bf16[64,2048]{1,0:T(8,128)(2,1)}, bf16[64,2048]{1,0:T(8,128)(2,1)S(1)}, u32[]{:S(2)}, u32[]{:S(2)}) %collective-permute-start.10) | collective-permute-done | bytes 262176 | tf_op jit(solution)/shard_map/ppermute | solution.py:25
  35.7 2.5 %shard_map.69 = f32[64,384]{1,0:T(8,128)S(1)} custom-call(bf16[384,2048]{1,0:T(8,128)(2,1)S(1)} %copy-done, s32[1,384]{1,0:T(1,128)S(1)} %get-tuple-element.66.stored_ref.refs_2_, bf16[64,2048]{1,0:T(8,128)(2,1)} %shard_map.65.refs_0_, bf16[64,2048]{1,0:T(8,128)(2,1)S(1)} %collective-permute-done.9.refs_1_, bf16[64,2048]{1,0:T(8,128)(2,1)} %collective-permute-done.5.refs_2_, ...), custom_call_target="tpu_custom_call" | custom-call | flops 99999997952 | tf_op jit(solution)/shard_map/pallas_call | solution.py:365
  38.8 2.2 %shard_map.70.refs_1_ = f32[384,512]{1,0:T(8,128)S(1)} custom-call(bf16[8192,512]{1,0:T(8,128)(2,1)S(1)} %copy-done.3, bf16[384,1536]{1,0:T(8,128)(2,1)} %collective-permute-done.7.refs_0_, f32[384,512]{1,0:T(8,128)S(1)} %shard_map.68.refs_1_), custom_call_target="tpu_custom_call" | custom-call | flops 99999997952 | tf_op jit(solution)/shard_map/pallas_call | solution.py:308
  42.0 1.4 %collective-permute-start.15 = (bf16[64,384]{1,0:T(8,128)(2,1)}, bf16[64,384]{1,0:T(8,128)(2,1)}, u32[]{:S(2)}, u32[]{:S(2)}) collective-permute-start(bf16[64,384]{1,0:T(8,128)(2,1)} %get-tuple-element.89), channel_id=1, source_target_pairs={{0,2},{1,3},{2,0},{3,1},{4,6},{5,7},{6,4},{7,5},{8,10},{9,11},{10,... | collective-permute-start | bytes 147464 | tf_op jit(solution)/shard_map/ppermute | solution.py:25
  43.4 1.4 %shard_map.71.refs_1_ = f32[384,512]{1,0:T(8,128)S(1)} custom-call(bf16[8192,512]{1,0:T(8,128)(2,1)S(1)} %copy-done.3, bf16[384,1536]{1,0:T(8,128)(2,1)S(1)} %collective-permute-done.12.refs_0_, f32[384,512]{1,0:T(8,128)S(1)} %shard_map.70.refs_1_), custom_call_target="tpu_custom_call" | custom-call | flops 99999997952 | tf_op jit(solution)/shard_map/pallas_call | solution.py:308
  45.3 1.4 %shard_map.72.refs_1_ = f32[384,512]{1,0:T(8,128)S(1)} custom-call(bf16[8192,512]{1,0:T(8,128)(2,1)S(1)} %copy-done.3, bf16[384,512]{1,0:T(8,128)(2,1)} %collective-permute-done.4.refs_0_, f32[384,512]{1,0:T(8,128)S(1)} %shard_map.71.refs_1_), custom_call_target="tpu_custom_call" | custom-call | flops 99999997952 | tf_op jit(solution)/shard_map/pallas_call | solution.py:308
  47.3 2.3 %shard_map.73 = bf16[384,512]{1,0:T(8,128)(2,1)} custom-call(bf16[8192,512]{1,0:T(8,128)(2,1)S(1)} %copy-done.3, bf16[384,512]{1,0:T(8,128)(2,1)S(1)} %collective-permute-done.14.refs_0_, f32[384,512]{1,0:T(8,128)S(1)} %shard_map.72.refs_1_, s32[1,384]{1,0:T(1,128)S(1)} %copy-done.12, f32[64,384]{1,0:T(8,128)S(1)} %get-tuple-element.83.refs_3_, ...), custom_call_target="tpu_custom_call" | custom-call | flops 99999997952 | tf_op jit(solution)/shard_map/pallas_call | solution.py:399
  (45 shorter events, 4.7 us)
Async XLA Ops:
  0.0 10.2 %copy-start.1 = (bf16[1,8192,16]{1,2,0:T(8,128)(2,1)S(1)}, bf16[1,8192,16]{1,2,0:T(8,128)(2,1)}, u32[]{:S(2)}) copy-start(bf16[1,8192,16]{1,2,0:T(8,128)(2,1)} %param.10) | copy-start | bytes 786436
  0.0 11.2 %copy-start = (bf16[384,2048]{1,0:T(8,128)(2,1)S(1)}, bf16[384,2048]{1,0:T(8,128)(2,1)}, u32[]{:S(2)}) copy-start(bf16[384,2048]{1,0:T(8,128)(2,1)} %tokens_ref.3) | copy-start | bytes 4718596
  0.0 14.2 %copy-start.9 = (s32[384,1]{0,1:T(1,128)S(1)}, s32[384,1]{0,1:T(1,128)}, u32[]{:S(2)}) copy-start(s32[384,1]{0,1:T(1,128)} %param.7) | copy-start | bytes 4612
  0.0 14.2 %copy-start.10 = (s32[4]{0:T(128)S(1)}, s32[4]{0:T(128)}, u32[]{:S(2)}) copy-start(s32[4]{0:T(128)} %placement_ref.1) | copy-start | bytes 52
  2.8 4.9 %collective-permute-start = (bf16[16,2048]{1,0:T(8,128)(2,1)}, bf16[16,2048]{1,0:T(8,128)(2,1)S(1)}, u32[]{:S(2)}, u32[]{:S(2)}) collective-permute-start(bf16[16,2048]{1,0:T(8,128)(2,1)} %get-tuple-element.47), channel_id=1, source_target_pairs={{0,1},{1,0},{2,3},{3,2},{4,5},{5,4},{6,7},{7,6},{8,9},{9,8},{10,11... | collective-permute-start | bytes 196616 | tf_op jit(solution)/shard_map/ppermute | solution.py:25
  3.3 5.5 %collective-permute-start.1 = (bf16[16,2048]{1,0:T(8,128)(2,1)}, bf16[16,2048]{1,0:T(8,128)(2,1)S(1)}, u32[]{:S(2)}, u32[]{:S(2)}) collective-permute-start(bf16[16,2048]{1,0:T(8,128)(2,1)} %get-tuple-element.49), channel_id=1, source_target_pairs={{0,2},{1,3},{2,0},{3,1},{4,6},{5,7},{6,4},{7,5},{8,10},{9,11},{10,... | collective-permute-start | bytes 196616 | tf_op jit(solution)/shard_map/ppermute | solution.py:25
  5.9 4.3 %collective-permute-start.2 = (bf16[16,2048]{1,0:T(8,128)(2,1)}, bf16[16,2048]{1,0:T(8,128)(2,1)S(1)}, u32[]{:S(2)}, u32[]{:S(2)}) collective-permute-start(bf16[16,2048]{1,0:T(8,128)(2,1)} %get-tuple-element.50), channel_id=1, source_target_pairs={{0,3},{1,2},{2,1},{3,0},{4,7},{5,6},{6,5},{7,4},{8,11},{9,10},{10,... | collective-permute-start | bytes 196616 | tf_op jit(solution)/shard_map/ppermute | solution.py:25
  5.9 32.3 %collective-permute-start.7 = (bf16[384,1536]{1,0:T(8,128)(2,1)}, bf16[384,1536]{1,0:T(8,128)(2,1)}, u32[]{:S(2)}, u32[]{:S(2)}) collective-permute-start(bf16[384,1536]{1,0:T(8,128)(2,1)} %get-tuple-element.65), channel_id=1, source_target_pairs={{0,2},{1,3},{2,0},{3,1},{4,6},{5,7},{6,4},{7,5},{8,10},{9,11},{10,... | collective-permute-start | bytes 3538952 | tf_op jit(solution)/shard_map/ppermute | solution.py:25
  11.3 7.9 %collective-permute-start.3 = (bf16[384,2048]{1,0:T(8,128)(2,1)S(1)}, bf16[384,2048]{1,0:T(8,128)(2,1)S(1)}, u32[]{:S(2)}, u32[]{:S(2)}) collective-permute-start(bf16[384,2048]{1,0:T(8,128)(2,1)S(1)} %copy-done), channel_id=1, source_target_pairs={{0,1},{1,0},{2,3},{3,2},{4,5},{5,4},{6,7},{7,6},{8,9},{9,8},{10,11... | collective-permute-start | bytes 4718600 | tf_op jit(solution)/shard_map/ppermute | solution.py:25
  11.7 15.3 %collective-permute-start.5 = (bf16[64,2048]{1,0:T(8,128)(2,1)}, bf16[64,2048]{1,0:T(8,128)(2,1)}, u32[]{:S(2)}, u32[]{:S(2)}) collective-permute-start(bf16[64,2048]{1,0:T(8,128)(2,1)} %shard_map.65.refs_0_), channel_id=1, source_target_pairs={{0,8},{4,12},{8,0},{12,4},{16,28},{20,24},{24,20},{28,16},{1,9},{5... | collective-permute-start | bytes 786440 | tf_op jit(solution)/shard_map/ppermute | solution.py:326
  14.3 3.4 %copy-start.2 = (bf16[8192,512]{1,0:T(8,128)(2,1)S(1)}, bf16[8192,512]{1,0:T(8,128)(2,1)}, u32[]{:S(2)}) copy-start(bf16[8192,512]{1,0:T(8,128)(2,1)} %weight_ref.13) | copy-start | bytes 25165828
  17.6 3.4 %copy-start.3 = (bf16[8192,512]{1,0:T(8,128)(2,1)S(1)}, bf16[8192,512]{1,0:T(8,128)(2,1)}, u32[]{:S(2)}) copy-start(bf16[8192,512]{1,0:T(8,128)(2,1)} %weight_ref.13) | copy-start | bytes 25165828
  19.2 16.6 %copy-start.11 = (s32[1,384]{1,0:T(1,128)}, s32[1,384]{1,0:T(1,128)S(1)}, u32[]{:S(2)}) copy-start(s32[1,384]{1,0:T(1,128)S(1)} %get-tuple-element.66.stored_ref.refs_2_) | copy-start | bytes 4612
  19.2 9.0 %collective-permute-start.6 = (bf16[64,512]{1,0:T(8,128)(2,1)S(1)}, bf16[64,512]{1,0:T(8,128)(2,1)S(1)}, u32[]{:S(2)}, u32[]{:S(2)}) collective-permute-start(bf16[64,512]{1,0:T(8,128)(2,1)S(1)} %bitcast.7), channel_id=1, source_target_pairs={{0,4},{4,0},{8,12},{12,8},{1,5},{5,1},{9,13},{13,9},{2,6},{6,2},{1... | collective-permute-start | bytes 196616 | tf_op jit(solution)/shard_map/ppermute | solution.py:25
  22.0 8.0 %copy-start.5 = (bf16[1,64,512]{2,1,0:T(8,128)(2,1)S(1)}, bf16[1,64,512]{2,1,0:T(8,128)(2,1)}, u32[]{:S(2)}) copy-start(bf16[1,64,512]{2,1,0:T(8,128)(2,1)} %param.11) | copy-start | bytes 196612
  22.0 11.8 %collective-permute-start.9 = (bf16[64,2048]{1,0:T(8,128)(2,1)}, bf16[64,2048]{1,0:T(8,128)(2,1)S(1)}, u32[]{:S(2)}, u32[]{:S(2)}) collective-permute-start(bf16[64,2048]{1,0:T(8,128)(2,1)} %shard_map.65.refs_0_), channel_id=1, source_target_pairs={{0,4},{4,0},{8,12},{12,8},{1,5},{5,1},{9,13},{13,9},{2,6},{6,2},{1... | collective-permute-start | bytes 786440 | tf_op jit(solution)/shard_map/ppermute | solution.py:25
  23.7 21.7 %collective-permute-start.4 = (bf16[384,512]{1,0:T(8,128)(2,1)}, bf16[384,512]{1,0:T(8,128)(2,1)}, u32[]{:S(2)}, u32[]{:S(2)}) collective-permute-start(bf16[384,512]{1,0:T(8,128)(2,1)} %get-tuple-element.56), channel_id=1, source_target_pairs={{0,2},{1,3},{2,0},{3,1},{4,6},{5,7},{6,4},{7,5},{8,10},{9,11},{10,... | collective-permute-start | bytes 1179656 | tf_op jit(solution)/shard_map/ppermute | solution.py:25
  28.2 7.6 %collective-permute-start.10 = (bf16[64,2048]{1,0:T(8,128)(2,1)}, bf16[64,2048]{1,0:T(8,128)(2,1)S(1)}, u32[]{:S(2)}, u32[]{:S(2)}) collective-permute-start(bf16[64,2048]{1,0:T(8,128)(2,1)} %collective-permute-done.5.refs_2_), channel_id=1, source_target_pairs={{0,16},{16,0},{1,17},{17,1},{2,18},{18,2},{3,19},{19,3},{4,20},{20... | collective-permute-start | bytes 786440 | tf_op jit(solution)/shard_map/ppermute | solution.py:25
  30.1 8.1 %collective-permute-start.8 = (bf16[64,512]{1,0:T(8,128)(2,1)S(1)}, bf16[64,512]{1,0:T(8,128)(2,1)S(1)}, u32[]{:S(2)}, u32[]{:S(2)}) collective-permute-start(bf16[64,512]{1,0:T(8,128)(2,1)S(1)} %bitcast.8), channel_id=1, source_target_pairs={{0,8},{4,12},{8,0},{12,4},{16,28},{20,24},{24,20},{28,16},{1,9},{5... | collective-permute-start | bytes 196616 | tf_op jit(solution)/shard_map/ppermute | solution.py:326
  38.2 3.1 %collective-permute-start.13 = (f32[64,384]{1,0:T(8,128)S(1)}, f32[64,384]{1,0:T(8,128)S(1)}, u32[]{:S(2)}, u32[]{:S(2)}) collective-permute-start(f32[64,384]{1,0:T(8,128)S(1)} %shard_map.69), channel_id=1, source_target_pairs={{0,1},{1,0},{2,3},{3,2},{4,5},{5,4},{6,7},{7,6},{8,9},{9,8},{10,11... | collective-permute-start | bytes 294920 | tf_op jit(solution)/shard_map/ppermute | solution.py:25
  38.3 5.1 %collective-permute-start.12 = (bf16[384,1536]{1,0:T(8,128)(2,1)}, bf16[384,1536]{1,0:T(8,128)(2,1)S(1)}, u32[]{:S(2)}, u32[]{:S(2)}) collective-permute-start(bf16[384,1536]{1,0:T(8,128)(2,1)} %collective-permute-done.7.refs_0_), channel_id=1, source_target_pairs={{0,1},{1,0},{2,3},{3,2},{4,5},{5,4},{6,7},{7,6},{8,9},{9,8},{10,11... | collective-permute-start | bytes 3538952 | tf_op jit(solution)/shard_map/ppermute | solution.py:25
  41.0 4.3 %collective-permute-start.11 = (bf16[64,512]{1,0:T(8,128)(2,1)S(1)}, bf16[64,512]{1,0:T(8,128)(2,1)S(1)}, u32[]{:S(2)}, u32[]{:S(2)}) collective-permute-start(bf16[64,512]{1,0:T(8,128)(2,1)S(1)} %collective-permute-done.8.refs_7_), channel_id=1, source_target_pairs={{0,16},{16,0},{1,17},{17,1},{2,18},{18,2},{3,19},{19,3},{4,20},{20... | collective-permute-start | bytes 196616 | tf_op jit(solution)/shard_map/ppermute | solution.py:25
  42.0 4.8 %collective-permute-start.15 = (bf16[64,384]{1,0:T(8,128)(2,1)}, bf16[64,384]{1,0:T(8,128)(2,1)}, u32[]{:S(2)}, u32[]{:S(2)}) collective-permute-start(bf16[64,384]{1,0:T(8,128)(2,1)} %get-tuple-element.89), channel_id=1, source_target_pairs={{0,2},{1,3},{2,0},{3,1},{4,6},{5,7},{6,4},{7,5},{8,10},{9,11},{10,... | collective-permute-start | bytes 147464 | tf_op jit(solution)/shard_map/ppermute | solution.py:25
  45.3 1.9 %collective-permute-start.14 = (bf16[384,512]{1,0:T(8,128)(2,1)}, bf16[384,512]{1,0:T(8,128)(2,1)S(1)}, u32[]{:S(2)}, u32[]{:S(2)}) collective-permute-start(bf16[384,512]{1,0:T(8,128)(2,1)} %collective-permute-done.4.refs_0_), channel_id=1, source_target_pairs={{0,1},{1,0},{2,3},{3,2},{4,5},{5,4},{6,7},{7,6},{8,9},{9,8},{10,11... | collective-permute-start | bytes 1179656 | tf_op jit(solution)/shard_map/ppermute | solution.py:25
  (5 other events, 10.7 us)

commit v18 on v16

--- a/solution.py
+++ b/solution.py
@@ -327,13 +327,12 @@
     far.append(send(1))
     single, single_up = fetch_near(own), fetch_near(up)
     total = products([(0, depth // 2, depth // 2, depth // 2)], [here], total)
-    fetched, single_up, total, up = chained(fetched, single_up, total, up)
+    fetched, single_up, total = chained(fetched, single_up, total)
     swapped = swap(fetched)
-    fetched_up = fetch_far(up)
     total, neighbour = chained(total, neighbour)
     total = products([(1, 0, 0, depth)], [neighbour], total)
-    fetched_up, total = chained(fetched_up, total)
-    swapped_up = swap(fetched_up)
+    total, up = chained(total, up)
+    fetched_up = fetch_far(up)
     single, swapped, total = chained(single, swapped, total)
     downs = [own] + single
     for pair in zip(fetched, swapped):
@@ -351,7 +350,8 @@
             pltpu.SemaphoreType.DMA((1 + slots, tiles)),
         ],
     )(tokens, stored, *downs)
-    far[0], partial = chained(far[0], partial)
+    far[0], fetched_up, partial = chained(far[0], fetched_up, partial)
+    swapped_up = swap(fetched_up)
     ups = [up] + single_up
     for pair in zip(fetched_up, swapped_up):
         ups += pair

time: 48.7 us -> 48.3 us (level)
  waiting for transfers between devices: 11.1 us -> 8.15 us
  starting transfers between devices: 14.6 us -> 17.3 us
    ppermute x2, waiting for transfers between devices: 5.69 us -> 2.41 us  [fetch_far(): lax.ppermute(value, ('parts', 'adapter'), route)]
    ppermute x2, starting transfers between devices: 2.66 us -> 4.59 us  [fetch_far(): lax.ppermute(value, ('parts', 'adapter'), route)]
    ppermute x14, starting transfers between devices: 11.9 us -> 12.7 us  [flipped(): return lax.ppermute(value, axis, [(i, i ^ flip) for i in range(count)])]
    unnamed x18 -> x14, local copies, waits for them, and re-layouts: 3.64 us -> 3.6 us
  transfers between devices with their start and end apart: 16 -> 16, of which waited for: 7 -> 5; matrix products, arithmetic and copies ran while one was open for 1% -> 1% of each run, Pallas kernels for 31% -> 31%
where the time goes in v18:
time: 48.3 us; the launch traced here: 47.9 us
  starting transfers between devices  17.3 us (36%)
  Pallas kernels  17 us (35%)
  waiting for transfers between devices  8.15 us (17%)
  local copies, waits for them, and re-layouts  4.67 us (10%)
  other arithmetic  0.63 us (1%)
    ppermute x14, starting transfers between devices, flipped(): return lax.ppermute(value, axis, [(i, i ^ flip) for i in range(count)])  12.7 us
    pallas_call x5, Pallas kernels, products(): call(functools.partial(products_kernel, tile, depth, places), jax.ShapeDt...  7.87 us
    ppermute x14, waiting for transfers between devices, flipped(): return lax.ppermute(value, axis, [(i, i ^ flip) for i in range(count)])  5.74 us
    ppermute x2, starting transfers between devices, fetch_far(): lax.ppermute(value, ('parts', 'adapter'), route)  4.59 us
    unnamed x14, local copies, waits for them, and re-layouts  3.6 us
    pallas_call x1, Pallas kernels, body(): call(functools.partial(shrink_kernel, tile, flips, pairs, slots), jax.Sha...  2.47 us
    ppermute x2, waiting for transfers between devices, fetch_far(): lax.ppermute(value, ('parts', 'adapter'), route)  2.41 us
    pallas_call x1, Pallas kernels, body(): call(functools.partial(cut_kernel, edges), [jax.ShapeDtypeStruct((rows, b...  2.23 us
  transfers between devices with their start and end apart: 16, of which 5 were waited for; matrix products, arithmetic and copies ran while one was open for 1% of the time, Pallas kernels for 31%

profile of v18, /device:TPU:0, one launch (start us, length us, event | category | flops | bytes accessed | tf_op | source)
XLA Modules:
  0.0 47.9 jit_solution(6714773845437252550)
XLA Ops:
  0.0 1.1 %dynamic-slice_bitcast_fusion = (bf16[16,2048]{1,0:T(8,128)(2,1)S(1)}, bf16[16,2048]{1,0:T(8,128)(2,1)S(1)}, bf16[16,2048]{1,0:T(8,128)(2,1)S(1)}, bf16[16,2048]{1,0:T(8,128)(2,1)S(1)}) fusion(bf16[1,8192,16]{1,2,0:T(8,128)(2,1)} %param.10, s32[]{:T(128)S(6)} %select_n.15, s32[]{:T(128)S(6)} %select_n.13, s32[]{:T(128)S(6)} %select_n.12, s32[]{:T(128)S(6)} %select_n.14), kind=kLoop, calls=%fused_computation | loop fusion | bytes 524304 | tf_op jit(solution)/shard_map/dynamic_slice | solution.py:230
  1.6 2.6 %collective-permute-start.1 = (bf16[16,2048]{1,0:T(8,128)(2,1)S(1)}, bf16[16,2048]{1,0:T(8,128)(2,1)S(1)}, u32[]{:S(2)}, u32[]{:S(2)}) collective-permute-start(bf16[16,2048]{1,0:T(8,128)(2,1)S(1)} %get-tuple-element.52), channel_id=1, source_target_pairs={{0,2},{1,3},{2,0},{3,1},{4,6},{5,7},{6,4},{7,5},{8,10},{9,11},{10,... | collective-permute-start | bytes 196616 | tf_op jit(solution)/shard_map/ppermute | solution.py:25
  4.3 2.2 %shard_map.66 = (bf16[384,1536]{1,0:T(8,128)(2,1)}, bf16[384,512]{1,0:T(8,128)(2,1)}) custom-call(bf16[384,2048]{1,0:T(8,128)(2,1)} %tokens_ref.1), custom_call_target="tpu_custom_call" | custom-call | tf_op jit(solution)/shard_map/pallas_call | solution.py:236
  6.5 1.8 %collective-permute-start.7 = (bf16[384,1536]{1,0:T(8,128)(2,1)}, bf16[384,1536]{1,0:T(8,128)(2,1)}, u32[]{:S(2)}, u32[]{:S(2)}) collective-permute-start(bf16[384,1536]{1,0:T(8,128)(2,1)} %get-tuple-element.69), channel_id=1, source_target_pairs={{0,2},{1,3},{2,0},{3,1},{4,6},{5,7},{6,4},{7,5},{8,10},{9,11},{10,... | collective-permute-start | bytes 3538952 | tf_op jit(solution)/shard_map/ppermute | solution.py:25
  9.1 2.7 %collective-permute-start.5 = (bf16[64,2048]{1,0:T(8,128)(2,1)}, bf16[64,2048]{1,0:T(8,128)(2,1)}, u32[]{:S(2)}, u32[]{:S(2)}) collective-permute-start(bf16[64,2048]{1,0:T(8,128)(2,1)} %shard_map.64.refs_0_), channel_id=1, source_target_pairs={{0,8},{4,12},{8,0},{12,4},{16,28},{20,24},{24,20},{28,16},{1,9},{5... | collective-permute-start | bytes 786440 | tf_op jit(solution)/shard_map/ppermute | solution.py:303
  11.8 3.4 %copy-done.1 = bf16[8192,512]{1,0:T(8,128)(2,1)S(1)} copy-done((bf16[8192,512]{1,0:T(8,128)(2,1)S(1)}, bf16[8192,512]{1,0:T(8,128)(2,1)}, u32[]{:S(2)}) %copy-start.1) | copy-done | bytes 8388632
  15.2 1.5 %shard_map.65 = (f32[384,512]{1,0:T(8,128)S(1)}, s32[1,384]{1,0:T(1,128)S(1)}) custom-call(s32[4]{0:T(128)S(1)} %copy-done.4, s32[1,384]{1,0:T(1,128)S(1)} %bitcast.18, bf16[8192,512]{1,0:T(8,128)(2,1)S(1)} %copy-done.1, bf16[384,2048]{1,0:T(8,128)(2,1)S(1)} %copy-done), custom_call_target="tpu_custom_call" | custom-call | flops 99999997952 | tf_op jit(solution)/shard_map/pallas_call | solution.py:314
  16.7 1.6 %collective-permute-start.6 = (bf16[64,512]{1,0:T(8,128)(2,1)}, bf16[64,512]{1,0:T(8,128)(2,1)S(1)}, u32[]{:S(2)}, u32[]{:S(2)}) collective-permute-start(bf16[64,512]{1,0:T(8,128)(2,1)} %bitcast.9.refs_5_), channel_id=1, source_target_pairs={{0,4},{4,0},{8,12},{12,8},{1,5},{5,1},{9,13},{13,9},{2,6},{6,2},{1... | collective-permute-start | bytes 196616 | tf_op jit(solution)/shard_map/ppermute | solution.py:25
  18.5 1.0 %shard_map.67.refs_1_ = f32[384,512]{1,0:T(8,128)S(1)} custom-call(bf16[8192,512]{1,0:T(8,128)(2,1)S(1)} %copy-done.2, bf16[384,2048]{1,0:T(8,128)(2,1)S(1)} %copy-done, f32[384,512]{1,0:T(8,128)S(1)} %get-tuple-element.62.refs_1_), custom_call_target="tpu_custom_call" | custom-call | flops 99999997952 | tf_op jit(solution)/shard_map/pallas_call | solution.py:285
  19.5 1.6 %collective-permute-start.9 = (bf16[64,2048]{1,0:T(8,128)(2,1)}, bf16[64,2048]{1,0:T(8,128)(2,1)S(1)}, u32[]{:S(2)}, u32[]{:S(2)}) collective-permute-start(bf16[64,2048]{1,0:T(8,128)(2,1)} %shard_map.64.refs_0_), channel_id=1, source_target_pairs={{0,4},{4,0},{8,12},{12,8},{1,5},{5,1},{9,13},{13,9},{2,6},{6,2},{1... | collective-permute-start | bytes 786440 | tf_op jit(solution)/shard_map/ppermute | solution.py:25
  21.1 1.2 %collective-permute-start.4 = (bf16[384,512]{1,0:T(8,128)(2,1)}, bf16[384,512]{1,0:T(8,128)(2,1)}, u32[]{:S(2)}, u32[]{:S(2)}) collective-permute-start(bf16[384,512]{1,0:T(8,128)(2,1)} %get-tuple-element.60), channel_id=1, source_target_pairs={{0,2},{1,3},{2,0},{3,1},{4,6},{5,7},{6,4},{7,5},{8,10},{9,11},{10,... | collective-permute-start | bytes 1179656 | tf_op jit(solution)/shard_map/ppermute | solution.py:25
  22.4 2.4 %collective-permute-done.5.refs_2_ = bf16[64,2048]{1,0:T(8,128)(2,1)} collective-permute-done((bf16[64,2048]{1,0:T(8,128)(2,1)}, bf16[64,2048]{1,0:T(8,128)(2,1)}, u32[]{:S(2)}, u32[]{:S(2)}) %collective-permute-start.5) | collective-permute-done | bytes 262176 | tf_op jit(solution)/shard_map/ppermute | solution.py:303
  24.8 1.2 %collective-permute-done.6.refs_6_ = bf16[64,512]{1,0:T(8,128)(2,1)S(1)} collective-permute-done((bf16[64,512]{1,0:T(8,128)(2,1)}, bf16[64,512]{1,0:T(8,128)(2,1)S(1)}, u32[]{:S(2)}, u32[]{:S(2)}) %collective-permute-start.6) | collective-permute-done | bytes 65568 | tf_op jit(solution)/shard_map/ppermute | solution.py:25
  26.0 1.9 %shard_map.68.refs_1_ = f32[384,512]{1,0:T(8,128)S(1)} custom-call(bf16[8192,512]{1,0:T(8,128)(2,1)S(1)} %copy-done.2, bf16[384,2048]{1,0:T(8,128)(2,1)S(1)} %collective-permute-done.3.refs_0_, f32[384,512]{1,0:T(8,128)S(1)} %shard_map.67.refs_1_), custom_call_target="tpu_custom_call" | custom-call | flops 99999997952 | tf_op jit(solution)/shard_map/pallas_call | solution.py:285
  27.9 1.9 %collective-permute-start.8 = (bf16[64,512]{1,0:T(8,128)(2,1)}, bf16[64,512]{1,0:T(8,128)(2,1)S(1)}, u32[]{:S(2)}, u32[]{:S(2)}) collective-permute-start(bf16[64,512]{1,0:T(8,128)(2,1)} %bitcast.9.refs_5_), channel_id=1, source_target_pairs={{0,8},{4,12},{8,0},{12,4},{16,28},{20,24},{24,20},{28,16},{1,9},{5... | collective-permute-start | bytes 196616 | tf_op jit(solution)/shard_map/ppermute | solution.py:303
  29.8 1.8 %collective-permute-done.9.refs_1_ = bf16[64,2048]{1,0:T(8,128)(2,1)S(1)} collective-permute-done((bf16[64,2048]{1,0:T(8,128)(2,1)}, bf16[64,2048]{1,0:T(8,128)(2,1)S(1)}, u32[]{:S(2)}, u32[]{:S(2)}) %collective-permute-start.9) | collective-permute-done | bytes 262176 | tf_op jit(solution)/shard_map/ppermute | solution.py:25
  31.6 2.3 %collective-permute-done.10.refs_3_ = bf16[64,2048]{1,0:T(8,128)(2,1)S(1)} collective-permute-done((bf16[64,2048]{1,0:T(8,128)(2,1)}, bf16[64,2048]{1,0:T(8,128)(2,1)S(1)}, u32[]{:S(2)}, u32[]{:S(2)}) %collective-permute-start.10) | collective-permute-done | bytes 262176 | tf_op jit(solution)/shard_map/ppermute | solution.py:25
  33.8 2.5 %shard_map.69 = f32[64,384]{1,0:T(8,128)S(1)} custom-call(bf16[384,2048]{1,0:T(8,128)(2,1)S(1)} %copy-done, s32[1,384]{1,0:T(1,128)S(1)} %get-tuple-element.70.stored_ref.refs_2_, bf16[64,2048]{1,0:T(8,128)(2,1)} %shard_map.64.refs_0_, bf16[64,2048]{1,0:T(8,128)(2,1)S(1)} %collective-permute-done.9.refs_1_, bf16[64,2048]{1,0:T(8,128)(2,1)} %collective-permute-done.5.refs_2_, ...), custom_call_target="tpu_custom_call" | custom-call | flops 99999997952 | tf_op jit(solution)/shard_map/pallas_call | solution.py:342
  36.9 2.2 %shard_map.70.refs_1_ = f32[384,512]{1,0:T(8,128)S(1)} custom-call(bf16[8192,512]{1,0:T(8,128)(2,1)S(1)} %copy-done.2, bf16[384,1536]{1,0:T(8,128)(2,1)} %collective-permute-done.7.refs_0_, f32[384,512]{1,0:T(8,128)S(1)} %shard_map.68.refs_1_), custom_call_target="tpu_custom_call" | custom-call | flops 99999997952 | tf_op jit(solution)/shard_map/pallas_call | solution.py:285
  39.1 1.1 %collective-permute-start.11 = (bf16[64,512]{1,0:T(8,128)(2,1)S(1)}, bf16[64,512]{1,0:T(8,128)(2,1)S(1)}, u32[]{:S(2)}, u32[]{:S(2)}) collective-permute-start(bf16[64,512]{1,0:T(8,128)(2,1)S(1)} %collective-permute-done.8.refs_7_), channel_id=1, source_target_pairs={{0,16},{16,0},{1,17},{17,1},{2,18},{18,2},{3,19},{19,3},{4,20},{20... | collective-permute-start | bytes 196616 | tf_op jit(solution)/shard_map/ppermute | solution.py:25
  40.8 1.5 %collective-permute-start.15 = (bf16[64,384]{1,0:T(8,128)(2,1)}, bf16[64,384]{1,0:T(8,128)(2,1)}, u32[]{:S(2)}, u32[]{:S(2)}) collective-permute-start(bf16[64,384]{1,0:T(8,128)(2,1)} %get-tuple-element.93), channel_id=1, source_target_pairs={{0,2},{1,3},{2,0},{3,1},{4,6},{5,7},{6,4},{7,5},{8,10},{9,11},{10,... | collective-permute-start | bytes 147464 | tf_op jit(solution)/shard_map/ppermute | solution.py:25
  42.3 1.4 %shard_map.71.refs_1_ = f32[384,512]{1,0:T(8,128)S(1)} custom-call(bf16[8192,512]{1,0:T(8,128)(2,1)S(1)} %copy-done.2, bf16[384,1536]{1,0:T(8,128)(2,1)S(1)} %collective-permute-done.12.refs_0_, f32[384,512]{1,0:T(8,128)S(1)} %shard_map.70.refs_1_), custom_call_target="tpu_custom_call" | custom-call | flops 99999997952 | tf_op jit(solution)/shard_map/pallas_call | solution.py:285
  43.9 1.4 %shard_map.72.refs_1_ = f32[384,512]{1,0:T(8,128)S(1)} custom-call(bf16[8192,512]{1,0:T(8,128)(2,1)S(1)} %copy-done.2, bf16[384,512]{1,0:T(8,128)(2,1)} %collective-permute-done.4.refs_0_, f32[384,512]{1,0:T(8,128)S(1)} %shard_map.71.refs_1_), custom_call_target="tpu_custom_call" | custom-call | flops 99999997952 | tf_op jit(solution)/shard_map/pallas_call | solution.py:285
  45.8 2.2 %shard_map.73 = bf16[384,512]{1,0:T(8,128)(2,1)} custom-call(bf16[8192,512]{1,0:T(8,128)(2,1)S(1)} %copy-done.2, bf16[384,512]{1,0:T(8,128)(2,1)S(1)} %collective-permute-done.14.refs_0_, f32[384,512]{1,0:T(8,128)S(1)} %shard_map.72.refs_1_, s32[1,384]{1,0:T(1,128)S(1)} %copy-done.6, f32[64,384]{1,0:T(8,128)S(1)} %get-tuple-element.87.refs_3_, ...), custom_call_target="tpu_custom_call" | custom-call | flops 99999997952 | tf_op jit(solution)/shard_map/pallas_call | solution.py:376
  (34 shorter events, 3.4 us)
Async XLA Ops:
  0.0 8.3 %copy-start = (bf16[384,2048]{1,0:T(8,128)(2,1)S(1)}, bf16[384,2048]{1,0:T(8,128)(2,1)}, u32[]{:S(2)}) copy-start(bf16[384,2048]{1,0:T(8,128)(2,1)} %tokens_ref.1) | copy-start | bytes 4718596
  0.0 11.8 %copy-start.3 = (s32[384,1]{0,1:T(1,128)S(1)}, s32[384,1]{0,1:T(1,128)}, u32[]{:S(2)}) copy-start(s32[384,1]{0,1:T(1,128)} %param.7) | copy-start | bytes 4612
  0.0 11.8 %copy-start.4 = (s32[4]{0:T(128)S(1)}, s32[4]{0:T(128)}, u32[]{:S(2)}) copy-start(s32[4]{0:T(128)} %placement_ref.1) | copy-start | bytes 52
  1.1 7.2 %collective-permute-start = (bf16[16,2048]{1,0:T(8,128)(2,1)S(1)}, bf16[16,2048]{1,0:T(8,128)(2,1)S(1)}, u32[]{:S(2)}, u32[]{:S(2)}) collective-permute-start(bf16[16,2048]{1,0:T(8,128)(2,1)S(1)} %get-tuple-element.50), channel_id=1, source_target_pairs={{0,1},{1,0},{2,3},{3,2},{4,5},{5,4},{6,7},{7,6},{8,9},{9,8},{10,11... | collective-permute-start | bytes 196616 | tf_op jit(solution)/shard_map/ppermute | solution.py:25
  1.6 6.7 %collective-permute-start.1 = (bf16[16,2048]{1,0:T(8,128)(2,1)S(1)}, bf16[16,2048]{1,0:T(8,128)(2,1)S(1)}, u32[]{:S(2)}, u32[]{:S(2)}) collective-permute-start(bf16[16,2048]{1,0:T(8,128)(2,1)S(1)} %get-tuple-element.52), channel_id=1, source_target_pairs={{0,2},{1,3},{2,0},{3,1},{4,6},{5,7},{6,4},{7,5},{8,10},{9,11},{10,... | collective-permute-start | bytes 196616 | tf_op jit(solution)/shard_map/ppermute | solution.py:25
  4.2 4.2 %collective-permute-start.2 = (bf16[16,2048]{1,0:T(8,128)(2,1)S(1)}, bf16[16,2048]{1,0:T(8,128)(2,1)S(1)}, u32[]{:S(2)}, u32[]{:S(2)}) collective-permute-start(bf16[16,2048]{1,0:T(8,128)(2,1)S(1)} %get-tuple-element.53), channel_id=1, source_target_pairs={{0,3},{1,2},{2,1},{3,0},{4,7},{5,6},{6,5},{7,4},{8,11},{9,10},{10,... | collective-permute-start | bytes 196616 | tf_op jit(solution)/shard_map/ppermute | solution.py:25
  6.5 29.8 %collective-permute-start.7 = (bf16[384,1536]{1,0:T(8,128)(2,1)}, bf16[384,1536]{1,0:T(8,128)(2,1)}, u32[]{:S(2)}, u32[]{:S(2)}) collective-permute-start(bf16[384,1536]{1,0:T(8,128)(2,1)} %get-tuple-element.69), channel_id=1, source_target_pairs={{0,2},{1,3},{2,0},{3,1},{4,6},{5,7},{6,4},{7,5},{8,10},{9,11},{10,... | collective-permute-start | bytes 3538952 | tf_op jit(solution)/shard_map/ppermute | solution.py:25
  8.3 8.4 %collective-permute-start.3 = (bf16[384,2048]{1,0:T(8,128)(2,1)S(1)}, bf16[384,2048]{1,0:T(8,128)(2,1)S(1)}, u32[]{:S(2)}, u32[]{:S(2)}) collective-permute-start(bf16[384,2048]{1,0:T(8,128)(2,1)S(1)} %copy-done), channel_id=1, source_target_pairs={{0,1},{1,0},{2,3},{3,2},{4,5},{5,4},{6,7},{7,6},{8,9},{9,8},{10,11... | collective-permute-start | bytes 4718600 | tf_op jit(solution)/shard_map/ppermute | solution.py:25
  9.1 15.7 %collective-permute-start.5 = (bf16[64,2048]{1,0:T(8,128)(2,1)}, bf16[64,2048]{1,0:T(8,128)(2,1)}, u32[]{:S(2)}, u32[]{:S(2)}) collective-permute-start(bf16[64,2048]{1,0:T(8,128)(2,1)} %shard_map.64.refs_0_), channel_id=1, source_target_pairs={{0,8},{4,12},{8,0},{12,4},{16,28},{20,24},{24,20},{28,16},{1,9},{5... | collective-permute-start | bytes 786440 | tf_op jit(solution)/shard_map/ppermute | solution.py:303
  11.8 3.4 %copy-start.1 = (bf16[8192,512]{1,0:T(8,128)(2,1)S(1)}, bf16[8192,512]{1,0:T(8,128)(2,1)}, u32[]{:S(2)}) copy-start(bf16[8192,512]{1,0:T(8,128)(2,1)} %weight_ref.13) | copy-start | bytes 25165828
  15.2 3.4 %copy-start.2 = (bf16[8192,512]{1,0:T(8,128)(2,1)S(1)}, bf16[8192,512]{1,0:T(8,128)(2,1)}, u32[]{:S(2)}) copy-start(bf16[8192,512]{1,0:T(8,128)(2,1)} %weight_ref.13) | copy-start | bytes 25165828
  16.7 17.2 %copy-start.5 = (s32[1,384]{1,0:T(1,128)}, s32[1,384]{1,0:T(1,128)S(1)}, u32[]{:S(2)}) copy-start(s32[1,384]{1,0:T(1,128)S(1)} %get-tuple-element.70.stored_ref.refs_2_) | copy-start | bytes 4612
  16.7 9.3 %collective-permute-start.6 = (bf16[64,512]{1,0:T(8,128)(2,1)}, bf16[64,512]{1,0:T(8,128)(2,1)S(1)}, u32[]{:S(2)}, u32[]{:S(2)}) collective-permute-start(bf16[64,512]{1,0:T(8,128)(2,1)} %bitcast.9.refs_5_), channel_id=1, source_target_pairs={{0,4},{4,0},{8,12},{12,8},{1,5},{5,1},{9,13},{13,9},{2,6},{6,2},{1... | collective-permute-start | bytes 196616 | tf_op jit(solution)/shard_map/ppermute | solution.py:25
  19.5 12.1 %collective-permute-start.9 = (bf16[64,2048]{1,0:T(8,128)(2,1)}, bf16[64,2048]{1,0:T(8,128)(2,1)S(1)}, u32[]{:S(2)}, u32[]{:S(2)}) collective-permute-start(bf16[64,2048]{1,0:T(8,128)(2,1)} %shard_map.64.refs_0_), channel_id=1, source_target_pairs={{0,4},{4,0},{8,12},{12,8},{1,5},{5,1},{9,13},{13,9},{2,6},{6,2},{1... | collective-permute-start | bytes 786440 | tf_op jit(solution)/shard_map/ppermute | solution.py:25
  21.1 22.6 %collective-permute-start.4 = (bf16[384,512]{1,0:T(8,128)(2,1)}, bf16[384,512]{1,0:T(8,128)(2,1)}, u32[]{:S(2)}, u32[]{:S(2)}) collective-permute-start(bf16[384,512]{1,0:T(8,128)(2,1)} %get-tuple-element.60), channel_id=1, source_target_pairs={{0,2},{1,3},{2,0},{3,1},{4,6},{5,7},{6,4},{7,5},{8,10},{9,11},{10,... | collective-permute-start | bytes 1179656 | tf_op jit(solution)/shard_map/ppermute | solution.py:25
  26.0 7.8 %collective-permute-start.10 = (bf16[64,2048]{1,0:T(8,128)(2,1)}, bf16[64,2048]{1,0:T(8,128)(2,1)S(1)}, u32[]{:S(2)}, u32[]{:S(2)}) collective-permute-start(bf16[64,2048]{1,0:T(8,128)(2,1)} %collective-permute-done.5.refs_2_), channel_id=1, source_target_pairs={{0,16},{16,0},{1,17},{17,1},{2,18},{18,2},{3,19},{19,3},{4,20},{20... | collective-permute-start | bytes 786440 | tf_op jit(solution)/shard_map/ppermute | solution.py:25
  27.9 8.4 %collective-permute-start.8 = (bf16[64,512]{1,0:T(8,128)(2,1)}, bf16[64,512]{1,0:T(8,128)(2,1)S(1)}, u32[]{:S(2)}, u32[]{:S(2)}) collective-permute-start(bf16[64,512]{1,0:T(8,128)(2,1)} %bitcast.9.refs_5_), channel_id=1, source_target_pairs={{0,8},{4,12},{8,0},{12,4},{16,28},{20,24},{24,20},{28,16},{1,9},{5... | collective-permute-start | bytes 196616 | tf_op jit(solution)/shard_map/ppermute | solution.py:303
  36.3 3.9 %collective-permute-start.13 = (f32[64,384]{1,0:T(8,128)S(1)}, f32[64,384]{1,0:T(8,128)S(1)}, u32[]{:S(2)}, u32[]{:S(2)}) collective-permute-start(f32[64,384]{1,0:T(8,128)S(1)} %shard_map.69), channel_id=1, source_target_pairs={{0,1},{1,0},{2,3},{3,2},{4,5},{5,4},{6,7},{7,6},{8,9},{9,8},{10,11... | collective-permute-start | bytes 294920 | tf_op jit(solution)/shard_map/ppermute | solution.py:25
  36.4 5.9 %collective-permute-start.12 = (bf16[384,1536]{1,0:T(8,128)(2,1)}, bf16[384,1536]{1,0:T(8,128)(2,1)S(1)}, u32[]{:S(2)}, u32[]{:S(2)}) collective-permute-start(bf16[384,1536]{1,0:T(8,128)(2,1)} %collective-permute-done.7.refs_0_), channel_id=1, source_target_pairs={{0,1},{1,0},{2,3},{3,2},{4,5},{5,4},{6,7},{7,6},{8,9},{9,8},{10,11... | collective-permute-start | bytes 3538952 | tf_op jit(solution)/shard_map/ppermute | solution.py:25
  39.1 4.6 %collective-permute-start.11 = (bf16[64,512]{1,0:T(8,128)(2,1)S(1)}, bf16[64,512]{1,0:T(8,128)(2,1)S(1)}, u32[]{:S(2)}, u32[]{:S(2)}) collective-permute-start(bf16[64,512]{1,0:T(8,128)(2,1)S(1)} %collective-permute-done.8.refs_7_), channel_id=1, source_target_pairs={{0,16},{16,0},{1,17},{17,1},{2,18},{18,2},{3,19},{19,3},{4,20},{20... | collective-permute-start | bytes 196616 | tf_op jit(solution)/shard_map/ppermute | solution.py:25
  40.8 4.5 %collective-permute-start.15 = (bf16[64,384]{1,0:T(8,128)(2,1)}, bf16[64,384]{1,0:T(8,128)(2,1)}, u32[]{:S(2)}, u32[]{:S(2)}) collective-permute-start(bf16[64,384]{1,0:T(8,128)(2,1)} %get-tuple-element.93), channel_id=1, source_target_pairs={{0,2},{1,3},{2,0},{3,1},{4,6},{5,7},{6,4},{7,5},{8,10},{9,11},{10,... | collective-permute-start | bytes 147464 | tf_op jit(solution)/shard_map/ppermute | solution.py:25
  43.7 2.0 %copy-start.6 = (s32[1,384]{1,0:T(1,128)S(1)}, s32[1,384]{1,0:T(1,128)}, u32[]{:S(2)}) copy-start(s32[1,384]{1,0:T(1,128)} %copy-done.5) | copy-start | bytes 4612
  43.8 2.0 %collective-permute-start.14 = (bf16[384,512]{1,0:T(8,128)(2,1)}, bf16[384,512]{1,0:T(8,128)(2,1)S(1)}, u32[]{:S(2)}, u32[]{:S(2)}) collective-permute-start(bf16[384,512]{1,0:T(8,128)(2,1)} %collective-permute-done.4.refs_0_), channel_id=1, source_target_pairs={{0,1},{1,0},{2,3},{3,2},{4,5},{5,4},{6,7},{7,6},{8,9},{9,8},{10,11... | collective-permute-start | bytes 1179656 | tf_op jit(solution)/shard_map/ppermute | solution.py:25

commit v19 on v18

--- a/solution.py
+++ b/solution.py
@@ -11,6 +11,8 @@
 LOWRANK_SCALE = 2.0
 CORES = 2
 LANES = 128
+FIRST = ((1, 3, 0, 2), (1, 2, 3, 0))
+SECOND = ((2, 0, 3, 1), (3, 0, 1, 2))
 CUTS = (0.75,)
 MIB = 1024 * 1024
 FREE = pl.CostEstimate(flops=0, bytes_accessed=0, transcendentals=0)
@@ -139,15 +141,27 @@
     add_tiles(held_ref, rows_ref, sems, out_ref)
 
 
-def owners_of(flips, pairs):
-    group, part = lax.axis_index("adapter"), lax.axis_index("parts")
-    owners = [group] + [group ^ flip for flip in flips]
-    for near, far in pairs:
-        owners += [group ^ (near + part * (far - near)), group ^ (far + part * (near - far))]
-    return owners
-
-
-def last_kernel(tile, depth, places, flips, pairs, slots, weight_ref, *refs):
+def is_mixed(groups, parts):
+    return groups == 4 and parts == 2
+
+
+def source(group, part, table):
+    found = 0
+    for p, targets in enumerate(table):
+        for z, target in enumerate(targets):
+            found = found + jnp.where((part == p) & (group == target), z, 0)
+    return found
+
+
+def owners_of(groups, mixed):
+    group = lax.axis_index("adapter")
+    if not mixed:
+        return [group ^ flip for flip in range(groups)]
+    part = lax.axis_index("parts")
+    return [group, source(group, part, FIRST), source(group, part, SECOND), group ^ (3 - part)]
+
+
+def last_kernel(tile, depth, places, slots, weight_ref, *refs):
     count = len(places)
     features = refs[:count]
     given, stored_ref, sum_ref, more_ref = refs[count : count + 4]
@@ -171,7 +185,7 @@
         copy.wait()
     shrunk = (sums_ref[...] + received_ref[...].astype(jnp.float32)).astype(jnp.bfloat16).astype(jnp.float32)
     spread = jnp.concatenate(
-        [jnp.where(stored_ref[...] == owner, shrunk, 0.0) for owner in owners_of(flips, pairs)], axis=0
+        [jnp.where(stored_ref[...] == owner, shrunk, 0.0) for owner in owners_of(slots, False)], axis=0
     )
     expanded = jnp.dot(
         spread.T.astype(jnp.bfloat16), stacked_ref[...], preferred_element_type=jnp.float32
@@ -180,7 +194,7 @@
     out_ref[...] = (total_ref[...] + LOWRANK_SCALE * expanded).astype(out_ref.dtype)
 
 
-def shrink_kernel(tile, flips, pairs, slots, tokens_ref, stored_ref, *refs):
+def shrink_kernel(tile, mixed, slots, tokens_ref, stored_ref, *refs):
     downs, out_ref, held_ref, down_ref, sums_ref, sems = (
         refs[:slots], refs[slots], *refs[slots + 1 :]
     )
@@ -207,7 +221,7 @@
 
     sums = sums_ref[...].T
     total = jnp.zeros(out_ref.shape, jnp.float32)
-    for b, owner in enumerate(owners_of(flips, pairs)):
+    for b, owner in enumerate(owners_of(slots, mixed)):
         total += jnp.where(stored_ref[...] == owner, sums[b * rank : (b + 1) * rank], 0.0)
     out_ref[...] = total
 
@@ -289,27 +303,19 @@
             tile_scratch(tile, rows, places, columns),
         )(frozen_projection_weight, *features, total)
 
-    flips = list(range(1, groups))
-    pairs = []
-    if parts == 2:
-        while len(flips) > 1:
-            pairs.append((flips.pop(-2), flips.pop(-1)))
-    routes = [
-        [(p * groups + z, p * groups + (z ^ pair[p])) for p in range(parts) for z in range(groups)]
-        for pair in pairs
-    ]
-
-    def fetch_far(value):
-        return [lax.ppermute(value, ("parts", "adapter"), route) for route in routes]
-
-    def fetch_near(value):
-        return [flipped(value, "adapter", flip) for flip in flips]
-
-    def swap(values):
-        return [flipped(value, "parts", 1) for value in values]
-
+    mixed = is_mixed(groups, parts)
     own, here = chained(own, tokens)
-    fetched = fetch_far(own)
+    if mixed:
+        held = [
+            lax.ppermute(
+                own,
+                ("parts", "adapter"),
+                [(p * groups + z, p * groups + table[p][z]) for p in range(parts) for z in range(groups)],
+            )
+            for table in (FIRST, SECOND)
+        ]
+    else:
+        held = [flipped(own, "adapter", flip) for flip in range(1, groups)]
     places = [(0, 0, 0, depth // 2)]
     total, stored = call(
         functools.partial(first_kernel, tile, depth, places, slots),
@@ -321,26 +327,26 @@
         tile_scratch(tile, rows, places, columns),
         [VECTOR, VECTOR],
     )(placement, tenant.reshape(1, rows), frozen_projection_weight, here)
-    total, own, up, neighbour, chunks[1] = chained(
-        total, own, lowrank_up_weight[0], neighbour, chunks[1]
-    )
+    total, up, neighbour, chunks[1] = chained(total, lowrank_up_weight[0], neighbour, chunks[1])
     far.append(send(1))
-    single, single_up = fetch_near(own), fetch_near(up)
+    ups = [up, flipped(up, "adapter", 1)]
     total = products([(0, depth // 2, depth // 2, depth // 2)], [here], total)
-    fetched, single_up, total = chained(fetched, single_up, total)
-    swapped = swap(fetched)
+    held, total = chained(held, total)
+    if mixed:
+        group, part = lax.axis_index("adapter"), lax.axis_index("parts")
+        far_one = jnp.where(source(group, part, FIRST) == (group ^ 1), held[1], held[0])
+        held.append(flipped(far_one, "parts", 1))
+    ups[1], total = chained(ups[1], total)
     total, neighbour = chained(total, neighbour)
     total = products([(1, 0, 0, depth)], [neighbour], total)
     total, up = chained(total, up)
-    fetched_up = fetch_far(up)
-    single, swapped, total = chained(single, swapped, total)
-    downs = [own] + single
-    for pair in zip(fetched, swapped):
-        downs += pair
+    later = [flipped(up, "adapter", flip) for flip in range(2, groups)]
+    held, total = chained(held, total)
+    downs = [own] + held
 
     tiles = depth // tile
     partial = call(
-        functools.partial(shrink_kernel, tile, flips, pairs, slots),
+        functools.partial(shrink_kernel, tile, mixed, slots),
         jax.ShapeDtypeStruct((rank, rows), jnp.float32),
         [ANYWHERE, VECTOR] + [ANYWHERE] * slots,
         [
@@ -350,11 +356,8 @@
             pltpu.SemaphoreType.DMA((1 + slots, tiles)),
         ],
     )(tokens, stored, *downs)
-    far[0], fetched_up, partial = chained(far[0], fetched_up, partial)
-    swapped_up = swap(fetched_up)
-    ups = [up] + single_up
-    for pair in zip(fetched_up, swapped_up):
-        ups += pair
+    far[0], later, partial = chained(far[0], later, partial)
+    ups += later
     near = across(0)
     total = products(far_places(0), far[0], total)
     flip = 1
@@ -374,7 +377,7 @@
 
     places = near_places(1)
     return call(
-        functools.partial(last_kernel, tile, depth, places, flips, pairs, slots),
+        functools.partial(last_kernel, tile, depth, places, slots),
         jax.ShapeDtypeStruct((rows, columns), jnp.bfloat16),
         [ANYWHERE] + [ANYWHERE] * len(near) + [VECTOR] * 2 + [ANYWHERE] * (2 + slots),
         [

time: 48.3 us -> 49.3 us (1.021)
  waiting for transfers between devices: 8.15 us -> 6.95 us
  starting transfers between devices: 17.3 us -> 18.5 us
  other arithmetic: 0.63 us -> 1.61 us
    ppermute x14, waiting for transfers between devices: 5.74 us -> 2.46 us  [flipped(): return lax.ppermute(value, axis, [(i, i ^ flip) for i in range(count)])]
    ppermute x14, starting transfers between devices: 12.7 us -> 15.9 us  [flipped(): return lax.ppermute(value, axis, [(i, i ^ flip) for i in range(count)])]
    ppermute x2, waiting for transfers between devices: 2.41 us -> 4.49 us  [body(): lax.ppermute(own, ('parts', 'adapter'), [(p * groups + z, p * groups + ta...]
    ppermute x2, starting transfers between devices: 4.59 us -> 2.64 us  [body(): lax.ppermute(own, ('parts', 'adapter'), [(p * groups + z, p * groups + ta...]
    select_n x0 -> x1, other arithmetic: none -> 0.98 us  [body(): jnp.where(source(group, part, FIRST) == group ^ 1, held[1], held[0])]
    unnamed x14 -> x32, local copies, waits for them, and re-layouts: 3.6 us -> 3.44 us
  transfers between devices with their start and end apart: 16 -> 16, of which waited for: 5 -> 4; matrix products, arithmetic and copies ran while one was open for 1% -> 3% of each run, Pallas kernels for 31% -> 30%
where the time goes in v19:
time: 49.3 us; the launch traced here: 49 us
  starting transfers between devices  18.5 us (38%)
  Pallas kernels  17.1 us (35%)
  waiting for transfers between devices  6.95 us (14%)
  local copies, waits for them, and re-layouts  4.51 us (9%)
  other arithmetic  1.61 us (3%)
    ppermute x14, starting transfers between devices, flipped(): return lax.ppermute(value, axis, [(i, i ^ flip) for i in range(count)])  15.9 us
    pallas_call x5, Pallas kernels, products(): call(functools.partial(products_kernel, tile, depth, places), jax.ShapeDt...  7.87 us
    ppermute x2, waiting for transfers between devices, body(): lax.ppermute(own, ('parts', 'adapter'), [(p * groups + z, p * groups + ta...  4.49 us
    unnamed x32, local copies, waits for them, and re-layouts  3.44 us
    ppermute x2, starting transfers between devices, body(): lax.ppermute(own, ('parts', 'adapter'), [(p * groups + z, p * groups + ta...  2.64 us
    pallas_call x1, Pallas kernels, body(): call(functools.partial(shrink_kernel, tile, mixed, slots), jax.ShapeDtype...  2.5 us
    ppermute x14, waiting for transfers between devices, flipped(): return lax.ppermute(value, axis, [(i, i ^ flip) for i in range(count)])  2.46 us
    pallas_call x1, Pallas kernels, body(): call(functools.partial(last_kernel, tile, depth, places, slots), jax.Shap...  2.27 us
  transfers between devices with their start and end apart: 16, of which 4 were waited for; matrix products, arithmetic and copies ran while one was open for 3% of the time, Pallas kernels for 30%

profile of v19, /device:TPU:0, one launch (start us, length us, event | category | flops | bytes accessed | tf_op | source)
XLA Modules:
  0.0 49.0 jit_solution(4206086193767539314)
XLA Ops:
  0.0 1.1 %dynamic-slice_bitcast_fusion = (bf16[16,2048]{1,0:T(8,128)(2,1)S(1)}, bf16[16,2048]{1,0:T(8,128)(2,1)S(1)}, bf16[16,2048]{1,0:T(8,128)(2,1)S(1)}, bf16[16,2048]{1,0:T(8,128)(2,1)S(1)}) fusion(bf16[1,8192,16]{1,2,0:T(8,128)(2,1)} %param.10, s32[]{:T(128)S(6)} %select_n.44, s32[]{:T(128)S(6)} %select_n.42, s32[]{:T(128)S(6)} %select_n.41, s32[]{:T(128)S(6)} %select_n.43), kind=kLoop, calls=%fused_computation.1 | loop fusion | bytes 524304 | tf_op jit(solution)/shard_map/dynamic_slice | solution.py:244
  1.6 2.6 %collective-permute-start.1 = (bf16[16,2048]{1,0:T(8,128)(2,1)S(1)}, bf16[16,2048]{1,0:T(8,128)(2,1)S(1)}, u32[]{:S(2)}, u32[]{:S(2)}) collective-permute-start(bf16[16,2048]{1,0:T(8,128)(2,1)S(1)} %get-tuple-element.55), channel_id=1, source_target_pairs={{0,2},{1,3},{2,0},{3,1},{4,6},{5,7},{6,4},{7,5},{8,10},{9,11},{10,... | collective-permute-start | bytes 196616 | tf_op jit(solution)/shard_map/ppermute | solution.py:27
  4.3 2.2 %shard_map.66 = (bf16[384,1536]{1,0:T(8,128)(2,1)}, bf16[384,512]{1,0:T(8,128)(2,1)}) custom-call(bf16[384,2048]{1,0:T(8,128)(2,1)} %tokens_ref.1), custom_call_target="tpu_custom_call" | custom-call | tf_op jit(solution)/shard_map/pallas_call | solution.py:250
  6.5 1.8 %collective-permute-start.8 = (bf16[384,1536]{1,0:T(8,128)(2,1)}, bf16[384,1536]{1,0:T(8,128)(2,1)}, u32[]{:S(2)}, u32[]{:S(2)}) collective-permute-start(bf16[384,1536]{1,0:T(8,128)(2,1)} %get-tuple-element.68), channel_id=1, source_target_pairs={{0,2},{1,3},{2,0},{3,1},{4,6},{5,7},{6,4},{7,5},{8,10},{9,11},{10,... | collective-permute-start | bytes 3538952 | tf_op jit(solution)/shard_map/ppermute | solution.py:27
  9.1 2.6 %collective-permute-start.7 = (bf16[64,2048]{1,0:T(8,128)(2,1)}, bf16[64,2048]{1,0:T(8,128)(2,1)}, u32[]{:S(2)}, u32[]{:S(2)}) collective-permute-start(bf16[64,2048]{1,0:T(8,128)(2,1)} %shard_map.64.refs_0_), channel_id=1, source_target_pairs={{0,8},{4,0},{8,12},{12,4},{16,28},{20,16},{24,20},{28,24},{1,9},{5... | collective-permute-start | bytes 786440 | tf_op jit(solution)/shard_map/ppermute | solution.py:310
  11.8 3.4 %copy-done.1 = bf16[8192,512]{1,0:T(8,128)(2,1)S(1)} copy-done((bf16[8192,512]{1,0:T(8,128)(2,1)S(1)}, bf16[8192,512]{1,0:T(8,128)(2,1)}, u32[]{:S(2)}) %copy-start.1) | copy-done | bytes 8388632
  15.1 1.5 %shard_map.65 = (f32[384,512]{1,0:T(8,128)S(1)}, s32[1,384]{1,0:T(1,128)S(1)}) custom-call(s32[4]{0:T(128)S(1)} %copy-done.13, s32[1,384]{1,0:T(1,128)S(1)} %bitcast.22, bf16[8192,512]{1,0:T(8,128)(2,1)S(1)} %copy-done.1, bf16[384,2048]{1,0:T(8,128)(2,1)S(1)} %copy-done), custom_call_target="tpu_custom_call" | custom-call | flops 99999997952 | tf_op jit(solution)/shard_map/pallas_call | solution.py:320
  16.7 2.0 %collective-permute-start.5 = (bf16[64,512]{1,0:T(8,128)(2,1)S(1)}, bf16[64,512]{1,0:T(8,128)(2,1)S(1)}, u32[]{:S(2)}, u32[]{:S(2)}) collective-permute-start(bf16[64,512]{1,0:T(8,128)(2,1)S(1)} %bitcast.18), channel_id=1, source_target_pairs={{0,4},{4,0},{8,12},{12,8},{1,5},{5,1},{9,13},{13,9},{2,6},{6,2},{1... | collective-permute-start | bytes 196616 | tf_op jit(solution)/shard_map/ppermute | solution.py:27
  18.6 1.2 %collective-permute-start.4 = (bf16[384,512]{1,0:T(8,128)(2,1)}, bf16[384,512]{1,0:T(8,128)(2,1)}, u32[]{:S(2)}, u32[]{:S(2)}) collective-permute-start(bf16[384,512]{1,0:T(8,128)(2,1)} %get-tuple-element.62), channel_id=1, source_target_pairs={{0,2},{1,3},{2,0},{3,1},{4,6},{5,7},{6,4},{7,5},{8,10},{9,11},{10,... | collective-permute-start | bytes 1179656 | tf_op jit(solution)/shard_map/ppermute | solution.py:27
  19.9 1.0 %shard_map.67.refs_1_ = f32[384,512]{1,0:T(8,128)S(1)} custom-call(bf16[8192,512]{1,0:T(8,128)(2,1)S(1)} %copy-done.2, bf16[384,2048]{1,0:T(8,128)(2,1)S(1)} %copy-done, f32[384,512]{1,0:T(8,128)S(1)} %get-tuple-element.65.refs_1_), custom_call_target="tpu_custom_call" | custom-call | flops 99999997952 | tf_op jit(solution)/shard_map/pallas_call | solution.py:299
  20.9 4.5 %collective-permute-done.6.refs_1_ = bf16[64,2048]{1,0:T(8,128)(2,1)} collective-permute-done((bf16[64,2048]{1,0:T(8,128)(2,1)}, bf16[64,2048]{1,0:T(8,128)(2,1)}, u32[]{:S(2)}, u32[]{:S(2)}) %collective-permute-start.6) | collective-permute-done | bytes 262176 | tf_op jit(solution)/shard_map/ppermute | solution.py:310
  25.4 1.0 %broadcast_select_fusion = bf16[64,2048]{1,0:T(8,128)(2,1)S(1)} fusion(bf16[64,2048]{1,0:T(8,128)(2,1)} %collective-permute-done.7.refs_2_, bf16[64,2048]{1,0:T(8,128)(2,1)} %collective-permute-done.6.refs_1_, pred[]{:T(512)S(6)} %eq.34), kind=kLoop, calls=%fused_computation | loop fusion | flops 131072 | bytes 786433 | tf_op jit(solution)/shard_map/jit(_where)/select_n | solution.py:337
  26.4 2.3 %collective-permute-start.11 = (bf16[64,2048]{1,0:T(8,128)(2,1)S(1)}, bf16[64,2048]{1,0:T(8,128)(2,1)S(1)}, u32[]{:S(2)}, u32[]{:S(2)}) collective-permute-start(bf16[64,2048]{1,0:T(8,128)(2,1)S(1)} %broadcast_select_fusion), channel_id=1, source_target_pairs={{0,16},{16,0},{1,17},{17,1},{2,18},{18,2},{3,19},{19,3},{4,20},{20... | collective-permute-start | bytes 786440 | tf_op jit(solution)/shard_map/ppermute | solution.py:27
  28.7 1.9 %shard_map.68.refs_1_ = f32[384,512]{1,0:T(8,128)S(1)} custom-call(bf16[8192,512]{1,0:T(8,128)(2,1)S(1)} %copy-done.2, bf16[384,2048]{1,0:T(8,128)(2,1)S(1)} %collective-permute-done.3.refs_0_, f32[384,512]{1,0:T(8,128)S(1)} %shard_map.67.refs_1_), custom_call_target="tpu_custom_call" | custom-call | flops 99999997952 | tf_op jit(solution)/shard_map/pallas_call | solution.py:299
  30.6 1.8 %collective-permute-start.10 = (bf16[64,512]{1,0:T(8,128)(2,1)S(1)}, bf16[64,512]{1,0:T(8,128)(2,1)S(1)}, u32[]{:S(2)}, u32[]{:S(2)}) collective-permute-start(bf16[64,512]{1,0:T(8,128)(2,1)S(1)} %bitcast.19), channel_id=1, source_target_pairs={{0,12},{4,8},{8,4},{12,0},{1,13},{5,9},{9,5},{13,1},{2,14},{6,10},... | collective-permute-start | bytes 196616 | tf_op jit(solution)/shard_map/ppermute | solution.py:27
  32.4 1.3 %collective-permute-start.9 = (bf16[64,512]{1,0:T(8,128)(2,1)S(1)}, bf16[64,512]{1,0:T(8,128)(2,1)S(1)}, u32[]{:S(2)}, u32[]{:S(2)}) collective-permute-start(bf16[64,512]{1,0:T(8,128)(2,1)S(1)} %bitcast.20), channel_id=1, source_target_pairs={{0,8},{4,12},{8,0},{12,4},{1,9},{5,13},{9,1},{13,5},{2,10},{6,14},... | collective-permute-start | bytes 196616 | tf_op jit(solution)/shard_map/ppermute | solution.py:27
  33.7 0.9 %collective-permute-done.11.refs_3_ = bf16[64,2048]{1,0:T(8,128)(2,1)S(1)} collective-permute-done((bf16[64,2048]{1,0:T(8,128)(2,1)S(1)}, bf16[64,2048]{1,0:T(8,128)(2,1)S(1)}, u32[]{:S(2)}, u32[]{:S(2)}) %collective-permute-start.11) | collective-permute-done | bytes 262176 | tf_op jit(solution)/shard_map/ppermute | solution.py:27
  34.6 2.5 %shard_map.69 = f32[64,384]{1,0:T(8,128)S(1)} custom-call(bf16[384,2048]{1,0:T(8,128)(2,1)S(1)} %copy-done, s32[1,384]{1,0:T(1,128)S(1)} %get-tuple-element.74.stored_ref.refs_2_, bf16[64,2048]{1,0:T(8,128)(2,1)} %shard_map.64.refs_0_, bf16[64,2048]{1,0:T(8,128)(2,1)} %collective-permute-done.6.refs_1_, bf16[64,2048]{1,0:T(8,128)(2,1)} %collective-permute-done.7.refs_2_, ...), custom_call_target="tpu_custom_call" | custom-call | flops 99999997952 | tf_op jit(solution)/shard_map/pallas_call | solution.py:348
  37.1 1.1 %collective-permute-done.9.refs_7_ = bf16[64,512]{1,0:T(8,128)(2,1)S(1)} collective-permute-done((bf16[64,512]{1,0:T(8,128)(2,1)S(1)}, bf16[64,512]{1,0:T(8,128)(2,1)S(1)}, u32[]{:S(2)}, u32[]{:S(2)}) %collective-permute-start.9) | collective-permute-done | bytes 65568 | tf_op jit(solution)/shard_map/ppermute | solution.py:27
  38.7 2.2 %shard_map.70.refs_1_ = f32[384,512]{1,0:T(8,128)S(1)} custom-call(bf16[8192,512]{1,0:T(8,128)(2,1)S(1)} %copy-done.2, bf16[384,1536]{1,0:T(8,128)(2,1)} %collective-permute-done.8.refs_0_, f32[384,512]{1,0:T(8,128)S(1)} %shard_map.68.refs_1_), custom_call_target="tpu_custom_call" | custom-call | flops 99999997952 | tf_op jit(solution)/shard_map/pallas_call | solution.py:299
  41.6 1.6 %collective-permute-start.15 = (bf16[64,384]{1,0:T(8,128)(2,1)}, bf16[64,384]{1,0:T(8,128)(2,1)}, u32[]{:S(2)}, u32[]{:S(2)}) collective-permute-start(bf16[64,384]{1,0:T(8,128)(2,1)} %get-tuple-element.99), channel_id=1, source_target_pairs={{0,2},{1,3},{2,0},{3,1},{4,6},{5,7},{6,4},{7,5},{8,10},{9,11},{10,... | collective-permute-start | bytes 147464 | tf_op jit(solution)/shard_map/ppermute | solution.py:27
  43.2 1.4 %shard_map.71.refs_1_ = f32[384,512]{1,0:T(8,128)S(1)} custom-call(bf16[8192,512]{1,0:T(8,128)(2,1)S(1)} %copy-done.2, bf16[384,1536]{1,0:T(8,128)(2,1)S(1)} %collective-permute-done.12.refs_0_, f32[384,512]{1,0:T(8,128)S(1)} %shard_map.70.refs_1_), custom_call_target="tpu_custom_call" | custom-call | flops 99999997952 | tf_op jit(solution)/shard_map/pallas_call | solution.py:299
  44.8 1.4 %shard_map.72.refs_1_ = f32[384,512]{1,0:T(8,128)S(1)} custom-call(bf16[8192,512]{1,0:T(8,128)(2,1)S(1)} %copy-done.2, bf16[384,512]{1,0:T(8,128)(2,1)} %collective-permute-done.4.refs_0_, f32[384,512]{1,0:T(8,128)S(1)} %shard_map.71.refs_1_), custom_call_target="tpu_custom_call" | custom-call | flops 99999997952 | tf_op jit(solution)/shard_map/pallas_call | solution.py:299
  46.7 2.3 %shard_map.73 = bf16[384,512]{1,0:T(8,128)(2,1)} custom-call(bf16[8192,512]{1,0:T(8,128)(2,1)S(1)} %copy-done.2, bf16[384,512]{1,0:T(8,128)(2,1)S(1)} %collective-permute-done.14.refs_0_, f32[384,512]{1,0:T(8,128)S(1)} %shard_map.72.refs_1_, s32[1,384]{1,0:T(1,128)S(1)} %copy-done.15, f32[64,384]{1,0:T(8,128)S(1)} %get-tuple-element.93.refs_3_, ...), custom_call_target="tpu_custom_call" | custom-call | flops 99999997952 | tf_op jit(solution)/shard_map/pallas_call | solution.py:379
  (53 shorter events, 3.2 us)
Async XLA Ops:
  0.0 11.7 %copy-start = (bf16[384,2048]{1,0:T(8,128)(2,1)S(1)}, bf16[384,2048]{1,0:T(8,128)(2,1)}, u32[]{:S(2)}) copy-start(bf16[384,2048]{1,0:T(8,128)(2,1)} %tokens_ref.1) | copy-start | bytes 4718596
  0.0 11.7 %copy-start.13 = (s32[4]{0:T(128)S(1)}, s32[4]{0:T(128)}, u32[]{:S(2)}) copy-start(s32[4]{0:T(128)} %placement_ref.1) | copy-start | bytes 52
  0.0 11.7 %copy-start.12 = (s32[384,1]{0,1:T(1,128)S(1)}, s32[384,1]{0,1:T(1,128)}, u32[]{:S(2)}) copy-start(s32[384,1]{0,1:T(1,128)} %param.7) | copy-start | bytes 4612
  1.1 7.2 %collective-permute-start = (bf16[16,2048]{1,0:T(8,128)(2,1)S(1)}, bf16[16,2048]{1,0:T(8,128)(2,1)S(1)}, u32[]{:S(2)}, u32[]{:S(2)}) collective-permute-start(bf16[16,2048]{1,0:T(8,128)(2,1)S(1)} %get-tuple-element.53), channel_id=1, source_target_pairs={{0,1},{1,0},{2,3},{3,2},{4,5},{5,4},{6,7},{7,6},{8,9},{9,8},{10,11... | collective-permute-start | bytes 196616 | tf_op jit(solution)/shard_map/ppermute | solution.py:27
  1.6 6.7 %collective-permute-start.1 = (bf16[16,2048]{1,0:T(8,128)(2,1)S(1)}, bf16[16,2048]{1,0:T(8,128)(2,1)S(1)}, u32[]{:S(2)}, u32[]{:S(2)}) collective-permute-start(bf16[16,2048]{1,0:T(8,128)(2,1)S(1)} %get-tuple-element.55), channel_id=1, source_target_pairs={{0,2},{1,3},{2,0},{3,1},{4,6},{5,7},{6,4},{7,5},{8,10},{9,11},{10,... | collective-permute-start | bytes 196616 | tf_op jit(solution)/shard_map/ppermute | solution.py:27
  4.2 4.1 %collective-permute-start.2 = (bf16[16,2048]{1,0:T(8,128)(2,1)S(1)}, bf16[16,2048]{1,0:T(8,128)(2,1)S(1)}, u32[]{:S(2)}, u32[]{:S(2)}) collective-permute-start(bf16[16,2048]{1,0:T(8,128)(2,1)S(1)} %get-tuple-element.56), channel_id=1, source_target_pairs={{0,3},{1,2},{2,1},{3,0},{4,7},{5,6},{6,5},{7,4},{8,11},{9,10},{10,... | collective-permute-start | bytes 196616 | tf_op jit(solution)/shard_map/ppermute | solution.py:27
  6.5 30.6 %collective-permute-start.8 = (bf16[384,1536]{1,0:T(8,128)(2,1)}, bf16[384,1536]{1,0:T(8,128)(2,1)}, u32[]{:S(2)}, u32[]{:S(2)}) collective-permute-start(bf16[384,1536]{1,0:T(8,128)(2,1)} %get-tuple-element.68), channel_id=1, source_target_pairs={{0,2},{1,3},{2,0},{3,1},{4,6},{5,7},{6,4},{7,5},{8,10},{9,11},{10,... | collective-permute-start | bytes 3538952 | tf_op jit(solution)/shard_map/ppermute | solution.py:27
  9.1 11.8 %collective-permute-start.7 = (bf16[64,2048]{1,0:T(8,128)(2,1)}, bf16[64,2048]{1,0:T(8,128)(2,1)}, u32[]{:S(2)}, u32[]{:S(2)}) collective-permute-start(bf16[64,2048]{1,0:T(8,128)(2,1)} %shard_map.64.refs_0_), channel_id=1, source_target_pairs={{0,8},{4,0},{8,12},{12,4},{16,28},{20,16},{24,20},{28,24},{1,9},{5... | collective-permute-start | bytes 786440 | tf_op jit(solution)/shard_map/ppermute | solution.py:310
  11.7 13.7 %collective-permute-start.6 = (bf16[64,2048]{1,0:T(8,128)(2,1)}, bf16[64,2048]{1,0:T(8,128)(2,1)}, u32[]{:S(2)}, u32[]{:S(2)}) collective-permute-start(bf16[64,2048]{1,0:T(8,128)(2,1)} %shard_map.64.refs_0_), channel_id=1, source_target_pairs={{0,4},{4,12},{8,0},{12,8},{16,20},{20,24},{24,28},{28,16},{1,5},{5... | collective-permute-start | bytes 786440 | tf_op jit(solution)/shard_map/ppermute | solution.py:310
  11.7 4.9 %collective-permute-start.3 = (bf16[384,2048]{1,0:T(8,128)(2,1)S(1)}, bf16[384,2048]{1,0:T(8,128)(2,1)S(1)}, u32[]{:S(2)}, u32[]{:S(2)}) collective-permute-start(bf16[384,2048]{1,0:T(8,128)(2,1)S(1)} %copy-done), channel_id=1, source_target_pairs={{0,1},{1,0},{2,3},{3,2},{4,5},{5,4},{6,7},{7,6},{8,9},{9,8},{10,11... | collective-permute-start | bytes 4718600 | tf_op jit(solution)/shard_map/ppermute | solution.py:27
  11.7 3.4 %copy-start.1 = (bf16[8192,512]{1,0:T(8,128)(2,1)S(1)}, bf16[8192,512]{1,0:T(8,128)(2,1)}, u32[]{:S(2)}) copy-start(bf16[8192,512]{1,0:T(8,128)(2,1)} %weight_ref.13) | copy-start | bytes 25165828
  15.1 4.8 %copy-start.2 = (bf16[8192,512]{1,0:T(8,128)(2,1)S(1)}, bf16[8192,512]{1,0:T(8,128)(2,1)}, u32[]{:S(2)}) copy-start(bf16[8192,512]{1,0:T(8,128)(2,1)} %weight_ref.13) | copy-start | bytes 25165828
  16.7 18.0 %copy-start.14 = (s32[1,384]{1,0:T(1,128)}, s32[1,384]{1,0:T(1,128)S(1)}, u32[]{:S(2)}) copy-start(s32[1,384]{1,0:T(1,128)S(1)} %get-tuple-element.74.stored_ref.refs_2_) | copy-start | bytes 4612
  16.7 12.0 %collective-permute-start.5 = (bf16[64,512]{1,0:T(8,128)(2,1)S(1)}, bf16[64,512]{1,0:T(8,128)(2,1)S(1)}, u32[]{:S(2)}, u32[]{:S(2)}) collective-permute-start(bf16[64,512]{1,0:T(8,128)(2,1)S(1)} %bitcast.18), channel_id=1, source_target_pairs={{0,4},{4,0},{8,12},{12,8},{1,5},{5,1},{9,13},{13,9},{2,6},{6,2},{1... | collective-permute-start | bytes 196616 | tf_op jit(solution)/shard_map/ppermute | solution.py:27
  18.6 26.1 %collective-permute-start.4 = (bf16[384,512]{1,0:T(8,128)(2,1)}, bf16[384,512]{1,0:T(8,128)(2,1)}, u32[]{:S(2)}, u32[]{:S(2)}) collective-permute-start(bf16[384,512]{1,0:T(8,128)(2,1)} %get-tuple-element.62), channel_id=1, source_target_pairs={{0,2},{1,3},{2,0},{3,1},{4,6},{5,7},{6,4},{7,5},{8,10},{9,11},{10,... | collective-permute-start | bytes 1179656 | tf_op jit(solution)/shard_map/ppermute | solution.py:27
  26.4 4.2 %copy-start.4 = (bf16[1,64,512]{2,1,0:T(8,128)(2,1)S(1)}, bf16[1,64,512]{2,1,0:T(8,128)(2,1)}, u32[]{:S(2)}) copy-start(bf16[1,64,512]{2,1,0:T(8,128)(2,1)} %param.11) | copy-start | bytes 196612
  26.4 8.2 %collective-permute-start.11 = (bf16[64,2048]{1,0:T(8,128)(2,1)S(1)}, bf16[64,2048]{1,0:T(8,128)(2,1)S(1)}, u32[]{:S(2)}, u32[]{:S(2)}) collective-permute-start(bf16[64,2048]{1,0:T(8,128)(2,1)S(1)} %broadcast_select_fusion), channel_id=1, source_target_pairs={{0,16},{16,0},{1,17},{17,1},{2,18},{18,2},{3,19},{19,3},{4,20},{20... | collective-permute-start | bytes 786440 | tf_op jit(solution)/shard_map/ppermute | solution.py:27
  30.6 6.5 %collective-permute-start.10 = (bf16[64,512]{1,0:T(8,128)(2,1)S(1)}, bf16[64,512]{1,0:T(8,128)(2,1)S(1)}, u32[]{:S(2)}, u32[]{:S(2)}) collective-permute-start(bf16[64,512]{1,0:T(8,128)(2,1)S(1)} %bitcast.19), channel_id=1, source_target_pairs={{0,12},{4,8},{8,4},{12,0},{1,13},{5,9},{9,5},{13,1},{2,14},{6,10},... | collective-permute-start | bytes 196616 | tf_op jit(solution)/shard_map/ppermute | solution.py:27
  32.4 5.8 %collective-permute-start.9 = (bf16[64,512]{1,0:T(8,128)(2,1)S(1)}, bf16[64,512]{1,0:T(8,128)(2,1)S(1)}, u32[]{:S(2)}, u32[]{:S(2)}) collective-permute-start(bf16[64,512]{1,0:T(8,128)(2,1)S(1)} %bitcast.20), channel_id=1, source_target_pairs={{0,8},{4,12},{8,0},{12,4},{1,9},{5,13},{9,1},{13,5},{2,10},{6,14},... | collective-permute-start | bytes 196616 | tf_op jit(solution)/shard_map/ppermute | solution.py:27
  37.1 3.8 %copy-start.8 = (bf16[64,512]{1,0:T(8,128)(2,1)}, bf16[64,512]{1,0:T(8,128)(2,1)S(1)}, u32[]{:S(2)}) copy-start(bf16[64,512]{1,0:T(8,128)(2,1)S(1)} %collective-permute-done.10.refs_8_) | copy-start | bytes 196612
  38.2 2.7 %collective-permute-start.13 = (f32[64,384]{1,0:T(8,128)S(1)}, f32[64,384]{1,0:T(8,128)S(1)}, u32[]{:S(2)}, u32[]{:S(2)}) collective-permute-start(f32[64,384]{1,0:T(8,128)S(1)} %shard_map.69), channel_id=1, source_target_pairs={{0,1},{1,0},{2,3},{3,2},{4,5},{5,4},{6,7},{7,6},{8,9},{9,8},{10,11... | collective-permute-start | bytes 294920 | tf_op jit(solution)/shard_map/ppermute | solution.py:27
  38.2 5.0 %collective-permute-start.12 = (bf16[384,1536]{1,0:T(8,128)(2,1)}, bf16[384,1536]{1,0:T(8,128)(2,1)S(1)}, u32[]{:S(2)}, u32[]{:S(2)}) collective-permute-start(bf16[384,1536]{1,0:T(8,128)(2,1)} %collective-permute-done.8.refs_0_), channel_id=1, source_target_pairs={{0,1},{1,0},{2,3},{3,2},{4,5},{5,4},{6,7},{7,6},{8,9},{9,8},{10,11... | collective-permute-start | bytes 3538952 | tf_op jit(solution)/shard_map/ppermute | solution.py:27
  41.6 4.6 %collective-permute-start.15 = (bf16[64,384]{1,0:T(8,128)(2,1)}, bf16[64,384]{1,0:T(8,128)(2,1)}, u32[]{:S(2)}, u32[]{:S(2)}) collective-permute-start(bf16[64,384]{1,0:T(8,128)(2,1)} %get-tuple-element.99), channel_id=1, source_target_pairs={{0,2},{1,3},{2,0},{3,1},{4,6},{5,7},{6,4},{7,5},{8,10},{9,11},{10,... | collective-permute-start | bytes 147464 | tf_op jit(solution)/shard_map/ppermute | solution.py:27
  44.7 2.0 %collective-permute-start.14 = (bf16[384,512]{1,0:T(8,128)(2,1)}, bf16[384,512]{1,0:T(8,128)(2,1)S(1)}, u32[]{:S(2)}, u32[]{:S(2)}) collective-permute-start(bf16[384,512]{1,0:T(8,128)(2,1)} %collective-permute-done.4.refs_0_), channel_id=1, source_target_pairs={{0,1},{1,0},{2,3},{3,2},{4,5},{5,4},{6,7},{7,6},{8,9},{9,8},{10,11... | collective-permute-start | bytes 1179656 | tf_op jit(solution)/shard_map/ppermute | solution.py:27
  (8 other events, 16.4 us)

commit v20 on v18

--- a/solution.py
+++ b/solution.py
@@ -247,8 +247,6 @@
         )(uncut)
     )
     pieces = [pieces[0]] + [flipped(pieces[f], "tensor", f) for f in range(1, tensors)]
-    pieces[1], here = chained(pieces[1], tokens)
-    neighbour = flipped(here, "tensor", 1)
     if down.shape[0] % 16 == 0:
         own = call(
             functools.partial(order_kernel, down.shape[0]),
@@ -321,18 +319,16 @@
         tile_scratch(tile, rows, places, columns),
         [VECTOR, VECTOR],
     )(placement, tenant.reshape(1, rows), frozen_projection_weight, here)
-    total, own, up, neighbour, chunks[1] = chained(
-        total, own, lowrank_up_weight[0], neighbour, chunks[1]
-    )
+    total, own, there, chunks[1] = chained(total, own, tokens, chunks[1])
+    neighbour = flipped(there, "tensor", 1)
     far.append(send(1))
-    single, single_up = fetch_near(own), fetch_near(up)
+    single = fetch_near(own)
     total = products([(0, depth // 2, depth // 2, depth // 2)], [here], total)
-    fetched, single_up, total = chained(fetched, single_up, total)
+    fetched, neighbour, total = chained(fetched, neighbour, total)
     swapped = swap(fetched)
-    total, neighbour = chained(total, neighbour)
     total = products([(1, 0, 0, depth)], [neighbour], total)
-    total, up = chained(total, up)
-    fetched_up = fetch_far(up)
+    total, up = chained(total, lowrank_up_weight[0])
+    fetched_up, single_up = fetch_far(up), fetch_near(up)
     single, swapped, total = chained(single, swapped, total)
     downs = [own] + single
     for pair in zip(fetched, swapped):

time: 48.3 us -> 48.3 us (level)
  waiting for transfers between devices: 8.15 us -> 6.27 us
  local copies, waits for them, and re-layouts: 4.67 us -> 6.24 us
    unnamed x14, local copies, waits for them, and re-layouts: 3.6 us -> 5.17 us
    ppermute x14, waiting for transfers between devices: 5.74 us -> 4.27 us  [flipped(): return lax.ppermute(value, axis, [(i, i ^ flip) for i in range(count)])]
    ppermute x2, starting transfers between devices: 4.59 us -> 5.82 us  [fetch_far(): lax.ppermute(value, ('parts', 'adapter'), route)]
    ppermute x14, starting transfers between devices: 12.7 us -> 11.9 us  [flipped(): return lax.ppermute(value, axis, [(i, i ^ flip) for i in range(count)])]
where the time goes in v20:
time: 48.3 us; the launch traced here: 47.9 us
  starting transfers between devices  17.7 us (37%)
  Pallas kernels  17 us (35%)
  waiting for transfers between devices  6.27 us (13%)
  local copies, waits for them, and re-layouts  6.24 us (13%)
  other arithmetic  0.62 us (1%)
    ppermute x14, starting transfers between devices, flipped(): return lax.ppermute(value, axis, [(i, i ^ flip) for i in range(count)])  11.9 us
    pallas_call x5, Pallas kernels, products(): call(functools.partial(products_kernel, tile, depth, places), jax.ShapeDt...  7.87 us
    ppermute x2, starting transfers between devices, fetch_far(): lax.ppermute(value, ('parts', 'adapter'), route)  5.82 us
    unnamed x14, local copies, waits for them, and re-layouts  5.17 us
    ppermute x14, waiting for transfers between devices, flipped(): return lax.ppermute(value, axis, [(i, i ^ flip) for i in range(count)])  4.27 us
    pallas_call x1, Pallas kernels, body(): call(functools.partial(shrink_kernel, tile, flips, pairs, slots), jax.Sha...  2.46 us
    pallas_call x1, Pallas kernels, body(): call(functools.partial(cut_kernel, edges), [jax.ShapeDtypeStruct((rows, b...  2.23 us
    pallas_call x1, Pallas kernels, body(): call(functools.partial(last_kernel, tile, depth, places, flips, pairs, sl...  2.16 us
  transfers between devices with their start and end apart: 16, of which 5 were waited for; matrix products, arithmetic and copies ran while one was open for 1% of the time, Pallas kernels for 31%

profile of v20, /device:TPU:0, one launch (start us, length us, event | category | flops | bytes accessed | tf_op | source)
XLA Modules:
  0.0 47.9 jit_solution(5719518123005963637)
XLA Ops:
  0.0 1.1 %dynamic-slice_bitcast_fusion = (bf16[16,2048]{1,0:T(8,128)(2,1)S(1)}, bf16[16,2048]{1,0:T(8,128)(2,1)S(1)}, bf16[16,2048]{1,0:T(8,128)(2,1)S(1)}, bf16[16,2048]{1,0:T(8,128)(2,1)S(1)}) fusion(bf16[1,8192,16]{1,2,0:T(8,128)(2,1)} %param.10, s32[]{:T(128)S(6)} %select_n.15, s32[]{:T(128)S(6)} %select_n.13, s32[]{:T(128)S(6)} %select_n.12, s32[]{:T(128)S(6)} %select_n.14), kind=kLoop, calls=%fused_computation | loop fusion | bytes 524304 | tf_op jit(solution)/shard_map/dynamic_slice | solution.py:230
  1.6 2.6 %collective-permute-start.1 = (bf16[16,2048]{1,0:T(8,128)(2,1)S(1)}, bf16[16,2048]{1,0:T(8,128)(2,1)S(1)}, u32[]{:S(2)}, u32[]{:S(2)}) collective-permute-start(bf16[16,2048]{1,0:T(8,128)(2,1)S(1)} %get-tuple-element.46), channel_id=1, source_target_pairs={{0,2},{1,3},{2,0},{3,1},{4,6},{5,7},{6,4},{7,5},{8,10},{9,11},{10,... | collective-permute-start | bytes 196616 | tf_op jit(solution)/shard_map/ppermute | solution.py:25
  4.3 2.2 %shard_map.66 = (bf16[384,1536]{1,0:T(8,128)(2,1)}, bf16[384,512]{1,0:T(8,128)(2,1)}) custom-call(bf16[384,2048]{1,0:T(8,128)(2,1)} %tokens_ref.1), custom_call_target="tpu_custom_call" | custom-call | tf_op jit(solution)/shard_map/pallas_call | solution.py:236
  6.5 1.8 %collective-permute-start.7 = (bf16[384,1536]{1,0:T(8,128)(2,1)}, bf16[384,1536]{1,0:T(8,128)(2,1)}, u32[]{:S(2)}, u32[]{:S(2)}) collective-permute-start(bf16[384,1536]{1,0:T(8,128)(2,1)} %get-tuple-element.59), channel_id=1, source_target_pairs={{0,2},{1,3},{2,0},{3,1},{4,6},{5,7},{6,4},{7,5},{8,10},{9,11},{10,... | collective-permute-start | bytes 3538952 | tf_op jit(solution)/shard_map/ppermute | solution.py:25
  9.1 2.7 %collective-permute-start.4 = (bf16[64,2048]{1,0:T(8,128)(2,1)}, bf16[64,2048]{1,0:T(8,128)(2,1)}, u32[]{:S(2)}, u32[]{:S(2)}) collective-permute-start(bf16[64,2048]{1,0:T(8,128)(2,1)} %shard_map.64.refs_0_), channel_id=1, source_target_pairs={{0,8},{4,12},{8,0},{12,4},{16,28},{20,24},{24,20},{28,16},{1,9},{5... | collective-permute-start | bytes 786440 | tf_op jit(solution)/shard_map/ppermute | solution.py:301
  11.7 3.4 %copy-done.1 = bf16[8192,512]{1,0:T(8,128)(2,1)S(1)} copy-done((bf16[8192,512]{1,0:T(8,128)(2,1)S(1)}, bf16[8192,512]{1,0:T(8,128)(2,1)}, u32[]{:S(2)}) %copy-start.1) | copy-done | bytes 8388632
  15.1 1.5 %shard_map.65 = (f32[384,512]{1,0:T(8,128)S(1)}, s32[1,384]{1,0:T(1,128)S(1)}) custom-call(s32[4]{0:T(128)S(1)} %copy-done.4, s32[1,384]{1,0:T(1,128)S(1)} %bitcast.18, bf16[8192,512]{1,0:T(8,128)(2,1)S(1)} %copy-done.1, bf16[384,2048]{1,0:T(8,128)(2,1)S(1)} %copy-done), custom_call_target="tpu_custom_call" | custom-call | flops 99999997952 | tf_op jit(solution)/shard_map/pallas_call | solution.py:312
  16.7 1.8 %copy-done.2 = bf16[8192,512]{1,0:T(8,128)(2,1)S(1)} copy-done((bf16[8192,512]{1,0:T(8,128)(2,1)S(1)}, bf16[8192,512]{1,0:T(8,128)(2,1)}, u32[]{:S(2)}) %copy-start.2) | copy-done | bytes 8388632
  18.5 1.0 %shard_map.67.refs_1_ = f32[384,512]{1,0:T(8,128)S(1)} custom-call(bf16[8192,512]{1,0:T(8,128)(2,1)S(1)} %copy-done.2, bf16[384,2048]{1,0:T(8,128)(2,1)S(1)} %copy-done, f32[384,512]{1,0:T(8,128)S(1)} %get-tuple-element.55.refs_1_), custom_call_target="tpu_custom_call" | custom-call | flops 99999997952 | tf_op jit(solution)/shard_map/pallas_call | solution.py:283
  19.4 1.6 %collective-permute-start.9 = (bf16[64,2048]{1,0:T(8,128)(2,1)}, bf16[64,2048]{1,0:T(8,128)(2,1)S(1)}, u32[]{:S(2)}, u32[]{:S(2)}) collective-permute-start(bf16[64,2048]{1,0:T(8,128)(2,1)} %shard_map.64.refs_0_), channel_id=1, source_target_pairs={{0,4},{4,0},{8,12},{12,8},{1,5},{5,1},{9,13},{13,9},{2,6},{6,2},{1... | collective-permute-start | bytes 786440 | tf_op jit(solution)/shard_map/ppermute | solution.py:25
  21.1 1.3 %collective-permute-start.3 = (bf16[384,512]{1,0:T(8,128)(2,1)}, bf16[384,512]{1,0:T(8,128)(2,1)}, u32[]{:S(2)}, u32[]{:S(2)}) collective-permute-start(bf16[384,512]{1,0:T(8,128)(2,1)} %get-tuple-element.53), channel_id=1, source_target_pairs={{0,2},{1,3},{2,0},{3,1},{4,6},{5,7},{6,4},{7,5},{8,10},{9,11},{10,... | collective-permute-start | bytes 1179656 | tf_op jit(solution)/shard_map/ppermute | solution.py:25
  22.4 2.0 %collective-permute-done.4.refs_2_ = bf16[64,2048]{1,0:T(8,128)(2,1)} collective-permute-done((bf16[64,2048]{1,0:T(8,128)(2,1)}, bf16[64,2048]{1,0:T(8,128)(2,1)}, u32[]{:S(2)}, u32[]{:S(2)}) %collective-permute-start.4) | collective-permute-done | bytes 262176 | tf_op jit(solution)/shard_map/ppermute | solution.py:301
  24.4 1.9 %shard_map.68.refs_1_ = f32[384,512]{1,0:T(8,128)S(1)} custom-call(bf16[8192,512]{1,0:T(8,128)(2,1)S(1)} %copy-done.2, bf16[384,2048]{1,0:T(8,128)(2,1)S(1)} %collective-permute-done.5.refs_0_, f32[384,512]{1,0:T(8,128)S(1)} %shard_map.67.refs_1_), custom_call_target="tpu_custom_call" | custom-call | flops 99999997952 | tf_op jit(solution)/shard_map/pallas_call | solution.py:283
  26.3 3.2 %collective-permute-start.8 = (bf16[64,512]{1,0:T(8,128)(2,1)}, bf16[64,512]{1,0:T(8,128)(2,1)S(1)}, u32[]{:S(2)}, u32[]{:S(2)}) collective-permute-start(bf16[64,512]{1,0:T(8,128)(2,1)} %bitcast.9.refs_5_), channel_id=1, source_target_pairs={{0,8},{4,12},{8,0},{12,4},{16,28},{20,24},{24,20},{28,16},{1,9},{5... | collective-permute-start | bytes 196616 | tf_op jit(solution)/shard_map/ppermute | solution.py:301
  29.4 1.1 %collective-permute-done.9.refs_1_ = bf16[64,2048]{1,0:T(8,128)(2,1)S(1)} collective-permute-done((bf16[64,2048]{1,0:T(8,128)(2,1)}, bf16[64,2048]{1,0:T(8,128)(2,1)S(1)}, u32[]{:S(2)}, u32[]{:S(2)}) %collective-permute-start.9) | collective-permute-done | bytes 262176 | tf_op jit(solution)/shard_map/ppermute | solution.py:25
  30.5 1.5 %collective-permute-done.10.refs_3_ = bf16[64,2048]{1,0:T(8,128)(2,1)S(1)} collective-permute-done((bf16[64,2048]{1,0:T(8,128)(2,1)}, bf16[64,2048]{1,0:T(8,128)(2,1)S(1)}, u32[]{:S(2)}, u32[]{:S(2)}) %collective-permute-start.10) | collective-permute-done | bytes 262176 | tf_op jit(solution)/shard_map/ppermute | solution.py:25
  31.9 2.5 %shard_map.69 = f32[64,384]{1,0:T(8,128)S(1)} custom-call(bf16[384,2048]{1,0:T(8,128)(2,1)S(1)} %copy-done, s32[1,384]{1,0:T(1,128)S(1)} %get-tuple-element.60.stored_ref.refs_2_, bf16[64,2048]{1,0:T(8,128)(2,1)} %shard_map.64.refs_0_, bf16[64,2048]{1,0:T(8,128)(2,1)S(1)} %collective-permute-done.9.refs_1_, bf16[64,2048]{1,0:T(8,128)(2,1)} %collective-permute-done.4.refs_2_, ...), custom_call_target="tpu_custom_call" | custom-call | flops 99999997952 | tf_op jit(solution)/shard_map/pallas_call | solution.py:338
  34.4 1.3 %collective-permute-done.7.refs_0_ = bf16[384,1536]{1,0:T(8,128)(2,1)} collective-permute-done((bf16[384,1536]{1,0:T(8,128)(2,1)}, bf16[384,1536]{1,0:T(8,128)(2,1)}, u32[]{:S(2)}, u32[]{:S(2)}) %collective-permute-start.7) | collective-permute-done | bytes 1179680 | tf_op jit(solution)/shard_map/ppermute | solution.py:25
  36.2 2.2 %shard_map.70.refs_1_ = f32[384,512]{1,0:T(8,128)S(1)} custom-call(bf16[8192,512]{1,0:T(8,128)(2,1)S(1)} %copy-done.2, bf16[384,1536]{1,0:T(8,128)(2,1)} %collective-permute-done.7.refs_0_, f32[384,512]{1,0:T(8,128)S(1)} %shard_map.68.refs_1_), custom_call_target="tpu_custom_call" | custom-call | flops 99999997952 | tf_op jit(solution)/shard_map/pallas_call | solution.py:283
  38.4 1.8 %collective-permute-start.11 = (bf16[64,512]{1,0:T(8,128)(2,1)S(1)}, bf16[64,512]{1,0:T(8,128)(2,1)S(1)}, u32[]{:S(2)}, u32[]{:S(2)}) collective-permute-start(bf16[64,512]{1,0:T(8,128)(2,1)S(1)} %collective-permute-done.8.refs_7_), channel_id=1, source_target_pairs={{0,16},{16,0},{1,17},{17,1},{2,18},{18,2},{3,19},{19,3},{4,20},{20... | collective-permute-start | bytes 196616 | tf_op jit(solution)/shard_map/ppermute | solution.py:25
  40.8 1.5 %collective-permute-start.15 = (bf16[64,384]{1,0:T(8,128)(2,1)}, bf16[64,384]{1,0:T(8,128)(2,1)}, u32[]{:S(2)}, u32[]{:S(2)}) collective-permute-start(bf16[64,384]{1,0:T(8,128)(2,1)} %get-tuple-element.83), channel_id=1, source_target_pairs={{0,2},{1,3},{2,0},{3,1},{4,6},{5,7},{6,4},{7,5},{8,10},{9,11},{10,... | collective-permute-start | bytes 147464 | tf_op jit(solution)/shard_map/ppermute | solution.py:25
  42.3 1.4 %shard_map.71.refs_1_ = f32[384,512]{1,0:T(8,128)S(1)} custom-call(bf16[8192,512]{1,0:T(8,128)(2,1)S(1)} %copy-done.2, bf16[384,1536]{1,0:T(8,128)(2,1)S(1)} %collective-permute-done.12.refs_0_, f32[384,512]{1,0:T(8,128)S(1)} %shard_map.70.refs_1_), custom_call_target="tpu_custom_call" | custom-call | flops 99999997952 | tf_op jit(solution)/shard_map/pallas_call | solution.py:283
  43.9 1.4 %shard_map.72.refs_1_ = f32[384,512]{1,0:T(8,128)S(1)} custom-call(bf16[8192,512]{1,0:T(8,128)(2,1)S(1)} %copy-done.2, bf16[384,512]{1,0:T(8,128)(2,1)} %collective-permute-done.3.refs_0_, f32[384,512]{1,0:T(8,128)S(1)} %shard_map.71.refs_1_), custom_call_target="tpu_custom_call" | custom-call | flops 99999997952 | tf_op jit(solution)/shard_map/pallas_call | solution.py:283
  45.8 2.2 %shard_map.73 = bf16[384,512]{1,0:T(8,128)(2,1)} custom-call(bf16[8192,512]{1,0:T(8,128)(2,1)S(1)} %copy-done.2, bf16[384,512]{1,0:T(8,128)(2,1)S(1)} %collective-permute-done.14.refs_0_, f32[384,512]{1,0:T(8,128)S(1)} %shard_map.72.refs_1_, s32[1,384]{1,0:T(1,128)S(1)} %copy-done.6, f32[64,384]{1,0:T(8,128)S(1)} %get-tuple-element.77.refs_3_, ...), custom_call_target="tpu_custom_call" | custom-call | flops 99999997952 | tf_op jit(solution)/shard_map/pallas_call | solution.py:372
  (34 shorter events, 3.2 us)
Async XLA Ops:
  0.0 11.7 %copy-start = (bf16[384,2048]{1,0:T(8,128)(2,1)S(1)}, bf16[384,2048]{1,0:T(8,128)(2,1)}, u32[]{:S(2)}) copy-start(bf16[384,2048]{1,0:T(8,128)(2,1)} %tokens_ref.1) | copy-start | bytes 4718596
  0.0 11.7 %copy-start.3 = (s32[384,1]{0,1:T(1,128)S(1)}, s32[384,1]{0,1:T(1,128)}, u32[]{:S(2)}) copy-start(s32[384,1]{0,1:T(1,128)} %param.7) | copy-start | bytes 4612
  0.0 11.7 %copy-start.4 = (s32[4]{0:T(128)S(1)}, s32[4]{0:T(128)}, u32[]{:S(2)}) copy-start(s32[4]{0:T(128)} %placement_ref.1) | copy-start | bytes 52
  1.1 7.2 %collective-permute-start = (bf16[16,2048]{1,0:T(8,128)(2,1)S(1)}, bf16[16,2048]{1,0:T(8,128)(2,1)S(1)}, u32[]{:S(2)}, u32[]{:S(2)}) collective-permute-start(bf16[16,2048]{1,0:T(8,128)(2,1)S(1)} %get-tuple-element.45), channel_id=1, source_target_pairs={{0,1},{1,0},{2,3},{3,2},{4,5},{5,4},{6,7},{7,6},{8,9},{9,8},{10,11... | collective-permute-start | bytes 196616 | tf_op jit(solution)/shard_map/ppermute | solution.py:25
  1.6 6.7 %collective-permute-start.1 = (bf16[16,2048]{1,0:T(8,128)(2,1)S(1)}, bf16[16,2048]{1,0:T(8,128)(2,1)S(1)}, u32[]{:S(2)}, u32[]{:S(2)}) collective-permute-start(bf16[16,2048]{1,0:T(8,128)(2,1)S(1)} %get-tuple-element.46), channel_id=1, source_target_pairs={{0,2},{1,3},{2,0},{3,1},{4,6},{5,7},{6,4},{7,5},{8,10},{9,11},{10,... | collective-permute-start | bytes 196616 | tf_op jit(solution)/shard_map/ppermute | solution.py:25
  4.2 4.1 %collective-permute-start.2 = (bf16[16,2048]{1,0:T(8,128)(2,1)S(1)}, bf16[16,2048]{1,0:T(8,128)(2,1)S(1)}, u32[]{:S(2)}, u32[]{:S(2)}) collective-permute-start(bf16[16,2048]{1,0:T(8,128)(2,1)S(1)} %get-tuple-element.47), channel_id=1, source_target_pairs={{0,3},{1,2},{2,1},{3,0},{4,7},{5,6},{6,5},{7,4},{8,11},{9,10},{10,... | collective-permute-start | bytes 196616 | tf_op jit(solution)/shard_map/ppermute | solution.py:25
  6.5 29.2 %collective-permute-start.7 = (bf16[384,1536]{1,0:T(8,128)(2,1)}, bf16[384,1536]{1,0:T(8,128)(2,1)}, u32[]{:S(2)}, u32[]{:S(2)}) collective-permute-start(bf16[384,1536]{1,0:T(8,128)(2,1)} %get-tuple-element.59), channel_id=1, source_target_pairs={{0,2},{1,3},{2,0},{3,1},{4,6},{5,7},{6,4},{7,5},{8,10},{9,11},{10,... | collective-permute-start | bytes 3538952 | tf_op jit(solution)/shard_map/ppermute | solution.py:25
  9.1 15.3 %collective-permute-start.4 = (bf16[64,2048]{1,0:T(8,128)(2,1)}, bf16[64,2048]{1,0:T(8,128)(2,1)}, u32[]{:S(2)}, u32[]{:S(2)}) collective-permute-start(bf16[64,2048]{1,0:T(8,128)(2,1)} %shard_map.64.refs_0_), channel_id=1, source_target_pairs={{0,8},{4,12},{8,0},{12,4},{16,28},{20,24},{24,20},{28,16},{1,9},{5... | collective-permute-start | bytes 786440 | tf_op jit(solution)/shard_map/ppermute | solution.py:301
  11.7 3.4 %copy-start.1 = (bf16[8192,512]{1,0:T(8,128)(2,1)S(1)}, bf16[8192,512]{1,0:T(8,128)(2,1)}, u32[]{:S(2)}) copy-start(bf16[8192,512]{1,0:T(8,128)(2,1)} %weight_ref.13) | copy-start | bytes 25165828
  15.1 3.4 %copy-start.2 = (bf16[8192,512]{1,0:T(8,128)(2,1)S(1)}, bf16[8192,512]{1,0:T(8,128)(2,1)}, u32[]{:S(2)}) copy-start(bf16[8192,512]{1,0:T(8,128)(2,1)} %weight_ref.13) | copy-start | bytes 25165828
  16.6 15.3 %copy-start.5 = (s32[1,384]{1,0:T(1,128)}, s32[1,384]{1,0:T(1,128)S(1)}, u32[]{:S(2)}) copy-start(s32[1,384]{1,0:T(1,128)S(1)} %get-tuple-element.60.stored_ref.refs_2_) | copy-start | bytes 4612
  16.6 7.7 %collective-permute-start.5 = (bf16[384,2048]{1,0:T(8,128)(2,1)S(1)}, bf16[384,2048]{1,0:T(8,128)(2,1)S(1)}, u32[]{:S(2)}, u32[]{:S(2)}) collective-permute-start(bf16[384,2048]{1,0:T(8,128)(2,1)S(1)} %copy-done), channel_id=1, source_target_pairs={{0,1},{1,0},{2,3},{3,2},{4,5},{5,4},{6,7},{7,6},{8,9},{9,8},{10,11... | collective-permute-start | bytes 4718600 | tf_op jit(solution)/shard_map/ppermute | solution.py:25
  19.4 11.0 %collective-permute-start.9 = (bf16[64,2048]{1,0:T(8,128)(2,1)}, bf16[64,2048]{1,0:T(8,128)(2,1)S(1)}, u32[]{:S(2)}, u32[]{:S(2)}) collective-permute-start(bf16[64,2048]{1,0:T(8,128)(2,1)} %shard_map.64.refs_0_), channel_id=1, source_target_pairs={{0,4},{4,0},{8,12},{12,8},{1,5},{5,1},{9,13},{13,9},{2,6},{6,2},{1... | collective-permute-start | bytes 786440 | tf_op jit(solution)/shard_map/ppermute | solution.py:25
  21.1 22.7 %collective-permute-start.3 = (bf16[384,512]{1,0:T(8,128)(2,1)}, bf16[384,512]{1,0:T(8,128)(2,1)}, u32[]{:S(2)}, u32[]{:S(2)}) collective-permute-start(bf16[384,512]{1,0:T(8,128)(2,1)} %get-tuple-element.53), channel_id=1, source_target_pairs={{0,2},{1,3},{2,0},{3,1},{4,6},{5,7},{6,4},{7,5},{8,10},{9,11},{10,... | collective-permute-start | bytes 1179656 | tf_op jit(solution)/shard_map/ppermute | solution.py:25
  24.4 7.6 %collective-permute-start.10 = (bf16[64,2048]{1,0:T(8,128)(2,1)}, bf16[64,2048]{1,0:T(8,128)(2,1)S(1)}, u32[]{:S(2)}, u32[]{:S(2)}) collective-permute-start(bf16[64,2048]{1,0:T(8,128)(2,1)} %collective-permute-done.4.refs_2_), channel_id=1, source_target_pairs={{0,16},{16,0},{1,17},{17,1},{2,18},{18,2},{3,19},{19,3},{4,20},{20... | collective-permute-start | bytes 786440 | tf_op jit(solution)/shard_map/ppermute | solution.py:25
  26.3 9.4 %collective-permute-start.8 = (bf16[64,512]{1,0:T(8,128)(2,1)}, bf16[64,512]{1,0:T(8,128)(2,1)S(1)}, u32[]{:S(2)}, u32[]{:S(2)}) collective-permute-start(bf16[64,512]{1,0:T(8,128)(2,1)} %bitcast.9.refs_5_), channel_id=1, source_target_pairs={{0,8},{4,12},{8,0},{12,4},{16,28},{20,24},{24,20},{28,16},{1,9},{5... | collective-permute-start | bytes 196616 | tf_op jit(solution)/shard_map/ppermute | solution.py:301
  30.5 13.3 %collective-permute-start.6 = (bf16[64,512]{1,0:T(8,128)(2,1)}, bf16[64,512]{1,0:T(8,128)(2,1)}, u32[]{:S(2)}, u32[]{:S(2)}) collective-permute-start(bf16[64,512]{1,0:T(8,128)(2,1)} %bitcast.9.refs_5_), channel_id=1, source_target_pairs={{0,4},{4,0},{8,12},{12,8},{1,5},{5,1},{9,13},{13,9},{2,6},{6,2},{1... | collective-permute-start | bytes 196616 | tf_op jit(solution)/shard_map/ppermute | solution.py:25
  35.7 4.5 %collective-permute-start.13 = (f32[64,384]{1,0:T(8,128)S(1)}, f32[64,384]{1,0:T(8,128)S(1)}, u32[]{:S(2)}, u32[]{:S(2)}) collective-permute-start(f32[64,384]{1,0:T(8,128)S(1)} %shard_map.69), channel_id=1, source_target_pairs={{0,1},{1,0},{2,3},{3,2},{4,5},{5,4},{6,7},{7,6},{8,9},{9,8},{10,11... | collective-permute-start | bytes 294920 | tf_op jit(solution)/shard_map/ppermute | solution.py:25
  35.7 6.7 %collective-permute-start.12 = (bf16[384,1536]{1,0:T(8,128)(2,1)}, bf16[384,1536]{1,0:T(8,128)(2,1)S(1)}, u32[]{:S(2)}, u32[]{:S(2)}) collective-permute-start(bf16[384,1536]{1,0:T(8,128)(2,1)} %collective-permute-done.7.refs_0_), channel_id=1, source_target_pairs={{0,1},{1,0},{2,3},{3,2},{4,5},{5,4},{6,7},{7,6},{8,9},{9,8},{10,11... | collective-permute-start | bytes 3538952 | tf_op jit(solution)/shard_map/ppermute | solution.py:25
  38.4 5.4 %collective-permute-start.11 = (bf16[64,512]{1,0:T(8,128)(2,1)S(1)}, bf16[64,512]{1,0:T(8,128)(2,1)S(1)}, u32[]{:S(2)}, u32[]{:S(2)}) collective-permute-start(bf16[64,512]{1,0:T(8,128)(2,1)S(1)} %collective-permute-done.8.refs_7_), channel_id=1, source_target_pairs={{0,16},{16,0},{1,17},{17,1},{2,18},{18,2},{3,19},{19,3},{4,20},{20... | collective-permute-start | bytes 196616 | tf_op jit(solution)/shard_map/ppermute | solution.py:25
  40.8 4.5 %collective-permute-start.15 = (bf16[64,384]{1,0:T(8,128)(2,1)}, bf16[64,384]{1,0:T(8,128)(2,1)}, u32[]{:S(2)}, u32[]{:S(2)}) collective-permute-start(bf16[64,384]{1,0:T(8,128)(2,1)} %get-tuple-element.83), channel_id=1, source_target_pairs={{0,2},{1,3},{2,0},{3,1},{4,6},{5,7},{6,4},{7,5},{8,10},{9,11},{10,... | collective-permute-start | bytes 147464 | tf_op jit(solution)/shard_map/ppermute | solution.py:25
  43.7 2.0 %copy-start.6 = (s32[1,384]{1,0:T(1,128)S(1)}, s32[1,384]{1,0:T(1,128)}, u32[]{:S(2)}) copy-start(s32[1,384]{1,0:T(1,128)} %copy-done.5) | copy-start | bytes 4612
  43.8 2.0 %collective-permute-start.14 = (bf16[384,512]{1,0:T(8,128)(2,1)}, bf16[384,512]{1,0:T(8,128)(2,1)S(1)}, u32[]{:S(2)}, u32[]{:S(2)}) collective-permute-start(bf16[384,512]{1,0:T(8,128)(2,1)} %collective-permute-done.3.refs_0_), channel_id=1, source_target_pairs={{0,1},{1,0},{2,3},{3,2},{4,5},{5,4},{6,7},{7,6},{8,9},{9,8},{10,11... | collective-permute-start | bytes 1179656 | tf_op jit(solution)/shard_map/ppermute | solution.py:25

commit v21 on v20

--- a/solution.py
+++ b/solution.py
@@ -136,6 +136,17 @@
     out_ref, held_ref, rows_ref, sems = refs[count + 1 :]
     start_tiles(tile, depth, places, features, weight_ref, held_ref, rows_ref, sems)
     out_ref[...] = given[...]
+    add_tiles(held_ref, rows_ref, sems, out_ref)
+
+
+def products_and_sum_kernel(tile, depth, places, weight_ref, *refs):
+    count = len(places)
+    features, (given, one, other) = refs[:count], refs[count : count + 3]
+    out_ref, sum_ref, rounded_ref, held_ref, rows_ref, sems = refs[count + 3 :]
+    start_tiles(tile, depth, places, features, weight_ref, held_ref, rows_ref, sems)
+    out_ref[...] = given[...]
+    sum_ref[...] = one[...] + other[...]
+    rounded_ref[...] = sum_ref[...].astype(rounded_ref.dtype)
     add_tiles(held_ref, rows_ref, sems, out_ref)
 
 
@@ -326,7 +337,7 @@
     total = products([(0, depth // 2, depth // 2, depth // 2)], [here], total)
     fetched, neighbour, total = chained(fetched, neighbour, total)
     swapped = swap(fetched)
-    total = products([(1, 0, 0, depth)], [neighbour], total)
+    total = products([(1, 0, 0, depth // 2)], [neighbour], total)
     total, up = chained(total, lowrank_up_weight[0])
     fetched_up, single_up = fetch_far(up), fetch_near(up)
     single, swapped, total = chained(single, swapped, total)
@@ -346,21 +357,32 @@
             pltpu.SemaphoreType.DMA((1 + slots, tiles)),
         ],
     )(tokens, stored, *downs)
-    far[0], fetched_up, partial = chained(far[0], fetched_up, partial)
-    swapped_up = swap(fetched_up)
+    received = flipped(partial, "tensor", 1)
+    total, partial = chained(total, partial)
+    total = products([(1, depth // 2, depth // 2, depth // 2)], [neighbour], total)
+    far[0], fetched_up, received, total = chained(far[0], fetched_up, received, total)
     ups = [up] + single_up
-    for pair in zip(fetched_up, swapped_up):
+    for pair in zip(fetched_up, swap(fetched_up)):
         ups += pair
     near = across(0)
-    total = products(far_places(0), far[0], total)
-    flip = 1
+    places = far_places(0)
+    total, partial, rounded = call(
+        functools.partial(products_and_sum_kernel, tile, depth, places),
+        [
+            jax.ShapeDtypeStruct((rows, columns), jnp.float32),
+            jax.ShapeDtypeStruct((rank, rows), jnp.float32),
+            jax.ShapeDtypeStruct((rank, rows), jnp.bfloat16),
+        ],
+        [ANYWHERE] + [ANYWHERE] * len(places) + [VECTOR] * 3,
+        tile_scratch(tile, rows, places, columns),
+        [VECTOR] * 3,
+    )(frozen_projection_weight, *far[0], total, partial, received)
+    flip = CORES
     while flip < tensors // 2:
-        received = flipped(partial, "tensor", flip)
-        if flip == 1:
-            received, total = chained(received, total)
-        partial += received
+        partial += flipped(partial, "tensor", flip)
+        rounded = partial.astype(jnp.bfloat16)
         flip *= 2
-    more = flipped(partial.astype(jnp.bfloat16), "tensor", flip)
+    more = flipped(rounded, "tensor", flip)
     total, partial = chained(total, partial)
     total = products(near_places(0), near, total)
     far[1], ups, total = chained(far[1], ups, total)

time: 48.3 us -> 48.4 us (level)
  waiting for transfers between devices: 6.27 us -> 7.19 us
  other arithmetic: 0.62 us -> 0 us
  starting transfers between devices: 17.7 us -> 17.1 us
    pallas_call x0 -> x1, Pallas kernels: none -> 2.46 us  [body(): call(functools.partial(products_and_sum_kernel, tile, depth, places), [ja...]
    pallas_call x5, Pallas kernels: 7.87 us -> 5.74 us  [products(): call(functools.partial(products_kernel, tile, depth, places), jax.ShapeDt...]
    ppermute x14, waiting for transfers between devices: 4.27 us -> 5.2 us  [flipped(): return lax.ppermute(value, axis, [(i, i ^ flip) for i in range(count)])]
    convert_element_type x1 -> x0, other arithmetic: 0.62 us -> none  [body(): more = flipped(partial.astype(jnp.bfloat16), 'tensor', flip)]
    ppermute x14, starting transfers between devices: 11.9 us -> 11.3 us  [flipped(): return lax.ppermute(value, axis, [(i, i ^ flip) for i in range(count)])]
  transfers between devices with their start and end apart: 16 -> 16, of which waited for: 5 -> 7; matrix products, arithmetic and copies ran while one was open for 1% -> 0% of each run, Pallas kernels for 31% -> 32%
where the time goes in v21:
time: 48.4 us; the launch traced here: 48 us
  Pallas kernels  17.3 us (36%)
  starting transfers between devices  17.1 us (35%)
  waiting for transfers between devices  7.19 us (15%)
  local copies, waits for them, and re-layouts  6.24 us (13%)
    ppermute x14, starting transfers between devices, flipped(): return lax.ppermute(value, axis, [(i, i ^ flip) for i in range(count)])  11.3 us
    ppermute x2, starting transfers between devices, fetch_far(): lax.ppermute(value, ('parts', 'adapter'), route)  5.82 us
    pallas_call x5, Pallas kernels, products(): call(functools.partial(products_kernel, tile, depth, places), jax.ShapeDt...  5.74 us
    ppermute x14, waiting for transfers between devices, flipped(): return lax.ppermute(value, axis, [(i, i ^ flip) for i in range(count)])  5.2 us
    unnamed x14, local copies, waits for them, and re-layouts  5.17 us
    pallas_call x1, Pallas kernels, body(): call(functools.partial(shrink_kernel, tile, flips, pairs, slots), jax.Sha...  2.46 us
    pallas_call x1, Pallas kernels, body(): call(functools.partial(products_and_sum_kernel, tile, depth, places), [ja...  2.46 us
    pallas_call x1, Pallas kernels, body(): call(functools.partial(cut_kernel, edges), [jax.ShapeDtypeStruct((rows, b...  2.23 us
  transfers between devices with their start and end apart: 16, of which 7 were waited for; matrix products, arithmetic and copies ran while one was open for 0% of the time, Pallas kernels for 32%

profile of v21, /device:TPU:0, one launch (start us, length us, event | category | flops | bytes accessed | tf_op | source)
XLA Modules:
  0.0 48.0 jit_solution(2492646899579049106)
XLA Ops:
  0.0 1.1 %dynamic-slice_bitcast_fusion = (bf16[16,2048]{1,0:T(8,128)(2,1)S(1)}, bf16[16,2048]{1,0:T(8,128)(2,1)S(1)}, bf16[16,2048]{1,0:T(8,128)(2,1)S(1)}, bf16[16,2048]{1,0:T(8,128)(2,1)S(1)}) fusion(bf16[1,8192,16]{1,2,0:T(8,128)(2,1)} %param.10, s32[]{:T(128)S(6)} %select_n.15, s32[]{:T(128)S(6)} %select_n.13, s32[]{:T(128)S(6)} %select_n.12, s32[]{:T(128)S(6)} %select_n.14), kind=kLoop, calls=%fused_computation | loop fusion | bytes 524304 | tf_op jit(solution)/shard_map/dynamic_slice | solution.py:241
  1.6 2.6 %collective-permute-start.1 = (bf16[16,2048]{1,0:T(8,128)(2,1)S(1)}, bf16[16,2048]{1,0:T(8,128)(2,1)S(1)}, u32[]{:S(2)}, u32[]{:S(2)}) collective-permute-start(bf16[16,2048]{1,0:T(8,128)(2,1)S(1)} %get-tuple-element.50), channel_id=1, source_target_pairs={{0,2},{1,3},{2,0},{3,1},{4,6},{5,7},{6,4},{7,5},{8,10},{9,11},{10,... | collective-permute-start | bytes 196616 | tf_op jit(solution)/shard_map/ppermute | solution.py:25
  4.3 2.2 %shard_map.66 = (bf16[384,1536]{1,0:T(8,128)(2,1)}, bf16[384,512]{1,0:T(8,128)(2,1)}) custom-call(bf16[384,2048]{1,0:T(8,128)(2,1)} %tokens_ref.1), custom_call_target="tpu_custom_call" | custom-call | tf_op jit(solution)/shard_map/pallas_call | solution.py:247
  6.5 1.8 %collective-permute-start.7 = (bf16[384,1536]{1,0:T(8,128)(2,1)}, bf16[384,1536]{1,0:T(8,128)(2,1)}, u32[]{:S(2)}, u32[]{:S(2)}) collective-permute-start(bf16[384,1536]{1,0:T(8,128)(2,1)} %get-tuple-element.63), channel_id=1, source_target_pairs={{0,2},{1,3},{2,0},{3,1},{4,6},{5,7},{6,4},{7,5},{8,10},{9,11},{10,... | collective-permute-start | bytes 3538952 | tf_op jit(solution)/shard_map/ppermute | solution.py:25
  9.1 2.7 %collective-permute-start.4 = (bf16[64,2048]{1,0:T(8,128)(2,1)}, bf16[64,2048]{1,0:T(8,128)(2,1)}, u32[]{:S(2)}, u32[]{:S(2)}) collective-permute-start(bf16[64,2048]{1,0:T(8,128)(2,1)} %shard_map.64.refs_0_), channel_id=1, source_target_pairs={{0,8},{4,12},{8,0},{12,4},{16,28},{20,24},{24,20},{28,16},{1,9},{5... | collective-permute-start | bytes 786440 | tf_op jit(solution)/shard_map/ppermute | solution.py:312
  11.7 3.4 %copy-done.1 = bf16[8192,512]{1,0:T(8,128)(2,1)S(1)} copy-done((bf16[8192,512]{1,0:T(8,128)(2,1)S(1)}, bf16[8192,512]{1,0:T(8,128)(2,1)}, u32[]{:S(2)}) %copy-start.1) | copy-done | bytes 8388632
  15.1 1.5 %shard_map.65 = (f32[384,512]{1,0:T(8,128)S(1)}, s32[1,384]{1,0:T(1,128)S(1)}) custom-call(s32[4]{0:T(128)S(1)} %copy-done.4, s32[1,384]{1,0:T(1,128)S(1)} %bitcast.18, bf16[8192,512]{1,0:T(8,128)(2,1)S(1)} %copy-done.1, bf16[384,2048]{1,0:T(8,128)(2,1)S(1)} %copy-done), custom_call_target="tpu_custom_call" | custom-call | flops 99999997952 | tf_op jit(solution)/shard_map/pallas_call | solution.py:323
  16.7 1.8 %copy-done.2 = bf16[8192,512]{1,0:T(8,128)(2,1)S(1)} copy-done((bf16[8192,512]{1,0:T(8,128)(2,1)S(1)}, bf16[8192,512]{1,0:T(8,128)(2,1)}, u32[]{:S(2)}) %copy-start.2) | copy-done | bytes 8388632
  19.4 1.6 %collective-permute-start.9 = (bf16[64,2048]{1,0:T(8,128)(2,1)}, bf16[64,2048]{1,0:T(8,128)(2,1)S(1)}, u32[]{:S(2)}, u32[]{:S(2)}) collective-permute-start(bf16[64,2048]{1,0:T(8,128)(2,1)} %shard_map.64.refs_0_), channel_id=1, source_target_pairs={{0,4},{4,0},{8,12},{12,8},{1,5},{5,1},{9,13},{13,9},{2,6},{6,2},{1... | collective-permute-start | bytes 786440 | tf_op jit(solution)/shard_map/ppermute | solution.py:25
  21.1 1.3 %collective-permute-start.3 = (bf16[384,512]{1,0:T(8,128)(2,1)}, bf16[384,512]{1,0:T(8,128)(2,1)}, u32[]{:S(2)}, u32[]{:S(2)}) collective-permute-start(bf16[384,512]{1,0:T(8,128)(2,1)} %get-tuple-element.57), channel_id=1, source_target_pairs={{0,2},{1,3},{2,0},{3,1},{4,6},{5,7},{6,4},{7,5},{8,10},{9,11},{10,... | collective-permute-start | bytes 1179656 | tf_op jit(solution)/shard_map/ppermute | solution.py:25
  22.4 2.0 %collective-permute-done.4.refs_2_ = bf16[64,2048]{1,0:T(8,128)(2,1)} collective-permute-done((bf16[64,2048]{1,0:T(8,128)(2,1)}, bf16[64,2048]{1,0:T(8,128)(2,1)}, u32[]{:S(2)}, u32[]{:S(2)}) %collective-permute-start.4) | collective-permute-done | bytes 262176 | tf_op jit(solution)/shard_map/ppermute | solution.py:312
  24.4 1.0 %shard_map.68.refs_1_ = f32[384,512]{1,0:T(8,128)S(1)} custom-call(bf16[8192,512]{1,0:T(8,128)(2,1)S(1)} %copy-done.2, bf16[384,2048]{1,0:T(8,128)(2,1)S(1)} %collective-permute-done.5.refs_0_, f32[384,512]{1,0:T(8,128)S(1)} %shard_map.67.refs_1_), custom_call_target="tpu_custom_call" | custom-call | flops 99999997952 | tf_op jit(solution)/shard_map/pallas_call | solution.py:294
  25.3 3.2 %collective-permute-start.8 = (bf16[64,512]{1,0:T(8,128)(2,1)}, bf16[64,512]{1,0:T(8,128)(2,1)}, u32[]{:S(2)}, u32[]{:S(2)}) collective-permute-start(bf16[64,512]{1,0:T(8,128)(2,1)} %bitcast.9.refs_5_), channel_id=1, source_target_pairs={{0,8},{4,12},{8,0},{12,4},{16,28},{20,24},{24,20},{28,16},{1,9},{5... | collective-permute-start | bytes 196616 | tf_op jit(solution)/shard_map/ppermute | solution.py:312
  28.5 2.0 %collective-permute-done.9.refs_1_ = bf16[64,2048]{1,0:T(8,128)(2,1)S(1)} collective-permute-done((bf16[64,2048]{1,0:T(8,128)(2,1)}, bf16[64,2048]{1,0:T(8,128)(2,1)S(1)}, u32[]{:S(2)}, u32[]{:S(2)}) %collective-permute-start.9) | collective-permute-done | bytes 262176 | tf_op jit(solution)/shard_map/ppermute | solution.py:25
  30.5 1.5 %collective-permute-done.10.refs_3_ = bf16[64,2048]{1,0:T(8,128)(2,1)S(1)} collective-permute-done((bf16[64,2048]{1,0:T(8,128)(2,1)}, bf16[64,2048]{1,0:T(8,128)(2,1)S(1)}, u32[]{:S(2)}, u32[]{:S(2)}) %collective-permute-start.10) | collective-permute-done | bytes 262176 | tf_op jit(solution)/shard_map/ppermute | solution.py:25
  31.9 2.5 %shard_map.69.refs_2_ = f32[64,384]{1,0:T(8,128)S(1)} custom-call(bf16[384,2048]{1,0:T(8,128)(2,1)S(1)} %copy-done, s32[1,384]{1,0:T(1,128)S(1)} %get-tuple-element.64.stored_ref.refs_2_, bf16[64,2048]{1,0:T(8,128)(2,1)} %shard_map.64.refs_0_, bf16[64,2048]{1,0:T(8,128)(2,1)S(1)} %collective-permute-done.9.refs_1_, ...), custom_call_target="tpu_custom_call" | custom-call | flops 99999997952 | tf_op jit(solution)/shard_map/pallas_call | solution.py:349
  34.5 1.0 %shard_map.70.refs_1_ = f32[384,512]{1,0:T(8,128)S(1)} custom-call(bf16[8192,512]{1,0:T(8,128)(2,1)S(1)} %copy-done.2, bf16[384,2048]{1,0:T(8,128)(2,1)S(1)} %collective-permute-done.5.refs_0_, f32[384,512]{1,0:T(8,128)S(1)} %shard_map.68.refs_1_), custom_call_target="tpu_custom_call" | custom-call | flops 99999997952 | tf_op jit(solution)/shard_map/pallas_call | solution.py:294
  36.1 2.5 %shard_map.71 = (f32[384,512]{1,0:T(8,128)S(1)}, f32[64,384]{1,0:T(8,128)S(1)}, bf16[64,384]{1,0:T(8,128)(2,1)}) custom-call(bf16[8192,512]{1,0:T(8,128)(2,1)S(1)} %copy-done.2, bf16[384,1536]{1,0:T(8,128)(2,1)} %collective-permute-done.7.refs_0_, f32[384,512]{1,0:T(8,128)S(1)} %shard_map.70.refs_1_, f32[64,384]{1,0:T(8,128)S(1)} %shard_map.69.refs_2_, ...), custom_call_target="tpu_custom_call" | custom-call | flops 99999997952 | tf_op jit(solution)/shard_map/pallas_call | solution.py:369
  38.5 1.5 %collective-permute-start.12 = (bf16[64,512]{1,0:T(8,128)(2,1)}, bf16[64,512]{1,0:T(8,128)(2,1)S(1)}, u32[]{:S(2)}, u32[]{:S(2)}) collective-permute-start(bf16[64,512]{1,0:T(8,128)(2,1)} %collective-permute-done.8.refs_7_), channel_id=1, source_target_pairs={{0,16},{16,0},{1,17},{17,1},{2,18},{18,2},{3,19},{19,3},{4,20},{20... | collective-permute-start | bytes 196616 | tf_op jit(solution)/shard_map/ppermute | solution.py:25
  40.0 1.5 %collective-permute-start.15 = (bf16[64,384]{1,0:T(8,128)(2,1)}, bf16[64,384]{1,0:T(8,128)(2,1)}, u32[]{:S(2)}, u32[]{:S(2)}) collective-permute-start(bf16[64,384]{1,0:T(8,128)(2,1)} %get-tuple-element.81), channel_id=1, source_target_pairs={{0,2},{1,3},{2,0},{3,1},{4,6},{5,7},{6,4},{7,5},{8,10},{9,11},{10,... | collective-permute-start | bytes 147464 | tf_op jit(solution)/shard_map/ppermute | solution.py:25
  41.5 1.4 %shard_map.72.refs_1_ = f32[384,512]{1,0:T(8,128)S(1)} custom-call(bf16[8192,512]{1,0:T(8,128)(2,1)S(1)} %copy-done.2, bf16[384,1536]{1,0:T(8,128)(2,1)S(1)} %collective-permute-done.13.refs_0_, f32[384,512]{1,0:T(8,128)S(1)} %get-tuple-element.79.refs_1_), custom_call_target="tpu_custom_call" | custom-call | flops 99999997952 | tf_op jit(solution)/shard_map/pallas_call | solution.py:294
  42.9 1.0 %collective-permute-done.3.refs_0_ = bf16[384,512]{1,0:T(8,128)(2,1)} collective-permute-done((bf16[384,512]{1,0:T(8,128)(2,1)}, bf16[384,512]{1,0:T(8,128)(2,1)}, u32[]{:S(2)}, u32[]{:S(2)}) %collective-permute-start.3) | collective-permute-done | bytes 393248 | tf_op jit(solution)/shard_map/ppermute | solution.py:25
  43.9 1.4 %shard_map.73.refs_1_ = f32[384,512]{1,0:T(8,128)S(1)} custom-call(bf16[8192,512]{1,0:T(8,128)(2,1)S(1)} %copy-done.2, bf16[384,512]{1,0:T(8,128)(2,1)} %collective-permute-done.3.refs_0_, f32[384,512]{1,0:T(8,128)S(1)} %shard_map.72.refs_1_), custom_call_target="tpu_custom_call" | custom-call | flops 99999997952 | tf_op jit(solution)/shard_map/pallas_call | solution.py:294
  45.8 2.2 %shard_map.74 = bf16[384,512]{1,0:T(8,128)(2,1)} custom-call(bf16[8192,512]{1,0:T(8,128)(2,1)S(1)} %copy-done.2, bf16[384,512]{1,0:T(8,128)(2,1)S(1)} %collective-permute-done.14.refs_0_, f32[384,512]{1,0:T(8,128)S(1)} %shard_map.73.refs_1_, s32[1,384]{1,0:T(1,128)S(1)} %copy-done.6, f32[64,384]{1,0:T(8,128)S(1)} %get-tuple-element.85.refs_3_, ...), custom_call_target="tpu_custom_call" | custom-call | flops 99999997952 | tf_op jit(solution)/shard_map/pallas_call | solution.py:394
  (34 shorter events, 3.6 us)
Async XLA Ops:
  0.0 11.7 %copy-start = (bf16[384,2048]{1,0:T(8,128)(2,1)S(1)}, bf16[384,2048]{1,0:T(8,128)(2,1)}, u32[]{:S(2)}) copy-start(bf16[384,2048]{1,0:T(8,128)(2,1)} %tokens_ref.1) | copy-start | bytes 4718596
  0.0 11.7 %copy-start.3 = (s32[384,1]{0,1:T(1,128)S(1)}, s32[384,1]{0,1:T(1,128)}, u32[]{:S(2)}) copy-start(s32[384,1]{0,1:T(1,128)} %param.7) | copy-start | bytes 4612
  0.0 11.7 %copy-start.4 = (s32[4]{0:T(128)S(1)}, s32[4]{0:T(128)}, u32[]{:S(2)}) copy-start(s32[4]{0:T(128)} %placement_ref.1) | copy-start | bytes 52
  1.1 7.2 %collective-permute-start = (bf16[16,2048]{1,0:T(8,128)(2,1)S(1)}, bf16[16,2048]{1,0:T(8,128)(2,1)S(1)}, u32[]{:S(2)}, u32[]{:S(2)}) collective-permute-start(bf16[16,2048]{1,0:T(8,128)(2,1)S(1)} %get-tuple-element.49), channel_id=1, source_target_pairs={{0,1},{1,0},{2,3},{3,2},{4,5},{5,4},{6,7},{7,6},{8,9},{9,8},{10,11... | collective-permute-start | bytes 196616 | tf_op jit(solution)/shard_map/ppermute | solution.py:25
  1.6 6.7 %collective-permute-start.1 = (bf16[16,2048]{1,0:T(8,128)(2,1)S(1)}, bf16[16,2048]{1,0:T(8,128)(2,1)S(1)}, u32[]{:S(2)}, u32[]{:S(2)}) collective-permute-start(bf16[16,2048]{1,0:T(8,128)(2,1)S(1)} %get-tuple-element.50), channel_id=1, source_target_pairs={{0,2},{1,3},{2,0},{3,1},{4,6},{5,7},{6,4},{7,5},{8,10},{9,11},{10,... | collective-permute-start | bytes 196616 | tf_op jit(solution)/shard_map/ppermute | solution.py:25
  4.2 4.1 %collective-permute-start.2 = (bf16[16,2048]{1,0:T(8,128)(2,1)S(1)}, bf16[16,2048]{1,0:T(8,128)(2,1)S(1)}, u32[]{:S(2)}, u32[]{:S(2)}) collective-permute-start(bf16[16,2048]{1,0:T(8,128)(2,1)S(1)} %get-tuple-element.51), channel_id=1, source_target_pairs={{0,3},{1,2},{2,1},{3,0},{4,7},{5,6},{6,5},{7,4},{8,11},{9,10},{10,... | collective-permute-start | bytes 196616 | tf_op jit(solution)/shard_map/ppermute | solution.py:25
  6.5 29.2 %collective-permute-start.7 = (bf16[384,1536]{1,0:T(8,128)(2,1)}, bf16[384,1536]{1,0:T(8,128)(2,1)}, u32[]{:S(2)}, u32[]{:S(2)}) collective-permute-start(bf16[384,1536]{1,0:T(8,128)(2,1)} %get-tuple-element.63), channel_id=1, source_target_pairs={{0,2},{1,3},{2,0},{3,1},{4,6},{5,7},{6,4},{7,5},{8,10},{9,11},{10,... | collective-permute-start | bytes 3538952 | tf_op jit(solution)/shard_map/ppermute | solution.py:25
  9.1 15.3 %collective-permute-start.4 = (bf16[64,2048]{1,0:T(8,128)(2,1)}, bf16[64,2048]{1,0:T(8,128)(2,1)}, u32[]{:S(2)}, u32[]{:S(2)}) collective-permute-start(bf16[64,2048]{1,0:T(8,128)(2,1)} %shard_map.64.refs_0_), channel_id=1, source_target_pairs={{0,8},{4,12},{8,0},{12,4},{16,28},{20,24},{24,20},{28,16},{1,9},{5... | collective-permute-start | bytes 786440 | tf_op jit(solution)/shard_map/ppermute | solution.py:312
  11.7 3.4 %copy-start.1 = (bf16[8192,512]{1,0:T(8,128)(2,1)S(1)}, bf16[8192,512]{1,0:T(8,128)(2,1)}, u32[]{:S(2)}) copy-start(bf16[8192,512]{1,0:T(8,128)(2,1)} %weight_ref.15) | copy-start | bytes 25165828
  15.1 3.4 %copy-start.2 = (bf16[8192,512]{1,0:T(8,128)(2,1)S(1)}, bf16[8192,512]{1,0:T(8,128)(2,1)}, u32[]{:S(2)}) copy-start(bf16[8192,512]{1,0:T(8,128)(2,1)} %weight_ref.15) | copy-start | bytes 25165828
  16.6 15.3 %copy-start.5 = (s32[1,384]{1,0:T(1,128)}, s32[1,384]{1,0:T(1,128)S(1)}, u32[]{:S(2)}) copy-start(s32[1,384]{1,0:T(1,128)S(1)} %get-tuple-element.64.stored_ref.refs_2_) | copy-start | bytes 4612
  16.6 7.7 %collective-permute-start.5 = (bf16[384,2048]{1,0:T(8,128)(2,1)S(1)}, bf16[384,2048]{1,0:T(8,128)(2,1)S(1)}, u32[]{:S(2)}, u32[]{:S(2)}) collective-permute-start(bf16[384,2048]{1,0:T(8,128)(2,1)S(1)} %copy-done), channel_id=1, source_target_pairs={{0,1},{1,0},{2,3},{3,2},{4,5},{5,4},{6,7},{7,6},{8,9},{9,8},{10,11... | collective-permute-start | bytes 4718600 | tf_op jit(solution)/shard_map/ppermute | solution.py:25
  19.4 11.0 %collective-permute-start.9 = (bf16[64,2048]{1,0:T(8,128)(2,1)}, bf16[64,2048]{1,0:T(8,128)(2,1)S(1)}, u32[]{:S(2)}, u32[]{:S(2)}) collective-permute-start(bf16[64,2048]{1,0:T(8,128)(2,1)} %shard_map.64.refs_0_), channel_id=1, source_target_pairs={{0,4},{4,0},{8,12},{12,8},{1,5},{5,1},{9,13},{13,9},{2,6},{6,2},{1... | collective-permute-start | bytes 786440 | tf_op jit(solution)/shard_map/ppermute | solution.py:25
  21.1 22.8 %collective-permute-start.3 = (bf16[384,512]{1,0:T(8,128)(2,1)}, bf16[384,512]{1,0:T(8,128)(2,1)}, u32[]{:S(2)}, u32[]{:S(2)}) collective-permute-start(bf16[384,512]{1,0:T(8,128)(2,1)} %get-tuple-element.57), channel_id=1, source_target_pairs={{0,2},{1,3},{2,0},{3,1},{4,6},{5,7},{6,4},{7,5},{8,10},{9,11},{10,... | collective-permute-start | bytes 1179656 | tf_op jit(solution)/shard_map/ppermute | solution.py:25
  24.4 7.6 %collective-permute-start.10 = (bf16[64,2048]{1,0:T(8,128)(2,1)}, bf16[64,2048]{1,0:T(8,128)(2,1)S(1)}, u32[]{:S(2)}, u32[]{:S(2)}) collective-permute-start(bf16[64,2048]{1,0:T(8,128)(2,1)} %collective-permute-done.4.refs_2_), channel_id=1, source_target_pairs={{0,16},{16,0},{1,17},{17,1},{2,18},{18,2},{3,19},{19,3},{4,20},{20... | collective-permute-start | bytes 786440 | tf_op jit(solution)/shard_map/ppermute | solution.py:25
  25.3 10.3 %collective-permute-start.8 = (bf16[64,512]{1,0:T(8,128)(2,1)}, bf16[64,512]{1,0:T(8,128)(2,1)}, u32[]{:S(2)}, u32[]{:S(2)}) collective-permute-start(bf16[64,512]{1,0:T(8,128)(2,1)} %bitcast.9.refs_5_), channel_id=1, source_target_pairs={{0,8},{4,12},{8,0},{12,4},{16,28},{20,24},{24,20},{28,16},{1,9},{5... | collective-permute-start | bytes 196616 | tf_op jit(solution)/shard_map/ppermute | solution.py:312
  30.5 13.4 %collective-permute-start.6 = (bf16[64,512]{1,0:T(8,128)(2,1)}, bf16[64,512]{1,0:T(8,128)(2,1)}, u32[]{:S(2)}, u32[]{:S(2)}) collective-permute-start(bf16[64,512]{1,0:T(8,128)(2,1)} %bitcast.9.refs_5_), channel_id=1, source_target_pairs={{0,4},{4,0},{8,12},{12,8},{1,5},{5,1},{9,13},{13,9},{2,6},{6,2},{1... | collective-permute-start | bytes 196616 | tf_op jit(solution)/shard_map/ppermute | solution.py:25
  34.4 1.4 %collective-permute-start.11 = (f32[64,384]{1,0:T(8,128)S(1)}, f32[64,384]{1,0:T(8,128)S(1)}, u32[]{:S(2)}, u32[]{:S(2)}) collective-permute-start(f32[64,384]{1,0:T(8,128)S(1)} %shard_map.69.refs_2_), channel_id=1, source_target_pairs={{0,1},{1,0},{2,3},{3,2},{4,5},{5,4},{6,7},{7,6},{8,9},{9,8},{10,11... | collective-permute-start | bytes 294920 | tf_op jit(solution)/shard_map/ppermute | solution.py:25
  35.8 5.7 %collective-permute-start.13 = (bf16[384,1536]{1,0:T(8,128)(2,1)}, bf16[384,1536]{1,0:T(8,128)(2,1)S(1)}, u32[]{:S(2)}, u32[]{:S(2)}) collective-permute-start(bf16[384,1536]{1,0:T(8,128)(2,1)} %collective-permute-done.7.refs_0_), channel_id=1, source_target_pairs={{0,1},{1,0},{2,3},{3,2},{4,5},{5,4},{6,7},{7,6},{8,9},{9,8},{10,11... | collective-permute-start | bytes 3538952 | tf_op jit(solution)/shard_map/ppermute | solution.py:25
  38.5 5.3 %collective-permute-start.12 = (bf16[64,512]{1,0:T(8,128)(2,1)}, bf16[64,512]{1,0:T(8,128)(2,1)S(1)}, u32[]{:S(2)}, u32[]{:S(2)}) collective-permute-start(bf16[64,512]{1,0:T(8,128)(2,1)} %collective-permute-done.8.refs_7_), channel_id=1, source_target_pairs={{0,16},{16,0},{1,17},{17,1},{2,18},{18,2},{3,19},{19,3},{4,20},{20... | collective-permute-start | bytes 196616 | tf_op jit(solution)/shard_map/ppermute | solution.py:25
  40.0 5.3 %collective-permute-start.15 = (bf16[64,384]{1,0:T(8,128)(2,1)}, bf16[64,384]{1,0:T(8,128)(2,1)}, u32[]{:S(2)}, u32[]{:S(2)}) collective-permute-start(bf16[64,384]{1,0:T(8,128)(2,1)} %get-tuple-element.81), channel_id=1, source_target_pairs={{0,2},{1,3},{2,0},{3,1},{4,6},{5,7},{6,4},{7,5},{8,10},{9,11},{10,... | collective-permute-start | bytes 147464 | tf_op jit(solution)/shard_map/ppermute | solution.py:25
  42.9 2.9 %copy-start.6 = (s32[1,384]{1,0:T(1,128)S(1)}, s32[1,384]{1,0:T(1,128)}, u32[]{:S(2)}) copy-start(s32[1,384]{1,0:T(1,128)} %copy-done.5) | copy-start | bytes 4612
  43.9 1.9 %collective-permute-start.14 = (bf16[384,512]{1,0:T(8,128)(2,1)}, bf16[384,512]{1,0:T(8,128)(2,1)S(1)}, u32[]{:S(2)}, u32[]{:S(2)}) collective-permute-start(bf16[384,512]{1,0:T(8,128)(2,1)} %collective-permute-done.3.refs_0_), channel_id=1, source_target_pairs={{0,1},{1,0},{2,3},{3,2},{4,5},{5,4},{6,7},{7,6},{8,9},{9,8},{10,11... | collective-permute-start | bytes 1179656 | tf_op jit(solution)/shard_map/ppermute | solution.py:25

commit v22 on v21

--- a/solution.py
+++ b/solution.py
@@ -11,7 +11,7 @@
 LOWRANK_SCALE = 2.0
 CORES = 2
 LANES = 128
-CUTS = (0.75,)
+CUTS = (0.0625, 0.8125)
 MIB = 1024 * 1024
 FREE = pl.CostEstimate(flops=0, bytes_accessed=0, transcendentals=0)
 LONG = pl.CostEstimate(flops=10**11, bytes_accessed=0, transcendentals=0)
@@ -41,6 +41,11 @@
     )
 
 
+def tile_of(*widths):
+    whole = math.gcd(*widths)
+    return max(t for t in range(1, whole + 1) if whole % t == 0 and (t == whole or t % LANES == 0) and t <= 640)
+
+
 def run_copies(pairs, sems):
     copies = [
         pltpu.make_async_copy(source, target, sems.at[i]) for i, (source, target) in enumerate(pairs)
@@ -51,11 +56,19 @@
         copy.wait()
 
 
+def first_cut_kernel(width, source_ref, out_ref, sems):
+    run_copies([(source_ref.at[:, pl.ds(0, width)], out_ref)], sems)
+
+
 def cut_kernel(edges, source_ref, *refs):
     outs, (held_ref, sems) = refs[:-2], refs[-2:]
     steps, rows = held_ref.shape[:2]
     copies = [
-        pltpu.make_async_copy(source_ref.at[pl.ds(i * rows, rows)], held_ref.at[i], sems.at[0, i])
+        pltpu.make_async_copy(
+            source_ref.at[pl.ds(i * rows, rows), pl.ds(edges[0], edges[-1] - edges[0])],
+            held_ref.at[i],
+            sems.at[0, i],
+        )
         for i in range(steps)
     ]
     for copy in copies:
@@ -66,7 +79,7 @@
         for m, (a, b, out) in enumerate(zip(edges, edges[1:], outs)):
             leaving.append(
                 pltpu.make_async_copy(
-                    held_ref.at[i, :, pl.ds(a, b - a)],
+                    held_ref.at[i, :, pl.ds(a - edges[0], b - a)],
                     out.at[pl.ds(i * rows, rows)],
                     sems.at[1 + m, i],
                 )
@@ -76,13 +89,15 @@
         copy.wait()
 
 
-def order_kernel(rank_part, *refs):
+def order_kernel(down_ref, other_ref, *refs):
     pieces, out_ref, sems = refs[:-2], refs[-2], refs[-1]
     me = lax.axis_index("tensor")
+    part, depth = down_ref.shape[0], out_ref.shape[1]
+    mine = pl.ds(pl.multiple_of(me * depth, LANES), depth)
     run_copies(
         [
-            (piece, out_ref.at[pl.ds(pl.multiple_of((me ^ f) * rank_part, rank_part), rank_part)])
-            for f, piece in enumerate(pieces)
+            (piece, out_ref.at[pl.ds(pl.multiple_of((me ^ f) * part, part), part)])
+            for f, piece in enumerate((down_ref.at[:, mine], other_ref.at[:, mine], *pieces))
         ],
         sems,
     )
@@ -233,53 +248,66 @@
     parts = lax.axis_size("parts")
     me = lax.axis_index("tensor")
     rank, columns = lowrank_up_weight.shape[1:]
-    edges = [0] + [int(depth * cut) // LANES * LANES for cut in CUTS] + [depth]
-    tile = math.gcd(*edges)
+    edges = [0] + [max(LANES, int(depth * cut) // LANES * LANES) for cut in CUTS] + [depth]
+    tile = tile_of(depth)
 
     down = lowrank_down_weight[0].T
-    pieces = [
-        lax.dynamic_slice_in_dim(down, (me ^ flip) * depth, depth, axis=1)
-        for flip in range(tensors)
-    ]
-    uncut, pieces = chained(tokens, pieces)
-    steps = 6
-    chunks = list(
-        call(
-            functools.partial(cut_kernel, edges),
-            [jax.ShapeDtypeStruct((rows, b - a), tokens.dtype) for a, b in zip(edges, edges[1:])],
-            [ANYWHERE],
-            [
-                pltpu.VMEM((steps, rows // steps, depth), tokens.dtype),
-                pltpu.SemaphoreType.DMA((len(edges), steps)),
-            ],
-            [ANYWHERE] * (len(edges) - 1),
-            cost=FREE,
-            mib=56,
-        )(uncut)
-    )
-    pieces = [pieces[0]] + [flipped(pieces[f], "tensor", f) for f in range(1, tensors)]
+
+    def cut(array, first):
+        ranges, steps = edges[first:], 6
+        return list(
+            call(
+                functools.partial(cut_kernel, ranges),
+                [jax.ShapeDtypeStruct((rows, b - a), array.dtype) for a, b in zip(ranges, ranges[1:])],
+                [ANYWHERE],
+                [
+                    pltpu.VMEM((steps, rows // steps, ranges[-1] - ranges[0]), array.dtype),
+                    pltpu.SemaphoreType.DMA((len(ranges), steps)),
+                ],
+                [ANYWHERE] * (len(ranges) - 1),
+                mib=56,
+            )(array)
+        )
+
+    def slice_for(array, flip):
+        return lax.dynamic_slice_in_dim(array, (me ^ flip) * depth, depth, axis=1)
+
+    other = flipped(down, "tensor", 1)
+    small = call(
+        functools.partial(first_cut_kernel, edges[1]),
+        jax.ShapeDtypeStruct((rows, edges[1]), tokens.dtype),
+        [ANYWHERE],
+        [pltpu.SemaphoreType.DMA((1,))],
+        mib=56,
+    )(tokens)
+    hops = range(CORES, tensors, CORES)
+    far = [[flipped(small, "tensor", hop) for hop in hops]]
+    other, rest, uncut = chained(other, down, tokens)
+    pieces = [slice_for(rest, flip) for flip in range(CORES, tensors)]
+    uncut, pieces = chained(uncut, pieces)
+    chunks = [small] + cut(uncut, 1)
+    pieces = [flipped(piece, "tensor", CORES + i) for i, piece in enumerate(pieces)]
     if down.shape[0] % 16 == 0:
         own = call(
-            functools.partial(order_kernel, down.shape[0]),
+            order_kernel,
             jax.ShapeDtypeStruct((rank, depth), down.dtype),
             [ANYWHERE] * tensors,
             [pltpu.SemaphoreType.DMA((tensors,))],
             ANYWHERE,
             cost=FREE,
-        )(*pieces)
+        )(down, other, *pieces)
     else:
+        pieces = [slice_for(down, 0), slice_for(other, 0)] + pieces
         none = jnp.zeros((), down.dtype)
         own = jnp.concatenate(
             [sum(jnp.where((me ^ f) == j, pieces[f], none) for f in range(tensors)) for j in range(tensors)],
             axis=0,
         )
 
-    hops = range(CORES, tensors, CORES)
-
     def send(m):
         return [flipped(chunks[m], "tensor", hop) for hop in hops]
 
-    far = [send(0)]
+    far.append(send(1))
 
     def across(m):
         return [flipped(value, "tensor", 1) for value in far[m]]
@@ -291,6 +319,7 @@
         return [(hop ^ 1, edges[m], 0, edges[m + 1] - edges[m]) for hop in hops]
 
     def products(places, features, total):
+        tile = tile_of(*[place[3] for place in places])
         return call(
             functools.partial(products_kernel, tile, depth, places),
             jax.ShapeDtypeStruct((rows, columns), jnp.float32),
@@ -317,8 +346,9 @@
     def swap(values):
         return [flipped(value, "parts", 1) for value in values]
 
-    own, here = chained(own, tokens)
+    own, here, far[0] = chained(own, tokens, far[0])
     fetched = fetch_far(own)
+    near = across(0)
     places = [(0, 0, 0, depth // 2)]
     total, stored = call(
         functools.partial(first_kernel, tile, depth, places, slots),
@@ -330,11 +360,13 @@
         tile_scratch(tile, rows, places, columns),
         [VECTOR, VECTOR],
     )(placement, tenant.reshape(1, rows), frozen_projection_weight, here)
-    total, own, there, chunks[1] = chained(total, own, tokens, chunks[1])
+    total, own, there, chunks[2] = chained(total, own, tokens, chunks[2])
     neighbour = flipped(there, "tensor", 1)
-    far.append(send(1))
+    far.append(send(2))
     single = fetch_near(own)
     total = products([(0, depth // 2, depth // 2, depth // 2)], [here], total)
+    near, total = chained(near, total)
+    total = products(far_places(0) + near_places(0), far[0] + near, total)
     fetched, neighbour, total = chained(fetched, neighbour, total)
     swapped = swap(fetched)
     total = products([(1, 0, 0, depth // 2)], [neighbour], total)
@@ -360,12 +392,13 @@
     received = flipped(partial, "tensor", 1)
     total, partial = chained(total, partial)
     total = products([(1, depth // 2, depth // 2, depth // 2)], [neighbour], total)
-    far[0], fetched_up, received, total = chained(far[0], fetched_up, received, total)
+    far[1], fetched_up, received, total = chained(far[1], fetched_up, received, total)
     ups = [up] + single_up
     for pair in zip(fetched_up, swap(fetched_up)):
         ups += pair
-    near = across(0)
-    places = far_places(0)
+    near = across(1)
+    places = far_places(1)
+    tile = tile_of(*[place[3] for place in places])
     total, partial, rounded = call(
         functools.partial(products_and_sum_kernel, tile, depth, places),
         [
@@ -376,7 +409,7 @@
         [ANYWHERE] + [ANYWHERE] * len(places) + [VECTOR] * 3,
         tile_scratch(tile, rows, places, columns),
         [VECTOR] * 3,
-    )(frozen_projection_weight, *far[0], total, partial, received)
+    )(frozen_projection_weight, *far[1], total, partial, received)
     flip = CORES
     while flip < tensors // 2:
         partial += flipped(partial, "tensor", flip)
@@ -384,13 +417,14 @@
         flip *= 2
     more = flipped(rounded, "tensor", flip)
     total, partial = chained(total, partial)
-    total = products(near_places(0), near, total)
-    far[1], ups, total = chained(far[1], ups, total)
-    near = across(1)
-    total = products(far_places(1), far[1], total)
+    total = products(near_places(1), near, total)
+    far[2], ups, total = chained(far[2], ups, total)
+    near = across(2)
+    total = products(far_places(2), far[2], total)
     near, more, total = chained(near, more, total)
 
-    places = near_places(1)
+    places = near_places(2)
+    tile = tile_of(*[place[3] for place in places])
     return call(
         functools.partial(last_kernel, tile, depth, places, flips, pairs, slots),
         jax.ShapeDtypeStruct((rows, columns), jnp.bfloat16),

time: 48.4 us -> 50.7 us (1.048)
  Pallas kernels: 17.3 us -> 20.2 us
  starting transfers between devices: 17.1 us -> 18.3 us
  local copies, waits for them, and re-layouts: 6.24 us -> 5.19 us
  waiting for transfers between devices: 7.19 us -> 6.29 us
    ppermute x14 -> x16, starting transfers between devices: 11.3 us -> 13.4 us  [flipped(): return lax.ppermute(value, axis, [(i, i ^ flip) for i in range(count)])]
    pallas_call x2 -> x3, Pallas kernels: 2.97 us -> 4.58 us  [the longest x1 2.31 us: cut(): call(functools.partial(cut_kernel, ranges), [jax.ShapeDtypeStruct((rows,...]
    ppermute x2, waiting for transfers between devices: 1.99 us -> 0.63 us  [fetch_far(): lax.ppermute(value, ('parts', 'adapter'), route)]
    pallas_call x5 -> x6, Pallas kernels: 5.74 us -> 6.98 us  [products(): call(functools.partial(products_kernel, tile, depth, places), jax.ShapeDt...]
    dynamic_slice x1, local copies, waits for them, and re-layouts: 1.07 us -> 0.01 us  [slice_for(): return lax.dynamic_slice_in_dim(array, (me ^ flip) * depth, depth, axis=1)]
    ppermute x2, starting transfers between devices: 5.82 us -> 4.93 us  [fetch_far(): lax.ppermute(value, ('parts', 'adapter'), route)]
    ppermute x14 -> x16, waiting for transfers between devices: 5.2 us -> 5.65 us  [flipped(): return lax.ppermute(value, axis, [(i, i ^ flip) for i in range(count)])]
    unnamed x14 -> x16, local copies, waits for them, and re-layouts: 5.17 us -> 5.18 us
  transfers between devices with their start and end apart: 16 -> 18, of which waited for: 7 -> 7; matrix products, arithmetic and copies ran while one was open for 0% -> 0% of each run, Pallas kernels for 32% -> 36%
where the time goes in v22:
time: 50.7 us; the launch traced here: 50.3 us
  Pallas kernels  20.2 us (40%)
  starting transfers between devices  18.3 us (36%)
  waiting for transfers between devices  6.29 us (12%)
  local copies, waits for them, and re-layouts  5.19 us (10%)
    ppermute x16, starting transfers between devices, flipped(): return lax.ppermute(value, axis, [(i, i ^ flip) for i in range(count)])  13.4 us
    pallas_call x6, Pallas kernels, products(): call(functools.partial(products_kernel, tile, depth, places), jax.ShapeDt...  6.98 us
    ppermute x16, waiting for transfers between devices, flipped(): return lax.ppermute(value, axis, [(i, i ^ flip) for i in range(count)])  5.65 us
    unnamed x16, local copies, waits for them, and re-layouts  5.18 us
    ppermute x2, starting transfers between devices, fetch_far(): lax.ppermute(value, ('parts', 'adapter'), route)  4.93 us
    pallas_call x1, Pallas kernels, body(): call(functools.partial(shrink_kernel, tile, flips, pairs, slots), jax.Sha...  2.49 us
    pallas_call x1, Pallas kernels, body(): call(functools.partial(products_and_sum_kernel, tile, depth, places), [ja...  2.46 us
    pallas_call x1, Pallas kernels, cut(): call(functools.partial(cut_kernel, ranges), [jax.ShapeDtypeStruct((rows,...  2.31 us
  transfers between devices with their start and end apart: 18, of which 7 were waited for; matrix products, arithmetic and copies ran while one was open for 0% of the time, Pallas kernels for 36%

profile of v22, /device:TPU:0, one launch (start us, length us, event | category | flops | bytes accessed | tf_op | source)
XLA Modules:
  0.0 50.3 jit_solution(8169380026162205739)
XLA Ops:
  0.5 1.5 %shard_map.65 = bf16[384,128]{1,0:T(8,128)(2,1)} custom-call(bf16[384,2048]{1,0:T(8,128)(2,1)} %tokens_ref.1), custom_call_target="tpu_custom_call" | custom-call | flops 99999997952 | tf_op jit(solution)/shard_map/pallas_call | solution.py:276
  2.0 2.6 %collective-permute-start.3 = (bf16[384,128]{1,0:T(8,128)(2,1)}, bf16[384,128]{1,0:T(8,128)(2,1)S(1)}, u32[]{:S(2)}, u32[]{:S(2)}) collective-permute-start(bf16[384,128]{1,0:T(8,128)(2,1)} %shard_map.65), channel_id=1, source_target_pairs={{0,2},{1,3},{2,0},{3,1},{4,6},{5,7},{6,4},{7,5},{8,10},{9,11},{10,... | collective-permute-start | bytes 294920 | tf_op jit(solution)/shard_map/ppermute | solution.py:25
  4.8 1.4 %collective-permute-start.2 = (bf16[16,2048]{1,0:T(8,128)(2,1)S(1)}, bf16[16,2048]{1,0:T(8,128)(2,1)S(1)}, u32[]{:S(2)}, u32[]{:S(2)}) collective-permute-start(bf16[16,2048]{1,0:T(8,128)(2,1)S(1)} %get-tuple-element.56), channel_id=1, source_target_pairs={{0,3},{1,2},{2,1},{3,0},{4,7},{5,6},{6,5},{7,4},{8,11},{9,10},{10,... | collective-permute-start | bytes 196616 | tf_op jit(solution)/shard_map/ppermute | solution.py:25
  6.2 2.3 %shard_map.67 = (bf16[384,1536]{1,0:T(8,128)(2,1)}, bf16[384,384]{1,0:T(8,128)(2,1)}) custom-call(bf16[384,2048]{1,0:T(8,128)(2,1)} %tokens_ref.1), custom_call_target="tpu_custom_call" | custom-call | flops 99999997952 | tf_op jit(solution)/shard_map/pallas_call | solution.py:259
  11.6 2.7 %collective-permute-start.5 = (bf16[64,2048]{1,0:T(8,128)(2,1)}, bf16[64,2048]{1,0:T(8,128)(2,1)}, u32[]{:S(2)}, u32[]{:S(2)}) collective-permute-start(bf16[64,2048]{1,0:T(8,128)(2,1)} %shard_map.64.refs_0_), channel_id=1, source_target_pairs={{0,8},{4,12},{8,0},{12,4},{16,28},{20,24},{24,20},{28,16},{1,9},{5... | collective-permute-start | bytes 786440 | tf_op jit(solution)/shard_map/ppermute | solution.py:341
  14.3 3.4 %copy-done.1 = bf16[8192,512]{1,0:T(8,128)(2,1)S(1)} copy-done((bf16[8192,512]{1,0:T(8,128)(2,1)S(1)}, bf16[8192,512]{1,0:T(8,128)(2,1)}, u32[]{:S(2)}) %copy-start.1) | copy-done | bytes 8388632
  17.7 1.5 %shard_map.66 = (f32[384,512]{1,0:T(8,128)S(1)}, s32[1,384]{1,0:T(1,128)S(1)}) custom-call(s32[4]{0:T(128)S(1)} %copy-done.5, s32[1,384]{1,0:T(1,128)S(1)} %bitcast.8, bf16[8192,512]{1,0:T(8,128)(2,1)S(1)} %copy-done.1, bf16[384,2048]{1,0:T(8,128)(2,1)S(1)} %copy-done.3), custom_call_target="tpu_custom_call" | custom-call | flops 99999997952 | tf_op jit(solution)/shard_map/pallas_call | solution.py:353
  19.3 1.8 %copy-done.2 = bf16[8192,512]{1,0:T(8,128)(2,1)S(1)} copy-done((bf16[8192,512]{1,0:T(8,128)(2,1)S(1)}, bf16[8192,512]{1,0:T(8,128)(2,1)}, u32[]{:S(2)}) %copy-start.2) | copy-done | bytes 8388632
  21.0 1.0 %shard_map.68.refs_2_ = f32[384,512]{1,0:T(8,128)S(1)} custom-call(bf16[8192,512]{1,0:T(8,128)(2,1)S(1)} %copy-done.2, bf16[384,2048]{1,0:T(8,128)(2,1)S(1)} %copy-done.3, f32[384,512]{1,0:T(8,128)S(1)} %get-tuple-element.65.refs_1_), custom_call_target="tpu_custom_call" | custom-call | flops 99999997952 | tf_op jit(solution)/shard_map/pallas_call | solution.py:323
  22.1 1.6 %collective-permute-start.11 = (bf16[64,2048]{1,0:T(8,128)(2,1)}, bf16[64,2048]{1,0:T(8,128)(2,1)}, u32[]{:S(2)}, u32[]{:S(2)}) collective-permute-start(bf16[64,2048]{1,0:T(8,128)(2,1)} %shard_map.64.refs_0_), channel_id=1, source_target_pairs={{0,4},{4,0},{8,12},{12,8},{1,5},{5,1},{9,13},{13,9},{2,6},{6,2},{1... | collective-permute-start | bytes 786440 | tf_op jit(solution)/shard_map/ppermute | solution.py:25
  23.7 1.5 %collective-permute-start.4 = (bf16[384,384]{1,0:T(8,128)(2,1)}, bf16[384,384]{1,0:T(8,128)(2,1)}, u32[]{:S(2)}, u32[]{:S(2)}) collective-permute-start(bf16[384,384]{1,0:T(8,128)(2,1)} %get-tuple-element.62), channel_id=1, source_target_pairs={{0,2},{1,3},{2,0},{3,1},{4,6},{5,7},{6,4},{7,5},{8,10},{9,11},{10,... | collective-permute-start | bytes 884744 | tf_op jit(solution)/shard_map/ppermute | solution.py:25
  25.3 1.1 %shard_map.69.refs_1_ = f32[384,512]{1,0:T(8,128)S(1)} custom-call(bf16[8192,512]{1,0:T(8,128)(2,1)S(1)} %copy-done.2, bf16[384,128]{1,0:T(8,128)(2,1)S(1)} %collective-permute-done.3.refs_0_, bf16[384,128]{1,0:T(8,128)(2,1)S(1)} %collective-permute-done.7.refs_1_, f32[384,512]{1,0:T(8,128)S(1)} %shard_map.68.refs_2_), custom_call_target="tpu_custom_call" | custom-call | flops 99999997952 | tf_op jit(solution)/shard_map/pallas_call | solution.py:323
  27.0 1.0 %collective-permute-start.12 = (bf16[64,2048]{1,0:T(8,128)(2,1)}, bf16[64,2048]{1,0:T(8,128)(2,1)S(1)}, u32[]{:S(2)}, u32[]{:S(2)}) collective-permute-start(bf16[64,2048]{1,0:T(8,128)(2,1)} %collective-permute-done.5.refs_2_), channel_id=1, source_target_pairs={{0,16},{16,0},{1,17},{17,1},{2,18},{18,2},{3,19},{19,3},{4,20},{20... | collective-permute-start | bytes 786440 | tf_op jit(solution)/shard_map/ppermute | solution.py:25
  29.0 2.2 %collective-permute-start.10 = (bf16[64,512]{1,0:T(8,128)(2,1)}, bf16[64,512]{1,0:T(8,128)(2,1)}, u32[]{:S(2)}, u32[]{:S(2)}) collective-permute-start(bf16[64,512]{1,0:T(8,128)(2,1)} %bitcast.4.refs_5_), channel_id=1, source_target_pairs={{0,8},{4,12},{8,0},{12,4},{16,28},{20,24},{24,20},{28,16},{1,9},{5... | collective-permute-start | bytes 196616 | tf_op jit(solution)/shard_map/ppermute | solution.py:341
  31.2 1.3 %collective-permute-done.11.refs_1_ = bf16[64,2048]{1,0:T(8,128)(2,1)} collective-permute-done((bf16[64,2048]{1,0:T(8,128)(2,1)}, bf16[64,2048]{1,0:T(8,128)(2,1)}, u32[]{:S(2)}, u32[]{:S(2)}) %collective-permute-start.11) | collective-permute-done | bytes 262176 | tf_op jit(solution)/shard_map/ppermute | solution.py:25
  32.7 2.1 %collective-permute-done.12.refs_3_ = bf16[64,2048]{1,0:T(8,128)(2,1)S(1)} collective-permute-done((bf16[64,2048]{1,0:T(8,128)(2,1)}, bf16[64,2048]{1,0:T(8,128)(2,1)S(1)}, u32[]{:S(2)}, u32[]{:S(2)}) %collective-permute-start.12) | collective-permute-done | bytes 262176 | tf_op jit(solution)/shard_map/ppermute | solution.py:25
  34.8 2.5 %shard_map.71.refs_2_ = f32[64,384]{1,0:T(8,128)S(1)} custom-call(bf16[384,2048]{1,0:T(8,128)(2,1)S(1)} %copy-done.3, s32[1,384]{1,0:T(1,128)S(1)} %get-tuple-element.72.stored_ref.refs_2_, bf16[64,2048]{1,0:T(8,128)(2,1)} %shard_map.64.refs_0_, bf16[64,2048]{1,0:T(8,128)(2,1)} %collective-permute-done.11.refs_1_, ...), custom_call_target="tpu_custom_call" | custom-call | flops 99999997952 | tf_op jit(solution)/shard_map/pallas_call | solution.py:381
  37.4 1.0 %shard_map.72.refs_1_ = f32[384,512]{1,0:T(8,128)S(1)} custom-call(bf16[8192,512]{1,0:T(8,128)(2,1)S(1)} %copy-done.2, bf16[384,2048]{1,0:T(8,128)(2,1)S(1)} %collective-permute-done.6.refs_0_, f32[384,512]{1,0:T(8,128)S(1)} %shard_map.70.refs_1_), custom_call_target="tpu_custom_call" | custom-call | flops 99999997952 | tf_op jit(solution)/shard_map/pallas_call | solution.py:323
  39.0 2.5 %shard_map.73 = (f32[384,512]{1,0:T(8,128)S(1)}, f32[64,384]{1,0:T(8,128)S(1)}, bf16[64,384]{1,0:T(8,128)(2,1)}) custom-call(bf16[8192,512]{1,0:T(8,128)(2,1)S(1)} %copy-done.2, bf16[384,1536]{1,0:T(8,128)(2,1)} %collective-permute-done.9.refs_0_, f32[384,512]{1,0:T(8,128)S(1)} %shard_map.72.refs_1_, f32[64,384]{1,0:T(8,128)S(1)} %shard_map.71.refs_2_, ...), custom_call_target="tpu_custom_call" | custom-call | flops 99999997952 | tf_op jit(solution)/shard_map/pallas_call | solution.py:402
  41.4 1.8 %collective-permute-start.14 = (bf16[64,512]{1,0:T(8,128)(2,1)}, bf16[64,512]{1,0:T(8,128)(2,1)S(1)}, u32[]{:S(2)}, u32[]{:S(2)}) collective-permute-start(bf16[64,512]{1,0:T(8,128)(2,1)} %collective-permute-done.10.refs_7_), channel_id=1, source_target_pairs={{0,16},{16,0},{1,17},{17,1},{2,18},{18,2},{3,19},{19,3},{4,20},{20... | collective-permute-start | bytes 196616 | tf_op jit(solution)/shard_map/ppermute | solution.py:25
  43.2 1.5 %collective-permute-start.17 = (bf16[64,384]{1,0:T(8,128)(2,1)}, bf16[64,384]{1,0:T(8,128)(2,1)}, u32[]{:S(2)}, u32[]{:S(2)}) collective-permute-start(bf16[64,384]{1,0:T(8,128)(2,1)} %get-tuple-element.89), channel_id=1, source_target_pairs={{0,2},{1,3},{2,0},{3,1},{4,6},{5,7},{6,4},{7,5},{8,10},{9,11},{10,... | collective-permute-start | bytes 147464 | tf_op jit(solution)/shard_map/ppermute | solution.py:25
  44.8 1.4 %shard_map.74.refs_1_ = f32[384,512]{1,0:T(8,128)S(1)} custom-call(bf16[8192,512]{1,0:T(8,128)(2,1)S(1)} %copy-done.2, bf16[384,1536]{1,0:T(8,128)(2,1)S(1)} %collective-permute-done.15.refs_0_, f32[384,512]{1,0:T(8,128)S(1)} %get-tuple-element.87.refs_1_), custom_call_target="tpu_custom_call" | custom-call | flops 99999997952 | tf_op jit(solution)/shard_map/pallas_call | solution.py:323
  46.3 1.5 %shard_map.75.refs_1_ = f32[384,512]{1,0:T(8,128)S(1)} custom-call(bf16[8192,512]{1,0:T(8,128)(2,1)S(1)} %copy-done.2, bf16[384,384]{1,0:T(8,128)(2,1)} %collective-permute-done.4.refs_0_, f32[384,512]{1,0:T(8,128)S(1)} %shard_map.74.refs_1_), custom_call_target="tpu_custom_call" | custom-call | flops 99999997952 | tf_op jit(solution)/shard_map/pallas_call | solution.py:323
  48.1 2.2 %shard_map.76 = bf16[384,512]{1,0:T(8,128)(2,1)} custom-call(bf16[8192,512]{1,0:T(8,128)(2,1)S(1)} %copy-done.2, bf16[384,384]{1,0:T(8,128)(2,1)S(1)} %collective-permute-done.16.refs_0_, f32[384,512]{1,0:T(8,128)S(1)} %shard_map.75.refs_1_, s32[1,384]{1,0:T(1,128)S(1)} %copy-done.7, f32[64,384]{1,0:T(8,128)S(1)} %get-tuple-element.93.refs_3_, ...), custom_call_target="tpu_custom_call" | custom-call | flops 99999997952 | tf_op jit(solution)/shard_map/pallas_call | solution.py:428
  (42 shorter events, 6.5 us)
Async XLA Ops:
  0.0 4.6 %copy-start = (bf16[1,8192,16]{1,2,0:T(8,128)(2,1)S(1)}, bf16[1,8192,16]{1,2,0:T(8,128)(2,1)}, u32[]{:S(2)}) copy-start(bf16[1,8192,16]{1,2,0:T(8,128)(2,1)} %param.10) | copy-start | bytes 786436
  0.0 4.6 %collective-permute-start = (bf16[16,8192]{1,0:T(8,128)(2,1)}, bf16[16,8192]{1,0:T(8,128)(2,1)S(1)}, u32[]{:S(2)}, u32[]{:S(2)}) collective-permute-start(bf16[16,8192]{1,0:T(8,128)(2,1)} %bitcast.5), channel_id=1, source_target_pairs={{0,1},{1,0},{2,3},{3,2},{4,5},{5,4},{6,7},{7,6},{8,9},{9,8},{10,11... | collective-permute-start | bytes 786440 | tf_op jit(solution)/shard_map/ppermute | solution.py:25
  2.0 9.6 %collective-permute-start.3 = (bf16[384,128]{1,0:T(8,128)(2,1)}, bf16[384,128]{1,0:T(8,128)(2,1)S(1)}, u32[]{:S(2)}, u32[]{:S(2)}) collective-permute-start(bf16[384,128]{1,0:T(8,128)(2,1)} %shard_map.65), channel_id=1, source_target_pairs={{0,2},{1,3},{2,0},{3,1},{4,6},{5,7},{6,4},{7,5},{8,10},{9,11},{10,... | collective-permute-start | bytes 294920 | tf_op jit(solution)/shard_map/ppermute | solution.py:25
  4.6 9.7 %copy-start.3 = (bf16[384,2048]{1,0:T(8,128)(2,1)S(1)}, bf16[384,2048]{1,0:T(8,128)(2,1)}, u32[]{:S(2)}) copy-start(bf16[384,2048]{1,0:T(8,128)(2,1)} %tokens_ref.1) | copy-start | bytes 4718596
  4.6 9.7 %copy-start.4 = (s32[384,1]{0,1:T(1,128)S(1)}, s32[384,1]{0,1:T(1,128)}, u32[]{:S(2)}) copy-start(s32[384,1]{0,1:T(1,128)} %param.7) | copy-start | bytes 4612
  4.6 9.6 %copy-start.5 = (s32[4]{0:T(128)S(1)}, s32[4]{0:T(128)}, u32[]{:S(2)}) copy-start(s32[4]{0:T(128)} %placement_ref.1) | copy-start | bytes 52
  4.6 5.2 %collective-permute-start.1 = (bf16[16,2048]{1,0:T(8,128)(2,1)S(1)}, bf16[16,2048]{1,0:T(8,128)(2,1)S(1)}, u32[]{:S(2)}, u32[]{:S(2)}) collective-permute-start(bf16[16,2048]{1,0:T(8,128)(2,1)S(1)} %get-tuple-element.55), channel_id=1, source_target_pairs={{0,2},{1,3},{2,0},{3,1},{4,6},{5,7},{6,4},{7,5},{8,10},{9,11},{10,... | collective-permute-start | bytes 196616 | tf_op jit(solution)/shard_map/ppermute | solution.py:25
  4.8 6.0 %collective-permute-start.2 = (bf16[16,2048]{1,0:T(8,128)(2,1)S(1)}, bf16[16,2048]{1,0:T(8,128)(2,1)S(1)}, u32[]{:S(2)}, u32[]{:S(2)}) collective-permute-start(bf16[16,2048]{1,0:T(8,128)(2,1)S(1)} %get-tuple-element.56), channel_id=1, source_target_pairs={{0,3},{1,2},{2,1},{3,0},{4,7},{5,6},{6,5},{7,4},{8,11},{9,10},{10,... | collective-permute-start | bytes 196616 | tf_op jit(solution)/shard_map/ppermute | solution.py:25
  8.6 29.8 %collective-permute-start.9 = (bf16[384,1536]{1,0:T(8,128)(2,1)}, bf16[384,1536]{1,0:T(8,128)(2,1)}, u32[]{:S(2)}, u32[]{:S(2)}) collective-permute-start(bf16[384,1536]{1,0:T(8,128)(2,1)} %get-tuple-element.71), channel_id=1, source_target_pairs={{0,2},{1,3},{2,0},{3,1},{4,6},{5,7},{6,4},{7,5},{8,10},{9,11},{10,... | collective-permute-start | bytes 3538952 | tf_op jit(solution)/shard_map/ppermute | solution.py:25
  11.6 15.5 %collective-permute-start.5 = (bf16[64,2048]{1,0:T(8,128)(2,1)}, bf16[64,2048]{1,0:T(8,128)(2,1)}, u32[]{:S(2)}, u32[]{:S(2)}) collective-permute-start(bf16[64,2048]{1,0:T(8,128)(2,1)} %shard_map.64.refs_0_), channel_id=1, source_target_pairs={{0,8},{4,12},{8,0},{12,4},{16,28},{20,24},{24,20},{28,16},{1,9},{5... | collective-permute-start | bytes 786440 | tf_op jit(solution)/shard_map/ppermute | solution.py:341
  14.3 3.4 %copy-start.1 = (bf16[8192,512]{1,0:T(8,128)(2,1)S(1)}, bf16[8192,512]{1,0:T(8,128)(2,1)}, u32[]{:S(2)}) copy-start(bf16[8192,512]{1,0:T(8,128)(2,1)} %weight_ref.17) | copy-start | bytes 25165828
  19.2 15.7 %copy-start.6 = (s32[1,384]{1,0:T(1,128)}, s32[1,384]{1,0:T(1,128)S(1)}, u32[]{:S(2)}) copy-start(s32[1,384]{1,0:T(1,128)S(1)} %get-tuple-element.72.stored_ref.refs_2_) | copy-start | bytes 4612
  19.2 4.5 %collective-permute-start.7 = (bf16[384,128]{1,0:T(8,128)(2,1)S(1)}, bf16[384,128]{1,0:T(8,128)(2,1)S(1)}, u32[]{:S(2)}, u32[]{:S(2)}) collective-permute-start(bf16[384,128]{1,0:T(8,128)(2,1)S(1)} %collective-permute-done.3.refs_0_), channel_id=1, source_target_pairs={{0,1},{1,0},{2,3},{3,2},{4,5},{5,4},{6,7},{7,6},{8,9},{9,8},{10,11... | collective-permute-start | bytes 294920 | tf_op jit(solution)/shard_map/ppermute | solution.py:25
  22.0 5.0 %collective-permute-start.6 = (bf16[384,2048]{1,0:T(8,128)(2,1)S(1)}, bf16[384,2048]{1,0:T(8,128)(2,1)S(1)}, u32[]{:S(2)}, u32[]{:S(2)}) collective-permute-start(bf16[384,2048]{1,0:T(8,128)(2,1)S(1)} %copy-done.3), channel_id=1, source_target_pairs={{0,1},{1,0},{2,3},{3,2},{4,5},{5,4},{6,7},{7,6},{8,9},{9,8},{10,11... | collective-permute-start | bytes 4718600 | tf_op jit(solution)/shard_map/ppermute | solution.py:25
  22.1 10.5 %collective-permute-start.11 = (bf16[64,2048]{1,0:T(8,128)(2,1)}, bf16[64,2048]{1,0:T(8,128)(2,1)}, u32[]{:S(2)}, u32[]{:S(2)}) collective-permute-start(bf16[64,2048]{1,0:T(8,128)(2,1)} %shard_map.64.refs_0_), channel_id=1, source_target_pairs={{0,4},{4,0},{8,12},{12,8},{1,5},{5,1},{9,13},{13,9},{2,6},{6,2},{1... | collective-permute-start | bytes 786440 | tf_op jit(solution)/shard_map/ppermute | solution.py:25
  23.7 22.5 %collective-permute-start.4 = (bf16[384,384]{1,0:T(8,128)(2,1)}, bf16[384,384]{1,0:T(8,128)(2,1)}, u32[]{:S(2)}, u32[]{:S(2)}) collective-permute-start(bf16[384,384]{1,0:T(8,128)(2,1)} %get-tuple-element.62), channel_id=1, source_target_pairs={{0,2},{1,3},{2,0},{3,1},{4,6},{5,7},{6,4},{7,5},{8,10},{9,11},{10,... | collective-permute-start | bytes 884744 | tf_op jit(solution)/shard_map/ppermute | solution.py:25
  27.0 7.8 %collective-permute-start.12 = (bf16[64,2048]{1,0:T(8,128)(2,1)}, bf16[64,2048]{1,0:T(8,128)(2,1)S(1)}, u32[]{:S(2)}, u32[]{:S(2)}) collective-permute-start(bf16[64,2048]{1,0:T(8,128)(2,1)} %collective-permute-done.5.refs_2_), channel_id=1, source_target_pairs={{0,16},{16,0},{1,17},{17,1},{2,18},{18,2},{3,19},{19,3},{4,20},{20... | collective-permute-start | bytes 786440 | tf_op jit(solution)/shard_map/ppermute | solution.py:25
  29.0 9.4 %collective-permute-start.10 = (bf16[64,512]{1,0:T(8,128)(2,1)}, bf16[64,512]{1,0:T(8,128)(2,1)}, u32[]{:S(2)}, u32[]{:S(2)}) collective-permute-start(bf16[64,512]{1,0:T(8,128)(2,1)} %bitcast.4.refs_5_), channel_id=1, source_target_pairs={{0,8},{4,12},{8,0},{12,4},{16,28},{20,24},{24,20},{28,16},{1,9},{5... | collective-permute-start | bytes 196616 | tf_op jit(solution)/shard_map/ppermute | solution.py:341
  32.5 13.7 %collective-permute-start.8 = (bf16[64,512]{1,0:T(8,128)(2,1)}, bf16[64,512]{1,0:T(8,128)(2,1)}, u32[]{:S(2)}, u32[]{:S(2)}) collective-permute-start(bf16[64,512]{1,0:T(8,128)(2,1)} %bitcast.4.refs_5_), channel_id=1, source_target_pairs={{0,4},{4,0},{8,12},{12,8},{1,5},{5,1},{9,13},{13,9},{2,6},{6,2},{1... | collective-permute-start | bytes 196616 | tf_op jit(solution)/shard_map/ppermute | solution.py:25
  37.3 1.4 %collective-permute-start.13 = (f32[64,384]{1,0:T(8,128)S(1)}, f32[64,384]{1,0:T(8,128)S(1)}, u32[]{:S(2)}, u32[]{:S(2)}) collective-permute-start(f32[64,384]{1,0:T(8,128)S(1)} %shard_map.71.refs_2_), channel_id=1, source_target_pairs={{0,1},{1,0},{2,3},{3,2},{4,5},{5,4},{6,7},{7,6},{8,9},{9,8},{10,11... | collective-permute-start | bytes 294920 | tf_op jit(solution)/shard_map/ppermute | solution.py:25
  38.7 6.1 %collective-permute-start.15 = (bf16[384,1536]{1,0:T(8,128)(2,1)}, bf16[384,1536]{1,0:T(8,128)(2,1)S(1)}, u32[]{:S(2)}, u32[]{:S(2)}) collective-permute-start(bf16[384,1536]{1,0:T(8,128)(2,1)} %collective-permute-done.9.refs_0_), channel_id=1, source_target_pairs={{0,1},{1,0},{2,3},{3,2},{4,5},{5,4},{6,7},{7,6},{8,9},{9,8},{10,11... | collective-permute-start | bytes 3538952 | tf_op jit(solution)/shard_map/ppermute | solution.py:25
  41.4 4.8 %collective-permute-start.14 = (bf16[64,512]{1,0:T(8,128)(2,1)}, bf16[64,512]{1,0:T(8,128)(2,1)S(1)}, u32[]{:S(2)}, u32[]{:S(2)}) collective-permute-start(bf16[64,512]{1,0:T(8,128)(2,1)} %collective-permute-done.10.refs_7_), channel_id=1, source_target_pairs={{0,16},{16,0},{1,17},{17,1},{2,18},{18,2},{3,19},{19,3},{4,20},{20... | collective-permute-start | bytes 196616 | tf_op jit(solution)/shard_map/ppermute | solution.py:25
  43.2 4.6 %collective-permute-start.17 = (bf16[64,384]{1,0:T(8,128)(2,1)}, bf16[64,384]{1,0:T(8,128)(2,1)}, u32[]{:S(2)}, u32[]{:S(2)}) collective-permute-start(bf16[64,384]{1,0:T(8,128)(2,1)} %get-tuple-element.89), channel_id=1, source_target_pairs={{0,2},{1,3},{2,0},{3,1},{4,6},{5,7},{6,4},{7,5},{8,10},{9,11},{10,... | collective-permute-start | bytes 147464 | tf_op jit(solution)/shard_map/ppermute | solution.py:25
  46.2 1.9 %collective-permute-start.16 = (bf16[384,384]{1,0:T(8,128)(2,1)}, bf16[384,384]{1,0:T(8,128)(2,1)S(1)}, u32[]{:S(2)}, u32[]{:S(2)}) collective-permute-start(bf16[384,384]{1,0:T(8,128)(2,1)} %collective-permute-done.4.refs_0_), channel_id=1, source_target_pairs={{0,1},{1,0},{2,3},{3,2},{4,5},{5,4},{6,7},{7,6},{8,9},{9,8},{10,11... | collective-permute-start | bytes 884744 | tf_op jit(solution)/shard_map/ppermute | solution.py:25
  (2 other events, 5.3 us)

commit v23 on v21

--- a/solution.py
+++ b/solution.py
@@ -76,13 +76,15 @@
         copy.wait()
 
 
-def order_kernel(rank_part, *refs):
+def order_kernel(down_ref, other_ref, *refs):
     pieces, out_ref, sems = refs[:-2], refs[-2], refs[-1]
     me = lax.axis_index("tensor")
+    part, depth = down_ref.shape[0], out_ref.shape[1]
+    mine = pl.ds(pl.multiple_of(me * depth, LANES), depth)
     run_copies(
         [
-            (piece, out_ref.at[pl.ds(pl.multiple_of((me ^ f) * rank_part, rank_part), rank_part)])
-            for f, piece in enumerate(pieces)
+            (piece, out_ref.at[pl.ds(pl.multiple_of((me ^ f) * part, part), part)])
+            for f, piece in enumerate((down_ref.at[:, mine], other_ref.at[:, mine], *pieces))
         ],
         sems,
     )
@@ -237,10 +239,12 @@
     tile = math.gcd(*edges)
 
     down = lowrank_down_weight[0].T
-    pieces = [
-        lax.dynamic_slice_in_dim(down, (me ^ flip) * depth, depth, axis=1)
-        for flip in range(tensors)
-    ]
+
+    def slice_for(array, flip):
+        return lax.dynamic_slice_in_dim(array, (me ^ flip) * depth, depth, axis=1)
+
+    other = flipped(down, "tensor", 1)
+    pieces = [slice_for(down, flip) for flip in range(CORES, tensors)]
     uncut, pieces = chained(tokens, pieces)
     steps = 6
     chunks = list(
@@ -257,17 +261,18 @@
             mib=56,
         )(uncut)
     )
-    pieces = [pieces[0]] + [flipped(pieces[f], "tensor", f) for f in range(1, tensors)]
+    pieces = [flipped(piece, "tensor", CORES + i) for i, piece in enumerate(pieces)]
     if down.shape[0] % 16 == 0:
         own = call(
-            functools.partial(order_kernel, down.shape[0]),
+            order_kernel,
             jax.ShapeDtypeStruct((rank, depth), down.dtype),
             [ANYWHERE] * tensors,
             [pltpu.SemaphoreType.DMA((tensors,))],
-            ANYWHERE,
+            VECTOR,
             cost=FREE,
-        )(*pieces)
+        )(down, other, *pieces)
     else:
+        pieces = [slice_for(down, 0), slice_for(other, 0)] + pieces
         none = jnp.zeros((), down.dtype)
         own = jnp.concatenate(
             [sum(jnp.where((me ^ f) == j, pieces[f], none) for f in range(tensors)) for j in range(tensors)],

time: 48.4 us -> 48.4 us (level)
  starting transfers between devices: 17.1 us -> 16.4 us
  waiting for transfers between devices: 7.19 us -> 7.76 us
    ppermute x14, starting transfers between devices: 11.3 us -> 10.6 us  [flipped(): return lax.ppermute(value, axis, [(i, i ^ flip) for i in range(count)])]
    unnamed x14 -> x16, local copies, waits for them, and re-layouts: 5.17 us -> 5.17 us
  transfers between devices with their start and end apart: 16 -> 16, of which waited for: 7 -> 7; matrix products, arithmetic and copies ran while one was open for 0% -> 2% of each run, Pallas kernels for 32% -> 32%
where the time goes in v23:
time: 48.4 us; the launch traced here: 48 us
  Pallas kernels  17.6 us (36%)
  starting transfers between devices  16.4 us (34%)
  waiting for transfers between devices  7.76 us (16%)
  local copies, waits for them, and re-layouts  6.1 us (13%)
    ppermute x14, starting transfers between devices, flipped(): return lax.ppermute(value, axis, [(i, i ^ flip) for i in range(count)])  10.6 us
    ppermute x2, starting transfers between devices, fetch_far(): lax.ppermute(value, ('parts', 'adapter'), route)  5.82 us
    pallas_call x5, Pallas kernels, products(): call(functools.partial(products_kernel, tile, depth, places), jax.ShapeDt...  5.74 us
    ppermute x14, waiting for transfers between devices, flipped(): return lax.ppermute(value, axis, [(i, i ^ flip) for i in range(count)])  5.54 us
    unnamed x16, local copies, waits for them, and re-layouts  5.17 us
    pallas_call x1, Pallas kernels, body(): call(functools.partial(shrink_kernel, tile, flips, pairs, slots), jax.Sha...  2.48 us
    pallas_call x1, Pallas kernels, body(): call(functools.partial(products_and_sum_kernel, tile, depth, places), [ja...  2.46 us
    pallas_call x1, Pallas kernels, body(): call(functools.partial(cut_kernel, edges), [jax.ShapeDtypeStruct((rows, b...  2.23 us
  transfers between devices with their start and end apart: 16, of which 7 were waited for; matrix products, arithmetic and copies ran while one was open for 2% of the time, Pallas kernels for 32%

profile of v23, /device:TPU:0, one launch (start us, length us, event | category | flops | bytes accessed | tf_op | source)
XLA Modules:
  0.0 48.0 jit_solution(10631686991478552480)
XLA Ops:
  1.5 2.7 %collective-permute-start.1 = (bf16[16,2048]{1,0:T(8,128)(2,1)S(1)}, bf16[16,2048]{1,0:T(8,128)(2,1)S(1)}, u32[]{:S(2)}, u32[]{:S(2)}) collective-permute-start(bf16[16,2048]{1,0:T(8,128)(2,1)S(1)} %get-tuple-element.46), channel_id=1, source_target_pairs={{0,2},{1,3},{2,0},{3,1},{4,6},{5,7},{6,4},{7,5},{8,10},{9,11},{10,... | collective-permute-start | bytes 196616 | tf_op jit(solution)/shard_map/ppermute | solution.py:25
  4.2 2.2 %shard_map.66 = (bf16[384,1536]{1,0:T(8,128)(2,1)}, bf16[384,512]{1,0:T(8,128)(2,1)}) custom-call(bf16[384,2048]{1,0:T(8,128)(2,1)} %tokens_ref.1), custom_call_target="tpu_custom_call" | custom-call | tf_op jit(solution)/shard_map/pallas_call | solution.py:251
  6.4 1.7 %collective-permute-start.7 = (bf16[384,1536]{1,0:T(8,128)(2,1)}, bf16[384,1536]{1,0:T(8,128)(2,1)}, u32[]{:S(2)}, u32[]{:S(2)}) collective-permute-start(bf16[384,1536]{1,0:T(8,128)(2,1)} %get-tuple-element.59), channel_id=1, source_target_pairs={{0,2},{1,3},{2,0},{3,1},{4,6},{5,7},{6,4},{7,5},{8,10},{9,11},{10,... | collective-permute-start | bytes 3538952 | tf_op jit(solution)/shard_map/ppermute | solution.py:25
  8.3 1.0 %shard_map.64.refs_0_ = bf16[64,2048]{1,0:T(8,128)(2,1)} custom-call(bf16[16,8192]{1,0:T(8,128)(2,1)S(1)} %bitcast.14, bf16[16,8192]{1,0:T(8,128)(2,1)S(1)} %collective-permute-done.other_ref, bf16[16,2048]{1,0:T(8,128)(2,1)S(1)} %collective-permute-done.1.refs_0_, bf16[16,2048]{1,0:T(8,128)(2,1)S(1)} %collective-permute-done.2.refs_1_), custom_call_target="tpu_custom_call" | custom-call | tf_op jit(solution)/shard_map/pallas_call | solution.py:266
  9.3 2.7 %collective-permute-start.4 = (bf16[64,2048]{1,0:T(8,128)(2,1)}, bf16[64,2048]{1,0:T(8,128)(2,1)}, u32[]{:S(2)}, u32[]{:S(2)}) collective-permute-start(bf16[64,2048]{1,0:T(8,128)(2,1)} %shard_map.64.refs_0_), channel_id=1, source_target_pairs={{0,8},{4,12},{8,0},{12,4},{16,28},{20,24},{24,20},{28,16},{1,9},{5... | collective-permute-start | bytes 786440 | tf_op jit(solution)/shard_map/ppermute | solution.py:317
  11.9 3.4 %copy-done.2 = bf16[8192,512]{1,0:T(8,128)(2,1)S(1)} copy-done((bf16[8192,512]{1,0:T(8,128)(2,1)S(1)}, bf16[8192,512]{1,0:T(8,128)(2,1)}, u32[]{:S(2)}) %copy-start.2) | copy-done | bytes 8388632
  15.3 1.5 %shard_map.65 = (f32[384,512]{1,0:T(8,128)S(1)}, s32[1,384]{1,0:T(1,128)S(1)}) custom-call(s32[4]{0:T(128)S(1)} %copy-done.5, s32[1,384]{1,0:T(1,128)S(1)} %bitcast.15, bf16[8192,512]{1,0:T(8,128)(2,1)S(1)} %copy-done.2, bf16[384,2048]{1,0:T(8,128)(2,1)S(1)} %copy-done), custom_call_target="tpu_custom_call" | custom-call | flops 99999997952 | tf_op jit(solution)/shard_map/pallas_call | solution.py:328
  16.9 1.8 %copy-done.3 = bf16[8192,512]{1,0:T(8,128)(2,1)S(1)} copy-done((bf16[8192,512]{1,0:T(8,128)(2,1)S(1)}, bf16[8192,512]{1,0:T(8,128)(2,1)}, u32[]{:S(2)}) %copy-start.3) | copy-done | bytes 8388632
  19.7 1.6 %collective-permute-start.9 = (bf16[64,2048]{1,0:T(8,128)(2,1)}, bf16[64,2048]{1,0:T(8,128)(2,1)S(1)}, u32[]{:S(2)}, u32[]{:S(2)}) collective-permute-start(bf16[64,2048]{1,0:T(8,128)(2,1)} %shard_map.64.refs_0_), channel_id=1, source_target_pairs={{0,4},{4,0},{8,12},{12,8},{1,5},{5,1},{9,13},{13,9},{2,6},{6,2},{1... | collective-permute-start | bytes 786440 | tf_op jit(solution)/shard_map/ppermute | solution.py:25
  21.3 1.1 %collective-permute-start.3 = (bf16[384,512]{1,0:T(8,128)(2,1)}, bf16[384,512]{1,0:T(8,128)(2,1)}, u32[]{:S(2)}, u32[]{:S(2)}) collective-permute-start(bf16[384,512]{1,0:T(8,128)(2,1)} %get-tuple-element.53), channel_id=1, source_target_pairs={{0,2},{1,3},{2,0},{3,1},{4,6},{5,7},{6,4},{7,5},{8,10},{9,11},{10,... | collective-permute-start | bytes 1179656 | tf_op jit(solution)/shard_map/ppermute | solution.py:25
  22.4 2.2 %collective-permute-done.4.refs_2_ = bf16[64,2048]{1,0:T(8,128)(2,1)} collective-permute-done((bf16[64,2048]{1,0:T(8,128)(2,1)}, bf16[64,2048]{1,0:T(8,128)(2,1)}, u32[]{:S(2)}, u32[]{:S(2)}) %collective-permute-start.4) | collective-permute-done | bytes 262176 | tf_op jit(solution)/shard_map/ppermute | solution.py:317
  24.6 1.0 %shard_map.68.refs_1_ = f32[384,512]{1,0:T(8,128)S(1)} custom-call(bf16[8192,512]{1,0:T(8,128)(2,1)S(1)} %copy-done.3, bf16[384,2048]{1,0:T(8,128)(2,1)S(1)} %collective-permute-done.5.refs_0_, f32[384,512]{1,0:T(8,128)S(1)} %shard_map.67.refs_1_), custom_call_target="tpu_custom_call" | custom-call | flops 99999997952 | tf_op jit(solution)/shard_map/pallas_call | solution.py:299
  25.6 3.2 %collective-permute-start.8 = (bf16[64,512]{1,0:T(8,128)(2,1)}, bf16[64,512]{1,0:T(8,128)(2,1)}, u32[]{:S(2)}, u32[]{:S(2)}) collective-permute-start(bf16[64,512]{1,0:T(8,128)(2,1)} %bitcast.8.refs_5_), channel_id=1, source_target_pairs={{0,8},{4,12},{8,0},{12,4},{16,28},{20,24},{24,20},{28,16},{1,9},{5... | collective-permute-start | bytes 196616 | tf_op jit(solution)/shard_map/ppermute | solution.py:317
  28.7 2.0 %collective-permute-done.9.refs_1_ = bf16[64,2048]{1,0:T(8,128)(2,1)S(1)} collective-permute-done((bf16[64,2048]{1,0:T(8,128)(2,1)}, bf16[64,2048]{1,0:T(8,128)(2,1)S(1)}, u32[]{:S(2)}, u32[]{:S(2)}) %collective-permute-start.9) | collective-permute-done | bytes 262176 | tf_op jit(solution)/shard_map/ppermute | solution.py:25
  30.7 1.5 %collective-permute-done.10.refs_3_ = bf16[64,2048]{1,0:T(8,128)(2,1)S(1)} collective-permute-done((bf16[64,2048]{1,0:T(8,128)(2,1)}, bf16[64,2048]{1,0:T(8,128)(2,1)S(1)}, u32[]{:S(2)}, u32[]{:S(2)}) %collective-permute-start.10) | collective-permute-done | bytes 262176 | tf_op jit(solution)/shard_map/ppermute | solution.py:25
  32.2 2.5 %shard_map.69.refs_2_ = f32[64,384]{1,0:T(8,128)S(1)} custom-call(bf16[384,2048]{1,0:T(8,128)(2,1)S(1)} %copy-done, s32[1,384]{1,0:T(1,128)S(1)} %get-tuple-element.60.stored_ref.refs_2_, bf16[64,2048]{1,0:T(8,128)(2,1)} %shard_map.64.refs_0_, bf16[64,2048]{1,0:T(8,128)(2,1)S(1)} %collective-permute-done.9.refs_1_, ...), custom_call_target="tpu_custom_call" | custom-call | flops 99999997952 | tf_op jit(solution)/shard_map/pallas_call | solution.py:354
  34.8 1.0 %shard_map.70.refs_1_ = f32[384,512]{1,0:T(8,128)S(1)} custom-call(bf16[8192,512]{1,0:T(8,128)(2,1)S(1)} %copy-done.3, bf16[384,2048]{1,0:T(8,128)(2,1)S(1)} %collective-permute-done.5.refs_0_, f32[384,512]{1,0:T(8,128)S(1)} %shard_map.68.refs_1_), custom_call_target="tpu_custom_call" | custom-call | flops 99999997952 | tf_op jit(solution)/shard_map/pallas_call | solution.py:299
  36.3 2.5 %shard_map.71 = (f32[384,512]{1,0:T(8,128)S(1)}, f32[64,384]{1,0:T(8,128)S(1)}, bf16[64,384]{1,0:T(8,128)(2,1)}) custom-call(bf16[8192,512]{1,0:T(8,128)(2,1)S(1)} %copy-done.3, bf16[384,1536]{1,0:T(8,128)(2,1)} %collective-permute-done.7.refs_0_, f32[384,512]{1,0:T(8,128)S(1)} %shard_map.70.refs_1_, f32[64,384]{1,0:T(8,128)S(1)} %shard_map.69.refs_2_, ...), custom_call_target="tpu_custom_call" | custom-call | flops 99999997952 | tf_op jit(solution)/shard_map/pallas_call | solution.py:374
  38.8 1.0 %collective-permute-start.12 = (bf16[64,512]{1,0:T(8,128)(2,1)}, bf16[64,512]{1,0:T(8,128)(2,1)S(1)}, u32[]{:S(2)}, u32[]{:S(2)}) collective-permute-start(bf16[64,512]{1,0:T(8,128)(2,1)} %collective-permute-done.8.refs_7_), channel_id=1, source_target_pairs={{0,16},{16,0},{1,17},{17,1},{2,18},{18,2},{3,19},{19,3},{4,20},{20... | collective-permute-start | bytes 196616 | tf_op jit(solution)/shard_map/ppermute | solution.py:25
  39.8 1.5 %collective-permute-start.15 = (bf16[64,384]{1,0:T(8,128)(2,1)}, bf16[64,384]{1,0:T(8,128)(2,1)}, u32[]{:S(2)}, u32[]{:S(2)}) collective-permute-start(bf16[64,384]{1,0:T(8,128)(2,1)} %get-tuple-element.77), channel_id=1, source_target_pairs={{0,2},{1,3},{2,0},{3,1},{4,6},{5,7},{6,4},{7,5},{8,10},{9,11},{10,... | collective-permute-start | bytes 147464 | tf_op jit(solution)/shard_map/ppermute | solution.py:25
  41.3 1.4 %shard_map.72.refs_1_ = f32[384,512]{1,0:T(8,128)S(1)} custom-call(bf16[8192,512]{1,0:T(8,128)(2,1)S(1)} %copy-done.3, bf16[384,1536]{1,0:T(8,128)(2,1)S(1)} %collective-permute-done.13.refs_0_, f32[384,512]{1,0:T(8,128)S(1)} %get-tuple-element.75.refs_1_), custom_call_target="tpu_custom_call" | custom-call | flops 99999997952 | tf_op jit(solution)/shard_map/pallas_call | solution.py:299
  42.7 1.2 %collective-permute-done.3.refs_0_ = bf16[384,512]{1,0:T(8,128)(2,1)} collective-permute-done((bf16[384,512]{1,0:T(8,128)(2,1)}, bf16[384,512]{1,0:T(8,128)(2,1)}, u32[]{:S(2)}, u32[]{:S(2)}) %collective-permute-start.3) | collective-permute-done | bytes 393248 | tf_op jit(solution)/shard_map/ppermute | solution.py:25
  43.9 1.4 %shard_map.73.refs_1_ = f32[384,512]{1,0:T(8,128)S(1)} custom-call(bf16[8192,512]{1,0:T(8,128)(2,1)S(1)} %copy-done.3, bf16[384,512]{1,0:T(8,128)(2,1)} %collective-permute-done.3.refs_0_, f32[384,512]{1,0:T(8,128)S(1)} %shard_map.72.refs_1_), custom_call_target="tpu_custom_call" | custom-call | flops 99999997952 | tf_op jit(solution)/shard_map/pallas_call | solution.py:299
  45.8 2.2 %shard_map.74 = bf16[384,512]{1,0:T(8,128)(2,1)} custom-call(bf16[8192,512]{1,0:T(8,128)(2,1)S(1)} %copy-done.3, bf16[384,512]{1,0:T(8,128)(2,1)S(1)} %collective-permute-done.14.refs_0_, f32[384,512]{1,0:T(8,128)S(1)} %shard_map.73.refs_1_, s32[1,384]{1,0:T(1,128)S(1)} %copy-done.7, f32[64,384]{1,0:T(8,128)S(1)} %get-tuple-element.81.refs_3_, ...), custom_call_target="tpu_custom_call" | custom-call | flops 99999997952 | tf_op jit(solution)/shard_map/pallas_call | solution.py:399
  (36 shorter events, 3.8 us)
Async XLA Ops:
  0.0 8.3 %copy-start.1 = (bf16[1,8192,16]{1,2,0:T(8,128)(2,1)S(1)}, bf16[1,8192,16]{1,2,0:T(8,128)(2,1)}, u32[]{:S(2)}) copy-start(bf16[1,8192,16]{1,2,0:T(8,128)(2,1)} %param.10) | copy-start | bytes 786436
  0.0 11.9 %copy-start = (bf16[384,2048]{1,0:T(8,128)(2,1)S(1)}, bf16[384,2048]{1,0:T(8,128)(2,1)}, u32[]{:S(2)}) copy-start(bf16[384,2048]{1,0:T(8,128)(2,1)} %tokens_ref.1) | copy-start | bytes 4718596
  0.0 11.9 %copy-start.4 = (s32[384,1]{0,1:T(1,128)S(1)}, s32[384,1]{0,1:T(1,128)}, u32[]{:S(2)}) copy-start(s32[384,1]{0,1:T(1,128)} %param.7) | copy-start | bytes 4612
  0.0 11.9 %copy-start.5 = (s32[4]{0:T(128)S(1)}, s32[4]{0:T(128)}, u32[]{:S(2)}) copy-start(s32[4]{0:T(128)} %placement_ref.1) | copy-start | bytes 52
  0.0 8.3 %collective-permute-start = (bf16[16,8192]{1,0:T(8,128)(2,1)}, bf16[16,8192]{1,0:T(8,128)(2,1)S(1)}, u32[]{:S(2)}, u32[]{:S(2)}) collective-permute-start(bf16[16,8192]{1,0:T(8,128)(2,1)} %bitcast.13), channel_id=1, source_target_pairs={{0,1},{1,0},{2,3},{3,2},{4,5},{5,4},{6,7},{7,6},{8,9},{9,8},{10,11... | collective-permute-start | bytes 786440 | tf_op jit(solution)/shard_map/ppermute | solution.py:25
  1.5 6.7 %collective-permute-start.1 = (bf16[16,2048]{1,0:T(8,128)(2,1)S(1)}, bf16[16,2048]{1,0:T(8,128)(2,1)S(1)}, u32[]{:S(2)}, u32[]{:S(2)}) collective-permute-start(bf16[16,2048]{1,0:T(8,128)(2,1)S(1)} %get-tuple-element.46), channel_id=1, source_target_pairs={{0,2},{1,3},{2,0},{3,1},{4,6},{5,7},{6,4},{7,5},{8,10},{9,11},{10,... | collective-permute-start | bytes 196616 | tf_op jit(solution)/shard_map/ppermute | solution.py:25
  4.1 4.1 %collective-permute-start.2 = (bf16[16,2048]{1,0:T(8,128)(2,1)S(1)}, bf16[16,2048]{1,0:T(8,128)(2,1)S(1)}, u32[]{:S(2)}, u32[]{:S(2)}) collective-permute-start(bf16[16,2048]{1,0:T(8,128)(2,1)S(1)} %get-tuple-element.47), channel_id=1, source_target_pairs={{0,3},{1,2},{2,1},{3,0},{4,7},{5,6},{6,5},{7,4},{8,11},{9,10},{10,... | collective-permute-start | bytes 196616 | tf_op jit(solution)/shard_map/ppermute | solution.py:25
  6.4 29.4 %collective-permute-start.7 = (bf16[384,1536]{1,0:T(8,128)(2,1)}, bf16[384,1536]{1,0:T(8,128)(2,1)}, u32[]{:S(2)}, u32[]{:S(2)}) collective-permute-start(bf16[384,1536]{1,0:T(8,128)(2,1)} %get-tuple-element.59), channel_id=1, source_target_pairs={{0,2},{1,3},{2,0},{3,1},{4,6},{5,7},{6,4},{7,5},{8,10},{9,11},{10,... | collective-permute-start | bytes 3538952 | tf_op jit(solution)/shard_map/ppermute | solution.py:25
  9.3 15.3 %collective-permute-start.4 = (bf16[64,2048]{1,0:T(8,128)(2,1)}, bf16[64,2048]{1,0:T(8,128)(2,1)}, u32[]{:S(2)}, u32[]{:S(2)}) collective-permute-start(bf16[64,2048]{1,0:T(8,128)(2,1)} %shard_map.64.refs_0_), channel_id=1, source_target_pairs={{0,8},{4,12},{8,0},{12,4},{16,28},{20,24},{24,20},{28,16},{1,9},{5... | collective-permute-start | bytes 786440 | tf_op jit(solution)/shard_map/ppermute | solution.py:317
  11.9 3.4 %copy-start.2 = (bf16[8192,512]{1,0:T(8,128)(2,1)S(1)}, bf16[8192,512]{1,0:T(8,128)(2,1)}, u32[]{:S(2)}) copy-start(bf16[8192,512]{1,0:T(8,128)(2,1)} %weight_ref.15) | copy-start | bytes 25165828
  15.3 3.4 %copy-start.3 = (bf16[8192,512]{1,0:T(8,128)(2,1)S(1)}, bf16[8192,512]{1,0:T(8,128)(2,1)}, u32[]{:S(2)}) copy-start(bf16[8192,512]{1,0:T(8,128)(2,1)} %weight_ref.15) | copy-start | bytes 25165828
  16.8 15.4 %copy-start.6 = (s32[1,384]{1,0:T(1,128)}, s32[1,384]{1,0:T(1,128)S(1)}, u32[]{:S(2)}) copy-start(s32[1,384]{1,0:T(1,128)S(1)} %get-tuple-element.60.stored_ref.refs_2_) | copy-start | bytes 4612
  16.8 7.8 %collective-permute-start.5 = (bf16[384,2048]{1,0:T(8,128)(2,1)S(1)}, bf16[384,2048]{1,0:T(8,128)(2,1)S(1)}, u32[]{:S(2)}, u32[]{:S(2)}) collective-permute-start(bf16[384,2048]{1,0:T(8,128)(2,1)S(1)} %copy-done), channel_id=1, source_target_pairs={{0,1},{1,0},{2,3},{3,2},{4,5},{5,4},{6,7},{7,6},{8,9},{9,8},{10,11... | collective-permute-start | bytes 4718600 | tf_op jit(solution)/shard_map/ppermute | solution.py:25
  19.7 11.1 %collective-permute-start.9 = (bf16[64,2048]{1,0:T(8,128)(2,1)}, bf16[64,2048]{1,0:T(8,128)(2,1)S(1)}, u32[]{:S(2)}, u32[]{:S(2)}) collective-permute-start(bf16[64,2048]{1,0:T(8,128)(2,1)} %shard_map.64.refs_0_), channel_id=1, source_target_pairs={{0,4},{4,0},{8,12},{12,8},{1,5},{5,1},{9,13},{13,9},{2,6},{6,2},{1... | collective-permute-start | bytes 786440 | tf_op jit(solution)/shard_map/ppermute | solution.py:25
  21.3 22.6 %collective-permute-start.3 = (bf16[384,512]{1,0:T(8,128)(2,1)}, bf16[384,512]{1,0:T(8,128)(2,1)}, u32[]{:S(2)}, u32[]{:S(2)}) collective-permute-start(bf16[384,512]{1,0:T(8,128)(2,1)} %get-tuple-element.53), channel_id=1, source_target_pairs={{0,2},{1,3},{2,0},{3,1},{4,6},{5,7},{6,4},{7,5},{8,10},{9,11},{10,... | collective-permute-start | bytes 1179656 | tf_op jit(solution)/shard_map/ppermute | solution.py:25
  24.6 7.6 %collective-permute-start.10 = (bf16[64,2048]{1,0:T(8,128)(2,1)}, bf16[64,2048]{1,0:T(8,128)(2,1)S(1)}, u32[]{:S(2)}, u32[]{:S(2)}) collective-permute-start(bf16[64,2048]{1,0:T(8,128)(2,1)} %collective-permute-done.4.refs_2_), channel_id=1, source_target_pairs={{0,16},{16,0},{1,17},{17,1},{2,18},{18,2},{3,19},{19,3},{4,20},{20... | collective-permute-start | bytes 786440 | tf_op jit(solution)/shard_map/ppermute | solution.py:25
  25.6 10.2 %collective-permute-start.8 = (bf16[64,512]{1,0:T(8,128)(2,1)}, bf16[64,512]{1,0:T(8,128)(2,1)}, u32[]{:S(2)}, u32[]{:S(2)}) collective-permute-start(bf16[64,512]{1,0:T(8,128)(2,1)} %bitcast.8.refs_5_), channel_id=1, source_target_pairs={{0,8},{4,12},{8,0},{12,4},{16,28},{20,24},{24,20},{28,16},{1,9},{5... | collective-permute-start | bytes 196616 | tf_op jit(solution)/shard_map/ppermute | solution.py:317
  30.7 13.2 %collective-permute-start.6 = (bf16[64,512]{1,0:T(8,128)(2,1)}, bf16[64,512]{1,0:T(8,128)(2,1)}, u32[]{:S(2)}, u32[]{:S(2)}) collective-permute-start(bf16[64,512]{1,0:T(8,128)(2,1)} %bitcast.8.refs_5_), channel_id=1, source_target_pairs={{0,4},{4,0},{8,12},{12,8},{1,5},{5,1},{9,13},{13,9},{2,6},{6,2},{1... | collective-permute-start | bytes 196616 | tf_op jit(solution)/shard_map/ppermute | solution.py:25
  34.7 1.4 %collective-permute-start.11 = (f32[64,384]{1,0:T(8,128)S(1)}, f32[64,384]{1,0:T(8,128)S(1)}, u32[]{:S(2)}, u32[]{:S(2)}) collective-permute-start(f32[64,384]{1,0:T(8,128)S(1)} %shard_map.69.refs_2_), channel_id=1, source_target_pairs={{0,1},{1,0},{2,3},{3,2},{4,5},{5,4},{6,7},{7,6},{8,9},{9,8},{10,11... | collective-permute-start | bytes 294920 | tf_op jit(solution)/shard_map/ppermute | solution.py:25
  36.1 5.2 %collective-permute-start.13 = (bf16[384,1536]{1,0:T(8,128)(2,1)}, bf16[384,1536]{1,0:T(8,128)(2,1)S(1)}, u32[]{:S(2)}, u32[]{:S(2)}) collective-permute-start(bf16[384,1536]{1,0:T(8,128)(2,1)} %collective-permute-done.7.refs_0_), channel_id=1, source_target_pairs={{0,1},{1,0},{2,3},{3,2},{4,5},{5,4},{6,7},{7,6},{8,9},{9,8},{10,11... | collective-permute-start | bytes 3538952 | tf_op jit(solution)/shard_map/ppermute | solution.py:25
  38.8 5.1 %collective-permute-start.12 = (bf16[64,512]{1,0:T(8,128)(2,1)}, bf16[64,512]{1,0:T(8,128)(2,1)S(1)}, u32[]{:S(2)}, u32[]{:S(2)}) collective-permute-start(bf16[64,512]{1,0:T(8,128)(2,1)} %collective-permute-done.8.refs_7_), channel_id=1, source_target_pairs={{0,16},{16,0},{1,17},{17,1},{2,18},{18,2},{3,19},{19,3},{4,20},{20... | collective-permute-start | bytes 196616 | tf_op jit(solution)/shard_map/ppermute | solution.py:25
  39.8 5.5 %collective-permute-start.15 = (bf16[64,384]{1,0:T(8,128)(2,1)}, bf16[64,384]{1,0:T(8,128)(2,1)}, u32[]{:S(2)}, u32[]{:S(2)}) collective-permute-start(bf16[64,384]{1,0:T(8,128)(2,1)} %get-tuple-element.77), channel_id=1, source_target_pairs={{0,2},{1,3},{2,0},{3,1},{4,6},{5,7},{6,4},{7,5},{8,10},{9,11},{10,... | collective-permute-start | bytes 147464 | tf_op jit(solution)/shard_map/ppermute | solution.py:25
  42.7 3.1 %copy-start.7 = (s32[1,384]{1,0:T(1,128)S(1)}, s32[1,384]{1,0:T(1,128)}, u32[]{:S(2)}) copy-start(s32[1,384]{1,0:T(1,128)} %copy-done.6) | copy-start | bytes 4612
  43.9 1.9 %collective-permute-start.14 = (bf16[384,512]{1,0:T(8,128)(2,1)}, bf16[384,512]{1,0:T(8,128)(2,1)S(1)}, u32[]{:S(2)}, u32[]{:S(2)}) collective-permute-start(bf16[384,512]{1,0:T(8,128)(2,1)} %collective-permute-done.3.refs_0_), channel_id=1, source_target_pairs={{0,1},{1,0},{2,3},{3,2},{4,5},{5,4},{6,7},{7,6},{8,9},{9,8},{10,11... | collective-permute-start | bytes 1179656 | tf_op jit(solution)/shard_map/ppermute | solution.py:25

commit v24 on v18

--- a/solution.py
+++ b/solution.py
@@ -100,8 +100,16 @@
             t += 1
 
 
-def add_tiles(held_ref, rows_ref, sems, total_ref):
-    @pl.loop(0, held_ref.shape[0])
+def add_tiles(held_ref, rows_ref, sems, total_ref, given_ref):
+    pltpu.make_async_copy(held_ref.at[0], held_ref.at[0], sems.at[0, 0]).wait()
+    pltpu.make_async_copy(rows_ref.at[0], rows_ref.at[0], sems.at[1, 0]).wait()
+    total_ref[...] = given_ref[...] + jnp.dot(
+        held_ref[0], rows_ref[0], preferred_element_type=jnp.float32
+    )
+    if held_ref.shape[0] == 1:
+        return
+
+    @pl.loop(1, held_ref.shape[0])
     def _(t):
         pltpu.make_async_copy(held_ref.at[t], held_ref.at[t], sems.at[0, t]).wait()
         pltpu.make_async_copy(rows_ref.at[t], rows_ref.at[t], sems.at[1, t]).wait()
@@ -127,7 +135,7 @@
     for slot in range(slots):
         stored = jnp.where(tenant_ref[...] == slot, placement_ref[slot], stored)
     stored_ref[...] = stored
-    add_tiles(held_ref, rows_ref, sems, out_ref)
+    add_tiles(held_ref, rows_ref, sems, out_ref, out_ref)
 
 
 def products_kernel(tile, depth, places, weight_ref, *refs):
@@ -135,8 +143,7 @@
     features, given = refs[:count], refs[count]
     out_ref, held_ref, rows_ref, sems = refs[count + 1 :]
     start_tiles(tile, depth, places, features, weight_ref, held_ref, rows_ref, sems)
-    out_ref[...] = given[...]
-    add_tiles(held_ref, rows_ref, sems, out_ref)
+    add_tiles(held_ref, rows_ref, sems, out_ref, given)
 
 
 def owners_of(flips, pairs):
@@ -165,16 +172,18 @@
     for copy in copies:
         copy.start()
     start_tiles(tile, depth, places, features, weight_ref, held_ref, rows_ref, sems)
-    total_ref[...] = given[...]
-    add_tiles(held_ref, rows_ref, sems, total_ref)
+    add_tiles(held_ref, rows_ref, sems, total_ref, given)
     for copy in copies:
         copy.wait()
     shrunk = (sums_ref[...] + received_ref[...].astype(jnp.float32)).astype(jnp.bfloat16).astype(jnp.float32)
     spread = jnp.concatenate(
         [jnp.where(stored_ref[...] == owner, shrunk, 0.0) for owner in owners_of(flips, pairs)], axis=0
     )
-    expanded = jnp.dot(
-        spread.T.astype(jnp.bfloat16), stacked_ref[...], preferred_element_type=jnp.float32
+    expanded = lax.dot_general(
+        spread.astype(jnp.bfloat16),
+        stacked_ref[...],
+        (((0,), (0,)), ((), ())),
+        preferred_element_type=jnp.float32,
     )
     expanded = expanded.astype(jnp.bfloat16).astype(jnp.float32)
     out_ref[...] = (total_ref[...] + LOWRANK_SCALE * expanded).astype(out_ref.dtype)

time: 48.3 us -> 48.2 us (level)
  transfers between devices with their start and end apart: 16 -> 16, of which waited for: 5 -> 5; matrix products, arithmetic and copies ran while one was open for 1% -> 1% of each run, Pallas kernels for 31% -> 30%
where the time goes in v24:
time: 48.2 us; the launch traced here: 47.8 us
  starting transfers between devices  17.5 us (36%)
  Pallas kernels  16.6 us (34%)
  waiting for transfers between devices  8.16 us (17%)
  local copies, waits for them, and re-layouts  4.79 us (10%)
  other arithmetic  0.63 us (1%)
    ppermute x14, starting transfers between devices, flipped(): return lax.ppermute(value, axis, [(i, i ^ flip) for i in range(count)])  12.8 us
    pallas_call x5, Pallas kernels, products(): call(functools.partial(products_kernel, tile, depth, places), jax.ShapeDt...  7.65 us
    ppermute x14, waiting for transfers between devices, flipped(): return lax.ppermute(value, axis, [(i, i ^ flip) for i in range(count)])  5.63 us
    ppermute x2, starting transfers between devices, fetch_far(): lax.ppermute(value, ('parts', 'adapter'), route)  4.68 us
    unnamed x14, local copies, waits for them, and re-layouts  3.72 us
    ppermute x2, waiting for transfers between devices, fetch_far(): lax.ppermute(value, ('parts', 'adapter'), route)  2.53 us
    pallas_call x1, Pallas kernels, body(): call(functools.partial(shrink_kernel, tile, flips, pairs, slots), jax.Sha...  2.48 us
    pallas_call x1, Pallas kernels, body(): call(functools.partial(cut_kernel, edges), [jax.ShapeDtypeStruct((rows, b...  2.23 us
  transfers between devices with their start and end apart: 16, of which 5 were waited for; matrix products, arithmetic and copies ran while one was open for 1% of the time, Pallas kernels for 30%

profile of v24, /device:TPU:0, one launch (start us, length us, event | category | flops | bytes accessed | tf_op | source)
XLA Modules:
  0.0 47.8 jit_solution(3957229135996350374)
XLA Ops:
  0.0 1.1 %dynamic-slice_bitcast_fusion = (bf16[16,2048]{1,0:T(8,128)(2,1)S(1)}, bf16[16,2048]{1,0:T(8,128)(2,1)S(1)}, bf16[16,2048]{1,0:T(8,128)(2,1)S(1)}, bf16[16,2048]{1,0:T(8,128)(2,1)S(1)}) fusion(bf16[1,8192,16]{1,2,0:T(8,128)(2,1)} %param.10, s32[]{:T(128)S(6)} %select_n.15, s32[]{:T(128)S(6)} %select_n.13, s32[]{:T(128)S(6)} %select_n.12, s32[]{:T(128)S(6)} %select_n.14), kind=kLoop, calls=%fused_computation | loop fusion | bytes 524304 | tf_op jit(solution)/shard_map/dynamic_slice | solution.py:239
  1.6 2.6 %collective-permute-start.1 = (bf16[16,2048]{1,0:T(8,128)(2,1)S(1)}, bf16[16,2048]{1,0:T(8,128)(2,1)S(1)}, u32[]{:S(2)}, u32[]{:S(2)}) collective-permute-start(bf16[16,2048]{1,0:T(8,128)(2,1)S(1)} %get-tuple-element.52), channel_id=1, source_target_pairs={{0,2},{1,3},{2,0},{3,1},{4,6},{5,7},{6,4},{7,5},{8,10},{9,11},{10,... | collective-permute-start | bytes 196616 | tf_op jit(solution)/shard_map/ppermute | solution.py:25
  4.3 2.2 %shard_map.66 = (bf16[384,1536]{1,0:T(8,128)(2,1)}, bf16[384,512]{1,0:T(8,128)(2,1)}) custom-call(bf16[384,2048]{1,0:T(8,128)(2,1)} %tokens_ref.1), custom_call_target="tpu_custom_call" | custom-call | tf_op jit(solution)/shard_map/pallas_call | solution.py:245
  6.5 1.8 %collective-permute-start.7 = (bf16[384,1536]{1,0:T(8,128)(2,1)}, bf16[384,1536]{1,0:T(8,128)(2,1)}, u32[]{:S(2)}, u32[]{:S(2)}) collective-permute-start(bf16[384,1536]{1,0:T(8,128)(2,1)} %get-tuple-element.69), channel_id=1, source_target_pairs={{0,2},{1,3},{2,0},{3,1},{4,6},{5,7},{6,4},{7,5},{8,10},{9,11},{10,... | collective-permute-start | bytes 3538952 | tf_op jit(solution)/shard_map/ppermute | solution.py:25
  9.1 2.7 %collective-permute-start.5 = (bf16[64,2048]{1,0:T(8,128)(2,1)}, bf16[64,2048]{1,0:T(8,128)(2,1)}, u32[]{:S(2)}, u32[]{:S(2)}) collective-permute-start(bf16[64,2048]{1,0:T(8,128)(2,1)} %shard_map.64.refs_0_), channel_id=1, source_target_pairs={{0,8},{4,12},{8,0},{12,4},{16,28},{20,24},{24,20},{28,16},{1,9},{5... | collective-permute-start | bytes 786440 | tf_op jit(solution)/shard_map/ppermute | solution.py:312
  11.8 3.4 %copy-done.1 = bf16[8192,512]{1,0:T(8,128)(2,1)S(1)} copy-done((bf16[8192,512]{1,0:T(8,128)(2,1)S(1)}, bf16[8192,512]{1,0:T(8,128)(2,1)}, u32[]{:S(2)}) %copy-start.1) | copy-done | bytes 8388632
  15.2 1.4 %shard_map.65 = (f32[384,512]{1,0:T(8,128)S(1)}, s32[1,384]{1,0:T(1,128)S(1)}) custom-call(s32[4]{0:T(128)S(1)} %copy-done.4, s32[1,384]{1,0:T(1,128)S(1)} %bitcast.18, bf16[8192,512]{1,0:T(8,128)(2,1)S(1)} %copy-done.1, bf16[384,2048]{1,0:T(8,128)(2,1)S(1)} %copy-done), custom_call_target="tpu_custom_call" | custom-call | flops 99999997952 | tf_op jit(solution)/shard_map/pallas_call | solution.py:323
  16.6 1.6 %collective-permute-start.6 = (bf16[64,512]{1,0:T(8,128)(2,1)}, bf16[64,512]{1,0:T(8,128)(2,1)S(1)}, u32[]{:S(2)}, u32[]{:S(2)}) collective-permute-start(bf16[64,512]{1,0:T(8,128)(2,1)} %bitcast.9.refs_5_), channel_id=1, source_target_pairs={{0,4},{4,0},{8,12},{12,8},{1,5},{5,1},{9,13},{13,9},{2,6},{6,2},{1... | collective-permute-start | bytes 196616 | tf_op jit(solution)/shard_map/ppermute | solution.py:25
  18.5 0.8 %shard_map.67.refs_1_ = f32[384,512]{1,0:T(8,128)S(1)} custom-call(bf16[8192,512]{1,0:T(8,128)(2,1)S(1)} %copy-done.2, bf16[384,2048]{1,0:T(8,128)(2,1)S(1)} %copy-done, f32[384,512]{1,0:T(8,128)S(1)} %get-tuple-element.62.refs_1_), custom_call_target="tpu_custom_call" | custom-call | flops 99999997952 | tf_op jit(solution)/shard_map/pallas_call | solution.py:294
  19.4 1.6 %collective-permute-start.9 = (bf16[64,2048]{1,0:T(8,128)(2,1)}, bf16[64,2048]{1,0:T(8,128)(2,1)S(1)}, u32[]{:S(2)}, u32[]{:S(2)}) collective-permute-start(bf16[64,2048]{1,0:T(8,128)(2,1)} %shard_map.64.refs_0_), channel_id=1, source_target_pairs={{0,4},{4,0},{8,12},{12,8},{1,5},{5,1},{9,13},{13,9},{2,6},{6,2},{1... | collective-permute-start | bytes 786440 | tf_op jit(solution)/shard_map/ppermute | solution.py:25
  21.0 1.2 %collective-permute-start.4 = (bf16[384,512]{1,0:T(8,128)(2,1)}, bf16[384,512]{1,0:T(8,128)(2,1)}, u32[]{:S(2)}, u32[]{:S(2)}) collective-permute-start(bf16[384,512]{1,0:T(8,128)(2,1)} %get-tuple-element.60), channel_id=1, source_target_pairs={{0,2},{1,3},{2,0},{3,1},{4,6},{5,7},{6,4},{7,5},{8,10},{9,11},{10,... | collective-permute-start | bytes 1179656 | tf_op jit(solution)/shard_map/ppermute | solution.py:25
  22.2 2.5 %collective-permute-done.5.refs_2_ = bf16[64,2048]{1,0:T(8,128)(2,1)} collective-permute-done((bf16[64,2048]{1,0:T(8,128)(2,1)}, bf16[64,2048]{1,0:T(8,128)(2,1)}, u32[]{:S(2)}, u32[]{:S(2)}) %collective-permute-start.5) | collective-permute-done | bytes 262176 | tf_op jit(solution)/shard_map/ppermute | solution.py:312
  24.8 1.1 %collective-permute-done.6.refs_6_ = bf16[64,512]{1,0:T(8,128)(2,1)S(1)} collective-permute-done((bf16[64,512]{1,0:T(8,128)(2,1)}, bf16[64,512]{1,0:T(8,128)(2,1)S(1)}, u32[]{:S(2)}, u32[]{:S(2)}) %collective-permute-start.6) | collective-permute-done | bytes 65568 | tf_op jit(solution)/shard_map/ppermute | solution.py:25
  25.9 1.8 %shard_map.68.refs_1_ = f32[384,512]{1,0:T(8,128)S(1)} custom-call(bf16[8192,512]{1,0:T(8,128)(2,1)S(1)} %copy-done.2, bf16[384,2048]{1,0:T(8,128)(2,1)S(1)} %collective-permute-done.3.refs_0_, f32[384,512]{1,0:T(8,128)S(1)} %shard_map.67.refs_1_), custom_call_target="tpu_custom_call" | custom-call | flops 99999997952 | tf_op jit(solution)/shard_map/pallas_call | solution.py:294
  27.8 2.0 %collective-permute-start.8 = (bf16[64,512]{1,0:T(8,128)(2,1)}, bf16[64,512]{1,0:T(8,128)(2,1)S(1)}, u32[]{:S(2)}, u32[]{:S(2)}) collective-permute-start(bf16[64,512]{1,0:T(8,128)(2,1)} %bitcast.9.refs_5_), channel_id=1, source_target_pairs={{0,8},{4,12},{8,0},{12,4},{16,28},{20,24},{24,20},{28,16},{1,9},{5... | collective-permute-start | bytes 196616 | tf_op jit(solution)/shard_map/ppermute | solution.py:312
  29.8 1.8 %collective-permute-done.9.refs_1_ = bf16[64,2048]{1,0:T(8,128)(2,1)S(1)} collective-permute-done((bf16[64,2048]{1,0:T(8,128)(2,1)}, bf16[64,2048]{1,0:T(8,128)(2,1)S(1)}, u32[]{:S(2)}, u32[]{:S(2)}) %collective-permute-start.9) | collective-permute-done | bytes 262176 | tf_op jit(solution)/shard_map/ppermute | solution.py:25
  31.6 2.2 %collective-permute-done.10.refs_3_ = bf16[64,2048]{1,0:T(8,128)(2,1)S(1)} collective-permute-done((bf16[64,2048]{1,0:T(8,128)(2,1)}, bf16[64,2048]{1,0:T(8,128)(2,1)S(1)}, u32[]{:S(2)}, u32[]{:S(2)}) %collective-permute-start.10) | collective-permute-done | bytes 262176 | tf_op jit(solution)/shard_map/ppermute | solution.py:25
  33.8 2.5 %shard_map.69 = f32[64,384]{1,0:T(8,128)S(1)} custom-call(bf16[384,2048]{1,0:T(8,128)(2,1)S(1)} %copy-done, s32[1,384]{1,0:T(1,128)S(1)} %get-tuple-element.70.stored_ref.refs_2_, bf16[64,2048]{1,0:T(8,128)(2,1)} %shard_map.64.refs_0_, bf16[64,2048]{1,0:T(8,128)(2,1)S(1)} %collective-permute-done.9.refs_1_, bf16[64,2048]{1,0:T(8,128)(2,1)} %collective-permute-done.5.refs_2_, ...), custom_call_target="tpu_custom_call" | custom-call | flops 99999997952 | tf_op jit(solution)/shard_map/pallas_call | solution.py:351
  36.9 2.2 %shard_map.70.refs_1_ = f32[384,512]{1,0:T(8,128)S(1)} custom-call(bf16[8192,512]{1,0:T(8,128)(2,1)S(1)} %copy-done.2, bf16[384,1536]{1,0:T(8,128)(2,1)} %collective-permute-done.7.refs_0_, f32[384,512]{1,0:T(8,128)S(1)} %shard_map.68.refs_1_), custom_call_target="tpu_custom_call" | custom-call | flops 99999997952 | tf_op jit(solution)/shard_map/pallas_call | solution.py:294
  39.1 1.1 %collective-permute-start.11 = (bf16[64,512]{1,0:T(8,128)(2,1)S(1)}, bf16[64,512]{1,0:T(8,128)(2,1)S(1)}, u32[]{:S(2)}, u32[]{:S(2)}) collective-permute-start(bf16[64,512]{1,0:T(8,128)(2,1)S(1)} %collective-permute-done.8.refs_7_), channel_id=1, source_target_pairs={{0,16},{16,0},{1,17},{17,1},{2,18},{18,2},{3,19},{19,3},{4,20},{20... | collective-permute-start | bytes 196616 | tf_op jit(solution)/shard_map/ppermute | solution.py:25
  40.8 1.5 %collective-permute-start.15 = (bf16[64,384]{1,0:T(8,128)(2,1)}, bf16[64,384]{1,0:T(8,128)(2,1)}, u32[]{:S(2)}, u32[]{:S(2)}) collective-permute-start(bf16[64,384]{1,0:T(8,128)(2,1)} %get-tuple-element.93), channel_id=1, source_target_pairs={{0,2},{1,3},{2,0},{3,1},{4,6},{5,7},{6,4},{7,5},{8,10},{9,11},{10,... | collective-permute-start | bytes 147464 | tf_op jit(solution)/shard_map/ppermute | solution.py:25
  42.3 1.4 %shard_map.71.refs_1_ = f32[384,512]{1,0:T(8,128)S(1)} custom-call(bf16[8192,512]{1,0:T(8,128)(2,1)S(1)} %copy-done.2, bf16[384,1536]{1,0:T(8,128)(2,1)S(1)} %collective-permute-done.12.refs_0_, f32[384,512]{1,0:T(8,128)S(1)} %shard_map.70.refs_1_), custom_call_target="tpu_custom_call" | custom-call | flops 99999997952 | tf_op jit(solution)/shard_map/pallas_call | solution.py:294
  43.8 1.4 %shard_map.72.refs_1_ = f32[384,512]{1,0:T(8,128)S(1)} custom-call(bf16[8192,512]{1,0:T(8,128)(2,1)S(1)} %copy-done.2, bf16[384,512]{1,0:T(8,128)(2,1)} %collective-permute-done.4.refs_0_, f32[384,512]{1,0:T(8,128)S(1)} %shard_map.71.refs_1_), custom_call_target="tpu_custom_call" | custom-call | flops 99999997952 | tf_op jit(solution)/shard_map/pallas_call | solution.py:294
  45.7 2.1 %shard_map.73 = bf16[384,512]{1,0:T(8,128)(2,1)} custom-call(bf16[8192,512]{1,0:T(8,128)(2,1)S(1)} %copy-done.2, bf16[384,512]{1,0:T(8,128)(2,1)S(1)} %collective-permute-done.14.refs_0_, f32[384,512]{1,0:T(8,128)S(1)} %shard_map.72.refs_1_, s32[1,384]{1,0:T(1,128)S(1)} %copy-done.6, f32[64,384]{1,0:T(8,128)S(1)} %get-tuple-element.87.refs_3_, ...), custom_call_target="tpu_custom_call" | custom-call | flops 99999997952 | tf_op jit(solution)/shard_map/pallas_call | solution.py:385
  (34 shorter events, 3.5 us)
Async XLA Ops:
  0.0 8.3 %copy-start = (bf16[384,2048]{1,0:T(8,128)(2,1)S(1)}, bf16[384,2048]{1,0:T(8,128)(2,1)}, u32[]{:S(2)}) copy-start(bf16[384,2048]{1,0:T(8,128)(2,1)} %tokens_ref.1) | copy-start | bytes 4718596
  0.0 11.8 %copy-start.3 = (s32[384,1]{0,1:T(1,128)S(1)}, s32[384,1]{0,1:T(1,128)}, u32[]{:S(2)}) copy-start(s32[384,1]{0,1:T(1,128)} %param.7) | copy-start | bytes 4612
  0.0 11.8 %copy-start.4 = (s32[4]{0:T(128)S(1)}, s32[4]{0:T(128)}, u32[]{:S(2)}) copy-start(s32[4]{0:T(128)} %placement_ref.1) | copy-start | bytes 52
  1.1 7.2 %collective-permute-start = (bf16[16,2048]{1,0:T(8,128)(2,1)S(1)}, bf16[16,2048]{1,0:T(8,128)(2,1)S(1)}, u32[]{:S(2)}, u32[]{:S(2)}) collective-permute-start(bf16[16,2048]{1,0:T(8,128)(2,1)S(1)} %get-tuple-element.50), channel_id=1, source_target_pairs={{0,1},{1,0},{2,3},{3,2},{4,5},{5,4},{6,7},{7,6},{8,9},{9,8},{10,11... | collective-permute-start | bytes 196616 | tf_op jit(solution)/shard_map/ppermute | solution.py:25
  1.6 6.7 %collective-permute-start.1 = (bf16[16,2048]{1,0:T(8,128)(2,1)S(1)}, bf16[16,2048]{1,0:T(8,128)(2,1)S(1)}, u32[]{:S(2)}, u32[]{:S(2)}) collective-permute-start(bf16[16,2048]{1,0:T(8,128)(2,1)S(1)} %get-tuple-element.52), channel_id=1, source_target_pairs={{0,2},{1,3},{2,0},{3,1},{4,6},{5,7},{6,4},{7,5},{8,10},{9,11},{10,... | collective-permute-start | bytes 196616 | tf_op jit(solution)/shard_map/ppermute | solution.py:25
  4.2 4.2 %collective-permute-start.2 = (bf16[16,2048]{1,0:T(8,128)(2,1)S(1)}, bf16[16,2048]{1,0:T(8,128)(2,1)S(1)}, u32[]{:S(2)}, u32[]{:S(2)}) collective-permute-start(bf16[16,2048]{1,0:T(8,128)(2,1)S(1)} %get-tuple-element.53), channel_id=1, source_target_pairs={{0,3},{1,2},{2,1},{3,0},{4,7},{5,6},{6,5},{7,4},{8,11},{9,10},{10,... | collective-permute-start | bytes 196616 | tf_op jit(solution)/shard_map/ppermute | solution.py:25
  6.5 29.8 %collective-permute-start.7 = (bf16[384,1536]{1,0:T(8,128)(2,1)}, bf16[384,1536]{1,0:T(8,128)(2,1)}, u32[]{:S(2)}, u32[]{:S(2)}) collective-permute-start(bf16[384,1536]{1,0:T(8,128)(2,1)} %get-tuple-element.69), channel_id=1, source_target_pairs={{0,2},{1,3},{2,0},{3,1},{4,6},{5,7},{6,4},{7,5},{8,10},{9,11},{10,... | collective-permute-start | bytes 3538952 | tf_op jit(solution)/shard_map/ppermute | solution.py:25
  8.3 8.3 %collective-permute-start.3 = (bf16[384,2048]{1,0:T(8,128)(2,1)S(1)}, bf16[384,2048]{1,0:T(8,128)(2,1)S(1)}, u32[]{:S(2)}, u32[]{:S(2)}) collective-permute-start(bf16[384,2048]{1,0:T(8,128)(2,1)S(1)} %copy-done), channel_id=1, source_target_pairs={{0,1},{1,0},{2,3},{3,2},{4,5},{5,4},{6,7},{7,6},{8,9},{9,8},{10,11... | collective-permute-start | bytes 4718600 | tf_op jit(solution)/shard_map/ppermute | solution.py:25
  9.1 15.7 %collective-permute-start.5 = (bf16[64,2048]{1,0:T(8,128)(2,1)}, bf16[64,2048]{1,0:T(8,128)(2,1)}, u32[]{:S(2)}, u32[]{:S(2)}) collective-permute-start(bf16[64,2048]{1,0:T(8,128)(2,1)} %shard_map.64.refs_0_), channel_id=1, source_target_pairs={{0,8},{4,12},{8,0},{12,4},{16,28},{20,24},{24,20},{28,16},{1,9},{5... | collective-permute-start | bytes 786440 | tf_op jit(solution)/shard_map/ppermute | solution.py:312
  11.8 3.4 %copy-start.1 = (bf16[8192,512]{1,0:T(8,128)(2,1)S(1)}, bf16[8192,512]{1,0:T(8,128)(2,1)}, u32[]{:S(2)}) copy-start(bf16[8192,512]{1,0:T(8,128)(2,1)} %weight_ref.13) | copy-start | bytes 25165828
  15.2 3.4 %copy-start.2 = (bf16[8192,512]{1,0:T(8,128)(2,1)S(1)}, bf16[8192,512]{1,0:T(8,128)(2,1)}, u32[]{:S(2)}) copy-start(bf16[8192,512]{1,0:T(8,128)(2,1)} %weight_ref.13) | copy-start | bytes 25165828
  16.6 17.2 %copy-start.5 = (s32[1,384]{1,0:T(1,128)}, s32[1,384]{1,0:T(1,128)S(1)}, u32[]{:S(2)}) copy-start(s32[1,384]{1,0:T(1,128)S(1)} %get-tuple-element.70.stored_ref.refs_2_) | copy-start | bytes 4612
  16.6 9.3 %collective-permute-start.6 = (bf16[64,512]{1,0:T(8,128)(2,1)}, bf16[64,512]{1,0:T(8,128)(2,1)S(1)}, u32[]{:S(2)}, u32[]{:S(2)}) collective-permute-start(bf16[64,512]{1,0:T(8,128)(2,1)} %bitcast.9.refs_5_), channel_id=1, source_target_pairs={{0,4},{4,0},{8,12},{12,8},{1,5},{5,1},{9,13},{13,9},{2,6},{6,2},{1... | collective-permute-start | bytes 196616 | tf_op jit(solution)/shard_map/ppermute | solution.py:25
  19.4 12.2 %collective-permute-start.9 = (bf16[64,2048]{1,0:T(8,128)(2,1)}, bf16[64,2048]{1,0:T(8,128)(2,1)S(1)}, u32[]{:S(2)}, u32[]{:S(2)}) collective-permute-start(bf16[64,2048]{1,0:T(8,128)(2,1)} %shard_map.64.refs_0_), channel_id=1, source_target_pairs={{0,4},{4,0},{8,12},{12,8},{1,5},{5,1},{9,13},{13,9},{2,6},{6,2},{1... | collective-permute-start | bytes 786440 | tf_op jit(solution)/shard_map/ppermute | solution.py:25
  21.0 22.7 %collective-permute-start.4 = (bf16[384,512]{1,0:T(8,128)(2,1)}, bf16[384,512]{1,0:T(8,128)(2,1)}, u32[]{:S(2)}, u32[]{:S(2)}) collective-permute-start(bf16[384,512]{1,0:T(8,128)(2,1)} %get-tuple-element.60), channel_id=1, source_target_pairs={{0,2},{1,3},{2,0},{3,1},{4,6},{5,7},{6,4},{7,5},{8,10},{9,11},{10,... | collective-permute-start | bytes 1179656 | tf_op jit(solution)/shard_map/ppermute | solution.py:25
  25.9 7.8 %collective-permute-start.10 = (bf16[64,2048]{1,0:T(8,128)(2,1)}, bf16[64,2048]{1,0:T(8,128)(2,1)S(1)}, u32[]{:S(2)}, u32[]{:S(2)}) collective-permute-start(bf16[64,2048]{1,0:T(8,128)(2,1)} %collective-permute-done.5.refs_2_), channel_id=1, source_target_pairs={{0,16},{16,0},{1,17},{17,1},{2,18},{18,2},{3,19},{19,3},{4,20},{20... | collective-permute-start | bytes 786440 | tf_op jit(solution)/shard_map/ppermute | solution.py:25
  27.8 8.5 %collective-permute-start.8 = (bf16[64,512]{1,0:T(8,128)(2,1)}, bf16[64,512]{1,0:T(8,128)(2,1)S(1)}, u32[]{:S(2)}, u32[]{:S(2)}) collective-permute-start(bf16[64,512]{1,0:T(8,128)(2,1)} %bitcast.9.refs_5_), channel_id=1, source_target_pairs={{0,8},{4,12},{8,0},{12,4},{16,28},{20,24},{24,20},{28,16},{1,9},{5... | collective-permute-start | bytes 196616 | tf_op jit(solution)/shard_map/ppermute | solution.py:312
  36.3 3.9 %collective-permute-start.13 = (f32[64,384]{1,0:T(8,128)S(1)}, f32[64,384]{1,0:T(8,128)S(1)}, u32[]{:S(2)}, u32[]{:S(2)}) collective-permute-start(f32[64,384]{1,0:T(8,128)S(1)} %shard_map.69), channel_id=1, source_target_pairs={{0,1},{1,0},{2,3},{3,2},{4,5},{5,4},{6,7},{7,6},{8,9},{9,8},{10,11... | collective-permute-start | bytes 294920 | tf_op jit(solution)/shard_map/ppermute | solution.py:25
  36.4 6.0 %collective-permute-start.12 = (bf16[384,1536]{1,0:T(8,128)(2,1)}, bf16[384,1536]{1,0:T(8,128)(2,1)S(1)}, u32[]{:S(2)}, u32[]{:S(2)}) collective-permute-start(bf16[384,1536]{1,0:T(8,128)(2,1)} %collective-permute-done.7.refs_0_), channel_id=1, source_target_pairs={{0,1},{1,0},{2,3},{3,2},{4,5},{5,4},{6,7},{7,6},{8,9},{9,8},{10,11... | collective-permute-start | bytes 3538952 | tf_op jit(solution)/shard_map/ppermute | solution.py:25
  39.1 4.6 %collective-permute-start.11 = (bf16[64,512]{1,0:T(8,128)(2,1)S(1)}, bf16[64,512]{1,0:T(8,128)(2,1)S(1)}, u32[]{:S(2)}, u32[]{:S(2)}) collective-permute-start(bf16[64,512]{1,0:T(8,128)(2,1)S(1)} %collective-permute-done.8.refs_7_), channel_id=1, source_target_pairs={{0,16},{16,0},{1,17},{17,1},{2,18},{18,2},{3,19},{19,3},{4,20},{20... | collective-permute-start | bytes 196616 | tf_op jit(solution)/shard_map/ppermute | solution.py:25
  40.8 4.4 %collective-permute-start.15 = (bf16[64,384]{1,0:T(8,128)(2,1)}, bf16[64,384]{1,0:T(8,128)(2,1)}, u32[]{:S(2)}, u32[]{:S(2)}) collective-permute-start(bf16[64,384]{1,0:T(8,128)(2,1)} %get-tuple-element.93), channel_id=1, source_target_pairs={{0,2},{1,3},{2,0},{3,1},{4,6},{5,7},{6,4},{7,5},{8,10},{9,11},{10,... | collective-permute-start | bytes 147464 | tf_op jit(solution)/shard_map/ppermute | solution.py:25
  43.7 2.0 %copy-start.6 = (s32[1,384]{1,0:T(1,128)S(1)}, s32[1,384]{1,0:T(1,128)}, u32[]{:S(2)}) copy-start(s32[1,384]{1,0:T(1,128)} %copy-done.5) | copy-start | bytes 4612
  43.7 2.0 %collective-permute-start.14 = (bf16[384,512]{1,0:T(8,128)(2,1)}, bf16[384,512]{1,0:T(8,128)(2,1)S(1)}, u32[]{:S(2)}, u32[]{:S(2)}) collective-permute-start(bf16[384,512]{1,0:T(8,128)(2,1)} %collective-permute-done.4.refs_0_), channel_id=1, source_target_pairs={{0,1},{1,0},{2,3},{3,2},{4,5},{5,4},{6,7},{7,6},{8,9},{9,8},{10,11... | collective-permute-start | bytes 1179656 | tf_op jit(solution)/shard_map/ppermute | solution.py:25

commit v25 on v24

--- a/solution.py
+++ b/solution.py
@@ -154,14 +154,12 @@
     return owners
 
 
-def last_kernel(tile, depth, places, flips, pairs, slots, weight_ref, *refs):
+def last_kernel(depth, places, flips, pairs, slots, weight_ref, *refs):
     count = len(places)
     features = refs[:count]
     given, stored_ref, sum_ref, more_ref = refs[count : count + 4]
     ups = refs[count + 4 : count + 4 + slots]
-    (
-        out_ref, total_ref, sums_ref, received_ref, stacked_ref, held_ref, rows_ref, sems, small_sems,
-    ) = refs[count + 4 + slots :]
+    out_ref, total_ref, sums_ref, received_ref, stacked_ref, small_sems = refs[count + 4 + slots :]
     rank = ups[0].shape[0]
     copies = [(sum_ref, sums_ref), (more_ref, received_ref)]
     copies += [(up, stacked_ref.at[pl.ds(b * rank, rank)]) for b, up in enumerate(ups)]
@@ -171,8 +169,15 @@
     ]
     for copy in copies:
         copy.start()
-    start_tiles(tile, depth, places, features, weight_ref, held_ref, rows_ref, sems)
-    add_tiles(held_ref, rows_ref, sems, total_ref, given)
+    me, sum_so_far = lax.axis_index("tensor"), given
+    for (flip, first, skip, width), part in zip(places, features):
+        start = pl.multiple_of((me ^ flip) * depth + first, LANES)
+        total_ref[...] = sum_so_far[...] + jnp.dot(
+            part[:, skip : skip + width],
+            weight_ref[pl.ds(start, width)],
+            preferred_element_type=jnp.float32,
+        )
+        sum_so_far = total_ref
     for copy in copies:
         copy.wait()
     shrunk = (sums_ref[...] + received_ref[...].astype(jnp.float32)).astype(jnp.bfloat16).astype(jnp.float32)
@@ -383,16 +388,15 @@
 
     places = near_places(1)
     return call(
-        functools.partial(last_kernel, tile, depth, places, flips, pairs, slots),
+        functools.partial(last_kernel, depth, places, flips, pairs, slots),
         jax.ShapeDtypeStruct((rows, columns), jnp.bfloat16),
-        [ANYWHERE] + [ANYWHERE] * len(near) + [VECTOR] * 2 + [ANYWHERE] * (2 + slots),
+        [VECTOR] * (len(near) + 3) + [ANYWHERE] * (2 + slots),
         [
             pltpu.VMEM((rows, columns), jnp.float32),
             pltpu.VMEM((rank, rows), jnp.float32),
             pltpu.VMEM((rank, rows), jnp.bfloat16),
             pltpu.VMEM((slots * rank, columns), jnp.bfloat16),
         ]
-        + tile_scratch(tile, rows, places, columns)
         + [pltpu.SemaphoreType.DMA((2 + slots,))],
     )(frozen_projection_weight, *near, total, stored, partial, more, *ups)
 

time: 48.2 us -> 48.2 us (level)
  no operation moved by 1% of the time
where the time goes in v25:
time: 48.2 us; the launch traced here: 47.8 us
  starting transfers between devices  17.5 us (36%)
  Pallas kernels  16.6 us (34%)
  waiting for transfers between devices  8.16 us (17%)
  local copies, waits for them, and re-layouts  4.79 us (10%)
  other arithmetic  0.63 us (1%)
    ppermute x14, starting transfers between devices, flipped(): return lax.ppermute(value, axis, [(i, i ^ flip) for i in range(count)])  12.8 us
    pallas_call x5, Pallas kernels, products(): call(functools.partial(products_kernel, tile, depth, places), jax.ShapeDt...  7.65 us
    ppermute x14, waiting for transfers between devices, flipped(): return lax.ppermute(value, axis, [(i, i ^ flip) for i in range(count)])  5.63 us
    ppermute x2, starting transfers between devices, fetch_far(): lax.ppermute(value, ('parts', 'adapter'), route)  4.68 us
    unnamed x14, local copies, waits for them, and re-layouts  3.72 us
    ppermute x2, waiting for transfers between devices, fetch_far(): lax.ppermute(value, ('parts', 'adapter'), route)  2.53 us
    pallas_call x1, Pallas kernels, body(): call(functools.partial(shrink_kernel, tile, flips, pairs, slots), jax.Sha...  2.48 us
    pallas_call x1, Pallas kernels, body(): call(functools.partial(cut_kernel, edges), [jax.ShapeDtypeStruct((rows, b...  2.23 us
  transfers between devices with their start and end apart: 16, of which 5 were waited for; matrix products, arithmetic and copies ran while one was open for 1% of the time, Pallas kernels for 30%

profile of v25, /device:TPU:0, one launch (start us, length us, event | category | flops | bytes accessed | tf_op | source)
XLA Modules:
  0.0 47.8 jit_solution(13206024601914546262)
XLA Ops:
  0.0 1.1 %dynamic-slice_bitcast_fusion = (bf16[16,2048]{1,0:T(8,128)(2,1)S(1)}, bf16[16,2048]{1,0:T(8,128)(2,1)S(1)}, bf16[16,2048]{1,0:T(8,128)(2,1)S(1)}, bf16[16,2048]{1,0:T(8,128)(2,1)S(1)}) fusion(bf16[1,8192,16]{1,2,0:T(8,128)(2,1)} %param.10, s32[]{:T(128)S(6)} %select_n.15, s32[]{:T(128)S(6)} %select_n.13, s32[]{:T(128)S(6)} %select_n.12, s32[]{:T(128)S(6)} %select_n.14), kind=kLoop, calls=%fused_computation | loop fusion | bytes 524304 | tf_op jit(solution)/shard_map/dynamic_slice | solution.py:244
  1.6 2.6 %collective-permute-start.1 = (bf16[16,2048]{1,0:T(8,128)(2,1)S(1)}, bf16[16,2048]{1,0:T(8,128)(2,1)S(1)}, u32[]{:S(2)}, u32[]{:S(2)}) collective-permute-start(bf16[16,2048]{1,0:T(8,128)(2,1)S(1)} %get-tuple-element.52), channel_id=1, source_target_pairs={{0,2},{1,3},{2,0},{3,1},{4,6},{5,7},{6,4},{7,5},{8,10},{9,11},{10,... | collective-permute-start | bytes 196616 | tf_op jit(solution)/shard_map/ppermute | solution.py:25
  4.3 2.2 %shard_map.66 = (bf16[384,1536]{1,0:T(8,128)(2,1)}, bf16[384,512]{1,0:T(8,128)(2,1)}) custom-call(bf16[384,2048]{1,0:T(8,128)(2,1)} %tokens_ref.1), custom_call_target="tpu_custom_call" | custom-call | tf_op jit(solution)/shard_map/pallas_call | solution.py:250
  6.5 1.8 %collective-permute-start.7 = (bf16[384,1536]{1,0:T(8,128)(2,1)}, bf16[384,1536]{1,0:T(8,128)(2,1)}, u32[]{:S(2)}, u32[]{:S(2)}) collective-permute-start(bf16[384,1536]{1,0:T(8,128)(2,1)} %get-tuple-element.69), channel_id=1, source_target_pairs={{0,2},{1,3},{2,0},{3,1},{4,6},{5,7},{6,4},{7,5},{8,10},{9,11},{10,... | collective-permute-start | bytes 3538952 | tf_op jit(solution)/shard_map/ppermute | solution.py:25
  9.1 2.7 %collective-permute-start.5 = (bf16[64,2048]{1,0:T(8,128)(2,1)}, bf16[64,2048]{1,0:T(8,128)(2,1)}, u32[]{:S(2)}, u32[]{:S(2)}) collective-permute-start(bf16[64,2048]{1,0:T(8,128)(2,1)} %shard_map.64.refs_0_), channel_id=1, source_target_pairs={{0,8},{4,12},{8,0},{12,4},{16,28},{20,24},{24,20},{28,16},{1,9},{5... | collective-permute-start | bytes 786440 | tf_op jit(solution)/shard_map/ppermute | solution.py:317
  11.8 3.4 %copy-done.1 = bf16[8192,512]{1,0:T(8,128)(2,1)S(1)} copy-done((bf16[8192,512]{1,0:T(8,128)(2,1)S(1)}, bf16[8192,512]{1,0:T(8,128)(2,1)}, u32[]{:S(2)}) %copy-start.1) | copy-done | bytes 8388632
  15.2 1.4 %shard_map.65 = (f32[384,512]{1,0:T(8,128)S(1)}, s32[1,384]{1,0:T(1,128)S(1)}) custom-call(s32[4]{0:T(128)S(1)} %copy-done.4, s32[1,384]{1,0:T(1,128)S(1)} %bitcast.18, bf16[8192,512]{1,0:T(8,128)(2,1)S(1)} %copy-done.1, bf16[384,2048]{1,0:T(8,128)(2,1)S(1)} %copy-done), custom_call_target="tpu_custom_call" | custom-call | flops 99999997952 | tf_op jit(solution)/shard_map/pallas_call | solution.py:328
  16.6 1.6 %collective-permute-start.6 = (bf16[64,512]{1,0:T(8,128)(2,1)}, bf16[64,512]{1,0:T(8,128)(2,1)S(1)}, u32[]{:S(2)}, u32[]{:S(2)}) collective-permute-start(bf16[64,512]{1,0:T(8,128)(2,1)} %bitcast.9.refs_5_), channel_id=1, source_target_pairs={{0,4},{4,0},{8,12},{12,8},{1,5},{5,1},{9,13},{13,9},{2,6},{6,2},{1... | collective-permute-start | bytes 196616 | tf_op jit(solution)/shard_map/ppermute | solution.py:25
  18.5 0.8 %shard_map.67.refs_1_ = f32[384,512]{1,0:T(8,128)S(1)} custom-call(bf16[8192,512]{1,0:T(8,128)(2,1)S(1)} %copy-done.2, bf16[384,2048]{1,0:T(8,128)(2,1)S(1)} %copy-done, f32[384,512]{1,0:T(8,128)S(1)} %get-tuple-element.62.refs_1_), custom_call_target="tpu_custom_call" | custom-call | flops 99999997952 | tf_op jit(solution)/shard_map/pallas_call | solution.py:299
  19.4 1.6 %collective-permute-start.9 = (bf16[64,2048]{1,0:T(8,128)(2,1)}, bf16[64,2048]{1,0:T(8,128)(2,1)S(1)}, u32[]{:S(2)}, u32[]{:S(2)}) collective-permute-start(bf16[64,2048]{1,0:T(8,128)(2,1)} %shard_map.64.refs_0_), channel_id=1, source_target_pairs={{0,4},{4,0},{8,12},{12,8},{1,5},{5,1},{9,13},{13,9},{2,6},{6,2},{1... | collective-permute-start | bytes 786440 | tf_op jit(solution)/shard_map/ppermute | solution.py:25
  21.0 1.2 %collective-permute-start.4 = (bf16[384,512]{1,0:T(8,128)(2,1)}, bf16[384,512]{1,0:T(8,128)(2,1)}, u32[]{:S(2)}, u32[]{:S(2)}) collective-permute-start(bf16[384,512]{1,0:T(8,128)(2,1)} %get-tuple-element.60), channel_id=1, source_target_pairs={{0,2},{1,3},{2,0},{3,1},{4,6},{5,7},{6,4},{7,5},{8,10},{9,11},{10,... | collective-permute-start | bytes 1179656 | tf_op jit(solution)/shard_map/ppermute | solution.py:25
  22.2 2.5 %collective-permute-done.5.refs_2_ = bf16[64,2048]{1,0:T(8,128)(2,1)} collective-permute-done((bf16[64,2048]{1,0:T(8,128)(2,1)}, bf16[64,2048]{1,0:T(8,128)(2,1)}, u32[]{:S(2)}, u32[]{:S(2)}) %collective-permute-start.5) | collective-permute-done | bytes 262176 | tf_op jit(solution)/shard_map/ppermute | solution.py:317
  24.8 1.1 %collective-permute-done.6.refs_6_ = bf16[64,512]{1,0:T(8,128)(2,1)S(1)} collective-permute-done((bf16[64,512]{1,0:T(8,128)(2,1)}, bf16[64,512]{1,0:T(8,128)(2,1)S(1)}, u32[]{:S(2)}, u32[]{:S(2)}) %collective-permute-start.6) | collective-permute-done | bytes 65568 | tf_op jit(solution)/shard_map/ppermute | solution.py:25
  25.9 1.8 %shard_map.68.refs_1_ = f32[384,512]{1,0:T(8,128)S(1)} custom-call(bf16[8192,512]{1,0:T(8,128)(2,1)S(1)} %copy-done.2, bf16[384,2048]{1,0:T(8,128)(2,1)S(1)} %collective-permute-done.3.refs_0_, f32[384,512]{1,0:T(8,128)S(1)} %shard_map.67.refs_1_), custom_call_target="tpu_custom_call" | custom-call | flops 99999997952 | tf_op jit(solution)/shard_map/pallas_call | solution.py:299
  27.8 2.0 %collective-permute-start.8 = (bf16[64,512]{1,0:T(8,128)(2,1)}, bf16[64,512]{1,0:T(8,128)(2,1)S(1)}, u32[]{:S(2)}, u32[]{:S(2)}) collective-permute-start(bf16[64,512]{1,0:T(8,128)(2,1)} %bitcast.9.refs_5_), channel_id=1, source_target_pairs={{0,8},{4,12},{8,0},{12,4},{16,28},{20,24},{24,20},{28,16},{1,9},{5... | collective-permute-start | bytes 196616 | tf_op jit(solution)/shard_map/ppermute | solution.py:317
  29.8 1.8 %collective-permute-done.9.refs_1_ = bf16[64,2048]{1,0:T(8,128)(2,1)S(1)} collective-permute-done((bf16[64,2048]{1,0:T(8,128)(2,1)}, bf16[64,2048]{1,0:T(8,128)(2,1)S(1)}, u32[]{:S(2)}, u32[]{:S(2)}) %collective-permute-start.9) | collective-permute-done | bytes 262176 | tf_op jit(solution)/shard_map/ppermute | solution.py:25
  31.6 2.2 %collective-permute-done.10.refs_3_ = bf16[64,2048]{1,0:T(8,128)(2,1)S(1)} collective-permute-done((bf16[64,2048]{1,0:T(8,128)(2,1)}, bf16[64,2048]{1,0:T(8,128)(2,1)S(1)}, u32[]{:S(2)}, u32[]{:S(2)}) %collective-permute-start.10) | collective-permute-done | bytes 262176 | tf_op jit(solution)/shard_map/ppermute | solution.py:25
  33.8 2.5 %shard_map.69 = f32[64,384]{1,0:T(8,128)S(1)} custom-call(bf16[384,2048]{1,0:T(8,128)(2,1)S(1)} %copy-done, s32[1,384]{1,0:T(1,128)S(1)} %get-tuple-element.70.stored_ref.refs_2_, bf16[64,2048]{1,0:T(8,128)(2,1)} %shard_map.64.refs_0_, bf16[64,2048]{1,0:T(8,128)(2,1)S(1)} %collective-permute-done.9.refs_1_, bf16[64,2048]{1,0:T(8,128)(2,1)} %collective-permute-done.5.refs_2_, ...), custom_call_target="tpu_custom_call" | custom-call | flops 99999997952 | tf_op jit(solution)/shard_map/pallas_call | solution.py:356
  36.9 2.2 %shard_map.70.refs_1_ = f32[384,512]{1,0:T(8,128)S(1)} custom-call(bf16[8192,512]{1,0:T(8,128)(2,1)S(1)} %copy-done.2, bf16[384,1536]{1,0:T(8,128)(2,1)} %collective-permute-done.7.refs_0_, f32[384,512]{1,0:T(8,128)S(1)} %shard_map.68.refs_1_), custom_call_target="tpu_custom_call" | custom-call | flops 99999997952 | tf_op jit(solution)/shard_map/pallas_call | solution.py:299
  39.1 1.1 %collective-permute-start.11 = (bf16[64,512]{1,0:T(8,128)(2,1)S(1)}, bf16[64,512]{1,0:T(8,128)(2,1)S(1)}, u32[]{:S(2)}, u32[]{:S(2)}) collective-permute-start(bf16[64,512]{1,0:T(8,128)(2,1)S(1)} %collective-permute-done.8.refs_7_), channel_id=1, source_target_pairs={{0,16},{16,0},{1,17},{17,1},{2,18},{18,2},{3,19},{19,3},{4,20},{20... | collective-permute-start | bytes 196616 | tf_op jit(solution)/shard_map/ppermute | solution.py:25
  40.8 1.5 %collective-permute-start.15 = (bf16[64,384]{1,0:T(8,128)(2,1)}, bf16[64,384]{1,0:T(8,128)(2,1)}, u32[]{:S(2)}, u32[]{:S(2)}) collective-permute-start(bf16[64,384]{1,0:T(8,128)(2,1)} %get-tuple-element.93), channel_id=1, source_target_pairs={{0,2},{1,3},{2,0},{3,1},{4,6},{5,7},{6,4},{7,5},{8,10},{9,11},{10,... | collective-permute-start | bytes 147464 | tf_op jit(solution)/shard_map/ppermute | solution.py:25
  42.3 1.4 %shard_map.71.refs_1_ = f32[384,512]{1,0:T(8,128)S(1)} custom-call(bf16[8192,512]{1,0:T(8,128)(2,1)S(1)} %copy-done.2, bf16[384,1536]{1,0:T(8,128)(2,1)S(1)} %collective-permute-done.12.refs_0_, f32[384,512]{1,0:T(8,128)S(1)} %shard_map.70.refs_1_), custom_call_target="tpu_custom_call" | custom-call | flops 99999997952 | tf_op jit(solution)/shard_map/pallas_call | solution.py:299
  43.8 1.4 %shard_map.72.refs_1_ = f32[384,512]{1,0:T(8,128)S(1)} custom-call(bf16[8192,512]{1,0:T(8,128)(2,1)S(1)} %copy-done.2, bf16[384,512]{1,0:T(8,128)(2,1)} %collective-permute-done.4.refs_0_, f32[384,512]{1,0:T(8,128)S(1)} %shard_map.71.refs_1_), custom_call_target="tpu_custom_call" | custom-call | flops 99999997952 | tf_op jit(solution)/shard_map/pallas_call | solution.py:299
  45.7 2.1 %shard_map.73 = bf16[384,512]{1,0:T(8,128)(2,1)} custom-call(bf16[8192,512]{1,0:T(8,128)(2,1)S(1)} %copy-done.2, bf16[384,512]{1,0:T(8,128)(2,1)S(1)} %collective-permute-done.14.refs_0_, f32[384,512]{1,0:T(8,128)S(1)} %shard_map.72.refs_1_, s32[1,384]{1,0:T(1,128)S(1)} %copy-done.6, f32[64,384]{1,0:T(8,128)S(1)} %get-tuple-element.87.refs_3_, ...), custom_call_target="tpu_custom_call" | custom-call | flops 99999997952 | tf_op jit(solution)/shard_map/pallas_call | solution.py:390
  (34 shorter events, 3.5 us)
Async XLA Ops:
  0.0 8.3 %copy-start = (bf16[384,2048]{1,0:T(8,128)(2,1)S(1)}, bf16[384,2048]{1,0:T(8,128)(2,1)}, u32[]{:S(2)}) copy-start(bf16[384,2048]{1,0:T(8,128)(2,1)} %tokens_ref.1) | copy-start | bytes 4718596
  0.0 11.8 %copy-start.3 = (s32[384,1]{0,1:T(1,128)S(1)}, s32[384,1]{0,1:T(1,128)}, u32[]{:S(2)}) copy-start(s32[384,1]{0,1:T(1,128)} %param.7) | copy-start | bytes 4612
  0.0 11.8 %copy-start.4 = (s32[4]{0:T(128)S(1)}, s32[4]{0:T(128)}, u32[]{:S(2)}) copy-start(s32[4]{0:T(128)} %placement_ref.1) | copy-start | bytes 52
  1.1 7.2 %collective-permute-start = (bf16[16,2048]{1,0:T(8,128)(2,1)S(1)}, bf16[16,2048]{1,0:T(8,128)(2,1)S(1)}, u32[]{:S(2)}, u32[]{:S(2)}) collective-permute-start(bf16[16,2048]{1,0:T(8,128)(2,1)S(1)} %get-tuple-element.50), channel_id=1, source_target_pairs={{0,1},{1,0},{2,3},{3,2},{4,5},{5,4},{6,7},{7,6},{8,9},{9,8},{10,11... | collective-permute-start | bytes 196616 | tf_op jit(solution)/shard_map/ppermute | solution.py:25
  1.6 6.7 %collective-permute-start.1 = (bf16[16,2048]{1,0:T(8,128)(2,1)S(1)}, bf16[16,2048]{1,0:T(8,128)(2,1)S(1)}, u32[]{:S(2)}, u32[]{:S(2)}) collective-permute-start(bf16[16,2048]{1,0:T(8,128)(2,1)S(1)} %get-tuple-element.52), channel_id=1, source_target_pairs={{0,2},{1,3},{2,0},{3,1},{4,6},{5,7},{6,4},{7,5},{8,10},{9,11},{10,... | collective-permute-start | bytes 196616 | tf_op jit(solution)/shard_map/ppermute | solution.py:25
  4.2 4.2 %collective-permute-start.2 = (bf16[16,2048]{1,0:T(8,128)(2,1)S(1)}, bf16[16,2048]{1,0:T(8,128)(2,1)S(1)}, u32[]{:S(2)}, u32[]{:S(2)}) collective-permute-start(bf16[16,2048]{1,0:T(8,128)(2,1)S(1)} %get-tuple-element.53), channel_id=1, source_target_pairs={{0,3},{1,2},{2,1},{3,0},{4,7},{5,6},{6,5},{7,4},{8,11},{9,10},{10,... | collective-permute-start | bytes 196616 | tf_op jit(solution)/shard_map/ppermute | solution.py:25
  6.5 29.8 %collective-permute-start.7 = (bf16[384,1536]{1,0:T(8,128)(2,1)}, bf16[384,1536]{1,0:T(8,128)(2,1)}, u32[]{:S(2)}, u32[]{:S(2)}) collective-permute-start(bf16[384,1536]{1,0:T(8,128)(2,1)} %get-tuple-element.69), channel_id=1, source_target_pairs={{0,2},{1,3},{2,0},{3,1},{4,6},{5,7},{6,4},{7,5},{8,10},{9,11},{10,... | collective-permute-start | bytes 3538952 | tf_op jit(solution)/shard_map/ppermute | solution.py:25
  8.3 8.3 %collective-permute-start.3 = (bf16[384,2048]{1,0:T(8,128)(2,1)S(1)}, bf16[384,2048]{1,0:T(8,128)(2,1)S(1)}, u32[]{:S(2)}, u32[]{:S(2)}) collective-permute-start(bf16[384,2048]{1,0:T(8,128)(2,1)S(1)} %copy-done), channel_id=1, source_target_pairs={{0,1},{1,0},{2,3},{3,2},{4,5},{5,4},{6,7},{7,6},{8,9},{9,8},{10,11... | collective-permute-start | bytes 4718600 | tf_op jit(solution)/shard_map/ppermute | solution.py:25
  9.1 15.7 %collective-permute-start.5 = (bf16[64,2048]{1,0:T(8,128)(2,1)}, bf16[64,2048]{1,0:T(8,128)(2,1)}, u32[]{:S(2)}, u32[]{:S(2)}) collective-permute-start(bf16[64,2048]{1,0:T(8,128)(2,1)} %shard_map.64.refs_0_), channel_id=1, source_target_pairs={{0,8},{4,12},{8,0},{12,4},{16,28},{20,24},{24,20},{28,16},{1,9},{5... | collective-permute-start | bytes 786440 | tf_op jit(solution)/shard_map/ppermute | solution.py:317
  11.8 3.4 %copy-start.1 = (bf16[8192,512]{1,0:T(8,128)(2,1)S(1)}, bf16[8192,512]{1,0:T(8,128)(2,1)}, u32[]{:S(2)}) copy-start(bf16[8192,512]{1,0:T(8,128)(2,1)} %weight_ref.13) | copy-start | bytes 25165828
  15.2 3.4 %copy-start.2 = (bf16[8192,512]{1,0:T(8,128)(2,1)S(1)}, bf16[8192,512]{1,0:T(8,128)(2,1)}, u32[]{:S(2)}) copy-start(bf16[8192,512]{1,0:T(8,128)(2,1)} %weight_ref.13) | copy-start | bytes 25165828
  16.6 17.2 %copy-start.5 = (s32[1,384]{1,0:T(1,128)}, s32[1,384]{1,0:T(1,128)S(1)}, u32[]{:S(2)}) copy-start(s32[1,384]{1,0:T(1,128)S(1)} %get-tuple-element.70.stored_ref.refs_2_) | copy-start | bytes 4612
  16.6 9.3 %collective-permute-start.6 = (bf16[64,512]{1,0:T(8,128)(2,1)}, bf16[64,512]{1,0:T(8,128)(2,1)S(1)}, u32[]{:S(2)}, u32[]{:S(2)}) collective-permute-start(bf16[64,512]{1,0:T(8,128)(2,1)} %bitcast.9.refs_5_), channel_id=1, source_target_pairs={{0,4},{4,0},{8,12},{12,8},{1,5},{5,1},{9,13},{13,9},{2,6},{6,2},{1... | collective-permute-start | bytes 196616 | tf_op jit(solution)/shard_map/ppermute | solution.py:25
  19.4 12.2 %collective-permute-start.9 = (bf16[64,2048]{1,0:T(8,128)(2,1)}, bf16[64,2048]{1,0:T(8,128)(2,1)S(1)}, u32[]{:S(2)}, u32[]{:S(2)}) collective-permute-start(bf16[64,2048]{1,0:T(8,128)(2,1)} %shard_map.64.refs_0_), channel_id=1, source_target_pairs={{0,4},{4,0},{8,12},{12,8},{1,5},{5,1},{9,13},{13,9},{2,6},{6,2},{1... | collective-permute-start | bytes 786440 | tf_op jit(solution)/shard_map/ppermute | solution.py:25
  21.0 22.7 %collective-permute-start.4 = (bf16[384,512]{1,0:T(8,128)(2,1)}, bf16[384,512]{1,0:T(8,128)(2,1)}, u32[]{:S(2)}, u32[]{:S(2)}) collective-permute-start(bf16[384,512]{1,0:T(8,128)(2,1)} %get-tuple-element.60), channel_id=1, source_target_pairs={{0,2},{1,3},{2,0},{3,1},{4,6},{5,7},{6,4},{7,5},{8,10},{9,11},{10,... | collective-permute-start | bytes 1179656 | tf_op jit(solution)/shard_map/ppermute | solution.py:25
  25.9 7.8 %collective-permute-start.10 = (bf16[64,2048]{1,0:T(8,128)(2,1)}, bf16[64,2048]{1,0:T(8,128)(2,1)S(1)}, u32[]{:S(2)}, u32[]{:S(2)}) collective-permute-start(bf16[64,2048]{1,0:T(8,128)(2,1)} %collective-permute-done.5.refs_2_), channel_id=1, source_target_pairs={{0,16},{16,0},{1,17},{17,1},{2,18},{18,2},{3,19},{19,3},{4,20},{20... | collective-permute-start | bytes 786440 | tf_op jit(solution)/shard_map/ppermute | solution.py:25
  27.8 8.5 %collective-permute-start.8 = (bf16[64,512]{1,0:T(8,128)(2,1)}, bf16[64,512]{1,0:T(8,128)(2,1)S(1)}, u32[]{:S(2)}, u32[]{:S(2)}) collective-permute-start(bf16[64,512]{1,0:T(8,128)(2,1)} %bitcast.9.refs_5_), channel_id=1, source_target_pairs={{0,8},{4,12},{8,0},{12,4},{16,28},{20,24},{24,20},{28,16},{1,9},{5... | collective-permute-start | bytes 196616 | tf_op jit(solution)/shard_map/ppermute | solution.py:317
  36.3 3.9 %collective-permute-start.13 = (f32[64,384]{1,0:T(8,128)S(1)}, f32[64,384]{1,0:T(8,128)S(1)}, u32[]{:S(2)}, u32[]{:S(2)}) collective-permute-start(f32[64,384]{1,0:T(8,128)S(1)} %shard_map.69), channel_id=1, source_target_pairs={{0,1},{1,0},{2,3},{3,2},{4,5},{5,4},{6,7},{7,6},{8,9},{9,8},{10,11... | collective-permute-start | bytes 294920 | tf_op jit(solution)/shard_map/ppermute | solution.py:25
  36.4 6.0 %collective-permute-start.12 = (bf16[384,1536]{1,0:T(8,128)(2,1)}, bf16[384,1536]{1,0:T(8,128)(2,1)S(1)}, u32[]{:S(2)}, u32[]{:S(2)}) collective-permute-start(bf16[384,1536]{1,0:T(8,128)(2,1)} %collective-permute-done.7.refs_0_), channel_id=1, source_target_pairs={{0,1},{1,0},{2,3},{3,2},{4,5},{5,4},{6,7},{7,6},{8,9},{9,8},{10,11... | collective-permute-start | bytes 3538952 | tf_op jit(solution)/shard_map/ppermute | solution.py:25
  39.1 4.6 %collective-permute-start.11 = (bf16[64,512]{1,0:T(8,128)(2,1)S(1)}, bf16[64,512]{1,0:T(8,128)(2,1)S(1)}, u32[]{:S(2)}, u32[]{:S(2)}) collective-permute-start(bf16[64,512]{1,0:T(8,128)(2,1)S(1)} %collective-permute-done.8.refs_7_), channel_id=1, source_target_pairs={{0,16},{16,0},{1,17},{17,1},{2,18},{18,2},{3,19},{19,3},{4,20},{20... | collective-permute-start | bytes 196616 | tf_op jit(solution)/shard_map/ppermute | solution.py:25
  40.8 4.4 %collective-permute-start.15 = (bf16[64,384]{1,0:T(8,128)(2,1)}, bf16[64,384]{1,0:T(8,128)(2,1)}, u32[]{:S(2)}, u32[]{:S(2)}) collective-permute-start(bf16[64,384]{1,0:T(8,128)(2,1)} %get-tuple-element.93), channel_id=1, source_target_pairs={{0,2},{1,3},{2,0},{3,1},{4,6},{5,7},{6,4},{7,5},{8,10},{9,11},{10,... | collective-permute-start | bytes 147464 | tf_op jit(solution)/shard_map/ppermute | solution.py:25
  43.7 2.0 %copy-start.6 = (s32[1,384]{1,0:T(1,128)S(1)}, s32[1,384]{1,0:T(1,128)}, u32[]{:S(2)}) copy-start(s32[1,384]{1,0:T(1,128)} %copy-done.5) | copy-start | bytes 4612
  43.7 2.0 %collective-permute-start.14 = (bf16[384,512]{1,0:T(8,128)(2,1)}, bf16[384,512]{1,0:T(8,128)(2,1)S(1)}, u32[]{:S(2)}, u32[]{:S(2)}) collective-permute-start(bf16[384,512]{1,0:T(8,128)(2,1)} %collective-permute-done.4.refs_0_), channel_id=1, source_target_pairs={{0,1},{1,0},{2,3},{3,2},{4,5},{5,4},{6,7},{7,6},{8,9},{9,8},{10,11... | collective-permute-start | bytes 1179656 | tf_op jit(solution)/shard_map/ppermute | solution.py:25

commit v26 on v25

--- a/solution.py
+++ b/solution.py
@@ -55,7 +55,11 @@
     outs, (held_ref, sems) = refs[:-2], refs[-2:]
     steps, rows = held_ref.shape[:2]
     copies = [
-        pltpu.make_async_copy(source_ref.at[pl.ds(i * rows, rows)], held_ref.at[i], sems.at[0, i])
+        pltpu.make_async_copy(
+            source_ref.at[pl.ds(i * rows, rows), pl.ds(edges[0], edges[-1] - edges[0])],
+            held_ref.at[i],
+            sems.at[0, i],
+        )
         for i in range(steps)
     ]
     for copy in copies:
@@ -66,7 +70,7 @@
         for m, (a, b, out) in enumerate(zip(edges, edges[1:], outs)):
             leaving.append(
                 pltpu.make_async_copy(
-                    held_ref.at[i, :, pl.ds(a, b - a)],
+                    held_ref.at[i, :, pl.ds(a - edges[0], b - a)],
                     out.at[pl.ds(i * rows, rows)],
                     sems.at[1 + m, i],
                 )
@@ -245,21 +249,22 @@
         for flip in range(tensors)
     ]
     uncut, pieces = chained(tokens, pieces)
-    steps = 6
-    chunks = list(
-        call(
-            functools.partial(cut_kernel, edges),
-            [jax.ShapeDtypeStruct((rows, b - a), tokens.dtype) for a, b in zip(edges, edges[1:])],
+
+    def cut(array, m, mib, steps=3):
+        ends = edges[m : m + 2]
+        return call(
+            functools.partial(cut_kernel, ends),
+            [jax.ShapeDtypeStruct((rows, ends[1] - ends[0]), array.dtype)],
             [ANYWHERE],
             [
-                pltpu.VMEM((steps, rows // steps, depth), tokens.dtype),
-                pltpu.SemaphoreType.DMA((len(edges), steps)),
+                pltpu.VMEM((steps, rows // steps, ends[1] - ends[0]), array.dtype),
+                pltpu.SemaphoreType.DMA((2, steps)),
             ],
-            [ANYWHERE] * (len(edges) - 1),
-            cost=FREE,
-            mib=56,
-        )(uncut)
-    )
+            [ANYWHERE],
+            mib=mib,
+        )(array)[0]
+
+    chunks = [cut(uncut, 0, 56)]
     pieces = [pieces[0]] + [flipped(pieces[f], "tensor", f) for f in range(1, tensors)]
     pieces[1], here = chained(pieces[1], tokens)
     neighbour = flipped(here, "tensor", 1)
@@ -335,9 +340,8 @@
         tile_scratch(tile, rows, places, columns),
         [VECTOR, VECTOR],
     )(placement, tenant.reshape(1, rows), frozen_projection_weight, here)
-    total, own, up, neighbour, chunks[1] = chained(
-        total, own, lowrank_up_weight[0], neighbour, chunks[1]
-    )
+    total, own, up, neighbour, uncut = chained(total, own, lowrank_up_weight[0], neighbour, tokens)
+    chunks.append(cut(uncut, 1, 24))
     far.append(send(1))
     single, single_up = fetch_near(own), fetch_near(up)
     total = products([(0, depth // 2, depth // 2, depth // 2)], [here], total)

time: 48.2 us -> 49 us (1.017)
  starting transfers between devices: 17.5 us -> 15.2 us
  local copies, waits for them, and re-layouts: 4.79 us -> 6.97 us
  Pallas kernels: 16.6 us -> 17.2 us
    unnamed x14 -> x24, local copies, waits for them, and re-layouts: 3.72 us -> 6.02 us
    ppermute x14, waiting for transfers between devices: 5.63 us -> 7.35 us  [flipped(): return lax.ppermute(value, axis, [(i, i ^ flip) for i in range(count)])]
    ppermute x2, waiting for transfers between devices: 2.53 us -> 0.97 us  [fetch_far(): lax.ppermute(value, ('parts', 'adapter'), route)]
    ppermute x14, starting transfers between devices: 12.8 us -> 11.5 us  [flipped(): return lax.ppermute(value, axis, [(i, i ^ flip) for i in range(count)])]
    ppermute x2, starting transfers between devices: 4.68 us -> 3.64 us  [fetch_far(): lax.ppermute(value, ('parts', 'adapter'), route)]
    pallas_call x1 -> x2, Pallas kernels: 2.23 us -> 2.91 us  [cut(): call(functools.partial(cut_kernel, ends), [jax.ShapeDtypeStruct((rows, en...]
  transfers between devices with their start and end apart: 16 -> 16, of which waited for: 5 -> 6; matrix products, arithmetic and copies ran while one was open for 1% -> 1% of each run, Pallas kernels for 30% -> 31%
where the time goes in v26:
time: 49 us; the launch traced here: 48.5 us
  Pallas kernels  17.2 us (35%)
  starting transfers between devices  15.2 us (31%)
  waiting for transfers between devices  8.32 us (17%)
  local copies, waits for them, and re-layouts  6.97 us (14%)
  other arithmetic  0.63 us (1%)
    ppermute x14, starting transfers between devices, flipped(): return lax.ppermute(value, axis, [(i, i ^ flip) for i in range(count)])  11.5 us
    pallas_call x5, Pallas kernels, products(): call(functools.partial(products_kernel, tile, depth, places), jax.ShapeDt...  7.64 us
    ppermute x14, waiting for transfers between devices, flipped(): return lax.ppermute(value, axis, [(i, i ^ flip) for i in range(count)])  7.35 us
    unnamed x24, local copies, waits for them, and re-layouts  6.02 us
    ppermute x2, starting transfers between devices, fetch_far(): lax.ppermute(value, ('parts', 'adapter'), route)  3.64 us
    pallas_call x2, Pallas kernels, cut(): call(functools.partial(cut_kernel, ends), [jax.ShapeDtypeStruct((rows, en...  2.91 us
    pallas_call x1, Pallas kernels, body(): call(functools.partial(shrink_kernel, tile, flips, pairs, slots), jax.Sha...  2.5 us
    pallas_call x1, Pallas kernels, body(): call(functools.partial(last_kernel, depth, places, flips, pairs, slots),...  2.04 us
  transfers between devices with their start and end apart: 16, of which 6 were waited for; matrix products, arithmetic and copies ran while one was open for 1% of the time, Pallas kernels for 31%

profile of v26, /device:TPU:0, one launch (start us, length us, event | category | flops | bytes accessed | tf_op | source)
XLA Modules:
  0.0 48.5 jit_solution(8366166108263213202)
XLA Ops:
  0.0 1.0 %dynamic-slice_bitcast_fusion = (bf16[16,2048]{1,0:T(8,128)(2,1)S(1)}, bf16[16,2048]{1,0:T(8,128)(2,1)S(1)}, bf16[16,2048]{1,0:T(8,128)(2,1)S(1)}, bf16[16,2048]{1,0:T(8,128)(2,1)S(1)}) fusion(bf16[1,8192,16]{1,2,0:T(8,128)(2,1)} %param.10, s32[]{:T(128)S(6)} %select_n.15, s32[]{:T(128)S(6)} %select_n.13, s32[]{:T(128)S(6)} %select_n.12, s32[]{:T(128)S(6)} %select_n.14), kind=kLoop, calls=%fused_computation | loop fusion | bytes 524304 | tf_op jit(solution)/shard_map/dynamic_slice | solution.py:248
  1.5 2.6 %collective-permute-start.1 = (bf16[16,2048]{1,0:T(8,128)(2,1)S(1)}, bf16[16,2048]{1,0:T(8,128)(2,1)S(1)}, u32[]{:S(2)}, u32[]{:S(2)}) collective-permute-start(bf16[16,2048]{1,0:T(8,128)(2,1)S(1)} %get-tuple-element.50), channel_id=1, source_target_pairs={{0,2},{1,3},{2,0},{3,1},{4,6},{5,7},{6,4},{7,5},{8,10},{9,11},{10,... | collective-permute-start | bytes 196616 | tf_op jit(solution)/shard_map/ppermute | solution.py:25
  4.1 2.1 %shard_map.69 = bf16[384,1536]{1,0:T(8,128)(2,1)} custom-call(bf16[384,2048]{1,0:T(8,128)(2,1)} %tokens_ref.1), custom_call_target="tpu_custom_call" | custom-call | flops 99999997952 | tf_op jit(solution)/shard_map/pallas_call | solution.py:255
  6.2 1.8 %collective-permute-start.7 = (bf16[384,1536]{1,0:T(8,128)(2,1)}, bf16[384,1536]{1,0:T(8,128)(2,1)}, u32[]{:S(2)}, u32[]{:S(2)}) collective-permute-start(bf16[384,1536]{1,0:T(8,128)(2,1)} %shard_map.69), channel_id=1, source_target_pairs={{0,2},{1,3},{2,0},{3,1},{4,6},{5,7},{6,4},{7,5},{8,10},{9,11},{10,... | collective-permute-start | bytes 3538952 | tf_op jit(solution)/shard_map/ppermute | solution.py:25
  8.9 2.7 %collective-permute-start.5 = (bf16[64,2048]{1,0:T(8,128)(2,1)}, bf16[64,2048]{1,0:T(8,128)(2,1)}, u32[]{:S(2)}, u32[]{:S(2)}) collective-permute-start(bf16[64,2048]{1,0:T(8,128)(2,1)} %shard_map.64.refs_0_), channel_id=1, source_target_pairs={{0,8},{4,12},{8,0},{12,4},{16,28},{20,24},{24,20},{28,16},{1,9},{5... | collective-permute-start | bytes 786440 | tf_op jit(solution)/shard_map/ppermute | solution.py:322
  11.5 3.4 %copy-done = bf16[8192,512]{1,0:T(8,128)(2,1)S(1)} copy-done((bf16[8192,512]{1,0:T(8,128)(2,1)S(1)}, bf16[8192,512]{1,0:T(8,128)(2,1)}, u32[]{:S(2)}) %copy-start) | copy-done | bytes 8388632
  14.9 1.4 %shard_map.65 = (f32[384,512]{1,0:T(8,128)S(1)}, s32[1,384]{1,0:T(1,128)S(1)}) custom-call(s32[4]{0:T(128)S(1)} %copy-done.9, s32[1,384]{1,0:T(1,128)S(1)} %bitcast.21, bf16[8192,512]{1,0:T(8,128)(2,1)S(1)} %copy-done, bf16[384,2048]{1,0:T(8,128)(2,1)S(1)} %copy-done.2), custom_call_target="tpu_custom_call" | custom-call | flops 99999997952 | tf_op jit(solution)/shard_map/pallas_call | solution.py:333
  16.3 2.0 %copy-done.1 = bf16[8192,512]{1,0:T(8,128)(2,1)S(1)} copy-done((bf16[8192,512]{1,0:T(8,128)(2,1)S(1)}, bf16[8192,512]{1,0:T(8,128)(2,1)}, u32[]{:S(2)}) %copy-start.1) | copy-done | bytes 8388632
  19.2 1.6 %collective-permute-start.6 = (bf16[64,512]{1,0:T(8,128)(2,1)S(1)}, bf16[64,512]{1,0:T(8,128)(2,1)S(1)}, u32[]{:S(2)}, u32[]{:S(2)}) collective-permute-start(bf16[64,512]{1,0:T(8,128)(2,1)S(1)} %bitcast.18), channel_id=1, source_target_pairs={{0,4},{4,0},{8,12},{12,8},{1,5},{5,1},{9,13},{13,9},{2,6},{6,2},{1... | collective-permute-start | bytes 196616 | tf_op jit(solution)/shard_map/ppermute | solution.py:25
  21.3 0.8 %shard_map.66 = bf16[384,512]{1,0:T(8,128)(2,1)} custom-call(bf16[384,2048]{1,0:T(8,128)(2,1)S(1)} %copy-done.2), custom_call_target="tpu_custom_call" | custom-call | flops 99999997952 | tf_op jit(solution)/shard_map/pallas_call | solution.py:255
  22.1 1.4 %collective-permute-start.4 = (bf16[384,512]{1,0:T(8,128)(2,1)}, bf16[384,512]{1,0:T(8,128)(2,1)}, u32[]{:S(2)}, u32[]{:S(2)}) collective-permute-start(bf16[384,512]{1,0:T(8,128)(2,1)} %shard_map.66), channel_id=1, source_target_pairs={{0,2},{1,3},{2,0},{3,1},{4,6},{5,7},{6,4},{7,5},{8,10},{9,11},{10,... | collective-permute-start | bytes 1179656 | tf_op jit(solution)/shard_map/ppermute | solution.py:25
  23.5 1.0 %collective-permute-done.5.refs_2_ = bf16[64,2048]{1,0:T(8,128)(2,1)} collective-permute-done((bf16[64,2048]{1,0:T(8,128)(2,1)}, bf16[64,2048]{1,0:T(8,128)(2,1)}, u32[]{:S(2)}, u32[]{:S(2)}) %collective-permute-start.5) | collective-permute-done | bytes 262176 | tf_op jit(solution)/shard_map/ppermute | solution.py:322
  24.5 1.3 %collective-permute-done.6.refs_6_ = bf16[64,512]{1,0:T(8,128)(2,1)S(1)} collective-permute-done((bf16[64,512]{1,0:T(8,128)(2,1)S(1)}, bf16[64,512]{1,0:T(8,128)(2,1)S(1)}, u32[]{:S(2)}, u32[]{:S(2)}) %collective-permute-start.6) | collective-permute-done | bytes 65568 | tf_op jit(solution)/shard_map/ppermute | solution.py:25
  26.4 0.9 %collective-permute-start.10 = (bf16[64,2048]{1,0:T(8,128)(2,1)}, bf16[64,2048]{1,0:T(8,128)(2,1)S(1)}, u32[]{:S(2)}, u32[]{:S(2)}) collective-permute-start(bf16[64,2048]{1,0:T(8,128)(2,1)} %collective-permute-done.5.refs_2_), channel_id=1, source_target_pairs={{0,16},{16,0},{1,17},{17,1},{2,18},{18,2},{3,19},{19,3},{4,20},{20... | collective-permute-start | bytes 786440 | tf_op jit(solution)/shard_map/ppermute | solution.py:25
  27.3 1.8 %shard_map.68.refs_1_ = f32[384,512]{1,0:T(8,128)S(1)} custom-call(bf16[8192,512]{1,0:T(8,128)(2,1)S(1)} %copy-done.1, bf16[384,2048]{1,0:T(8,128)(2,1)S(1)} %collective-permute-done.3.refs_0_, f32[384,512]{1,0:T(8,128)S(1)} %shard_map.67.refs_1_), custom_call_target="tpu_custom_call" | custom-call | flops 99999997952 | tf_op jit(solution)/shard_map/pallas_call | solution.py:304
  29.2 1.0 %collective-permute-start.8 = (bf16[64,512]{1,0:T(8,128)(2,1)S(1)}, bf16[64,512]{1,0:T(8,128)(2,1)S(1)}, u32[]{:S(2)}, u32[]{:S(2)}) collective-permute-start(bf16[64,512]{1,0:T(8,128)(2,1)S(1)} %bitcast.19), channel_id=1, source_target_pairs={{0,8},{4,12},{8,0},{12,4},{16,28},{20,24},{24,20},{28,16},{1,9},{5... | collective-permute-start | bytes 196616 | tf_op jit(solution)/shard_map/ppermute | solution.py:322
  30.2 1.3 %collective-permute-done.9.refs_1_ = bf16[64,2048]{1,0:T(8,128)(2,1)} collective-permute-done((bf16[64,2048]{1,0:T(8,128)(2,1)}, bf16[64,2048]{1,0:T(8,128)(2,1)}, u32[]{:S(2)}, u32[]{:S(2)}) %collective-permute-start.9) | collective-permute-done | bytes 262176 | tf_op jit(solution)/shard_map/ppermute | solution.py:25
  31.4 3.5 %collective-permute-done.10.refs_3_ = bf16[64,2048]{1,0:T(8,128)(2,1)S(1)} collective-permute-done((bf16[64,2048]{1,0:T(8,128)(2,1)}, bf16[64,2048]{1,0:T(8,128)(2,1)S(1)}, u32[]{:S(2)}, u32[]{:S(2)}) %collective-permute-start.10) | collective-permute-done | bytes 262176 | tf_op jit(solution)/shard_map/ppermute | solution.py:25
  34.9 2.5 %shard_map.70 = f32[64,384]{1,0:T(8,128)S(1)} custom-call(bf16[384,2048]{1,0:T(8,128)(2,1)S(1)} %copy-done.2, s32[1,384]{1,0:T(1,128)S(1)} %get-tuple-element.66.stored_ref.refs_2_, bf16[64,2048]{1,0:T(8,128)(2,1)} %shard_map.64.refs_0_, bf16[64,2048]{1,0:T(8,128)(2,1)} %collective-permute-done.9.refs_1_, bf16[64,2048]{1,0:T(8,128)(2,1)} %collective-permute-done.5.refs_2_, ...), custom_call_target="tpu_custom_call" | custom-call | flops 99999997952 | tf_op jit(solution)/shard_map/pallas_call | solution.py:360
  38.0 2.2 %shard_map.71.refs_1_ = f32[384,512]{1,0:T(8,128)S(1)} custom-call(bf16[8192,512]{1,0:T(8,128)(2,1)S(1)} %copy-done.1, bf16[384,1536]{1,0:T(8,128)(2,1)} %collective-permute-done.7.refs_0_, f32[384,512]{1,0:T(8,128)S(1)} %shard_map.68.refs_1_), custom_call_target="tpu_custom_call" | custom-call | flops 99999997952 | tf_op jit(solution)/shard_map/pallas_call | solution.py:304
  41.2 1.2 %collective-permute-start.15 = (bf16[64,384]{1,0:T(8,128)(2,1)}, bf16[64,384]{1,0:T(8,128)(2,1)}, u32[]{:S(2)}, u32[]{:S(2)}) collective-permute-start(bf16[64,384]{1,0:T(8,128)(2,1)} %get-tuple-element.89), channel_id=1, source_target_pairs={{0,2},{1,3},{2,0},{3,1},{4,6},{5,7},{6,4},{7,5},{8,10},{9,11},{10,... | collective-permute-start | bytes 147464 | tf_op jit(solution)/shard_map/ppermute | solution.py:25
  42.4 1.4 %shard_map.72.refs_1_ = f32[384,512]{1,0:T(8,128)S(1)} custom-call(bf16[8192,512]{1,0:T(8,128)(2,1)S(1)} %copy-done.1, bf16[384,1536]{1,0:T(8,128)(2,1)S(1)} %collective-permute-done.12.refs_0_, f32[384,512]{1,0:T(8,128)S(1)} %shard_map.71.refs_1_), custom_call_target="tpu_custom_call" | custom-call | flops 99999997952 | tf_op jit(solution)/shard_map/pallas_call | solution.py:304
  44.6 1.4 %shard_map.73.refs_1_ = f32[384,512]{1,0:T(8,128)S(1)} custom-call(bf16[8192,512]{1,0:T(8,128)(2,1)S(1)} %copy-done.1, bf16[384,512]{1,0:T(8,128)(2,1)} %collective-permute-done.4.refs_0_, f32[384,512]{1,0:T(8,128)S(1)} %shard_map.72.refs_1_), custom_call_target="tpu_custom_call" | custom-call | flops 99999997952 | tf_op jit(solution)/shard_map/pallas_call | solution.py:304
  46.5 2.0 %shard_map.74 = bf16[384,512]{1,0:T(8,128)(2,1)} custom-call(bf16[8192,512]{1,0:T(8,128)(2,1)S(1)} %copy-done.1, bf16[384,512]{1,0:T(8,128)(2,1)S(1)} %collective-permute-done.14.refs_0_, f32[384,512]{1,0:T(8,128)S(1)} %shard_map.73.refs_1_, s32[1,384]{1,0:T(1,128)S(1)} %copy-done.11, f32[64,384]{1,0:T(8,128)S(1)} %get-tuple-element.83.refs_3_, ...), custom_call_target="tpu_custom_call" | custom-call | flops 99999997952 | tf_op jit(solution)/shard_map/pallas_call | solution.py:394
  (45 shorter events, 6.3 us)
Async XLA Ops:
  1.0 7.1 %copy-start.2 = (bf16[384,2048]{1,0:T(8,128)(2,1)S(1)}, bf16[384,2048]{1,0:T(8,128)(2,1)}, u32[]{:S(2)}) copy-start(bf16[384,2048]{1,0:T(8,128)(2,1)} %tokens_ref.1) | copy-start | bytes 4718596
  1.0 10.6 %copy-start.8 = (s32[384,1]{0,1:T(1,128)S(1)}, s32[384,1]{0,1:T(1,128)}, u32[]{:S(2)}) copy-start(s32[384,1]{0,1:T(1,128)} %param.7) | copy-start | bytes 4612
  1.0 10.5 %copy-start.9 = (s32[4]{0:T(128)S(1)}, s32[4]{0:T(128)}, u32[]{:S(2)}) copy-start(s32[4]{0:T(128)} %placement_ref.1) | copy-start | bytes 52
  1.0 7.0 %collective-permute-start = (bf16[16,2048]{1,0:T(8,128)(2,1)S(1)}, bf16[16,2048]{1,0:T(8,128)(2,1)S(1)}, u32[]{:S(2)}, u32[]{:S(2)}) collective-permute-start(bf16[16,2048]{1,0:T(8,128)(2,1)S(1)} %get-tuple-element.48), channel_id=1, source_target_pairs={{0,1},{1,0},{2,3},{3,2},{4,5},{5,4},{6,7},{7,6},{8,9},{9,8},{10,11... | collective-permute-start | bytes 196616 | tf_op jit(solution)/shard_map/ppermute | solution.py:25
  1.5 6.6 %collective-permute-start.1 = (bf16[16,2048]{1,0:T(8,128)(2,1)S(1)}, bf16[16,2048]{1,0:T(8,128)(2,1)S(1)}, u32[]{:S(2)}, u32[]{:S(2)}) collective-permute-start(bf16[16,2048]{1,0:T(8,128)(2,1)S(1)} %get-tuple-element.50), channel_id=1, source_target_pairs={{0,2},{1,3},{2,0},{3,1},{4,6},{5,7},{6,4},{7,5},{8,10},{9,11},{10,... | collective-permute-start | bytes 196616 | tf_op jit(solution)/shard_map/ppermute | solution.py:25
  4.1 4.0 %collective-permute-start.2 = (bf16[16,2048]{1,0:T(8,128)(2,1)S(1)}, bf16[16,2048]{1,0:T(8,128)(2,1)S(1)}, u32[]{:S(2)}, u32[]{:S(2)}) collective-permute-start(bf16[16,2048]{1,0:T(8,128)(2,1)S(1)} %get-tuple-element.51), channel_id=1, source_target_pairs={{0,3},{1,2},{2,1},{3,0},{4,7},{5,6},{6,5},{7,4},{8,11},{9,10},{10,... | collective-permute-start | bytes 196616 | tf_op jit(solution)/shard_map/ppermute | solution.py:25
  6.2 31.2 %collective-permute-start.7 = (bf16[384,1536]{1,0:T(8,128)(2,1)}, bf16[384,1536]{1,0:T(8,128)(2,1)}, u32[]{:S(2)}, u32[]{:S(2)}) collective-permute-start(bf16[384,1536]{1,0:T(8,128)(2,1)} %shard_map.69), channel_id=1, source_target_pairs={{0,2},{1,3},{2,0},{3,1},{4,6},{5,7},{6,4},{7,5},{8,10},{9,11},{10,... | collective-permute-start | bytes 3538952 | tf_op jit(solution)/shard_map/ppermute | solution.py:25
  8.0 8.3 %collective-permute-start.3 = (bf16[384,2048]{1,0:T(8,128)(2,1)S(1)}, bf16[384,2048]{1,0:T(8,128)(2,1)S(1)}, u32[]{:S(2)}, u32[]{:S(2)}) collective-permute-start(bf16[384,2048]{1,0:T(8,128)(2,1)S(1)} %copy-done.2), channel_id=1, source_target_pairs={{0,1},{1,0},{2,3},{3,2},{4,5},{5,4},{6,7},{7,6},{8,9},{9,8},{10,11... | collective-permute-start | bytes 4718600 | tf_op jit(solution)/shard_map/ppermute | solution.py:25
  8.9 15.6 %collective-permute-start.5 = (bf16[64,2048]{1,0:T(8,128)(2,1)}, bf16[64,2048]{1,0:T(8,128)(2,1)}, u32[]{:S(2)}, u32[]{:S(2)}) collective-permute-start(bf16[64,2048]{1,0:T(8,128)(2,1)} %shard_map.64.refs_0_), channel_id=1, source_target_pairs={{0,8},{4,12},{8,0},{12,4},{16,28},{20,24},{24,20},{28,16},{1,9},{5... | collective-permute-start | bytes 786440 | tf_op jit(solution)/shard_map/ppermute | solution.py:322
  11.5 3.4 %copy-start = (bf16[8192,512]{1,0:T(8,128)(2,1)S(1)}, bf16[8192,512]{1,0:T(8,128)(2,1)}, u32[]{:S(2)}) copy-start(bf16[8192,512]{1,0:T(8,128)(2,1)} %weight_ref.13) | copy-start | bytes 25165828
  14.9 3.4 %copy-start.1 = (bf16[8192,512]{1,0:T(8,128)(2,1)S(1)}, bf16[8192,512]{1,0:T(8,128)(2,1)}, u32[]{:S(2)}) copy-start(bf16[8192,512]{1,0:T(8,128)(2,1)} %weight_ref.13) | copy-start | bytes 25165828
  16.3 18.6 %copy-start.10 = (s32[1,384]{1,0:T(1,128)}, s32[1,384]{1,0:T(1,128)S(1)}, u32[]{:S(2)}) copy-start(s32[1,384]{1,0:T(1,128)S(1)} %get-tuple-element.66.stored_ref.refs_2_) | copy-start | bytes 4612
  19.2 6.6 %collective-permute-start.6 = (bf16[64,512]{1,0:T(8,128)(2,1)S(1)}, bf16[64,512]{1,0:T(8,128)(2,1)S(1)}, u32[]{:S(2)}, u32[]{:S(2)}) collective-permute-start(bf16[64,512]{1,0:T(8,128)(2,1)S(1)} %bitcast.18), channel_id=1, source_target_pairs={{0,4},{4,0},{8,12},{12,8},{1,5},{5,1},{9,13},{13,9},{2,6},{6,2},{1... | collective-permute-start | bytes 196616 | tf_op jit(solution)/shard_map/ppermute | solution.py:25
  20.8 10.6 %collective-permute-start.9 = (bf16[64,2048]{1,0:T(8,128)(2,1)}, bf16[64,2048]{1,0:T(8,128)(2,1)}, u32[]{:S(2)}, u32[]{:S(2)}) collective-permute-start(bf16[64,2048]{1,0:T(8,128)(2,1)} %shard_map.64.refs_0_), channel_id=1, source_target_pairs={{0,4},{4,0},{8,12},{12,8},{1,5},{5,1},{9,13},{13,9},{2,6},{6,2},{1... | collective-permute-start | bytes 786440 | tf_op jit(solution)/shard_map/ppermute | solution.py:25
  22.1 7.1 %copy-start.4 = (bf16[1,64,512]{2,1,0:T(8,128)(2,1)S(1)}, bf16[1,64,512]{2,1,0:T(8,128)(2,1)}, u32[]{:S(2)}) copy-start(bf16[1,64,512]{2,1,0:T(8,128)(2,1)} %param.11) | copy-start | bytes 196612
  22.1 22.4 %collective-permute-start.4 = (bf16[384,512]{1,0:T(8,128)(2,1)}, bf16[384,512]{1,0:T(8,128)(2,1)}, u32[]{:S(2)}, u32[]{:S(2)}) collective-permute-start(bf16[384,512]{1,0:T(8,128)(2,1)} %shard_map.66), channel_id=1, source_target_pairs={{0,2},{1,3},{2,0},{3,1},{4,6},{5,7},{6,4},{7,5},{8,10},{9,11},{10,... | collective-permute-start | bytes 1179656 | tf_op jit(solution)/shard_map/ppermute | solution.py:25
  26.4 8.5 %collective-permute-start.10 = (bf16[64,2048]{1,0:T(8,128)(2,1)}, bf16[64,2048]{1,0:T(8,128)(2,1)S(1)}, u32[]{:S(2)}, u32[]{:S(2)}) collective-permute-start(bf16[64,2048]{1,0:T(8,128)(2,1)} %collective-permute-done.5.refs_2_), channel_id=1, source_target_pairs={{0,16},{16,0},{1,17},{17,1},{2,18},{18,2},{3,19},{19,3},{4,20},{20... | collective-permute-start | bytes 786440 | tf_op jit(solution)/shard_map/ppermute | solution.py:25
  29.2 8.3 %collective-permute-start.8 = (bf16[64,512]{1,0:T(8,128)(2,1)S(1)}, bf16[64,512]{1,0:T(8,128)(2,1)S(1)}, u32[]{:S(2)}, u32[]{:S(2)}) collective-permute-start(bf16[64,512]{1,0:T(8,128)(2,1)S(1)} %bitcast.19), channel_id=1, source_target_pairs={{0,8},{4,12},{8,0},{12,4},{16,28},{20,24},{24,20},{28,16},{1,9},{5... | collective-permute-start | bytes 196616 | tf_op jit(solution)/shard_map/ppermute | solution.py:322
  37.4 3.1 %collective-permute-start.13 = (f32[64,384]{1,0:T(8,128)S(1)}, f32[64,384]{1,0:T(8,128)S(1)}, u32[]{:S(2)}, u32[]{:S(2)}) collective-permute-start(f32[64,384]{1,0:T(8,128)S(1)} %shard_map.70), channel_id=1, source_target_pairs={{0,1},{1,0},{2,3},{3,2},{4,5},{5,4},{6,7},{7,6},{8,9},{9,8},{10,11... | collective-permute-start | bytes 294920 | tf_op jit(solution)/shard_map/ppermute | solution.py:25
  37.5 4.9 %collective-permute-start.12 = (bf16[384,1536]{1,0:T(8,128)(2,1)}, bf16[384,1536]{1,0:T(8,128)(2,1)S(1)}, u32[]{:S(2)}, u32[]{:S(2)}) collective-permute-start(bf16[384,1536]{1,0:T(8,128)(2,1)} %collective-permute-done.7.refs_0_), channel_id=1, source_target_pairs={{0,1},{1,0},{2,3},{3,2},{4,5},{5,4},{6,7},{7,6},{8,9},{9,8},{10,11... | collective-permute-start | bytes 3538952 | tf_op jit(solution)/shard_map/ppermute | solution.py:25
  40.2 4.3 %collective-permute-start.11 = (bf16[64,512]{1,0:T(8,128)(2,1)S(1)}, bf16[64,512]{1,0:T(8,128)(2,1)S(1)}, u32[]{:S(2)}, u32[]{:S(2)}) collective-permute-start(bf16[64,512]{1,0:T(8,128)(2,1)S(1)} %collective-permute-done.8.refs_7_), channel_id=1, source_target_pairs={{0,16},{16,0},{1,17},{17,1},{2,18},{18,2},{3,19},{19,3},{4,20},{20... | collective-permute-start | bytes 196616 | tf_op jit(solution)/shard_map/ppermute | solution.py:25
  41.2 4.8 %collective-permute-start.15 = (bf16[64,384]{1,0:T(8,128)(2,1)}, bf16[64,384]{1,0:T(8,128)(2,1)}, u32[]{:S(2)}, u32[]{:S(2)}) collective-permute-start(bf16[64,384]{1,0:T(8,128)(2,1)} %get-tuple-element.89), channel_id=1, source_target_pairs={{0,2},{1,3},{2,0},{3,1},{4,6},{5,7},{6,4},{7,5},{8,10},{9,11},{10,... | collective-permute-start | bytes 147464 | tf_op jit(solution)/shard_map/ppermute | solution.py:25
  43.7 2.8 %copy-start.5 = (bf16[1,64,512]{2,1,0:T(8,128)(2,1)S(1)}, bf16[1,64,512]{2,1,0:T(8,128)(2,1)}, u32[]{:S(2)}) copy-start(bf16[1,64,512]{2,1,0:T(8,128)(2,1)} %param.11) | copy-start | bytes 196612
  44.5 1.9 %collective-permute-start.14 = (bf16[384,512]{1,0:T(8,128)(2,1)}, bf16[384,512]{1,0:T(8,128)(2,1)S(1)}, u32[]{:S(2)}, u32[]{:S(2)}) collective-permute-start(bf16[384,512]{1,0:T(8,128)(2,1)} %collective-permute-done.4.refs_0_), channel_id=1, source_target_pairs={{0,1},{1,0},{2,3},{3,2},{4,5},{5,4},{6,7},{7,6},{8,9},{9,8},{10,11... | collective-permute-start | bytes 1179656 | tf_op jit(solution)/shard_map/ppermute | solution.py:25
  (4 other events, 7.0 us)

commit v27 on v25

--- a/solution.py
+++ b/solution.py
@@ -245,7 +245,7 @@
         for flip in range(tensors)
     ]
     uncut, pieces = chained(tokens, pieces)
-    steps = 6
+    steps = 3
     chunks = list(
         call(
             functools.partial(cut_kernel, edges),

time: 48.2 us -> 48.2 us (level)
  no operation moved by 1% of the time
where the time goes in v27:
time: 48.2 us; the launch traced here: 47.8 us
  starting transfers between devices  17.5 us (36%)
  Pallas kernels  16.6 us (34%)
  waiting for transfers between devices  8.18 us (17%)
  local copies, waits for them, and re-layouts  4.79 us (10%)
  other arithmetic  0.63 us (1%)
    ppermute x14, starting transfers between devices, flipped(): return lax.ppermute(value, axis, [(i, i ^ flip) for i in range(count)])  12.8 us
    pallas_call x5, Pallas kernels, products(): call(functools.partial(products_kernel, tile, depth, places), jax.ShapeDt...  7.65 us
    ppermute x14, waiting for transfers between devices, flipped(): return lax.ppermute(value, axis, [(i, i ^ flip) for i in range(count)])  5.63 us
    ppermute x2, starting transfers between devices, fetch_far(): lax.ppermute(value, ('parts', 'adapter'), route)  4.68 us
    unnamed x14, local copies, waits for them, and re-layouts  3.72 us
    ppermute x2, waiting for transfers between devices, fetch_far(): lax.ppermute(value, ('parts', 'adapter'), route)  2.55 us
    pallas_call x1, Pallas kernels, body(): call(functools.partial(shrink_kernel, tile, flips, pairs, slots), jax.Sha...  2.47 us
    pallas_call x1, Pallas kernels, body(): call(functools.partial(cut_kernel, edges), [jax.ShapeDtypeStruct((rows, b...  2.25 us
  transfers between devices with their start and end apart: 16, of which 5 were waited for; matrix products, arithmetic and copies ran while one was open for 1% of the time, Pallas kernels for 30%

profile of v27, /device:TPU:0, one launch (start us, length us, event | category | flops | bytes accessed | tf_op | source)
XLA Modules:
  0.0 47.8 jit_solution(10690885878095299953)
XLA Ops:
  0.0 1.1 %dynamic-slice_bitcast_fusion = (bf16[16,2048]{1,0:T(8,128)(2,1)S(1)}, bf16[16,2048]{1,0:T(8,128)(2,1)S(1)}, bf16[16,2048]{1,0:T(8,128)(2,1)S(1)}, bf16[16,2048]{1,0:T(8,128)(2,1)S(1)}) fusion(bf16[1,8192,16]{1,2,0:T(8,128)(2,1)} %param.10, s32[]{:T(128)S(6)} %select_n.15, s32[]{:T(128)S(6)} %select_n.13, s32[]{:T(128)S(6)} %select_n.12, s32[]{:T(128)S(6)} %select_n.14), kind=kLoop, calls=%fused_computation | loop fusion | bytes 524304 | tf_op jit(solution)/shard_map/dynamic_slice | solution.py:244
  1.6 2.6 %collective-permute-start.1 = (bf16[16,2048]{1,0:T(8,128)(2,1)S(1)}, bf16[16,2048]{1,0:T(8,128)(2,1)S(1)}, u32[]{:S(2)}, u32[]{:S(2)}) collective-permute-start(bf16[16,2048]{1,0:T(8,128)(2,1)S(1)} %get-tuple-element.52), channel_id=1, source_target_pairs={{0,2},{1,3},{2,0},{3,1},{4,6},{5,7},{6,4},{7,5},{8,10},{9,11},{10,... | collective-permute-start | bytes 196616 | tf_op jit(solution)/shard_map/ppermute | solution.py:25
  4.3 2.2 %shard_map.66 = (bf16[384,1536]{1,0:T(8,128)(2,1)}, bf16[384,512]{1,0:T(8,128)(2,1)}) custom-call(bf16[384,2048]{1,0:T(8,128)(2,1)} %tokens_ref.1), custom_call_target="tpu_custom_call" | custom-call | tf_op jit(solution)/shard_map/pallas_call | solution.py:250
  6.5 1.8 %collective-permute-start.7 = (bf16[384,1536]{1,0:T(8,128)(2,1)}, bf16[384,1536]{1,0:T(8,128)(2,1)}, u32[]{:S(2)}, u32[]{:S(2)}) collective-permute-start(bf16[384,1536]{1,0:T(8,128)(2,1)} %get-tuple-element.69), channel_id=1, source_target_pairs={{0,2},{1,3},{2,0},{3,1},{4,6},{5,7},{6,4},{7,5},{8,10},{9,11},{10,... | collective-permute-start | bytes 3538952 | tf_op jit(solution)/shard_map/ppermute | solution.py:25
  9.1 2.7 %collective-permute-start.5 = (bf16[64,2048]{1,0:T(8,128)(2,1)}, bf16[64,2048]{1,0:T(8,128)(2,1)}, u32[]{:S(2)}, u32[]{:S(2)}) collective-permute-start(bf16[64,2048]{1,0:T(8,128)(2,1)} %shard_map.64.refs_0_), channel_id=1, source_target_pairs={{0,8},{4,12},{8,0},{12,4},{16,28},{20,24},{24,20},{28,16},{1,9},{5... | collective-permute-start | bytes 786440 | tf_op jit(solution)/shard_map/ppermute | solution.py:317
  11.8 3.4 %copy-done.1 = bf16[8192,512]{1,0:T(8,128)(2,1)S(1)} copy-done((bf16[8192,512]{1,0:T(8,128)(2,1)S(1)}, bf16[8192,512]{1,0:T(8,128)(2,1)}, u32[]{:S(2)}) %copy-start.1) | copy-done | bytes 8388632
  15.2 1.4 %shard_map.65 = (f32[384,512]{1,0:T(8,128)S(1)}, s32[1,384]{1,0:T(1,128)S(1)}) custom-call(s32[4]{0:T(128)S(1)} %copy-done.4, s32[1,384]{1,0:T(1,128)S(1)} %bitcast.18, bf16[8192,512]{1,0:T(8,128)(2,1)S(1)} %copy-done.1, bf16[384,2048]{1,0:T(8,128)(2,1)S(1)} %copy-done), custom_call_target="tpu_custom_call" | custom-call | flops 99999997952 | tf_op jit(solution)/shard_map/pallas_call | solution.py:328
  16.6 1.6 %collective-permute-start.6 = (bf16[64,512]{1,0:T(8,128)(2,1)}, bf16[64,512]{1,0:T(8,128)(2,1)S(1)}, u32[]{:S(2)}, u32[]{:S(2)}) collective-permute-start(bf16[64,512]{1,0:T(8,128)(2,1)} %bitcast.9.refs_5_), channel_id=1, source_target_pairs={{0,4},{4,0},{8,12},{12,8},{1,5},{5,1},{9,13},{13,9},{2,6},{6,2},{1... | collective-permute-start | bytes 196616 | tf_op jit(solution)/shard_map/ppermute | solution.py:25
  18.6 0.8 %shard_map.67.refs_1_ = f32[384,512]{1,0:T(8,128)S(1)} custom-call(bf16[8192,512]{1,0:T(8,128)(2,1)S(1)} %copy-done.2, bf16[384,2048]{1,0:T(8,128)(2,1)S(1)} %copy-done, f32[384,512]{1,0:T(8,128)S(1)} %get-tuple-element.62.refs_1_), custom_call_target="tpu_custom_call" | custom-call | flops 99999997952 | tf_op jit(solution)/shard_map/pallas_call | solution.py:299
  19.4 1.6 %collective-permute-start.9 = (bf16[64,2048]{1,0:T(8,128)(2,1)}, bf16[64,2048]{1,0:T(8,128)(2,1)S(1)}, u32[]{:S(2)}, u32[]{:S(2)}) collective-permute-start(bf16[64,2048]{1,0:T(8,128)(2,1)} %shard_map.64.refs_0_), channel_id=1, source_target_pairs={{0,4},{4,0},{8,12},{12,8},{1,5},{5,1},{9,13},{13,9},{2,6},{6,2},{1... | collective-permute-start | bytes 786440 | tf_op jit(solution)/shard_map/ppermute | solution.py:25
  21.0 1.2 %collective-permute-start.4 = (bf16[384,512]{1,0:T(8,128)(2,1)}, bf16[384,512]{1,0:T(8,128)(2,1)}, u32[]{:S(2)}, u32[]{:S(2)}) collective-permute-start(bf16[384,512]{1,0:T(8,128)(2,1)} %get-tuple-element.60), channel_id=1, source_target_pairs={{0,2},{1,3},{2,0},{3,1},{4,6},{5,7},{6,4},{7,5},{8,10},{9,11},{10,... | collective-permute-start | bytes 1179656 | tf_op jit(solution)/shard_map/ppermute | solution.py:25
  22.2 2.5 %collective-permute-done.5.refs_2_ = bf16[64,2048]{1,0:T(8,128)(2,1)} collective-permute-done((bf16[64,2048]{1,0:T(8,128)(2,1)}, bf16[64,2048]{1,0:T(8,128)(2,1)}, u32[]{:S(2)}, u32[]{:S(2)}) %collective-permute-start.5) | collective-permute-done | bytes 262176 | tf_op jit(solution)/shard_map/ppermute | solution.py:317
  24.8 1.1 %collective-permute-done.6.refs_6_ = bf16[64,512]{1,0:T(8,128)(2,1)S(1)} collective-permute-done((bf16[64,512]{1,0:T(8,128)(2,1)}, bf16[64,512]{1,0:T(8,128)(2,1)S(1)}, u32[]{:S(2)}, u32[]{:S(2)}) %collective-permute-start.6) | collective-permute-done | bytes 65568 | tf_op jit(solution)/shard_map/ppermute | solution.py:25
  25.9 1.8 %shard_map.68.refs_1_ = f32[384,512]{1,0:T(8,128)S(1)} custom-call(bf16[8192,512]{1,0:T(8,128)(2,1)S(1)} %copy-done.2, bf16[384,2048]{1,0:T(8,128)(2,1)S(1)} %collective-permute-done.3.refs_0_, f32[384,512]{1,0:T(8,128)S(1)} %shard_map.67.refs_1_), custom_call_target="tpu_custom_call" | custom-call | flops 99999997952 | tf_op jit(solution)/shard_map/pallas_call | solution.py:299
  27.8 2.0 %collective-permute-start.8 = (bf16[64,512]{1,0:T(8,128)(2,1)}, bf16[64,512]{1,0:T(8,128)(2,1)S(1)}, u32[]{:S(2)}, u32[]{:S(2)}) collective-permute-start(bf16[64,512]{1,0:T(8,128)(2,1)} %bitcast.9.refs_5_), channel_id=1, source_target_pairs={{0,8},{4,12},{8,0},{12,4},{16,28},{20,24},{24,20},{28,16},{1,9},{5... | collective-permute-start | bytes 196616 | tf_op jit(solution)/shard_map/ppermute | solution.py:317
  29.8 1.8 %collective-permute-done.9.refs_1_ = bf16[64,2048]{1,0:T(8,128)(2,1)S(1)} collective-permute-done((bf16[64,2048]{1,0:T(8,128)(2,1)}, bf16[64,2048]{1,0:T(8,128)(2,1)S(1)}, u32[]{:S(2)}, u32[]{:S(2)}) %collective-permute-start.9) | collective-permute-done | bytes 262176 | tf_op jit(solution)/shard_map/ppermute | solution.py:25
  31.6 2.2 %collective-permute-done.10.refs_3_ = bf16[64,2048]{1,0:T(8,128)(2,1)S(1)} collective-permute-done((bf16[64,2048]{1,0:T(8,128)(2,1)}, bf16[64,2048]{1,0:T(8,128)(2,1)S(1)}, u32[]{:S(2)}, u32[]{:S(2)}) %collective-permute-start.10) | collective-permute-done | bytes 262176 | tf_op jit(solution)/shard_map/ppermute | solution.py:25
  33.8 2.5 %shard_map.69 = f32[64,384]{1,0:T(8,128)S(1)} custom-call(bf16[384,2048]{1,0:T(8,128)(2,1)S(1)} %copy-done, s32[1,384]{1,0:T(1,128)S(1)} %get-tuple-element.70.stored_ref.refs_2_, bf16[64,2048]{1,0:T(8,128)(2,1)} %shard_map.64.refs_0_, bf16[64,2048]{1,0:T(8,128)(2,1)S(1)} %collective-permute-done.9.refs_1_, bf16[64,2048]{1,0:T(8,128)(2,1)} %collective-permute-done.5.refs_2_, ...), custom_call_target="tpu_custom_call" | custom-call | flops 99999997952 | tf_op jit(solution)/shard_map/pallas_call | solution.py:356
  36.9 2.2 %shard_map.70.refs_1_ = f32[384,512]{1,0:T(8,128)S(1)} custom-call(bf16[8192,512]{1,0:T(8,128)(2,1)S(1)} %copy-done.2, bf16[384,1536]{1,0:T(8,128)(2,1)} %collective-permute-done.7.refs_0_, f32[384,512]{1,0:T(8,128)S(1)} %shard_map.68.refs_1_), custom_call_target="tpu_custom_call" | custom-call | flops 99999997952 | tf_op jit(solution)/shard_map/pallas_call | solution.py:299
  39.1 1.2 %collective-permute-start.11 = (bf16[64,512]{1,0:T(8,128)(2,1)S(1)}, bf16[64,512]{1,0:T(8,128)(2,1)S(1)}, u32[]{:S(2)}, u32[]{:S(2)}) collective-permute-start(bf16[64,512]{1,0:T(8,128)(2,1)S(1)} %collective-permute-done.8.refs_7_), channel_id=1, source_target_pairs={{0,16},{16,0},{1,17},{17,1},{2,18},{18,2},{3,19},{19,3},{4,20},{20... | collective-permute-start | bytes 196616 | tf_op jit(solution)/shard_map/ppermute | solution.py:25
  40.9 1.5 %collective-permute-start.15 = (bf16[64,384]{1,0:T(8,128)(2,1)}, bf16[64,384]{1,0:T(8,128)(2,1)}, u32[]{:S(2)}, u32[]{:S(2)}) collective-permute-start(bf16[64,384]{1,0:T(8,128)(2,1)} %get-tuple-element.93), channel_id=1, source_target_pairs={{0,2},{1,3},{2,0},{3,1},{4,6},{5,7},{6,4},{7,5},{8,10},{9,11},{10,... | collective-permute-start | bytes 147464 | tf_op jit(solution)/shard_map/ppermute | solution.py:25
  42.3 1.4 %shard_map.71.refs_1_ = f32[384,512]{1,0:T(8,128)S(1)} custom-call(bf16[8192,512]{1,0:T(8,128)(2,1)S(1)} %copy-done.2, bf16[384,1536]{1,0:T(8,128)(2,1)S(1)} %collective-permute-done.12.refs_0_, f32[384,512]{1,0:T(8,128)S(1)} %shard_map.70.refs_1_), custom_call_target="tpu_custom_call" | custom-call | flops 99999997952 | tf_op jit(solution)/shard_map/pallas_call | solution.py:299
  43.8 1.4 %shard_map.72.refs_1_ = f32[384,512]{1,0:T(8,128)S(1)} custom-call(bf16[8192,512]{1,0:T(8,128)(2,1)S(1)} %copy-done.2, bf16[384,512]{1,0:T(8,128)(2,1)} %collective-permute-done.4.refs_0_, f32[384,512]{1,0:T(8,128)S(1)} %shard_map.71.refs_1_), custom_call_target="tpu_custom_call" | custom-call | flops 99999997952 | tf_op jit(solution)/shard_map/pallas_call | solution.py:299
  45.7 2.1 %shard_map.73 = bf16[384,512]{1,0:T(8,128)(2,1)} custom-call(bf16[8192,512]{1,0:T(8,128)(2,1)S(1)} %copy-done.2, bf16[384,512]{1,0:T(8,128)(2,1)S(1)} %collective-permute-done.14.refs_0_, f32[384,512]{1,0:T(8,128)S(1)} %shard_map.72.refs_1_, s32[1,384]{1,0:T(1,128)S(1)} %copy-done.6, f32[64,384]{1,0:T(8,128)S(1)} %get-tuple-element.87.refs_3_, ...), custom_call_target="tpu_custom_call" | custom-call | flops 99999997952 | tf_op jit(solution)/shard_map/pallas_call | solution.py:390
  (34 shorter events, 3.5 us)
Async XLA Ops:
  0.0 8.3 %copy-start = (bf16[384,2048]{1,0:T(8,128)(2,1)S(1)}, bf16[384,2048]{1,0:T(8,128)(2,1)}, u32[]{:S(2)}) copy-start(bf16[384,2048]{1,0:T(8,128)(2,1)} %tokens_ref.1) | copy-start | bytes 4718596
  0.0 11.8 %copy-start.3 = (s32[384,1]{0,1:T(1,128)S(1)}, s32[384,1]{0,1:T(1,128)}, u32[]{:S(2)}) copy-start(s32[384,1]{0,1:T(1,128)} %param.7) | copy-start | bytes 4612
  0.0 11.8 %copy-start.4 = (s32[4]{0:T(128)S(1)}, s32[4]{0:T(128)}, u32[]{:S(2)}) copy-start(s32[4]{0:T(128)} %placement_ref.1) | copy-start | bytes 52
  1.1 7.2 %collective-permute-start = (bf16[16,2048]{1,0:T(8,128)(2,1)S(1)}, bf16[16,2048]{1,0:T(8,128)(2,1)S(1)}, u32[]{:S(2)}, u32[]{:S(2)}) collective-permute-start(bf16[16,2048]{1,0:T(8,128)(2,1)S(1)} %get-tuple-element.50), channel_id=1, source_target_pairs={{0,1},{1,0},{2,3},{3,2},{4,5},{5,4},{6,7},{7,6},{8,9},{9,8},{10,11... | collective-permute-start | bytes 196616 | tf_op jit(solution)/shard_map/ppermute | solution.py:25
  1.6 6.8 %collective-permute-start.1 = (bf16[16,2048]{1,0:T(8,128)(2,1)S(1)}, bf16[16,2048]{1,0:T(8,128)(2,1)S(1)}, u32[]{:S(2)}, u32[]{:S(2)}) collective-permute-start(bf16[16,2048]{1,0:T(8,128)(2,1)S(1)} %get-tuple-element.52), channel_id=1, source_target_pairs={{0,2},{1,3},{2,0},{3,1},{4,6},{5,7},{6,4},{7,5},{8,10},{9,11},{10,... | collective-permute-start | bytes 196616 | tf_op jit(solution)/shard_map/ppermute | solution.py:25
  4.2 4.2 %collective-permute-start.2 = (bf16[16,2048]{1,0:T(8,128)(2,1)S(1)}, bf16[16,2048]{1,0:T(8,128)(2,1)S(1)}, u32[]{:S(2)}, u32[]{:S(2)}) collective-permute-start(bf16[16,2048]{1,0:T(8,128)(2,1)S(1)} %get-tuple-element.53), channel_id=1, source_target_pairs={{0,3},{1,2},{2,1},{3,0},{4,7},{5,6},{6,5},{7,4},{8,11},{9,10},{10,... | collective-permute-start | bytes 196616 | tf_op jit(solution)/shard_map/ppermute | solution.py:25
  6.5 29.8 %collective-permute-start.7 = (bf16[384,1536]{1,0:T(8,128)(2,1)}, bf16[384,1536]{1,0:T(8,128)(2,1)}, u32[]{:S(2)}, u32[]{:S(2)}) collective-permute-start(bf16[384,1536]{1,0:T(8,128)(2,1)} %get-tuple-element.69), channel_id=1, source_target_pairs={{0,2},{1,3},{2,0},{3,1},{4,6},{5,7},{6,4},{7,5},{8,10},{9,11},{10,... | collective-permute-start | bytes 3538952 | tf_op jit(solution)/shard_map/ppermute | solution.py:25
  8.3 8.3 %collective-permute-start.3 = (bf16[384,2048]{1,0:T(8,128)(2,1)S(1)}, bf16[384,2048]{1,0:T(8,128)(2,1)S(1)}, u32[]{:S(2)}, u32[]{:S(2)}) collective-permute-start(bf16[384,2048]{1,0:T(8,128)(2,1)S(1)} %copy-done), channel_id=1, source_target_pairs={{0,1},{1,0},{2,3},{3,2},{4,5},{5,4},{6,7},{7,6},{8,9},{9,8},{10,11... | collective-permute-start | bytes 4718600 | tf_op jit(solution)/shard_map/ppermute | solution.py:25
  9.1 15.7 %collective-permute-start.5 = (bf16[64,2048]{1,0:T(8,128)(2,1)}, bf16[64,2048]{1,0:T(8,128)(2,1)}, u32[]{:S(2)}, u32[]{:S(2)}) collective-permute-start(bf16[64,2048]{1,0:T(8,128)(2,1)} %shard_map.64.refs_0_), channel_id=1, source_target_pairs={{0,8},{4,12},{8,0},{12,4},{16,28},{20,24},{24,20},{28,16},{1,9},{5... | collective-permute-start | bytes 786440 | tf_op jit(solution)/shard_map/ppermute | solution.py:317
  11.8 3.4 %copy-start.1 = (bf16[8192,512]{1,0:T(8,128)(2,1)S(1)}, bf16[8192,512]{1,0:T(8,128)(2,1)}, u32[]{:S(2)}) copy-start(bf16[8192,512]{1,0:T(8,128)(2,1)} %weight_ref.13) | copy-start | bytes 25165828
  15.2 3.4 %copy-start.2 = (bf16[8192,512]{1,0:T(8,128)(2,1)S(1)}, bf16[8192,512]{1,0:T(8,128)(2,1)}, u32[]{:S(2)}) copy-start(bf16[8192,512]{1,0:T(8,128)(2,1)} %weight_ref.13) | copy-start | bytes 25165828
  16.6 17.2 %copy-start.5 = (s32[1,384]{1,0:T(1,128)}, s32[1,384]{1,0:T(1,128)S(1)}, u32[]{:S(2)}) copy-start(s32[1,384]{1,0:T(1,128)S(1)} %get-tuple-element.70.stored_ref.refs_2_) | copy-start | bytes 4612
  16.6 9.3 %collective-permute-start.6 = (bf16[64,512]{1,0:T(8,128)(2,1)}, bf16[64,512]{1,0:T(8,128)(2,1)S(1)}, u32[]{:S(2)}, u32[]{:S(2)}) collective-permute-start(bf16[64,512]{1,0:T(8,128)(2,1)} %bitcast.9.refs_5_), channel_id=1, source_target_pairs={{0,4},{4,0},{8,12},{12,8},{1,5},{5,1},{9,13},{13,9},{2,6},{6,2},{1... | collective-permute-start | bytes 196616 | tf_op jit(solution)/shard_map/ppermute | solution.py:25
  19.4 12.2 %collective-permute-start.9 = (bf16[64,2048]{1,0:T(8,128)(2,1)}, bf16[64,2048]{1,0:T(8,128)(2,1)S(1)}, u32[]{:S(2)}, u32[]{:S(2)}) collective-permute-start(bf16[64,2048]{1,0:T(8,128)(2,1)} %shard_map.64.refs_0_), channel_id=1, source_target_pairs={{0,4},{4,0},{8,12},{12,8},{1,5},{5,1},{9,13},{13,9},{2,6},{6,2},{1... | collective-permute-start | bytes 786440 | tf_op jit(solution)/shard_map/ppermute | solution.py:25
  21.0 22.7 %collective-permute-start.4 = (bf16[384,512]{1,0:T(8,128)(2,1)}, bf16[384,512]{1,0:T(8,128)(2,1)}, u32[]{:S(2)}, u32[]{:S(2)}) collective-permute-start(bf16[384,512]{1,0:T(8,128)(2,1)} %get-tuple-element.60), channel_id=1, source_target_pairs={{0,2},{1,3},{2,0},{3,1},{4,6},{5,7},{6,4},{7,5},{8,10},{9,11},{10,... | collective-permute-start | bytes 1179656 | tf_op jit(solution)/shard_map/ppermute | solution.py:25
  25.9 7.8 %collective-permute-start.10 = (bf16[64,2048]{1,0:T(8,128)(2,1)}, bf16[64,2048]{1,0:T(8,128)(2,1)S(1)}, u32[]{:S(2)}, u32[]{:S(2)}) collective-permute-start(bf16[64,2048]{1,0:T(8,128)(2,1)} %collective-permute-done.5.refs_2_), channel_id=1, source_target_pairs={{0,16},{16,0},{1,17},{17,1},{2,18},{18,2},{3,19},{19,3},{4,20},{20... | collective-permute-start | bytes 786440 | tf_op jit(solution)/shard_map/ppermute | solution.py:25
  27.8 8.5 %collective-permute-start.8 = (bf16[64,512]{1,0:T(8,128)(2,1)}, bf16[64,512]{1,0:T(8,128)(2,1)S(1)}, u32[]{:S(2)}, u32[]{:S(2)}) collective-permute-start(bf16[64,512]{1,0:T(8,128)(2,1)} %bitcast.9.refs_5_), channel_id=1, source_target_pairs={{0,8},{4,12},{8,0},{12,4},{16,28},{20,24},{24,20},{28,16},{1,9},{5... | collective-permute-start | bytes 196616 | tf_op jit(solution)/shard_map/ppermute | solution.py:317
  36.3 3.9 %collective-permute-start.13 = (f32[64,384]{1,0:T(8,128)S(1)}, f32[64,384]{1,0:T(8,128)S(1)}, u32[]{:S(2)}, u32[]{:S(2)}) collective-permute-start(f32[64,384]{1,0:T(8,128)S(1)} %shard_map.69), channel_id=1, source_target_pairs={{0,1},{1,0},{2,3},{3,2},{4,5},{5,4},{6,7},{7,6},{8,9},{9,8},{10,11... | collective-permute-start | bytes 294920 | tf_op jit(solution)/shard_map/ppermute | solution.py:25
  36.4 6.0 %collective-permute-start.12 = (bf16[384,1536]{1,0:T(8,128)(2,1)}, bf16[384,1536]{1,0:T(8,128)(2,1)S(1)}, u32[]{:S(2)}, u32[]{:S(2)}) collective-permute-start(bf16[384,1536]{1,0:T(8,128)(2,1)} %collective-permute-done.7.refs_0_), channel_id=1, source_target_pairs={{0,1},{1,0},{2,3},{3,2},{4,5},{5,4},{6,7},{7,6},{8,9},{9,8},{10,11... | collective-permute-start | bytes 3538952 | tf_op jit(solution)/shard_map/ppermute | solution.py:25
  39.1 4.7 %collective-permute-start.11 = (bf16[64,512]{1,0:T(8,128)(2,1)S(1)}, bf16[64,512]{1,0:T(8,128)(2,1)S(1)}, u32[]{:S(2)}, u32[]{:S(2)}) collective-permute-start(bf16[64,512]{1,0:T(8,128)(2,1)S(1)} %collective-permute-done.8.refs_7_), channel_id=1, source_target_pairs={{0,16},{16,0},{1,17},{17,1},{2,18},{18,2},{3,19},{19,3},{4,20},{20... | collective-permute-start | bytes 196616 | tf_op jit(solution)/shard_map/ppermute | solution.py:25
  40.9 4.4 %collective-permute-start.15 = (bf16[64,384]{1,0:T(8,128)(2,1)}, bf16[64,384]{1,0:T(8,128)(2,1)}, u32[]{:S(2)}, u32[]{:S(2)}) collective-permute-start(bf16[64,384]{1,0:T(8,128)(2,1)} %get-tuple-element.93), channel_id=1, source_target_pairs={{0,2},{1,3},{2,0},{3,1},{4,6},{5,7},{6,4},{7,5},{8,10},{9,11},{10,... | collective-permute-start | bytes 147464 | tf_op jit(solution)/shard_map/ppermute | solution.py:25
  43.7 2.0 %copy-start.6 = (s32[1,384]{1,0:T(1,128)S(1)}, s32[1,384]{1,0:T(1,128)}, u32[]{:S(2)}) copy-start(s32[1,384]{1,0:T(1,128)} %copy-done.5) | copy-start | bytes 4612
  43.7 2.0 %collective-permute-start.14 = (bf16[384,512]{1,0:T(8,128)(2,1)}, bf16[384,512]{1,0:T(8,128)(2,1)S(1)}, u32[]{:S(2)}, u32[]{:S(2)}) collective-permute-start(bf16[384,512]{1,0:T(8,128)(2,1)} %collective-permute-done.4.refs_0_), channel_id=1, source_target_pairs={{0,1},{1,0},{2,3},{3,2},{4,5},{5,4},{6,7},{7,6},{8,9},{9,8},{10,11... | collective-permute-start | bytes 1179656 | tf_op jit(solution)/shard_map/ppermute | solution.py:25

commit v28 on v24

--- a/solution.py
+++ b/solution.py
@@ -154,13 +154,13 @@
     return owners
 
 
-def last_kernel(tile, depth, places, flips, pairs, slots, weight_ref, *refs):
+def spread_kernel(tile, depth, places, flips, pairs, slots, weight_ref, *refs):
     count = len(places)
     features = refs[:count]
     given, stored_ref, sum_ref, more_ref = refs[count : count + 4]
     ups = refs[count + 4 : count + 4 + slots]
     (
-        out_ref, total_ref, sums_ref, received_ref, stacked_ref, held_ref, rows_ref, sems, small_sems,
+        out_ref, spread_ref, stacked_ref, sums_ref, received_ref, held_ref, rows_ref, sems, small_sems,
     ) = refs[count + 4 + slots :]
     rank = ups[0].shape[0]
     copies = [(sum_ref, sums_ref), (more_ref, received_ref)]
@@ -172,21 +172,33 @@
     for copy in copies:
         copy.start()
     start_tiles(tile, depth, places, features, weight_ref, held_ref, rows_ref, sems)
-    add_tiles(held_ref, rows_ref, sems, total_ref, given)
+    add_tiles(held_ref, rows_ref, sems, out_ref, given)
     for copy in copies:
         copy.wait()
     shrunk = (sums_ref[...] + received_ref[...].astype(jnp.float32)).astype(jnp.bfloat16).astype(jnp.float32)
-    spread = jnp.concatenate(
-        [jnp.where(stored_ref[...] == owner, shrunk, 0.0) for owner in owners_of(flips, pairs)], axis=0
-    )
+    for b, owner in enumerate(owners_of(flips, pairs)):
+        block = jnp.where(stored_ref[...] == owner, shrunk, 0.0)
+        spread_ref[b * rank : (b + 1) * rank] = block.astype(spread_ref.dtype)
+
+
+def last_kernel(depth, places, weight_ref, *refs):
+    count = len(places)
+    features = refs[:count]
+    given, spread_ref, stacked_ref, out_ref, total_ref = refs[count:]
     expanded = lax.dot_general(
-        spread.astype(jnp.bfloat16),
-        stacked_ref[...],
-        (((0,), (0,)), ((), ())),
-        preferred_element_type=jnp.float32,
+        spread_ref[...], stacked_ref[...], (((0,), (0,)), ((), ())), preferred_element_type=jnp.float32
     )
     expanded = expanded.astype(jnp.bfloat16).astype(jnp.float32)
-    out_ref[...] = (total_ref[...] + LOWRANK_SCALE * expanded).astype(out_ref.dtype)
+    total_ref[...] = given[...] + LOWRANK_SCALE * expanded
+    me = lax.axis_index("tensor")
+    for (flip, first, skip, width), part in zip(places, features):
+        start = pl.multiple_of((me ^ flip) * depth + first, LANES)
+        total_ref[...] += jnp.dot(
+            part[:, skip : skip + width],
+            weight_ref[pl.ds(start, width)],
+            preferred_element_type=jnp.float32,
+        )
+    out_ref[...] = total_ref[...].astype(out_ref.dtype)
 
 
 def shrink_kernel(tile, flips, pairs, slots, tokens_ref, stored_ref, *refs):
@@ -378,23 +390,27 @@
     total = products(near_places(0), near, total)
     far[1], ups, total = chained(far[1], ups, total)
     near = across(1)
-    total = products(far_places(1), far[1], total)
-    near, more, total = chained(near, more, total)
-
-    places = near_places(1)
-    return call(
-        functools.partial(last_kernel, tile, depth, places, flips, pairs, slots),
-        jax.ShapeDtypeStruct((rows, columns), jnp.bfloat16),
-        [ANYWHERE] + [ANYWHERE] * len(near) + [VECTOR] * 2 + [ANYWHERE] * (2 + slots),
+    places = far_places(1)
+    total, spread, stacked = call(
+        functools.partial(spread_kernel, tile, depth, places, flips, pairs, slots),
         [
-            pltpu.VMEM((rows, columns), jnp.float32),
-            pltpu.VMEM((rank, rows), jnp.float32),
-            pltpu.VMEM((rank, rows), jnp.bfloat16),
-            pltpu.VMEM((slots * rank, columns), jnp.bfloat16),
-        ]
+            jax.ShapeDtypeStruct((rows, columns), jnp.float32),
+            jax.ShapeDtypeStruct((slots * rank, rows), jnp.bfloat16),
+            jax.ShapeDtypeStruct((slots * rank, columns), jnp.bfloat16),
+        ],
+        [ANYWHERE] * (1 + len(places)) + [VECTOR] * 2 + [ANYWHERE] * (2 + slots),
+        [pltpu.VMEM((rank, rows), jnp.float32), pltpu.VMEM((rank, rows), jnp.bfloat16)]
         + tile_scratch(tile, rows, places, columns)
         + [pltpu.SemaphoreType.DMA((2 + slots,))],
-    )(frozen_projection_weight, *near, total, stored, partial, more, *ups)
+        [VECTOR] * 3,
+    )(frozen_projection_weight, *far[1], total, stored, partial, more, *ups)
+    near, total = chained(near, total)
+    return call(
+        functools.partial(last_kernel, depth, near_places(1)),
+        jax.ShapeDtypeStruct((rows, columns), jnp.bfloat16),
+        [VECTOR] * (len(near) + 4),
+        [pltpu.VMEM((rows, columns), jnp.float32)],
+    )(frozen_projection_weight, *near, total, spread, stacked)
 
 
 def solution(mesh):

time: 48.2 us -> 48 us (level)
  waiting for transfers between devices: 8.16 us -> 8.98 us
  other arithmetic: 0.63 us -> 0.01 us
    pallas_call x5 -> x4, Pallas kernels: 7.65 us -> 6.22 us  [products(): call(functools.partial(products_kernel, tile, depth, places), jax.ShapeDt...]
    pallas_call x1 -> x2, Pallas kernels: 2.1 us -> 3.21 us  [the longest x1 1.96 us: body(): call(functools.partial(spread_kernel, tile, depth, places, flips, pairs,...]
    ppermute x14, waiting for transfers between devices: 5.63 us -> 6.45 us  [flipped(): return lax.ppermute(value, axis, [(i, i ^ flip) for i in range(count)])]
    convert_element_type x1, other arithmetic: 0.63 us -> 0.01 us  [body(): more = flipped(partial.astype(jnp.bfloat16), 'tensor', flip)]
  transfers between devices with their start and end apart: 16 -> 16, of which waited for: 5 -> 7; matrix products, arithmetic and copies ran while one was open for 1% -> 0% of each run, Pallas kernels for 30% -> 31%
where the time goes in v28:
time: 48 us; the launch traced here: 47.7 us
  starting transfers between devices  17.5 us (36%)
  Pallas kernels  16.2 us (34%)
  waiting for transfers between devices  8.98 us (19%)
  local copies, waits for them, and re-layouts  4.79 us (10%)
    ppermute x14, starting transfers between devices, flipped(): return lax.ppermute(value, axis, [(i, i ^ flip) for i in range(count)])  12.8 us
    ppermute x14, waiting for transfers between devices, flipped(): return lax.ppermute(value, axis, [(i, i ^ flip) for i in range(count)])  6.45 us
    pallas_call x4, Pallas kernels, products(): call(functools.partial(products_kernel, tile, depth, places), jax.ShapeDt...  6.22 us
    ppermute x2, starting transfers between devices, fetch_far(): lax.ppermute(value, ('parts', 'adapter'), route)  4.68 us
    unnamed x14, local copies, waits for them, and re-layouts  3.72 us
    ppermute x2, waiting for transfers between devices, fetch_far(): lax.ppermute(value, ('parts', 'adapter'), route)  2.53 us
    pallas_call x1, Pallas kernels, body(): call(functools.partial(shrink_kernel, tile, flips, pairs, slots), jax.Sha...  2.46 us
    pallas_call x1, Pallas kernels, body(): call(functools.partial(cut_kernel, edges), [jax.ShapeDtypeStruct((rows, b...  2.23 us
  transfers between devices with their start and end apart: 16, of which 7 were waited for; matrix products, arithmetic and copies ran while one was open for 0% of the time, Pallas kernels for 31%

profile of v28, /device:TPU:0, one launch (start us, length us, event | category | flops | bytes accessed | tf_op | source)
XLA Modules:
  0.0 47.7 jit_solution(12482231954275213727)
XLA Ops:
  0.0 1.1 %dynamic-slice_bitcast_fusion = (bf16[16,2048]{1,0:T(8,128)(2,1)S(1)}, bf16[16,2048]{1,0:T(8,128)(2,1)S(1)}, bf16[16,2048]{1,0:T(8,128)(2,1)S(1)}, bf16[16,2048]{1,0:T(8,128)(2,1)S(1)}) fusion(bf16[1,8192,16]{1,2,0:T(8,128)(2,1)} %param.10, s32[]{:T(128)S(6)} %select_n.15, s32[]{:T(128)S(6)} %select_n.13, s32[]{:T(128)S(6)} %select_n.12, s32[]{:T(128)S(6)} %select_n.14), kind=kLoop, calls=%fused_computation | loop fusion | bytes 524304 | tf_op jit(solution)/shard_map/dynamic_slice | solution.py:251
  1.6 2.6 %collective-permute-start.1 = (bf16[16,2048]{1,0:T(8,128)(2,1)S(1)}, bf16[16,2048]{1,0:T(8,128)(2,1)S(1)}, u32[]{:S(2)}, u32[]{:S(2)}) collective-permute-start(bf16[16,2048]{1,0:T(8,128)(2,1)S(1)} %get-tuple-element.54), channel_id=1, source_target_pairs={{0,2},{1,3},{2,0},{3,1},{4,6},{5,7},{6,4},{7,5},{8,10},{9,11},{10,... | collective-permute-start | bytes 196616 | tf_op jit(solution)/shard_map/ppermute | solution.py:25
  4.3 2.2 %shard_map.66 = (bf16[384,1536]{1,0:T(8,128)(2,1)}, bf16[384,512]{1,0:T(8,128)(2,1)}) custom-call(bf16[384,2048]{1,0:T(8,128)(2,1)} %tokens_ref.1), custom_call_target="tpu_custom_call" | custom-call | tf_op jit(solution)/shard_map/pallas_call | solution.py:257
  6.5 1.8 %collective-permute-start.7 = (bf16[384,1536]{1,0:T(8,128)(2,1)}, bf16[384,1536]{1,0:T(8,128)(2,1)}, u32[]{:S(2)}, u32[]{:S(2)}) collective-permute-start(bf16[384,1536]{1,0:T(8,128)(2,1)} %get-tuple-element.71), channel_id=1, source_target_pairs={{0,2},{1,3},{2,0},{3,1},{4,6},{5,7},{6,4},{7,5},{8,10},{9,11},{10,... | collective-permute-start | bytes 3538952 | tf_op jit(solution)/shard_map/ppermute | solution.py:25
  9.1 2.7 %collective-permute-start.5 = (bf16[64,2048]{1,0:T(8,128)(2,1)}, bf16[64,2048]{1,0:T(8,128)(2,1)}, u32[]{:S(2)}, u32[]{:S(2)}) collective-permute-start(bf16[64,2048]{1,0:T(8,128)(2,1)} %shard_map.64.refs_0_), channel_id=1, source_target_pairs={{0,8},{4,12},{8,0},{12,4},{16,28},{20,24},{24,20},{28,16},{1,9},{5... | collective-permute-start | bytes 786440 | tf_op jit(solution)/shard_map/ppermute | solution.py:324
  11.8 3.4 %copy-done.1 = bf16[8192,512]{1,0:T(8,128)(2,1)S(1)} copy-done((bf16[8192,512]{1,0:T(8,128)(2,1)S(1)}, bf16[8192,512]{1,0:T(8,128)(2,1)}, u32[]{:S(2)}) %copy-start.1) | copy-done | bytes 8388632
  15.1 1.4 %shard_map.65 = (f32[384,512]{1,0:T(8,128)S(1)}, s32[1,384]{1,0:T(1,128)S(1)}) custom-call(s32[4]{0:T(128)S(1)} %copy-done.4, s32[1,384]{1,0:T(1,128)S(1)} %bitcast.18, bf16[8192,512]{1,0:T(8,128)(2,1)S(1)} %copy-done.1, bf16[384,2048]{1,0:T(8,128)(2,1)S(1)} %copy-done), custom_call_target="tpu_custom_call" | custom-call | flops 99999997952 | tf_op jit(solution)/shard_map/pallas_call | solution.py:335
  16.6 1.6 %collective-permute-start.6 = (bf16[64,512]{1,0:T(8,128)(2,1)}, bf16[64,512]{1,0:T(8,128)(2,1)S(1)}, u32[]{:S(2)}, u32[]{:S(2)}) collective-permute-start(bf16[64,512]{1,0:T(8,128)(2,1)} %bitcast.9.refs_5_), channel_id=1, source_target_pairs={{0,4},{4,0},{8,12},{12,8},{1,5},{5,1},{9,13},{13,9},{2,6},{6,2},{1... | collective-permute-start | bytes 196616 | tf_op jit(solution)/shard_map/ppermute | solution.py:25
  18.5 0.8 %shard_map.67.refs_1_ = f32[384,512]{1,0:T(8,128)S(1)} custom-call(bf16[8192,512]{1,0:T(8,128)(2,1)S(1)} %copy-done.2, bf16[384,2048]{1,0:T(8,128)(2,1)S(1)} %copy-done, f32[384,512]{1,0:T(8,128)S(1)} %get-tuple-element.64.refs_1_), custom_call_target="tpu_custom_call" | custom-call | flops 99999997952 | tf_op jit(solution)/shard_map/pallas_call | solution.py:306
  19.4 1.6 %collective-permute-start.9 = (bf16[64,2048]{1,0:T(8,128)(2,1)}, bf16[64,2048]{1,0:T(8,128)(2,1)S(1)}, u32[]{:S(2)}, u32[]{:S(2)}) collective-permute-start(bf16[64,2048]{1,0:T(8,128)(2,1)} %shard_map.64.refs_0_), channel_id=1, source_target_pairs={{0,4},{4,0},{8,12},{12,8},{1,5},{5,1},{9,13},{13,9},{2,6},{6,2},{1... | collective-permute-start | bytes 786440 | tf_op jit(solution)/shard_map/ppermute | solution.py:25
  21.0 1.2 %collective-permute-start.4 = (bf16[384,512]{1,0:T(8,128)(2,1)}, bf16[384,512]{1,0:T(8,128)(2,1)}, u32[]{:S(2)}, u32[]{:S(2)}) collective-permute-start(bf16[384,512]{1,0:T(8,128)(2,1)} %get-tuple-element.62), channel_id=1, source_target_pairs={{0,2},{1,3},{2,0},{3,1},{4,6},{5,7},{6,4},{7,5},{8,10},{9,11},{10,... | collective-permute-start | bytes 1179656 | tf_op jit(solution)/shard_map/ppermute | solution.py:25
  22.2 2.5 %collective-permute-done.5.refs_2_ = bf16[64,2048]{1,0:T(8,128)(2,1)} collective-permute-done((bf16[64,2048]{1,0:T(8,128)(2,1)}, bf16[64,2048]{1,0:T(8,128)(2,1)}, u32[]{:S(2)}, u32[]{:S(2)}) %collective-permute-start.5) | collective-permute-done | bytes 262176 | tf_op jit(solution)/shard_map/ppermute | solution.py:324
  24.8 1.1 %collective-permute-done.6.refs_6_ = bf16[64,512]{1,0:T(8,128)(2,1)S(1)} collective-permute-done((bf16[64,512]{1,0:T(8,128)(2,1)}, bf16[64,512]{1,0:T(8,128)(2,1)S(1)}, u32[]{:S(2)}, u32[]{:S(2)}) %collective-permute-start.6) | collective-permute-done | bytes 65568 | tf_op jit(solution)/shard_map/ppermute | solution.py:25
  25.9 1.8 %shard_map.68.refs_1_ = f32[384,512]{1,0:T(8,128)S(1)} custom-call(bf16[8192,512]{1,0:T(8,128)(2,1)S(1)} %copy-done.2, bf16[384,2048]{1,0:T(8,128)(2,1)S(1)} %collective-permute-done.3.refs_0_, f32[384,512]{1,0:T(8,128)S(1)} %shard_map.67.refs_1_), custom_call_target="tpu_custom_call" | custom-call | flops 99999997952 | tf_op jit(solution)/shard_map/pallas_call | solution.py:306
  27.7 2.0 %collective-permute-start.8 = (bf16[64,512]{1,0:T(8,128)(2,1)}, bf16[64,512]{1,0:T(8,128)(2,1)S(1)}, u32[]{:S(2)}, u32[]{:S(2)}) collective-permute-start(bf16[64,512]{1,0:T(8,128)(2,1)} %bitcast.9.refs_5_), channel_id=1, source_target_pairs={{0,8},{4,12},{8,0},{12,4},{16,28},{20,24},{24,20},{28,16},{1,9},{5... | collective-permute-start | bytes 196616 | tf_op jit(solution)/shard_map/ppermute | solution.py:324
  29.8 1.8 %collective-permute-done.9.refs_1_ = bf16[64,2048]{1,0:T(8,128)(2,1)S(1)} collective-permute-done((bf16[64,2048]{1,0:T(8,128)(2,1)}, bf16[64,2048]{1,0:T(8,128)(2,1)S(1)}, u32[]{:S(2)}, u32[]{:S(2)}) %collective-permute-start.9) | collective-permute-done | bytes 262176 | tf_op jit(solution)/shard_map/ppermute | solution.py:25
  31.6 2.2 %collective-permute-done.10.refs_3_ = bf16[64,2048]{1,0:T(8,128)(2,1)S(1)} collective-permute-done((bf16[64,2048]{1,0:T(8,128)(2,1)}, bf16[64,2048]{1,0:T(8,128)(2,1)S(1)}, u32[]{:S(2)}, u32[]{:S(2)}) %collective-permute-start.10) | collective-permute-done | bytes 262176 | tf_op jit(solution)/shard_map/ppermute | solution.py:25
  33.8 2.5 %shard_map.69 = f32[64,384]{1,0:T(8,128)S(1)} custom-call(bf16[384,2048]{1,0:T(8,128)(2,1)S(1)} %copy-done, s32[1,384]{1,0:T(1,128)S(1)} %get-tuple-element.72.stored_ref.refs_2_, bf16[64,2048]{1,0:T(8,128)(2,1)} %shard_map.64.refs_0_, bf16[64,2048]{1,0:T(8,128)(2,1)S(1)} %collective-permute-done.9.refs_1_, bf16[64,2048]{1,0:T(8,128)(2,1)} %collective-permute-done.5.refs_2_, ...), custom_call_target="tpu_custom_call" | custom-call | flops 99999997952 | tf_op jit(solution)/shard_map/pallas_call | solution.py:363
  36.8 2.2 %shard_map.70.refs_1_ = f32[384,512]{1,0:T(8,128)S(1)} custom-call(bf16[8192,512]{1,0:T(8,128)(2,1)S(1)} %copy-done.2, bf16[384,1536]{1,0:T(8,128)(2,1)} %collective-permute-done.7.refs_0_, f32[384,512]{1,0:T(8,128)S(1)} %shard_map.68.refs_1_), custom_call_target="tpu_custom_call" | custom-call | flops 99999997952 | tf_op jit(solution)/shard_map/pallas_call | solution.py:306
  39.0 1.2 %collective-permute-start.11 = (bf16[64,512]{1,0:T(8,128)(2,1)S(1)}, bf16[64,512]{1,0:T(8,128)(2,1)S(1)}, u32[]{:S(2)}, u32[]{:S(2)}) collective-permute-start(bf16[64,512]{1,0:T(8,128)(2,1)S(1)} %collective-permute-done.8.refs_7_), channel_id=1, source_target_pairs={{0,16},{16,0},{1,17},{17,1},{2,18},{18,2},{3,19},{19,3},{4,20},{20... | collective-permute-start | bytes 196616 | tf_op jit(solution)/shard_map/ppermute | solution.py:25
  40.2 1.6 %collective-permute-start.15 = (bf16[64,384]{1,0:T(8,128)(2,1)S(1)}, bf16[64,384]{1,0:T(8,128)(2,1)S(1)}, u32[]{:S(2)}, u32[]{:S(2)}) collective-permute-start(bf16[64,384]{1,0:T(8,128)(2,1)S(1)} %get-tuple-element.97), channel_id=1, source_target_pairs={{0,2},{1,3},{2,0},{3,1},{4,6},{5,7},{6,4},{7,5},{8,10},{9,11},{10,... | collective-permute-start | bytes 147464 | tf_op jit(solution)/shard_map/ppermute | solution.py:25
  41.8 1.4 %shard_map.71.refs_1_ = f32[384,512]{1,0:T(8,128)S(1)} custom-call(bf16[8192,512]{1,0:T(8,128)(2,1)S(1)} %copy-done.2, bf16[384,1536]{1,0:T(8,128)(2,1)S(1)} %collective-permute-done.12.refs_0_, f32[384,512]{1,0:T(8,128)S(1)} %shard_map.70.refs_1_), custom_call_target="tpu_custom_call" | custom-call | flops 99999997952 | tf_op jit(solution)/shard_map/pallas_call | solution.py:306
  44.5 2.0 %shard_map.72 = (f32[384,512]{1,0:T(8,128)S(1)}, bf16[256,384]{1,0:T(8,128)(2,1)S(1)}, bf16[256,512]{1,0:T(8,128)(2,1)S(1)}) custom-call(bf16[8192,512]{1,0:T(8,128)(2,1)S(1)} %copy-done.2, bf16[384,512]{1,0:T(8,128)(2,1)} %collective-permute-done.4.refs_0_, f32[384,512]{1,0:T(8,128)S(1)} %shard_map.71.refs_1_, s32[1,384]{1,0:T(1,128)S(1)} %copy-done.6, ...), custom_call_target="tpu_custom_call" | custom-call | flops 99999997952 | tf_op jit(solution)/shard_map/pallas_call | solution.py:394
  46.4 1.2 %shard_map.73 = bf16[384,512]{1,0:T(8,128)(2,1)} custom-call(bf16[8192,512]{1,0:T(8,128)(2,1)S(1)} %copy-done.2, bf16[384,512]{1,0:T(8,128)(2,1)S(1)} %collective-permute-done.14.refs_0_, f32[384,512]{1,0:T(8,128)S(1)} %get-tuple-element.94.refs_1_, bf16[256,384]{1,0:T(8,128)(2,1)S(1)} %get-tuple-element.95.refs_2_, ...), custom_call_target="tpu_custom_call" | custom-call | flops 99999997952 | tf_op jit(solution)/shard_map/pallas_call | solution.py:408
  (34 shorter events, 3.7 us)
Async XLA Ops:
  0.0 8.3 %copy-start = (bf16[384,2048]{1,0:T(8,128)(2,1)S(1)}, bf16[384,2048]{1,0:T(8,128)(2,1)}, u32[]{:S(2)}) copy-start(bf16[384,2048]{1,0:T(8,128)(2,1)} %tokens_ref.1) | copy-start | bytes 4718596
  0.0 11.8 %copy-start.3 = (s32[384,1]{0,1:T(1,128)S(1)}, s32[384,1]{0,1:T(1,128)}, u32[]{:S(2)}) copy-start(s32[384,1]{0,1:T(1,128)} %param.7) | copy-start | bytes 4612
  0.0 11.8 %copy-start.4 = (s32[4]{0:T(128)S(1)}, s32[4]{0:T(128)}, u32[]{:S(2)}) copy-start(s32[4]{0:T(128)} %placement_ref.1) | copy-start | bytes 52
  1.1 7.2 %collective-permute-start = (bf16[16,2048]{1,0:T(8,128)(2,1)S(1)}, bf16[16,2048]{1,0:T(8,128)(2,1)S(1)}, u32[]{:S(2)}, u32[]{:S(2)}) collective-permute-start(bf16[16,2048]{1,0:T(8,128)(2,1)S(1)} %get-tuple-element.52), channel_id=1, source_target_pairs={{0,1},{1,0},{2,3},{3,2},{4,5},{5,4},{6,7},{7,6},{8,9},{9,8},{10,11... | collective-permute-start | bytes 196616 | tf_op jit(solution)/shard_map/ppermute | solution.py:25
  1.6 6.7 %collective-permute-start.1 = (bf16[16,2048]{1,0:T(8,128)(2,1)S(1)}, bf16[16,2048]{1,0:T(8,128)(2,1)S(1)}, u32[]{:S(2)}, u32[]{:S(2)}) collective-permute-start(bf16[16,2048]{1,0:T(8,128)(2,1)S(1)} %get-tuple-element.54), channel_id=1, source_target_pairs={{0,2},{1,3},{2,0},{3,1},{4,6},{5,7},{6,4},{7,5},{8,10},{9,11},{10,... | collective-permute-start | bytes 196616 | tf_op jit(solution)/shard_map/ppermute | solution.py:25
  4.2 4.2 %collective-permute-start.2 = (bf16[16,2048]{1,0:T(8,128)(2,1)S(1)}, bf16[16,2048]{1,0:T(8,128)(2,1)S(1)}, u32[]{:S(2)}, u32[]{:S(2)}) collective-permute-start(bf16[16,2048]{1,0:T(8,128)(2,1)S(1)} %get-tuple-element.55), channel_id=1, source_target_pairs={{0,3},{1,2},{2,1},{3,0},{4,7},{5,6},{6,5},{7,4},{8,11},{9,10},{10,... | collective-permute-start | bytes 196616 | tf_op jit(solution)/shard_map/ppermute | solution.py:25
  6.5 29.7 %collective-permute-start.7 = (bf16[384,1536]{1,0:T(8,128)(2,1)}, bf16[384,1536]{1,0:T(8,128)(2,1)}, u32[]{:S(2)}, u32[]{:S(2)}) collective-permute-start(bf16[384,1536]{1,0:T(8,128)(2,1)} %get-tuple-element.71), channel_id=1, source_target_pairs={{0,2},{1,3},{2,0},{3,1},{4,6},{5,7},{6,4},{7,5},{8,10},{9,11},{10,... | collective-permute-start | bytes 3538952 | tf_op jit(solution)/shard_map/ppermute | solution.py:25
  8.3 8.3 %collective-permute-start.3 = (bf16[384,2048]{1,0:T(8,128)(2,1)S(1)}, bf16[384,2048]{1,0:T(8,128)(2,1)S(1)}, u32[]{:S(2)}, u32[]{:S(2)}) collective-permute-start(bf16[384,2048]{1,0:T(8,128)(2,1)S(1)} %copy-done), channel_id=1, source_target_pairs={{0,1},{1,0},{2,3},{3,2},{4,5},{5,4},{6,7},{7,6},{8,9},{9,8},{10,11... | collective-permute-start | bytes 4718600 | tf_op jit(solution)/shard_map/ppermute | solution.py:25
  9.1 15.7 %collective-permute-start.5 = (bf16[64,2048]{1,0:T(8,128)(2,1)}, bf16[64,2048]{1,0:T(8,128)(2,1)}, u32[]{:S(2)}, u32[]{:S(2)}) collective-permute-start(bf16[64,2048]{1,0:T(8,128)(2,1)} %shard_map.64.refs_0_), channel_id=1, source_target_pairs={{0,8},{4,12},{8,0},{12,4},{16,28},{20,24},{24,20},{28,16},{1,9},{5... | collective-permute-start | bytes 786440 | tf_op jit(solution)/shard_map/ppermute | solution.py:324
  11.8 3.4 %copy-start.1 = (bf16[8192,512]{1,0:T(8,128)(2,1)S(1)}, bf16[8192,512]{1,0:T(8,128)(2,1)}, u32[]{:S(2)}) copy-start(bf16[8192,512]{1,0:T(8,128)(2,1)} %weight_ref.13) | copy-start | bytes 25165828
  15.1 3.4 %copy-start.2 = (bf16[8192,512]{1,0:T(8,128)(2,1)S(1)}, bf16[8192,512]{1,0:T(8,128)(2,1)}, u32[]{:S(2)}) copy-start(bf16[8192,512]{1,0:T(8,128)(2,1)} %weight_ref.13) | copy-start | bytes 25165828
  16.6 17.2 %copy-start.5 = (s32[1,384]{1,0:T(1,128)}, s32[1,384]{1,0:T(1,128)S(1)}, u32[]{:S(2)}) copy-start(s32[1,384]{1,0:T(1,128)S(1)} %get-tuple-element.72.stored_ref.refs_2_) | copy-start | bytes 4612
  16.6 9.3 %collective-permute-start.6 = (bf16[64,512]{1,0:T(8,128)(2,1)}, bf16[64,512]{1,0:T(8,128)(2,1)S(1)}, u32[]{:S(2)}, u32[]{:S(2)}) collective-permute-start(bf16[64,512]{1,0:T(8,128)(2,1)} %bitcast.9.refs_5_), channel_id=1, source_target_pairs={{0,4},{4,0},{8,12},{12,8},{1,5},{5,1},{9,13},{13,9},{2,6},{6,2},{1... | collective-permute-start | bytes 196616 | tf_op jit(solution)/shard_map/ppermute | solution.py:25
  19.4 12.2 %collective-permute-start.9 = (bf16[64,2048]{1,0:T(8,128)(2,1)}, bf16[64,2048]{1,0:T(8,128)(2,1)S(1)}, u32[]{:S(2)}, u32[]{:S(2)}) collective-permute-start(bf16[64,2048]{1,0:T(8,128)(2,1)} %shard_map.64.refs_0_), channel_id=1, source_target_pairs={{0,4},{4,0},{8,12},{12,8},{1,5},{5,1},{9,13},{13,9},{2,6},{6,2},{1... | collective-permute-start | bytes 786440 | tf_op jit(solution)/shard_map/ppermute | solution.py:25
  21.0 23.0 %collective-permute-start.4 = (bf16[384,512]{1,0:T(8,128)(2,1)}, bf16[384,512]{1,0:T(8,128)(2,1)}, u32[]{:S(2)}, u32[]{:S(2)}) collective-permute-start(bf16[384,512]{1,0:T(8,128)(2,1)} %get-tuple-element.62), channel_id=1, source_target_pairs={{0,2},{1,3},{2,0},{3,1},{4,6},{5,7},{6,4},{7,5},{8,10},{9,11},{10,... | collective-permute-start | bytes 1179656 | tf_op jit(solution)/shard_map/ppermute | solution.py:25
  25.9 7.9 %collective-permute-start.10 = (bf16[64,2048]{1,0:T(8,128)(2,1)}, bf16[64,2048]{1,0:T(8,128)(2,1)S(1)}, u32[]{:S(2)}, u32[]{:S(2)}) collective-permute-start(bf16[64,2048]{1,0:T(8,128)(2,1)} %collective-permute-done.5.refs_2_), channel_id=1, source_target_pairs={{0,16},{16,0},{1,17},{17,1},{2,18},{18,2},{3,19},{19,3},{4,20},{20... | collective-permute-start | bytes 786440 | tf_op jit(solution)/shard_map/ppermute | solution.py:25
  27.7 8.5 %collective-permute-start.8 = (bf16[64,512]{1,0:T(8,128)(2,1)}, bf16[64,512]{1,0:T(8,128)(2,1)S(1)}, u32[]{:S(2)}, u32[]{:S(2)}) collective-permute-start(bf16[64,512]{1,0:T(8,128)(2,1)} %bitcast.9.refs_5_), channel_id=1, source_target_pairs={{0,8},{4,12},{8,0},{12,4},{16,28},{20,24},{24,20},{28,16},{1,9},{5... | collective-permute-start | bytes 196616 | tf_op jit(solution)/shard_map/ppermute | solution.py:324
  36.3 3.9 %collective-permute-start.13 = (f32[64,384]{1,0:T(8,128)S(1)}, f32[64,384]{1,0:T(8,128)S(1)}, u32[]{:S(2)}, u32[]{:S(2)}) collective-permute-start(f32[64,384]{1,0:T(8,128)S(1)} %shard_map.69), channel_id=1, source_target_pairs={{0,1},{1,0},{2,3},{3,2},{4,5},{5,4},{6,7},{7,6},{8,9},{9,8},{10,11... | collective-permute-start | bytes 294920 | tf_op jit(solution)/shard_map/ppermute | solution.py:25
  36.3 5.5 %collective-permute-start.12 = (bf16[384,1536]{1,0:T(8,128)(2,1)}, bf16[384,1536]{1,0:T(8,128)(2,1)S(1)}, u32[]{:S(2)}, u32[]{:S(2)}) collective-permute-start(bf16[384,1536]{1,0:T(8,128)(2,1)} %collective-permute-done.7.refs_0_), channel_id=1, source_target_pairs={{0,1},{1,0},{2,3},{3,2},{4,5},{5,4},{6,7},{7,6},{8,9},{9,8},{10,11... | collective-permute-start | bytes 3538952 | tf_op jit(solution)/shard_map/ppermute | solution.py:25
  39.0 4.3 %collective-permute-start.11 = (bf16[64,512]{1,0:T(8,128)(2,1)S(1)}, bf16[64,512]{1,0:T(8,128)(2,1)S(1)}, u32[]{:S(2)}, u32[]{:S(2)}) collective-permute-start(bf16[64,512]{1,0:T(8,128)(2,1)S(1)} %collective-permute-done.8.refs_7_), channel_id=1, source_target_pairs={{0,16},{16,0},{1,17},{17,1},{2,18},{18,2},{3,19},{19,3},{4,20},{20... | collective-permute-start | bytes 196616 | tf_op jit(solution)/shard_map/ppermute | solution.py:25
  40.2 4.2 %copy-start.6 = (s32[1,384]{1,0:T(1,128)S(1)}, s32[1,384]{1,0:T(1,128)}, u32[]{:S(2)}) copy-start(s32[1,384]{1,0:T(1,128)} %copy-done.5) | copy-start | bytes 4612
  40.2 4.2 %collective-permute-start.15 = (bf16[64,384]{1,0:T(8,128)(2,1)S(1)}, bf16[64,384]{1,0:T(8,128)(2,1)S(1)}, u32[]{:S(2)}, u32[]{:S(2)}) collective-permute-start(bf16[64,384]{1,0:T(8,128)(2,1)S(1)} %get-tuple-element.97), channel_id=1, source_target_pairs={{0,2},{1,3},{2,0},{3,1},{4,6},{5,7},{6,4},{7,5},{8,10},{9,11},{10,... | collective-permute-start | bytes 147464 | tf_op jit(solution)/shard_map/ppermute | solution.py:25
  44.0 2.4 %collective-permute-start.14 = (bf16[384,512]{1,0:T(8,128)(2,1)}, bf16[384,512]{1,0:T(8,128)(2,1)S(1)}, u32[]{:S(2)}, u32[]{:S(2)}) collective-permute-start(bf16[384,512]{1,0:T(8,128)(2,1)} %collective-permute-done.4.refs_0_), channel_id=1, source_target_pairs={{0,1},{1,0},{2,3},{3,2},{4,5},{5,4},{6,7},{7,6},{8,9},{9,8},{10,11... | collective-permute-start | bytes 1179656 | tf_op jit(solution)/shard_map/ppermute | solution.py:25

commit v29 on v28

--- a/solution.py
+++ b/solution.py
@@ -169,16 +169,18 @@
         pltpu.make_async_copy(source, target, small_sems.at[i])
         for i, (source, target) in enumerate(copies)
     ]
+    start_tiles(tile, depth, places, features, weight_ref, held_ref, rows_ref, sems)
     for copy in copies:
         copy.start()
-    start_tiles(tile, depth, places, features, weight_ref, held_ref, rows_ref, sems)
     add_tiles(held_ref, rows_ref, sems, out_ref, given)
-    for copy in copies:
+    for copy in copies[:2]:
         copy.wait()
     shrunk = (sums_ref[...] + received_ref[...].astype(jnp.float32)).astype(jnp.bfloat16).astype(jnp.float32)
     for b, owner in enumerate(owners_of(flips, pairs)):
         block = jnp.where(stored_ref[...] == owner, shrunk, 0.0)
         spread_ref[b * rank : (b + 1) * rank] = block.astype(spread_ref.dtype)
+    for copy in copies[2:]:
+        copy.wait()
 
 
 def last_kernel(depth, places, weight_ref, *refs):

time: 48 us -> 47.6 us (level)
  no operation moved by 1% of the time
where the time goes in v29:
time: 47.6 us; the launch traced here: 47.2 us
  starting transfers between devices  17.5 us (37%)
  Pallas kernels  15.8 us (33%)
  waiting for transfers between devices  8.98 us (19%)
  local copies, waits for them, and re-layouts  4.79 us (10%)
    ppermute x14, starting transfers between devices, flipped(): return lax.ppermute(value, axis, [(i, i ^ flip) for i in range(count)])  12.8 us
    ppermute x14, waiting for transfers between devices, flipped(): return lax.ppermute(value, axis, [(i, i ^ flip) for i in range(count)])  6.45 us
    pallas_call x4, Pallas kernels, products(): call(functools.partial(products_kernel, tile, depth, places), jax.ShapeDt...  6.22 us
    ppermute x2, starting transfers between devices, fetch_far(): lax.ppermute(value, ('parts', 'adapter'), route)  4.68 us
    unnamed x14, local copies, waits for them, and re-layouts  3.72 us
    ppermute x2, waiting for transfers between devices, fetch_far(): lax.ppermute(value, ('parts', 'adapter'), route)  2.53 us
    pallas_call x1, Pallas kernels, body(): call(functools.partial(shrink_kernel, tile, flips, pairs, slots), jax.Sha...  2.46 us
    pallas_call x1, Pallas kernels, body(): call(functools.partial(cut_kernel, edges), [jax.ShapeDtypeStruct((rows, b...  2.23 us
  transfers between devices with their start and end apart: 16, of which 7 were waited for; matrix products, arithmetic and copies ran while one was open for 0% of the time, Pallas kernels for 31%

profile of v29, /device:TPU:0, one launch (start us, length us, event | category | flops | bytes accessed | tf_op | source)
XLA Modules:
  0.0 47.2 jit_solution(6926975038750305470)
XLA Ops:
  0.0 1.1 %dynamic-slice_bitcast_fusion = (bf16[16,2048]{1,0:T(8,128)(2,1)S(1)}, bf16[16,2048]{1,0:T(8,128)(2,1)S(1)}, bf16[16,2048]{1,0:T(8,128)(2,1)S(1)}, bf16[16,2048]{1,0:T(8,128)(2,1)S(1)}) fusion(bf16[1,8192,16]{1,2,0:T(8,128)(2,1)} %param.10, s32[]{:T(128)S(6)} %select_n.15, s32[]{:T(128)S(6)} %select_n.13, s32[]{:T(128)S(6)} %select_n.12, s32[]{:T(128)S(6)} %select_n.14), kind=kLoop, calls=%fused_computation | loop fusion | bytes 524304 | tf_op jit(solution)/shard_map/dynamic_slice | solution.py:253
  1.6 2.6 %collective-permute-start.1 = (bf16[16,2048]{1,0:T(8,128)(2,1)S(1)}, bf16[16,2048]{1,0:T(8,128)(2,1)S(1)}, u32[]{:S(2)}, u32[]{:S(2)}) collective-permute-start(bf16[16,2048]{1,0:T(8,128)(2,1)S(1)} %get-tuple-element.54), channel_id=1, source_target_pairs={{0,2},{1,3},{2,0},{3,1},{4,6},{5,7},{6,4},{7,5},{8,10},{9,11},{10,... | collective-permute-start | bytes 196616 | tf_op jit(solution)/shard_map/ppermute | solution.py:25
  4.3 2.2 %shard_map.66 = (bf16[384,1536]{1,0:T(8,128)(2,1)}, bf16[384,512]{1,0:T(8,128)(2,1)}) custom-call(bf16[384,2048]{1,0:T(8,128)(2,1)} %tokens_ref.1), custom_call_target="tpu_custom_call" | custom-call | tf_op jit(solution)/shard_map/pallas_call | solution.py:259
  6.5 1.8 %collective-permute-start.7 = (bf16[384,1536]{1,0:T(8,128)(2,1)}, bf16[384,1536]{1,0:T(8,128)(2,1)}, u32[]{:S(2)}, u32[]{:S(2)}) collective-permute-start(bf16[384,1536]{1,0:T(8,128)(2,1)} %get-tuple-element.71), channel_id=1, source_target_pairs={{0,2},{1,3},{2,0},{3,1},{4,6},{5,7},{6,4},{7,5},{8,10},{9,11},{10,... | collective-permute-start | bytes 3538952 | tf_op jit(solution)/shard_map/ppermute | solution.py:25
  9.1 2.7 %collective-permute-start.5 = (bf16[64,2048]{1,0:T(8,128)(2,1)}, bf16[64,2048]{1,0:T(8,128)(2,1)}, u32[]{:S(2)}, u32[]{:S(2)}) collective-permute-start(bf16[64,2048]{1,0:T(8,128)(2,1)} %shard_map.64.refs_0_), channel_id=1, source_target_pairs={{0,8},{4,12},{8,0},{12,4},{16,28},{20,24},{24,20},{28,16},{1,9},{5... | collective-permute-start | bytes 786440 | tf_op jit(solution)/shard_map/ppermute | solution.py:326
  11.8 3.4 %copy-done.1 = bf16[8192,512]{1,0:T(8,128)(2,1)S(1)} copy-done((bf16[8192,512]{1,0:T(8,128)(2,1)S(1)}, bf16[8192,512]{1,0:T(8,128)(2,1)}, u32[]{:S(2)}) %copy-start.1) | copy-done | bytes 8388632
  15.1 1.4 %shard_map.65 = (f32[384,512]{1,0:T(8,128)S(1)}, s32[1,384]{1,0:T(1,128)S(1)}) custom-call(s32[4]{0:T(128)S(1)} %copy-done.4, s32[1,384]{1,0:T(1,128)S(1)} %bitcast.18, bf16[8192,512]{1,0:T(8,128)(2,1)S(1)} %copy-done.1, bf16[384,2048]{1,0:T(8,128)(2,1)S(1)} %copy-done), custom_call_target="tpu_custom_call" | custom-call | flops 99999997952 | tf_op jit(solution)/shard_map/pallas_call | solution.py:337
  16.6 1.6 %collective-permute-start.6 = (bf16[64,512]{1,0:T(8,128)(2,1)}, bf16[64,512]{1,0:T(8,128)(2,1)S(1)}, u32[]{:S(2)}, u32[]{:S(2)}) collective-permute-start(bf16[64,512]{1,0:T(8,128)(2,1)} %bitcast.9.refs_5_), channel_id=1, source_target_pairs={{0,4},{4,0},{8,12},{12,8},{1,5},{5,1},{9,13},{13,9},{2,6},{6,2},{1... | collective-permute-start | bytes 196616 | tf_op jit(solution)/shard_map/ppermute | solution.py:25
  18.5 0.8 %shard_map.67.refs_1_ = f32[384,512]{1,0:T(8,128)S(1)} custom-call(bf16[8192,512]{1,0:T(8,128)(2,1)S(1)} %copy-done.2, bf16[384,2048]{1,0:T(8,128)(2,1)S(1)} %copy-done, f32[384,512]{1,0:T(8,128)S(1)} %get-tuple-element.64.refs_1_), custom_call_target="tpu_custom_call" | custom-call | flops 99999997952 | tf_op jit(solution)/shard_map/pallas_call | solution.py:308
  19.4 1.6 %collective-permute-start.9 = (bf16[64,2048]{1,0:T(8,128)(2,1)}, bf16[64,2048]{1,0:T(8,128)(2,1)S(1)}, u32[]{:S(2)}, u32[]{:S(2)}) collective-permute-start(bf16[64,2048]{1,0:T(8,128)(2,1)} %shard_map.64.refs_0_), channel_id=1, source_target_pairs={{0,4},{4,0},{8,12},{12,8},{1,5},{5,1},{9,13},{13,9},{2,6},{6,2},{1... | collective-permute-start | bytes 786440 | tf_op jit(solution)/shard_map/ppermute | solution.py:25
  21.0 1.2 %collective-permute-start.4 = (bf16[384,512]{1,0:T(8,128)(2,1)}, bf16[384,512]{1,0:T(8,128)(2,1)}, u32[]{:S(2)}, u32[]{:S(2)}) collective-permute-start(bf16[384,512]{1,0:T(8,128)(2,1)} %get-tuple-element.62), channel_id=1, source_target_pairs={{0,2},{1,3},{2,0},{3,1},{4,6},{5,7},{6,4},{7,5},{8,10},{9,11},{10,... | collective-permute-start | bytes 1179656 | tf_op jit(solution)/shard_map/ppermute | solution.py:25
  22.2 2.5 %collective-permute-done.5.refs_2_ = bf16[64,2048]{1,0:T(8,128)(2,1)} collective-permute-done((bf16[64,2048]{1,0:T(8,128)(2,1)}, bf16[64,2048]{1,0:T(8,128)(2,1)}, u32[]{:S(2)}, u32[]{:S(2)}) %collective-permute-start.5) | collective-permute-done | bytes 262176 | tf_op jit(solution)/shard_map/ppermute | solution.py:326
  24.8 1.1 %collective-permute-done.6.refs_6_ = bf16[64,512]{1,0:T(8,128)(2,1)S(1)} collective-permute-done((bf16[64,512]{1,0:T(8,128)(2,1)}, bf16[64,512]{1,0:T(8,128)(2,1)S(1)}, u32[]{:S(2)}, u32[]{:S(2)}) %collective-permute-start.6) | collective-permute-done | bytes 65568 | tf_op jit(solution)/shard_map/ppermute | solution.py:25
  25.9 1.8 %shard_map.68.refs_1_ = f32[384,512]{1,0:T(8,128)S(1)} custom-call(bf16[8192,512]{1,0:T(8,128)(2,1)S(1)} %copy-done.2, bf16[384,2048]{1,0:T(8,128)(2,1)S(1)} %collective-permute-done.3.refs_0_, f32[384,512]{1,0:T(8,128)S(1)} %shard_map.67.refs_1_), custom_call_target="tpu_custom_call" | custom-call | flops 99999997952 | tf_op jit(solution)/shard_map/pallas_call | solution.py:308
  27.7 2.0 %collective-permute-start.8 = (bf16[64,512]{1,0:T(8,128)(2,1)}, bf16[64,512]{1,0:T(8,128)(2,1)S(1)}, u32[]{:S(2)}, u32[]{:S(2)}) collective-permute-start(bf16[64,512]{1,0:T(8,128)(2,1)} %bitcast.9.refs_5_), channel_id=1, source_target_pairs={{0,8},{4,12},{8,0},{12,4},{16,28},{20,24},{24,20},{28,16},{1,9},{5... | collective-permute-start | bytes 196616 | tf_op jit(solution)/shard_map/ppermute | solution.py:326
  29.8 1.8 %collective-permute-done.9.refs_1_ = bf16[64,2048]{1,0:T(8,128)(2,1)S(1)} collective-permute-done((bf16[64,2048]{1,0:T(8,128)(2,1)}, bf16[64,2048]{1,0:T(8,128)(2,1)S(1)}, u32[]{:S(2)}, u32[]{:S(2)}) %collective-permute-start.9) | collective-permute-done | bytes 262176 | tf_op jit(solution)/shard_map/ppermute | solution.py:25
  31.6 2.2 %collective-permute-done.10.refs_3_ = bf16[64,2048]{1,0:T(8,128)(2,1)S(1)} collective-permute-done((bf16[64,2048]{1,0:T(8,128)(2,1)}, bf16[64,2048]{1,0:T(8,128)(2,1)S(1)}, u32[]{:S(2)}, u32[]{:S(2)}) %collective-permute-start.10) | collective-permute-done | bytes 262176 | tf_op jit(solution)/shard_map/ppermute | solution.py:25
  33.8 2.5 %shard_map.69 = f32[64,384]{1,0:T(8,128)S(1)} custom-call(bf16[384,2048]{1,0:T(8,128)(2,1)S(1)} %copy-done, s32[1,384]{1,0:T(1,128)S(1)} %get-tuple-element.72.stored_ref.refs_2_, bf16[64,2048]{1,0:T(8,128)(2,1)} %shard_map.64.refs_0_, bf16[64,2048]{1,0:T(8,128)(2,1)S(1)} %collective-permute-done.9.refs_1_, bf16[64,2048]{1,0:T(8,128)(2,1)} %collective-permute-done.5.refs_2_, ...), custom_call_target="tpu_custom_call" | custom-call | flops 99999997952 | tf_op jit(solution)/shard_map/pallas_call | solution.py:365
  36.8 2.2 %shard_map.70.refs_1_ = f32[384,512]{1,0:T(8,128)S(1)} custom-call(bf16[8192,512]{1,0:T(8,128)(2,1)S(1)} %copy-done.2, bf16[384,1536]{1,0:T(8,128)(2,1)} %collective-permute-done.7.refs_0_, f32[384,512]{1,0:T(8,128)S(1)} %shard_map.68.refs_1_), custom_call_target="tpu_custom_call" | custom-call | flops 99999997952 | tf_op jit(solution)/shard_map/pallas_call | solution.py:308
  39.0 1.2 %collective-permute-start.11 = (bf16[64,512]{1,0:T(8,128)(2,1)S(1)}, bf16[64,512]{1,0:T(8,128)(2,1)S(1)}, u32[]{:S(2)}, u32[]{:S(2)}) collective-permute-start(bf16[64,512]{1,0:T(8,128)(2,1)S(1)} %collective-permute-done.8.refs_7_), channel_id=1, source_target_pairs={{0,16},{16,0},{1,17},{17,1},{2,18},{18,2},{3,19},{19,3},{4,20},{20... | collective-permute-start | bytes 196616 | tf_op jit(solution)/shard_map/ppermute | solution.py:25
  40.2 1.6 %collective-permute-start.15 = (bf16[64,384]{1,0:T(8,128)(2,1)S(1)}, bf16[64,384]{1,0:T(8,128)(2,1)S(1)}, u32[]{:S(2)}, u32[]{:S(2)}) collective-permute-start(bf16[64,384]{1,0:T(8,128)(2,1)S(1)} %get-tuple-element.97), channel_id=1, source_target_pairs={{0,2},{1,3},{2,0},{3,1},{4,6},{5,7},{6,4},{7,5},{8,10},{9,11},{10,... | collective-permute-start | bytes 147464 | tf_op jit(solution)/shard_map/ppermute | solution.py:25
  41.8 1.4 %shard_map.71.refs_1_ = f32[384,512]{1,0:T(8,128)S(1)} custom-call(bf16[8192,512]{1,0:T(8,128)(2,1)S(1)} %copy-done.2, bf16[384,1536]{1,0:T(8,128)(2,1)S(1)} %collective-permute-done.12.refs_0_, f32[384,512]{1,0:T(8,128)S(1)} %shard_map.70.refs_1_), custom_call_target="tpu_custom_call" | custom-call | flops 99999997952 | tf_op jit(solution)/shard_map/pallas_call | solution.py:308
  44.5 1.5 %shard_map.72 = (f32[384,512]{1,0:T(8,128)S(1)}, bf16[256,384]{1,0:T(8,128)(2,1)S(1)}, bf16[256,512]{1,0:T(8,128)(2,1)S(1)}) custom-call(bf16[8192,512]{1,0:T(8,128)(2,1)S(1)} %copy-done.2, bf16[384,512]{1,0:T(8,128)(2,1)} %collective-permute-done.4.refs_0_, f32[384,512]{1,0:T(8,128)S(1)} %shard_map.71.refs_1_, s32[1,384]{1,0:T(1,128)S(1)} %copy-done.6, ...), custom_call_target="tpu_custom_call" | custom-call | flops 99999997952 | tf_op jit(solution)/shard_map/pallas_call | solution.py:396
  46.0 1.2 %shard_map.73 = bf16[384,512]{1,0:T(8,128)(2,1)} custom-call(bf16[8192,512]{1,0:T(8,128)(2,1)S(1)} %copy-done.2, bf16[384,512]{1,0:T(8,128)(2,1)S(1)} %collective-permute-done.14.refs_0_, f32[384,512]{1,0:T(8,128)S(1)} %get-tuple-element.94.refs_1_, bf16[256,384]{1,0:T(8,128)(2,1)S(1)} %get-tuple-element.95.refs_2_, ...), custom_call_target="tpu_custom_call" | custom-call | flops 99999997952 | tf_op jit(solution)/shard_map/pallas_call | solution.py:410
  (34 shorter events, 3.7 us)
Async XLA Ops:
  0.0 8.3 %copy-start = (bf16[384,2048]{1,0:T(8,128)(2,1)S(1)}, bf16[384,2048]{1,0:T(8,128)(2,1)}, u32[]{:S(2)}) copy-start(bf16[384,2048]{1,0:T(8,128)(2,1)} %tokens_ref.1) | copy-start | bytes 4718596
  0.0 11.8 %copy-start.3 = (s32[384,1]{0,1:T(1,128)S(1)}, s32[384,1]{0,1:T(1,128)}, u32[]{:S(2)}) copy-start(s32[384,1]{0,1:T(1,128)} %param.7) | copy-start | bytes 4612
  0.0 11.8 %copy-start.4 = (s32[4]{0:T(128)S(1)}, s32[4]{0:T(128)}, u32[]{:S(2)}) copy-start(s32[4]{0:T(128)} %placement_ref.1) | copy-start | bytes 52
  1.1 7.2 %collective-permute-start = (bf16[16,2048]{1,0:T(8,128)(2,1)S(1)}, bf16[16,2048]{1,0:T(8,128)(2,1)S(1)}, u32[]{:S(2)}, u32[]{:S(2)}) collective-permute-start(bf16[16,2048]{1,0:T(8,128)(2,1)S(1)} %get-tuple-element.52), channel_id=1, source_target_pairs={{0,1},{1,0},{2,3},{3,2},{4,5},{5,4},{6,7},{7,6},{8,9},{9,8},{10,11... | collective-permute-start | bytes 196616 | tf_op jit(solution)/shard_map/ppermute | solution.py:25
  1.6 6.7 %collective-permute-start.1 = (bf16[16,2048]{1,0:T(8,128)(2,1)S(1)}, bf16[16,2048]{1,0:T(8,128)(2,1)S(1)}, u32[]{:S(2)}, u32[]{:S(2)}) collective-permute-start(bf16[16,2048]{1,0:T(8,128)(2,1)S(1)} %get-tuple-element.54), channel_id=1, source_target_pairs={{0,2},{1,3},{2,0},{3,1},{4,6},{5,7},{6,4},{7,5},{8,10},{9,11},{10,... | collective-permute-start | bytes 196616 | tf_op jit(solution)/shard_map/ppermute | solution.py:25
  4.2 4.2 %collective-permute-start.2 = (bf16[16,2048]{1,0:T(8,128)(2,1)S(1)}, bf16[16,2048]{1,0:T(8,128)(2,1)S(1)}, u32[]{:S(2)}, u32[]{:S(2)}) collective-permute-start(bf16[16,2048]{1,0:T(8,128)(2,1)S(1)} %get-tuple-element.55), channel_id=1, source_target_pairs={{0,3},{1,2},{2,1},{3,0},{4,7},{5,6},{6,5},{7,4},{8,11},{9,10},{10,... | collective-permute-start | bytes 196616 | tf_op jit(solution)/shard_map/ppermute | solution.py:25
  6.5 29.7 %collective-permute-start.7 = (bf16[384,1536]{1,0:T(8,128)(2,1)}, bf16[384,1536]{1,0:T(8,128)(2,1)}, u32[]{:S(2)}, u32[]{:S(2)}) collective-permute-start(bf16[384,1536]{1,0:T(8,128)(2,1)} %get-tuple-element.71), channel_id=1, source_target_pairs={{0,2},{1,3},{2,0},{3,1},{4,6},{5,7},{6,4},{7,5},{8,10},{9,11},{10,... | collective-permute-start | bytes 3538952 | tf_op jit(solution)/shard_map/ppermute | solution.py:25
  8.3 8.3 %collective-permute-start.3 = (bf16[384,2048]{1,0:T(8,128)(2,1)S(1)}, bf16[384,2048]{1,0:T(8,128)(2,1)S(1)}, u32[]{:S(2)}, u32[]{:S(2)}) collective-permute-start(bf16[384,2048]{1,0:T(8,128)(2,1)S(1)} %copy-done), channel_id=1, source_target_pairs={{0,1},{1,0},{2,3},{3,2},{4,5},{5,4},{6,7},{7,6},{8,9},{9,8},{10,11... | collective-permute-start | bytes 4718600 | tf_op jit(solution)/shard_map/ppermute | solution.py:25
  9.1 15.7 %collective-permute-start.5 = (bf16[64,2048]{1,0:T(8,128)(2,1)}, bf16[64,2048]{1,0:T(8,128)(2,1)}, u32[]{:S(2)}, u32[]{:S(2)}) collective-permute-start(bf16[64,2048]{1,0:T(8,128)(2,1)} %shard_map.64.refs_0_), channel_id=1, source_target_pairs={{0,8},{4,12},{8,0},{12,4},{16,28},{20,24},{24,20},{28,16},{1,9},{5... | collective-permute-start | bytes 786440 | tf_op jit(solution)/shard_map/ppermute | solution.py:326
  11.8 3.4 %copy-start.1 = (bf16[8192,512]{1,0:T(8,128)(2,1)S(1)}, bf16[8192,512]{1,0:T(8,128)(2,1)}, u32[]{:S(2)}) copy-start(bf16[8192,512]{1,0:T(8,128)(2,1)} %weight_ref.13) | copy-start | bytes 25165828
  15.1 3.4 %copy-start.2 = (bf16[8192,512]{1,0:T(8,128)(2,1)S(1)}, bf16[8192,512]{1,0:T(8,128)(2,1)}, u32[]{:S(2)}) copy-start(bf16[8192,512]{1,0:T(8,128)(2,1)} %weight_ref.13) | copy-start | bytes 25165828
  16.6 17.2 %copy-start.5 = (s32[1,384]{1,0:T(1,128)}, s32[1,384]{1,0:T(1,128)S(1)}, u32[]{:S(2)}) copy-start(s32[1,384]{1,0:T(1,128)S(1)} %get-tuple-element.72.stored_ref.refs_2_) | copy-start | bytes 4612
  16.6 9.3 %collective-permute-start.6 = (bf16[64,512]{1,0:T(8,128)(2,1)}, bf16[64,512]{1,0:T(8,128)(2,1)S(1)}, u32[]{:S(2)}, u32[]{:S(2)}) collective-permute-start(bf16[64,512]{1,0:T(8,128)(2,1)} %bitcast.9.refs_5_), channel_id=1, source_target_pairs={{0,4},{4,0},{8,12},{12,8},{1,5},{5,1},{9,13},{13,9},{2,6},{6,2},{1... | collective-permute-start | bytes 196616 | tf_op jit(solution)/shard_map/ppermute | solution.py:25
  19.4 12.2 %collective-permute-start.9 = (bf16[64,2048]{1,0:T(8,128)(2,1)}, bf16[64,2048]{1,0:T(8,128)(2,1)S(1)}, u32[]{:S(2)}, u32[]{:S(2)}) collective-permute-start(bf16[64,2048]{1,0:T(8,128)(2,1)} %shard_map.64.refs_0_), channel_id=1, source_target_pairs={{0,4},{4,0},{8,12},{12,8},{1,5},{5,1},{9,13},{13,9},{2,6},{6,2},{1... | collective-permute-start | bytes 786440 | tf_op jit(solution)/shard_map/ppermute | solution.py:25
  21.0 23.0 %collective-permute-start.4 = (bf16[384,512]{1,0:T(8,128)(2,1)}, bf16[384,512]{1,0:T(8,128)(2,1)}, u32[]{:S(2)}, u32[]{:S(2)}) collective-permute-start(bf16[384,512]{1,0:T(8,128)(2,1)} %get-tuple-element.62), channel_id=1, source_target_pairs={{0,2},{1,3},{2,0},{3,1},{4,6},{5,7},{6,4},{7,5},{8,10},{9,11},{10,... | collective-permute-start | bytes 1179656 | tf_op jit(solution)/shard_map/ppermute | solution.py:25
  25.9 7.9 %collective-permute-start.10 = (bf16[64,2048]{1,0:T(8,128)(2,1)}, bf16[64,2048]{1,0:T(8,128)(2,1)S(1)}, u32[]{:S(2)}, u32[]{:S(2)}) collective-permute-start(bf16[64,2048]{1,0:T(8,128)(2,1)} %collective-permute-done.5.refs_2_), channel_id=1, source_target_pairs={{0,16},{16,0},{1,17},{17,1},{2,18},{18,2},{3,19},{19,3},{4,20},{20... | collective-permute-start | bytes 786440 | tf_op jit(solution)/shard_map/ppermute | solution.py:25
  27.7 8.5 %collective-permute-start.8 = (bf16[64,512]{1,0:T(8,128)(2,1)}, bf16[64,512]{1,0:T(8,128)(2,1)S(1)}, u32[]{:S(2)}, u32[]{:S(2)}) collective-permute-start(bf16[64,512]{1,0:T(8,128)(2,1)} %bitcast.9.refs_5_), channel_id=1, source_target_pairs={{0,8},{4,12},{8,0},{12,4},{16,28},{20,24},{24,20},{28,16},{1,9},{5... | collective-permute-start | bytes 196616 | tf_op jit(solution)/shard_map/ppermute | solution.py:326
  36.3 3.9 %collective-permute-start.13 = (f32[64,384]{1,0:T(8,128)S(1)}, f32[64,384]{1,0:T(8,128)S(1)}, u32[]{:S(2)}, u32[]{:S(2)}) collective-permute-start(f32[64,384]{1,0:T(8,128)S(1)} %shard_map.69), channel_id=1, source_target_pairs={{0,1},{1,0},{2,3},{3,2},{4,5},{5,4},{6,7},{7,6},{8,9},{9,8},{10,11... | collective-permute-start | bytes 294920 | tf_op jit(solution)/shard_map/ppermute | solution.py:25
  36.3 5.5 %collective-permute-start.12 = (bf16[384,1536]{1,0:T(8,128)(2,1)}, bf16[384,1536]{1,0:T(8,128)(2,1)S(1)}, u32[]{:S(2)}, u32[]{:S(2)}) collective-permute-start(bf16[384,1536]{1,0:T(8,128)(2,1)} %collective-permute-done.7.refs_0_), channel_id=1, source_target_pairs={{0,1},{1,0},{2,3},{3,2},{4,5},{5,4},{6,7},{7,6},{8,9},{9,8},{10,11... | collective-permute-start | bytes 3538952 | tf_op jit(solution)/shard_map/ppermute | solution.py:25
  39.0 4.3 %collective-permute-start.11 = (bf16[64,512]{1,0:T(8,128)(2,1)S(1)}, bf16[64,512]{1,0:T(8,128)(2,1)S(1)}, u32[]{:S(2)}, u32[]{:S(2)}) collective-permute-start(bf16[64,512]{1,0:T(8,128)(2,1)S(1)} %collective-permute-done.8.refs_7_), channel_id=1, source_target_pairs={{0,16},{16,0},{1,17},{17,1},{2,18},{18,2},{3,19},{19,3},{4,20},{20... | collective-permute-start | bytes 196616 | tf_op jit(solution)/shard_map/ppermute | solution.py:25
  40.2 4.2 %copy-start.6 = (s32[1,384]{1,0:T(1,128)S(1)}, s32[1,384]{1,0:T(1,128)}, u32[]{:S(2)}) copy-start(s32[1,384]{1,0:T(1,128)} %copy-done.5) | copy-start | bytes 4612
  40.2 4.2 %collective-permute-start.15 = (bf16[64,384]{1,0:T(8,128)(2,1)S(1)}, bf16[64,384]{1,0:T(8,128)(2,1)S(1)}, u32[]{:S(2)}, u32[]{:S(2)}) collective-permute-start(bf16[64,384]{1,0:T(8,128)(2,1)S(1)} %get-tuple-element.97), channel_id=1, source_target_pairs={{0,2},{1,3},{2,0},{3,1},{4,6},{5,7},{6,4},{7,5},{8,10},{9,11},{10,... | collective-permute-start | bytes 147464 | tf_op jit(solution)/shard_map/ppermute | solution.py:25
  44.0 2.0 %collective-permute-start.14 = (bf16[384,512]{1,0:T(8,128)(2,1)}, bf16[384,512]{1,0:T(8,128)(2,1)S(1)}, u32[]{:S(2)}, u32[]{:S(2)}) collective-permute-start(bf16[384,512]{1,0:T(8,128)(2,1)} %collective-permute-done.4.refs_0_), channel_id=1, source_target_pairs={{0,1},{1,0},{2,3},{3,2},{4,5},{5,4},{6,7},{7,6},{8,9},{9,8},{10,11... | collective-permute-start | bytes 1179656 | tf_op jit(solution)/shard_map/ppermute | solution.py:25

commit v30 on v29

--- a/solution.py
+++ b/solution.py
@@ -93,10 +93,10 @@
     for (flip, first, skip, width), part in zip(places, features):
         for k in range(0, width, tile):
             start = pl.multiple_of((me ^ flip) * depth + first + k, LANES)
+            pltpu.make_async_copy(part.at[:, pl.ds(skip + k, tile)], held_ref.at[t], sems.at[0, t]).start()
             pltpu.make_async_copy(
                 weight_ref.at[pl.ds(start, tile)], rows_ref.at[t], sems.at[1, t]
             ).start()
-            pltpu.make_async_copy(part.at[:, pl.ds(skip + k, tile)], held_ref.at[t], sems.at[0, t]).start()
             t += 1
 
 

time: 47.6 us -> 47.5 us (level)
  no operation moved by 1% of the time
where the time goes in v30:
time: 47.5 us; the launch traced here: 47.2 us
  starting transfers between devices  17.5 us (37%)
  Pallas kernels  15.7 us (33%)
  waiting for transfers between devices  9.02 us (19%)
  local copies, waits for them, and re-layouts  4.79 us (10%)
    ppermute x14, starting transfers between devices, flipped(): return lax.ppermute(value, axis, [(i, i ^ flip) for i in range(count)])  12.8 us
    ppermute x14, waiting for transfers between devices, flipped(): return lax.ppermute(value, axis, [(i, i ^ flip) for i in range(count)])  6.49 us
    pallas_call x4, Pallas kernels, products(): call(functools.partial(products_kernel, tile, depth, places), jax.ShapeDt...  6.19 us
    ppermute x2, starting transfers between devices, fetch_far(): lax.ppermute(value, ('parts', 'adapter'), route)  4.68 us
    unnamed x14, local copies, waits for them, and re-layouts  3.72 us
    ppermute x2, waiting for transfers between devices, fetch_far(): lax.ppermute(value, ('parts', 'adapter'), route)  2.52 us
    pallas_call x1, Pallas kernels, body(): call(functools.partial(shrink_kernel, tile, flips, pairs, slots), jax.Sha...  2.46 us
    pallas_call x1, Pallas kernels, body(): call(functools.partial(cut_kernel, edges), [jax.ShapeDtypeStruct((rows, b...  2.23 us
  transfers between devices with their start and end apart: 16, of which 7 were waited for; matrix products, arithmetic and copies ran while one was open for 0% of the time, Pallas kernels for 31%

profile of v30, /device:TPU:0, one launch (start us, length us, event | category | flops | bytes accessed | tf_op | source)
XLA Modules:
  0.0 47.2 jit_solution(18021079065141325698)
XLA Ops:
  0.0 1.1 %dynamic-slice_bitcast_fusion = (bf16[16,2048]{1,0:T(8,128)(2,1)S(1)}, bf16[16,2048]{1,0:T(8,128)(2,1)S(1)}, bf16[16,2048]{1,0:T(8,128)(2,1)S(1)}, bf16[16,2048]{1,0:T(8,128)(2,1)S(1)}) fusion(bf16[1,8192,16]{1,2,0:T(8,128)(2,1)} %param.10, s32[]{:T(128)S(6)} %select_n.15, s32[]{:T(128)S(6)} %select_n.13, s32[]{:T(128)S(6)} %select_n.12, s32[]{:T(128)S(6)} %select_n.14), kind=kLoop, calls=%fused_computation | loop fusion | bytes 524304 | tf_op jit(solution)/shard_map/dynamic_slice | solution.py:253
  1.6 2.6 %collective-permute-start.1 = (bf16[16,2048]{1,0:T(8,128)(2,1)S(1)}, bf16[16,2048]{1,0:T(8,128)(2,1)S(1)}, u32[]{:S(2)}, u32[]{:S(2)}) collective-permute-start(bf16[16,2048]{1,0:T(8,128)(2,1)S(1)} %get-tuple-element.54), channel_id=1, source_target_pairs={{0,2},{1,3},{2,0},{3,1},{4,6},{5,7},{6,4},{7,5},{8,10},{9,11},{10,... | collective-permute-start | bytes 196616 | tf_op jit(solution)/shard_map/ppermute | solution.py:25
  4.3 2.2 %shard_map.66 = (bf16[384,1536]{1,0:T(8,128)(2,1)}, bf16[384,512]{1,0:T(8,128)(2,1)}) custom-call(bf16[384,2048]{1,0:T(8,128)(2,1)} %tokens_ref.1), custom_call_target="tpu_custom_call" | custom-call | tf_op jit(solution)/shard_map/pallas_call | solution.py:259
  6.5 1.8 %collective-permute-start.7 = (bf16[384,1536]{1,0:T(8,128)(2,1)}, bf16[384,1536]{1,0:T(8,128)(2,1)}, u32[]{:S(2)}, u32[]{:S(2)}) collective-permute-start(bf16[384,1536]{1,0:T(8,128)(2,1)} %get-tuple-element.71), channel_id=1, source_target_pairs={{0,2},{1,3},{2,0},{3,1},{4,6},{5,7},{6,4},{7,5},{8,10},{9,11},{10,... | collective-permute-start | bytes 3538952 | tf_op jit(solution)/shard_map/ppermute | solution.py:25
  9.1 2.7 %collective-permute-start.5 = (bf16[64,2048]{1,0:T(8,128)(2,1)}, bf16[64,2048]{1,0:T(8,128)(2,1)}, u32[]{:S(2)}, u32[]{:S(2)}) collective-permute-start(bf16[64,2048]{1,0:T(8,128)(2,1)} %shard_map.64.refs_0_), channel_id=1, source_target_pairs={{0,8},{4,12},{8,0},{12,4},{16,28},{20,24},{24,20},{28,16},{1,9},{5... | collective-permute-start | bytes 786440 | tf_op jit(solution)/shard_map/ppermute | solution.py:326
  11.8 3.4 %copy-done.1 = bf16[8192,512]{1,0:T(8,128)(2,1)S(1)} copy-done((bf16[8192,512]{1,0:T(8,128)(2,1)S(1)}, bf16[8192,512]{1,0:T(8,128)(2,1)}, u32[]{:S(2)}) %copy-start.1) | copy-done | bytes 8388632
  15.1 1.4 %shard_map.65 = (f32[384,512]{1,0:T(8,128)S(1)}, s32[1,384]{1,0:T(1,128)S(1)}) custom-call(s32[4]{0:T(128)S(1)} %copy-done.4, s32[1,384]{1,0:T(1,128)S(1)} %bitcast.18, bf16[8192,512]{1,0:T(8,128)(2,1)S(1)} %copy-done.1, bf16[384,2048]{1,0:T(8,128)(2,1)S(1)} %copy-done), custom_call_target="tpu_custom_call" | custom-call | flops 99999997952 | tf_op jit(solution)/shard_map/pallas_call | solution.py:337
  16.6 1.6 %collective-permute-start.6 = (bf16[64,512]{1,0:T(8,128)(2,1)}, bf16[64,512]{1,0:T(8,128)(2,1)S(1)}, u32[]{:S(2)}, u32[]{:S(2)}) collective-permute-start(bf16[64,512]{1,0:T(8,128)(2,1)} %bitcast.9.refs_5_), channel_id=1, source_target_pairs={{0,4},{4,0},{8,12},{12,8},{1,5},{5,1},{9,13},{13,9},{2,6},{6,2},{1... | collective-permute-start | bytes 196616 | tf_op jit(solution)/shard_map/ppermute | solution.py:25
  18.5 0.8 %shard_map.67.refs_1_ = f32[384,512]{1,0:T(8,128)S(1)} custom-call(bf16[8192,512]{1,0:T(8,128)(2,1)S(1)} %copy-done.2, bf16[384,2048]{1,0:T(8,128)(2,1)S(1)} %copy-done, f32[384,512]{1,0:T(8,128)S(1)} %get-tuple-element.64.refs_1_), custom_call_target="tpu_custom_call" | custom-call | flops 99999997952 | tf_op jit(solution)/shard_map/pallas_call | solution.py:308
  19.4 1.6 %collective-permute-start.9 = (bf16[64,2048]{1,0:T(8,128)(2,1)}, bf16[64,2048]{1,0:T(8,128)(2,1)S(1)}, u32[]{:S(2)}, u32[]{:S(2)}) collective-permute-start(bf16[64,2048]{1,0:T(8,128)(2,1)} %shard_map.64.refs_0_), channel_id=1, source_target_pairs={{0,4},{4,0},{8,12},{12,8},{1,5},{5,1},{9,13},{13,9},{2,6},{6,2},{1... | collective-permute-start | bytes 786440 | tf_op jit(solution)/shard_map/ppermute | solution.py:25
  21.0 1.2 %collective-permute-start.4 = (bf16[384,512]{1,0:T(8,128)(2,1)}, bf16[384,512]{1,0:T(8,128)(2,1)}, u32[]{:S(2)}, u32[]{:S(2)}) collective-permute-start(bf16[384,512]{1,0:T(8,128)(2,1)} %get-tuple-element.62), channel_id=1, source_target_pairs={{0,2},{1,3},{2,0},{3,1},{4,6},{5,7},{6,4},{7,5},{8,10},{9,11},{10,... | collective-permute-start | bytes 1179656 | tf_op jit(solution)/shard_map/ppermute | solution.py:25
  22.2 2.5 %collective-permute-done.5.refs_2_ = bf16[64,2048]{1,0:T(8,128)(2,1)} collective-permute-done((bf16[64,2048]{1,0:T(8,128)(2,1)}, bf16[64,2048]{1,0:T(8,128)(2,1)}, u32[]{:S(2)}, u32[]{:S(2)}) %collective-permute-start.5) | collective-permute-done | bytes 262176 | tf_op jit(solution)/shard_map/ppermute | solution.py:326
  24.8 1.1 %collective-permute-done.6.refs_6_ = bf16[64,512]{1,0:T(8,128)(2,1)S(1)} collective-permute-done((bf16[64,512]{1,0:T(8,128)(2,1)}, bf16[64,512]{1,0:T(8,128)(2,1)S(1)}, u32[]{:S(2)}, u32[]{:S(2)}) %collective-permute-start.6) | collective-permute-done | bytes 65568 | tf_op jit(solution)/shard_map/ppermute | solution.py:25
  25.9 1.8 %shard_map.68.refs_1_ = f32[384,512]{1,0:T(8,128)S(1)} custom-call(bf16[8192,512]{1,0:T(8,128)(2,1)S(1)} %copy-done.2, bf16[384,2048]{1,0:T(8,128)(2,1)S(1)} %collective-permute-done.3.refs_0_, f32[384,512]{1,0:T(8,128)S(1)} %shard_map.67.refs_1_), custom_call_target="tpu_custom_call" | custom-call | flops 99999997952 | tf_op jit(solution)/shard_map/pallas_call | solution.py:308
  27.7 2.0 %collective-permute-start.8 = (bf16[64,512]{1,0:T(8,128)(2,1)}, bf16[64,512]{1,0:T(8,128)(2,1)S(1)}, u32[]{:S(2)}, u32[]{:S(2)}) collective-permute-start(bf16[64,512]{1,0:T(8,128)(2,1)} %bitcast.9.refs_5_), channel_id=1, source_target_pairs={{0,8},{4,12},{8,0},{12,4},{16,28},{20,24},{24,20},{28,16},{1,9},{5... | collective-permute-start | bytes 196616 | tf_op jit(solution)/shard_map/ppermute | solution.py:326
  29.8 1.8 %collective-permute-done.9.refs_1_ = bf16[64,2048]{1,0:T(8,128)(2,1)S(1)} collective-permute-done((bf16[64,2048]{1,0:T(8,128)(2,1)}, bf16[64,2048]{1,0:T(8,128)(2,1)S(1)}, u32[]{:S(2)}, u32[]{:S(2)}) %collective-permute-start.9) | collective-permute-done | bytes 262176 | tf_op jit(solution)/shard_map/ppermute | solution.py:25
  31.6 2.2 %collective-permute-done.10.refs_3_ = bf16[64,2048]{1,0:T(8,128)(2,1)S(1)} collective-permute-done((bf16[64,2048]{1,0:T(8,128)(2,1)}, bf16[64,2048]{1,0:T(8,128)(2,1)S(1)}, u32[]{:S(2)}, u32[]{:S(2)}) %collective-permute-start.10) | collective-permute-done | bytes 262176 | tf_op jit(solution)/shard_map/ppermute | solution.py:25
  33.8 2.5 %shard_map.69 = f32[64,384]{1,0:T(8,128)S(1)} custom-call(bf16[384,2048]{1,0:T(8,128)(2,1)S(1)} %copy-done, s32[1,384]{1,0:T(1,128)S(1)} %get-tuple-element.72.stored_ref.refs_2_, bf16[64,2048]{1,0:T(8,128)(2,1)} %shard_map.64.refs_0_, bf16[64,2048]{1,0:T(8,128)(2,1)S(1)} %collective-permute-done.9.refs_1_, bf16[64,2048]{1,0:T(8,128)(2,1)} %collective-permute-done.5.refs_2_, ...), custom_call_target="tpu_custom_call" | custom-call | flops 99999997952 | tf_op jit(solution)/shard_map/pallas_call | solution.py:365
  36.8 2.2 %shard_map.70.refs_1_ = f32[384,512]{1,0:T(8,128)S(1)} custom-call(bf16[8192,512]{1,0:T(8,128)(2,1)S(1)} %copy-done.2, bf16[384,1536]{1,0:T(8,128)(2,1)} %collective-permute-done.7.refs_0_, f32[384,512]{1,0:T(8,128)S(1)} %shard_map.68.refs_1_), custom_call_target="tpu_custom_call" | custom-call | flops 99999997952 | tf_op jit(solution)/shard_map/pallas_call | solution.py:308
  39.0 1.2 %collective-permute-start.11 = (bf16[64,512]{1,0:T(8,128)(2,1)S(1)}, bf16[64,512]{1,0:T(8,128)(2,1)S(1)}, u32[]{:S(2)}, u32[]{:S(2)}) collective-permute-start(bf16[64,512]{1,0:T(8,128)(2,1)S(1)} %collective-permute-done.8.refs_7_), channel_id=1, source_target_pairs={{0,16},{16,0},{1,17},{17,1},{2,18},{18,2},{3,19},{19,3},{4,20},{20... | collective-permute-start | bytes 196616 | tf_op jit(solution)/shard_map/ppermute | solution.py:25
  40.2 1.6 %collective-permute-start.15 = (bf16[64,384]{1,0:T(8,128)(2,1)S(1)}, bf16[64,384]{1,0:T(8,128)(2,1)S(1)}, u32[]{:S(2)}, u32[]{:S(2)}) collective-permute-start(bf16[64,384]{1,0:T(8,128)(2,1)S(1)} %get-tuple-element.97), channel_id=1, source_target_pairs={{0,2},{1,3},{2,0},{3,1},{4,6},{5,7},{6,4},{7,5},{8,10},{9,11},{10,... | collective-permute-start | bytes 147464 | tf_op jit(solution)/shard_map/ppermute | solution.py:25
  41.8 1.4 %shard_map.71.refs_1_ = f32[384,512]{1,0:T(8,128)S(1)} custom-call(bf16[8192,512]{1,0:T(8,128)(2,1)S(1)} %copy-done.2, bf16[384,1536]{1,0:T(8,128)(2,1)S(1)} %collective-permute-done.12.refs_0_, f32[384,512]{1,0:T(8,128)S(1)} %shard_map.70.refs_1_), custom_call_target="tpu_custom_call" | custom-call | flops 99999997952 | tf_op jit(solution)/shard_map/pallas_call | solution.py:308
  44.5 1.5 %shard_map.72 = (f32[384,512]{1,0:T(8,128)S(1)}, bf16[256,384]{1,0:T(8,128)(2,1)S(1)}, bf16[256,512]{1,0:T(8,128)(2,1)S(1)}) custom-call(bf16[8192,512]{1,0:T(8,128)(2,1)S(1)} %copy-done.2, bf16[384,512]{1,0:T(8,128)(2,1)} %collective-permute-done.4.refs_0_, f32[384,512]{1,0:T(8,128)S(1)} %shard_map.71.refs_1_, s32[1,384]{1,0:T(1,128)S(1)} %copy-done.6, ...), custom_call_target="tpu_custom_call" | custom-call | flops 99999997952 | tf_op jit(solution)/shard_map/pallas_call | solution.py:396
  46.0 1.2 %shard_map.73 = bf16[384,512]{1,0:T(8,128)(2,1)} custom-call(bf16[8192,512]{1,0:T(8,128)(2,1)S(1)} %copy-done.2, bf16[384,512]{1,0:T(8,128)(2,1)S(1)} %collective-permute-done.14.refs_0_, f32[384,512]{1,0:T(8,128)S(1)} %get-tuple-element.94.refs_1_, bf16[256,384]{1,0:T(8,128)(2,1)S(1)} %get-tuple-element.95.refs_2_, ...), custom_call_target="tpu_custom_call" | custom-call | flops 99999997952 | tf_op jit(solution)/shard_map/pallas_call | solution.py:410
  (34 shorter events, 3.7 us)
Async XLA Ops:
  0.0 8.3 %copy-start = (bf16[384,2048]{1,0:T(8,128)(2,1)S(1)}, bf16[384,2048]{1,0:T(8,128)(2,1)}, u32[]{:S(2)}) copy-start(bf16[384,2048]{1,0:T(8,128)(2,1)} %tokens_ref.1) | copy-start | bytes 4718596
  0.0 11.8 %copy-start.3 = (s32[384,1]{0,1:T(1,128)S(1)}, s32[384,1]{0,1:T(1,128)}, u32[]{:S(2)}) copy-start(s32[384,1]{0,1:T(1,128)} %param.7) | copy-start | bytes 4612
  0.0 11.8 %copy-start.4 = (s32[4]{0:T(128)S(1)}, s32[4]{0:T(128)}, u32[]{:S(2)}) copy-start(s32[4]{0:T(128)} %placement_ref.1) | copy-start | bytes 52
  1.1 7.2 %collective-permute-start = (bf16[16,2048]{1,0:T(8,128)(2,1)S(1)}, bf16[16,2048]{1,0:T(8,128)(2,1)S(1)}, u32[]{:S(2)}, u32[]{:S(2)}) collective-permute-start(bf16[16,2048]{1,0:T(8,128)(2,1)S(1)} %get-tuple-element.52), channel_id=1, source_target_pairs={{0,1},{1,0},{2,3},{3,2},{4,5},{5,4},{6,7},{7,6},{8,9},{9,8},{10,11... | collective-permute-start | bytes 196616 | tf_op jit(solution)/shard_map/ppermute | solution.py:25
  1.6 6.7 %collective-permute-start.1 = (bf16[16,2048]{1,0:T(8,128)(2,1)S(1)}, bf16[16,2048]{1,0:T(8,128)(2,1)S(1)}, u32[]{:S(2)}, u32[]{:S(2)}) collective-permute-start(bf16[16,2048]{1,0:T(8,128)(2,1)S(1)} %get-tuple-element.54), channel_id=1, source_target_pairs={{0,2},{1,3},{2,0},{3,1},{4,6},{5,7},{6,4},{7,5},{8,10},{9,11},{10,... | collective-permute-start | bytes 196616 | tf_op jit(solution)/shard_map/ppermute | solution.py:25
  4.2 4.2 %collective-permute-start.2 = (bf16[16,2048]{1,0:T(8,128)(2,1)S(1)}, bf16[16,2048]{1,0:T(8,128)(2,1)S(1)}, u32[]{:S(2)}, u32[]{:S(2)}) collective-permute-start(bf16[16,2048]{1,0:T(8,128)(2,1)S(1)} %get-tuple-element.55), channel_id=1, source_target_pairs={{0,3},{1,2},{2,1},{3,0},{4,7},{5,6},{6,5},{7,4},{8,11},{9,10},{10,... | collective-permute-start | bytes 196616 | tf_op jit(solution)/shard_map/ppermute | solution.py:25
  6.5 29.7 %collective-permute-start.7 = (bf16[384,1536]{1,0:T(8,128)(2,1)}, bf16[384,1536]{1,0:T(8,128)(2,1)}, u32[]{:S(2)}, u32[]{:S(2)}) collective-permute-start(bf16[384,1536]{1,0:T(8,128)(2,1)} %get-tuple-element.71), channel_id=1, source_target_pairs={{0,2},{1,3},{2,0},{3,1},{4,6},{5,7},{6,4},{7,5},{8,10},{9,11},{10,... | collective-permute-start | bytes 3538952 | tf_op jit(solution)/shard_map/ppermute | solution.py:25
  8.3 8.3 %collective-permute-start.3 = (bf16[384,2048]{1,0:T(8,128)(2,1)S(1)}, bf16[384,2048]{1,0:T(8,128)(2,1)S(1)}, u32[]{:S(2)}, u32[]{:S(2)}) collective-permute-start(bf16[384,2048]{1,0:T(8,128)(2,1)S(1)} %copy-done), channel_id=1, source_target_pairs={{0,1},{1,0},{2,3},{3,2},{4,5},{5,4},{6,7},{7,6},{8,9},{9,8},{10,11... | collective-permute-start | bytes 4718600 | tf_op jit(solution)/shard_map/ppermute | solution.py:25
  9.1 15.7 %collective-permute-start.5 = (bf16[64,2048]{1,0:T(8,128)(2,1)}, bf16[64,2048]{1,0:T(8,128)(2,1)}, u32[]{:S(2)}, u32[]{:S(2)}) collective-permute-start(bf16[64,2048]{1,0:T(8,128)(2,1)} %shard_map.64.refs_0_), channel_id=1, source_target_pairs={{0,8},{4,12},{8,0},{12,4},{16,28},{20,24},{24,20},{28,16},{1,9},{5... | collective-permute-start | bytes 786440 | tf_op jit(solution)/shard_map/ppermute | solution.py:326
  11.8 3.4 %copy-start.1 = (bf16[8192,512]{1,0:T(8,128)(2,1)S(1)}, bf16[8192,512]{1,0:T(8,128)(2,1)}, u32[]{:S(2)}) copy-start(bf16[8192,512]{1,0:T(8,128)(2,1)} %weight_ref.13) | copy-start | bytes 25165828
  15.1 3.4 %copy-start.2 = (bf16[8192,512]{1,0:T(8,128)(2,1)S(1)}, bf16[8192,512]{1,0:T(8,128)(2,1)}, u32[]{:S(2)}) copy-start(bf16[8192,512]{1,0:T(8,128)(2,1)} %weight_ref.13) | copy-start | bytes 25165828
  16.5 17.2 %copy-start.5 = (s32[1,384]{1,0:T(1,128)}, s32[1,384]{1,0:T(1,128)S(1)}, u32[]{:S(2)}) copy-start(s32[1,384]{1,0:T(1,128)S(1)} %get-tuple-element.72.stored_ref.refs_2_) | copy-start | bytes 4612
  16.6 9.3 %collective-permute-start.6 = (bf16[64,512]{1,0:T(8,128)(2,1)}, bf16[64,512]{1,0:T(8,128)(2,1)S(1)}, u32[]{:S(2)}, u32[]{:S(2)}) collective-permute-start(bf16[64,512]{1,0:T(8,128)(2,1)} %bitcast.9.refs_5_), channel_id=1, source_target_pairs={{0,4},{4,0},{8,12},{12,8},{1,5},{5,1},{9,13},{13,9},{2,6},{6,2},{1... | collective-permute-start | bytes 196616 | tf_op jit(solution)/shard_map/ppermute | solution.py:25
  19.4 12.2 %collective-permute-start.9 = (bf16[64,2048]{1,0:T(8,128)(2,1)}, bf16[64,2048]{1,0:T(8,128)(2,1)S(1)}, u32[]{:S(2)}, u32[]{:S(2)}) collective-permute-start(bf16[64,2048]{1,0:T(8,128)(2,1)} %shard_map.64.refs_0_), channel_id=1, source_target_pairs={{0,4},{4,0},{8,12},{12,8},{1,5},{5,1},{9,13},{13,9},{2,6},{6,2},{1... | collective-permute-start | bytes 786440 | tf_op jit(solution)/shard_map/ppermute | solution.py:25
  21.0 23.0 %collective-permute-start.4 = (bf16[384,512]{1,0:T(8,128)(2,1)}, bf16[384,512]{1,0:T(8,128)(2,1)}, u32[]{:S(2)}, u32[]{:S(2)}) collective-permute-start(bf16[384,512]{1,0:T(8,128)(2,1)} %get-tuple-element.62), channel_id=1, source_target_pairs={{0,2},{1,3},{2,0},{3,1},{4,6},{5,7},{6,4},{7,5},{8,10},{9,11},{10,... | collective-permute-start | bytes 1179656 | tf_op jit(solution)/shard_map/ppermute | solution.py:25
  25.9 7.9 %collective-permute-start.10 = (bf16[64,2048]{1,0:T(8,128)(2,1)}, bf16[64,2048]{1,0:T(8,128)(2,1)S(1)}, u32[]{:S(2)}, u32[]{:S(2)}) collective-permute-start(bf16[64,2048]{1,0:T(8,128)(2,1)} %collective-permute-done.5.refs_2_), channel_id=1, source_target_pairs={{0,16},{16,0},{1,17},{17,1},{2,18},{18,2},{3,19},{19,3},{4,20},{20... | collective-permute-start | bytes 786440 | tf_op jit(solution)/shard_map/ppermute | solution.py:25
  27.7 8.5 %collective-permute-start.8 = (bf16[64,512]{1,0:T(8,128)(2,1)}, bf16[64,512]{1,0:T(8,128)(2,1)S(1)}, u32[]{:S(2)}, u32[]{:S(2)}) collective-permute-start(bf16[64,512]{1,0:T(8,128)(2,1)} %bitcast.9.refs_5_), channel_id=1, source_target_pairs={{0,8},{4,12},{8,0},{12,4},{16,28},{20,24},{24,20},{28,16},{1,9},{5... | collective-permute-start | bytes 196616 | tf_op jit(solution)/shard_map/ppermute | solution.py:326
  36.3 3.9 %collective-permute-start.13 = (f32[64,384]{1,0:T(8,128)S(1)}, f32[64,384]{1,0:T(8,128)S(1)}, u32[]{:S(2)}, u32[]{:S(2)}) collective-permute-start(f32[64,384]{1,0:T(8,128)S(1)} %shard_map.69), channel_id=1, source_target_pairs={{0,1},{1,0},{2,3},{3,2},{4,5},{5,4},{6,7},{7,6},{8,9},{9,8},{10,11... | collective-permute-start | bytes 294920 | tf_op jit(solution)/shard_map/ppermute | solution.py:25
  36.3 5.4 %collective-permute-start.12 = (bf16[384,1536]{1,0:T(8,128)(2,1)}, bf16[384,1536]{1,0:T(8,128)(2,1)S(1)}, u32[]{:S(2)}, u32[]{:S(2)}) collective-permute-start(bf16[384,1536]{1,0:T(8,128)(2,1)} %collective-permute-done.7.refs_0_), channel_id=1, source_target_pairs={{0,1},{1,0},{2,3},{3,2},{4,5},{5,4},{6,7},{7,6},{8,9},{9,8},{10,11... | collective-permute-start | bytes 3538952 | tf_op jit(solution)/shard_map/ppermute | solution.py:25
  39.0 4.3 %collective-permute-start.11 = (bf16[64,512]{1,0:T(8,128)(2,1)S(1)}, bf16[64,512]{1,0:T(8,128)(2,1)S(1)}, u32[]{:S(2)}, u32[]{:S(2)}) collective-permute-start(bf16[64,512]{1,0:T(8,128)(2,1)S(1)} %collective-permute-done.8.refs_7_), channel_id=1, source_target_pairs={{0,16},{16,0},{1,17},{17,1},{2,18},{18,2},{3,19},{19,3},{4,20},{20... | collective-permute-start | bytes 196616 | tf_op jit(solution)/shard_map/ppermute | solution.py:25
  40.2 4.3 %copy-start.6 = (s32[1,384]{1,0:T(1,128)S(1)}, s32[1,384]{1,0:T(1,128)}, u32[]{:S(2)}) copy-start(s32[1,384]{1,0:T(1,128)} %copy-done.5) | copy-start | bytes 4612
  40.2 4.3 %collective-permute-start.15 = (bf16[64,384]{1,0:T(8,128)(2,1)S(1)}, bf16[64,384]{1,0:T(8,128)(2,1)S(1)}, u32[]{:S(2)}, u32[]{:S(2)}) collective-permute-start(bf16[64,384]{1,0:T(8,128)(2,1)S(1)} %get-tuple-element.97), channel_id=1, source_target_pairs={{0,2},{1,3},{2,0},{3,1},{4,6},{5,7},{6,4},{7,5},{8,10},{9,11},{10,... | collective-permute-start | bytes 147464 | tf_op jit(solution)/shard_map/ppermute | solution.py:25
  44.0 1.9 %collective-permute-start.14 = (bf16[384,512]{1,0:T(8,128)(2,1)}, bf16[384,512]{1,0:T(8,128)(2,1)S(1)}, u32[]{:S(2)}, u32[]{:S(2)}) collective-permute-start(bf16[384,512]{1,0:T(8,128)(2,1)} %collective-permute-done.4.refs_0_), channel_id=1, source_target_pairs={{0,1},{1,0},{2,3},{3,2},{4,5},{5,4},{6,7},{7,6},{8,9},{9,8},{10,11... | collective-permute-start | bytes 1179656 | tf_op jit(solution)/shard_map/ppermute | solution.py:25
